TPU v7x, 32 devices: a whole 2x2x4 slice. The times are simulated.
32 devices in a mesh: slab: 4 (over y, core), seq: 8 (over z, x).
Axes of the slice: x: 2, y: 2, z: 4, core: 2. Of those that a mesh axis runs over, the one named last changes fastest.
Arguments:
- query: bfloat16 [8192, 3072], P(('slab', 'seq')), may hold values from -9 to 9
- key: bfloat16 [8192, 3072], P(('slab', 'seq')), may hold values from -9 to 9
- value: bfloat16 [8192, 3072], P(('slab', 'seq')), may hold values from -6 to 6
- d_out: bfloat16 [8192, 3072], P(('slab', 'seq')), may hold values from -6 to 6
- pattern: int32 [48, 64, 8], P('seq', 'slab'), may hold values from 0 to 63, as said below
Outputs:
- attended: bfloat16 [8192, 3072], P(('slab', 'seq'))
- grad_query: bfloat16 [8192, 3072], P(('slab', 'seq'))
- grad_key: bfloat16 [8192, 3072], P(('slab', 'seq'))
- grad_value: bfloat16 [8192, 3072], P(('slab', 'seq'))
Inputs may be any that keep to these rules, and one draw needn't show every extreme that they name: Every list pattern[h, b] holds 8 distinct blocks: first b itself, then blocks of b's own slab, and blocks of the adjacent slabs only (slab of block k is k // 16). A list of a slab with two neighbours holds 2 blocks of each; a list of the first or the last slab holds 2 blocks of its one neighbour. For each slab and each adjacent slab, the lists of every head together reference exactly 4 blocks of that adjacent slab, the same set for all heads.
All inputs are finite; a program needn't handle non-finite values.
Results may differ from a plain program's by a relative error of at most 0.0081.
Values may be sent and summed in bfloat16 or wider, within the bound.
No kernel may reach another device: no remote copies, remote signals or barrier semaphores. Data moves between devices by JAX's collectives and lax.ppermute only.
A program may use at most 128 MiB of HBM per device.

v0:
```python
import jax
import jax.numpy as jnp
from jax import lax
from jax.sharding import PartitionSpec as P

CROSS = 4


def from_behind(x, axis, by):
    count = lax.axis_size(axis)
    pairs = [(i, i + by) for i in range(count) if 0 <= i + by < count]
    return lax.ppermute(x, axis, pairs)


def pick_blocks(table, chosen):
    return jax.vmap(lambda single, index_rows: single[index_rows])(table, chosen)


def add_blocks(accum, chosen, contrib):
    return jax.vmap(lambda single, index_rows, terms: single.at[index_rows].add(terms))(
        accum, chosen, contrib
    )


def attend(query_slab, grad_slab, window, local_ids, head_dim):
    heads_here, blocks, per_list = local_ids.shape
    slab_rows, columns = query_slab.shape
    block_rows = slab_rows // blocks
    window_blocks = window.shape[1]
    group = 4
    turns = blocks // group
    scaling = head_dim ** (-0.5)
    tables = window.reshape(2, window_blocks, block_rows, heads_here, head_dim).transpose(
        0, 3, 1, 2, 4
    )
    key_table = tables[0]
    value_table = tables[1]
    query_steps = query_slab.reshape(turns, group, block_rows, heads_here, head_dim).transpose(
        0, 3, 1, 2, 4
    )
    grad_steps = grad_slab.reshape(turns, group, block_rows, heads_here, head_dim).transpose(
        0, 3, 1, 2, 4
    )
    list_steps = local_ids.reshape(heads_here, turns, group, per_list).transpose(1, 0, 2, 3)
    shaped = (heads_here, group * per_list, block_rows, head_dim)

    def one_step(running, inputs):
        key_accum, value_accum = running
        query_group, grad_group, lists = inputs
        flat_lists = lists.reshape(heads_here, group * per_list)
        key_group = pick_blocks(key_table, flat_lists).reshape(
            heads_here, group, per_list * block_rows, head_dim
        )
        value_group = pick_blocks(value_table, flat_lists).reshape(
            heads_here, group, per_list * block_rows, head_dim
        )
        scores = (
            jnp.einsum(
                "hgid,hgjd->hgij", query_group, key_group, preferred_element_type=jnp.float32
            )
            * scaling
        )
        row_max = jnp.max(scores, axis=-1, keepdims=True)
        weights = jnp.exp(scores - row_max)
        weights = weights / jnp.sum(weights, axis=-1, keepdims=True)
        weights_low = weights.astype(jnp.bfloat16)
        attended = jnp.einsum(
            "hgij,hgjd->hgid", weights_low, value_group, preferred_element_type=jnp.float32
        ).astype(jnp.bfloat16)
        grad_prob = jnp.einsum(
            "hgid,hgjd->hgij", grad_group, value_group, preferred_element_type=jnp.float32
        )
        correction = jnp.sum(weights * grad_prob, axis=-1, keepdims=True)
        grad_score = (weights * (grad_prob - correction)).astype(jnp.bfloat16)
        grad_query = (
            jnp.einsum("hgij,hgjd->hgid", grad_score, key_group, preferred_element_type=jnp.float32)
            * scaling
        ).astype(jnp.bfloat16)
        key_terms = (
            jnp.einsum(
                "hgij,hgid->hgjd", grad_score, query_group, preferred_element_type=jnp.float32
            )
            * scaling
        )
        value_terms = jnp.einsum(
            "hgij,hgid->hgjd", weights_low, grad_group, preferred_element_type=jnp.float32
        )
        key_accum = add_blocks(key_accum, flat_lists, key_terms.reshape(shaped))
        value_accum = add_blocks(value_accum, flat_lists, value_terms.reshape(shaped))
        return ((key_accum, value_accum), (attended, grad_query))

    empty = jnp.zeros((heads_here, window_blocks, block_rows, head_dim), jnp.float32)
    sums, produced = lax.scan(one_step, (empty, empty), (query_steps, grad_steps, list_steps))
    attended = produced[0].transpose(0, 2, 3, 1, 4).reshape(slab_rows, columns)
    grad_query = produced[1].transpose(0, 2, 3, 1, 4).reshape(slab_rows, columns)
    gradients = (
        jnp.stack([sums[0], sums[1]])
        .transpose(0, 2, 3, 1, 4)
        .reshape(2, window_blocks, block_rows, columns)
    )
    return (attended, grad_query, gradients)


def local(query, key, value, d_out, pattern):
    heads_here, blocks, per_list = pattern.shape
    query_slab, key_slab, value_slab, grad_slab = (
        lax.all_to_all(query, "seq", split_axis=1, concat_axis=0, tiled=True),
        lax.all_to_all(key, "seq", split_axis=1, concat_axis=0, tiled=True),
        lax.all_to_all(value, "seq", split_axis=1, concat_axis=0, tiled=True),
        lax.all_to_all(d_out, "seq", split_axis=1, concat_axis=0, tiled=True),
    )
    slab_rows, columns = query_slab.shape
    head_dim = columns // heads_here
    block_rows = slab_rows // blocks
    own_base = lax.axis_index("slab") * blocks
    key_value = jnp.stack([key_slab, value_slab])
    block_ids = jnp.arange(blocks, dtype=jnp.int32)
    flat_lists = pattern.reshape(-1)
    reverse_rank = blocks - 1 - block_ids
    hits_prev = jnp.any(flat_lists[:, None] == (own_base - blocks + block_ids)[None, :], axis=0)
    hits_next = jnp.any(flat_lists[:, None] == (own_base + blocks + block_ids)[None, :], axis=0)
    need_prev = lax.top_k(hits_prev.astype(jnp.int32) * blocks + reverse_rank, CROSS)[1]
    need_next = lax.top_k(hits_next.astype(jnp.int32) * blocks + reverse_rank, CROSS)[1]
    asked_next = from_behind(need_prev, "slab", -1)
    asked_prev = from_behind(need_next, "slab", 1)
    blocked = key_value.reshape(2, blocks, block_rows, columns)
    came_prev = from_behind(blocked[:, asked_next], "slab", 1)
    came_next = from_behind(blocked[:, asked_prev], "slab", -1)
    window = jnp.concatenate([came_prev, blocked, came_next], axis=1)
    rank_ids = jnp.arange(CROSS, dtype=jnp.int32)
    prev_global = own_base - blocks + need_prev
    next_global = own_base + blocks + need_next
    pos_prev = jnp.sum(jnp.where(pattern[..., None] == prev_global, rank_ids, 0), axis=-1)
    pos_next = jnp.sum(jnp.where(pattern[..., None] == next_global, rank_ids, 0), axis=-1)
    in_own = (pattern >= own_base) & (pattern < own_base + blocks)
    local_ids = jnp.where(
        in_own,
        CROSS + pattern - own_base,
        jnp.where(pattern < own_base, pos_prev, CROSS + blocks + pos_next),
    )
    attended, grad_query, gradients = attend(query_slab, grad_slab, window, local_ids, head_dim)
    back_later = from_behind(gradients[:, :CROSS].astype(jnp.bfloat16), "slab", -1)
    back_earlier = from_behind(gradients[:, CROSS + blocks :].astype(jnp.bfloat16), "slab", 1)
    totals = gradients[:, CROSS : CROSS + blocks]
    totals = totals.at[:, asked_next].add(back_later.astype(jnp.float32))
    totals = totals.at[:, asked_prev].add(back_earlier.astype(jnp.float32))
    grad_key = totals[0].reshape(slab_rows, columns).astype(jnp.bfloat16)
    grad_value = totals[1].reshape(slab_rows, columns).astype(jnp.bfloat16)
    return (
        lax.all_to_all(attended, "seq", split_axis=0, concat_axis=1, tiled=True),
        lax.all_to_all(grad_query, "seq", split_axis=0, concat_axis=1, tiled=True),
        lax.all_to_all(grad_key, "seq", split_axis=0, concat_axis=1, tiled=True),
        lax.all_to_all(grad_value, "seq", split_axis=0, concat_axis=1, tiled=True),
    )


def solution(mesh):
    placed = (
        P(("slab", "seq"), None),
        P(("slab", "seq"), None),
        P(("slab", "seq"), None),
        P(("slab", "seq"), None),
        P("seq", "slab", None),
    )
    return jax.shard_map(
        local,
        mesh=mesh,
        in_specs=placed,
        out_specs=(
            P(("slab", "seq"), None),
            P(("slab", "seq"), None),
            P(("slab", "seq"), None),
            P(("slab", "seq"), None),
        ),
        check_vma=False,
    )
```

profile of v0, /device:TPU:8, one launch (start us, length us, event | category | flops | bytes accessed | tf_op | source)
XLA Modules:
  0.0 1323.7 jit_solution(5186527066698221810)
XLA Ops:
  11.1 32.7 %all-to-all-done = bf16[256,8,384]{0,2,1:T(8,128)(2,1)S(1)} async-done(((bf16[256,8,384]{0,2,1:T(8,128)(2,1)}), bf16[256,8,384]{0,2,1:T(8,128)(2,1)S(1)}, u32[]{:S(2)}, u32[]{:S(2)}) %all-to-all-start) | async-done | bytes 1572896 | tf_op jit(solution)/shard_map/all_to_all | solution.py:107
  52.8 32.1 %all-to-all-done.1 = bf16[256,8,384]{0,2,1:T(8,128)(2,1)S(1)} async-done(((bf16[256,8,384]{0,2,1:T(8,128)(2,1)}), bf16[256,8,384]{0,2,1:T(8,128)(2,1)S(1)}, u32[]{:S(2)}, u32[]{:S(2)}) %all-to-all-start.1) | async-done | bytes 1572896 | tf_op jit(solution)/shard_map/all_to_all | solution.py:108
  94.2 30.7 %all-to-all-done.2 = bf16[256,8,384]{0,2,1:T(8,128)(2,1)} async-done(((bf16[256,8,384]{0,2,1:T(8,128)(2,1)}), bf16[256,8,384]{0,2,1:T(8,128)(2,1)}, u32[]{:S(2)}, u32[]{:S(2)}) %all-to-all-start.2) | async-done | bytes 1572896 | tf_op jit(solution)/shard_map/all_to_all | solution.py:109
  207.1 931.1 %while.16 = (s32[]{:T(128)}, f32[6,24,128,64]{2,3,1,0:T(8,128)}, f32[6,24,128,64]{2,3,1,0:T(8,128)}, bf16[4,6,4,128,64]{3,4,2,1,0:T(8,128)(2,1)}, bf16[4,6,4,128...) while((s32[]{:T(128)}, f32[6,24,128,64]{2,3,1,0:T(8,128)}, ...), condition=%wide.region_12.13_spmd, body=%wide.region_6.12_spmd.sunk | while | flops 2487296256 | bytes 321751488 | solution.py:93
  209.3 11.8 gather_fusion.1
  221.1 11.8 gather_fusion
  242.0 15.8 %fusion.77 = (f32[6,4,128]{2,1,0:T(4,128)S(1)}, f32[6,4,128,1024]{3,2,1,0:T(8,128)}) fusion(f32[6,4,128,1024]{3,2,1,0:T(8,128)} %fusion.76), kind=kOutput, calls=%fused_computation.71.clone.1 | output fusion | flops 12583935 | bytes 25178112 | tf_op jit(solution)/shard_map/while/body/eval_jaxpr/sub | solution.py:64
  257.8 17.1 %fusion.79 = bf16[4,6,4,128,64]{3,4,2,1,0:T(8,128)(2,1)} fusion(bf16[4,6,4,128,64]{3,4,2,1,0:T(8,128)(2,1)} %get-tuple-element.258, s32[]{:T(128)S(6)} %copy.218, bf16[6,4,1024,64]{3,2,1,0:T(8,128)(2,1)} %bitcast.128, f32[6,4,128]{2,1,0:T(4,128)S(1)} %get-tuple-element.240, f32[6,4,128,1024]{3,2,1,0:T(8,128)} %fusion.76), kind=kOutput, calls=%fused_computation.27.clone.1 | convolution fusion | flops 418582528 | bytes 31862788 | tf_op jit(solution)/shard_map/while/body/eval_jaxpr/hgij,hgjd->hgid/dot_general | solution.py:67
  274.9 16.1 %fusion.78 = f32[6,4,1024,64]{2,3,1,0:T(8,128)} fusion(bf16[1,6,4,128,64]{3,2,0,4,1:T(4,128)(2,1)S(1)} %get-tuple-element.241, f32[6,4,128]{2,1,0:T(4,128)S(1)} %get-tuple-element.240, f32[6,4,128,1024]{3,2,1,0:T(8,128)} %fusion.76), kind=kOutput, calls=%fused_computation.18.clone.1 | convolution fusion | flops 418385920 | bytes 19279872 | tf_op jit(solution)/shard_map/while/body/eval_jaxpr/hgij,hgid->hgjd/dot_general | solution.py:85
  291.0 9.4 copy.207
  317.4 31.7 %scatter_fusion.1 = f32[6,24,128,64]{2,3,1,0:T(8,128)} fusion(f32[6,24,128,64]{2,3,1,0:T(8,128)} %get-tuple-element.257, s32[192]{0:T(256)S(1)} %reshape.216, f32[192,128,64]{1,2,0:T(8,128)} %copy.208), kind=kCustom, calls=%fused_computation.5.clone.1 | custom fusion | flops 1572864 | bytes 18875904 | tf_op jit(solution)/shard_map/while/body/eval_jaxpr/vmap()/scatter-add | solution.py:20
  349.1 11.4 multiply_reduce_fusion.3
  360.4 12.2 multiply_convert_fusion.2
  406.0 31.7 %scatter_fusion = f32[6,24,128,64]{2,3,1,0:T(8,128)} fusion(f32[6,24,128,64]{2,3,1,0:T(8,128)} %get-tuple-element.256, s32[192]{0:T(256)S(1)} %reshape.216, f32[192,128,64]{1,2,0:T(8,128)} %copy.206), kind=kCustom, calls=%fused_computation.4.clone.1 | custom fusion | flops 1572864 | bytes 18875904 | tf_op jit(solution)/shard_map/while/body/eval_jaxpr/vmap()/scatter-add | solution.py:20
  439.6 11.8 gather_fusion.1
  451.4 11.8 gather_fusion
  472.2 15.8 %fusion.77 = (f32[6,4,128]{2,1,0:T(4,128)S(1)}, f32[6,4,128,1024]{3,2,1,0:T(8,128)}) fusion(f32[6,4,128,1024]{3,2,1,0:T(8,128)} %fusion.76), kind=kOutput, calls=%fused_computation.71.clone.1 | output fusion | flops 12583935 | bytes 25178112 | tf_op jit(solution)/shard_map/while/body/eval_jaxpr/sub | solution.py:64
  488.0 17.3 %fusion.79 = bf16[4,6,4,128,64]{3,4,2,1,0:T(8,128)(2,1)} fusion(bf16[4,6,4,128,64]{3,4,2,1,0:T(8,128)(2,1)} %get-tuple-element.258, s32[]{:T(128)S(6)} %copy.218, bf16[6,4,1024,64]{3,2,1,0:T(8,128)(2,1)} %bitcast.128, f32[6,4,128]{2,1,0:T(4,128)S(1)} %get-tuple-element.240, f32[6,4,128,1024]{3,2,1,0:T(8,128)} %fusion.76), kind=kOutput, calls=%fused_computation.27.clone.1 | convolution fusion | flops 418582528 | bytes 31862788 | tf_op jit(solution)/shard_map/while/body/eval_jaxpr/hgij,hgjd->hgid/dot_general | solution.py:67
  505.3 16.1 %fusion.78 = f32[6,4,1024,64]{2,3,1,0:T(8,128)} fusion(bf16[1,6,4,128,64]{3,2,0,4,1:T(4,128)(2,1)S(1)} %get-tuple-element.241, f32[6,4,128]{2,1,0:T(4,128)S(1)} %get-tuple-element.240, f32[6,4,128,1024]{3,2,1,0:T(8,128)} %fusion.76), kind=kOutput, calls=%fused_computation.18.clone.1 | convolution fusion | flops 418385920 | bytes 19279872 | tf_op jit(solution)/shard_map/while/body/eval_jaxpr/hgij,hgid->hgjd/dot_general | solution.py:85
  521.5 9.4 copy.207
  547.8 31.7 %scatter_fusion.1 = f32[6,24,128,64]{2,3,1,0:T(8,128)} fusion(f32[6,24,128,64]{2,3,1,0:T(8,128)} %get-tuple-element.257, s32[192]{0:T(256)S(1)} %reshape.216, f32[192,128,64]{1,2,0:T(8,128)} %copy.208), kind=kCustom, calls=%fused_computation.5.clone.1 | custom fusion | flops 1572864 | bytes 18875904 | tf_op jit(solution)/shard_map/while/body/eval_jaxpr/vmap()/scatter-add | solution.py:20
  579.5 11.4 multiply_reduce_fusion.3
  590.9 12.0 multiply_convert_fusion.2
  636.2 31.6 %scatter_fusion = f32[6,24,128,64]{2,3,1,0:T(8,128)} fusion(f32[6,24,128,64]{2,3,1,0:T(8,128)} %get-tuple-element.256, s32[192]{0:T(256)S(1)} %reshape.216, f32[192,128,64]{1,2,0:T(8,128)} %copy.206), kind=kCustom, calls=%fused_computation.4.clone.1 | custom fusion | flops 1572864 | bytes 18875904 | tf_op jit(solution)/shard_map/while/body/eval_jaxpr/vmap()/scatter-add | solution.py:20
  669.9 11.8 gather_fusion.1
  681.8 11.8 gather_fusion
  702.6 15.8 %fusion.77 = (f32[6,4,128]{2,1,0:T(4,128)S(1)}, f32[6,4,128,1024]{3,2,1,0:T(8,128)}) fusion(f32[6,4,128,1024]{3,2,1,0:T(8,128)} %fusion.76), kind=kOutput, calls=%fused_computation.71.clone.1 | output fusion | flops 12583935 | bytes 25178112 | tf_op jit(solution)/shard_map/while/body/eval_jaxpr/sub | solution.py:64
  718.4 17.1 %fusion.79 = bf16[4,6,4,128,64]{3,4,2,1,0:T(8,128)(2,1)} fusion(bf16[4,6,4,128,64]{3,4,2,1,0:T(8,128)(2,1)} %get-tuple-element.258, s32[]{:T(128)S(6)} %copy.218, bf16[6,4,1024,64]{3,2,1,0:T(8,128)(2,1)} %bitcast.128, f32[6,4,128]{2,1,0:T(4,128)S(1)} %get-tuple-element.240, f32[6,4,128,1024]{3,2,1,0:T(8,128)} %fusion.76), kind=kOutput, calls=%fused_computation.27.clone.1 | convolution fusion | flops 418582528 | bytes 31862788 | tf_op jit(solution)/shard_map/while/body/eval_jaxpr/hgij,hgjd->hgid/dot_general | solution.py:67
  735.5 16.1 %fusion.78 = f32[6,4,1024,64]{2,3,1,0:T(8,128)} fusion(bf16[1,6,4,128,64]{3,2,0,4,1:T(4,128)(2,1)S(1)} %get-tuple-element.241, f32[6,4,128]{2,1,0:T(4,128)S(1)} %get-tuple-element.240, f32[6,4,128,1024]{3,2,1,0:T(8,128)} %fusion.76), kind=kOutput, calls=%fused_computation.18.clone.1 | convolution fusion | flops 418385920 | bytes 19279872 | tf_op jit(solution)/shard_map/while/body/eval_jaxpr/hgij,hgid->hgjd/dot_general | solution.py:85
  751.7 9.4 copy.207
  778.0 31.7 %scatter_fusion.1 = f32[6,24,128,64]{2,3,1,0:T(8,128)} fusion(f32[6,24,128,64]{2,3,1,0:T(8,128)} %get-tuple-element.257, s32[192]{0:T(256)S(1)} %reshape.216, f32[192,128,64]{1,2,0:T(8,128)} %copy.208), kind=kCustom, calls=%fused_computation.5.clone.1 | custom fusion | flops 1572864 | bytes 18875904 | tf_op jit(solution)/shard_map/while/body/eval_jaxpr/vmap()/scatter-add | solution.py:20
  809.7 11.4 multiply_reduce_fusion.3
  821.1 12.2 multiply_convert_fusion.2
  866.6 31.6 %scatter_fusion = f32[6,24,128,64]{2,3,1,0:T(8,128)} fusion(f32[6,24,128,64]{2,3,1,0:T(8,128)} %get-tuple-element.256, s32[192]{0:T(256)S(1)} %reshape.216, f32[192,128,64]{1,2,0:T(8,128)} %copy.206), kind=kCustom, calls=%fused_computation.4.clone.1 | custom fusion | flops 1572864 | bytes 18875904 | tf_op jit(solution)/shard_map/while/body/eval_jaxpr/vmap()/scatter-add | solution.py:20
  900.1 11.8 gather_fusion.1
  911.9 11.8 gather_fusion
  923.7 9.1 fusion.76
  932.8 15.8 %fusion.77 = (f32[6,4,128]{2,1,0:T(4,128)S(1)}, f32[6,4,128,1024]{3,2,1,0:T(8,128)}) fusion(f32[6,4,128,1024]{3,2,1,0:T(8,128)} %fusion.76), kind=kOutput, calls=%fused_computation.71.clone.1 | output fusion | flops 12583935 | bytes 25178112 | tf_op jit(solution)/shard_map/while/body/eval_jaxpr/sub | solution.py:64
  948.6 17.3 %fusion.79 = bf16[4,6,4,128,64]{3,4,2,1,0:T(8,128)(2,1)} fusion(bf16[4,6,4,128,64]{3,4,2,1,0:T(8,128)(2,1)} %get-tuple-element.258, s32[]{:T(128)S(6)} %copy.218, bf16[6,4,1024,64]{3,2,1,0:T(8,128)(2,1)} %bitcast.128, f32[6,4,128]{2,1,0:T(4,128)S(1)} %get-tuple-element.240, f32[6,4,128,1024]{3,2,1,0:T(8,128)} %fusion.76), kind=kOutput, calls=%fused_computation.27.clone.1 | convolution fusion | flops 418582528 | bytes 31862788 | tf_op jit(solution)/shard_map/while/body/eval_jaxpr/hgij,hgjd->hgid/dot_general | solution.py:67
  965.9 16.1 %fusion.78 = f32[6,4,1024,64]{2,3,1,0:T(8,128)} fusion(bf16[1,6,4,128,64]{3,2,0,4,1:T(4,128)(2,1)S(1)} %get-tuple-element.241, f32[6,4,128]{2,1,0:T(4,128)S(1)} %get-tuple-element.240, f32[6,4,128,1024]{3,2,1,0:T(8,128)} %fusion.76), kind=kOutput, calls=%fused_computation.18.clone.1 | convolution fusion | flops 418385920 | bytes 19279872 | tf_op jit(solution)/shard_map/while/body/eval_jaxpr/hgij,hgid->hgjd/dot_general | solution.py:85
  982.0 9.4 copy.207
  1008.4 31.7 %scatter_fusion.1 = f32[6,24,128,64]{2,3,1,0:T(8,128)} fusion(f32[6,24,128,64]{2,3,1,0:T(8,128)} %get-tuple-element.257, s32[192]{0:T(256)S(1)} %reshape.216, f32[192,128,64]{1,2,0:T(8,128)} %copy.208), kind=kCustom, calls=%fused_computation.5.clone.1 | custom fusion | flops 1572864 | bytes 18875904 | tf_op jit(solution)/shard_map/while/body/eval_jaxpr/vmap()/scatter-add | solution.py:20
  1040.1 11.4 multiply_reduce_fusion.3
  1051.5 12.0 multiply_convert_fusion.2
  1096.8 31.7 %scatter_fusion = f32[6,24,128,64]{2,3,1,0:T(8,128)} fusion(f32[6,24,128,64]{2,3,1,0:T(8,128)} %get-tuple-element.256, s32[192]{0:T(256)S(1)} %reshape.216, f32[192,128,64]{1,2,0:T(8,128)} %copy.206), kind=kCustom, calls=%fused_computation.4.clone.1 | custom fusion | flops 1572864 | bytes 18875904 | tf_op jit(solution)/shard_map/while/body/eval_jaxpr/vmap()/scatter-add | solution.py:20
  1165.5 19.9 %all-to-all-done.5 = bf16[8,256,384]{1,2,0:T(8,128)(2,1)S(1)} async-done(((bf16[8,256,384]{1,2,0:T(8,128)(2,1)}), bf16[8,256,384]{1,2,0:T(8,128)(2,1)S(1)}, u32[]{:S(2)}, u32[]{:S(2)}) %all-to-all-start.5) | async-done | bytes 1572896 | tf_op jit(solution)/shard_map/all_to_all | solution.py:151
  1236.5 43.0 %all_to_all.134 = bf16[8,256,384]{2,1,0:T(8,128)(2,1)} all-to-all(bf16[8,256,384]{2,1,0:T(8,128)(2,1)} %bitcast.150), channel_id=1, replica_groups=mesh['slab'=4,'seq'=8] {'seq'}, dimensions={0} | all-to-all | bytes 3145728 | tf_op jit(solution)/shard_map/all_to_all | solution.py:152
  1291.8 28.2 %all-to-all-done.7 = bf16[8,256,384]{2,1,0:T(8,128)(2,1)} async-done(((bf16[8,256,384]{2,1,0:T(8,128)(2,1)}), bf16[8,256,384]{2,1,0:T(8,128)(2,1)}, u32[]{:S(2)}, u32[]{:S(2)}) %all-to-all-start.7) | async-done | bytes 1572896 | tf_op jit(solution)/shard_map/all_to_all | solution.py:153
  (184 shorter events, 439.6 us)
Async XLA Ops:
  0.6 9.0 copy-start.1
  3.3 40.5 %all-to-all-start = ((bf16[256,8,384]{0,2,1:T(8,128)(2,1)}), bf16[256,8,384]{0,2,1:T(8,128)(2,1)S(1)}, u32[]{:S(2)}, u32[]{:S(2)}) async-start(bf16[256,8,384]{0,2,1:T(8,128)(2,1)} %bitcast.8), calls=%async_computation | async-start | bytes 3145728 | tf_op jit(solution)/shard_map/all_to_all | solution.py:107
  43.9 50.4 %copy-start = (bf16[256,8,384]{0,2,1:T(8,128)(2,1)}, bf16[256,8,384]{0,2,1:T(8,128)(2,1)S(1)}, u32[]{:S(2)}) copy-start(bf16[256,8,384]{0,2,1:T(8,128)(2,1)S(1)} %all-to-all-done) | copy-start | bytes 4718596
  43.9 41.1 %all-to-all-start.1 = ((bf16[256,8,384]{0,2,1:T(8,128)(2,1)}), bf16[256,8,384]{0,2,1:T(8,128)(2,1)S(1)}, u32[]{:S(2)}, u32[]{:S(2)}) async-start(bf16[256,8,384]{0,2,1:T(8,128)(2,1)} %bitcast.145), calls=%async_computation.1 | async-start | bytes 3145728 | tf_op jit(solution)/shard_map/all_to_all | solution.py:108
  50.2 82.3 %copy-start.2 = (s32[6,16,8]{1,2,0:T(8,128)S(1)}, s32[6,16,8]{1,2,0:T(8,128)}, u32[]{:S(2)}) copy-start(s32[6,16,8]{1,2,0:T(8,128)} %param.11) | copy-start | bytes 9220
  85.0 40.0 %all-to-all-start.2 = ((bf16[256,8,384]{0,2,1:T(8,128)(2,1)}), bf16[256,8,384]{0,2,1:T(8,128)(2,1)}, u32[]{:S(2)}, u32[]{:S(2)}) async-start(bf16[256,8,384]{0,2,1:T(8,128)(2,1)} %bitcast.146), calls=%async_computation.2 | async-start | bytes 3145728 | tf_op jit(solution)/shard_map/all_to_all | solution.py:109
  125.0 42.8 %all-to-all-start.3 = ((bf16[256,8,384]{0,2,1:T(8,128)(2,1)}), bf16[256,8,384]{0,2,1:T(8,128)(2,1)}, u32[]{:S(2)}, u32[]{:S(2)}) async-start(bf16[256,8,384]{0,2,1:T(8,128)(2,1)} %bitcast.22), calls=%async_computation.3 | async-start | bytes 3145728 | tf_op jit(solution)/shard_map/all_to_all | solution.py:110
  134.2 5.6 collective-permute-start
  136.8 3.8 collective-permute-start.2
  139.8 0.8 copy-start.3
  140.6 0.6 copy-start.5
  154.9 19.9 %collective-permute-start.3 = (bf16[2,4,128,384]{3,2,1,0:T(8,128)(2,1)}, bf16[2,4,128,384]{3,2,1,0:T(8,128)(2,1)}, u32[]{:S(2)}, u32[]{:S(2)}) collective-permute-start(bf16[2,4,128,384]{3,2,1,0:T(8,128)(2,1)} %bitcast.93), channel_id=1, source_target_pairs={{8,0},{16,8},{24,16},{9,1},{17,9},{25,17},{10,2},{18,10},{26,18},{... | collective-permute-start | bytes 2359304 | tf_op jit(solution)/shard_map/ppermute | solution.py:12
  156.2 18.6 %collective-permute-start.1 = (bf16[2,4,128,384]{3,2,0,1:T(8,128)(2,1)}, bf16[2,4,128,384]{3,2,0,1:T(8,128)(2,1)}, u32[]{:S(2)}, u32[]{:S(2)}) collective-permute-start(bf16[2,4,128,384]{3,2,0,1:T(8,128)(2,1)} %bitcast.153), channel_id=1, source_target_pairs={{0,8},{8,16},{16,24},{1,9},{9,17},{17,25},{2,10},{10,18},{18,26},{... | collective-permute-start | bytes 2359304 | tf_op jit(solution)/shard_map/ppermute | solution.py:12
  317.4 55.3 %slice-start = ((s8[6291456]{0:T(1024)(128)(4,1)}), s8[2097152]{0:T(1024)(128)(4,1)S(1)}, s32[]{:S(2)}) async-start(s8[6291456]{0:T(1024)(128)(4,1)} %bitcast.123), calls=%async_computation.8 | async-start | bytes 4194304 | tf_op jit(solution)/shard_map/while
  349.1 23.6 %slice-start.1 = ((s8[6291456]{0:T(1024)(128)(4,1)}), s8[4194304]{0:T(1024)(128)(4,1)S(1)}, s32[]{:S(2)}) async-start(s8[6291456]{0:T(1024)(128)(4,1)} %bitcast.123), calls=%async_computation.9 | async-start | bytes 8388608 | tf_op jit(solution)/shard_map/while
  547.8 55.1 %slice-start = ((s8[6291456]{0:T(1024)(128)(4,1)}), s8[2097152]{0:T(1024)(128)(4,1)S(1)}, s32[]{:S(2)}) async-start(s8[6291456]{0:T(1024)(128)(4,1)} %bitcast.123), calls=%async_computation.8 | async-start | bytes 4194304 | tf_op jit(solution)/shard_map/while
  579.5 23.4 %slice-start.1 = ((s8[6291456]{0:T(1024)(128)(4,1)}), s8[4194304]{0:T(1024)(128)(4,1)S(1)}, s32[]{:S(2)}) async-start(s8[6291456]{0:T(1024)(128)(4,1)} %bitcast.123), calls=%async_computation.9 | async-start | bytes 8388608 | tf_op jit(solution)/shard_map/while
  778.0 55.3 %slice-start = ((s8[6291456]{0:T(1024)(128)(4,1)}), s8[2097152]{0:T(1024)(128)(4,1)S(1)}, s32[]{:S(2)}) async-start(s8[6291456]{0:T(1024)(128)(4,1)} %bitcast.123), calls=%async_computation.8 | async-start | bytes 4194304 | tf_op jit(solution)/shard_map/while
  809.7 23.6 %slice-start.1 = ((s8[6291456]{0:T(1024)(128)(4,1)}), s8[4194304]{0:T(1024)(128)(4,1)S(1)}, s32[]{:S(2)}) async-start(s8[6291456]{0:T(1024)(128)(4,1)} %bitcast.123), calls=%async_computation.9 | async-start | bytes 8388608 | tf_op jit(solution)/shard_map/while
  1008.4 55.1 %slice-start = ((s8[6291456]{0:T(1024)(128)(4,1)}), s8[2097152]{0:T(1024)(128)(4,1)S(1)}, s32[]{:S(2)}) async-start(s8[6291456]{0:T(1024)(128)(4,1)} %bitcast.123), calls=%async_computation.8 | async-start | bytes 4194304 | tf_op jit(solution)/shard_map/while
  1040.1 23.4 %slice-start.1 = ((s8[6291456]{0:T(1024)(128)(4,1)}), s8[4194304]{0:T(1024)(128)(4,1)S(1)}, s32[]{:S(2)}) async-start(s8[6291456]{0:T(1024)(128)(4,1)} %bitcast.123), calls=%async_computation.9 | async-start | bytes 8388608 | tf_op jit(solution)/shard_map/while
  1143.3 42.1 %all-to-all-start.5 = ((bf16[8,256,384]{1,2,0:T(8,128)(2,1)}), bf16[8,256,384]{1,2,0:T(8,128)(2,1)S(1)}, u32[]{:S(2)}, u32[]{:S(2)}) async-start(bf16[8,256,384]{1,2,0:T(8,128)(2,1)} %copy.158), calls=%async_computation.5 | async-start | bytes 3145728 | tf_op jit(solution)/shard_map/all_to_all | solution.py:151
  1154.4 8.3 slice-start.2
  1157.4 5.2 slice-start.3
  1185.4 51.1 %all-to-all-start.4 = ((bf16[8,256,384]{1,2,0:T(8,128)(2,1)}), bf16[8,256,384]{1,2,0:T(8,128)(2,1)S(1)}, u32[]{:S(2)}, u32[]{:S(2)}) async-start(bf16[8,256,384]{1,2,0:T(8,128)(2,1)} %copy.156), calls=%async_computation.4 | async-start | bytes 3145728 | tf_op jit(solution)/shard_map/all_to_all | solution.py:150
  1198.7 13.5 %collective-permute-start.5 = (bf16[2,4,128,384]{2,3,1,0:T(8,128)(2,1)}, bf16[2,4,128,384]{2,3,1,0:T(8,128)(2,1)}, u32[]{:S(2)}, u32[]{:S(2)}) collective-permute-start(bf16[2,4,128,384]{2,3,1,0:T(8,128)(2,1)} %get-tuple-element.155), channel_id=1, source_target_pairs={{0,8},{8,16},{16,24},{1,9},{9,17},{17,25},{2,10},{10,18},{18,26},{... | collective-permute-start | bytes 2359304 | tf_op jit(solution)/shard_map/ppermute | solution.py:12
  1201.3 16.4 %collective-permute-start.4 = (bf16[2,4,128,384]{2,3,1,0:T(8,128)(2,1)}, bf16[2,4,128,384]{2,3,1,0:T(8,128)(2,1)}, u32[]{:S(2)}, u32[]{:S(2)}) collective-permute-start(bf16[2,4,128,384]{2,3,1,0:T(8,128)(2,1)} %get-tuple-element.156), channel_id=1, source_target_pairs={{8,0},{16,8},{24,16},{9,1},{17,9},{25,17},{10,2},{18,10},{26,18},{... | collective-permute-start | bytes 2359304 | tf_op jit(solution)/shard_map/ppermute | solution.py:12
  1212.3 10.8 copy-start.4
  1214.6 12.7 copy-start.6
  1279.5 40.5 %all-to-all-start.7 = ((bf16[8,256,384]{2,1,0:T(8,128)(2,1)}), bf16[8,256,384]{2,1,0:T(8,128)(2,1)}, u32[]{:S(2)}, u32[]{:S(2)}) async-start(bf16[8,256,384]{2,1,0:T(8,128)(2,1)} %bitcast.149), calls=%async_computation.7 | async-start | bytes 3145728 | tf_op jit(solution)/shard_map/all_to_all | solution.py:153
where the time goes:
time: 1340 us; the launch traced here: 1320 us
  local copies, waits for them, and re-layouts  416 us (31%)
  other arithmetic  396 us (30%)
  matrix products  254 us (19%)
  waiting for transfers between devices  144 us (11%)
  starting transfers between devices  58.4 us (4%)
  blocking collectives  43 us (3%)
    scatter-add x12, other arithmetic, add_blocks(): single.at[index_rows].add(terms)  253 us
    gather x8, local copies, waits for them, and re-layouts, pick_blocks(): single[index_rows]  94.4 us
    dot_general x4, matrix products, one_step(): jnp.einsum('hgij,hgjd->hgid', weights_low, value_group, preferred_element...  68.9 us
    reshape x8, local copies, waits for them, and re-layouts, one_step(): key_accum = add_blocks(key_accum, flat_lists, key_terms.reshape(shaped))  67.8 us
    reshape x8, local copies, waits for them, and re-layouts, one_step(): value_terms.reshape(shaped)  67.6 us
    dot_general x4, matrix products, one_step(): jnp.einsum('hgij,hgid->hgjd', weights_low, grad_group, preferred_element_...  64.6 us
    sub x4, other arithmetic, one_step(): weights = jnp.exp(scores - row_max)  63.1 us
    convert_element_type x4, other arithmetic, one_step(): grad_score = (weights * (grad_prob - correction)).astype(jnp.bfloat16)  48.5 us
  transfers between devices with their start and end apart: 13, of which 6 were waited for; matrix products, arithmetic and copies ran while one was open for 7% of the time, Pallas kernels for 0%

commit v1 on v0

v1 whole, which is shorter than its diff:
```python
import functools

import jax
import jax.numpy as jnp
from jax import lax
from jax.experimental import pallas as pl
from jax.experimental.pallas import tpu as pltpu
from jax.sharding import PartitionSpec as P

CROSS = 4
VMEM_LIMIT = 48 * 1024 * 1024


def from_behind(x, axis, by):
    count = lax.axis_size(axis)
    pairs = [(i, i + by) for i in range(count) if 0 <= i + by < count]
    return lax.ppermute(x, axis, pairs)


def pair_halves(left, right, head_dim):
    first = jnp.concatenate([left[:, :head_dim], right[:, :head_dim]], axis=1)
    second = jnp.concatenate([left[:, head_dim:], right[:, head_dim:]], axis=1)
    return first, second


def pack_kernel(query, key, value, d_out, message, *, head_dim):
    for pair in range(message.shape[1] // 2):
        lanes = pl.ds(pair * 2 * head_dim, 2 * head_dim)
        key_value = pair_halves(key[:, lanes], value[:, lanes], head_dim)
        query_grad = pair_halves(query[:, lanes], d_out[:, lanes], head_dim)
        for side in range(2):
            message[0, 2 * pair + side, 0] = key_value[side]
            message[0, 2 * pair + side, 1] = query_grad[side]


def pack(arrays, chunk, chunk_heads, heads_here, peers, head_dim):
    rows = arrays[0].shape[0]
    chunks = heads_here // chunk_heads
    shape = (peers, chunk_heads, 2, rows, 2 * head_dim)
    if chunk_heads % 2:
        low = chunk * chunk_heads
        cut = [
            x.reshape(rows, peers, heads_here, head_dim)[:, :, low : low + chunk_heads]
            for x in arrays
        ]
        query, key, value, d_out = cut
        both = jnp.stack(
            [jnp.concatenate([key, value], -1), jnp.concatenate([query, d_out], -1)]
        )
        return both.transpose(2, 3, 0, 1, 4)
    source = pl.BlockSpec(
        (rows, chunk_heads * head_dim), lambda peer: (0, peer * chunks + chunk)
    )
    return pl.pallas_call(
        functools.partial(pack_kernel, head_dim=head_dim),
        grid=(peers,),
        in_specs=[source] * 4,
        out_specs=pl.BlockSpec((1,) + shape[1:], lambda peer: (peer, 0, 0, 0, 0)),
        out_shape=jax.ShapeDtypeStruct(shape, arrays[0].dtype),
        compiler_params=pltpu.CompilerParams(vmem_limit_bytes=VMEM_LIMIT),
        name="pack",
    )(*arrays)


def unpack_kernel(message, *refs, head_dim):
    attended, grad_query, grad_key, grad_value = refs[-4:]
    for pair in range(message.shape[1] // 2):
        lanes = pl.ds(pair * 2 * head_dim, 2 * head_dim)
        key_grad, value_grad = pair_halves(
            message[0, 2 * pair, 0], message[0, 2 * pair + 1, 0], head_dim
        )
        query_grad, out = pair_halves(
            message[0, 2 * pair, 1], message[0, 2 * pair + 1, 1], head_dim
        )
        attended[:, lanes] = out
        grad_query[:, lanes] = query_grad
        grad_key[:, lanes] = key_grad
        grad_value[:, lanes] = value_grad


def unpack(message, chunk, heads_here, earlier):
    peers, chunk_heads, _, rows, pair_dim = message.shape
    head_dim = pair_dim // 2
    chunks = heads_here // chunk_heads
    columns = peers * heads_here * head_dim
    target = pl.BlockSpec(
        (rows, chunk_heads * head_dim), lambda peer: (0, peer * chunks + chunk)
    )
    return pl.pallas_call(
        functools.partial(unpack_kernel, head_dim=head_dim),
        grid=(peers,),
        in_specs=[pl.BlockSpec((1,) + message.shape[1:], lambda peer: (peer, 0, 0, 0, 0))]
        + [pl.BlockSpec(memory_space=pl.ANY)] * len(earlier),
        out_specs=[target] * 4,
        out_shape=[jax.ShapeDtypeStruct((rows, columns), message.dtype)] * 4,
        input_output_aliases={1 + i: i for i in range(len(earlier))},
        compiler_params=pltpu.CompilerParams(vmem_limit_bytes=VMEM_LIMIT),
        name="unpack",
    )(message, *earlier)


def unpack_all(messages, heads_here):
    if messages[0].shape[1] % 2 == 0:
        outs = ()
        for chunk, message in enumerate(messages):
            outs = unpack(message, chunk, heads_here, outs)
        return tuple(outs)
    whole = jnp.concatenate(messages, axis=1)
    peers, _, _, rows, pair_dim = whole.shape
    head_dim = pair_dim // 2
    parts = whole.reshape(peers, heads_here, 2, rows, 2, head_dim)
    parts = parts.transpose(2, 4, 3, 0, 1, 5).reshape(2, 2, rows, -1)
    return (parts[1, 1], parts[1, 0], parts[0, 0], parts[0, 1])


def pick_kernel(asked, message, picked):
    picked[0] = message[0, :, 0]


def pick(message, asked, block_rows):
    _, chunk_heads, _, rows, lanes = message.shape
    each = rows // block_rows
    return pl.pallas_call(
        pick_kernel,
        grid_spec=pltpu.PrefetchScalarGridSpec(
            num_scalar_prefetch=1,
            grid=(asked.shape[0],),
            in_specs=[
                pl.BlockSpec(
                    (1, chunk_heads, 1, block_rows, lanes),
                    lambda i, ids: (
                        lax.div(ids[i], each),
                        0,
                        0,
                        lax.rem(ids[i], each),
                        0,
                    ),
                )
            ],
            out_specs=pl.BlockSpec(
                (1, chunk_heads, block_rows, lanes), lambda i, ids: (i, 0, 0, 0)
            ),
        ),
        out_shape=jax.ShapeDtypeStruct(
            (asked.shape[0], chunk_heads, block_rows, lanes), message.dtype
        ),
        name="pick",
    )(asked, message)


def attend_kernel(
    lists,
    message,
    came_prev,
    came_next,
    back,
    own,
    to_prev,
    to_next,
    table,
    turned,
    sums,
    *,
    block_rows,
    head_dim,
    per_list,
):
    head = pl.program_id(0)
    peers, _, _, rows, lanes = message.shape
    each = rows // block_rows
    blocks = peers * each
    window = blocks + 2 * CROSS
    scaling = head_dim ** (-0.5)
    for i in range(CROSS):
        table[i] = came_prev[i, 0]
        table[CROSS + blocks + i] = came_next[i, 0]
    for peer in range(peers):
        for i in range(each):
            table[CROSS + peer * each + i] = message[
                peer, 0, 0, i * block_rows : (i + 1) * block_rows
            ]

    def turn(i, carry):
        turned[i] = table[i].T
        sums[i] = jnp.zeros(sums.shape[1:], sums.dtype)
        return carry

    lax.fori_loop(0, window, turn, 0)
    left = lax.broadcasted_iota(jnp.int32, (block_rows, lanes), 1) < head_dim

    def one_block(block, carry):
        ids = [lists[head, block, j] for j in range(per_list)]
        peer = lax.div(block, each)
        start = pl.multiple_of(lax.rem(block, each) * block_rows, block_rows)
        query_grad = message[peer, 0, 1, pl.ds(start, block_rows)]
        nothing = jnp.zeros_like(query_grad)
        apart = jnp.concatenate(
            [jnp.where(left, query_grad, nothing), jnp.where(left, nothing, query_grad)],
            axis=0,
        )
        key_value = jnp.concatenate([table[i] for i in ids], axis=0)
        both = lax.dot_general(
            key_value, apart, (((1,), (1,)), ((), ())), preferred_element_type=jnp.float32
        )
        scores = both[:, :block_rows]
        grad_prob = both[:, block_rows:]
        top = jnp.max(scores, axis=0, keepdims=True)
        weights = jnp.exp((scores - top) * scaling)
        weights = weights * (1.0 / jnp.sum(weights, axis=0, keepdims=True))
        correction = jnp.sum(weights * grad_prob, axis=0, keepdims=True)
        grad_score = weights * (grad_prob - correction)
        low = jnp.concatenate(
            [grad_score.astype(jnp.bfloat16), weights.astype(jnp.bfloat16)], axis=1
        )
        terms = jnp.dot(low, apart, preferred_element_type=jnp.float32)
        for j, i in enumerate(ids):
            sums[i] += terms[j * block_rows : (j + 1) * block_rows]
        key_value_turned = jnp.concatenate([turned[i] for i in ids], axis=1)
        out = jnp.dot(key_value_turned, low, preferred_element_type=jnp.float32)
        out = jnp.concatenate(
            [out[:head_dim, :block_rows] * scaling, out[head_dim:, block_rows:]], axis=0
        )
        back[peer, 0, 0, pl.ds(start, block_rows)] = out.T.astype(back.dtype)
        return carry

    lax.fori_loop(0, blocks, one_block, 0)
    factor = jnp.where(left, scaling, 1.0)
    for i in range(CROSS):
        to_prev[i, 0] = (sums[i] * factor).astype(to_prev.dtype)
        to_next[i, 0] = (sums[CROSS + blocks + i] * factor).astype(to_next.dtype)

    def finish(i, carry):
        own[0, i] = sums[CROSS + i] * factor
        return carry

    lax.fori_loop(0, blocks, finish, 0)


def attend(message, came_prev, came_next, lists, block_rows):
    peers, chunk_heads, _, rows, lanes = message.shape
    per_list = lists.shape[-1]
    blocks = peers * rows // block_rows
    window = blocks + 2 * CROSS
    cross_spec = pl.BlockSpec(
        (CROSS, 1, block_rows, lanes), lambda head, ids: (0, head, 0, 0)
    )
    cross_shape = jax.ShapeDtypeStruct(came_prev.shape, message.dtype)
    return pl.pallas_call(
        functools.partial(
            attend_kernel, block_rows=block_rows, head_dim=lanes // 2, per_list=per_list
        ),
        grid_spec=pltpu.PrefetchScalarGridSpec(
            num_scalar_prefetch=1,
            grid=(chunk_heads,),
            in_specs=[
                pl.BlockSpec(
                    (peers, 1, 2, rows, lanes), lambda head, ids: (0, head, 0, 0, 0)
                ),
                cross_spec,
                cross_spec,
            ],
            out_specs=[
                pl.BlockSpec(
                    (peers, 1, 1, rows, lanes), lambda head, ids: (0, head, 1, 0, 0)
                ),
                pl.BlockSpec(
                    (1, blocks, block_rows, lanes), lambda head, ids: (head, 0, 0, 0)
                ),
                cross_spec,
                cross_spec,
            ],
            scratch_shapes=[
                pltpu.VMEM((window, block_rows, lanes), message.dtype),
                pltpu.VMEM((window, lanes, block_rows), message.dtype),
                pltpu.VMEM((window, block_rows, lanes), jnp.float32),
            ],
        ),
        out_shape=[
            jax.ShapeDtypeStruct(message.shape, message.dtype),
            jax.ShapeDtypeStruct((chunk_heads, blocks, block_rows, lanes), jnp.float32),
            cross_shape,
            cross_shape,
        ],
        compiler_params=pltpu.CompilerParams(vmem_limit_bytes=VMEM_LIMIT),
        name="attend",
    )(lists, message, came_prev, came_next)


def finish_kernel(asked, own, later, earlier, back_in, back, sums, *, block_rows):
    del back_in
    peers, _, _, rows, _ = back.shape
    each = rows // block_rows
    sums[...] = own[0]
    for i in range(CROSS):
        sums[asked[i]] += later[i, 0].astype(jnp.float32)
    for i in range(CROSS):
        sums[asked[CROSS + i]] += earlier[i, 0].astype(jnp.float32)
    for peer in range(peers):
        for i in range(each):
            back[peer, 0, 0, i * block_rows : (i + 1) * block_rows] = sums[
                peer * each + i
            ].astype(back.dtype)


def finish(back, own, later, earlier, asked):
    peers, chunk_heads, _, rows, lanes = back.shape
    _, blocks, block_rows, _ = own.shape
    cross_spec = pl.BlockSpec(
        (CROSS, 1, block_rows, lanes), lambda head, ids: (0, head, 0, 0)
    )
    return pl.pallas_call(
        functools.partial(finish_kernel, block_rows=block_rows),
        grid_spec=pltpu.PrefetchScalarGridSpec(
            num_scalar_prefetch=1,
            grid=(chunk_heads,),
            in_specs=[
                pl.BlockSpec(
                    (1, blocks, block_rows, lanes), lambda head, ids: (head, 0, 0, 0)
                ),
                cross_spec,
                cross_spec,
                pl.BlockSpec(memory_space=pl.ANY),
            ],
            out_specs=pl.BlockSpec(
                (peers, 1, 1, rows, lanes), lambda head, ids: (0, head, 0, 0, 0)
            ),
            scratch_shapes=[pltpu.VMEM((blocks, block_rows, lanes), jnp.float32)],
        ),
        out_shape=jax.ShapeDtypeStruct(back.shape, back.dtype),
        input_output_aliases={4: 0},
        compiler_params=pltpu.CompilerParams(vmem_limit_bytes=VMEM_LIMIT),
        name="finish",
    )(asked, own, later, earlier, back)


def exchange(message):
    return lax.all_to_all(message, "seq", split_axis=0, concat_axis=0, tiled=True)


def local(query, key, value, d_out, pattern):
    heads_here, blocks, _ = pattern.shape
    peers = lax.axis_size("seq")
    rows, columns = query.shape
    head_dim = columns // (peers * heads_here)
    block_rows = rows * peers // blocks
    chunks = 3 if heads_here % 3 == 0 else 1
    chunk_heads = heads_here // chunks
    arrays = (query, key, value, d_out)

    own_base = lax.axis_index("slab") * blocks
    block_ids = jnp.arange(blocks, dtype=jnp.int32)
    flat_lists = pattern.reshape(-1)
    reverse_rank = blocks - 1 - block_ids
    hits_prev = jnp.any(flat_lists[:, None] == (own_base - blocks + block_ids)[None, :], axis=0)
    hits_next = jnp.any(flat_lists[:, None] == (own_base + blocks + block_ids)[None, :], axis=0)
    need_prev = lax.top_k(hits_prev.astype(jnp.int32) * blocks + reverse_rank, CROSS)[1]
    need_next = lax.top_k(hits_next.astype(jnp.int32) * blocks + reverse_rank, CROSS)[1]
    asked_next = from_behind(need_prev, "slab", -1)
    asked_prev = from_behind(need_next, "slab", 1)
    asked = jnp.concatenate([asked_next, asked_prev])
    rank_ids = jnp.arange(CROSS, dtype=jnp.int32)
    prev_global = own_base - blocks + need_prev
    next_global = own_base + blocks + need_next
    pos_prev = jnp.sum(jnp.where(pattern[..., None] == prev_global, rank_ids, 0), axis=-1)
    pos_next = jnp.sum(jnp.where(pattern[..., None] == next_global, rank_ids, 0), axis=-1)
    in_own = (pattern >= own_base) & (pattern < own_base + blocks)
    local_ids = jnp.where(
        in_own,
        CROSS + pattern - own_base,
        jnp.where(pattern < own_base, pos_prev, CROSS + blocks + pos_next),
    )

    came = [
        exchange(pack(arrays, chunk, chunk_heads, heads_here, peers, head_dim))
        for chunk in range(chunks)
    ]
    sent = []
    for chunk in range(chunks):
        picked = pick(came[chunk], asked, block_rows)
        came_prev = from_behind(picked[:CROSS], "slab", 1)
        came_next = from_behind(picked[CROSS:], "slab", -1)
        lists = local_ids[chunk * chunk_heads : (chunk + 1) * chunk_heads]
        back, own, to_prev, to_next = attend(
            came[chunk], came_prev, came_next, lists, block_rows
        )
        later = from_behind(to_prev, "slab", -1)
        earlier = from_behind(to_next, "slab", 1)
        sent.append(exchange(finish(back, own, later, earlier, asked)))
    return unpack_all(sent, heads_here)


def solution(mesh):
    tokens = P(("slab", "seq"), None)
    return jax.shard_map(
        local,
        mesh=mesh,
        in_specs=(tokens, tokens, tokens, tokens, P("seq", "slab", None)),
        out_specs=(tokens, tokens, tokens, tokens),
        check_vma=False,
    )
```

time: 1340 us -> 422 us (0.31)
  local copies, waits for them, and re-layouts: 416 us -> 15.9 us
  other arithmetic: 396 us -> 3.4 us
  matrix products: 254 us -> 0 us
  Pallas kernels: 0 us -> 176 us
  blocking collectives: 43 us -> 0 us
  starting transfers between devices: 58.4 us -> 86.3 us
    scatter-add x14 -> x0, other arithmetic: 262 us -> none  [the longest x12 253 us: add_blocks(): single.at[index_rows].add(terms)]
    dot_general x24 -> x0, matrix products: 254 us -> none  [the longest x4 68.9 us: one_step(): jnp.einsum('hgij,hgjd->hgid', weights_low, value_group, preferred_element...]
    pallas_call x0 -> x15, Pallas kernels: none -> 176 us  [the longest x3 126 us: attend(): pl.pallas_call(functools.partial(attend_kernel, block_rows=block_rows, he...]
    reshape x22 -> x0, local copies, waits for them, and re-layouts: 143 us -> none  [the longest x8 67.8 us: one_step(): key_accum = add_blocks(key_accum, flat_lists, key_terms.reshape(shaped))]
    gather x11 -> x0, local copies, waits for them, and re-layouts: 103 us -> none  [the longest x8 94.4 us: pick_blocks(): single[index_rows]]
    sub x4 -> x0, other arithmetic: 63.1 us -> none  [one_step(): weights = jnp.exp(scores - row_max)]
    convert_element_type x6 -> x0, other arithmetic: 53.3 us -> none  [the longest x4 48.5 us: one_step(): grad_score = (weights * (grad_prob - correction)).astype(jnp.bfloat16)]
    all_to_all x1 -> x0, blocking collectives: 43 us -> none  [local(): lax.all_to_all(grad_key, 'seq', split_axis=0, concat_axis=1, tiled=True)]
  transfers between devices with their start and end apart: 13 -> 20, of which waited for: 6 -> 10; matrix products, arithmetic and copies ran while one was open for 7% -> 2% of each run, Pallas kernels for 0% -> 40%
where the time goes in v1:
time: 422 us; the launch traced here: 414 us
  Pallas kernels  176 us (42%)
  waiting for transfers between devices  131 us (31%)
  starting transfers between devices  86.3 us (20%)
  local copies, waits for them, and re-layouts  15.9 us (4%)
    pallas_call x3, Pallas kernels, attend(): pl.pallas_call(functools.partial(attend_kernel, block_rows=block_rows, he...  126 us
    all_to_all x6, waiting for transfers between devices, exchange(): lax.all_to_all(message, 'seq', split_axis=0, concat_axis=0, tiled=True)  113 us
    ppermute x14, starting transfers between devices, from_behind(): return lax.ppermute(x, axis, pairs)  48.6 us
    all_to_all x6, starting transfers between devices, exchange(): lax.all_to_all(message, 'seq', split_axis=0, concat_axis=0, tiled=True)  37.6 us
    ppermute x14, waiting for transfers between devices, from_behind(): return lax.ppermute(x, axis, pairs)  17.9 us
    pallas_call x3, Pallas kernels, pack(): pl.pallas_call(functools.partial(pack_kernel, head_dim=head_dim), grid=(p...  17 us
    pallas_call x3, Pallas kernels, unpack(): pl.pallas_call(functools.partial(unpack_kernel, head_dim=head_dim), grid=...  15.4 us
    pallas_call x3, Pallas kernels, pick(): pl.pallas_call(pick_kernel, grid_spec=pltpu.PrefetchScalarGridSpec(num_sc...  14.7 us
  transfers between devices with their start and end apart: 20, of which 10 were waited for; matrix products, arithmetic and copies ran while one was open for 2% of the time, Pallas kernels for 40%

profile of v1, /device:TPU:8, one launch (start us, length us, event | category | flops | bytes accessed | tf_op | source)
XLA Modules:
  0.0 414.0 jit_solution(9592860084979747975)
XLA Ops:
  0.6 1.4 copy-done
  2.0 1.4 copy-done.2
  3.5 1.4 copy-done.4
  4.9 5.6 %pack.5 = bf16[8,2,2,256,128]{4,3,2,1,0:T(8,128)(2,1)} custom-call(bf16[256,3072]{1,0:T(8,128)(2,1)S(1)} %copy-done, bf16[256,3072]{1,0:T(8,128)(2,1)S(1)} %copy-done.2, bf16[256,3072]{1,0:T(8,128)(2,1)S(1)} %copy-done.4, bf16[256,3072]{1,0:T(8,128)(2,1)} %d_out.5), custom_call_target="tpu_custom_call" | custom-call | tf_op jit(solution)/shard_map/pack/pallas_call | solution.py:54
  10.5 6.5 %all-to-all-start.4 = ((bf16[8,2,2,256,128]{4,3,2,1,0:T(8,128)(2,1)}), bf16[8,2,2,256,128]{4,3,2,1,0:T(8,128)(2,1)}, u32[]{:S(2)}, u32[]{:S(2)}) async-start(bf16[8,2,2,256,128]{4,3,2,1,0:T(8,128)(2,1)} %pack.5), calls=%async_computation.4 | async-start | bytes 4194304 | tf_op jit(solution)/shard_map/all_to_all | solution.py:337
  17.0 1.4 copy-done.5
  18.4 5.7 %pack.4 = bf16[8,2,2,256,128]{4,3,2,1,0:T(8,128)(2,1)} custom-call(bf16[256,3072]{1,0:T(8,128)(2,1)S(1)} %copy-done.1, bf16[256,3072]{1,0:T(8,128)(2,1)S(1)} %copy-done.3, bf16[256,3072]{1,0:T(8,128)(2,1)S(1)} %copy-done.5, bf16[256,3072]{1,0:T(8,128)(2,1)} %d_out.5), custom_call_target="tpu_custom_call" | custom-call | tf_op jit(solution)/shard_map/pack/pallas_call | solution.py:54
  24.1 38.7 %all-to-all-done.4.message = bf16[8,2,2,256,128]{4,3,2,1,0:T(8,128)(2,1)} async-done(((bf16[8,2,2,256,128]{4,3,2,1,0:T(8,128)(2,1)}), bf16[8,2,2,256,128]{4,3,2,1,0:T(8,128)(2,1)}, u32[]{:S(2)}, u32[]{:S(2)}) %all-to-all-start.4) | async-done | bytes 2097184 | tf_op jit(solution)/shard_map/all_to_all | solution.py:337
  62.8 6.8 %all-to-all-start.2 = ((bf16[8,2,2,256,128]{4,3,2,1,0:T(8,128)(2,1)}), bf16[8,2,2,256,128]{4,3,2,1,0:T(8,128)(2,1)}, u32[]{:S(2)}, u32[]{:S(2)}) async-start(bf16[8,2,2,256,128]{4,3,2,1,0:T(8,128)(2,1)} %pack.4), calls=%async_computation.2 | async-start | bytes 4194304 | tf_op jit(solution)/shard_map/all_to_all | solution.py:337
  69.6 1.4 copy-done.6
  71.0 5.7 %pack.3 = bf16[8,2,2,256,128]{4,3,2,1,0:T(8,128)(2,1)} custom-call(bf16[256,3072]{1,0:T(8,128)(2,1)S(1)} %copy-done.1, bf16[256,3072]{1,0:T(8,128)(2,1)S(1)} %copy-done.3, bf16[256,3072]{1,0:T(8,128)(2,1)S(1)} %copy-done.6, bf16[256,3072]{1,0:T(8,128)(2,1)} %d_out.5), custom_call_target="tpu_custom_call" | custom-call | tf_op jit(solution)/shard_map/pack/pallas_call | solution.py:54
  76.6 38.2 %all-to-all-done.2.message = bf16[8,2,2,256,128]{4,3,2,1,0:T(8,128)(2,1)} async-done(((bf16[8,2,2,256,128]{4,3,2,1,0:T(8,128)(2,1)}), bf16[8,2,2,256,128]{4,3,2,1,0:T(8,128)(2,1)}, u32[]{:S(2)}, u32[]{:S(2)}) %all-to-all-start.2) | async-done | bytes 2097184 | tf_op jit(solution)/shard_map/all_to_all | solution.py:337
  114.9 6.3 %all-to-all-start = ((bf16[8,2,2,256,128]{4,3,2,1,0:T(8,128)(2,1)}), bf16[8,2,2,256,128]{4,3,2,1,0:T(8,128)(2,1)S(1)}, u32[]{:S(2)}, u32[]{:S(2)}) async-start(bf16[8,2,2,256,128]{4,3,2,1,0:T(8,128)(2,1)} %pack.3), calls=%async_computation | async-start | bytes 4194304 | tf_op jit(solution)/shard_map/all_to_all | solution.py:337
  122.8 1.3 collective-permute-start.1
  125.4 1.3 collective-permute-start
  127.0 3.2 collective-permute-done
  130.7 4.9 %pick.5 = bf16[8,2,128,128]{3,2,1,0:T(8,128)(2,1)} custom-call(s32[8]{0:T(128)} %pad_add_fusion.asked, bf16[8,2,2,256,128]{4,3,2,1,0:T(8,128)(2,1)} %all-to-all-done.4.message), custom_call_target="tpu_custom_call" | custom-call | tf_op jit(solution)/shard_map/pick/pallas_call | solution.py:123
  136.7 5.1 %collective-permute-start.10 = (bf16[4,2,128,128]{3,2,1,0:T(8,128)(2,1)S(1)}, bf16[4,2,128,128]{3,2,1,0:T(8,128)(2,1)S(1)}, u32[]{:S(2)}, u32[]{:S(2)}) collective-permute-start(bf16[4,2,128,128]{3,2,1,0:T(8,128)(2,1)S(1)} %get-tuple-element.57), channel_id=1, source_target_pairs={{0,8},{8,16},{16,24},{1,9},{9,17},{17,25},{2,10},{10,18},{18,26},{... | collective-permute-start | bytes 786440 | tf_op jit(solution)/shard_map/ppermute | solution.py:17
  141.8 1.3 collective-permute-start.11
  143.1 2.1 collective-permute-done.11.came_next
  145.2 42.1 %attend.5 = (bf16[8,2,2,256,128]{4,3,2,1,0:T(8,128)(2,1)S(1)}, f32[2,16,128,128]{3,2,1,0:T(8,128)S(1)}, bf16[4,2,128,128]{3,2,1,0:T(8,128)(2,1)S(1)}, bf16[4,2,128,128]{3,2,1,0:T(8,128)(2,1)S(1)}) custom-call(s32[2,16,8]{2,1,0:T(8,128)S(1)} %get-tuple-element.62.lists, bf16[8,2,2,256,128]{4,3,2,1,0:T(8,128)(2,1)} %all-to-all-done.4.message, ...), custom_call_target="tpu_custom_call" | custom-call | tf_op jit(solution)/shard_map/attend/pallas_call | solution.py:248
  187.3 1.3 collective-permute-start.12
  188.6 7.1 %collective-permute-start.13 = (bf16[4,2,128,128]{3,2,1,0:T(8,128)(2,1)S(1)}, bf16[4,2,128,128]{3,2,1,0:T(8,128)(2,1)S(1)}, u32[]{:S(2)}, u32[]{:S(2)}) collective-permute-start(bf16[4,2,128,128]{3,2,1,0:T(8,128)(2,1)S(1)} %get-tuple-element.42), channel_id=1, source_target_pairs={{0,8},{8,16},{16,24},{1,9},{9,17},{17,25},{2,10},{10,18},{18,26},{... | collective-permute-start | bytes 786440 | tf_op jit(solution)/shard_map/ppermute | solution.py:17
  197.9 1.4 copy-done.8
  199.3 1.3 copy-done.13
  200.6 6.0 %all-to-all-start.5 = ((bf16[8,2,2,256,128]{4,3,2,1,0:T(8,128)(2,1)}), bf16[8,2,2,256,128]{4,3,2,1,0:T(8,128)(2,1)S(1)}, u32[]{:S(2)}, u32[]{:S(2)}) async-start(bf16[8,2,2,256,128]{4,3,2,1,0:T(8,128)(2,1)} %copy-done.8), calls=%async_computation.5 | async-start | bytes 4194304 | tf_op jit(solution)/shard_map/all_to_all | solution.py:337
  206.6 4.9 %pick.4 = bf16[8,2,128,128]{3,2,1,0:T(8,128)(2,1)} custom-call(s32[8]{0:T(128)} %pad_add_fusion.asked, bf16[8,2,2,256,128]{4,3,2,1,0:T(8,128)(2,1)} %all-to-all-done.2.message), custom_call_target="tpu_custom_call" | custom-call | tf_op jit(solution)/shard_map/pick/pallas_call | solution.py:123
  212.6 5.7 %collective-permute-start.6 = (bf16[4,2,128,128]{3,2,1,0:T(8,128)(2,1)S(1)}, bf16[4,2,128,128]{3,2,1,0:T(8,128)(2,1)S(1)}, u32[]{:S(2)}, u32[]{:S(2)}) collective-permute-start(bf16[4,2,128,128]{3,2,1,0:T(8,128)(2,1)S(1)} %get-tuple-element.59), channel_id=1, source_target_pairs={{0,8},{8,16},{16,24},{1,9},{9,17},{17,25},{2,10},{10,18},{18,26},{... | collective-permute-start | bytes 786440 | tf_op jit(solution)/shard_map/ppermute | solution.py:17
  218.4 1.3 collective-permute-start.7
  219.7 4.7 %collective-permute-done.7.came_next = bf16[4,2,128,128]{3,2,1,0:T(8,128)(2,1)S(1)} collective-permute-done((bf16[4,2,128,128]{3,2,1,0:T(8,128)(2,1)S(1)}, bf16[4,2,128,128]{3,2,1,0:T(8,128)(2,1)S(1)}, u32[]{:S(2)}, u32[]{:S(2)}) %collective-permute-start.7) | collective-permute-done | bytes 262176 | tf_op jit(solution)/shard_map/ppermute | solution.py:17
  224.3 42.1 %attend.4 = (bf16[8,2,2,256,128]{4,3,2,1,0:T(8,128)(2,1)S(1)}, f32[2,16,128,128]{3,2,1,0:T(8,128)S(1)}, bf16[4,2,128,128]{3,2,1,0:T(8,128)(2,1)S(1)}, bf16[4,2,128,128]{3,2,1,0:T(8,128)(2,1)S(1)}) custom-call(s32[2,16,8]{2,1,0:T(8,128)S(1)} %get-tuple-element.63.lists, bf16[8,2,2,256,128]{4,3,2,1,0:T(8,128)(2,1)} %all-to-all-done.2.message, ...), custom_call_target="tpu_custom_call" | custom-call | tf_op jit(solution)/shard_map/attend/pallas_call | solution.py:248
  266.4 1.3 collective-permute-start.8
  267.7 7.3 %collective-permute-start.9 = (bf16[4,2,128,128]{3,2,1,0:T(8,128)(2,1)S(1)}, bf16[4,2,128,128]{3,2,1,0:T(8,128)(2,1)S(1)}, u32[]{:S(2)}, u32[]{:S(2)}) collective-permute-start(bf16[4,2,128,128]{3,2,1,0:T(8,128)(2,1)S(1)} %get-tuple-element.38), channel_id=1, source_target_pairs={{0,8},{8,16},{16,24},{1,9},{9,17},{17,25},{2,10},{10,18},{18,26},{... | collective-permute-start | bytes 786440 | tf_op jit(solution)/shard_map/ppermute | solution.py:17
  277.2 1.3 copy-done.9
  278.6 6.0 %all-to-all-start.3 = ((bf16[8,2,2,256,128]{4,3,2,1,0:T(8,128)(2,1)}), bf16[8,2,2,256,128]{4,3,2,1,0:T(8,128)(2,1)}, u32[]{:S(2)}, u32[]{:S(2)}) async-start(bf16[8,2,2,256,128]{4,3,2,1,0:T(8,128)(2,1)} %copy-done.9), calls=%async_computation.3 | async-start | bytes 4194304 | tf_op jit(solution)/shard_map/all_to_all | solution.py:337
  284.6 4.9 %pick.3 = bf16[8,2,128,128]{3,2,1,0:T(8,128)(2,1)} custom-call(s32[8]{0:T(128)} %pad_add_fusion.asked, bf16[8,2,2,256,128]{4,3,2,1,0:T(8,128)(2,1)} %copy-done.13), custom_call_target="tpu_custom_call" | custom-call | tf_op jit(solution)/shard_map/pick/pallas_call | solution.py:123
  290.6 5.7 %collective-permute-start.2 = (bf16[4,2,128,128]{3,2,1,0:T(8,128)(2,1)S(1)}, bf16[4,2,128,128]{3,2,1,0:T(8,128)(2,1)S(1)}, u32[]{:S(2)}, u32[]{:S(2)}) collective-permute-start(bf16[4,2,128,128]{3,2,1,0:T(8,128)(2,1)S(1)} %get-tuple-element.61), channel_id=1, source_target_pairs={{0,8},{8,16},{16,24},{1,9},{9,17},{17,25},{2,10},{10,18},{18,26},{... | collective-permute-start | bytes 786440 | tf_op jit(solution)/shard_map/ppermute | solution.py:17
  296.3 1.3 collective-permute-start.3
  297.7 4.7 %collective-permute-done.3.came_next = bf16[4,2,128,128]{3,2,1,0:T(8,128)(2,1)S(1)} collective-permute-done((bf16[4,2,128,128]{3,2,1,0:T(8,128)(2,1)S(1)}, bf16[4,2,128,128]{3,2,1,0:T(8,128)(2,1)S(1)}, u32[]{:S(2)}, u32[]{:S(2)}) %collective-permute-start.3) | collective-permute-done | bytes 262176 | tf_op jit(solution)/shard_map/ppermute | solution.py:17
  302.3 42.1 %attend.3 = (bf16[8,2,2,256,128]{4,3,2,1,0:T(8,128)(2,1)S(1)}, f32[2,16,128,128]{3,2,1,0:T(8,128)S(1)}, bf16[4,2,128,128]{3,2,1,0:T(8,128)(2,1)S(1)}, bf16[4,2,128,128]{3,2,1,0:T(8,128)(2,1)S(1)}) custom-call(s32[2,16,8]{2,1,0:T(8,128)S(1)} %get-tuple-element.64.lists, bf16[8,2,2,256,128]{4,3,2,1,0:T(8,128)(2,1)} %copy-done.13, ...), custom_call_target="tpu_custom_call" | custom-call | tf_op jit(solution)/shard_map/attend/pallas_call | solution.py:248
  344.4 1.3 collective-permute-start.4
  345.7 7.3 %collective-permute-start.5 = (bf16[4,2,128,128]{3,2,1,0:T(8,128)(2,1)S(1)}, bf16[4,2,128,128]{3,2,1,0:T(8,128)(2,1)S(1)}, u32[]{:S(2)}, u32[]{:S(2)}) collective-permute-start(bf16[4,2,128,128]{3,2,1,0:T(8,128)(2,1)S(1)} %get-tuple-element.34), channel_id=1, source_target_pairs={{0,8},{8,16},{16,24},{1,9},{9,17},{17,25},{2,10},{10,18},{18,26},{... | collective-permute-start | bytes 786440 | tf_op jit(solution)/shard_map/ppermute | solution.py:17
  355.2 1.3 copy-done.7
  356.5 6.0 %all-to-all-start.1 = ((bf16[8,2,2,256,128]{4,3,2,1,0:T(8,128)(2,1)}), bf16[8,2,2,256,128]{4,3,2,1,0:T(8,128)(2,1)}, u32[]{:S(2)}, u32[]{:S(2)}) async-start(bf16[8,2,2,256,128]{4,3,2,1,0:T(8,128)(2,1)} %copy-done.7), calls=%async_computation.1 | async-start | bytes 4194304 | tf_op jit(solution)/shard_map/all_to_all | solution.py:337
  362.5 3.4 unpack.3
  365.9 6.0 %unpack.4 = (bf16[256,3072]{1,0:T(8,128)(2,1)}, bf16[256,3072]{1,0:T(8,128)(2,1)}, bf16[256,3072]{1,0:T(8,128)(2,1)}, bf16[256,3072]{1,0:T(8,128)(2,1)}) custom-call(bf16[8,2,2,256,128]{4,3,2,1,0:T(8,128)(2,1)} %all-to-all-done.3.message, ...), custom_call_target="tpu_custom_call", output_to_operand_aliasing={{0}: (1, {}), {1}: (2, {}), {2}: (3, {}), {3}: (4, {})} | custom-call | tf_op jit(solution)/shard_map/unpack/pallas_call | solution.py:89
  371.9 36.1 %all-to-all-done.1.message = bf16[8,2,2,256,128]{4,3,2,1,0:T(8,128)(2,1)} async-done(((bf16[8,2,2,256,128]{4,3,2,1,0:T(8,128)(2,1)}), bf16[8,2,2,256,128]{4,3,2,1,0:T(8,128)(2,1)}, u32[]{:S(2)}, u32[]{:S(2)}) %all-to-all-start.1) | async-done | bytes 2097184 | tf_op jit(solution)/shard_map/all_to_all | solution.py:337
  408.0 6.0 %unpack.5 = (bf16[256,3072]{1,0:T(8,128)(2,1)}, bf16[256,3072]{1,0:T(8,128)(2,1)}, bf16[256,3072]{1,0:T(8,128)(2,1)}, bf16[256,3072]{1,0:T(8,128)(2,1)}) custom-call(bf16[8,2,2,256,128]{4,3,2,1,0:T(8,128)(2,1)} %all-to-all-done.1.message, ...), custom_call_target="tpu_custom_call", output_to_operand_aliasing={{0}: (1, {}), {1}: (2, {}), {2}: (3, {}), {3}: (4, {})} | custom-call | tf_op jit(solution)/shard_map/unpack/pallas_call | solution.py:89
  (58 shorter events, 13.7 us)
Async XLA Ops:
  0.6 1.4 copy-start
  2.0 1.4 copy-start.2
  3.4 1.4 copy-start.4
  10.5 6.5 %copy-start.1 = (bf16[256,3072]{1,0:T(8,128)(2,1)S(1)}, bf16[256,3072]{1,0:T(8,128)(2,1)}, u32[]{:S(2)}) copy-start(bf16[256,3072]{1,0:T(8,128)(2,1)} %query.5) | copy-start | bytes 4718596
  10.5 6.5 %copy-start.3 = (bf16[256,3072]{1,0:T(8,128)(2,1)S(1)}, bf16[256,3072]{1,0:T(8,128)(2,1)}, u32[]{:S(2)}) copy-start(bf16[256,3072]{1,0:T(8,128)(2,1)} %key.5) | copy-start | bytes 4718596
  10.5 52.3 %all-to-all-start.4 = ((bf16[8,2,2,256,128]{4,3,2,1,0:T(8,128)(2,1)}), bf16[8,2,2,256,128]{4,3,2,1,0:T(8,128)(2,1)}, u32[]{:S(2)}, u32[]{:S(2)}) async-start(bf16[8,2,2,256,128]{4,3,2,1,0:T(8,128)(2,1)} %pack.5), calls=%async_computation.4 | async-start | bytes 4194304 | tf_op jit(solution)/shard_map/all_to_all | solution.py:337
  17.0 1.4 copy-start.5
  62.8 52.1 %all-to-all-start.2 = ((bf16[8,2,2,256,128]{4,3,2,1,0:T(8,128)(2,1)}), bf16[8,2,2,256,128]{4,3,2,1,0:T(8,128)(2,1)}, u32[]{:S(2)}, u32[]{:S(2)}) async-start(bf16[8,2,2,256,128]{4,3,2,1,0:T(8,128)(2,1)} %pack.4), calls=%async_computation.2 | async-start | bytes 4194304 | tf_op jit(solution)/shard_map/all_to_all | solution.py:337
  69.6 1.4 copy-start.6
  76.6 44.5 %copy-start.14 = (s32[6,16,8]{1,2,0:T(8,128)S(1)}, s32[6,16,8]{1,2,0:T(8,128)}, u32[]{:S(2)}) copy-start(s32[6,16,8]{1,2,0:T(8,128)} %param.9) | copy-start | bytes 9220
  114.9 84.5 %all-to-all-start = ((bf16[8,2,2,256,128]{4,3,2,1,0:T(8,128)(2,1)}), bf16[8,2,2,256,128]{4,3,2,1,0:T(8,128)(2,1)S(1)}, u32[]{:S(2)}, u32[]{:S(2)}) async-start(bf16[8,2,2,256,128]{4,3,2,1,0:T(8,128)(2,1)} %pack.3), calls=%async_computation | async-start | bytes 4194304 | tf_op jit(solution)/shard_map/all_to_all | solution.py:337
  122.8 4.1 %collective-permute-start.1 = (s32[4]{0:T(128)S(1)}, s32[4]{0:T(128)S(1)}, u32[]{:S(2)}, u32[]{:S(2)}) collective-permute-start(s32[4]{0:T(128)S(1)} %get-tuple-element.68), channel_id=1, source_target_pairs={{0,8},{8,16},{16,24},{1,9},{9,17},{17,25},{2,10},{10,18},{18,26},{... | collective-permute-start | bytes 56 | tf_op jit(solution)/shard_map/ppermute | solution.py:17
  125.4 4.7 %collective-permute-start = (s32[4]{0:T(128)S(1)}, s32[4]{0:T(128)S(1)}, u32[]{:S(2)}, u32[]{:S(2)}) collective-permute-start(s32[4]{0:T(128)S(1)} %get-tuple-element.66), channel_id=1, source_target_pairs={{8,0},{16,8},{24,16},{9,1},{17,9},{25,17},{10,2},{18,10},{26,18},{... | collective-permute-start | bytes 56 | tf_op jit(solution)/shard_map/ppermute | solution.py:17
  135.6 61.2 %copy-start.10 = (s32[8]{0:T(128)S(1)}, s32[8]{0:T(128)}, u32[]{:S(2)}) copy-start(s32[8]{0:T(128)} %pad_add_fusion.asked) | copy-start | bytes 100
  136.7 6.4 %collective-permute-start.10 = (bf16[4,2,128,128]{3,2,1,0:T(8,128)(2,1)S(1)}, bf16[4,2,128,128]{3,2,1,0:T(8,128)(2,1)S(1)}, u32[]{:S(2)}, u32[]{:S(2)}) collective-permute-start(bf16[4,2,128,128]{3,2,1,0:T(8,128)(2,1)S(1)} %get-tuple-element.57), channel_id=1, source_target_pairs={{0,8},{8,16},{16,24},{1,9},{9,17},{17,25},{2,10},{10,18},{18,26},{... | collective-permute-start | bytes 786440 | tf_op jit(solution)/shard_map/ppermute | solution.py:17
  141.8 3.4 collective-permute-start.11
  187.3 8.4 %collective-permute-start.12 = (bf16[4,2,128,128]{3,2,1,0:T(8,128)(2,1)S(1)}, bf16[4,2,128,128]{3,2,1,0:T(8,128)(2,1)S(1)}, u32[]{:S(2)}, u32[]{:S(2)}) collective-permute-start(bf16[4,2,128,128]{3,2,1,0:T(8,128)(2,1)S(1)} %get-tuple-element.41), channel_id=1, source_target_pairs={{8,0},{16,8},{24,16},{9,1},{17,9},{25,17},{10,2},{18,10},{26,18},{... | collective-permute-start | bytes 786440 | tf_op jit(solution)/shard_map/ppermute | solution.py:17
  188.6 8.2 %collective-permute-start.13 = (bf16[4,2,128,128]{3,2,1,0:T(8,128)(2,1)S(1)}, bf16[4,2,128,128]{3,2,1,0:T(8,128)(2,1)S(1)}, u32[]{:S(2)}, u32[]{:S(2)}) collective-permute-start(bf16[4,2,128,128]{3,2,1,0:T(8,128)(2,1)S(1)} %get-tuple-element.42), channel_id=1, source_target_pairs={{0,8},{8,16},{16,24},{1,9},{9,17},{17,25},{2,10},{10,18},{18,26},{... | collective-permute-start | bytes 786440 | tf_op jit(solution)/shard_map/ppermute | solution.py:17
  197.9 1.4 copy-start.8
  199.3 1.3 copy-start.13
  200.6 78.0 %all-to-all-start.5 = ((bf16[8,2,2,256,128]{4,3,2,1,0:T(8,128)(2,1)}), bf16[8,2,2,256,128]{4,3,2,1,0:T(8,128)(2,1)S(1)}, u32[]{:S(2)}, u32[]{:S(2)}) async-start(bf16[8,2,2,256,128]{4,3,2,1,0:T(8,128)(2,1)} %copy-done.8), calls=%async_computation.5 | async-start | bytes 4194304 | tf_op jit(solution)/shard_map/all_to_all | solution.py:337
  211.5 64.6 %copy-start.11 = (s32[8]{0:T(128)S(1)}, s32[8]{0:T(128)}, u32[]{:S(2)}) copy-start(s32[8]{0:T(128)} %pad_add_fusion.asked) | copy-start | bytes 100
  212.6 7.1 %collective-permute-start.6 = (bf16[4,2,128,128]{3,2,1,0:T(8,128)(2,1)S(1)}, bf16[4,2,128,128]{3,2,1,0:T(8,128)(2,1)S(1)}, u32[]{:S(2)}, u32[]{:S(2)}) collective-permute-start(bf16[4,2,128,128]{3,2,1,0:T(8,128)(2,1)S(1)} %get-tuple-element.59), channel_id=1, source_target_pairs={{0,8},{8,16},{16,24},{1,9},{9,17},{17,25},{2,10},{10,18},{18,26},{... | collective-permute-start | bytes 786440 | tf_op jit(solution)/shard_map/ppermute | solution.py:17
  218.4 6.0 %collective-permute-start.7 = (bf16[4,2,128,128]{3,2,1,0:T(8,128)(2,1)S(1)}, bf16[4,2,128,128]{3,2,1,0:T(8,128)(2,1)S(1)}, u32[]{:S(2)}, u32[]{:S(2)}) collective-permute-start(bf16[4,2,128,128]{3,2,1,0:T(8,128)(2,1)S(1)} %get-tuple-element.58), channel_id=1, source_target_pairs={{8,0},{16,8},{24,16},{9,1},{17,9},{25,17},{10,2},{18,10},{26,18},{... | collective-permute-start | bytes 786440 | tf_op jit(solution)/shard_map/ppermute | solution.py:17
  266.4 8.6 %collective-permute-start.8 = (bf16[4,2,128,128]{3,2,1,0:T(8,128)(2,1)S(1)}, bf16[4,2,128,128]{3,2,1,0:T(8,128)(2,1)S(1)}, u32[]{:S(2)}, u32[]{:S(2)}) collective-permute-start(bf16[4,2,128,128]{3,2,1,0:T(8,128)(2,1)S(1)} %get-tuple-element.37), channel_id=1, source_target_pairs={{8,0},{16,8},{24,16},{9,1},{17,9},{25,17},{10,2},{18,10},{26,18},{... | collective-permute-start | bytes 786440 | tf_op jit(solution)/shard_map/ppermute | solution.py:17
  267.7 8.4 %collective-permute-start.9 = (bf16[4,2,128,128]{3,2,1,0:T(8,128)(2,1)S(1)}, bf16[4,2,128,128]{3,2,1,0:T(8,128)(2,1)S(1)}, u32[]{:S(2)}, u32[]{:S(2)}) collective-permute-start(bf16[4,2,128,128]{3,2,1,0:T(8,128)(2,1)S(1)} %get-tuple-element.38), channel_id=1, source_target_pairs={{0,8},{8,16},{16,24},{1,9},{9,17},{17,25},{2,10},{10,18},{18,26},{... | collective-permute-start | bytes 786440 | tf_op jit(solution)/shard_map/ppermute | solution.py:17
  277.2 1.4 copy-start.9
  278.6 77.9 %all-to-all-start.3 = ((bf16[8,2,2,256,128]{4,3,2,1,0:T(8,128)(2,1)}), bf16[8,2,2,256,128]{4,3,2,1,0:T(8,128)(2,1)}, u32[]{:S(2)}, u32[]{:S(2)}) async-start(bf16[8,2,2,256,128]{4,3,2,1,0:T(8,128)(2,1)} %copy-done.9), calls=%async_computation.3 | async-start | bytes 4194304 | tf_op jit(solution)/shard_map/all_to_all | solution.py:337
  289.5 64.6 %copy-start.12 = (s32[8]{0:T(128)S(1)}, s32[8]{0:T(128)}, u32[]{:S(2)}) copy-start(s32[8]{0:T(128)} %pad_add_fusion.asked) | copy-start | bytes 100
  290.6 7.1 %collective-permute-start.2 = (bf16[4,2,128,128]{3,2,1,0:T(8,128)(2,1)S(1)}, bf16[4,2,128,128]{3,2,1,0:T(8,128)(2,1)S(1)}, u32[]{:S(2)}, u32[]{:S(2)}) collective-permute-start(bf16[4,2,128,128]{3,2,1,0:T(8,128)(2,1)S(1)} %get-tuple-element.61), channel_id=1, source_target_pairs={{0,8},{8,16},{16,24},{1,9},{9,17},{17,25},{2,10},{10,18},{18,26},{... | collective-permute-start | bytes 786440 | tf_op jit(solution)/shard_map/ppermute | solution.py:17
  296.3 6.0 %collective-permute-start.3 = (bf16[4,2,128,128]{3,2,1,0:T(8,128)(2,1)S(1)}, bf16[4,2,128,128]{3,2,1,0:T(8,128)(2,1)S(1)}, u32[]{:S(2)}, u32[]{:S(2)}) collective-permute-start(bf16[4,2,128,128]{3,2,1,0:T(8,128)(2,1)S(1)} %get-tuple-element.60), channel_id=1, source_target_pairs={{8,0},{16,8},{24,16},{9,1},{17,9},{25,17},{10,2},{18,10},{26,18},{... | collective-permute-start | bytes 786440 | tf_op jit(solution)/shard_map/ppermute | solution.py:17
  344.4 8.6 %collective-permute-start.4 = (bf16[4,2,128,128]{3,2,1,0:T(8,128)(2,1)S(1)}, bf16[4,2,128,128]{3,2,1,0:T(8,128)(2,1)S(1)}, u32[]{:S(2)}, u32[]{:S(2)}) collective-permute-start(bf16[4,2,128,128]{3,2,1,0:T(8,128)(2,1)S(1)} %get-tuple-element.33), channel_id=1, source_target_pairs={{8,0},{16,8},{24,16},{9,1},{17,9},{25,17},{10,2},{18,10},{26,18},{... | collective-permute-start | bytes 786440 | tf_op jit(solution)/shard_map/ppermute | solution.py:17
  345.7 8.4 %collective-permute-start.5 = (bf16[4,2,128,128]{3,2,1,0:T(8,128)(2,1)S(1)}, bf16[4,2,128,128]{3,2,1,0:T(8,128)(2,1)S(1)}, u32[]{:S(2)}, u32[]{:S(2)}) collective-permute-start(bf16[4,2,128,128]{3,2,1,0:T(8,128)(2,1)S(1)} %get-tuple-element.34), channel_id=1, source_target_pairs={{0,8},{8,16},{16,24},{1,9},{9,17},{17,25},{2,10},{10,18},{18,26},{... | collective-permute-start | bytes 786440 | tf_op jit(solution)/shard_map/ppermute | solution.py:17
  355.2 1.3 copy-start.7
  356.5 51.5 %all-to-all-start.1 = ((bf16[8,2,2,256,128]{4,3,2,1,0:T(8,128)(2,1)}), bf16[8,2,2,256,128]{4,3,2,1,0:T(8,128)(2,1)}, u32[]{:S(2)}, u32[]{:S(2)}) async-start(bf16[8,2,2,256,128]{4,3,2,1,0:T(8,128)(2,1)} %copy-done.7), calls=%async_computation.1 | async-start | bytes 4194304 | tf_op jit(solution)/shard_map/all_to_all | solution.py:337

commit v2 on v1

v2 whole, which is shorter than its diff:
```python
import functools
import math

import jax
import jax.numpy as jnp
from jax import lax
from jax.experimental import pallas as pl
from jax.experimental.pallas import tpu as pltpu
from jax.sharding import PartitionSpec as P

CROSS = 4
CHUNKS = 2
LANES = 128
SMALL_VMEM = 24 * 1024 * 1024
LARGE_VMEM = 40 * 1024 * 1024


def from_behind(x, axis, by):
    count = lax.axis_size(axis)
    pairs = [(i, i + by) for i in range(count) if 0 <= i + by < count]
    return lax.ppermute(x, axis, pairs)


def pack_kernel(query, key, value, d_out, message, stage, ready, in_sems, out_sems, *, spans):
    sources = (key, value, query, d_out)
    head_dim = ready.shape[-1] // 2

    def fetch(peer, i):
        _, low, high = spans[peer]
        width = high - low
        return pltpu.make_async_copy(
            sources[i].at[:, pl.ds(low, width)],
            stage.at[i, peer, :, pl.ds(0, width)],
            in_sems.at[i, peer],
        )

    def send(peer):
        return pltpu.make_async_copy(ready.at[peer], message.at[peer], out_sems.at[peer])

    for peer in range(len(spans)):
        for i in range(4):
            fetch(peer, i).start()
    for peer, (first, low, _) in enumerate(spans):
        for i in range(4):
            fetch(peer, i).wait()
        for head in range(ready.shape[1]):
            at = first + head * head_dim - low
            for kind in range(2):
                ready[peer, head, kind] = jnp.concatenate(
                    [
                        stage[2 * kind, peer, :, at : at + head_dim],
                        stage[2 * kind + 1, peer, :, at : at + head_dim],
                    ],
                    axis=1,
                )
        send(peer).start()
    for peer in range(len(spans)):
        send(peer).wait()


def pack(arrays, start, chunk_heads, heads_here, peers, head_dim):
    rows = arrays[0].shape[0]
    shape = (peers, chunk_heads, 2, rows, 2 * head_dim)
    spans = []
    for peer in range(peers):
        first = (peer * heads_here + start) * head_dim
        last = first + chunk_heads * head_dim
        spans.append((first, first // LANES * LANES, -(-last // LANES) * LANES))
    width = max(high - low for _, low, high in spans)
    dtype = arrays[0].dtype
    anywhere = pl.BlockSpec(memory_space=pltpu.HBM)
    return pl.pallas_call(
        functools.partial(pack_kernel, spans=spans),
        in_specs=[anywhere] * 4,
        out_specs=pl.BlockSpec(memory_space=pl.ANY),
        out_shape=jax.ShapeDtypeStruct(shape, dtype),
        scratch_shapes=[
            pltpu.VMEM((4, peers, rows, width), dtype),
            pltpu.VMEM(shape, dtype),
            pltpu.SemaphoreType.DMA((4, peers)),
            pltpu.SemaphoreType.DMA((peers,)),
        ],
        compiler_params=pltpu.CompilerParams(vmem_limit_bytes=SMALL_VMEM),
        name="pack",
    )(*arrays)


def unpack_kernel(*refs, chunk, chunks_before, jobs):
    messages = refs[: chunk + 1]
    outs = refs[chunk + 1 + 4 * chunks_before :][:4]
    stages = refs[-2 - chunk - 1 : -2]
    ready, sems = refs[-2], refs[-1]
    in_sems, out_sems = sems.at[0], sems.at[1]
    head_dim = ready.shape[-1] // 2
    needed = sorted({place for job in jobs for place in job[1:]})
    slots = {place: i for i, place in enumerate(needed)}

    def fetch(place):
        which, peer, head = place
        return pltpu.make_async_copy(
            messages[which].at[peer, head],
            stages[which].at[peer, head],
            in_sems.at[slots[place]],
        )

    def send(job, i):
        tile = jobs[job][0]
        return pltpu.make_async_copy(
            ready.at[i, job],
            outs[i].at[:, pl.ds(tile * LANES, LANES)],
            out_sems.at[4 * job + i],
        )

    for place in needed:
        fetch(place).start()
    waited = set()
    for job, (tile, left, right) in enumerate(jobs):
        for place in (left, right):
            if place not in waited:
                fetch(place).wait()
                waited.add(place)
        sides = [stages[which][peer, head] for which, peer, head in (left, right)]
        for i, (kind, at) in enumerate(((1, head_dim), (1, 0), (0, 0), (0, head_dim))):
            ready[i, job] = jnp.concatenate(
                [side[kind, :, at : at + head_dim] for side in sides], axis=1
            )
            send(job, i).start()
    for job in range(len(jobs)):
        for i in range(4):
            send(job, i).wait()


def unpack(messages, starts, heads_here, earlier):
    chunk = len(messages) - 1
    peers, _, _, rows, pair_dim = messages[0].shape
    head_dim = pair_dim // 2
    columns = peers * heads_here * head_dim
    dtype = messages[0].dtype

    def place_of(head):
        peer, local_head = divmod(head, heads_here)
        which = max(c for c, start in enumerate(starts) if start <= local_head)
        return which, peer, local_head - starts[which]

    jobs = []
    for tile in range(columns // LANES):
        left, right = place_of(2 * tile), place_of(2 * tile + 1)
        if max(left[0], right[0]) == chunk:
            jobs.append((tile, left, right))
    if not jobs:
        return earlier
    copies = max(2 * len(jobs), 4 * len(jobs))
    return pl.pallas_call(
        functools.partial(
            unpack_kernel,
            chunk=chunk,
            chunks_before=1 if earlier else 0,
            jobs=jobs,
        ),
        in_specs=[pl.BlockSpec(memory_space=pl.ANY)] * (chunk + 1 + len(earlier)),
        out_specs=[pl.BlockSpec(memory_space=pltpu.HBM)] * 4,
        out_shape=[jax.ShapeDtypeStruct((rows, columns), dtype)] * 4,
        input_output_aliases={chunk + 1 + i: i for i in range(len(earlier))},
        scratch_shapes=[pltpu.VMEM(m.shape, dtype) for m in messages]
        + [
            pltpu.VMEM((4, len(jobs), rows, LANES), dtype),
            pltpu.SemaphoreType.DMA((2, copies)),
        ],
        compiler_params=pltpu.CompilerParams(vmem_limit_bytes=SMALL_VMEM),
        name="unpack",
    )(*messages, *earlier)


def pick_kernel(asked, message, for_next, for_prev, sems, *, block_rows):
    each = message.shape[3] // block_rows

    def copy(i):
        target = for_next if i < CROSS else for_prev
        start = pl.multiple_of(lax.rem(asked[i], each) * block_rows, block_rows)
        return pltpu.make_async_copy(
            message.at[lax.div(asked[i], each), :, 0, pl.ds(start, block_rows)],
            target.at[i % CROSS],
            sems.at[i],
        )

    for i in range(2 * CROSS):
        copy(i).start()
    for i in range(2 * CROSS):
        copy(i).wait()


def pick(message, asked, block_rows):
    _, chunk_heads, _, _, lanes = message.shape
    picked = jax.ShapeDtypeStruct((CROSS, chunk_heads, block_rows, lanes), message.dtype)
    return pl.pallas_call(
        functools.partial(pick_kernel, block_rows=block_rows),
        in_specs=[
            pl.BlockSpec(memory_space=pltpu.SMEM),
            pl.BlockSpec(memory_space=pl.ANY),
        ],
        out_specs=[pl.BlockSpec(memory_space=pl.ANY)] * 2,
        out_shape=[picked, picked],
        scratch_shapes=[pltpu.SemaphoreType.DMA((2 * CROSS,))],
        name="pick",
    )(asked, message)


def attend_kernel(
    lists,
    message,
    came_prev,
    came_next,
    back,
    own,
    to_prev,
    to_next,
    table,
    turned,
    sums,
    both_even,
    both_odd,
    low_even,
    low_odd,
    *,
    block_rows,
    head_dim,
    per_list,
):
    peers, heads, _, rows, lanes = message.shape
    each = rows // block_rows
    blocks = peers * each
    window = blocks + 2 * CROSS
    units = heads * blocks
    keys = per_list * block_rows
    scaling = head_dim ** (-0.5)
    exponent = scaling * math.log2(math.e)
    both = (both_even, both_odd)
    low = (low_even, low_odd)
    step_rows = 64

    for head in range(heads):
        for i in range(CROSS):
            table[head, i] = came_prev[i, head]
            table[head, CROSS + blocks + i] = came_next[i, head]

        def fill(peer, carry):
            for i in range(each):
                table[head, CROSS + peer * each + i] = message[
                    peer, head, 0, i * block_rows : (i + 1) * block_rows
                ]
            return carry

        lax.fori_loop(0, peers, fill, 0)

        def turn(i, carry):
            turned[head, i] = table[head, i].T
            sums[head, i] = jnp.zeros(sums.shape[2:], sums.dtype)
            return carry

        lax.fori_loop(0, window, turn, 0)

    left = lax.broadcasted_iota(jnp.int32, (block_rows, lanes), 1) < head_dim

    def locate(unit):
        head = lax.div(unit, blocks)
        block = lax.rem(unit, blocks)
        ids = [lists[head, block, j] for j in range(per_list)]
        peer = lax.div(block, each)
        start = pl.multiple_of(lax.rem(block, each) * block_rows, block_rows)
        return head, ids, peer, pl.ds(start, block_rows)

    def apart_of(head, peer, here):
        query_grad = message[peer, head, 1, here]
        nothing = jnp.zeros_like(query_grad)
        return jnp.concatenate(
            [jnp.where(left, query_grad, nothing), jnp.where(left, nothing, query_grad)],
            axis=0,
        )

    def score(unit, slot):
        head, ids, peer, here = locate(unit)
        key_value = jnp.concatenate([table[head, i] for i in ids], axis=0)
        both[slot][...] = lax.dot_general(
            key_value,
            apart_of(head, peer, here),
            (((1,), (1,)), ((), ())),
            preferred_element_type=jnp.float32,
        )

    def soften(slot):
        source, target = both[slot], low[slot]
        parts = [slice(i, i + step_rows) for i in range(0, keys, step_rows)]
        top = source[parts[0], :block_rows]
        for part in parts[1:]:
            top = jnp.maximum(top, source[part, :block_rows])
        top = jnp.max(top, axis=0, keepdims=True)
        total = jnp.zeros((step_rows, block_rows), jnp.float32)
        mixed = jnp.zeros((step_rows, block_rows), jnp.float32)
        for part in parts:
            raised = jnp.exp2((source[part, :block_rows] - top) * exponent)
            source[part, :block_rows] = raised
            total += raised
            mixed += raised * source[part, block_rows:]
        inverse = 1.0 / jnp.sum(total, axis=0, keepdims=True)
        correction = jnp.sum(mixed, axis=0, keepdims=True) * inverse
        for part in parts:
            weights = source[part, :block_rows] * inverse
            target[part, block_rows:] = weights.astype(jnp.bfloat16)
            target[part, :block_rows] = (
                weights * (source[part, block_rows:] - correction)
            ).astype(jnp.bfloat16)

    def combine(unit, slot):
        head, ids, peer, here = locate(unit)
        products = low[slot][...]
        terms = jnp.dot(
            products, apart_of(head, peer, here), preferred_element_type=jnp.float32
        )
        for j, i in enumerate(ids):
            sums[head, i] += terms[j * block_rows : (j + 1) * block_rows]
        key_value = jnp.concatenate([turned[head, i] for i in ids], axis=1)
        out = jnp.dot(key_value, products, preferred_element_type=jnp.float32)
        out = jnp.concatenate(
            [out[:head_dim, :block_rows] * scaling, out[head_dim:, block_rows:]], axis=0
        )
        back[peer, head, 1, here] = out.T.astype(back.dtype)

    score(0, 0)
    score(1, 1)
    soften(0)

    def step(i, carry):
        for slot in range(2):
            unit = 2 * i + slot
            combine(unit - 2, slot)
            score(unit, slot)
            soften(1 - slot)
        return carry

    lax.fori_loop(1, units // 2, step, 0)
    combine(units - 2, 0)
    soften(1)
    combine(units - 1, 1)

    factor = jnp.where(left, scaling, 1.0)
    for head in range(heads):
        for i in range(CROSS):
            to_prev[i, head] = (sums[head, i] * factor).astype(to_prev.dtype)
            to_next[i, head] = (sums[head, CROSS + blocks + i] * factor).astype(to_next.dtype)

        def finish(i, carry):
            own[head, i] = sums[head, CROSS + i] * factor
            return carry

        lax.fori_loop(0, blocks, finish, 0)


def attend(message, came_prev, came_next, lists, block_rows):
    peers, chunk_heads, _, rows, lanes = message.shape
    per_list = lists.shape[-1]
    keys = per_list * block_rows
    blocks = peers * rows // block_rows
    window = blocks + 2 * CROSS
    inside = pl.BlockSpec(memory_space=pltpu.VMEM)
    cross_shape = jax.ShapeDtypeStruct(came_prev.shape, message.dtype)
    return pl.pallas_call(
        functools.partial(
            attend_kernel, block_rows=block_rows, head_dim=lanes // 2, per_list=per_list
        ),
        in_specs=[pl.BlockSpec(memory_space=pltpu.SMEM), inside, inside, inside],
        out_specs=[inside] * 4,
        out_shape=[
            jax.ShapeDtypeStruct(message.shape, message.dtype),
            jax.ShapeDtypeStruct((chunk_heads, blocks, block_rows, lanes), jnp.float32),
            cross_shape,
            cross_shape,
        ],
        scratch_shapes=[
            pltpu.VMEM((chunk_heads, window, block_rows, lanes), message.dtype),
            pltpu.VMEM((chunk_heads, window, lanes, block_rows), message.dtype),
            pltpu.VMEM((chunk_heads, window, block_rows, lanes), jnp.float32),
            pltpu.VMEM((keys, 2 * block_rows), jnp.float32),
            pltpu.VMEM((keys, 2 * block_rows), jnp.float32),
            pltpu.VMEM((keys, 2 * block_rows), message.dtype),
            pltpu.VMEM((keys, 2 * block_rows), message.dtype),
        ],
        compiler_params=pltpu.CompilerParams(vmem_limit_bytes=LARGE_VMEM),
        name="attend",
    )(lists, message, came_prev, came_next)


def finish_kernel(asked, own, later, earlier, back_in, back, sums, *, block_rows):
    del back_in
    peers, _, _, rows, _ = back.shape
    each = rows // block_rows
    sums[...] = own[0]
    for i in range(CROSS):
        sums[asked[i]] += later[i, 0].astype(jnp.float32)
    for i in range(CROSS):
        sums[asked[CROSS + i]] += earlier[i, 0].astype(jnp.float32)
    for peer in range(peers):
        for i in range(each):
            back[peer, 0, 0, i * block_rows : (i + 1) * block_rows] = sums[
                peer * each + i
            ].astype(back.dtype)


def finish(back, own, later, earlier, asked):
    peers, chunk_heads, _, rows, lanes = back.shape
    _, blocks, block_rows, _ = own.shape
    cross_spec = pl.BlockSpec(
        (CROSS, 1, block_rows, lanes), lambda head, ids: (0, head, 0, 0)
    )
    return pl.pallas_call(
        functools.partial(finish_kernel, block_rows=block_rows),
        grid_spec=pltpu.PrefetchScalarGridSpec(
            num_scalar_prefetch=1,
            grid=(chunk_heads,),
            in_specs=[
                pl.BlockSpec(
                    (1, blocks, block_rows, lanes), lambda head, ids: (head, 0, 0, 0)
                ),
                cross_spec,
                cross_spec,
                pl.BlockSpec(memory_space=pl.ANY),
            ],
            out_specs=pl.BlockSpec(
                (peers, 1, 1, rows, lanes), lambda head, ids: (0, head, 0, 0, 0)
            ),
            scratch_shapes=[pltpu.VMEM((blocks, block_rows, lanes), jnp.float32)],
        ),
        out_shape=jax.ShapeDtypeStruct(back.shape, back.dtype),
        input_output_aliases={4: 0},
        compiler_params=pltpu.CompilerParams(vmem_limit_bytes=SMALL_VMEM),
        name="finish",
    )(asked, own, later, earlier, back)


def exchange(message):
    return lax.all_to_all(message, "seq", split_axis=0, concat_axis=0, tiled=True)


def local(query, key, value, d_out, pattern):
    heads_here, blocks, _ = pattern.shape
    peers = lax.axis_size("seq")
    rows, columns = query.shape
    head_dim = columns // (peers * heads_here)
    block_rows = rows * peers // blocks
    chunks = min(CHUNKS, heads_here)
    starts = [-(-heads_here * i // chunks) for i in range(chunks)]
    sizes = [end - start for start, end in zip(starts, starts[1:] + [heads_here])]
    arrays = (query, key, value, d_out)

    own_base = lax.axis_index("slab") * blocks
    block_ids = jnp.arange(blocks, dtype=jnp.int32)
    flat_lists = pattern.reshape(-1)
    reverse_rank = blocks - 1 - block_ids
    hits_prev = jnp.any(flat_lists[:, None] == (own_base - blocks + block_ids)[None, :], axis=0)
    hits_next = jnp.any(flat_lists[:, None] == (own_base + blocks + block_ids)[None, :], axis=0)
    need_prev = lax.top_k(hits_prev.astype(jnp.int32) * blocks + reverse_rank, CROSS)[1]
    need_next = lax.top_k(hits_next.astype(jnp.int32) * blocks + reverse_rank, CROSS)[1]
    asked_next = from_behind(need_prev, "slab", -1)
    asked_prev = from_behind(need_next, "slab", 1)
    asked = jnp.concatenate([asked_next, asked_prev])
    rank_ids = jnp.arange(CROSS, dtype=jnp.int32)
    prev_global = own_base - blocks + need_prev
    next_global = own_base + blocks + need_next
    pos_prev = jnp.sum(jnp.where(pattern[..., None] == prev_global, rank_ids, 0), axis=-1)
    pos_next = jnp.sum(jnp.where(pattern[..., None] == next_global, rank_ids, 0), axis=-1)
    in_own = (pattern >= own_base) & (pattern < own_base + blocks)
    local_ids = jnp.where(
        in_own,
        CROSS + pattern - own_base,
        jnp.where(pattern < own_base, pos_prev, CROSS + blocks + pos_next),
    )

    came = [
        exchange(pack(arrays, start, size, heads_here, peers, head_dim))
        for start, size in zip(starts, sizes)
    ]
    received = []
    outs = ()
    for message, start, size in zip(came, starts, sizes):
        for_next, for_prev = pick(message, asked, block_rows)
        came_prev = from_behind(for_next, "slab", 1)
        came_next = from_behind(for_prev, "slab", -1)
        back, own, to_prev, to_next = attend(
            message, came_prev, came_next, local_ids[start : start + size], block_rows
        )
        later = from_behind(to_prev, "slab", -1)
        earlier = from_behind(to_next, "slab", 1)
        received.append(exchange(finish(back, own, later, earlier, asked)))
        outs = unpack(received, starts, heads_here, outs)
    return tuple(outs)


def solution(mesh):
    tokens = P(("slab", "seq"), None)
    return jax.shard_map(
        local,
        mesh=mesh,
        in_specs=(tokens, tokens, tokens, tokens, P("seq", "slab", None)),
        out_specs=(tokens, tokens, tokens, tokens),
        check_vma=False,
    )
```

time: 422 us -> 369 us (0.87)
  Pallas kernels: 176 us -> 140 us
  starting transfers between devices: 86.3 us -> 61 us
  local copies, waits for them, and re-layouts: 15.9 us -> 23.6 us
    pallas_call x3 -> x2, Pallas kernels: 126 us -> 69.2 us  [attend(): pl.pallas_call(functools.partial(attend_kernel, block_rows=block_rows, he...]
    pallas_call x9 -> x6, Pallas kernels: 47.1 us -> 67.9 us  [the longest x2 51.6 us: pick(): pl.pallas_call(functools.partial(pick_kernel, block_rows=block_rows), in_...]
    all_to_all x6 -> x4, starting transfers between devices: 37.6 us -> 24.3 us  [exchange(): lax.all_to_all(message, 'seq', split_axis=0, concat_axis=0, tiled=True)]
    ppermute x14 -> x10, starting transfers between devices: 48.6 us -> 36.7 us  [from_behind(): return lax.ppermute(x, axis, pairs)]
    unnamed x31 -> x39, local copies, waits for them, and re-layouts: 12.4 us -> 23.4 us
    all_to_all x6 -> x4, waiting for transfers between devices: 113 us -> 122 us  [exchange(): lax.all_to_all(message, 'seq', split_axis=0, concat_axis=0, tiled=True)]
    ppermute x14 -> x10, waiting for transfers between devices: 17.9 us -> 12.4 us  [from_behind(): return lax.ppermute(x, axis, pairs)]
  transfers between devices with their start and end apart: 20 -> 14, of which waited for: 10 -> 9; matrix products, arithmetic and copies ran while one was open for 2% -> 1% of each run, Pallas kernels for 40% -> 36%
where the time goes in v2:
time: 369 us; the launch traced here: 363 us
  Pallas kernels  140 us (38%)
  waiting for transfers between devices  134 us (36%)
  starting transfers between devices  61 us (17%)
  local copies, waits for them, and re-layouts  23.6 us (6%)
    all_to_all x4, waiting for transfers between devices, exchange(): lax.all_to_all(message, 'seq', split_axis=0, concat_axis=0, tiled=True)  122 us
    pallas_call x2, Pallas kernels, attend(): pl.pallas_call(functools.partial(attend_kernel, block_rows=block_rows, he...  69.2 us
    pallas_call x2, Pallas kernels, pick(): pl.pallas_call(functools.partial(pick_kernel, block_rows=block_rows), in_...  51.6 us
    ppermute x10, starting transfers between devices, from_behind(): return lax.ppermute(x, axis, pairs)  36.7 us
    all_to_all x4, starting transfers between devices, exchange(): lax.all_to_all(message, 'seq', split_axis=0, concat_axis=0, tiled=True)  24.3 us
    unnamed x39, local copies, waits for them, and re-layouts  23.4 us
    ppermute x10, waiting for transfers between devices, from_behind(): return lax.ppermute(x, axis, pairs)  12.4 us
    pallas_call x2, Pallas kernels, unpack(): pl.pallas_call(functools.partial(unpack_kernel, chunk=chunk, chunks_befor...  8.61 us
  transfers between devices with their start and end apart: 14, of which 9 were waited for; matrix products, arithmetic and copies ran while one was open for 1% of the time, Pallas kernels for 36%

profile of v2, /device:TPU:8, one launch (start us, length us, event | category | flops | bytes accessed | tf_op | source)
XLA Modules:
  0.0 363.2 jit_solution(9867806848491778809)
XLA Ops:
  0.6 1.4 copy-done.8
  2.0 1.4 copy-done.10
  3.5 1.4 copy-done.12
  4.9 1.4 copy-done.14
  6.3 3.8 %pack.2 = bf16[8,3,2,256,128]{4,3,2,1,0:T(8,128)(2,1)S(1)} custom-call(bf16[256,3072]{1,0:T(8,128)(2,1)S(1)} %copy-done.8, bf16[256,3072]{1,0:T(8,128)(2,1)S(1)} %copy-done.10, bf16[256,3072]{1,0:T(8,128)(2,1)S(1)} %copy-done.12, bf16[256,3072]{1,0:T(8,128)(2,1)S(1)} %copy-done.14), custom_call_target="tpu_custom_call" | custom-call | tf_op jit(solution)/shard_map/pack/pallas_call | solution.py:72
  10.1 1.7 copy-done.7
  11.8 6.3 %all-to-all-start = ((bf16[8,3,2,256,128]{4,3,2,1,0:T(8,128)(2,1)}), bf16[8,3,2,256,128]{4,3,2,1,0:T(8,128)(2,1)S(1)}, u32[]{:S(2)}, u32[]{:S(2)}) async-start(bf16[8,3,2,256,128]{4,3,2,1,0:T(8,128)(2,1)} %copy-done.7), calls=%async_computation | async-start | bytes 6291456 | tf_op jit(solution)/shard_map/all_to_all | solution.py:440
  18.1 1.4 copy-done.9
  19.5 1.4 copy-done.11
  20.9 1.4 copy-done.13
  22.3 1.4 copy-done.15
  23.7 3.8 %pack.3 = bf16[8,3,2,256,128]{4,3,2,1,0:T(8,128)(2,1)S(1)} custom-call(bf16[256,3072]{1,0:T(8,128)(2,1)S(1)} %copy-done.9, bf16[256,3072]{1,0:T(8,128)(2,1)S(1)} %copy-done.11, bf16[256,3072]{1,0:T(8,128)(2,1)S(1)} %copy-done.13, bf16[256,3072]{1,0:T(8,128)(2,1)S(1)} %copy-done.15), custom_call_target="tpu_custom_call" | custom-call | tf_op jit(solution)/shard_map/pack/pallas_call | solution.py:72
  27.5 1.6 copy-done.4
  29.2 57.1 %all-to-all-done.message = bf16[8,3,2,256,128]{4,3,2,1,0:T(8,128)(2,1)S(1)} async-done(((bf16[8,3,2,256,128]{4,3,2,1,0:T(8,128)(2,1)}), bf16[8,3,2,256,128]{4,3,2,1,0:T(8,128)(2,1)S(1)}, u32[]{:S(2)}, u32[]{:S(2)}) %all-to-all-start) | async-done | bytes 3145760 | tf_op jit(solution)/shard_map/all_to_all | solution.py:440
  86.3 1.7 copy-done.2
  88.0 6.1 %all-to-all-start.2 = ((bf16[8,3,2,256,128]{4,3,2,1,0:T(8,128)(2,1)}), bf16[8,3,2,256,128]{4,3,2,1,0:T(8,128)(2,1)S(1)}, u32[]{:S(2)}, u32[]{:S(2)}) async-start(bf16[8,3,2,256,128]{4,3,2,1,0:T(8,128)(2,1)} %copy-done.4), calls=%async_computation.2 | async-start | bytes 6291456 | tf_op jit(solution)/shard_map/all_to_all | solution.py:440
  94.5 1.2 top_k.17
  95.8 1.3 collective-permute-start
  97.1 1.2 top_k.24
  98.3 3.0 collective-permute-start.1
  102.1 0.6 pad_add_fusion.asked
  102.7 25.8 %pick.2 = (bf16[4,3,128,128]{3,2,1,0:T(8,128)(2,1)}, bf16[4,3,128,128]{3,2,1,0:T(8,128)(2,1)}) custom-call(s32[8]{0:T(128)} %pad_add_fusion.asked, bf16[8,3,2,256,128]{4,3,2,1,0:T(8,128)(2,1)} %copy-done.2), custom_call_target="tpu_custom_call" | custom-call | tf_op jit(solution)/shard_map/pick/pallas_call | solution.py:195
  128.5 3.0 collective-permute-start.2
  131.5 1.3 collective-permute-start.3
  133.0 4.0 %collective-permute-done.3.came_next = bf16[4,3,128,128]{3,2,1,0:T(8,128)(2,1)S(1)} collective-permute-done((bf16[4,3,128,128]{3,2,1,0:T(8,128)(2,1)}, bf16[4,3,128,128]{3,2,1,0:T(8,128)(2,1)S(1)}, u32[]{:S(2)}, u32[]{:S(2)}) %collective-permute-start.3) | collective-permute-done | bytes 393248 | tf_op jit(solution)/shard_map/ppermute | solution.py:21
  137.1 1.9 copy-done.3
  138.9 34.6 %attend.2 = (bf16[8,3,2,256,128]{4,3,2,1,0:T(8,128)(2,1)S(1)}, f32[3,16,128,128]{3,2,1,0:T(8,128)S(1)}, bf16[4,3,128,128]{3,2,1,0:T(8,128)(2,1)S(1)}, bf16[4,3,128,128]{3,2,1,0:T(8,128)(2,1)S(1)}) custom-call(s32[3,16,8]{2,1,0:T(8,128)S(1)} %get-tuple-element.49.lists, bf16[8,3,2,256,128]{4,3,2,1,0:T(8,128)(2,1)S(1)} %copy-done.3, ...), custom_call_target="tpu_custom_call" | custom-call | tf_op jit(solution)/shard_map/attend/pallas_call | solution.py:366
  173.5 1.3 collective-permute-start.4
  174.8 8.8 %collective-permute-start.5 = (bf16[4,3,128,128]{3,2,1,0:T(8,128)(2,1)S(1)}, bf16[4,3,128,128]{3,2,1,0:T(8,128)(2,1)S(1)}, u32[]{:S(2)}, u32[]{:S(2)}) collective-permute-start(bf16[4,3,128,128]{3,2,1,0:T(8,128)(2,1)S(1)} %get-tuple-element.32), channel_id=1, source_target_pairs={{0,8},{8,16},{16,24},{1,9},{9,17},{17,25},{2,10},{10,18},{18,26},{... | collective-permute-start | bytes 1179656 | tf_op jit(solution)/shard_map/ppermute | solution.py:21
  183.7 1.3 collective-permute-done.5.earlier
  185.0 1.3 finish.2
  186.4 1.7 copy-done.6
  188.0 1.7 copy-done
  189.8 6.0 %all-to-all-start.1 = ((bf16[8,3,2,256,128]{4,3,2,1,0:T(8,128)(2,1)}), bf16[8,3,2,256,128]{4,3,2,1,0:T(8,128)(2,1)}, u32[]{:S(2)}, u32[]{:S(2)}) async-start(bf16[8,3,2,256,128]{4,3,2,1,0:T(8,128)(2,1)} %copy-done.6), calls=%async_computation.1 | async-start | bytes 6291456 | tf_op jit(solution)/shard_map/all_to_all | solution.py:440
  195.8 25.8 %pick.3 = (bf16[4,3,128,128]{3,2,1,0:T(8,128)(2,1)}, bf16[4,3,128,128]{3,2,1,0:T(8,128)(2,1)}) custom-call(s32[8]{0:T(128)} %pad_add_fusion.asked, bf16[8,3,2,256,128]{4,3,2,1,0:T(8,128)(2,1)} %copy-done), custom_call_target="tpu_custom_call" | custom-call | tf_op jit(solution)/shard_map/pick/pallas_call | solution.py:195
  221.6 6.5 %collective-permute-start.6 = (bf16[4,3,128,128]{3,2,1,0:T(8,128)(2,1)}, bf16[4,3,128,128]{3,2,1,0:T(8,128)(2,1)S(1)}, u32[]{:S(2)}, u32[]{:S(2)}) collective-permute-start(bf16[4,3,128,128]{3,2,1,0:T(8,128)(2,1)} %get-tuple-element.34), channel_id=1, source_target_pairs={{0,8},{8,16},{16,24},{1,9},{9,17},{17,25},{2,10},{10,18},{18,26},{... | collective-permute-start | bytes 1179656 | tf_op jit(solution)/shard_map/ppermute | solution.py:21
  228.0 1.3 collective-permute-start.7
  229.5 4.8 %collective-permute-done.7.came_next = bf16[4,3,128,128]{3,2,1,0:T(8,128)(2,1)S(1)} collective-permute-done((bf16[4,3,128,128]{3,2,1,0:T(8,128)(2,1)}, bf16[4,3,128,128]{3,2,1,0:T(8,128)(2,1)S(1)}, u32[]{:S(2)}, u32[]{:S(2)}) %collective-permute-start.7) | collective-permute-done | bytes 393248 | tf_op jit(solution)/shard_map/ppermute | solution.py:21
  234.4 34.6 %attend.3 = (bf16[8,3,2,256,128]{4,3,2,1,0:T(8,128)(2,1)S(1)}, f32[3,16,128,128]{3,2,1,0:T(8,128)S(1)}, bf16[4,3,128,128]{3,2,1,0:T(8,128)(2,1)S(1)}, bf16[4,3,128,128]{3,2,1,0:T(8,128)(2,1)S(1)}) custom-call(s32[3,16,8]{2,1,0:T(8,128)S(1)} %get-tuple-element.48.lists, bf16[8,3,2,256,128]{4,3,2,1,0:T(8,128)(2,1)S(1)} %copy-done.1, ...), custom_call_target="tpu_custom_call" | custom-call | tf_op jit(solution)/shard_map/attend/pallas_call | solution.py:366
  269.0 1.3 collective-permute-start.8
  270.3 8.9 %collective-permute-start.9 = (bf16[4,3,128,128]{3,2,1,0:T(8,128)(2,1)S(1)}, bf16[4,3,128,128]{3,2,1,0:T(8,128)(2,1)S(1)}, u32[]{:S(2)}, u32[]{:S(2)}) collective-permute-start(bf16[4,3,128,128]{3,2,1,0:T(8,128)(2,1)S(1)} %get-tuple-element.38), channel_id=1, source_target_pairs={{0,8},{8,16},{16,24},{1,9},{9,17},{17,25},{2,10},{10,18},{18,26},{... | collective-permute-start | bytes 1179656 | tf_op jit(solution)/shard_map/ppermute | solution.py:21
  279.2 1.3 collective-permute-done.9.earlier
  280.5 1.3 finish.3
  281.9 1.7 copy-done.5
  283.6 6.0 %all-to-all-start.3 = ((bf16[8,3,2,256,128]{4,3,2,1,0:T(8,128)(2,1)}), bf16[8,3,2,256,128]{4,3,2,1,0:T(8,128)(2,1)}, u32[]{:S(2)}, u32[]{:S(2)}) async-start(bf16[8,3,2,256,128]{4,3,2,1,0:T(8,128)(2,1)} %copy-done.5), calls=%async_computation.3 | async-start | bytes 6291456 | tf_op jit(solution)/shard_map/all_to_all | solution.py:440
  289.6 3.3 unpack.2
  292.9 64.9 %all-to-all-done.3.refs_1_ = bf16[8,3,2,256,128]{4,3,2,1,0:T(8,128)(2,1)} async-done(((bf16[8,3,2,256,128]{4,3,2,1,0:T(8,128)(2,1)}), bf16[8,3,2,256,128]{4,3,2,1,0:T(8,128)(2,1)}, u32[]{:S(2)}, u32[]{:S(2)}) %all-to-all-start.3) | async-done | bytes 3145760 | tf_op jit(solution)/shard_map/all_to_all | solution.py:440
  357.7 5.3 %unpack.3 = (bf16[256,3072]{1,0:T(8,128)(2,1)}, bf16[256,3072]{1,0:T(8,128)(2,1)}, bf16[256,3072]{1,0:T(8,128)(2,1)}, bf16[256,3072]{1,0:T(8,128)(2,1)}) custom-call(bf16[8,3,2,256,128]{4,3,2,1,0:T(8,128)(2,1)} %all-to-all-done.1.refs_0_, ...), custom_call_target="tpu_custom_call", output_to_operand_aliasing={{0}: (2, {}), {1}: (3, {}), {2}: (4, {}), {3}: (5, {})} | custom-call | tf_op jit(solution)/shard_map/unpack/pallas_call | solution.py:153
  (46 shorter events, 1.6 us)
Async XLA Ops:
  0.6 1.4 copy-start.8
  2.0 1.4 copy-start.10
  3.4 1.4 copy-start.12
  4.9 1.4 copy-start.14
  10.1 1.7 copy-start.7
  11.8 74.5 %all-to-all-start = ((bf16[8,3,2,256,128]{4,3,2,1,0:T(8,128)(2,1)}), bf16[8,3,2,256,128]{4,3,2,1,0:T(8,128)(2,1)S(1)}, u32[]{:S(2)}, u32[]{:S(2)}) async-start(bf16[8,3,2,256,128]{4,3,2,1,0:T(8,128)(2,1)} %copy-done.7), calls=%async_computation | async-start | bytes 6291456 | tf_op jit(solution)/shard_map/all_to_all | solution.py:440
  18.1 1.4 copy-start.9
  19.5 1.4 copy-start.11
  20.9 1.4 copy-start.13
  22.3 1.4 copy-start.15
  27.5 1.7 copy-start.4
  29.2 64.9 %copy-start.18 = (s32[6,16,8]{1,2,0:T(8,128)S(1)}, s32[6,16,8]{1,2,0:T(8,128)}, u32[]{:S(2)}) copy-start(s32[6,16,8]{1,2,0:T(8,128)} %param.9) | copy-start | bytes 9220
  86.3 1.7 copy-start.2
  88.0 100.0 %all-to-all-start.2 = ((bf16[8,3,2,256,128]{4,3,2,1,0:T(8,128)(2,1)}), bf16[8,3,2,256,128]{4,3,2,1,0:T(8,128)(2,1)S(1)}, u32[]{:S(2)}, u32[]{:S(2)}) async-start(bf16[8,3,2,256,128]{4,3,2,1,0:T(8,128)(2,1)} %copy-done.4), calls=%async_computation.2 | async-start | bytes 6291456 | tf_op jit(solution)/shard_map/all_to_all | solution.py:440
  95.8 5.8 %collective-permute-start = (s32[4]{0:T(128)S(1)}, s32[4]{0:T(128)S(1)}, u32[]{:S(2)}, u32[]{:S(2)}) collective-permute-start(s32[4]{0:T(128)S(1)} %get-tuple-element.51), channel_id=1, source_target_pairs={{8,0},{16,8},{24,16},{9,1},{17,9},{25,17},{10,2},{18,10},{26,18},{... | collective-permute-start | bytes 56 | tf_op jit(solution)/shard_map/ppermute | solution.py:21
  98.3 3.8 %collective-permute-start.1 = (s32[4]{0:T(128)S(1)}, s32[4]{0:T(128)S(1)}, u32[]{:S(2)}, u32[]{:S(2)}) collective-permute-start(s32[4]{0:T(128)S(1)} %get-tuple-element.53), channel_id=1, source_target_pairs={{0,8},{8,16},{16,24},{1,9},{9,17},{17,25},{2,10},{10,18},{18,26},{... | collective-permute-start | bytes 56 | tf_op jit(solution)/shard_map/ppermute | solution.py:21
  102.7 82.3 %copy-start.16 = (s32[8]{0:T(128)S(1)}, s32[8]{0:T(128)}, u32[]{:S(2)}) copy-start(s32[8]{0:T(128)} %pad_add_fusion.asked) | copy-start | bytes 100
  128.5 4.5 %collective-permute-start.2 = (bf16[4,3,128,128]{3,2,1,0:T(8,128)(2,1)}, bf16[4,3,128,128]{3,2,1,0:T(8,128)(2,1)S(1)}, u32[]{:S(2)}, u32[]{:S(2)}) collective-permute-start(bf16[4,3,128,128]{3,2,1,0:T(8,128)(2,1)} %get-tuple-element.28), channel_id=1, source_target_pairs={{0,8},{8,16},{16,24},{1,9},{9,17},{17,25},{2,10},{10,18},{18,26},{... | collective-permute-start | bytes 1179656 | tf_op jit(solution)/shard_map/ppermute | solution.py:21
  131.5 5.6 %collective-permute-start.3 = (bf16[4,3,128,128]{3,2,1,0:T(8,128)(2,1)}, bf16[4,3,128,128]{3,2,1,0:T(8,128)(2,1)S(1)}, u32[]{:S(2)}, u32[]{:S(2)}) collective-permute-start(bf16[4,3,128,128]{3,2,1,0:T(8,128)(2,1)} %get-tuple-element.29), channel_id=1, source_target_pairs={{8,0},{16,8},{24,16},{9,1},{17,9},{25,17},{10,2},{18,10},{26,18},{... | collective-permute-start | bytes 1179656 | tf_op jit(solution)/shard_map/ppermute | solution.py:21
  137.1 1.9 copy-start.3
  173.5 10.1 %collective-permute-start.4 = (bf16[4,3,128,128]{3,2,1,0:T(8,128)(2,1)S(1)}, bf16[4,3,128,128]{3,2,1,0:T(8,128)(2,1)S(1)}, u32[]{:S(2)}, u32[]{:S(2)}) collective-permute-start(bf16[4,3,128,128]{3,2,1,0:T(8,128)(2,1)S(1)} %get-tuple-element.31), channel_id=1, source_target_pairs={{8,0},{16,8},{24,16},{9,1},{17,9},{25,17},{10,2},{18,10},{26,18},{... | collective-permute-start | bytes 1179656 | tf_op jit(solution)/shard_map/ppermute | solution.py:21
  174.8 10.1 %collective-permute-start.5 = (bf16[4,3,128,128]{3,2,1,0:T(8,128)(2,1)S(1)}, bf16[4,3,128,128]{3,2,1,0:T(8,128)(2,1)S(1)}, u32[]{:S(2)}, u32[]{:S(2)}) collective-permute-start(bf16[4,3,128,128]{3,2,1,0:T(8,128)(2,1)S(1)} %get-tuple-element.32), channel_id=1, source_target_pairs={{0,8},{8,16},{16,24},{1,9},{9,17},{17,25},{2,10},{10,18},{18,26},{... | collective-permute-start | bytes 1179656 | tf_op jit(solution)/shard_map/ppermute | solution.py:21
  186.3 1.7 copy-start.6
  188.0 1.7 copy-start
  189.8 93.8 %all-to-all-start.1 = ((bf16[8,3,2,256,128]{4,3,2,1,0:T(8,128)(2,1)}), bf16[8,3,2,256,128]{4,3,2,1,0:T(8,128)(2,1)}, u32[]{:S(2)}, u32[]{:S(2)}) async-start(bf16[8,3,2,256,128]{4,3,2,1,0:T(8,128)(2,1)} %copy-done.6), calls=%async_computation.1 | async-start | bytes 6291456 | tf_op jit(solution)/shard_map/all_to_all | solution.py:440
  195.8 38.6 %copy-start.1 = (bf16[8,3,2,256,128]{4,3,2,1,0:T(8,128)(2,1)S(1)}, bf16[8,3,2,256,128]{4,3,2,1,0:T(8,128)(2,1)}, u32[]{:S(2)}) copy-start(bf16[8,3,2,256,128]{4,3,2,1,0:T(8,128)(2,1)} %copy-done) | copy-start | bytes 9437188
  195.8 84.8 %copy-start.17 = (s32[8]{0:T(128)S(1)}, s32[8]{0:T(128)}, u32[]{:S(2)}) copy-start(s32[8]{0:T(128)} %pad_add_fusion.asked) | copy-start | bytes 100
  221.6 8.0 %collective-permute-start.6 = (bf16[4,3,128,128]{3,2,1,0:T(8,128)(2,1)}, bf16[4,3,128,128]{3,2,1,0:T(8,128)(2,1)S(1)}, u32[]{:S(2)}, u32[]{:S(2)}) collective-permute-start(bf16[4,3,128,128]{3,2,1,0:T(8,128)(2,1)} %get-tuple-element.34), channel_id=1, source_target_pairs={{0,8},{8,16},{16,24},{1,9},{9,17},{17,25},{2,10},{10,18},{18,26},{... | collective-permute-start | bytes 1179656 | tf_op jit(solution)/shard_map/ppermute | solution.py:21
  228.0 6.3 %collective-permute-start.7 = (bf16[4,3,128,128]{3,2,1,0:T(8,128)(2,1)}, bf16[4,3,128,128]{3,2,1,0:T(8,128)(2,1)S(1)}, u32[]{:S(2)}, u32[]{:S(2)}) collective-permute-start(bf16[4,3,128,128]{3,2,1,0:T(8,128)(2,1)} %get-tuple-element.35), channel_id=1, source_target_pairs={{8,0},{16,8},{24,16},{9,1},{17,9},{25,17},{10,2},{18,10},{26,18},{... | collective-permute-start | bytes 1179656 | tf_op jit(solution)/shard_map/ppermute | solution.py:21
  269.0 10.2 %collective-permute-start.8 = (bf16[4,3,128,128]{3,2,1,0:T(8,128)(2,1)S(1)}, bf16[4,3,128,128]{3,2,1,0:T(8,128)(2,1)S(1)}, u32[]{:S(2)}, u32[]{:S(2)}) collective-permute-start(bf16[4,3,128,128]{3,2,1,0:T(8,128)(2,1)S(1)} %get-tuple-element.37), channel_id=1, source_target_pairs={{8,0},{16,8},{24,16},{9,1},{17,9},{25,17},{10,2},{18,10},{26,18},{... | collective-permute-start | bytes 1179656 | tf_op jit(solution)/shard_map/ppermute | solution.py:21
  270.3 10.3 %collective-permute-start.9 = (bf16[4,3,128,128]{3,2,1,0:T(8,128)(2,1)S(1)}, bf16[4,3,128,128]{3,2,1,0:T(8,128)(2,1)S(1)}, u32[]{:S(2)}, u32[]{:S(2)}) collective-permute-start(bf16[4,3,128,128]{3,2,1,0:T(8,128)(2,1)S(1)} %get-tuple-element.38), channel_id=1, source_target_pairs={{0,8},{8,16},{16,24},{1,9},{9,17},{17,25},{2,10},{10,18},{18,26},{... | collective-permute-start | bytes 1179656 | tf_op jit(solution)/shard_map/ppermute | solution.py:21
  281.9 1.7 copy-start.5
  283.6 74.1 %all-to-all-start.3 = ((bf16[8,3,2,256,128]{4,3,2,1,0:T(8,128)(2,1)}), bf16[8,3,2,256,128]{4,3,2,1,0:T(8,128)(2,1)}, u32[]{:S(2)}, u32[]{:S(2)}) async-start(bf16[8,3,2,256,128]{4,3,2,1,0:T(8,128)(2,1)} %copy-done.5), calls=%async_computation.3 | async-start | bytes 6291456 | tf_op jit(solution)/shard_map/all_to_all | solution.py:440

commit v3 on v2

--- a/solution.py
+++ b/solution.py
@@ -15,13 +15,18 @@
 LARGE_VMEM = 40 * 1024 * 1024
 
 
+def in_hbm(x):
+    return pltpu.with_memory_space_constraint(x, pltpu.HBM)
+
+
 def from_behind(x, axis, by):
     count = lax.axis_size(axis)
     pairs = [(i, i + by) for i in range(count) if 0 <= i + by < count]
     return lax.ppermute(x, axis, pairs)
 
 
-def pack_kernel(query, key, value, d_out, message, stage, ready, in_sems, out_sems, *, spans):
+def pack_kernel(query, key, value, d_out, *refs, spans):
+    message, stage, ready, in_sems, out_sems = refs[-5:]
     sources = (key, value, query, d_out)
     head_dim = ready.shape[-1] // 2
 
@@ -58,7 +63,7 @@
         send(peer).wait()
 
 
-def pack(arrays, start, chunk_heads, heads_here, peers, head_dim):
+def pack(arrays, start, chunk_heads, heads_here, peers, head_dim, after):
     rows = arrays[0].shape[0]
     shape = (peers, chunk_heads, 2, rows, 2 * head_dim)
     spans = []
@@ -71,9 +76,9 @@
     anywhere = pl.BlockSpec(memory_space=pltpu.HBM)
     return pl.pallas_call(
         functools.partial(pack_kernel, spans=spans),
-        in_specs=[anywhere] * 4,
-        out_specs=pl.BlockSpec(memory_space=pl.ANY),
-        out_shape=jax.ShapeDtypeStruct(shape, dtype),
+        in_specs=[anywhere] * 4 + [pl.BlockSpec(memory_space=pl.ANY)] * len(after),
+        out_specs=anywhere,
+        out_shape=pltpu.HBM(shape, dtype),
         scratch_shapes=[
             pltpu.VMEM((4, peers, rows, width), dtype),
             pltpu.VMEM(shape, dtype),
@@ -82,7 +87,7 @@
         ],
         compiler_params=pltpu.CompilerParams(vmem_limit_bytes=SMALL_VMEM),
         name="pack",
-    )(*arrays)
+    )(*[in_hbm(x) for x in arrays], *after)
 
 
 def unpack_kernel(*refs, chunk, chunks_before, jobs):
@@ -157,9 +162,9 @@
             chunks_before=1 if earlier else 0,
             jobs=jobs,
         ),
-        in_specs=[pl.BlockSpec(memory_space=pl.ANY)] * (chunk + 1 + len(earlier)),
+        in_specs=[pl.BlockSpec(memory_space=pltpu.HBM)] * (chunk + 1 + len(earlier)),
         out_specs=[pl.BlockSpec(memory_space=pltpu.HBM)] * 4,
-        out_shape=[jax.ShapeDtypeStruct((rows, columns), dtype)] * 4,
+        out_shape=[pltpu.HBM((rows, columns), dtype)] * 4,
         input_output_aliases={chunk + 1 + i: i for i in range(len(earlier))},
         scratch_shapes=[pltpu.VMEM(m.shape, dtype) for m in messages]
         + [
@@ -168,7 +173,7 @@
         ],
         compiler_params=pltpu.CompilerParams(vmem_limit_bytes=SMALL_VMEM),
         name="unpack",
-    )(*messages, *earlier)
+    )(*[in_hbm(x) for x in (*messages, *earlier)])
 
 
 def pick_kernel(asked, message, for_next, for_prev, sems, *, block_rows):
@@ -196,13 +201,13 @@
         functools.partial(pick_kernel, block_rows=block_rows),
         in_specs=[
             pl.BlockSpec(memory_space=pltpu.SMEM),
-            pl.BlockSpec(memory_space=pl.ANY),
+            pl.BlockSpec(memory_space=pltpu.HBM),
         ],
-        out_specs=[pl.BlockSpec(memory_space=pl.ANY)] * 2,
+        out_specs=[pl.BlockSpec(memory_space=pltpu.VMEM)] * 2,
         out_shape=[picked, picked],
         scratch_shapes=[pltpu.SemaphoreType.DMA((2 * CROSS,))],
         name="pick",
-    )(asked, message)
+    )(asked, in_hbm(message))
 
 
 def attend_kernel(
@@ -370,7 +375,7 @@
         in_specs=[pl.BlockSpec(memory_space=pltpu.SMEM), inside, inside, inside],
         out_specs=[inside] * 4,
         out_shape=[
-            jax.ShapeDtypeStruct(message.shape, message.dtype),
+            pltpu.HBM(message.shape, message.dtype),
             jax.ShapeDtypeStruct((chunk_heads, blocks, block_rows, lanes), jnp.float32),
             cross_shape,
             cross_shape,
@@ -386,7 +391,7 @@
         ],
         compiler_params=pltpu.CompilerParams(vmem_limit_bytes=LARGE_VMEM),
         name="attend",
-    )(lists, message, came_prev, came_next)
+    )(lists, in_hbm(message), came_prev, came_next)
 
 
 def finish_kernel(asked, own, later, earlier, back_in, back, sums, *, block_rows):
@@ -422,18 +427,18 @@
                 ),
                 cross_spec,
                 cross_spec,
-                pl.BlockSpec(memory_space=pl.ANY),
+                pl.BlockSpec(memory_space=pltpu.HBM),
             ],
             out_specs=pl.BlockSpec(
                 (peers, 1, 1, rows, lanes), lambda head, ids: (0, head, 0, 0, 0)
             ),
             scratch_shapes=[pltpu.VMEM((blocks, block_rows, lanes), jnp.float32)],
         ),
-        out_shape=jax.ShapeDtypeStruct(back.shape, back.dtype),
+        out_shape=pltpu.HBM(back.shape, back.dtype),
         input_output_aliases={4: 0},
         compiler_params=pltpu.CompilerParams(vmem_limit_bytes=SMALL_VMEM),
         name="finish",
-    )(asked, own, later, earlier, back)
+    )(asked, own, later, earlier, in_hbm(back))
 
 
 def exchange(message):
@@ -474,10 +479,10 @@
         jnp.where(pattern < own_base, pos_prev, CROSS + blocks + pos_next),
     )
 
-    came = [
-        exchange(pack(arrays, start, size, heads_here, peers, head_dim))
-        for start, size in zip(starts, sizes)
-    ]
+    came = []
+    for start, size in zip(starts, sizes):
+        after = (asked, local_ids) if came else ()
+        came.append(exchange(pack(arrays, start, size, heads_here, peers, head_dim, after)))
     received = []
     outs = ()
     for message, start, size in zip(came, starts, sizes):

time: 369 us -> 314 us (0.85)
  Pallas kernels: 140 us -> 102 us
  local copies, waits for them, and re-layouts: 23.6 us -> 2.02 us
  waiting for transfers between devices: 134 us -> 146 us
  starting transfers between devices: 61 us -> 55.9 us
    pallas_call x2, Pallas kernels: 51.6 us -> 5.93 us  [pick(): pl.pallas_call(functools.partial(pick_kernel, block_rows=block_rows), in_...]
    unnamed x39 -> x13, local copies, waits for them, and re-layouts: 23.4 us -> 1.77 us
    all_to_all x4, waiting for transfers between devices: 122 us -> 134 us  [exchange(): lax.all_to_all(message, 'seq', split_axis=0, concat_axis=0, tiled=True)]
    ppermute x10, starting transfers between devices: 36.7 us -> 29.9 us  [from_behind(): return lax.ppermute(x, axis, pairs)]
    pallas_call x2, Pallas kernels: 69.2 us -> 74.5 us  [attend(): pl.pallas_call(functools.partial(attend_kernel, block_rows=block_rows, he...]
  transfers between devices with their start and end apart: 14 -> 14, of which waited for: 9 -> 11; matrix products, arithmetic and copies ran while one was open for 1% -> 1% of each run, Pallas kernels for 36% -> 30%
where the time goes in v3:
time: 314 us; the launch traced here: 310 us
  waiting for transfers between devices  146 us (46%)
  Pallas kernels  102 us (32%)
  starting transfers between devices  55.9 us (18%)
    all_to_all x4, waiting for transfers between devices, exchange(): lax.all_to_all(message, 'seq', split_axis=0, concat_axis=0, tiled=True)  134 us
    pallas_call x2, Pallas kernels, attend(): pl.pallas_call(functools.partial(attend_kernel, block_rows=block_rows, he...  74.5 us
    ppermute x10, starting transfers between devices, from_behind(): return lax.ppermute(x, axis, pairs)  29.9 us
    all_to_all x4, starting transfers between devices, exchange(): lax.all_to_all(message, 'seq', split_axis=0, concat_axis=0, tiled=True)  26 us
    ppermute x10, waiting for transfers between devices, from_behind(): return lax.ppermute(x, axis, pairs)  11.5 us
    pallas_call x2, Pallas kernels, unpack(): pl.pallas_call(functools.partial(unpack_kernel, chunk=chunk, chunks_befor...  8.61 us
    pallas_call x2, Pallas kernels, pack(): pl.pallas_call(functools.partial(pack_kernel, spans=spans), in_specs=[any...  7.79 us
  transfers between devices with their start and end apart: 14, of which 11 were waited for; matrix products, arithmetic and copies ran while one was open for 1% of the time, Pallas kernels for 30%

profile of v3, /device:TPU:8, one launch (start us, length us, event | category | flops | bytes accessed | tf_op | source)
XLA Modules:
  0.0 309.9 jit_solution(4094767501600278834)
XLA Ops:
  0.6 3.9 %pack.2 = bf16[8,3,2,256,128]{4,3,2,1,0:T(8,128)(2,1)} custom-call(bf16[256,3072]{1,0:T(8,128)(2,1)} %query.3, bf16[256,3072]{1,0:T(8,128)(2,1)} %key.3, bf16[256,3072]{1,0:T(8,128)(2,1)} %value.3, bf16[256,3072]{1,0:T(8,128)(2,1)} %d_out.3), custom_call_target="tpu_custom_call" | custom-call | tf_op jit(solution)/shard_map/pack/pallas_call | solution.py:77
  4.5 0.0 copy-start.5
  4.5 6.3 %all-to-all-start = ((bf16[8,3,2,256,128]{4,3,2,1,0:T(8,128)(2,1)}), bf16[8,3,2,256,128]{4,3,2,1,0:T(8,128)(2,1)S(1)}, u32[]{:S(2)}, u32[]{:S(2)}) async-start(bf16[8,3,2,256,128]{4,3,2,1,0:T(8,128)(2,1)} %pack.2), calls=%async_computation | async-start | bytes 6291456 | tf_op jit(solution)/shard_map/all_to_all | solution.py:445
  10.8 0.1 copy.26
  10.9 0.1 eq.22
  11.0 0.2 compare_reduce_fusion.1
  11.2 1.2 top_k.17
  12.5 1.3 collective-permute-start
  13.8 1.2 top_k.24
  15.0 3.0 collective-permute-start.1
  18.0 0.1 select_reduce_fusion
  18.1 0.1 copy.31
  18.2 0.1 copy.32
  18.3 0.5 collective-permute-done.1
  18.8 0.1 pad_add_fusion.asked.refs_0_
  18.9 3.9 %pack.3 = bf16[8,3,2,256,128]{4,3,2,1,0:T(8,128)(2,1)} custom-call(bf16[256,3072]{1,0:T(8,128)(2,1)} %query.3, bf16[256,3072]{1,0:T(8,128)(2,1)} %key.3, bf16[256,3072]{1,0:T(8,128)(2,1)} %value.3, bf16[256,3072]{1,0:T(8,128)(2,1)} %d_out.3, s32[8]{0:T(128)S(1)} %pad_add_fusion.asked.refs_0_, s32[6,16,8]{2,1,0:T(8,128)S(1)} %select_select_fusion.refs_1_), custom_call_target="tpu_custom_call" | custom-call | tf_op jit(solution)/shard_map/pack/pallas_call | solution.py:77
  22.8 56.2 %all-to-all-done.message = bf16[8,3,2,256,128]{4,3,2,1,0:T(8,128)(2,1)S(1)} async-done(((bf16[8,3,2,256,128]{4,3,2,1,0:T(8,128)(2,1)}), bf16[8,3,2,256,128]{4,3,2,1,0:T(8,128)(2,1)S(1)}, u32[]{:S(2)}, u32[]{:S(2)}) %all-to-all-start) | async-done | bytes 3145760 | tf_op jit(solution)/shard_map/all_to_all | solution.py:445
  79.1 6.8 %all-to-all-start.2 = ((bf16[8,3,2,256,128]{4,3,2,1,0:T(8,128)(2,1)}), bf16[8,3,2,256,128]{4,3,2,1,0:T(8,128)(2,1)}, u32[]{:S(2)}, u32[]{:S(2)}) async-start(bf16[8,3,2,256,128]{4,3,2,1,0:T(8,128)(2,1)} %pack.3), calls=%async_computation.2 | async-start | bytes 6291456 | tf_op jit(solution)/shard_map/all_to_all | solution.py:445
  85.9 3.0 pick.2
  88.8 1.3 collective-permute-start.2
  90.2 1.3 collective-permute-start.3
  91.5 0.2 collective-permute-done.2.came_prev
  91.7 4.0 %collective-permute-done.3.came_next = bf16[4,3,128,128]{3,2,1,0:T(8,128)(2,1)S(1)} collective-permute-done((bf16[4,3,128,128]{3,2,1,0:T(8,128)(2,1)}, bf16[4,3,128,128]{3,2,1,0:T(8,128)(2,1)S(1)}, u32[]{:S(2)}, u32[]{:S(2)}) %collective-permute-start.3) | collective-permute-done | bytes 393248 | tf_op jit(solution)/shard_map/ppermute | solution.py:25
  95.7 37.2 %attend.2 = (bf16[8,3,2,256,128]{4,3,2,1,0:T(8,128)(2,1)}, f32[3,16,128,128]{3,2,1,0:T(8,128)S(1)}, bf16[4,3,128,128]{3,2,1,0:T(8,128)(2,1)S(1)}, bf16[4,3,128,128]{3,2,1,0:T(8,128)(2,1)S(1)}) custom-call(s32[3,16,8]{2,1,0:T(8,128)S(1)} %get-tuple-element.49.lists, bf16[8,3,2,256,128]{4,3,2,1,0:T(8,128)(2,1)} %copy-done.3, ...), custom_call_target="tpu_custom_call" | custom-call | tf_op jit(solution)/shard_map/attend/pallas_call | solution.py:371
  133.0 1.3 collective-permute-start.4
  134.2 8.9 %collective-permute-start.5 = (bf16[4,3,128,128]{3,2,1,0:T(8,128)(2,1)S(1)}, bf16[4,3,128,128]{3,2,1,0:T(8,128)(2,1)S(1)}, u32[]{:S(2)}, u32[]{:S(2)}) collective-permute-start(bf16[4,3,128,128]{3,2,1,0:T(8,128)(2,1)S(1)} %get-tuple-element.32), channel_id=1, source_target_pairs={{0,8},{8,16},{16,24},{1,9},{9,17},{17,25},{2,10},{10,18},{18,26},{... | collective-permute-start | bytes 1179656 | tf_op jit(solution)/shard_map/ppermute | solution.py:25
  143.2 0.0 collective-permute-done.4.later
  143.2 1.3 collective-permute-done.5.earlier
  144.5 2.6 finish.2
  147.1 6.5 %all-to-all-done.2.message = bf16[8,3,2,256,128]{4,3,2,1,0:T(8,128)(2,1)} async-done(((bf16[8,3,2,256,128]{4,3,2,1,0:T(8,128)(2,1)}), bf16[8,3,2,256,128]{4,3,2,1,0:T(8,128)(2,1)}, u32[]{:S(2)}, u32[]{:S(2)}) %all-to-all-start.2) | async-done | bytes 3145760 | tf_op jit(solution)/shard_map/all_to_all | solution.py:445
  153.6 6.2 %all-to-all-start.1 = ((bf16[8,3,2,256,128]{4,3,2,1,0:T(8,128)(2,1)}), bf16[8,3,2,256,128]{4,3,2,1,0:T(8,128)(2,1)S(1)}, u32[]{:S(2)}, u32[]{:S(2)}) async-start(bf16[8,3,2,256,128]{4,3,2,1,0:T(8,128)(2,1)} %finish.2), calls=%async_computation.1 | async-start | bytes 6291456 | tf_op jit(solution)/shard_map/all_to_all | solution.py:445
  159.8 3.0 pick.3
  162.8 1.4 collective-permute-start.6
  164.2 1.3 collective-permute-start.7
  165.5 0.2 collective-permute-done.6.came_prev
  165.7 4.0 %collective-permute-done.7.came_next = bf16[4,3,128,128]{3,2,1,0:T(8,128)(2,1)S(1)} collective-permute-done((bf16[4,3,128,128]{3,2,1,0:T(8,128)(2,1)}, bf16[4,3,128,128]{3,2,1,0:T(8,128)(2,1)S(1)}, u32[]{:S(2)}, u32[]{:S(2)}) %collective-permute-start.7) | collective-permute-done | bytes 393248 | tf_op jit(solution)/shard_map/ppermute | solution.py:25
  169.6 37.3 %attend.3 = (bf16[8,3,2,256,128]{4,3,2,1,0:T(8,128)(2,1)}, f32[3,16,128,128]{3,2,1,0:T(8,128)S(1)}, bf16[4,3,128,128]{3,2,1,0:T(8,128)(2,1)S(1)}, bf16[4,3,128,128]{3,2,1,0:T(8,128)(2,1)S(1)}) custom-call(s32[3,16,8]{2,1,0:T(8,128)S(1)} %get-tuple-element.48.lists, bf16[8,3,2,256,128]{4,3,2,1,0:T(8,128)(2,1)} %all-to-all-done.2.message, ...), custom_call_target="tpu_custom_call" | custom-call | tf_op jit(solution)/shard_map/attend/pallas_call | solution.py:371
  206.9 1.3 collective-permute-start.8
  208.2 8.8 %collective-permute-start.9 = (bf16[4,3,128,128]{3,2,1,0:T(8,128)(2,1)S(1)}, bf16[4,3,128,128]{3,2,1,0:T(8,128)(2,1)S(1)}, u32[]{:S(2)}, u32[]{:S(2)}) collective-permute-start(bf16[4,3,128,128]{3,2,1,0:T(8,128)(2,1)S(1)} %get-tuple-element.38), channel_id=1, source_target_pairs={{0,8},{8,16},{16,24},{1,9},{9,17},{17,25},{2,10},{10,18},{18,26},{... | collective-permute-start | bytes 1179656 | tf_op jit(solution)/shard_map/ppermute | solution.py:25
  217.1 0.0 collective-permute-done.8.later
  217.1 1.3 collective-permute-done.9.earlier
  218.4 2.6 finish.3
  220.9 7.3 %all-to-all-done.1.refs_0_ = bf16[8,3,2,256,128]{4,3,2,1,0:T(8,128)(2,1)S(1)} async-done(((bf16[8,3,2,256,128]{4,3,2,1,0:T(8,128)(2,1)}), bf16[8,3,2,256,128]{4,3,2,1,0:T(8,128)(2,1)S(1)}, u32[]{:S(2)}, u32[]{:S(2)}) %all-to-all-start.1) | async-done | bytes 3145760 | tf_op jit(solution)/shard_map/all_to_all | solution.py:445
  228.2 1.7 copy-done.4
  229.9 6.8 %all-to-all-start.3 = ((bf16[8,3,2,256,128]{4,3,2,1,0:T(8,128)(2,1)}), bf16[8,3,2,256,128]{4,3,2,1,0:T(8,128)(2,1)}, u32[]{:S(2)}, u32[]{:S(2)}) async-start(bf16[8,3,2,256,128]{4,3,2,1,0:T(8,128)(2,1)} %finish.3), calls=%async_computation.3 | async-start | bytes 6291456 | tf_op jit(solution)/shard_map/all_to_all | solution.py:445
  236.7 3.3 %unpack.2 = (bf16[256,3072]{1,0:T(8,128)(2,1)}, bf16[256,3072]{1,0:T(8,128)(2,1)}, bf16[256,3072]{1,0:T(8,128)(2,1)}, bf16[256,3072]{1,0:T(8,128)(2,1)}) custom-call(bf16[8,3,2,256,128]{4,3,2,1,0:T(8,128)(2,1)} %copy-done.4), custom_call_target="tpu_custom_call" | custom-call | tf_op jit(solution)/shard_map/unpack/pallas_call | solution.py:158
  240.0 64.4 %all-to-all-done.3.refs_1_ = bf16[8,3,2,256,128]{4,3,2,1,0:T(8,128)(2,1)} async-done(((bf16[8,3,2,256,128]{4,3,2,1,0:T(8,128)(2,1)}), bf16[8,3,2,256,128]{4,3,2,1,0:T(8,128)(2,1)}, u32[]{:S(2)}, u32[]{:S(2)}) %all-to-all-start.3) | async-done | bytes 3145760 | tf_op jit(solution)/shard_map/all_to_all | solution.py:445
  304.4 5.3 %unpack.3 = (bf16[256,3072]{1,0:T(8,128)(2,1)}, bf16[256,3072]{1,0:T(8,128)(2,1)}, bf16[256,3072]{1,0:T(8,128)(2,1)}, bf16[256,3072]{1,0:T(8,128)(2,1)}) custom-call(bf16[8,3,2,256,128]{4,3,2,1,0:T(8,128)(2,1)} %copy-done.4, ...), custom_call_target="tpu_custom_call", output_to_operand_aliasing={{0}: (2, {}), {1}: (3, {}), {2}: (4, {}), {3}: (5, {})} | custom-call | tf_op jit(solution)/shard_map/unpack/pallas_call | solution.py:158
  (20 shorter events, 0.1 us)
Async XLA Ops:
  4.5 6.3 %copy-start.5 = (s32[6,16,8]{1,2,0:T(8,128)S(1)}, s32[6,16,8]{1,2,0:T(8,128)}, u32[]{:S(2)}) copy-start(s32[6,16,8]{1,2,0:T(8,128)} %param.9) | copy-start | bytes 9220
  4.5 74.5 %all-to-all-start = ((bf16[8,3,2,256,128]{4,3,2,1,0:T(8,128)(2,1)}), bf16[8,3,2,256,128]{4,3,2,1,0:T(8,128)(2,1)S(1)}, u32[]{:S(2)}, u32[]{:S(2)}) async-start(bf16[8,3,2,256,128]{4,3,2,1,0:T(8,128)(2,1)} %pack.2), calls=%async_computation | async-start | bytes 6291456 | tf_op jit(solution)/shard_map/all_to_all | solution.py:445
  12.5 5.9 %collective-permute-start = (s32[4]{0:T(128)S(1)}, s32[4]{0:T(128)S(1)}, u32[]{:S(2)}, u32[]{:S(2)}) collective-permute-start(s32[4]{0:T(128)S(1)} %get-tuple-element.51), channel_id=1, source_target_pairs={{8,0},{16,8},{24,16},{9,1},{17,9},{25,17},{10,2},{18,10},{26,18},{... | collective-permute-start | bytes 56 | tf_op jit(solution)/shard_map/ppermute | solution.py:25
  15.0 3.8 %collective-permute-start.1 = (s32[4]{0:T(128)S(1)}, s32[4]{0:T(128)S(1)}, u32[]{:S(2)}, u32[]{:S(2)}) collective-permute-start(s32[4]{0:T(128)S(1)} %get-tuple-element.53), channel_id=1, source_target_pairs={{0,8},{8,16},{16,24},{1,9},{9,17},{17,25},{2,10},{10,18},{18,26},{... | collective-permute-start | bytes 56 | tf_op jit(solution)/shard_map/ppermute | solution.py:25
  18.9 3.9 %copy-start = (s32[8]{0:T(128)}, s32[8]{0:T(128)S(1)}, u32[]{:S(2)}) copy-start(s32[8]{0:T(128)S(1)} %pad_add_fusion.asked.refs_0_) | copy-start | bytes 100
  79.1 6.8 %copy-start.3 = (bf16[8,3,2,256,128]{4,3,2,1,0:T(8,128)(2,1)}, bf16[8,3,2,256,128]{4,3,2,1,0:T(8,128)(2,1)S(1)}, u32[]{:S(2)}) copy-start(bf16[8,3,2,256,128]{4,3,2,1,0:T(8,128)(2,1)S(1)} %all-to-all-done.message) | copy-start | bytes 9437188
  79.1 74.5 %all-to-all-start.2 = ((bf16[8,3,2,256,128]{4,3,2,1,0:T(8,128)(2,1)}), bf16[8,3,2,256,128]{4,3,2,1,0:T(8,128)(2,1)}, u32[]{:S(2)}, u32[]{:S(2)}) async-start(bf16[8,3,2,256,128]{4,3,2,1,0:T(8,128)(2,1)} %pack.3), calls=%async_computation.2 | async-start | bytes 6291456 | tf_op jit(solution)/shard_map/all_to_all | solution.py:445
  85.9 58.6 %copy-start.1 = (s32[8]{0:T(128)S(1)}, s32[8]{0:T(128)}, u32[]{:S(2)}) copy-start(s32[8]{0:T(128)} %copy-done) | copy-start | bytes 100
  88.8 2.8 collective-permute-start.2
  90.2 5.6 %collective-permute-start.3 = (bf16[4,3,128,128]{3,2,1,0:T(8,128)(2,1)}, bf16[4,3,128,128]{3,2,1,0:T(8,128)(2,1)S(1)}, u32[]{:S(2)}, u32[]{:S(2)}) collective-permute-start(bf16[4,3,128,128]{3,2,1,0:T(8,128)(2,1)} %get-tuple-element.29), channel_id=1, source_target_pairs={{8,0},{16,8},{24,16},{9,1},{17,9},{25,17},{10,2},{18,10},{26,18},{... | collective-permute-start | bytes 1179656 | tf_op jit(solution)/shard_map/ppermute | solution.py:25
  133.0 10.2 %collective-permute-start.4 = (bf16[4,3,128,128]{3,2,1,0:T(8,128)(2,1)S(1)}, bf16[4,3,128,128]{3,2,1,0:T(8,128)(2,1)S(1)}, u32[]{:S(2)}, u32[]{:S(2)}) collective-permute-start(bf16[4,3,128,128]{3,2,1,0:T(8,128)(2,1)S(1)} %get-tuple-element.31), channel_id=1, source_target_pairs={{8,0},{16,8},{24,16},{9,1},{17,9},{25,17},{10,2},{18,10},{26,18},{... | collective-permute-start | bytes 1179656 | tf_op jit(solution)/shard_map/ppermute | solution.py:25
  134.2 10.3 %collective-permute-start.5 = (bf16[4,3,128,128]{3,2,1,0:T(8,128)(2,1)S(1)}, bf16[4,3,128,128]{3,2,1,0:T(8,128)(2,1)S(1)}, u32[]{:S(2)}, u32[]{:S(2)}) collective-permute-start(bf16[4,3,128,128]{3,2,1,0:T(8,128)(2,1)S(1)} %get-tuple-element.32), channel_id=1, source_target_pairs={{0,8},{8,16},{16,24},{1,9},{9,17},{17,25},{2,10},{10,18},{18,26},{... | collective-permute-start | bytes 1179656 | tf_op jit(solution)/shard_map/ppermute | solution.py:25
  153.6 74.6 %all-to-all-start.1 = ((bf16[8,3,2,256,128]{4,3,2,1,0:T(8,128)(2,1)}), bf16[8,3,2,256,128]{4,3,2,1,0:T(8,128)(2,1)S(1)}, u32[]{:S(2)}, u32[]{:S(2)}) async-start(bf16[8,3,2,256,128]{4,3,2,1,0:T(8,128)(2,1)} %finish.2), calls=%async_computation.1 | async-start | bytes 6291456 | tf_op jit(solution)/shard_map/all_to_all | solution.py:445
  159.8 58.6 %copy-start.2 = (s32[8]{0:T(128)S(1)}, s32[8]{0:T(128)}, u32[]{:S(2)}) copy-start(s32[8]{0:T(128)} %copy-done) | copy-start | bytes 100
  162.8 2.9 collective-permute-start.6
  164.2 5.5 %collective-permute-start.7 = (bf16[4,3,128,128]{3,2,1,0:T(8,128)(2,1)}, bf16[4,3,128,128]{3,2,1,0:T(8,128)(2,1)S(1)}, u32[]{:S(2)}, u32[]{:S(2)}) collective-permute-start(bf16[4,3,128,128]{3,2,1,0:T(8,128)(2,1)} %get-tuple-element.35), channel_id=1, source_target_pairs={{8,0},{16,8},{24,16},{9,1},{17,9},{25,17},{10,2},{18,10},{26,18},{... | collective-permute-start | bytes 1179656 | tf_op jit(solution)/shard_map/ppermute | solution.py:25
  206.9 10.1 %collective-permute-start.8 = (bf16[4,3,128,128]{3,2,1,0:T(8,128)(2,1)S(1)}, bf16[4,3,128,128]{3,2,1,0:T(8,128)(2,1)S(1)}, u32[]{:S(2)}, u32[]{:S(2)}) collective-permute-start(bf16[4,3,128,128]{3,2,1,0:T(8,128)(2,1)S(1)} %get-tuple-element.37), channel_id=1, source_target_pairs={{8,0},{16,8},{24,16},{9,1},{17,9},{25,17},{10,2},{18,10},{26,18},{... | collective-permute-start | bytes 1179656 | tf_op jit(solution)/shard_map/ppermute | solution.py:25
  208.2 10.1 %collective-permute-start.9 = (bf16[4,3,128,128]{3,2,1,0:T(8,128)(2,1)S(1)}, bf16[4,3,128,128]{3,2,1,0:T(8,128)(2,1)S(1)}, u32[]{:S(2)}, u32[]{:S(2)}) collective-permute-start(bf16[4,3,128,128]{3,2,1,0:T(8,128)(2,1)S(1)} %get-tuple-element.38), channel_id=1, source_target_pairs={{0,8},{8,16},{16,24},{1,9},{9,17},{17,25},{2,10},{10,18},{18,26},{... | collective-permute-start | bytes 1179656 | tf_op jit(solution)/shard_map/ppermute | solution.py:25
  228.2 1.7 copy-start.4
  229.9 74.5 %all-to-all-start.3 = ((bf16[8,3,2,256,128]{4,3,2,1,0:T(8,128)(2,1)}), bf16[8,3,2,256,128]{4,3,2,1,0:T(8,128)(2,1)}, u32[]{:S(2)}, u32[]{:S(2)}) async-start(bf16[8,3,2,256,128]{4,3,2,1,0:T(8,128)(2,1)} %finish.3), calls=%async_computation.3 | async-start | bytes 6291456 | tf_op jit(solution)/shard_map/all_to_all | solution.py:445

commit v4 on v3

v4 whole, which is shorter than its diff:
```python
import functools
import math

import jax
import jax.numpy as jnp
from jax import lax
from jax.experimental import pallas as pl
from jax.experimental.pallas import tpu as pltpu
from jax.sharding import PartitionSpec as P

CROSS = 4
CHUNKS = 2
LANES = 128
SMALL_VMEM = 24 * 1024 * 1024
LARGE_VMEM = 40 * 1024 * 1024


def in_hbm(x):
    return pltpu.with_memory_space_constraint(x, pltpu.HBM)


def from_behind(x, axis, by):
    count = lax.axis_size(axis)
    pairs = [(i, i + by) for i in range(count) if 0 <= i + by < count]
    return lax.ppermute(x, axis, pairs)


def hold_kernel(*refs):
    del refs


def hold(arrays, after):
    count = len(arrays)
    anywhere = pl.BlockSpec(memory_space=pltpu.HBM)
    return pl.pallas_call(
        hold_kernel,
        in_specs=[anywhere] * (count + len(after)),
        out_specs=[anywhere] * count,
        out_shape=[pltpu.HBM(x.shape, x.dtype) for x in arrays],
        input_output_aliases={i: i for i in range(count)},
        name="hold",
    )(*[in_hbm(x) for x in (*arrays, *after)])


def exchange(messages, before=None):
    count = len(messages)
    half = count // 2
    messages = list(messages)
    if before is not None:
        messages[1:half] = hold(messages[1:half], before[1:half])
        messages[half:] = hold(messages[half:], before[-1:])
    received = list(messages)
    for k in range(count - 1, 0, -1):
        pairs = [(i, i ^ k) for i in range(count)]
        received[k] = lax.ppermute(messages[k], "seq", pairs)
    return received


def pack_kernel(me, query, key, value, d_out, *refs, first, heads, peers, per_peer, head_dim):
    messages = refs[-4 - peers : -4]
    stage, ready, in_sems, out_sems = refs[-4:]
    sources = (key, value, query, d_out)
    aligned = per_peer % LANES == 0
    order = range(peers - 1, -1, -1)

    def span(item):
        if aligned:
            base, begin = pl.multiple_of((me[0] ^ item) * per_peer, LANES), first
        else:
            base, begin = 0, item * per_peer + first
        low = begin // LANES * LANES
        high = -(-(begin + heads * head_dim) // LANES) * LANES
        return base + low, high - low, begin - low

    def fetch(item, i):
        low, width, _ = span(item)
        return pltpu.make_async_copy(
            sources[i].at[:, pl.ds(low, width)],
            stage.at[i, item, :, pl.ds(0, width)],
            in_sems.at[i, item],
        )

    def send(item):
        slot = item if aligned else me[0] ^ item
        return pltpu.make_async_copy(ready.at[slot], messages[item], out_sems.at[item])

    for item in order:
        for i in range(4):
            fetch(item, i).start()
    for item in order:
        for i in range(4):
            fetch(item, i).wait()
        at = span(item)[2]
        for head in range(heads):
            lanes = slice(at + head * head_dim, at + (head + 1) * head_dim)
            for kind in range(2):
                ready[item, head, kind] = jnp.concatenate(
                    [stage[2 * kind, item, :, lanes], stage[2 * kind + 1, item, :, lanes]],
                    axis=1,
                )
        if aligned:
            send(item).start()
    if not aligned:
        for item in order:
            send(item).start()
    for item in order:
        send(item).wait()


def pack(me, arrays, start, heads, heads_here, peers, head_dim, after):
    rows = arrays[0].shape[0]
    dtype = arrays[0].dtype
    shape = (heads, 2, rows, 2 * head_dim)
    width = (-(-heads * head_dim // LANES) + 1) * LANES
    anywhere = pl.BlockSpec(memory_space=pltpu.HBM)
    return pl.pallas_call(
        functools.partial(
            pack_kernel,
            first=start * head_dim,
            heads=heads,
            peers=peers,
            per_peer=heads_here * head_dim,
            head_dim=head_dim,
        ),
        in_specs=[pl.BlockSpec(memory_space=pltpu.SMEM)]
        + [anywhere] * 4
        + [pl.BlockSpec(memory_space=pl.ANY)] * len(after),
        out_specs=[anywhere] * peers,
        out_shape=[pltpu.HBM(shape, dtype)] * peers,
        scratch_shapes=[
            pltpu.VMEM((4, peers, rows, width), dtype),
            pltpu.VMEM((peers,) + shape, dtype),
            pltpu.SemaphoreType.DMA((4, peers)),
            pltpu.SemaphoreType.DMA((peers,)),
        ],
        compiler_params=pltpu.CompilerParams(vmem_limit_bytes=SMALL_VMEM),
        name="pack",
    )(me, *[in_hbm(x) for x in arrays], *after)


def unpack_kernel(me, *refs, chunk, peers, earlier, jobs):
    groups = [refs[c * peers : (c + 1) * peers] for c in range(chunk + 1)]
    outs = refs[(chunk + 1) * peers + earlier :][:4]
    stages = refs[-3 - chunk - 1 : -3]
    ready, in_sems, out_sems = refs[-3:]
    head_dim = ready.shape[-1] // 2
    used = sorted({(which, peer) for job in jobs for which, peer, _ in job[1:]})
    chunks_used = sorted({which for which, _ in used})
    heads_used = {
        c: sorted({head for job in jobs for which, _, head in job[1:] if which == c})
        for c in chunks_used
    }

    def fetch(which, item, slot):
        heads = heads_used[which]
        some = pl.ds(heads[0], heads[-1] - heads[0] + 1)
        return pltpu.make_async_copy(
            groups[which][item].at[some],
            stages[which].at[slot, some],
            in_sems.at[which, slot],
        )

    def send(job, i):
        tile = jobs[job][0]
        return pltpu.make_async_copy(
            ready.at[i, job],
            outs[i].at[:, pl.ds(tile * LANES, LANES)],
            out_sems.at[4 * job + i],
        )

    for item in range(peers):
        for which in chunks_used:
            fetch(which, item, me[0] ^ item).start()
    waited = set()

    def wait_for(which, peer):
        if (which, peer) not in waited:
            fetch(which, 0, peer).wait()
            waited.add((which, peer))

    for job, (tile, left, right) in enumerate(jobs):
        for which, peer, _ in (left, right):
            wait_for(which, peer)
        sides = [stages[which][peer, head] for which, peer, head in (left, right)]
        for i, (kind, at) in enumerate(((1, head_dim), (1, 0), (0, 0), (0, head_dim))):
            ready[i, job] = jnp.concatenate(
                [side[kind, :, at : at + head_dim] for side in sides], axis=1
            )
            send(job, i).start()
    for which in chunks_used:
        for peer in range(peers):
            wait_for(which, peer)
    for job in range(len(jobs)):
        for i in range(4):
            send(job, i).wait()


def unpack(me, messages, starts, heads_here, earlier):
    chunk = len(messages) - 1
    peers = len(messages[0])
    _, _, rows, pair_dim = messages[0][0].shape
    head_dim = pair_dim // 2
    columns = peers * heads_here * head_dim
    dtype = messages[0][0].dtype

    def place_of(head):
        peer, local_head = divmod(head, heads_here)
        which = max(c for c, start in enumerate(starts) if start <= local_head)
        return which, peer, local_head - starts[which]

    jobs = []
    for tile in range(columns // LANES):
        left, right = place_of(2 * tile), place_of(2 * tile + 1)
        if max(left[0], right[0]) == chunk:
            jobs.append((tile, left, right))
    if not jobs:
        return earlier
    flat = [x for group in messages for x in group]
    anywhere = pl.BlockSpec(memory_space=pltpu.HBM)
    return pl.pallas_call(
        functools.partial(
            unpack_kernel, chunk=chunk, peers=peers, earlier=len(earlier), jobs=jobs
        ),
        in_specs=[pl.BlockSpec(memory_space=pltpu.SMEM)]
        + [anywhere] * (len(flat) + len(earlier)),
        out_specs=[anywhere] * 4,
        out_shape=[pltpu.HBM((rows, columns), dtype)] * 4,
        input_output_aliases={1 + len(flat) + i: i for i in range(len(earlier))},
        scratch_shapes=[pltpu.VMEM((peers,) + m[0].shape, dtype) for m in messages]
        + [
            pltpu.VMEM((4, len(jobs), rows, LANES), dtype),
            pltpu.SemaphoreType.DMA((chunk + 1, peers)),
            pltpu.SemaphoreType.DMA((4 * len(jobs),)),
        ],
        compiler_params=pltpu.CompilerParams(vmem_limit_bytes=SMALL_VMEM),
        name="unpack",
    )(me, *[in_hbm(x) for x in (*flat, *earlier)])


def pick_kernel(me, asked, *refs, block_rows):
    peers = len(refs) - 4
    for_next, for_prev, stage, sems = refs[peers:]
    rows = stage.shape[2]
    each = rows // block_rows

    def fetch(item):
        slot = me[0] ^ item
        return pltpu.make_async_copy(refs[item].at[:, 0], stage.at[slot], sems.at[item])

    for item in range(peers):
        fetch(item).start()
    for item in range(peers):
        fetch(item).wait()
    for i in range(2 * CROSS):
        target = for_next if i < CROSS else for_prev
        peer = lax.div(asked[i], each)
        start = pl.multiple_of(lax.rem(asked[i], each) * block_rows, block_rows)
        target[i % CROSS] = stage[peer, :, pl.ds(start, block_rows)]


def pick(me, messages, asked, block_rows):
    heads, _, rows, lanes = messages[0].shape
    dtype = messages[0].dtype
    peers = len(messages)
    picked = jax.ShapeDtypeStruct((CROSS, heads, block_rows, lanes), dtype)
    return pl.pallas_call(
        functools.partial(pick_kernel, block_rows=block_rows),
        in_specs=[pl.BlockSpec(memory_space=pltpu.SMEM)] * 2
        + [pl.BlockSpec(memory_space=pltpu.HBM)] * peers,
        out_specs=[pl.BlockSpec(memory_space=pltpu.VMEM)] * 2,
        out_shape=[picked, picked],
        scratch_shapes=[
            pltpu.VMEM((peers, heads, rows, lanes), dtype),
            pltpu.SemaphoreType.DMA((peers,)),
        ],
        compiler_params=pltpu.CompilerParams(vmem_limit_bytes=SMALL_VMEM),
        name="pick",
    )(me, asked, *[in_hbm(x) for x in messages])


def attend_kernel(me, lists, came_prev, came_next, *refs, block_rows, head_dim, per_list):
    peers = len(refs) - 13
    messages = refs[:peers]
    back, own, to_prev, to_next = refs[peers : peers + 4]
    message, table, turned, sums, both_even, both_odd, low_even, low_odd, sems = refs[peers + 4 :]
    _, heads, _, rows, lanes = message.shape
    each = rows // block_rows
    blocks = peers * each
    window = blocks + 2 * CROSS
    units = heads * blocks
    keys = per_list * block_rows
    scaling = head_dim ** (-0.5)
    exponent = scaling * math.log2(math.e)
    both = (both_even, both_odd)
    low = (low_even, low_odd)
    step_rows = 64

    def fetch(item):
        slot = me[0] ^ item
        return pltpu.make_async_copy(messages[item], message.at[slot], sems.at[item])

    for item in range(peers):
        fetch(item).start()
    for item in range(peers):
        fetch(item).wait()
    for head in range(heads):
        for i in range(CROSS):
            table[head, i] = came_prev[i, head]
            table[head, CROSS + blocks + i] = came_next[i, head]

        def fill(peer, carry):
            for i in range(each):
                table[head, CROSS + peer * each + i] = message[
                    peer, head, 0, i * block_rows : (i + 1) * block_rows
                ]
            return carry

        lax.fori_loop(0, peers, fill, 0)

        def turn(i, carry):
            turned[head, i] = table[head, i].T
            sums[head, i] = jnp.zeros(sums.shape[2:], sums.dtype)
            return carry

        lax.fori_loop(0, window, turn, 0)

    left = lax.broadcasted_iota(jnp.int32, (block_rows, lanes), 1) < head_dim

    def locate(unit):
        head = lax.div(unit, blocks)
        block = lax.rem(unit, blocks)
        ids = [lists[head, block, j] for j in range(per_list)]
        peer = lax.div(block, each)
        start = pl.multiple_of(lax.rem(block, each) * block_rows, block_rows)
        return head, ids, peer, pl.ds(start, block_rows)

    def apart_of(head, peer, here):
        query_grad = message[peer, head, 1, here]
        nothing = jnp.zeros_like(query_grad)
        return jnp.concatenate(
            [jnp.where(left, query_grad, nothing), jnp.where(left, nothing, query_grad)],
            axis=0,
        )

    def score(unit, slot):
        head, ids, peer, here = locate(unit)
        key_value = jnp.concatenate([table[head, i] for i in ids], axis=0)
        both[slot][...] = lax.dot_general(
            key_value,
            apart_of(head, peer, here),
            (((1,), (1,)), ((), ())),
            preferred_element_type=jnp.float32,
        )

    def soften(slot):
        source, target = both[slot], low[slot]
        parts = [slice(i, i + step_rows) for i in range(0, keys, step_rows)]
        top = source[parts[0], :block_rows]
        for part in parts[1:]:
            top = jnp.maximum(top, source[part, :block_rows])
        top = jnp.max(top, axis=0, keepdims=True)
        total = jnp.zeros((step_rows, block_rows), jnp.float32)
        mixed = jnp.zeros((step_rows, block_rows), jnp.float32)
        for part in parts:
            raised = jnp.exp2((source[part, :block_rows] - top) * exponent)
            source[part, :block_rows] = raised
            total += raised
            mixed += raised * source[part, block_rows:]
        inverse = 1.0 / jnp.sum(total, axis=0, keepdims=True)
        correction = jnp.sum(mixed, axis=0, keepdims=True) * inverse
        for part in parts:
            weights = source[part, :block_rows] * inverse
            target[part, block_rows:] = weights.astype(jnp.bfloat16)
            target[part, :block_rows] = (
                weights * (source[part, block_rows:] - correction)
            ).astype(jnp.bfloat16)

    def combine(unit, slot):
        head, ids, peer, here = locate(unit)
        products = low[slot][...]
        terms = jnp.dot(
            products, apart_of(head, peer, here), preferred_element_type=jnp.float32
        )
        for j, i in enumerate(ids):
            sums[head, i] += terms[j * block_rows : (j + 1) * block_rows]
        key_value = jnp.concatenate([turned[head, i] for i in ids], axis=1)
        out = jnp.dot(key_value, products, preferred_element_type=jnp.float32)
        out = jnp.concatenate(
            [out[:head_dim, :block_rows] * scaling, out[head_dim:, block_rows:]], axis=0
        )
        back[peer, head, here] = out.T.astype(back.dtype)

    score(0, 0)
    score(1, 1)
    soften(0)

    def step(i, carry):
        for slot in range(2):
            unit = 2 * i + slot
            combine(unit - 2, slot)
            score(unit, slot)
            soften(1 - slot)
        return carry

    lax.fori_loop(1, units // 2, step, 0)
    combine(units - 2, 0)
    soften(1)
    combine(units - 1, 1)

    factor = jnp.where(left, scaling, 1.0)
    for head in range(heads):
        for i in range(CROSS):
            to_prev[i, head] = (sums[head, i] * factor).astype(to_prev.dtype)
            to_next[i, head] = (sums[head, CROSS + blocks + i] * factor).astype(to_next.dtype)

        def finish(i, carry):
            own[head, i] = sums[head, CROSS + i] * factor
            return carry

        lax.fori_loop(0, blocks, finish, 0)


def attend(me, messages, came_prev, came_next, lists, block_rows):
    heads, _, rows, lanes = messages[0].shape
    dtype = messages[0].dtype
    peers = len(messages)
    per_list = lists.shape[-1]
    keys = per_list * block_rows
    blocks = peers * rows // block_rows
    window = blocks + 2 * CROSS
    inside = pl.BlockSpec(memory_space=pltpu.VMEM)
    scalars = pl.BlockSpec(memory_space=pltpu.SMEM)
    cross_shape = jax.ShapeDtypeStruct(came_prev.shape, dtype)
    return pl.pallas_call(
        functools.partial(
            attend_kernel, block_rows=block_rows, head_dim=lanes // 2, per_list=per_list
        ),
        in_specs=[scalars, scalars, inside, inside]
        + [pl.BlockSpec(memory_space=pltpu.HBM)] * peers,
        out_specs=[inside] * 4,
        out_shape=[
            pltpu.VMEM((peers, heads, rows, lanes), dtype),
            pltpu.VMEM((heads, blocks, block_rows, lanes), jnp.float32),
            cross_shape,
            cross_shape,
        ],
        scratch_shapes=[
            pltpu.VMEM((peers,) + messages[0].shape, dtype),
            pltpu.VMEM((heads, window, block_rows, lanes), dtype),
            pltpu.VMEM((heads, window, lanes, block_rows), dtype),
            pltpu.VMEM((heads, window, block_rows, lanes), jnp.float32),
            pltpu.VMEM((keys, 2 * block_rows), jnp.float32),
            pltpu.VMEM((keys, 2 * block_rows), jnp.float32),
            pltpu.VMEM((keys, 2 * block_rows), dtype),
            pltpu.VMEM((keys, 2 * block_rows), dtype),
            pltpu.SemaphoreType.DMA((peers,)),
        ],
        compiler_params=pltpu.CompilerParams(vmem_limit_bytes=LARGE_VMEM),
        name="attend",
    )(me, lists, came_prev, came_next, *[in_hbm(x) for x in messages])


def finish_kernel(me, asked, back, own, later, earlier, *refs, block_rows):
    peers = len(refs) - 3
    messages = refs[:peers]
    sums, ready, sems = refs[peers:]
    _, heads, _, rows, _ = ready.shape
    each = rows // block_rows

    def send(item, head):
        return pltpu.make_async_copy(
            ready.at[me[0] ^ item, head], messages[item].at[head], sems.at[item, head]
        )

    for head in range(heads):
        sums[...] = own[head]
        for i in range(CROSS):
            sums[asked[i]] += later[i, head].astype(jnp.float32)
        for i in range(CROSS):
            sums[asked[CROSS + i]] += earlier[i, head].astype(jnp.float32)
        for peer in range(peers):
            ready[peer, head, 1] = back[peer, head]
            for i in range(each):
                ready[peer, head, 0, i * block_rows : (i + 1) * block_rows] = sums[
                    peer * each + i
                ].astype(ready.dtype)
        for item in range(peers - 1, -1, -1):
            send(item, head).start()
    for head in range(heads):
        for item in range(peers):
            send(item, head).wait()


def finish(me, back, own, later, earlier, asked):
    peers, heads, rows, lanes = back.shape
    _, blocks, block_rows, _ = own.shape
    inside = pl.BlockSpec(memory_space=pltpu.VMEM)
    scalars = pl.BlockSpec(memory_space=pltpu.SMEM)
    shape = (heads, 2, rows, lanes)
    return pl.pallas_call(
        functools.partial(finish_kernel, block_rows=block_rows),
        in_specs=[scalars, scalars] + [inside] * 4,
        out_specs=[pl.BlockSpec(memory_space=pltpu.HBM)] * peers,
        out_shape=[pltpu.HBM(shape, back.dtype)] * peers,
        scratch_shapes=[
            pltpu.VMEM((blocks, block_rows, lanes), jnp.float32),
            pltpu.VMEM((peers,) + shape, back.dtype),
            pltpu.SemaphoreType.DMA((peers, heads)),
        ],
        compiler_params=pltpu.CompilerParams(vmem_limit_bytes=SMALL_VMEM),
        name="finish",
    )(
        me,
        asked,
        pltpu.with_memory_space_constraint(back, pltpu.VMEM),
        pltpu.with_memory_space_constraint(own, pltpu.VMEM),
        later,
        earlier,
    )


def local(query, key, value, d_out, pattern):
    heads_here, blocks, _ = pattern.shape
    peers = lax.axis_size("seq")
    rows, columns = query.shape
    head_dim = columns // (peers * heads_here)
    block_rows = rows * peers // blocks
    chunks = min(CHUNKS, heads_here)
    starts = [-(-heads_here * i // chunks) for i in range(chunks)]
    sizes = [end - start for start, end in zip(starts, starts[1:] + [heads_here])]
    arrays = (query, key, value, d_out)

    own_base = lax.axis_index("slab") * blocks
    block_ids = jnp.arange(blocks, dtype=jnp.int32)
    flat_lists = pattern.reshape(-1)
    reverse_rank = blocks - 1 - block_ids
    hits_prev = jnp.any(flat_lists[:, None] == (own_base - blocks + block_ids)[None, :], axis=0)
    hits_next = jnp.any(flat_lists[:, None] == (own_base + blocks + block_ids)[None, :], axis=0)
    need_prev = lax.top_k(hits_prev.astype(jnp.int32) * blocks + reverse_rank, CROSS)[1]
    need_next = lax.top_k(hits_next.astype(jnp.int32) * blocks + reverse_rank, CROSS)[1]
    asked_next = from_behind(need_prev, "slab", -1)
    asked_prev = from_behind(need_next, "slab", 1)
    asked = jnp.concatenate([asked_next, asked_prev])
    rank_ids = jnp.arange(CROSS, dtype=jnp.int32)
    prev_global = own_base - blocks + need_prev
    next_global = own_base + blocks + need_next
    pos_prev = jnp.sum(jnp.where(pattern[..., None] == prev_global, rank_ids, 0), axis=-1)
    pos_next = jnp.sum(jnp.where(pattern[..., None] == next_global, rank_ids, 0), axis=-1)
    in_own = (pattern >= own_base) & (pattern < own_base + blocks)
    local_ids = jnp.where(
        in_own,
        CROSS + pattern - own_base,
        jnp.where(pattern < own_base, pos_prev, CROSS + blocks + pos_next),
    )

    me = lax.axis_index("seq").astype(jnp.int32).reshape(1)
    came = []
    for start, size in zip(starts, sizes):
        after = (asked, local_ids) if came else ()
        packed = pack(me, arrays, start, size, heads_here, peers, head_dim, after)
        came.append(exchange(packed, came[-1] if came else None))
    received = []
    outs = ()
    for messages, start, size in zip(came, starts, sizes):
        for_next, for_prev = pick(me, messages, asked, block_rows)
        came_prev = from_behind(for_next, "slab", 1)
        came_next = from_behind(for_prev, "slab", -1)
        back, own, to_prev, to_next = attend(
            me, messages, came_prev, came_next, local_ids[start : start + size], block_rows
        )
        later = from_behind(to_prev, "slab", -1)
        earlier = from_behind(to_next, "slab", 1)
        received.append(exchange(finish(me, back, own, later, earlier, asked)))
        outs = unpack(me, received, starts, heads_here, outs)
    return tuple(outs)


def solution(mesh):
    tokens = P(("slab", "seq"), None)
    return jax.shard_map(
        local,
        mesh=mesh,
        in_specs=(tokens, tokens, tokens, tokens, P("seq", "slab", None)),
        out_specs=(tokens, tokens, tokens, tokens),
        check_vma=False,
    )
```

time: 314 us -> 399 us (1.27)
  waiting for transfers between devices: 146 us -> 233 us
  Pallas kernels: 102 us -> 97.7 us
  starting transfers between devices: 55.9 us -> 60 us
    ppermute x0 -> x28, waiting for transfers between devices: none -> 232 us  [exchange(): received[k] = lax.ppermute(messages[k], 'seq', pairs)]
    all_to_all x4 -> x0, waiting for transfers between devices: 134 us -> none  [exchange(): lax.all_to_all(message, 'seq', split_axis=0, concat_axis=0, tiled=True)]
    ppermute x0 -> x28, starting transfers between devices: none -> 39.5 us  [exchange(): received[k] = lax.ppermute(messages[k], 'seq', pairs)]
    all_to_all x4 -> x0, starting transfers between devices: 26 us -> none  [exchange(): lax.all_to_all(message, 'seq', split_axis=0, concat_axis=0, tiled=True)]
    ppermute x10, waiting for transfers between devices: 11.5 us -> 0.82 us  [from_behind(): return lax.ppermute(x, axis, pairs)]
    ppermute x10, starting transfers between devices: 29.9 us -> 20.5 us  [from_behind(): return lax.ppermute(x, axis, pairs)]
    pallas_call x6 -> x8, Pallas kernels: 21.6 us -> 20.6 us  [the longest x2 7.8 us: pack(): pl.pallas_call(functools.partial(pack_kernel, first=start * head_dim, hea...]
  transfers between devices with their start and end apart: 14 -> 38, of which waited for: 11 -> 20; matrix products, arithmetic and copies ran while one was open for 1% -> 0% of each run, Pallas kernels for 30% -> 23%
where the time goes in v4:
time: 399 us; the launch traced here: 398 us
  waiting for transfers between devices  233 us (58%)
  Pallas kernels  97.7 us (24%)
  starting transfers between devices  60 us (15%)
    ppermute x28, waiting for transfers between devices, exchange(): received[k] = lax.ppermute(messages[k], 'seq', pairs)  232 us
    pallas_call x2, Pallas kernels, attend(): pl.pallas_call(functools.partial(attend_kernel, block_rows=block_rows, he...  72.8 us
    ppermute x28, starting transfers between devices, exchange(): received[k] = lax.ppermute(messages[k], 'seq', pairs)  39.5 us
    ppermute x10, starting transfers between devices, from_behind(): return lax.ppermute(x, axis, pairs)  20.5 us
  transfers between devices with their start and end apart: 38, of which 20 were waited for; matrix products, arithmetic and copies ran while one was open for 0% of the time, Pallas kernels for 23%

profile of v4, /device:TPU:8, one launch (start us, length us, event | category | flops | bytes accessed | tf_op | source)
XLA Modules:
  0.0 398.0 jit_solution(14306546696426567848)
XLA Ops:
  4.3 3.9 pack.2
  8.2 1.6 collective-permute-start.2
  10.3 1.5 collective-permute-start.4
  11.8 2.5 collective-permute-start.8
  15.8 1.9 collective-permute-start.1
  19.9 3.9 pack.3
  23.8 13.4 %collective-permute-done.2.refs_1_.refs_3_ = bf16[3,2,256,128]{3,2,1,0:T(8,128)(2,1)S(1)} collective-permute-done((bf16[3,2,256,128]{3,2,1,0:T(8,128)(2,1)}, bf16[3,2,256,128]{3,2,1,0:T(8,128)(2,1)S(1)}, u32[]{:S(2)}, u32[]{:S(2)}) %collective-permute-start.2) | collective-permute-done | bytes 393248 | tf_op jit(solution)/shard_map/ppermute | solution.py:55
  37.2 1.6 collective-permute-start.7
  38.9 6.1 %collective-permute-done.4.refs_3_.refs_5_ = bf16[3,2,256,128]{3,2,1,0:T(8,128)(2,1)S(1)} collective-permute-done((bf16[3,2,256,128]{3,2,1,0:T(8,128)(2,1)}, bf16[3,2,256,128]{3,2,1,0:T(8,128)(2,1)S(1)}, u32[]{:S(2)}, u32[]{:S(2)}) %collective-permute-start.4) | collective-permute-done | bytes 393248 | tf_op jit(solution)/shard_map/ppermute | solution.py:55
  45.8 3.8 collective-permute-start.21
  49.5 17.7 %collective-permute-done.5.refs_4_ = bf16[3,2,256,128]{3,2,1,0:T(8,128)(2,1)S(1)} collective-permute-done((bf16[3,2,256,128]{3,2,1,0:T(8,128)(2,1)}, bf16[3,2,256,128]{3,2,1,0:T(8,128)(2,1)S(1)}, u32[]{:S(2)}, u32[]{:S(2)}) %collective-permute-start.5) | collective-permute-done | bytes 393248 | tf_op jit(solution)/shard_map/ppermute | solution.py:55
  67.2 2.1 collective-permute-start.22
  69.4 6.3 %collective-permute-done.6.refs_5_ = bf16[3,2,256,128]{3,2,1,0:T(8,128)(2,1)S(1)} collective-permute-done((bf16[3,2,256,128]{3,2,1,0:T(8,128)(2,1)}, bf16[3,2,256,128]{3,2,1,0:T(8,128)(2,1)S(1)}, u32[]{:S(2)}, u32[]{:S(2)}) %collective-permute-start.6) | collective-permute-done | bytes 393248 | tf_op jit(solution)/shard_map/ppermute | solution.py:55
  75.7 3.2 collective-permute-start.23
  78.9 14.3 %collective-permute-done.7.refs_6_ = bf16[3,2,256,128]{3,2,1,0:T(8,128)(2,1)S(1)} collective-permute-done((bf16[3,2,256,128]{3,2,1,0:T(8,128)(2,1)S(1)}, bf16[3,2,256,128]{3,2,1,0:T(8,128)(2,1)S(1)}, u32[]{:S(2)}, u32[]{:S(2)}) %collective-permute-start.7) | collective-permute-done | bytes 393248 | tf_op jit(solution)/shard_map/ppermute | solution.py:55
  93.3 1.7 collective-permute-start.25
  95.3 2.1 pick.2
  97.5 1.3 collective-permute-start.9
  98.8 27.4 %collective-permute-done.23.refs_4_ = bf16[3,2,256,128]{3,2,1,0:T(8,128)(2,1)S(1)} collective-permute-done((bf16[3,2,256,128]{3,2,1,0:T(8,128)(2,1)}, bf16[3,2,256,128]{3,2,1,0:T(8,128)(2,1)S(1)}, u32[]{:S(2)}, u32[]{:S(2)}) %collective-permute-start.23) | collective-permute-done | bytes 393248 | tf_op jit(solution)/shard_map/ppermute | solution.py:55
  127.5 7.1 %collective-permute-done.24.refs_5_ = bf16[3,2,256,128]{3,2,1,0:T(8,128)(2,1)S(1)} collective-permute-done((bf16[3,2,256,128]{3,2,1,0:T(8,128)(2,1)}, bf16[3,2,256,128]{3,2,1,0:T(8,128)(2,1)S(1)}, u32[]{:S(2)}, u32[]{:S(2)}) %collective-permute-start.24) | collective-permute-done | bytes 393248 | tf_op jit(solution)/shard_map/ppermute | solution.py:55
  134.6 9.2 %collective-permute-done.25.refs_6_ = bf16[3,2,256,128]{3,2,1,0:T(8,128)(2,1)S(1)} collective-permute-done((bf16[3,2,256,128]{3,2,1,0:T(8,128)(2,1)}, bf16[3,2,256,128]{3,2,1,0:T(8,128)(2,1)S(1)}, u32[]{:S(2)}, u32[]{:S(2)}) %collective-permute-start.25) | collective-permute-done | bytes 393248 | tf_op jit(solution)/shard_map/ppermute | solution.py:55
  143.8 8.3 %collective-permute-done.26.refs_7_ = bf16[3,2,256,128]{3,2,1,0:T(8,128)(2,1)S(1)} collective-permute-done((bf16[3,2,256,128]{3,2,1,0:T(8,128)(2,1)}, bf16[3,2,256,128]{3,2,1,0:T(8,128)(2,1)S(1)}, u32[]{:S(2)}, u32[]{:S(2)}) %collective-permute-start.26) | collective-permute-done | bytes 393248 | tf_op jit(solution)/shard_map/ppermute | solution.py:55
  152.9 2.1 pick.3
  155.0 1.9 collective-permute-start.27
  158.3 36.4 %attend.2 = (bf16[8,3,256,128]{3,2,1,0:T(8,128)(2,1)S(1)}, f32[3,16,128,128]{3,2,1,0:T(8,128)S(1)}, bf16[4,3,128,128]{3,2,1,0:T(8,128)(2,1)S(1)}, bf16[4,3,128,128]{3,2,1,0:T(8,128)(2,1)S(1)}) custom-call(s32[1]{0:T(128)} %bitcast.me, s32[3,16,8]{2,1,0:T(8,128)S(1)} %get-tuple-element.127.lists, ...), custom_call_target="tpu_custom_call" | custom-call | tf_op jit(solution)/shard_map/attend/pallas_call | solution.py:434
  196.0 4.4 %collective-permute-start.12 = (bf16[4,3,128,128]{3,2,1,0:T(8,128)(2,1)S(1)}, bf16[4,3,128,128]{3,2,1,0:T(8,128)(2,1)S(1)}, u32[]{:S(2)}, u32[]{:S(2)}) collective-permute-start(bf16[4,3,128,128]{3,2,1,0:T(8,128)(2,1)S(1)} %get-tuple-element.80), channel_id=1, source_target_pairs={{0,8},{8,16},{16,24},{1,9},{9,17},{17,25},{2,10},{10,18},{18,26},{... | collective-permute-start | bytes 1179656 | tf_op jit(solution)/shard_map/ppermute | solution.py:25
  200.5 36.4 %attend.3 = (bf16[8,3,256,128]{3,2,1,0:T(8,128)(2,1)S(1)}, f32[3,16,128,128]{3,2,1,0:T(8,128)S(1)}, bf16[4,3,128,128]{3,2,1,0:T(8,128)(2,1)S(1)}, bf16[4,3,128,128]{3,2,1,0:T(8,128)(2,1)S(1)}) custom-call(s32[1]{0:T(128)} %bitcast.me, s32[3,16,8]{2,1,0:T(8,128)S(1)} %get-tuple-element.126.lists, ...), custom_call_target="tpu_custom_call" | custom-call | tf_op jit(solution)/shard_map/attend/pallas_call | solution.py:434
  238.2 4.5 %collective-permute-start.30 = (bf16[4,3,128,128]{3,2,1,0:T(8,128)(2,1)S(1)}, bf16[4,3,128,128]{3,2,1,0:T(8,128)(2,1)S(1)}, u32[]{:S(2)}, u32[]{:S(2)}) collective-permute-start(bf16[4,3,128,128]{3,2,1,0:T(8,128)(2,1)S(1)} %get-tuple-element.109), channel_id=1, source_target_pairs={{0,8},{8,16},{16,24},{1,9},{9,17},{17,25},{2,10},{10,18},{18,26},{... | collective-permute-start | bytes 1179656 | tf_op jit(solution)/shard_map/ppermute | solution.py:25
  242.7 2.6 finish.2
  245.3 1.6 collective-permute-start.13
  246.9 2.0 collective-permute-start.15
  249.4 3.3 collective-permute-start.17
  252.7 2.6 finish.3
  255.4 1.5 collective-permute-done.13.refs_1_
  257.9 14.0 %collective-permute-done.14.refs_2_ = bf16[3,2,256,128]{3,2,1,0:T(8,128)(2,1)S(1)} collective-permute-done((bf16[3,2,256,128]{3,2,1,0:T(8,128)(2,1)}, bf16[3,2,256,128]{3,2,1,0:T(8,128)(2,1)S(1)}, u32[]{:S(2)}, u32[]{:S(2)}) %collective-permute-start.14) | collective-permute-done | bytes 393248 | tf_op jit(solution)/shard_map/ppermute | solution.py:55
  271.9 8.4 %collective-permute-done.15.refs_3_ = bf16[3,2,256,128]{3,2,1,0:T(8,128)(2,1)S(1)} collective-permute-done((bf16[3,2,256,128]{3,2,1,0:T(8,128)(2,1)}, bf16[3,2,256,128]{3,2,1,0:T(8,128)(2,1)S(1)}, u32[]{:S(2)}, u32[]{:S(2)}) %collective-permute-start.15) | collective-permute-done | bytes 393248 | tf_op jit(solution)/shard_map/ppermute | solution.py:55
  280.4 3.8 collective-permute-start.32
  284.2 16.9 %collective-permute-done.17.refs_5_ = bf16[3,2,256,128]{3,2,1,0:T(8,128)(2,1)S(1)} collective-permute-done((bf16[3,2,256,128]{3,2,1,0:T(8,128)(2,1)}, bf16[3,2,256,128]{3,2,1,0:T(8,128)(2,1)S(1)}, u32[]{:S(2)}, u32[]{:S(2)}) %collective-permute-start.17) | collective-permute-done | bytes 393248 | tf_op jit(solution)/shard_map/ppermute | solution.py:55
  301.1 3.9 collective-permute-start.33
  305.0 6.0 %collective-permute-done.18.refs_6_ = bf16[3,2,256,128]{3,2,1,0:T(8,128)(2,1)S(1)} collective-permute-done((bf16[3,2,256,128]{3,2,1,0:T(8,128)(2,1)S(1)}, bf16[3,2,256,128]{3,2,1,0:T(8,128)(2,1)S(1)}, u32[]{:S(2)}, u32[]{:S(2)}) %collective-permute-start.18) | collective-permute-done | bytes 393248 | tf_op jit(solution)/shard_map/ppermute | solution.py:55
  311.0 22.7 %collective-permute-done.19.refs_7_ = bf16[3,2,256,128]{3,2,1,0:T(8,128)(2,1)S(1)} collective-permute-done((bf16[3,2,256,128]{3,2,1,0:T(8,128)(2,1)S(1)}, bf16[3,2,256,128]{3,2,1,0:T(8,128)(2,1)S(1)}, u32[]{:S(2)}, u32[]{:S(2)}) %collective-permute-start.19) | collective-permute-done | bytes 393248 | tf_op jit(solution)/shard_map/ppermute | solution.py:55
  334.8 2.0 collective-permute-start.37
  336.8 3.2 unpack.2
  340.1 26.0 %collective-permute-done.34.refs_12_ = bf16[3,2,256,128]{3,2,1,0:T(8,128)(2,1)S(1)} collective-permute-done((bf16[3,2,256,128]{3,2,1,0:T(8,128)(2,1)}, bf16[3,2,256,128]{3,2,1,0:T(8,128)(2,1)S(1)}, u32[]{:S(2)}, u32[]{:S(2)}) %collective-permute-start.34) | collective-permute-done | bytes 393248 | tf_op jit(solution)/shard_map/ppermute | solution.py:55
  366.1 8.4 %collective-permute-done.35.refs_13_ = bf16[3,2,256,128]{3,2,1,0:T(8,128)(2,1)S(1)} collective-permute-done((bf16[3,2,256,128]{3,2,1,0:T(8,128)(2,1)}, bf16[3,2,256,128]{3,2,1,0:T(8,128)(2,1)S(1)}, u32[]{:S(2)}, u32[]{:S(2)}) %collective-permute-start.35) | collective-permute-done | bytes 393248 | tf_op jit(solution)/shard_map/ppermute | solution.py:55
  374.5 9.8 %collective-permute-done.36.refs_14_ = bf16[3,2,256,128]{3,2,1,0:T(8,128)(2,1)S(1)} collective-permute-done((bf16[3,2,256,128]{3,2,1,0:T(8,128)(2,1)}, bf16[3,2,256,128]{3,2,1,0:T(8,128)(2,1)S(1)}, u32[]{:S(2)}, u32[]{:S(2)}) %collective-permute-start.36) | collective-permute-done | bytes 393248 | tf_op jit(solution)/shard_map/ppermute | solution.py:55
  384.3 8.3 %collective-permute-done.37.refs_15_ = bf16[3,2,256,128]{3,2,1,0:T(8,128)(2,1)S(1)} collective-permute-done((bf16[3,2,256,128]{3,2,1,0:T(8,128)(2,1)}, bf16[3,2,256,128]{3,2,1,0:T(8,128)(2,1)S(1)}, u32[]{:S(2)}, u32[]{:S(2)}) %collective-permute-start.37) | collective-permute-done | bytes 393248 | tf_op jit(solution)/shard_map/ppermute | solution.py:55
  393.4 4.4 %unpack.3 = (bf16[256,3072]{1,0:T(8,128)(2,1)}, bf16[256,3072]{1,0:T(8,128)(2,1)}, bf16[256,3072]{1,0:T(8,128)(2,1)}, bf16[256,3072]{1,0:T(8,128)(2,1)}) custom-call(s32[1]{0:T(128)} %bitcast.me, bf16[3,2,256,128]{3,2,1,0:T(8,128)(2,1)} %get-tuple-element.81.refs_0_, ...), custom_call_target="tpu_custom_call", output_to_operand_aliasing={{0}: (17, {}), {1}: (18, {}), {2}: (19, {}), {3}: (20, {})} | custom-call | tf_op jit(solution)/shard_map/unpack/pallas_call | solution.py:220
  (124 shorter events, 18.3 us)
Async XLA Ops:
  3.0 12.8 %collective-permute-start = (s32[4]{0:T(128)S(1)}, s32[4]{0:T(128)S(1)}, u32[]{:S(2)}, u32[]{:S(2)}) collective-permute-start(s32[4]{0:T(128)S(1)} %get-tuple-element.129), channel_id=1, source_target_pairs={{8,0},{16,8},{24,16},{9,1},{17,9},{25,17},{10,2},{18,10},{26,18},{... | collective-permute-start | bytes 56 | tf_op jit(solution)/shard_map/ppermute | solution.py:25
  8.2 29.0 %collective-permute-start.2 = (bf16[3,2,256,128]{3,2,1,0:T(8,128)(2,1)}, bf16[3,2,256,128]{3,2,1,0:T(8,128)(2,1)S(1)}, u32[]{:S(2)}, u32[]{:S(2)}) collective-permute-start(bf16[3,2,256,128]{3,2,1,0:T(8,128)(2,1)} %get-tuple-element.68), channel_id=1, source_target_pairs={{0,1},{1,0},{2,3},{3,2},{4,5},{5,4},{6,7},{7,6},{8,9},{9,8},{10,11... | collective-permute-start | bytes 1179656 | tf_op jit(solution)/shard_map/ppermute | solution.py:55
  9.8 27.4 %collective-permute-start.3 = (bf16[3,2,256,128]{3,2,1,0:T(8,128)(2,1)}, bf16[3,2,256,128]{3,2,1,0:T(8,128)(2,1)S(1)}, u32[]{:S(2)}, u32[]{:S(2)}) collective-permute-start(bf16[3,2,256,128]{3,2,1,0:T(8,128)(2,1)} %get-tuple-element.69), channel_id=1, source_target_pairs={{0,2},{1,3},{2,0},{3,1},{4,6},{5,7},{6,4},{7,5},{8,10},{9,11},{10,... | collective-permute-start | bytes 1179656 | tf_op jit(solution)/shard_map/ppermute | solution.py:55
  10.3 34.7 %collective-permute-start.4 = (bf16[3,2,256,128]{3,2,1,0:T(8,128)(2,1)}, bf16[3,2,256,128]{3,2,1,0:T(8,128)(2,1)S(1)}, u32[]{:S(2)}, u32[]{:S(2)}) collective-permute-start(bf16[3,2,256,128]{3,2,1,0:T(8,128)(2,1)} %get-tuple-element.70), channel_id=1, source_target_pairs={{0,3},{1,2},{2,1},{3,0},{4,7},{5,6},{6,5},{7,4},{8,11},{9,10},{10,... | collective-permute-start | bytes 1179656 | tf_op jit(solution)/shard_map/ppermute | solution.py:55
  11.8 34.0 %collective-permute-start.8 = (bf16[3,2,256,128]{3,2,1,0:T(8,128)(2,1)}, bf16[3,2,256,128]{3,2,1,0:T(8,128)(2,1)S(1)}, u32[]{:S(2)}, u32[]{:S(2)}) collective-permute-start(bf16[3,2,256,128]{3,2,1,0:T(8,128)(2,1)} %get-tuple-element.74), channel_id=1, source_target_pairs={{0,7},{1,6},{2,5},{3,4},{4,3},{5,2},{6,1},{7,0},{8,15},{9,14},{10,... | collective-permute-start | bytes 1179656 | tf_op jit(solution)/shard_map/ppermute | solution.py:55
  15.8 2.7 collective-permute-start.1
  18.5 48.7 %collective-permute-start.5 = (bf16[3,2,256,128]{3,2,1,0:T(8,128)(2,1)}, bf16[3,2,256,128]{3,2,1,0:T(8,128)(2,1)S(1)}, u32[]{:S(2)}, u32[]{:S(2)}) collective-permute-start(bf16[3,2,256,128]{3,2,1,0:T(8,128)(2,1)} %get-tuple-element.71), channel_id=1, source_target_pairs={{0,4},{1,5},{2,6},{3,7},{4,0},{5,1},{6,2},{7,3},{8,12},{9,13},{10,... | collective-permute-start | bytes 1179656 | tf_op jit(solution)/shard_map/ppermute | solution.py:55
  37.2 38.4 %collective-permute-start.6 = (bf16[3,2,256,128]{3,2,1,0:T(8,128)(2,1)}, bf16[3,2,256,128]{3,2,1,0:T(8,128)(2,1)S(1)}, u32[]{:S(2)}, u32[]{:S(2)}) collective-permute-start(bf16[3,2,256,128]{3,2,1,0:T(8,128)(2,1)} %get-tuple-element.72), channel_id=1, source_target_pairs={{0,5},{1,4},{2,7},{3,6},{4,1},{5,0},{6,3},{7,2},{8,13},{9,12},{10,... | collective-permute-start | bytes 1179656 | tf_op jit(solution)/shard_map/ppermute | solution.py:55
  37.2 56.0 %collective-permute-start.7 = (bf16[3,2,256,128]{3,2,1,0:T(8,128)(2,1)S(1)}, bf16[3,2,256,128]{3,2,1,0:T(8,128)(2,1)S(1)}, u32[]{:S(2)}, u32[]{:S(2)}) collective-permute-start(bf16[3,2,256,128]{3,2,1,0:T(8,128)(2,1)S(1)} %copy-done.30), channel_id=1, source_target_pairs={{0,6},{1,7},{2,4},{3,5},{4,2},{5,3},{6,0},{7,1},{8,14},{9,15},{10,... | collective-permute-start | bytes 1179656 | tf_op jit(solution)/shard_map/ppermute | solution.py:55
  45.7 47.6 %collective-permute-start.20 = (bf16[3,2,256,128]{3,2,1,0:T(8,128)(2,1)}, bf16[3,2,256,128]{3,2,1,0:T(8,128)(2,1)S(1)}, u32[]{:S(2)}, u32[]{:S(2)}) collective-permute-start(bf16[3,2,256,128]{3,2,1,0:T(8,128)(2,1)} %get-tuple-element.93), channel_id=1, source_target_pairs={{0,1},{1,0},{2,3},{3,2},{4,5},{5,4},{6,7},{7,6},{8,9},{9,8},{10,11... | collective-permute-start | bytes 1179656 | tf_op jit(solution)/shard_map/ppermute | solution.py:55
  45.8 49.2 %collective-permute-start.21 = (bf16[3,2,256,128]{3,2,1,0:T(8,128)(2,1)}, bf16[3,2,256,128]{3,2,1,0:T(8,128)(2,1)S(1)}, u32[]{:S(2)}, u32[]{:S(2)}) collective-permute-start(bf16[3,2,256,128]{3,2,1,0:T(8,128)(2,1)} %get-tuple-element.94), channel_id=1, source_target_pairs={{0,2},{1,3},{2,0},{3,1},{4,6},{5,7},{6,4},{7,5},{8,10},{9,11},{10,... | collective-permute-start | bytes 1179656 | tf_op jit(solution)/shard_map/ppermute | solution.py:55
  67.2 28.1 %copy-start.11 = (bf16[3,2,256,128]{3,2,1,0:T(8,128)(2,1)}, bf16[3,2,256,128]{3,2,1,0:T(8,128)(2,1)S(1)}, u32[]{:S(2)}) copy-start(bf16[3,2,256,128]{3,2,1,0:T(8,128)(2,1)S(1)} %collective-permute-done.5.refs_4_) | copy-start | bytes 1179652
  67.2 30.3 %collective-permute-start.22 = (bf16[3,2,256,128]{3,2,1,0:T(8,128)(2,1)S(1)}, bf16[3,2,256,128]{3,2,1,0:T(8,128)(2,1)S(1)}, u32[]{:S(2)}, u32[]{:S(2)}) collective-permute-start(bf16[3,2,256,128]{3,2,1,0:T(8,128)(2,1)S(1)} %copy-done.28), channel_id=1, source_target_pairs={{0,3},{1,2},{2,1},{3,0},{4,7},{5,6},{6,5},{7,4},{8,11},{9,10},{10,... | collective-permute-start | bytes 1179656 | tf_op jit(solution)/shard_map/ppermute | solution.py:55
  75.7 50.6 %collective-permute-start.23 = (bf16[3,2,256,128]{3,2,1,0:T(8,128)(2,1)}, bf16[3,2,256,128]{3,2,1,0:T(8,128)(2,1)S(1)}, u32[]{:S(2)}, u32[]{:S(2)}) collective-permute-start(bf16[3,2,256,128]{3,2,1,0:T(8,128)(2,1)} %get-tuple-element.100), channel_id=1, source_target_pairs={{0,4},{1,5},{2,6},{3,7},{4,0},{5,1},{6,2},{7,3},{8,12},{9,13},{10,... | collective-permute-start | bytes 1179656 | tf_op jit(solution)/shard_map/ppermute | solution.py:55
  93.3 41.4 %collective-permute-start.24 = (bf16[3,2,256,128]{3,2,1,0:T(8,128)(2,1)}, bf16[3,2,256,128]{3,2,1,0:T(8,128)(2,1)S(1)}, u32[]{:S(2)}, u32[]{:S(2)}) collective-permute-start(bf16[3,2,256,128]{3,2,1,0:T(8,128)(2,1)} %get-tuple-element.101), channel_id=1, source_target_pairs={{0,5},{1,4},{2,7},{3,6},{4,1},{5,0},{6,3},{7,2},{8,13},{9,12},{10,... | collective-permute-start | bytes 1179656 | tf_op jit(solution)/shard_map/ppermute | solution.py:55
  93.3 50.5 %collective-permute-start.25 = (bf16[3,2,256,128]{3,2,1,0:T(8,128)(2,1)}, bf16[3,2,256,128]{3,2,1,0:T(8,128)(2,1)S(1)}, u32[]{:S(2)}, u32[]{:S(2)}) collective-permute-start(bf16[3,2,256,128]{3,2,1,0:T(8,128)(2,1)} %get-tuple-element.102), channel_id=1, source_target_pairs={{0,6},{1,7},{2,4},{3,5},{4,2},{5,3},{6,0},{7,1},{8,14},{9,15},{10,... | collective-permute-start | bytes 1179656 | tf_op jit(solution)/shard_map/ppermute | solution.py:55
  95.0 57.1 %collective-permute-start.26 = (bf16[3,2,256,128]{3,2,1,0:T(8,128)(2,1)}, bf16[3,2,256,128]{3,2,1,0:T(8,128)(2,1)S(1)}, u32[]{:S(2)}, u32[]{:S(2)}) collective-permute-start(bf16[3,2,256,128]{3,2,1,0:T(8,128)(2,1)} %get-tuple-element.103), channel_id=1, source_target_pairs={{0,7},{1,6},{2,5},{3,4},{4,3},{5,2},{6,1},{7,0},{8,15},{9,14},{10,... | collective-permute-start | bytes 1179656 | tf_op jit(solution)/shard_map/ppermute | solution.py:55
  97.5 54.6 %copy-start.16 = (bf16[3,2,256,128]{3,2,1,0:T(8,128)(2,1)}, bf16[3,2,256,128]{3,2,1,0:T(8,128)(2,1)S(1)}, u32[]{:S(2)}) copy-start(bf16[3,2,256,128]{3,2,1,0:T(8,128)(2,1)S(1)} %collective-permute-done.22.refs_3_) | copy-start | bytes 1179652
  97.5 60.7 %collective-permute-start.9 = (bf16[4,3,128,128]{3,2,1,0:T(8,128)(2,1)S(1)}, bf16[4,3,128,128]{3,2,1,0:T(8,128)(2,1)S(1)}, u32[]{:S(2)}, u32[]{:S(2)}) collective-permute-start(bf16[4,3,128,128]{3,2,1,0:T(8,128)(2,1)S(1)} %get-tuple-element.75), channel_id=1, source_target_pairs={{0,8},{8,16},{16,24},{1,9},{9,17},{17,25},{2,10},{10,18},{18,26},{... | collective-permute-start | bytes 1179656 | tf_op jit(solution)/shard_map/ppermute | solution.py:25
  126.2 25.9 %copy-start.17 = (bf16[3,2,256,128]{3,2,1,0:T(8,128)(2,1)}, bf16[3,2,256,128]{3,2,1,0:T(8,128)(2,1)S(1)}, u32[]{:S(2)}) copy-start(bf16[3,2,256,128]{3,2,1,0:T(8,128)(2,1)S(1)} %collective-permute-done.23.refs_4_) | copy-start | bytes 1179652
  126.2 32.1 %collective-permute-start.10 = (bf16[4,3,128,128]{3,2,1,0:T(8,128)(2,1)S(1)}, bf16[4,3,128,128]{3,2,1,0:T(8,128)(2,1)S(1)}, u32[]{:S(2)}, u32[]{:S(2)}) collective-permute-start(bf16[4,3,128,128]{3,2,1,0:T(8,128)(2,1)S(1)} %get-tuple-element.76), channel_id=1, source_target_pairs={{8,0},{16,8},{24,16},{9,1},{17,9},{25,17},{10,2},{18,10},{26,18},{... | collective-permute-start | bytes 1179656 | tf_op jit(solution)/shard_map/ppermute | solution.py:25
  155.0 45.5 %collective-permute-start.27 = (bf16[4,3,128,128]{3,2,1,0:T(8,128)(2,1)S(1)}, bf16[4,3,128,128]{3,2,1,0:T(8,128)(2,1)S(1)}, u32[]{:S(2)}, u32[]{:S(2)}) collective-permute-start(bf16[4,3,128,128]{3,2,1,0:T(8,128)(2,1)S(1)} %get-tuple-element.104), channel_id=1, source_target_pairs={{0,8},{8,16},{16,24},{1,9},{9,17},{17,25},{2,10},{10,18},{18,26},{... | collective-permute-start | bytes 1179656 | tf_op jit(solution)/shard_map/ppermute | solution.py:25
  156.9 43.5 %collective-permute-start.28 = (bf16[4,3,128,128]{3,2,1,0:T(8,128)(2,1)S(1)}, bf16[4,3,128,128]{3,2,1,0:T(8,128)(2,1)S(1)}, u32[]{:S(2)}, u32[]{:S(2)}) collective-permute-start(bf16[4,3,128,128]{3,2,1,0:T(8,128)(2,1)S(1)} %get-tuple-element.105), channel_id=1, source_target_pairs={{8,0},{16,8},{24,16},{9,1},{17,9},{25,17},{10,2},{18,10},{26,18},{... | collective-permute-start | bytes 1179656 | tf_op jit(solution)/shard_map/ppermute | solution.py:25
  194.7 48.0 %collective-permute-start.11 = (bf16[4,3,128,128]{3,2,1,0:T(8,128)(2,1)S(1)}, bf16[4,3,128,128]{3,2,1,0:T(8,128)(2,1)S(1)}, u32[]{:S(2)}, u32[]{:S(2)}) collective-permute-start(bf16[4,3,128,128]{3,2,1,0:T(8,128)(2,1)S(1)} %get-tuple-element.79), channel_id=1, source_target_pairs={{8,0},{16,8},{24,16},{9,1},{17,9},{25,17},{10,2},{18,10},{26,18},{... | collective-permute-start | bytes 1179656 | tf_op jit(solution)/shard_map/ppermute | solution.py:25
  196.0 46.7 %collective-permute-start.12 = (bf16[4,3,128,128]{3,2,1,0:T(8,128)(2,1)S(1)}, bf16[4,3,128,128]{3,2,1,0:T(8,128)(2,1)S(1)}, u32[]{:S(2)}, u32[]{:S(2)}) collective-permute-start(bf16[4,3,128,128]{3,2,1,0:T(8,128)(2,1)S(1)} %get-tuple-element.80), channel_id=1, source_target_pairs={{0,8},{8,16},{16,24},{1,9},{9,17},{17,25},{2,10},{10,18},{18,26},{... | collective-permute-start | bytes 1179656 | tf_op jit(solution)/shard_map/ppermute | solution.py:25
  236.9 12.0 %collective-permute-start.29 = (bf16[4,3,128,128]{3,2,1,0:T(8,128)(2,1)S(1)}, bf16[4,3,128,128]{3,2,1,0:T(8,128)(2,1)S(1)}, u32[]{:S(2)}, u32[]{:S(2)}) collective-permute-start(bf16[4,3,128,128]{3,2,1,0:T(8,128)(2,1)S(1)} %get-tuple-element.108), channel_id=1, source_target_pairs={{8,0},{16,8},{24,16},{9,1},{17,9},{25,17},{10,2},{18,10},{26,18},{... | collective-permute-start | bytes 1179656 | tf_op jit(solution)/shard_map/ppermute | solution.py:25
  238.2 11.2 %collective-permute-start.30 = (bf16[4,3,128,128]{3,2,1,0:T(8,128)(2,1)S(1)}, bf16[4,3,128,128]{3,2,1,0:T(8,128)(2,1)S(1)}, u32[]{:S(2)}, u32[]{:S(2)}) collective-permute-start(bf16[4,3,128,128]{3,2,1,0:T(8,128)(2,1)S(1)} %get-tuple-element.109), channel_id=1, source_target_pairs={{0,8},{8,16},{16,24},{1,9},{9,17},{17,25},{2,10},{10,18},{18,26},{... | collective-permute-start | bytes 1179656 | tf_op jit(solution)/shard_map/ppermute | solution.py:25
  245.3 11.6 %collective-permute-start.13 = (bf16[3,2,256,128]{3,2,1,0:T(8,128)(2,1)}, bf16[3,2,256,128]{3,2,1,0:T(8,128)(2,1)S(1)}, u32[]{:S(2)}, u32[]{:S(2)}) collective-permute-start(bf16[3,2,256,128]{3,2,1,0:T(8,128)(2,1)} %get-tuple-element.82), channel_id=1, source_target_pairs={{0,1},{1,0},{2,3},{3,2},{4,5},{5,4},{6,7},{7,6},{8,9},{9,8},{10,11... | collective-permute-start | bytes 1179656 | tf_op jit(solution)/shard_map/ppermute | solution.py:55
  246.9 25.1 %collective-permute-start.14 = (bf16[3,2,256,128]{3,2,1,0:T(8,128)(2,1)}, bf16[3,2,256,128]{3,2,1,0:T(8,128)(2,1)S(1)}, u32[]{:S(2)}, u32[]{:S(2)}) collective-permute-start(bf16[3,2,256,128]{3,2,1,0:T(8,128)(2,1)} %get-tuple-element.83), channel_id=1, source_target_pairs={{0,2},{1,3},{2,0},{3,1},{4,6},{5,7},{6,4},{7,5},{8,10},{9,11},{10,... | collective-permute-start | bytes 1179656 | tf_op jit(solution)/shard_map/ppermute | solution.py:55
  246.9 33.5 %collective-permute-start.15 = (bf16[3,2,256,128]{3,2,1,0:T(8,128)(2,1)}, bf16[3,2,256,128]{3,2,1,0:T(8,128)(2,1)S(1)}, u32[]{:S(2)}, u32[]{:S(2)}) collective-permute-start(bf16[3,2,256,128]{3,2,1,0:T(8,128)(2,1)} %get-tuple-element.84), channel_id=1, source_target_pairs={{0,3},{1,2},{2,1},{3,0},{4,7},{5,6},{6,5},{7,4},{8,11},{9,10},{10,... | collective-permute-start | bytes 1179656 | tf_op jit(solution)/shard_map/ppermute | solution.py:55
  248.9 31.5 %collective-permute-start.16 = (bf16[3,2,256,128]{3,2,1,0:T(8,128)(2,1)}, bf16[3,2,256,128]{3,2,1,0:T(8,128)(2,1)S(1)}, u32[]{:S(2)}, u32[]{:S(2)}) collective-permute-start(bf16[3,2,256,128]{3,2,1,0:T(8,128)(2,1)} %get-tuple-element.85), channel_id=1, source_target_pairs={{0,4},{1,5},{2,6},{3,7},{4,0},{5,1},{6,2},{7,3},{8,12},{9,13},{10,... | collective-permute-start | bytes 1179656 | tf_op jit(solution)/shard_map/ppermute | solution.py:55
  249.4 51.7 %collective-permute-start.17 = (bf16[3,2,256,128]{3,2,1,0:T(8,128)(2,1)}, bf16[3,2,256,128]{3,2,1,0:T(8,128)(2,1)S(1)}, u32[]{:S(2)}, u32[]{:S(2)}) collective-permute-start(bf16[3,2,256,128]{3,2,1,0:T(8,128)(2,1)} %get-tuple-element.86), channel_id=1, source_target_pairs={{0,5},{1,4},{2,7},{3,6},{4,1},{5,0},{6,3},{7,2},{8,13},{9,12},{10,... | collective-permute-start | bytes 1179656 | tf_op jit(solution)/shard_map/ppermute | solution.py:55
  256.9 79.9 %copy-start.4 = (bf16[3,2,256,128]{3,2,1,0:T(8,128)(2,1)}, bf16[3,2,256,128]{3,2,1,0:T(8,128)(2,1)S(1)}, u32[]{:S(2)}) copy-start(bf16[3,2,256,128]{3,2,1,0:T(8,128)(2,1)S(1)} %collective-permute-done.13.refs_1_) | copy-start | bytes 1179652
  256.9 54.1 %collective-permute-start.18 = (bf16[3,2,256,128]{3,2,1,0:T(8,128)(2,1)S(1)}, bf16[3,2,256,128]{3,2,1,0:T(8,128)(2,1)S(1)}, u32[]{:S(2)}, u32[]{:S(2)}) collective-permute-start(bf16[3,2,256,128]{3,2,1,0:T(8,128)(2,1)S(1)} %copy-done.32), channel_id=1, source_target_pairs={{0,6},{1,7},{2,4},{3,5},{4,2},{5,3},{6,0},{7,1},{8,14},{9,15},{10,... | collective-permute-start | bytes 1179656 | tf_op jit(solution)/shard_map/ppermute | solution.py:55
  271.9 64.8 %copy-start.5 = (bf16[3,2,256,128]{3,2,1,0:T(8,128)(2,1)}, bf16[3,2,256,128]{3,2,1,0:T(8,128)(2,1)S(1)}, u32[]{:S(2)}) copy-start(bf16[3,2,256,128]{3,2,1,0:T(8,128)(2,1)S(1)} %collective-permute-done.14.refs_2_) | copy-start | bytes 1179652
  271.9 61.7 %collective-permute-start.19 = (bf16[3,2,256,128]{3,2,1,0:T(8,128)(2,1)S(1)}, bf16[3,2,256,128]{3,2,1,0:T(8,128)(2,1)S(1)}, u32[]{:S(2)}, u32[]{:S(2)}) collective-permute-start(bf16[3,2,256,128]{3,2,1,0:T(8,128)(2,1)S(1)} %copy-done.31), channel_id=1, source_target_pairs={{0,7},{1,6},{2,5},{3,4},{4,3},{5,2},{6,1},{7,0},{8,15},{9,14},{10,... | collective-permute-start | bytes 1179656 | tf_op jit(solution)/shard_map/ppermute | solution.py:55
  280.4 56.4 %copy-start.6 = (bf16[3,2,256,128]{3,2,1,0:T(8,128)(2,1)}, bf16[3,2,256,128]{3,2,1,0:T(8,128)(2,1)S(1)}, u32[]{:S(2)}) copy-start(bf16[3,2,256,128]{3,2,1,0:T(8,128)(2,1)S(1)} %collective-permute-done.15.refs_3_) | copy-start | bytes 1179652
  280.4 53.3 %collective-permute-start.31 = (bf16[3,2,256,128]{3,2,1,0:T(8,128)(2,1)}, bf16[3,2,256,128]{3,2,1,0:T(8,128)(2,1)S(1)}, u32[]{:S(2)}, u32[]{:S(2)}) collective-permute-start(bf16[3,2,256,128]{3,2,1,0:T(8,128)(2,1)} %get-tuple-element.111), channel_id=1, source_target_pairs={{0,1},{1,0},{2,3},{3,2},{4,5},{5,4},{6,7},{7,6},{8,9},{9,8},{10,11... | collective-permute-start | bytes 1179656 | tf_op jit(solution)/shard_map/ppermute | solution.py:55
  280.4 56.4 %copy-start.7 = (bf16[3,2,256,128]{3,2,1,0:T(8,128)(2,1)}, bf16[3,2,256,128]{3,2,1,0:T(8,128)(2,1)S(1)}, u32[]{:S(2)}) copy-start(bf16[3,2,256,128]{3,2,1,0:T(8,128)(2,1)S(1)} %collective-permute-done.16.refs_4_) | copy-start | bytes 1179652
  280.4 54.4 %collective-permute-start.32 = (bf16[3,2,256,128]{3,2,1,0:T(8,128)(2,1)}, bf16[3,2,256,128]{3,2,1,0:T(8,128)(2,1)S(1)}, u32[]{:S(2)}, u32[]{:S(2)}) collective-permute-start(bf16[3,2,256,128]{3,2,1,0:T(8,128)(2,1)} %get-tuple-element.112), channel_id=1, source_target_pairs={{0,2},{1,3},{2,0},{3,1},{4,6},{5,7},{6,4},{7,5},{8,10},{9,11},{10,... | collective-permute-start | bytes 1179656 | tf_op jit(solution)/shard_map/ppermute | solution.py:55
  301.1 35.7 %copy-start.8 = (bf16[3,2,256,128]{3,2,1,0:T(8,128)(2,1)}, bf16[3,2,256,128]{3,2,1,0:T(8,128)(2,1)S(1)}, u32[]{:S(2)}) copy-start(bf16[3,2,256,128]{3,2,1,0:T(8,128)(2,1)S(1)} %collective-permute-done.17.refs_5_) | copy-start | bytes 1179652
  301.1 38.9 %collective-permute-start.33 = (bf16[3,2,256,128]{3,2,1,0:T(8,128)(2,1)}, bf16[3,2,256,128]{3,2,1,0:T(8,128)(2,1)S(1)}, u32[]{:S(2)}, u32[]{:S(2)}) collective-permute-start(bf16[3,2,256,128]{3,2,1,0:T(8,128)(2,1)} %get-tuple-element.113), channel_id=1, source_target_pairs={{0,3},{1,2},{2,1},{3,0},{4,7},{5,6},{6,5},{7,4},{8,11},{9,10},{10,... | collective-permute-start | bytes 1179656 | tf_op jit(solution)/shard_map/ppermute | solution.py:55
  311.0 55.1 %collective-permute-start.34 = (bf16[3,2,256,128]{3,2,1,0:T(8,128)(2,1)}, bf16[3,2,256,128]{3,2,1,0:T(8,128)(2,1)S(1)}, u32[]{:S(2)}, u32[]{:S(2)}) collective-permute-start(bf16[3,2,256,128]{3,2,1,0:T(8,128)(2,1)} %get-tuple-element.114), channel_id=1, source_target_pairs={{0,4},{1,5},{2,6},{3,7},{4,0},{5,1},{6,2},{7,3},{8,12},{9,13},{10,... | collective-permute-start | bytes 1179656 | tf_op jit(solution)/shard_map/ppermute | solution.py:55
  333.7 40.8 %collective-permute-start.35 = (bf16[3,2,256,128]{3,2,1,0:T(8,128)(2,1)}, bf16[3,2,256,128]{3,2,1,0:T(8,128)(2,1)S(1)}, u32[]{:S(2)}, u32[]{:S(2)}) collective-permute-start(bf16[3,2,256,128]{3,2,1,0:T(8,128)(2,1)} %get-tuple-element.115), channel_id=1, source_target_pairs={{0,5},{1,4},{2,7},{3,6},{4,1},{5,0},{6,3},{7,2},{8,13},{9,12},{10,... | collective-permute-start | bytes 1179656 | tf_op jit(solution)/shard_map/ppermute | solution.py:55
  333.7 50.6 %collective-permute-start.36 = (bf16[3,2,256,128]{3,2,1,0:T(8,128)(2,1)}, bf16[3,2,256,128]{3,2,1,0:T(8,128)(2,1)S(1)}, u32[]{:S(2)}, u32[]{:S(2)}) collective-permute-start(bf16[3,2,256,128]{3,2,1,0:T(8,128)(2,1)} %get-tuple-element.116), channel_id=1, source_target_pairs={{0,6},{1,7},{2,4},{3,5},{4,2},{5,3},{6,0},{7,1},{8,14},{9,15},{10,... | collective-permute-start | bytes 1179656 | tf_op jit(solution)/shard_map/ppermute | solution.py:55
  334.8 57.9 %collective-permute-start.37 = (bf16[3,2,256,128]{3,2,1,0:T(8,128)(2,1)}, bf16[3,2,256,128]{3,2,1,0:T(8,128)(2,1)S(1)}, u32[]{:S(2)}, u32[]{:S(2)}) collective-permute-start(bf16[3,2,256,128]{3,2,1,0:T(8,128)(2,1)} %get-tuple-element.117), channel_id=1, source_target_pairs={{0,7},{1,6},{2,5},{3,4},{4,3},{5,2},{6,1},{7,0},{8,15},{9,14},{10,... | collective-permute-start | bytes 1179656 | tf_op jit(solution)/shard_map/ppermute | solution.py:55
  340.1 52.6 %copy-start.23 = (bf16[3,2,256,128]{3,2,1,0:T(8,128)(2,1)}, bf16[3,2,256,128]{3,2,1,0:T(8,128)(2,1)S(1)}, u32[]{:S(2)}) copy-start(bf16[3,2,256,128]{3,2,1,0:T(8,128)(2,1)S(1)} %collective-permute-done.33.refs_11_) | copy-start | bytes 1179652
  366.1 26.6 %copy-start.24 = (bf16[3,2,256,128]{3,2,1,0:T(8,128)(2,1)}, bf16[3,2,256,128]{3,2,1,0:T(8,128)(2,1)S(1)}, u32[]{:S(2)}) copy-start(bf16[3,2,256,128]{3,2,1,0:T(8,128)(2,1)S(1)} %collective-permute-done.34.refs_12_) | copy-start | bytes 1179652
  (23 other events, 216.3 us)

commit v5 on v4

--- a/solution.py
+++ b/solution.py
@@ -23,6 +23,22 @@
     count = lax.axis_size(axis)
     pairs = [(i, i + by) for i in range(count) if 0 <= i + by < count]
     return lax.ppermute(x, axis, pairs)
+
+
+def part_of(messages, me, item):
+    if len(messages) == 1:
+        return messages[0].at[item], item
+    return messages[item], me[0] ^ item
+
+
+def message_shape(messages):
+    return messages[0].shape[-4:]
+
+
+def message_outs(peers, shape, dtype, apart):
+    if apart:
+        return [pltpu.HBM(shape, dtype)] * peers
+    return [pltpu.HBM((peers,) + shape, dtype)]
 
 
 def hold_kernel(*refs):
@@ -42,13 +58,10 @@
     )(*[in_hbm(x) for x in (*arrays, *after)])
 
 
-def exchange(messages, before=None):
+def exchange(messages):
+    if len(messages) == 1:
+        return [lax.all_to_all(messages[0], "seq", split_axis=0, concat_axis=0, tiled=True)]
     count = len(messages)
-    half = count // 2
-    messages = list(messages)
-    if before is not None:
-        messages[1:half] = hold(messages[1:half], before[1:half])
-        messages[half:] = hold(messages[half:], before[-1:])
     received = list(messages)
     for k in range(count - 1, 0, -1):
         pairs = [(i, i ^ k) for i in range(count)]
@@ -56,11 +69,14 @@
     return received
 
 
-def pack_kernel(me, query, key, value, d_out, *refs, first, heads, peers, per_peer, head_dim):
-    messages = refs[-4 - peers : -4]
+def pack_kernel(
+    me, query, key, value, d_out, *refs, first, heads, peers, apart, per_peer, head_dim
+):
+    messages = refs[-4 - (peers if apart else 1) : -4]
     stage, ready, in_sems, out_sems = refs[-4:]
     sources = (key, value, query, d_out)
-    aligned = per_peer % LANES == 0
+    aligned = apart and per_peer % LANES == 0
+    at_once = aligned or not apart
     order = range(peers - 1, -1, -1)
 
     def span(item):
@@ -81,8 +97,10 @@
         )
 
     def send(item):
-        slot = item if aligned else me[0] ^ item
-        return pltpu.make_async_copy(ready.at[slot], messages[item], out_sems.at[item])
+        target, peer = part_of(messages, me, item)
+        return pltpu.make_async_copy(
+            ready.at[item if aligned else peer], target, out_sems.at[item]
+        )
 
     for item in order:
         for i in range(4):
@@ -98,35 +116,37 @@
                     [stage[2 * kind, item, :, lanes], stage[2 * kind + 1, item, :, lanes]],
                     axis=1,
                 )
-        if aligned:
+        if at_once:
             send(item).start()
-    if not aligned:
+    if not at_once:
         for item in order:
             send(item).start()
     for item in order:
         send(item).wait()
 
 
-def pack(me, arrays, start, heads, heads_here, peers, head_dim, after):
+def pack(me, arrays, start, heads, heads_here, peers, head_dim, apart, after):
     rows = arrays[0].shape[0]
     dtype = arrays[0].dtype
     shape = (heads, 2, rows, 2 * head_dim)
     width = (-(-heads * head_dim // LANES) + 1) * LANES
     anywhere = pl.BlockSpec(memory_space=pltpu.HBM)
+    outs = message_outs(peers, shape, dtype, apart)
     return pl.pallas_call(
         functools.partial(
             pack_kernel,
             first=start * head_dim,
             heads=heads,
             peers=peers,
+            apart=apart,
             per_peer=heads_here * head_dim,
             head_dim=head_dim,
         ),
         in_specs=[pl.BlockSpec(memory_space=pltpu.SMEM)]
         + [anywhere] * 4
         + [pl.BlockSpec(memory_space=pl.ANY)] * len(after),
-        out_specs=[anywhere] * peers,
-        out_shape=[pltpu.HBM(shape, dtype)] * peers,
+        out_specs=[anywhere] * len(outs),
+        out_shape=outs,
         scratch_shapes=[
             pltpu.VMEM((4, peers, rows, width), dtype),
             pltpu.VMEM((peers,) + shape, dtype),
@@ -138,9 +158,10 @@
     )(me, *[in_hbm(x) for x in arrays], *after)
 
 
-def unpack_kernel(me, *refs, chunk, peers, earlier, jobs):
-    groups = [refs[c * peers : (c + 1) * peers] for c in range(chunk + 1)]
-    outs = refs[(chunk + 1) * peers + earlier :][:4]
+def unpack_kernel(me, *refs, chunk, peers, counts, earlier, jobs):
+    ends = [sum(counts[: c + 1]) for c in range(chunk + 1)]
+    groups = [refs[end - count : end] for end, count in zip(ends, counts)]
+    outs = refs[ends[-1] + earlier :][:4]
     stages = refs[-3 - chunk - 1 : -3]
     ready, in_sems, out_sems = refs[-3:]
     head_dim = ready.shape[-1] // 2
@@ -151,13 +172,13 @@
         for c in chunks_used
     }
 
-    def fetch(which, item, slot):
+    def fetch(which, item, slot=None):
         heads = heads_used[which]
         some = pl.ds(heads[0], heads[-1] - heads[0] + 1)
+        source, peer = part_of(groups[which], me, item)
+        slot = peer if slot is None else slot
         return pltpu.make_async_copy(
-            groups[which][item].at[some],
-            stages[which].at[slot, some],
-            in_sems.at[which, slot],
+            source.at[some], stages[which].at[slot, some], in_sems.at[which, slot]
         )
 
     def send(job, i):
@@ -170,7 +191,7 @@
 
     for item in range(peers):
         for which in chunks_used:
-            fetch(which, item, me[0] ^ item).start()
+            fetch(which, item).start()
     waited = set()
 
     def wait_for(which, peer):
@@ -197,8 +218,8 @@
 
 def unpack(me, messages, starts, heads_here, earlier):
     chunk = len(messages) - 1
-    peers = len(messages[0])
-    _, _, rows, pair_dim = messages[0][0].shape
+    peers = lax.axis_size("seq")
+    _, _, rows, pair_dim = message_shape(messages[0])
     head_dim = pair_dim // 2
     columns = peers * heads_here * head_dim
     dtype = messages[0][0].dtype
@@ -219,14 +240,19 @@
     anywhere = pl.BlockSpec(memory_space=pltpu.HBM)
     return pl.pallas_call(
         functools.partial(
-            unpack_kernel, chunk=chunk, peers=peers, earlier=len(earlier), jobs=jobs
+            unpack_kernel,
+            chunk=chunk,
+            peers=peers,
+            counts=[len(group) for group in messages],
+            earlier=len(earlier),
+            jobs=jobs,
         ),
         in_specs=[pl.BlockSpec(memory_space=pltpu.SMEM)]
         + [anywhere] * (len(flat) + len(earlier)),
         out_specs=[anywhere] * 4,
         out_shape=[pltpu.HBM((rows, columns), dtype)] * 4,
         input_output_aliases={1 + len(flat) + i: i for i in range(len(earlier))},
-        scratch_shapes=[pltpu.VMEM((peers,) + m[0].shape, dtype) for m in messages]
+        scratch_shapes=[pltpu.VMEM((peers,) + message_shape(m), dtype) for m in messages]
         + [
             pltpu.VMEM((4, len(jobs), rows, LANES), dtype),
             pltpu.SemaphoreType.DMA((chunk + 1, peers)),
@@ -237,15 +263,14 @@
     )(me, *[in_hbm(x) for x in (*flat, *earlier)])
 
 
-def pick_kernel(me, asked, *refs, block_rows):
-    peers = len(refs) - 4
-    for_next, for_prev, stage, sems = refs[peers:]
-    rows = stage.shape[2]
+def pick_kernel(me, asked, *refs, count, block_rows):
+    for_next, for_prev, stage, sems = refs[-4:]
+    peers, _, rows, _ = stage.shape
     each = rows // block_rows
 
     def fetch(item):
-        slot = me[0] ^ item
-        return pltpu.make_async_copy(refs[item].at[:, 0], stage.at[slot], sems.at[item])
+        source, peer = part_of(refs[:count], me, item)
+        return pltpu.make_async_copy(source.at[:, 0], stage.at[peer], sems.at[item])
 
     for item in range(peers):
         fetch(item).start()
@@ -258,15 +283,15 @@
         target[i % CROSS] = stage[peer, :, pl.ds(start, block_rows)]
 
 
-def pick(me, messages, asked, block_rows):
-    heads, _, rows, lanes = messages[0].shape
+def pick(me, messages, asked, block_rows, after):
+    heads, _, rows, lanes = message_shape(messages)
     dtype = messages[0].dtype
-    peers = len(messages)
+    peers = lax.axis_size("seq")
     picked = jax.ShapeDtypeStruct((CROSS, heads, block_rows, lanes), dtype)
     return pl.pallas_call(
-        functools.partial(pick_kernel, block_rows=block_rows),
+        functools.partial(pick_kernel, count=len(messages), block_rows=block_rows),
         in_specs=[pl.BlockSpec(memory_space=pltpu.SMEM)] * 2
-        + [pl.BlockSpec(memory_space=pltpu.HBM)] * peers,
+        + [pl.BlockSpec(memory_space=pltpu.HBM)] * (len(messages) + len(after)),
         out_specs=[pl.BlockSpec(memory_space=pltpu.VMEM)] * 2,
         out_shape=[picked, picked],
         scratch_shapes=[
@@ -275,15 +300,14 @@
         ],
         compiler_params=pltpu.CompilerParams(vmem_limit_bytes=SMALL_VMEM),
         name="pick",
-    )(me, asked, *[in_hbm(x) for x in messages])
+    )(me, asked, *[in_hbm(x) for x in (*messages, *after)])
 
 
 def attend_kernel(me, lists, came_prev, came_next, *refs, block_rows, head_dim, per_list):
-    peers = len(refs) - 13
-    messages = refs[:peers]
-    back, own, to_prev, to_next = refs[peers : peers + 4]
-    message, table, turned, sums, both_even, both_odd, low_even, low_odd, sems = refs[peers + 4 :]
-    _, heads, _, rows, lanes = message.shape
+    messages = refs[:-13]
+    back, own, to_prev, to_next = refs[-13:-9]
+    message, table, turned, sums, both_even, both_odd, low_even, low_odd, sems = refs[-9:]
+    peers, heads, _, rows, lanes = message.shape
     each = rows // block_rows
     blocks = peers * each
     window = blocks + 2 * CROSS
@@ -296,8 +320,8 @@
     step_rows = 64
 
     def fetch(item):
-        slot = me[0] ^ item
-        return pltpu.make_async_copy(messages[item], message.at[slot], sems.at[item])
+        source, peer = part_of(messages, me, item)
+        return pltpu.make_async_copy(source, message.at[peer], sems.at[item])
 
     for item in range(peers):
         fetch(item).start()
@@ -421,9 +445,10 @@
 
 
 def attend(me, messages, came_prev, came_next, lists, block_rows):
-    heads, _, rows, lanes = messages[0].shape
+    shape = message_shape(messages)
+    heads, _, rows, lanes = shape
     dtype = messages[0].dtype
-    peers = len(messages)
+    peers = lax.axis_size("seq")
     per_list = lists.shape[-1]
     keys = per_list * block_rows
     blocks = peers * rows // block_rows
@@ -436,7 +461,7 @@
             attend_kernel, block_rows=block_rows, head_dim=lanes // 2, per_list=per_list
         ),
         in_specs=[scalars, scalars, inside, inside]
-        + [pl.BlockSpec(memory_space=pltpu.HBM)] * peers,
+        + [pl.BlockSpec(memory_space=pltpu.HBM)] * len(messages),
         out_specs=[inside] * 4,
         out_shape=[
             pltpu.VMEM((peers, heads, rows, lanes), dtype),
@@ -445,7 +470,7 @@
             cross_shape,
         ],
         scratch_shapes=[
-            pltpu.VMEM((peers,) + messages[0].shape, dtype),
+            pltpu.VMEM((peers,) + shape, dtype),
             pltpu.VMEM((heads, window, block_rows, lanes), dtype),
             pltpu.VMEM((heads, window, lanes, block_rows), dtype),
             pltpu.VMEM((heads, window, block_rows, lanes), jnp.float32),
@@ -461,15 +486,15 @@
 
 
 def finish_kernel(me, asked, back, own, later, earlier, *refs, block_rows):
-    peers = len(refs) - 3
-    messages = refs[:peers]
-    sums, ready, sems = refs[peers:]
-    _, heads, _, rows, _ = ready.shape
+    messages = refs[:-3]
+    sums, ready, sems = refs[-3:]
+    peers, heads, _, rows, _ = ready.shape
     each = rows // block_rows
 
     def send(item, head):
+        target, peer = part_of(messages, me, item)
         return pltpu.make_async_copy(
-            ready.at[me[0] ^ item, head], messages[item].at[head], sems.at[item, head]
+            ready.at[peer, head], target.at[head], sems.at[item, head]
         )
 
     for head in range(heads):
@@ -491,17 +516,18 @@
             send(item, head).wait()
 
 
-def finish(me, back, own, later, earlier, asked):
+def finish(me, back, own, later, earlier, asked, apart):
     peers, heads, rows, lanes = back.shape
     _, blocks, block_rows, _ = own.shape
     inside = pl.BlockSpec(memory_space=pltpu.VMEM)
     scalars = pl.BlockSpec(memory_space=pltpu.SMEM)
     shape = (heads, 2, rows, lanes)
+    outs = message_outs(peers, shape, back.dtype, apart)
     return pl.pallas_call(
         functools.partial(finish_kernel, block_rows=block_rows),
         in_specs=[scalars, scalars] + [inside] * 4,
-        out_specs=[pl.BlockSpec(memory_space=pltpu.HBM)] * peers,
-        out_shape=[pltpu.HBM(shape, back.dtype)] * peers,
+        out_specs=[pl.BlockSpec(memory_space=pltpu.HBM)] * len(outs),
+        out_shape=outs,
         scratch_shapes=[
             pltpu.VMEM((blocks, block_rows, lanes), jnp.float32),
             pltpu.VMEM((peers,) + shape, back.dtype),
@@ -554,15 +580,21 @@
     )
 
     me = lax.axis_index("seq").astype(jnp.int32).reshape(1)
+    me = lax.axis_index("seq").astype(jnp.int32).reshape(1)
+    last = chunks - 1
     came = []
-    for start, size in zip(starts, sizes):
+    for chunk, (start, size) in enumerate(zip(starts, sizes)):
         after = (asked, local_ids) if came else ()
-        packed = pack(me, arrays, start, size, heads_here, peers, head_dim, after)
-        came.append(exchange(packed, came[-1] if came else None))
+        packed = pack(
+            me, arrays, start, size, heads_here, peers, head_dim, chunk == 0, after
+        )
+        if chunk == 1:
+            packed = hold(packed, came[0][peers // 2 :])
+        came.append(exchange(packed))
     received = []
-    outs = ()
-    for messages, start, size in zip(came, starts, sizes):
-        for_next, for_prev = pick(me, messages, asked, block_rows)
+    outs = finished = ()
+    for chunk, (messages, start, size) in enumerate(zip(came, starts, sizes)):
+        for_next, for_prev = pick(me, messages, asked, block_rows, finished[:1])
         came_prev = from_behind(for_next, "slab", 1)
         came_next = from_behind(for_prev, "slab", -1)
         back, own, to_prev, to_next = attend(
@@ -570,7 +602,8 @@
         )
         later = from_behind(to_prev, "slab", -1)
         earlier = from_behind(to_next, "slab", 1)
-        received.append(exchange(finish(me, back, own, later, earlier, asked)))
+        finished = finish(me, back, own, later, earlier, asked, chunk == last)
+        received.append(exchange(finished))
         outs = unpack(me, received, starts, heads_here, outs)
     return tuple(outs)
 

time: 399 us -> 370 us (0.927); the launches traced: 398 us -> 365 us
  waiting for transfers between devices: 233 us -> 195 us
    ppermute x28 -> x14, waiting for transfers between devices: 232 us -> 183 us  [exchange(): received[k] = lax.ppermute(messages[k], 'seq', pairs)]
    ppermute x28 -> x14, starting transfers between devices: 39.5 us -> 18.2 us  [exchange(): received[k] = lax.ppermute(messages[k], 'seq', pairs)]
    ppermute x10, starting transfers between devices: 20.5 us -> 33.7 us  [from_behind(): return lax.ppermute(x, axis, pairs)]
    ppermute x10, waiting for transfers between devices: 0.82 us -> 12.2 us  [from_behind(): return lax.ppermute(x, axis, pairs)]
    all_to_all x0 -> x2, starting transfers between devices: none -> 9.77 us  [exchange(): lax.all_to_all(messages[0], 'seq', split_axis=0, concat_axis=0, tiled=True)]
  transfers between devices with their start and end apart: 38 -> 26, of which waited for: 20 -> 18; matrix products, arithmetic and copies ran while one was open for 0% -> 0% of each run, Pallas kernels for 23% -> 26%
where the time goes in v5:
time: 370 us; the launch traced here: 365 us
  waiting for transfers between devices  195 us (53%)
  Pallas kernels  97.5 us (26%)
  starting transfers between devices  61.7 us (17%)
  local copies, waits for them, and re-layouts  6.6 us (2%)
    ppermute x14, waiting for transfers between devices, exchange(): received[k] = lax.ppermute(messages[k], 'seq', pairs)  183 us
    pallas_call x2, Pallas kernels, attend(): pl.pallas_call(functools.partial(attend_kernel, block_rows=block_rows, he...  72.8 us
    ppermute x10, starting transfers between devices, from_behind(): return lax.ppermute(x, axis, pairs)  33.7 us
    ppermute x14, starting transfers between devices, exchange(): received[k] = lax.ppermute(messages[k], 'seq', pairs)  18.2 us
    ppermute x10, waiting for transfers between devices, from_behind(): return lax.ppermute(x, axis, pairs)  12.2 us
    all_to_all x2, starting transfers between devices, exchange(): lax.all_to_all(messages[0], 'seq', split_axis=0, concat_axis=0, tiled=True)  9.77 us
    pallas_call x2, Pallas kernels, pack(): pl.pallas_call(functools.partial(pack_kernel, first=start * head_dim, hea...  7.77 us
    pallas_call x2, Pallas kernels, unpack(): pl.pallas_call(functools.partial(unpack_kernel, chunk=chunk, peers=peers,...  7.44 us
  transfers between devices with their start and end apart: 26, of which 18 were waited for; matrix products, arithmetic and copies ran while one was open for 0% of the time, Pallas kernels for 26%

profile of v5, /device:TPU:8, one launch (start us, length us, event | category | flops | bytes accessed | tf_op | source)
XLA Modules:
  0.0 364.9 jit_solution(16776350752612019782)
XLA Ops:
  3.0 1.3 collective-permute-start
  4.3 3.9 %pack.2 = (bf16[3,2,256,128]{3,2,1,0:T(8,128)(2,1)}, bf16[3,2,256,128]{3,2,1,0:T(8,128)(2,1)}, bf16[3,2,256,128]{3,2,1,0:T(8,128)(2,1)}, bf16[3,2,256,128]{3,2,1...) custom-call(s32[1]{0:T(128)} %bitcast.me, ...), custom_call_target="tpu_custom_call" | custom-call | tf_op jit(solution)/shard_map/pack/pallas_call | solution.py:135
  8.2 2.7 collective-permute-start.5
  12.2 1.6 collective-permute-start.7
  14.2 1.3 top_k.24
  15.7 1.9 collective-permute-start.1
  18.6 3.9 %pack.3.refs_0_ = bf16[8,3,2,256,128]{4,3,2,1,0:T(8,128)(2,1)} custom-call(s32[1]{0:T(128)} %bitcast.me, bf16[256,3072]{1,0:T(8,128)(2,1)} %query.3, bf16[256,3072]{1,0:T(8,128)(2,1)} %key.3, bf16[256,3072]{1,0:T(8,128)(2,1)} %value.3, bf16[256,3072]{1,0:T(8,128)(2,1)} %d_out.3, s32[8]{0:T(128)S(1)} %pad_add_fusion.asked.refs_0_, ...), custom_call_target="tpu_custom_call" | custom-call | tf_op jit(solution)/shard_map/pack/pallas_call | solution.py:135
  22.4 31.9 %collective-permute-done.5.refs_4_.refs_1_ = bf16[3,2,256,128]{3,2,1,0:T(8,128)(2,1)S(1)} collective-permute-done((bf16[3,2,256,128]{3,2,1,0:T(8,128)(2,1)}, bf16[3,2,256,128]{3,2,1,0:T(8,128)(2,1)S(1)}, u32[]{:S(2)}, u32[]{:S(2)}) %collective-permute-start.5) | collective-permute-done | bytes 393248 | tf_op jit(solution)/shard_map/ppermute | solution.py:68
  54.3 8.4 %collective-permute-done.6.refs_5_.refs_2_ = bf16[3,2,256,128]{3,2,1,0:T(8,128)(2,1)S(1)} collective-permute-done((bf16[3,2,256,128]{3,2,1,0:T(8,128)(2,1)}, bf16[3,2,256,128]{3,2,1,0:T(8,128)(2,1)S(1)}, u32[]{:S(2)}, u32[]{:S(2)}) %collective-permute-start.6) | collective-permute-done | bytes 393248 | tf_op jit(solution)/shard_map/ppermute | solution.py:68
  62.7 8.4 %collective-permute-done.7.refs_6_.refs_3_ = bf16[3,2,256,128]{3,2,1,0:T(8,128)(2,1)S(1)} collective-permute-done((bf16[3,2,256,128]{3,2,1,0:T(8,128)(2,1)}, bf16[3,2,256,128]{3,2,1,0:T(8,128)(2,1)S(1)}, u32[]{:S(2)}, u32[]{:S(2)}) %collective-permute-start.7) | collective-permute-done | bytes 393248 | tf_op jit(solution)/shard_map/ppermute | solution.py:68
  71.2 9.0 %collective-permute-done.8.refs_7_.refs_4_ = bf16[3,2,256,128]{3,2,1,0:T(8,128)(2,1)S(1)} collective-permute-done((bf16[3,2,256,128]{3,2,1,0:T(8,128)(2,1)}, bf16[3,2,256,128]{3,2,1,0:T(8,128)(2,1)S(1)}, u32[]{:S(2)}, u32[]{:S(2)}) %collective-permute-start.8) | collective-permute-done | bytes 393248 | tf_op jit(solution)/shard_map/ppermute | solution.py:68
  80.9 5.5 %all-to-all-start.1 = ((bf16[8,3,2,256,128]{4,3,2,1,0:T(8,128)(2,1)}), bf16[8,3,2,256,128]{4,3,2,1,0:T(8,128)(2,1)S(1)}, u32[]{:S(2)}, u32[]{:S(2)}) async-start(bf16[8,3,2,256,128]{4,3,2,1,0:T(8,128)(2,1)} %hold.1), calls=%async_computation.1 | async-start | bytes 6291456 | tf_op jit(solution)/shard_map/all_to_all | solution.py:63
  86.4 1.5 collective-permute-start.2
  88.4 1.5 collective-permute-start.4
  89.9 30.5 %collective-permute-done.2.refs_1_ = bf16[3,2,256,128]{3,2,1,0:T(8,128)(2,1)S(1)} collective-permute-done((bf16[3,2,256,128]{3,2,1,0:T(8,128)(2,1)}, bf16[3,2,256,128]{3,2,1,0:T(8,128)(2,1)S(1)}, u32[]{:S(2)}, u32[]{:S(2)}) %collective-permute-start.2) | collective-permute-done | bytes 393248 | tf_op jit(solution)/shard_map/ppermute | solution.py:68
  120.3 28.0 %collective-permute-done.3.refs_2_ = bf16[3,2,256,128]{3,2,1,0:T(8,128)(2,1)S(1)} collective-permute-done((bf16[3,2,256,128]{3,2,1,0:T(8,128)(2,1)}, bf16[3,2,256,128]{3,2,1,0:T(8,128)(2,1)S(1)}, u32[]{:S(2)}, u32[]{:S(2)}) %collective-permute-start.3) | collective-permute-done | bytes 393248 | tf_op jit(solution)/shard_map/ppermute | solution.py:68
  148.4 8.4 %collective-permute-done.4.refs_3_ = bf16[3,2,256,128]{3,2,1,0:T(8,128)(2,1)S(1)} collective-permute-done((bf16[3,2,256,128]{3,2,1,0:T(8,128)(2,1)}, bf16[3,2,256,128]{3,2,1,0:T(8,128)(2,1)S(1)}, u32[]{:S(2)}, u32[]{:S(2)}) %collective-permute-start.4) | collective-permute-done | bytes 393248 | tf_op jit(solution)/shard_map/ppermute | solution.py:68
  157.6 2.1 pick.2
  159.7 1.3 collective-permute-start.9
  161.0 1.3 collective-permute-start.10
  162.3 4.1 %collective-permute-done.10.came_next = bf16[4,3,128,128]{3,2,1,0:T(8,128)(2,1)S(1)} collective-permute-done((bf16[4,3,128,128]{3,2,1,0:T(8,128)(2,1)S(1)}, bf16[4,3,128,128]{3,2,1,0:T(8,128)(2,1)S(1)}, u32[]{:S(2)}, u32[]{:S(2)}) %collective-permute-start.10) | collective-permute-done | bytes 393248 | tf_op jit(solution)/shard_map/ppermute | solution.py:25
  166.5 36.4 %attend.2 = (bf16[8,3,256,128]{3,2,1,0:T(8,128)(2,1)S(1)}, f32[3,16,128,128]{3,2,1,0:T(8,128)S(1)}, bf16[4,3,128,128]{3,2,1,0:T(8,128)(2,1)S(1)}, bf16[4,3,128,128]{3,2,1,0:T(8,128)(2,1)S(1)}) custom-call(s32[1]{0:T(128)} %bitcast.me, s32[3,16,8]{2,1,0:T(8,128)S(1)} %get-tuple-element.81.lists, ...), custom_call_target="tpu_custom_call" | custom-call | tf_op jit(solution)/shard_map/attend/pallas_call | solution.py:459
  202.9 1.3 collective-permute-start.11
  204.2 8.5 %collective-permute-start.12 = (bf16[4,3,128,128]{3,2,1,0:T(8,128)(2,1)S(1)}, bf16[4,3,128,128]{3,2,1,0:T(8,128)(2,1)S(1)}, u32[]{:S(2)}, u32[]{:S(2)}) collective-permute-start(bf16[4,3,128,128]{3,2,1,0:T(8,128)(2,1)S(1)} %get-tuple-element.57), channel_id=1, source_target_pairs={{0,8},{8,16},{16,24},{1,9},{9,17},{17,25},{2,10},{10,18},{18,26},{... | collective-permute-start | bytes 1179656 | tf_op jit(solution)/shard_map/ppermute | solution.py:25
  212.7 1.3 collective-permute-done.12.earlier
  214.0 2.6 finish.2.refs_1_
  216.7 1.7 copy-done.1
  218.3 4.3 %all-to-all-start = ((bf16[8,3,2,256,128]{4,3,2,1,0:T(8,128)(2,1)}), bf16[8,3,2,256,128]{4,3,2,1,0:T(8,128)(2,1)S(1)}, u32[]{:S(2)}, u32[]{:S(2)}) async-start(bf16[8,3,2,256,128]{4,3,2,1,0:T(8,128)(2,1)} %finish.2.refs_1_), calls=%async_computation | async-start | bytes 6291456 | tf_op jit(solution)/shard_map/all_to_all | solution.py:63
  222.6 2.1 pick.3
  224.8 6.5 %collective-permute-start.13 = (bf16[4,3,128,128]{3,2,1,0:T(8,128)(2,1)S(1)}, bf16[4,3,128,128]{3,2,1,0:T(8,128)(2,1)S(1)}, u32[]{:S(2)}, u32[]{:S(2)}) collective-permute-start(bf16[4,3,128,128]{3,2,1,0:T(8,128)(2,1)S(1)} %get-tuple-element.58), channel_id=1, source_target_pairs={{0,8},{8,16},{16,24},{1,9},{9,17},{17,25},{2,10},{10,18},{18,26},{... | collective-permute-start | bytes 1179656 | tf_op jit(solution)/shard_map/ppermute | solution.py:25
  231.2 1.3 collective-permute-start.14
  232.5 4.8 %collective-permute-done.14.came_next = bf16[4,3,128,128]{3,2,1,0:T(8,128)(2,1)S(1)} collective-permute-done((bf16[4,3,128,128]{3,2,1,0:T(8,128)(2,1)S(1)}, bf16[4,3,128,128]{3,2,1,0:T(8,128)(2,1)S(1)}, u32[]{:S(2)}, u32[]{:S(2)}) %collective-permute-start.14) | collective-permute-done | bytes 393248 | tf_op jit(solution)/shard_map/ppermute | solution.py:25
  237.4 36.4 %attend.3 = (bf16[8,3,256,128]{3,2,1,0:T(8,128)(2,1)S(1)}, f32[3,16,128,128]{3,2,1,0:T(8,128)S(1)}, bf16[4,3,128,128]{3,2,1,0:T(8,128)(2,1)S(1)}, bf16[4,3,128,128]{3,2,1,0:T(8,128)(2,1)S(1)}) custom-call(s32[1]{0:T(128)} %bitcast.me, s32[3,16,8]{2,1,0:T(8,128)S(1)} %get-tuple-element.80.lists, ...), custom_call_target="tpu_custom_call" | custom-call | tf_op jit(solution)/shard_map/attend/pallas_call | solution.py:459
  273.8 1.3 collective-permute-start.15
  275.1 9.0 %collective-permute-start.16 = (bf16[4,3,128,128]{3,2,1,0:T(8,128)(2,1)S(1)}, bf16[4,3,128,128]{3,2,1,0:T(8,128)(2,1)S(1)}, u32[]{:S(2)}, u32[]{:S(2)}) collective-permute-start(bf16[4,3,128,128]{3,2,1,0:T(8,128)(2,1)S(1)} %get-tuple-element.63), channel_id=1, source_target_pairs={{0,8},{8,16},{16,24},{1,9},{9,17},{17,25},{2,10},{10,18},{18,26},{... | collective-permute-start | bytes 1179656 | tf_op jit(solution)/shard_map/ppermute | solution.py:25
  285.2 2.6 finish.3
  287.9 1.5 collective-permute-start.17
  289.9 1.5 collective-permute-start.19
  291.4 2.4 collective-permute-start.20
  293.8 1.5 collective-permute-start.21
  295.9 1.5 collective-permute-start.22
  297.4 17.3 %collective-permute-done.18.refs_3_ = bf16[3,2,256,128]{3,2,1,0:T(8,128)(2,1)S(1)} collective-permute-done((bf16[3,2,256,128]{3,2,1,0:T(8,128)(2,1)}, bf16[3,2,256,128]{3,2,1,0:T(8,128)(2,1)S(1)}, u32[]{:S(2)}, u32[]{:S(2)}) %collective-permute-start.18) | collective-permute-done | bytes 393248 | tf_op jit(solution)/shard_map/ppermute | solution.py:68
  315.4 1.6 copy-done
  317.1 3.0 unpack.2
  320.1 3.1 collective-permute-done.19.refs_4_
  324.0 26.9 %collective-permute-done.22.refs_7_ = bf16[3,2,256,128]{3,2,1,0:T(8,128)(2,1)} collective-permute-done((bf16[3,2,256,128]{3,2,1,0:T(8,128)(2,1)}, bf16[3,2,256,128]{3,2,1,0:T(8,128)(2,1)}, u32[]{:S(2)}, u32[]{:S(2)}) %collective-permute-start.22) | collective-permute-done | bytes 393248 | tf_op jit(solution)/shard_map/ppermute | solution.py:68
  350.9 9.4 %collective-permute-done.23.refs_8_ = bf16[3,2,256,128]{3,2,1,0:T(8,128)(2,1)} collective-permute-done((bf16[3,2,256,128]{3,2,1,0:T(8,128)(2,1)}, bf16[3,2,256,128]{3,2,1,0:T(8,128)(2,1)}, u32[]{:S(2)}, u32[]{:S(2)}) %collective-permute-start.23) | collective-permute-done | bytes 393248 | tf_op jit(solution)/shard_map/ppermute | solution.py:68
  360.3 4.4 %unpack.3 = (bf16[256,3072]{1,0:T(8,128)(2,1)}, bf16[256,3072]{1,0:T(8,128)(2,1)}, bf16[256,3072]{1,0:T(8,128)(2,1)}, bf16[256,3072]{1,0:T(8,128)(2,1)}) custom-call(s32[1]{0:T(128)} %bitcast.me, bf16[8,3,2,256,128]{4,3,2,1,0:T(8,128)(2,1)} %copy-done, ...), custom_call_target="tpu_custom_call", output_to_operand_aliasing={{0}: (10, {}), {1}: (11, {}), {2}: (12, {}), {3}: (13, {})} | custom-call | tf_op jit(solution)/shard_map/unpack/pallas_call | solution.py:241
  (57 shorter events, 11.2 us)
Async XLA Ops:
  3.0 12.7 %collective-permute-start = (s32[4]{0:T(128)S(1)}, s32[4]{0:T(128)S(1)}, u32[]{:S(2)}, u32[]{:S(2)}) collective-permute-start(s32[4]{0:T(128)S(1)} %get-tuple-element.83), channel_id=1, source_target_pairs={{8,0},{16,8},{24,16},{9,1},{17,9},{25,17},{10,2},{18,10},{26,18},{... | collective-permute-start | bytes 56 | tf_op jit(solution)/shard_map/ppermute | solution.py:25
  4.3 11.1 %copy-start.11 = (s32[6,16,8]{1,2,0:T(8,128)S(1)}, s32[6,16,8]{1,2,0:T(8,128)}, u32[]{:S(2)}) copy-start(s32[6,16,8]{1,2,0:T(8,128)} %param.9) | copy-start | bytes 9220
  8.2 46.1 %collective-permute-start.5 = (bf16[3,2,256,128]{3,2,1,0:T(8,128)(2,1)}, bf16[3,2,256,128]{3,2,1,0:T(8,128)(2,1)S(1)}, u32[]{:S(2)}, u32[]{:S(2)}) collective-permute-start(bf16[3,2,256,128]{3,2,1,0:T(8,128)(2,1)} %get-tuple-element.48), channel_id=1, source_target_pairs={{0,4},{1,5},{2,6},{3,7},{4,0},{5,1},{6,2},{7,3},{8,12},{9,13},{10,... | collective-permute-start | bytes 1179656 | tf_op jit(solution)/shard_map/ppermute | solution.py:68
  10.9 51.8 %collective-permute-start.6 = (bf16[3,2,256,128]{3,2,1,0:T(8,128)(2,1)}, bf16[3,2,256,128]{3,2,1,0:T(8,128)(2,1)S(1)}, u32[]{:S(2)}, u32[]{:S(2)}) collective-permute-start(bf16[3,2,256,128]{3,2,1,0:T(8,128)(2,1)} %get-tuple-element.49), channel_id=1, source_target_pairs={{0,5},{1,4},{2,7},{3,6},{4,1},{5,0},{6,3},{7,2},{8,13},{9,12},{10,... | collective-permute-start | bytes 1179656 | tf_op jit(solution)/shard_map/ppermute | solution.py:68
  12.2 59.0 %collective-permute-start.7 = (bf16[3,2,256,128]{3,2,1,0:T(8,128)(2,1)}, bf16[3,2,256,128]{3,2,1,0:T(8,128)(2,1)S(1)}, u32[]{:S(2)}, u32[]{:S(2)}) collective-permute-start(bf16[3,2,256,128]{3,2,1,0:T(8,128)(2,1)} %get-tuple-element.50), channel_id=1, source_target_pairs={{0,6},{1,7},{2,4},{3,5},{4,2},{5,3},{6,0},{7,1},{8,14},{9,15},{10,... | collective-permute-start | bytes 1179656 | tf_op jit(solution)/shard_map/ppermute | solution.py:68
  13.7 66.4 %collective-permute-start.8 = (bf16[3,2,256,128]{3,2,1,0:T(8,128)(2,1)}, bf16[3,2,256,128]{3,2,1,0:T(8,128)(2,1)S(1)}, u32[]{:S(2)}, u32[]{:S(2)}) collective-permute-start(bf16[3,2,256,128]{3,2,1,0:T(8,128)(2,1)} %get-tuple-element.51), channel_id=1, source_target_pairs={{0,7},{1,6},{2,5},{3,4},{4,3},{5,2},{6,1},{7,0},{8,15},{9,14},{10,... | collective-permute-start | bytes 1179656 | tf_op jit(solution)/shard_map/ppermute | solution.py:68
  15.7 2.7 collective-permute-start.1
  54.3 25.8 %copy-start.2 = (bf16[3,2,256,128]{3,2,1,0:T(8,128)(2,1)}, bf16[3,2,256,128]{3,2,1,0:T(8,128)(2,1)S(1)}, u32[]{:S(2)}) copy-start(bf16[3,2,256,128]{3,2,1,0:T(8,128)(2,1)S(1)} %collective-permute-done.5.refs_4_.refs_1_) | copy-start | bytes 1179652
  62.7 17.4 %copy-start.3 = (bf16[3,2,256,128]{3,2,1,0:T(8,128)(2,1)}, bf16[3,2,256,128]{3,2,1,0:T(8,128)(2,1)S(1)}, u32[]{:S(2)}) copy-start(bf16[3,2,256,128]{3,2,1,0:T(8,128)(2,1)S(1)} %collective-permute-done.6.refs_5_.refs_2_) | copy-start | bytes 1179652
  71.2 9.0 %copy-start.4 = (bf16[3,2,256,128]{3,2,1,0:T(8,128)(2,1)}, bf16[3,2,256,128]{3,2,1,0:T(8,128)(2,1)S(1)}, u32[]{:S(2)}) copy-start(bf16[3,2,256,128]{3,2,1,0:T(8,128)(2,1)S(1)} %collective-permute-done.7.refs_6_.refs_3_) | copy-start | bytes 1179652
  80.2 0.7 copy-start.5
  80.9 135.7 %all-to-all-start.1 = ((bf16[8,3,2,256,128]{4,3,2,1,0:T(8,128)(2,1)}), bf16[8,3,2,256,128]{4,3,2,1,0:T(8,128)(2,1)S(1)}, u32[]{:S(2)}, u32[]{:S(2)}) async-start(bf16[8,3,2,256,128]{4,3,2,1,0:T(8,128)(2,1)} %hold.1), calls=%async_computation.1 | async-start | bytes 6291456 | tf_op jit(solution)/shard_map/all_to_all | solution.py:63
  86.4 34.0 %collective-permute-start.2 = (bf16[3,2,256,128]{3,2,1,0:T(8,128)(2,1)}, bf16[3,2,256,128]{3,2,1,0:T(8,128)(2,1)S(1)}, u32[]{:S(2)}, u32[]{:S(2)}) collective-permute-start(bf16[3,2,256,128]{3,2,1,0:T(8,128)(2,1)} %get-tuple-element.45), channel_id=1, source_target_pairs={{0,1},{1,0},{2,3},{3,2},{4,5},{5,4},{6,7},{7,6},{8,9},{9,8},{10,11... | collective-permute-start | bytes 1179656 | tf_op jit(solution)/shard_map/ppermute | solution.py:68
  87.8 60.5 %collective-permute-start.3 = (bf16[3,2,256,128]{3,2,1,0:T(8,128)(2,1)}, bf16[3,2,256,128]{3,2,1,0:T(8,128)(2,1)S(1)}, u32[]{:S(2)}, u32[]{:S(2)}) collective-permute-start(bf16[3,2,256,128]{3,2,1,0:T(8,128)(2,1)} %get-tuple-element.46), channel_id=1, source_target_pairs={{0,2},{1,3},{2,0},{3,1},{4,6},{5,7},{6,4},{7,5},{8,10},{9,11},{10,... | collective-permute-start | bytes 1179656 | tf_op jit(solution)/shard_map/ppermute | solution.py:68
  88.4 68.4 %collective-permute-start.4 = (bf16[3,2,256,128]{3,2,1,0:T(8,128)(2,1)}, bf16[3,2,256,128]{3,2,1,0:T(8,128)(2,1)S(1)}, u32[]{:S(2)}, u32[]{:S(2)}) collective-permute-start(bf16[3,2,256,128]{3,2,1,0:T(8,128)(2,1)} %get-tuple-element.47), channel_id=1, source_target_pairs={{0,3},{1,2},{2,1},{3,0},{4,7},{5,6},{6,5},{7,4},{8,11},{9,10},{10,... | collective-permute-start | bytes 1179656 | tf_op jit(solution)/shard_map/ppermute | solution.py:68
  120.3 36.5 %copy-start.6 = (bf16[3,2,256,128]{3,2,1,0:T(8,128)(2,1)}, bf16[3,2,256,128]{3,2,1,0:T(8,128)(2,1)S(1)}, u32[]{:S(2)}) copy-start(bf16[3,2,256,128]{3,2,1,0:T(8,128)(2,1)S(1)} %collective-permute-done.2.refs_1_) | copy-start | bytes 1179652
  148.4 8.5 %copy-start.7 = (bf16[3,2,256,128]{3,2,1,0:T(8,128)(2,1)}, bf16[3,2,256,128]{3,2,1,0:T(8,128)(2,1)S(1)}, u32[]{:S(2)}) copy-start(bf16[3,2,256,128]{3,2,1,0:T(8,128)(2,1)S(1)} %collective-permute-done.3.refs_2_) | copy-start | bytes 1179652
  156.8 0.7 copy-start.8
  159.7 2.6 collective-permute-start.9
  161.0 5.5 %collective-permute-start.10 = (bf16[4,3,128,128]{3,2,1,0:T(8,128)(2,1)S(1)}, bf16[4,3,128,128]{3,2,1,0:T(8,128)(2,1)S(1)}, u32[]{:S(2)}, u32[]{:S(2)}) collective-permute-start(bf16[4,3,128,128]{3,2,1,0:T(8,128)(2,1)S(1)} %get-tuple-element.53), channel_id=1, source_target_pairs={{8,0},{16,8},{24,16},{9,1},{17,9},{25,17},{10,2},{18,10},{26,18},{... | collective-permute-start | bytes 1179656 | tf_op jit(solution)/shard_map/ppermute | solution.py:25
  202.9 9.8 %collective-permute-start.11 = (bf16[4,3,128,128]{3,2,1,0:T(8,128)(2,1)S(1)}, bf16[4,3,128,128]{3,2,1,0:T(8,128)(2,1)S(1)}, u32[]{:S(2)}, u32[]{:S(2)}) collective-permute-start(bf16[4,3,128,128]{3,2,1,0:T(8,128)(2,1)S(1)} %get-tuple-element.56), channel_id=1, source_target_pairs={{8,0},{16,8},{24,16},{9,1},{17,9},{25,17},{10,2},{18,10},{26,18},{... | collective-permute-start | bytes 1179656 | tf_op jit(solution)/shard_map/ppermute | solution.py:25
  204.2 9.8 %collective-permute-start.12 = (bf16[4,3,128,128]{3,2,1,0:T(8,128)(2,1)S(1)}, bf16[4,3,128,128]{3,2,1,0:T(8,128)(2,1)S(1)}, u32[]{:S(2)}, u32[]{:S(2)}) collective-permute-start(bf16[4,3,128,128]{3,2,1,0:T(8,128)(2,1)S(1)} %get-tuple-element.57), channel_id=1, source_target_pairs={{0,8},{8,16},{16,24},{1,9},{9,17},{17,25},{2,10},{10,18},{18,26},{... | collective-permute-start | bytes 1179656 | tf_op jit(solution)/shard_map/ppermute | solution.py:25
  216.7 1.7 copy-start.1
  218.3 97.1 %all-to-all-start = ((bf16[8,3,2,256,128]{4,3,2,1,0:T(8,128)(2,1)}), bf16[8,3,2,256,128]{4,3,2,1,0:T(8,128)(2,1)S(1)}, u32[]{:S(2)}, u32[]{:S(2)}) async-start(bf16[8,3,2,256,128]{4,3,2,1,0:T(8,128)(2,1)} %finish.2.refs_1_), calls=%async_computation | async-start | bytes 6291456 | tf_op jit(solution)/shard_map/all_to_all | solution.py:63
  224.8 7.8 %collective-permute-start.13 = (bf16[4,3,128,128]{3,2,1,0:T(8,128)(2,1)S(1)}, bf16[4,3,128,128]{3,2,1,0:T(8,128)(2,1)S(1)}, u32[]{:S(2)}, u32[]{:S(2)}) collective-permute-start(bf16[4,3,128,128]{3,2,1,0:T(8,128)(2,1)S(1)} %get-tuple-element.58), channel_id=1, source_target_pairs={{0,8},{8,16},{16,24},{1,9},{9,17},{17,25},{2,10},{10,18},{18,26},{... | collective-permute-start | bytes 1179656 | tf_op jit(solution)/shard_map/ppermute | solution.py:25
  231.2 6.1 %collective-permute-start.14 = (bf16[4,3,128,128]{3,2,1,0:T(8,128)(2,1)S(1)}, bf16[4,3,128,128]{3,2,1,0:T(8,128)(2,1)S(1)}, u32[]{:S(2)}, u32[]{:S(2)}) collective-permute-start(bf16[4,3,128,128]{3,2,1,0:T(8,128)(2,1)S(1)} %get-tuple-element.59), channel_id=1, source_target_pairs={{8,0},{16,8},{24,16},{9,1},{17,9},{25,17},{10,2},{18,10},{26,18},{... | collective-permute-start | bytes 1179656 | tf_op jit(solution)/shard_map/ppermute | solution.py:25
  273.8 10.3 %collective-permute-start.15 = (bf16[4,3,128,128]{3,2,1,0:T(8,128)(2,1)S(1)}, bf16[4,3,128,128]{3,2,1,0:T(8,128)(2,1)S(1)}, u32[]{:S(2)}, u32[]{:S(2)}) collective-permute-start(bf16[4,3,128,128]{3,2,1,0:T(8,128)(2,1)S(1)} %get-tuple-element.62), channel_id=1, source_target_pairs={{8,0},{16,8},{24,16},{9,1},{17,9},{25,17},{10,2},{18,10},{26,18},{... | collective-permute-start | bytes 1179656 | tf_op jit(solution)/shard_map/ppermute | solution.py:25
  275.1 10.1 %collective-permute-start.16 = (bf16[4,3,128,128]{3,2,1,0:T(8,128)(2,1)S(1)}, bf16[4,3,128,128]{3,2,1,0:T(8,128)(2,1)S(1)}, u32[]{:S(2)}, u32[]{:S(2)}) collective-permute-start(bf16[4,3,128,128]{3,2,1,0:T(8,128)(2,1)S(1)} %get-tuple-element.63), channel_id=1, source_target_pairs={{0,8},{8,16},{16,24},{1,9},{9,17},{17,25},{2,10},{10,18},{18,26},{... | collective-permute-start | bytes 1179656 | tf_op jit(solution)/shard_map/ppermute | solution.py:25
  287.9 8.1 %collective-permute-start.17 = (bf16[3,2,256,128]{3,2,1,0:T(8,128)(2,1)}, bf16[3,2,256,128]{3,2,1,0:T(8,128)(2,1)S(1)}, u32[]{:S(2)}, u32[]{:S(2)}) collective-permute-start(bf16[3,2,256,128]{3,2,1,0:T(8,128)(2,1)} %get-tuple-element.65), channel_id=1, source_target_pairs={{0,1},{1,0},{2,3},{3,2},{4,5},{5,4},{6,7},{7,6},{8,9},{9,8},{10,11... | collective-permute-start | bytes 1179656 | tf_op jit(solution)/shard_map/ppermute | solution.py:68
  289.4 25.3 %collective-permute-start.18 = (bf16[3,2,256,128]{3,2,1,0:T(8,128)(2,1)}, bf16[3,2,256,128]{3,2,1,0:T(8,128)(2,1)S(1)}, u32[]{:S(2)}, u32[]{:S(2)}) collective-permute-start(bf16[3,2,256,128]{3,2,1,0:T(8,128)(2,1)} %get-tuple-element.66), channel_id=1, source_target_pairs={{0,2},{1,3},{2,0},{3,1},{4,6},{5,7},{6,4},{7,5},{8,10},{9,11},{10,... | collective-permute-start | bytes 1179656 | tf_op jit(solution)/shard_map/ppermute | solution.py:68
  289.9 33.3 %collective-permute-start.19 = (bf16[3,2,256,128]{3,2,1,0:T(8,128)(2,1)}, bf16[3,2,256,128]{3,2,1,0:T(8,128)(2,1)}, u32[]{:S(2)}, u32[]{:S(2)}) collective-permute-start(bf16[3,2,256,128]{3,2,1,0:T(8,128)(2,1)} %get-tuple-element.67), channel_id=1, source_target_pairs={{0,3},{1,2},{2,1},{3,0},{4,7},{5,6},{6,5},{7,4},{8,11},{9,10},{10,... | collective-permute-start | bytes 1179656 | tf_op jit(solution)/shard_map/ppermute | solution.py:68
  291.4 31.8 %collective-permute-start.20 = (bf16[3,2,256,128]{3,2,1,0:T(8,128)(2,1)}, bf16[3,2,256,128]{3,2,1,0:T(8,128)(2,1)}, u32[]{:S(2)}, u32[]{:S(2)}) collective-permute-start(bf16[3,2,256,128]{3,2,1,0:T(8,128)(2,1)} %get-tuple-element.68), channel_id=1, source_target_pairs={{0,4},{1,5},{2,6},{3,7},{4,0},{5,1},{6,2},{7,3},{8,12},{9,13},{10,... | collective-permute-start | bytes 1179656 | tf_op jit(solution)/shard_map/ppermute | solution.py:68
  293.8 30.3 %collective-permute-start.21 = (bf16[3,2,256,128]{3,2,1,0:T(8,128)(2,1)}, bf16[3,2,256,128]{3,2,1,0:T(8,128)(2,1)}, u32[]{:S(2)}, u32[]{:S(2)}) collective-permute-start(bf16[3,2,256,128]{3,2,1,0:T(8,128)(2,1)} %get-tuple-element.69), channel_id=1, source_target_pairs={{0,5},{1,4},{2,7},{3,6},{4,1},{5,0},{6,3},{7,2},{8,13},{9,12},{10,... | collective-permute-start | bytes 1179656 | tf_op jit(solution)/shard_map/ppermute | solution.py:68
  295.9 64.4 %copy-start.9 = (bf16[3,2,256,128]{3,2,1,0:T(8,128)(2,1)}, bf16[3,2,256,128]{3,2,1,0:T(8,128)(2,1)S(1)}, u32[]{:S(2)}) copy-start(bf16[3,2,256,128]{3,2,1,0:T(8,128)(2,1)S(1)} %collective-permute-done.17.refs_2_) | copy-start | bytes 1179652
  295.9 55.0 %collective-permute-start.22 = (bf16[3,2,256,128]{3,2,1,0:T(8,128)(2,1)}, bf16[3,2,256,128]{3,2,1,0:T(8,128)(2,1)}, u32[]{:S(2)}, u32[]{:S(2)}) collective-permute-start(bf16[3,2,256,128]{3,2,1,0:T(8,128)(2,1)} %get-tuple-element.70), channel_id=1, source_target_pairs={{0,6},{1,7},{2,4},{3,5},{4,2},{5,3},{6,0},{7,1},{8,14},{9,15},{10,... | collective-permute-start | bytes 1179656 | tf_op jit(solution)/shard_map/ppermute | solution.py:68
  314.7 0.8 copy-start.10
  315.4 44.9 %collective-permute-start.23 = (bf16[3,2,256,128]{3,2,1,0:T(8,128)(2,1)}, bf16[3,2,256,128]{3,2,1,0:T(8,128)(2,1)}, u32[]{:S(2)}, u32[]{:S(2)}) collective-permute-start(bf16[3,2,256,128]{3,2,1,0:T(8,128)(2,1)} %get-tuple-element.71), channel_id=1, source_target_pairs={{0,7},{1,6},{2,5},{3,4},{4,3},{5,2},{6,1},{7,0},{8,15},{9,14},{10,... | collective-permute-start | bytes 1179656 | tf_op jit(solution)/shard_map/ppermute | solution.py:68
  315.4 1.6 copy-start

commit v6 on v5

--- a/solution.py
+++ b/solution.py
@@ -589,7 +589,7 @@
             me, arrays, start, size, heads_here, peers, head_dim, chunk == 0, after
         )
         if chunk == 1:
-            packed = hold(packed, came[0][peers // 2 :])
+            packed = hold(packed, came[0][1:])
         came.append(exchange(packed))
     received = []
     outs = finished = ()

time: 370 us -> 312 us (0.84); the launches traced: 365 us -> 312 us
  waiting for transfers between devices: 195 us -> 147 us
    ppermute x14, waiting for transfers between devices: 183 us -> 129 us  [exchange(): received[k] = lax.ppermute(messages[k], 'seq', pairs)]
    all_to_all x2, waiting for transfers between devices: 0.01 us -> 10.8 us  [exchange(): lax.all_to_all(messages[0], 'seq', split_axis=0, concat_axis=0, tiled=True)]
    ppermute x10, waiting for transfers between devices: 12.2 us -> 7.03 us  [from_behind(): return lax.ppermute(x, axis, pairs)]
    ppermute x10, starting transfers between devices: 33.7 us -> 29.3 us  [from_behind(): return lax.ppermute(x, axis, pairs)]
  transfers between devices with their start and end apart: 26 -> 26, of which waited for: 18 -> 16; matrix products, arithmetic and copies ran while one was open for 0% -> 1% of each run, Pallas kernels for 26% -> 29%
where the time goes in v6:
time: 312 us
  waiting for transfers between devices  147 us (47%)
  Pallas kernels  97.5 us (31%)
  starting transfers between devices  59.3 us (19%)
  local copies, waits for them, and re-layouts  3.47 us (1%)
    ppermute x14, waiting for transfers between devices, exchange(): received[k] = lax.ppermute(messages[k], 'seq', pairs)  129 us
    pallas_call x2, Pallas kernels, attend(): pl.pallas_call(functools.partial(attend_kernel, block_rows=block_rows, he...  72.8 us
    ppermute x10, starting transfers between devices, from_behind(): return lax.ppermute(x, axis, pairs)  29.3 us
    ppermute x14, starting transfers between devices, exchange(): received[k] = lax.ppermute(messages[k], 'seq', pairs)  17.4 us
    all_to_all x2, starting transfers between devices, exchange(): lax.all_to_all(messages[0], 'seq', split_axis=0, concat_axis=0, tiled=True)  12.6 us
    all_to_all x2, waiting for transfers between devices, exchange(): lax.all_to_all(messages[0], 'seq', split_axis=0, concat_axis=0, tiled=True)  10.8 us
    pallas_call x2, Pallas kernels, pack(): pl.pallas_call(functools.partial(pack_kernel, first=start * head_dim, hea...  7.78 us
    pallas_call x2, Pallas kernels, unpack(): pl.pallas_call(functools.partial(unpack_kernel, chunk=chunk, peers=peers,...  7.44 us
  transfers between devices with their start and end apart: 26, of which 16 were waited for; matrix products, arithmetic and copies ran while one was open for 1% of the time, Pallas kernels for 29%

profile of v6, /device:TPU:8, one launch (start us, length us, event | category | flops | bytes accessed | tf_op | source)
XLA Modules:
  0.0 311.5 jit_solution(2545073464134624491)
XLA Ops:
  0.6 3.9 %pack.2 = (bf16[3,2,256,128]{3,2,1,0:T(8,128)(2,1)}, bf16[3,2,256,128]{3,2,1,0:T(8,128)(2,1)}, bf16[3,2,256,128]{3,2,1,0:T(8,128)(2,1)}, bf16[3,2,256,128]{3,2,1...) custom-call(s32[1]{0:T(128)} %bitcast.me, ...), custom_call_target="tpu_custom_call" | custom-call | tf_op jit(solution)/shard_map/pack/pallas_call | solution.py:135
  4.6 1.6 collective-permute-start.2
  7.0 1.3 top_k.17
  8.3 1.3 collective-permute-start
  9.6 1.3 top_k.24
  10.9 3.0 collective-permute-start.1
  13.9 1.6 collective-permute-start.4
  15.5 2.6 collective-permute-start.5
  19.4 1.6 collective-permute-start.7
  21.7 3.9 %pack.3.refs_0_ = bf16[8,3,2,256,128]{4,3,2,1,0:T(8,128)(2,1)} custom-call(s32[1]{0:T(128)} %bitcast.me, bf16[256,3072]{1,0:T(8,128)(2,1)} %query.3, bf16[256,3072]{1,0:T(8,128)(2,1)} %key.3, bf16[256,3072]{1,0:T(8,128)(2,1)} %value.3, bf16[256,3072]{1,0:T(8,128)(2,1)} %d_out.3, s32[8]{0:T(128)S(1)} %pad_add_fusion.asked.refs_0_, ...), custom_call_target="tpu_custom_call" | custom-call | tf_op jit(solution)/shard_map/pack/pallas_call | solution.py:135
  25.7 9.0 %collective-permute-done.4.refs_3_ = bf16[3,2,256,128]{3,2,1,0:T(8,128)(2,1)S(1)} collective-permute-done((bf16[3,2,256,128]{3,2,1,0:T(8,128)(2,1)}, bf16[3,2,256,128]{3,2,1,0:T(8,128)(2,1)S(1)}, u32[]{:S(2)}, u32[]{:S(2)}) %collective-permute-start.4) | collective-permute-done | bytes 393248 | tf_op jit(solution)/shard_map/ppermute | solution.py:68
  34.7 27.0 %collective-permute-done.5.refs_4_ = bf16[3,2,256,128]{3,2,1,0:T(8,128)(2,1)S(1)} collective-permute-done((bf16[3,2,256,128]{3,2,1,0:T(8,128)(2,1)}, bf16[3,2,256,128]{3,2,1,0:T(8,128)(2,1)S(1)}, u32[]{:S(2)}, u32[]{:S(2)}) %collective-permute-start.5) | collective-permute-done | bytes 393248 | tf_op jit(solution)/shard_map/ppermute | solution.py:68
  61.7 8.4 %collective-permute-done.6.refs_5_ = bf16[3,2,256,128]{3,2,1,0:T(8,128)(2,1)S(1)} collective-permute-done((bf16[3,2,256,128]{3,2,1,0:T(8,128)(2,1)}, bf16[3,2,256,128]{3,2,1,0:T(8,128)(2,1)S(1)}, u32[]{:S(2)}, u32[]{:S(2)}) %collective-permute-start.6) | collective-permute-done | bytes 393248 | tf_op jit(solution)/shard_map/ppermute | solution.py:68
  70.1 8.4 %collective-permute-done.7.refs_6_ = bf16[3,2,256,128]{3,2,1,0:T(8,128)(2,1)S(1)} collective-permute-done((bf16[3,2,256,128]{3,2,1,0:T(8,128)(2,1)}, bf16[3,2,256,128]{3,2,1,0:T(8,128)(2,1)S(1)}, u32[]{:S(2)}, u32[]{:S(2)}) %collective-permute-start.7) | collective-permute-done | bytes 393248 | tf_op jit(solution)/shard_map/ppermute | solution.py:68
  78.5 8.9 %collective-permute-done.8.refs_7_ = bf16[3,2,256,128]{3,2,1,0:T(8,128)(2,1)S(1)} collective-permute-done((bf16[3,2,256,128]{3,2,1,0:T(8,128)(2,1)}, bf16[3,2,256,128]{3,2,1,0:T(8,128)(2,1)S(1)}, u32[]{:S(2)}, u32[]{:S(2)}) %collective-permute-start.8) | collective-permute-done | bytes 393248 | tf_op jit(solution)/shard_map/ppermute | solution.py:68
  88.2 5.4 %all-to-all-start.1 = ((bf16[8,3,2,256,128]{4,3,2,1,0:T(8,128)(2,1)}), bf16[8,3,2,256,128]{4,3,2,1,0:T(8,128)(2,1)}, u32[]{:S(2)}, u32[]{:S(2)}) async-start(bf16[8,3,2,256,128]{4,3,2,1,0:T(8,128)(2,1)} %hold.1), calls=%async_computation.1 | async-start | bytes 6291456 | tf_op jit(solution)/shard_map/all_to_all | solution.py:63
  93.7 2.1 pick.2
  95.8 1.4 collective-permute-start.9
  97.2 1.3 collective-permute-start.10
  98.5 2.3 collective-permute-done.10.came_next
  100.8 36.4 %attend.2 = (bf16[8,3,256,128]{3,2,1,0:T(8,128)(2,1)S(1)}, f32[3,16,128,128]{3,2,1,0:T(8,128)S(1)}, bf16[4,3,128,128]{3,2,1,0:T(8,128)(2,1)S(1)}, bf16[4,3,128,128]{3,2,1,0:T(8,128)(2,1)S(1)}) custom-call(s32[1]{0:T(128)} %bitcast.me, s32[3,16,8]{2,1,0:T(8,128)S(1)} %get-tuple-element.81.lists, ...), custom_call_target="tpu_custom_call" | custom-call | tf_op jit(solution)/shard_map/attend/pallas_call | solution.py:459
  137.2 1.3 collective-permute-start.11
  138.5 8.8 %collective-permute-start.12 = (bf16[4,3,128,128]{3,2,1,0:T(8,128)(2,1)S(1)}, bf16[4,3,128,128]{3,2,1,0:T(8,128)(2,1)S(1)}, u32[]{:S(2)}, u32[]{:S(2)}) collective-permute-start(bf16[4,3,128,128]{3,2,1,0:T(8,128)(2,1)S(1)} %get-tuple-element.57), channel_id=1, source_target_pairs={{0,8},{8,16},{16,24},{1,9},{9,17},{17,25},{2,10},{10,18},{18,26},{... | collective-permute-start | bytes 1179656 | tf_op jit(solution)/shard_map/ppermute | solution.py:25
  147.4 1.3 collective-permute-done.12.earlier
  148.7 2.6 finish.2.refs_1_
  151.3 10.8 %all-to-all-done.1.refs_0_ = bf16[8,3,2,256,128]{4,3,2,1,0:T(8,128)(2,1)} async-done(((bf16[8,3,2,256,128]{4,3,2,1,0:T(8,128)(2,1)}), bf16[8,3,2,256,128]{4,3,2,1,0:T(8,128)(2,1)}, u32[]{:S(2)}, u32[]{:S(2)}) %all-to-all-start.1) | async-done | bytes 3145760 | tf_op jit(solution)/shard_map/all_to_all | solution.py:63
  162.1 7.2 %all-to-all-start = ((bf16[8,3,2,256,128]{4,3,2,1,0:T(8,128)(2,1)}), bf16[8,3,2,256,128]{4,3,2,1,0:T(8,128)(2,1)S(1)}, u32[]{:S(2)}, u32[]{:S(2)}) async-start(bf16[8,3,2,256,128]{4,3,2,1,0:T(8,128)(2,1)} %finish.2.refs_1_), calls=%async_computation | async-start | bytes 6291456 | tf_op jit(solution)/shard_map/all_to_all | solution.py:63
  169.3 2.1 pick.3
  171.4 1.3 collective-permute-start.13
  172.7 1.3 collective-permute-start.14
  174.0 2.3 collective-permute-done.14.came_next
  176.3 36.4 %attend.3 = (bf16[8,3,256,128]{3,2,1,0:T(8,128)(2,1)S(1)}, f32[3,16,128,128]{3,2,1,0:T(8,128)S(1)}, bf16[4,3,128,128]{3,2,1,0:T(8,128)(2,1)S(1)}, bf16[4,3,128,128]{3,2,1,0:T(8,128)(2,1)S(1)}) custom-call(s32[1]{0:T(128)} %bitcast.me, s32[3,16,8]{2,1,0:T(8,128)S(1)} %get-tuple-element.80.lists, ...), custom_call_target="tpu_custom_call" | custom-call | tf_op jit(solution)/shard_map/attend/pallas_call | solution.py:459
  212.8 1.3 collective-permute-start.15
  214.1 8.3 %collective-permute-start.16 = (bf16[4,3,128,128]{3,2,1,0:T(8,128)(2,1)S(1)}, bf16[4,3,128,128]{3,2,1,0:T(8,128)(2,1)S(1)}, u32[]{:S(2)}, u32[]{:S(2)}) collective-permute-start(bf16[4,3,128,128]{3,2,1,0:T(8,128)(2,1)S(1)} %get-tuple-element.63), channel_id=1, source_target_pairs={{0,8},{8,16},{16,24},{1,9},{9,17},{17,25},{2,10},{10,18},{18,26},{... | collective-permute-start | bytes 1179656 | tf_op jit(solution)/shard_map/ppermute | solution.py:25
  223.5 2.6 finish.3
  226.1 1.5 collective-permute-start.17
  228.2 1.5 collective-permute-start.19
  229.7 2.1 collective-permute-start.20
  231.8 1.7 collective-permute-start.21
  233.5 3.0 collective-permute-done.17.refs_2_
  236.6 20.1 %collective-permute-done.18.refs_3_ = bf16[3,2,256,128]{3,2,1,0:T(8,128)(2,1)S(1)} collective-permute-done((bf16[3,2,256,128]{3,2,1,0:T(8,128)(2,1)}, bf16[3,2,256,128]{3,2,1,0:T(8,128)(2,1)S(1)}, u32[]{:S(2)}, u32[]{:S(2)}) %collective-permute-start.18) | collective-permute-done | bytes 393248 | tf_op jit(solution)/shard_map/ppermute | solution.py:68
  258.0 1.6 copy-done
  259.6 3.0 unpack.2
  262.7 5.7 %collective-permute-done.19.refs_4_ = bf16[3,2,256,128]{3,2,1,0:T(8,128)(2,1)} collective-permute-done((bf16[3,2,256,128]{3,2,1,0:T(8,128)(2,1)}, bf16[3,2,256,128]{3,2,1,0:T(8,128)(2,1)}, u32[]{:S(2)}, u32[]{:S(2)}) %collective-permute-start.19) | collective-permute-done | bytes 393248 | tf_op jit(solution)/shard_map/ppermute | solution.py:68
  268.4 19.8 %collective-permute-done.21.refs_6_ = bf16[3,2,256,128]{3,2,1,0:T(8,128)(2,1)} collective-permute-done((bf16[3,2,256,128]{3,2,1,0:T(8,128)(2,1)}, bf16[3,2,256,128]{3,2,1,0:T(8,128)(2,1)}, u32[]{:S(2)}, u32[]{:S(2)}) %collective-permute-start.21) | collective-permute-done | bytes 393248 | tf_op jit(solution)/shard_map/ppermute | solution.py:68
  288.2 10.9 %collective-permute-done.22.refs_7_ = bf16[3,2,256,128]{3,2,1,0:T(8,128)(2,1)} collective-permute-done((bf16[3,2,256,128]{3,2,1,0:T(8,128)(2,1)}, bf16[3,2,256,128]{3,2,1,0:T(8,128)(2,1)}, u32[]{:S(2)}, u32[]{:S(2)}) %collective-permute-start.22) | collective-permute-done | bytes 393248 | tf_op jit(solution)/shard_map/ppermute | solution.py:68
  299.1 7.8 %collective-permute-done.23.refs_8_ = bf16[3,2,256,128]{3,2,1,0:T(8,128)(2,1)} collective-permute-done((bf16[3,2,256,128]{3,2,1,0:T(8,128)(2,1)}, bf16[3,2,256,128]{3,2,1,0:T(8,128)(2,1)}, u32[]{:S(2)}, u32[]{:S(2)}) %collective-permute-start.23) | collective-permute-done | bytes 393248 | tf_op jit(solution)/shard_map/ppermute | solution.py:68
  306.9 4.4 %unpack.3 = (bf16[256,3072]{1,0:T(8,128)(2,1)}, bf16[256,3072]{1,0:T(8,128)(2,1)}, bf16[256,3072]{1,0:T(8,128)(2,1)}, bf16[256,3072]{1,0:T(8,128)(2,1)}) custom-call(s32[1]{0:T(128)} %bitcast.me, bf16[8,3,2,256,128]{4,3,2,1,0:T(8,128)(2,1)} %copy-done, ...), custom_call_target="tpu_custom_call", output_to_operand_aliasing={{0}: (10, {}), {1}: (11, {}), {2}: (12, {}), {3}: (13, {})} | custom-call | tf_op jit(solution)/shard_map/unpack/pallas_call | solution.py:241
  (55 shorter events, 6.6 us)
Async XLA Ops:
  0.6 5.9 %copy-start.10 = (s32[6,16,8]{1,2,0:T(8,128)S(1)}, s32[6,16,8]{1,2,0:T(8,128)}, u32[]{:S(2)}) copy-start(s32[6,16,8]{1,2,0:T(8,128)} %param.9) | copy-start | bytes 9220
  4.6 14.8 %collective-permute-start.2 = (bf16[3,2,256,128]{3,2,1,0:T(8,128)(2,1)}, bf16[3,2,256,128]{3,2,1,0:T(8,128)(2,1)S(1)}, u32[]{:S(2)}, u32[]{:S(2)}) collective-permute-start(bf16[3,2,256,128]{3,2,1,0:T(8,128)(2,1)} %get-tuple-element.45), channel_id=1, source_target_pairs={{0,1},{1,0},{2,3},{3,2},{4,5},{5,4},{6,7},{7,6},{8,9},{9,8},{10,11... | collective-permute-start | bytes 1179656 | tf_op jit(solution)/shard_map/ppermute | solution.py:68
  6.1 14.9 %collective-permute-start.3 = (bf16[3,2,256,128]{3,2,1,0:T(8,128)(2,1)}, bf16[3,2,256,128]{3,2,1,0:T(8,128)(2,1)S(1)}, u32[]{:S(2)}, u32[]{:S(2)}) collective-permute-start(bf16[3,2,256,128]{3,2,1,0:T(8,128)(2,1)} %get-tuple-element.46), channel_id=1, source_target_pairs={{0,2},{1,3},{2,0},{3,1},{4,6},{5,7},{6,4},{7,5},{8,10},{9,11},{10,... | collective-permute-start | bytes 1179656 | tf_op jit(solution)/shard_map/ppermute | solution.py:68
  8.3 7.3 %collective-permute-start = (s32[4]{0:T(128)S(1)}, s32[4]{0:T(128)S(1)}, u32[]{:S(2)}, u32[]{:S(2)}) collective-permute-start(s32[4]{0:T(128)S(1)} %get-tuple-element.83), channel_id=1, source_target_pairs={{8,0},{16,8},{24,16},{9,1},{17,9},{25,17},{10,2},{18,10},{26,18},{... | collective-permute-start | bytes 56 | tf_op jit(solution)/shard_map/ppermute | solution.py:25
  10.9 7.2 %collective-permute-start.1 = (s32[4]{0:T(128)S(1)}, s32[4]{0:T(128)S(1)}, u32[]{:S(2)}, u32[]{:S(2)}) collective-permute-start(s32[4]{0:T(128)S(1)} %get-tuple-element.85), channel_id=1, source_target_pairs={{0,8},{8,16},{16,24},{1,9},{9,17},{17,25},{2,10},{10,18},{18,26},{... | collective-permute-start | bytes 56 | tf_op jit(solution)/shard_map/ppermute | solution.py:25
  13.9 20.8 %collective-permute-start.4 = (bf16[3,2,256,128]{3,2,1,0:T(8,128)(2,1)}, bf16[3,2,256,128]{3,2,1,0:T(8,128)(2,1)S(1)}, u32[]{:S(2)}, u32[]{:S(2)}) collective-permute-start(bf16[3,2,256,128]{3,2,1,0:T(8,128)(2,1)} %get-tuple-element.47), channel_id=1, source_target_pairs={{0,3},{1,2},{2,1},{3,0},{4,7},{5,6},{6,5},{7,4},{8,11},{9,10},{10,... | collective-permute-start | bytes 1179656 | tf_op jit(solution)/shard_map/ppermute | solution.py:68
  15.5 46.2 %collective-permute-start.5 = (bf16[3,2,256,128]{3,2,1,0:T(8,128)(2,1)}, bf16[3,2,256,128]{3,2,1,0:T(8,128)(2,1)S(1)}, u32[]{:S(2)}, u32[]{:S(2)}) collective-permute-start(bf16[3,2,256,128]{3,2,1,0:T(8,128)(2,1)} %get-tuple-element.48), channel_id=1, source_target_pairs={{0,4},{1,5},{2,6},{3,7},{4,0},{5,1},{6,2},{7,3},{8,12},{9,13},{10,... | collective-permute-start | bytes 1179656 | tf_op jit(solution)/shard_map/ppermute | solution.py:68
  18.1 52.0 %collective-permute-start.6 = (bf16[3,2,256,128]{3,2,1,0:T(8,128)(2,1)}, bf16[3,2,256,128]{3,2,1,0:T(8,128)(2,1)S(1)}, u32[]{:S(2)}, u32[]{:S(2)}) collective-permute-start(bf16[3,2,256,128]{3,2,1,0:T(8,128)(2,1)} %get-tuple-element.49), channel_id=1, source_target_pairs={{0,5},{1,4},{2,7},{3,6},{4,1},{5,0},{6,3},{7,2},{8,13},{9,12},{10,... | collective-permute-start | bytes 1179656 | tf_op jit(solution)/shard_map/ppermute | solution.py:68
  19.4 6.2 %copy-start.1 = (bf16[3,2,256,128]{3,2,1,0:T(8,128)(2,1)}, bf16[3,2,256,128]{3,2,1,0:T(8,128)(2,1)S(1)}, u32[]{:S(2)}) copy-start(bf16[3,2,256,128]{3,2,1,0:T(8,128)(2,1)S(1)} %collective-permute-done.2.refs_1_) | copy-start | bytes 1179652
  19.4 59.2 %collective-permute-start.7 = (bf16[3,2,256,128]{3,2,1,0:T(8,128)(2,1)}, bf16[3,2,256,128]{3,2,1,0:T(8,128)(2,1)S(1)}, u32[]{:S(2)}, u32[]{:S(2)}) collective-permute-start(bf16[3,2,256,128]{3,2,1,0:T(8,128)(2,1)} %get-tuple-element.50), channel_id=1, source_target_pairs={{0,6},{1,7},{2,4},{3,5},{4,2},{5,3},{6,0},{7,1},{8,14},{9,15},{10,... | collective-permute-start | bytes 1179656 | tf_op jit(solution)/shard_map/ppermute | solution.py:68
  21.0 4.7 %copy-start.2 = (bf16[3,2,256,128]{3,2,1,0:T(8,128)(2,1)}, bf16[3,2,256,128]{3,2,1,0:T(8,128)(2,1)S(1)}, u32[]{:S(2)}) copy-start(bf16[3,2,256,128]{3,2,1,0:T(8,128)(2,1)S(1)} %collective-permute-done.3.refs_2_) | copy-start | bytes 1179652
  21.0 66.5 %collective-permute-start.8 = (bf16[3,2,256,128]{3,2,1,0:T(8,128)(2,1)}, bf16[3,2,256,128]{3,2,1,0:T(8,128)(2,1)S(1)}, u32[]{:S(2)}, u32[]{:S(2)}) collective-permute-start(bf16[3,2,256,128]{3,2,1,0:T(8,128)(2,1)} %get-tuple-element.51), channel_id=1, source_target_pairs={{0,7},{1,6},{2,5},{3,4},{4,3},{5,2},{6,1},{7,0},{8,15},{9,14},{10,... | collective-permute-start | bytes 1179656 | tf_op jit(solution)/shard_map/ppermute | solution.py:68
  34.7 52.8 %copy-start.3 = (bf16[3,2,256,128]{3,2,1,0:T(8,128)(2,1)}, bf16[3,2,256,128]{3,2,1,0:T(8,128)(2,1)S(1)}, u32[]{:S(2)}) copy-start(bf16[3,2,256,128]{3,2,1,0:T(8,128)(2,1)S(1)} %collective-permute-done.4.refs_3_) | copy-start | bytes 1179652
  61.7 25.8 %copy-start.4 = (bf16[3,2,256,128]{3,2,1,0:T(8,128)(2,1)}, bf16[3,2,256,128]{3,2,1,0:T(8,128)(2,1)S(1)}, u32[]{:S(2)}) copy-start(bf16[3,2,256,128]{3,2,1,0:T(8,128)(2,1)S(1)} %collective-permute-done.5.refs_4_) | copy-start | bytes 1179652
  70.1 17.4 %copy-start.5 = (bf16[3,2,256,128]{3,2,1,0:T(8,128)(2,1)}, bf16[3,2,256,128]{3,2,1,0:T(8,128)(2,1)S(1)}, u32[]{:S(2)}) copy-start(bf16[3,2,256,128]{3,2,1,0:T(8,128)(2,1)S(1)} %collective-permute-done.6.refs_5_) | copy-start | bytes 1179652
  78.5 8.9 %copy-start.6 = (bf16[3,2,256,128]{3,2,1,0:T(8,128)(2,1)}, bf16[3,2,256,128]{3,2,1,0:T(8,128)(2,1)S(1)}, u32[]{:S(2)}) copy-start(bf16[3,2,256,128]{3,2,1,0:T(8,128)(2,1)S(1)} %collective-permute-done.7.refs_6_) | copy-start | bytes 1179652
  87.5 0.8 copy-start.7
  88.2 73.9 %all-to-all-start.1 = ((bf16[8,3,2,256,128]{4,3,2,1,0:T(8,128)(2,1)}), bf16[8,3,2,256,128]{4,3,2,1,0:T(8,128)(2,1)}, u32[]{:S(2)}, u32[]{:S(2)}) async-start(bf16[8,3,2,256,128]{4,3,2,1,0:T(8,128)(2,1)} %hold.1), calls=%async_computation.1 | async-start | bytes 6291456 | tf_op jit(solution)/shard_map/all_to_all | solution.py:63
  95.8 2.7 collective-permute-start.9
  97.2 3.6 %collective-permute-start.10 = (bf16[4,3,128,128]{3,2,1,0:T(8,128)(2,1)S(1)}, bf16[4,3,128,128]{3,2,1,0:T(8,128)(2,1)S(1)}, u32[]{:S(2)}, u32[]{:S(2)}) collective-permute-start(bf16[4,3,128,128]{3,2,1,0:T(8,128)(2,1)S(1)} %get-tuple-element.53), channel_id=1, source_target_pairs={{8,0},{16,8},{24,16},{9,1},{17,9},{25,17},{10,2},{18,10},{26,18},{... | collective-permute-start | bytes 1179656 | tf_op jit(solution)/shard_map/ppermute | solution.py:25
  137.2 10.2 %collective-permute-start.11 = (bf16[4,3,128,128]{3,2,1,0:T(8,128)(2,1)S(1)}, bf16[4,3,128,128]{3,2,1,0:T(8,128)(2,1)S(1)}, u32[]{:S(2)}, u32[]{:S(2)}) collective-permute-start(bf16[4,3,128,128]{3,2,1,0:T(8,128)(2,1)S(1)} %get-tuple-element.56), channel_id=1, source_target_pairs={{8,0},{16,8},{24,16},{9,1},{17,9},{25,17},{10,2},{18,10},{26,18},{... | collective-permute-start | bytes 1179656 | tf_op jit(solution)/shard_map/ppermute | solution.py:25
  138.5 10.2 %collective-permute-start.12 = (bf16[4,3,128,128]{3,2,1,0:T(8,128)(2,1)S(1)}, bf16[4,3,128,128]{3,2,1,0:T(8,128)(2,1)S(1)}, u32[]{:S(2)}, u32[]{:S(2)}) collective-permute-start(bf16[4,3,128,128]{3,2,1,0:T(8,128)(2,1)S(1)} %get-tuple-element.57), channel_id=1, source_target_pairs={{0,8},{8,16},{16,24},{1,9},{9,17},{17,25},{2,10},{10,18},{18,26},{... | collective-permute-start | bytes 1179656 | tf_op jit(solution)/shard_map/ppermute | solution.py:25
  162.1 95.9 %all-to-all-start = ((bf16[8,3,2,256,128]{4,3,2,1,0:T(8,128)(2,1)}), bf16[8,3,2,256,128]{4,3,2,1,0:T(8,128)(2,1)S(1)}, u32[]{:S(2)}, u32[]{:S(2)}) async-start(bf16[8,3,2,256,128]{4,3,2,1,0:T(8,128)(2,1)} %finish.2.refs_1_), calls=%async_computation | async-start | bytes 6291456 | tf_op jit(solution)/shard_map/all_to_all | solution.py:63
  171.4 2.6 collective-permute-start.13
  172.7 3.6 %collective-permute-start.14 = (bf16[4,3,128,128]{3,2,1,0:T(8,128)(2,1)S(1)}, bf16[4,3,128,128]{3,2,1,0:T(8,128)(2,1)S(1)}, u32[]{:S(2)}, u32[]{:S(2)}) collective-permute-start(bf16[4,3,128,128]{3,2,1,0:T(8,128)(2,1)S(1)} %get-tuple-element.59), channel_id=1, source_target_pairs={{8,0},{16,8},{24,16},{9,1},{17,9},{25,17},{10,2},{18,10},{26,18},{... | collective-permute-start | bytes 1179656 | tf_op jit(solution)/shard_map/ppermute | solution.py:25
  212.8 9.6 %collective-permute-start.15 = (bf16[4,3,128,128]{3,2,1,0:T(8,128)(2,1)S(1)}, bf16[4,3,128,128]{3,2,1,0:T(8,128)(2,1)S(1)}, u32[]{:S(2)}, u32[]{:S(2)}) collective-permute-start(bf16[4,3,128,128]{3,2,1,0:T(8,128)(2,1)S(1)} %get-tuple-element.62), channel_id=1, source_target_pairs={{8,0},{16,8},{24,16},{9,1},{17,9},{25,17},{10,2},{18,10},{26,18},{... | collective-permute-start | bytes 1179656 | tf_op jit(solution)/shard_map/ppermute | solution.py:25
  214.1 9.5 %collective-permute-start.16 = (bf16[4,3,128,128]{3,2,1,0:T(8,128)(2,1)S(1)}, bf16[4,3,128,128]{3,2,1,0:T(8,128)(2,1)S(1)}, u32[]{:S(2)}, u32[]{:S(2)}) collective-permute-start(bf16[4,3,128,128]{3,2,1,0:T(8,128)(2,1)S(1)} %get-tuple-element.63), channel_id=1, source_target_pairs={{0,8},{8,16},{16,24},{1,9},{9,17},{17,25},{2,10},{10,18},{18,26},{... | collective-permute-start | bytes 1179656 | tf_op jit(solution)/shard_map/ppermute | solution.py:25
  226.1 10.4 %collective-permute-start.17 = (bf16[3,2,256,128]{3,2,1,0:T(8,128)(2,1)}, bf16[3,2,256,128]{3,2,1,0:T(8,128)(2,1)S(1)}, u32[]{:S(2)}, u32[]{:S(2)}) collective-permute-start(bf16[3,2,256,128]{3,2,1,0:T(8,128)(2,1)} %get-tuple-element.65), channel_id=1, source_target_pairs={{0,1},{1,0},{2,3},{3,2},{4,5},{5,4},{6,7},{7,6},{8,9},{9,8},{10,11... | collective-permute-start | bytes 1179656 | tf_op jit(solution)/shard_map/ppermute | solution.py:68
  227.7 29.0 %collective-permute-start.18 = (bf16[3,2,256,128]{3,2,1,0:T(8,128)(2,1)}, bf16[3,2,256,128]{3,2,1,0:T(8,128)(2,1)S(1)}, u32[]{:S(2)}, u32[]{:S(2)}) collective-permute-start(bf16[3,2,256,128]{3,2,1,0:T(8,128)(2,1)} %get-tuple-element.66), channel_id=1, source_target_pairs={{0,2},{1,3},{2,0},{3,1},{4,6},{5,7},{6,4},{7,5},{8,10},{9,11},{10,... | collective-permute-start | bytes 1179656 | tf_op jit(solution)/shard_map/ppermute | solution.py:68
  228.2 40.2 %collective-permute-start.19 = (bf16[3,2,256,128]{3,2,1,0:T(8,128)(2,1)}, bf16[3,2,256,128]{3,2,1,0:T(8,128)(2,1)}, u32[]{:S(2)}, u32[]{:S(2)}) collective-permute-start(bf16[3,2,256,128]{3,2,1,0:T(8,128)(2,1)} %get-tuple-element.67), channel_id=1, source_target_pairs={{0,3},{1,2},{2,1},{3,0},{4,7},{5,6},{6,5},{7,4},{8,11},{9,10},{10,... | collective-permute-start | bytes 1179656 | tf_op jit(solution)/shard_map/ppermute | solution.py:68
  229.7 38.7 %collective-permute-start.20 = (bf16[3,2,256,128]{3,2,1,0:T(8,128)(2,1)}, bf16[3,2,256,128]{3,2,1,0:T(8,128)(2,1)}, u32[]{:S(2)}, u32[]{:S(2)}) collective-permute-start(bf16[3,2,256,128]{3,2,1,0:T(8,128)(2,1)} %get-tuple-element.68), channel_id=1, source_target_pairs={{0,4},{1,5},{2,6},{3,7},{4,0},{5,1},{6,2},{7,3},{8,12},{9,13},{10,... | collective-permute-start | bytes 1179656 | tf_op jit(solution)/shard_map/ppermute | solution.py:68
  231.8 56.4 %collective-permute-start.21 = (bf16[3,2,256,128]{3,2,1,0:T(8,128)(2,1)}, bf16[3,2,256,128]{3,2,1,0:T(8,128)(2,1)}, u32[]{:S(2)}, u32[]{:S(2)}) collective-permute-start(bf16[3,2,256,128]{3,2,1,0:T(8,128)(2,1)} %get-tuple-element.69), channel_id=1, source_target_pairs={{0,5},{1,4},{2,7},{3,6},{4,1},{5,0},{6,3},{7,2},{8,13},{9,12},{10,... | collective-permute-start | bytes 1179656 | tf_op jit(solution)/shard_map/ppermute | solution.py:68
  236.5 70.4 %copy-start.8 = (bf16[3,2,256,128]{3,2,1,0:T(8,128)(2,1)}, bf16[3,2,256,128]{3,2,1,0:T(8,128)(2,1)S(1)}, u32[]{:S(2)}) copy-start(bf16[3,2,256,128]{3,2,1,0:T(8,128)(2,1)S(1)} %collective-permute-done.17.refs_2_) | copy-start | bytes 1179652
  236.5 62.6 %collective-permute-start.22 = (bf16[3,2,256,128]{3,2,1,0:T(8,128)(2,1)}, bf16[3,2,256,128]{3,2,1,0:T(8,128)(2,1)}, u32[]{:S(2)}, u32[]{:S(2)}) collective-permute-start(bf16[3,2,256,128]{3,2,1,0:T(8,128)(2,1)} %get-tuple-element.70), channel_id=1, source_target_pairs={{0,6},{1,7},{2,4},{3,5},{4,2},{5,3},{6,0},{7,1},{8,14},{9,15},{10,... | collective-permute-start | bytes 1179656 | tf_op jit(solution)/shard_map/ppermute | solution.py:68
  256.7 0.7 copy-start.9
  257.4 49.5 %collective-permute-start.23 = (bf16[3,2,256,128]{3,2,1,0:T(8,128)(2,1)}, bf16[3,2,256,128]{3,2,1,0:T(8,128)(2,1)}, u32[]{:S(2)}, u32[]{:S(2)}) collective-permute-start(bf16[3,2,256,128]{3,2,1,0:T(8,128)(2,1)} %get-tuple-element.71), channel_id=1, source_target_pairs={{0,7},{1,6},{2,5},{3,4},{4,3},{5,2},{6,1},{7,0},{8,15},{9,14},{10,... | collective-permute-start | bytes 1179656 | tf_op jit(solution)/shard_map/ppermute | solution.py:68
  258.0 1.6 copy-start

commit v7 on v6

--- a/solution.py
+++ b/solution.py
@@ -63,7 +63,7 @@
         return [lax.all_to_all(messages[0], "seq", split_axis=0, concat_axis=0, tiled=True)]
     count = len(messages)
     received = list(messages)
-    for k in range(count - 1, 0, -1):
+    for k in range(1, count):
         pairs = [(i, i ^ k) for i in range(count)]
         received[k] = lax.ppermute(messages[k], "seq", pairs)
     return received

time: 312 us -> 312 us (level)
  no operation moved by 1% of the time
where the time goes in v7:
time: 312 us
  waiting for transfers between devices  147 us (47%)
  Pallas kernels  97.5 us (31%)
  starting transfers between devices  59.3 us (19%)
  local copies, waits for them, and re-layouts  3.47 us (1%)
    ppermute x14, waiting for transfers between devices, exchange(): received[k] = lax.ppermute(messages[k], 'seq', pairs)  129 us
    pallas_call x2, Pallas kernels, attend(): pl.pallas_call(functools.partial(attend_kernel, block_rows=block_rows, he...  72.8 us
    ppermute x10, starting transfers between devices, from_behind(): return lax.ppermute(x, axis, pairs)  29.3 us
    ppermute x14, starting transfers between devices, exchange(): received[k] = lax.ppermute(messages[k], 'seq', pairs)  17.4 us
    all_to_all x2, starting transfers between devices, exchange(): lax.all_to_all(messages[0], 'seq', split_axis=0, concat_axis=0, tiled=True)  12.6 us
    all_to_all x2, waiting for transfers between devices, exchange(): lax.all_to_all(messages[0], 'seq', split_axis=0, concat_axis=0, tiled=True)  10.8 us
    pallas_call x2, Pallas kernels, pack(): pl.pallas_call(functools.partial(pack_kernel, first=start * head_dim, hea...  7.78 us
    pallas_call x2, Pallas kernels, unpack(): pl.pallas_call(functools.partial(unpack_kernel, chunk=chunk, peers=peers,...  7.44 us
  transfers between devices with their start and end apart: 26, of which 16 were waited for; matrix products, arithmetic and copies ran while one was open for 1% of the time, Pallas kernels for 29%

profile of v7, /device:TPU:8, one launch (start us, length us, event | category | flops | bytes accessed | tf_op | source)
XLA Modules:
  0.0 311.5 jit_solution(2545073464134624491)
XLA Ops:
  0.6 3.9 %pack.2 = (bf16[3,2,256,128]{3,2,1,0:T(8,128)(2,1)}, bf16[3,2,256,128]{3,2,1,0:T(8,128)(2,1)}, bf16[3,2,256,128]{3,2,1,0:T(8,128)(2,1)}, bf16[3,2,256,128]{3,2,1...) custom-call(s32[1]{0:T(128)} %bitcast.me, ...), custom_call_target="tpu_custom_call" | custom-call | tf_op jit(solution)/shard_map/pack/pallas_call | solution.py:135
  4.6 1.6 collective-permute-start.2
  7.0 1.3 top_k.17
  8.3 1.3 collective-permute-start
  9.6 1.3 top_k.24
  10.9 3.0 collective-permute-start.1
  13.9 1.6 collective-permute-start.4
  15.5 2.6 collective-permute-start.5
  19.4 1.6 collective-permute-start.7
  21.7 3.9 %pack.3.refs_0_ = bf16[8,3,2,256,128]{4,3,2,1,0:T(8,128)(2,1)} custom-call(s32[1]{0:T(128)} %bitcast.me, bf16[256,3072]{1,0:T(8,128)(2,1)} %query.3, bf16[256,3072]{1,0:T(8,128)(2,1)} %key.3, bf16[256,3072]{1,0:T(8,128)(2,1)} %value.3, bf16[256,3072]{1,0:T(8,128)(2,1)} %d_out.3, s32[8]{0:T(128)S(1)} %pad_add_fusion.asked.refs_0_, ...), custom_call_target="tpu_custom_call" | custom-call | tf_op jit(solution)/shard_map/pack/pallas_call | solution.py:135
  25.7 9.0 %collective-permute-done.4.refs_3_ = bf16[3,2,256,128]{3,2,1,0:T(8,128)(2,1)S(1)} collective-permute-done((bf16[3,2,256,128]{3,2,1,0:T(8,128)(2,1)}, bf16[3,2,256,128]{3,2,1,0:T(8,128)(2,1)S(1)}, u32[]{:S(2)}, u32[]{:S(2)}) %collective-permute-start.4) | collective-permute-done | bytes 393248 | tf_op jit(solution)/shard_map/ppermute | solution.py:68
  34.7 27.0 %collective-permute-done.5.refs_4_ = bf16[3,2,256,128]{3,2,1,0:T(8,128)(2,1)S(1)} collective-permute-done((bf16[3,2,256,128]{3,2,1,0:T(8,128)(2,1)}, bf16[3,2,256,128]{3,2,1,0:T(8,128)(2,1)S(1)}, u32[]{:S(2)}, u32[]{:S(2)}) %collective-permute-start.5) | collective-permute-done | bytes 393248 | tf_op jit(solution)/shard_map/ppermute | solution.py:68
  61.7 8.4 %collective-permute-done.6.refs_5_ = bf16[3,2,256,128]{3,2,1,0:T(8,128)(2,1)S(1)} collective-permute-done((bf16[3,2,256,128]{3,2,1,0:T(8,128)(2,1)}, bf16[3,2,256,128]{3,2,1,0:T(8,128)(2,1)S(1)}, u32[]{:S(2)}, u32[]{:S(2)}) %collective-permute-start.6) | collective-permute-done | bytes 393248 | tf_op jit(solution)/shard_map/ppermute | solution.py:68
  70.1 8.4 %collective-permute-done.7.refs_6_ = bf16[3,2,256,128]{3,2,1,0:T(8,128)(2,1)S(1)} collective-permute-done((bf16[3,2,256,128]{3,2,1,0:T(8,128)(2,1)}, bf16[3,2,256,128]{3,2,1,0:T(8,128)(2,1)S(1)}, u32[]{:S(2)}, u32[]{:S(2)}) %collective-permute-start.7) | collective-permute-done | bytes 393248 | tf_op jit(solution)/shard_map/ppermute | solution.py:68
  78.5 8.9 %collective-permute-done.8.refs_7_ = bf16[3,2,256,128]{3,2,1,0:T(8,128)(2,1)S(1)} collective-permute-done((bf16[3,2,256,128]{3,2,1,0:T(8,128)(2,1)}, bf16[3,2,256,128]{3,2,1,0:T(8,128)(2,1)S(1)}, u32[]{:S(2)}, u32[]{:S(2)}) %collective-permute-start.8) | collective-permute-done | bytes 393248 | tf_op jit(solution)/shard_map/ppermute | solution.py:68
  88.2 5.4 %all-to-all-start.1 = ((bf16[8,3,2,256,128]{4,3,2,1,0:T(8,128)(2,1)}), bf16[8,3,2,256,128]{4,3,2,1,0:T(8,128)(2,1)}, u32[]{:S(2)}, u32[]{:S(2)}) async-start(bf16[8,3,2,256,128]{4,3,2,1,0:T(8,128)(2,1)} %hold.1), calls=%async_computation.1 | async-start | bytes 6291456 | tf_op jit(solution)/shard_map/all_to_all | solution.py:63
  93.7 2.1 pick.2
  95.8 1.4 collective-permute-start.9
  97.2 1.3 collective-permute-start.10
  98.5 2.3 collective-permute-done.10.came_next
  100.8 36.4 %attend.2 = (bf16[8,3,256,128]{3,2,1,0:T(8,128)(2,1)S(1)}, f32[3,16,128,128]{3,2,1,0:T(8,128)S(1)}, bf16[4,3,128,128]{3,2,1,0:T(8,128)(2,1)S(1)}, bf16[4,3,128,128]{3,2,1,0:T(8,128)(2,1)S(1)}) custom-call(s32[1]{0:T(128)} %bitcast.me, s32[3,16,8]{2,1,0:T(8,128)S(1)} %get-tuple-element.81.lists, ...), custom_call_target="tpu_custom_call" | custom-call | tf_op jit(solution)/shard_map/attend/pallas_call | solution.py:459
  137.2 1.3 collective-permute-start.11
  138.5 8.8 %collective-permute-start.12 = (bf16[4,3,128,128]{3,2,1,0:T(8,128)(2,1)S(1)}, bf16[4,3,128,128]{3,2,1,0:T(8,128)(2,1)S(1)}, u32[]{:S(2)}, u32[]{:S(2)}) collective-permute-start(bf16[4,3,128,128]{3,2,1,0:T(8,128)(2,1)S(1)} %get-tuple-element.57), channel_id=1, source_target_pairs={{0,8},{8,16},{16,24},{1,9},{9,17},{17,25},{2,10},{10,18},{18,26},{... | collective-permute-start | bytes 1179656 | tf_op jit(solution)/shard_map/ppermute | solution.py:25
  147.4 1.3 collective-permute-done.12.earlier
  148.7 2.6 finish.2.refs_1_
  151.3 10.8 %all-to-all-done.1.refs_0_ = bf16[8,3,2,256,128]{4,3,2,1,0:T(8,128)(2,1)} async-done(((bf16[8,3,2,256,128]{4,3,2,1,0:T(8,128)(2,1)}), bf16[8,3,2,256,128]{4,3,2,1,0:T(8,128)(2,1)}, u32[]{:S(2)}, u32[]{:S(2)}) %all-to-all-start.1) | async-done | bytes 3145760 | tf_op jit(solution)/shard_map/all_to_all | solution.py:63
  162.1 7.2 %all-to-all-start = ((bf16[8,3,2,256,128]{4,3,2,1,0:T(8,128)(2,1)}), bf16[8,3,2,256,128]{4,3,2,1,0:T(8,128)(2,1)S(1)}, u32[]{:S(2)}, u32[]{:S(2)}) async-start(bf16[8,3,2,256,128]{4,3,2,1,0:T(8,128)(2,1)} %finish.2.refs_1_), calls=%async_computation | async-start | bytes 6291456 | tf_op jit(solution)/shard_map/all_to_all | solution.py:63
  169.3 2.1 pick.3
  171.4 1.3 collective-permute-start.13
  172.7 1.3 collective-permute-start.14
  174.0 2.3 collective-permute-done.14.came_next
  176.3 36.4 %attend.3 = (bf16[8,3,256,128]{3,2,1,0:T(8,128)(2,1)S(1)}, f32[3,16,128,128]{3,2,1,0:T(8,128)S(1)}, bf16[4,3,128,128]{3,2,1,0:T(8,128)(2,1)S(1)}, bf16[4,3,128,128]{3,2,1,0:T(8,128)(2,1)S(1)}) custom-call(s32[1]{0:T(128)} %bitcast.me, s32[3,16,8]{2,1,0:T(8,128)S(1)} %get-tuple-element.80.lists, ...), custom_call_target="tpu_custom_call" | custom-call | tf_op jit(solution)/shard_map/attend/pallas_call | solution.py:459
  212.8 1.3 collective-permute-start.15
  214.1 8.3 %collective-permute-start.16 = (bf16[4,3,128,128]{3,2,1,0:T(8,128)(2,1)S(1)}, bf16[4,3,128,128]{3,2,1,0:T(8,128)(2,1)S(1)}, u32[]{:S(2)}, u32[]{:S(2)}) collective-permute-start(bf16[4,3,128,128]{3,2,1,0:T(8,128)(2,1)S(1)} %get-tuple-element.63), channel_id=1, source_target_pairs={{0,8},{8,16},{16,24},{1,9},{9,17},{17,25},{2,10},{10,18},{18,26},{... | collective-permute-start | bytes 1179656 | tf_op jit(solution)/shard_map/ppermute | solution.py:25
  223.5 2.6 finish.3
  226.1 1.5 collective-permute-start.17
  228.2 1.5 collective-permute-start.19
  229.7 2.1 collective-permute-start.20
  231.8 1.7 collective-permute-start.21
  233.5 3.0 collective-permute-done.17.refs_2_
  236.6 20.1 %collective-permute-done.18.refs_3_ = bf16[3,2,256,128]{3,2,1,0:T(8,128)(2,1)S(1)} collective-permute-done((bf16[3,2,256,128]{3,2,1,0:T(8,128)(2,1)}, bf16[3,2,256,128]{3,2,1,0:T(8,128)(2,1)S(1)}, u32[]{:S(2)}, u32[]{:S(2)}) %collective-permute-start.18) | collective-permute-done | bytes 393248 | tf_op jit(solution)/shard_map/ppermute | solution.py:68
  258.0 1.6 copy-done
  259.6 3.0 unpack.2
  262.7 5.7 %collective-permute-done.19.refs_4_ = bf16[3,2,256,128]{3,2,1,0:T(8,128)(2,1)} collective-permute-done((bf16[3,2,256,128]{3,2,1,0:T(8,128)(2,1)}, bf16[3,2,256,128]{3,2,1,0:T(8,128)(2,1)}, u32[]{:S(2)}, u32[]{:S(2)}) %collective-permute-start.19) | collective-permute-done | bytes 393248 | tf_op jit(solution)/shard_map/ppermute | solution.py:68
  268.4 19.8 %collective-permute-done.21.refs_6_ = bf16[3,2,256,128]{3,2,1,0:T(8,128)(2,1)} collective-permute-done((bf16[3,2,256,128]{3,2,1,0:T(8,128)(2,1)}, bf16[3,2,256,128]{3,2,1,0:T(8,128)(2,1)}, u32[]{:S(2)}, u32[]{:S(2)}) %collective-permute-start.21) | collective-permute-done | bytes 393248 | tf_op jit(solution)/shard_map/ppermute | solution.py:68
  288.2 10.9 %collective-permute-done.22.refs_7_ = bf16[3,2,256,128]{3,2,1,0:T(8,128)(2,1)} collective-permute-done((bf16[3,2,256,128]{3,2,1,0:T(8,128)(2,1)}, bf16[3,2,256,128]{3,2,1,0:T(8,128)(2,1)}, u32[]{:S(2)}, u32[]{:S(2)}) %collective-permute-start.22) | collective-permute-done | bytes 393248 | tf_op jit(solution)/shard_map/ppermute | solution.py:68
  299.1 7.8 %collective-permute-done.23.refs_8_ = bf16[3,2,256,128]{3,2,1,0:T(8,128)(2,1)} collective-permute-done((bf16[3,2,256,128]{3,2,1,0:T(8,128)(2,1)}, bf16[3,2,256,128]{3,2,1,0:T(8,128)(2,1)}, u32[]{:S(2)}, u32[]{:S(2)}) %collective-permute-start.23) | collective-permute-done | bytes 393248 | tf_op jit(solution)/shard_map/ppermute | solution.py:68
  306.9 4.4 %unpack.3 = (bf16[256,3072]{1,0:T(8,128)(2,1)}, bf16[256,3072]{1,0:T(8,128)(2,1)}, bf16[256,3072]{1,0:T(8,128)(2,1)}, bf16[256,3072]{1,0:T(8,128)(2,1)}) custom-call(s32[1]{0:T(128)} %bitcast.me, bf16[8,3,2,256,128]{4,3,2,1,0:T(8,128)(2,1)} %copy-done, ...), custom_call_target="tpu_custom_call", output_to_operand_aliasing={{0}: (10, {}), {1}: (11, {}), {2}: (12, {}), {3}: (13, {})} | custom-call | tf_op jit(solution)/shard_map/unpack/pallas_call | solution.py:241
  (55 shorter events, 6.6 us)
Async XLA Ops:
  0.6 5.9 %copy-start.10 = (s32[6,16,8]{1,2,0:T(8,128)S(1)}, s32[6,16,8]{1,2,0:T(8,128)}, u32[]{:S(2)}) copy-start(s32[6,16,8]{1,2,0:T(8,128)} %param.9) | copy-start | bytes 9220
  4.6 14.8 %collective-permute-start.2 = (bf16[3,2,256,128]{3,2,1,0:T(8,128)(2,1)}, bf16[3,2,256,128]{3,2,1,0:T(8,128)(2,1)S(1)}, u32[]{:S(2)}, u32[]{:S(2)}) collective-permute-start(bf16[3,2,256,128]{3,2,1,0:T(8,128)(2,1)} %get-tuple-element.45), channel_id=1, source_target_pairs={{0,1},{1,0},{2,3},{3,2},{4,5},{5,4},{6,7},{7,6},{8,9},{9,8},{10,11... | collective-permute-start | bytes 1179656 | tf_op jit(solution)/shard_map/ppermute | solution.py:68
  6.1 14.9 %collective-permute-start.3 = (bf16[3,2,256,128]{3,2,1,0:T(8,128)(2,1)}, bf16[3,2,256,128]{3,2,1,0:T(8,128)(2,1)S(1)}, u32[]{:S(2)}, u32[]{:S(2)}) collective-permute-start(bf16[3,2,256,128]{3,2,1,0:T(8,128)(2,1)} %get-tuple-element.46), channel_id=1, source_target_pairs={{0,2},{1,3},{2,0},{3,1},{4,6},{5,7},{6,4},{7,5},{8,10},{9,11},{10,... | collective-permute-start | bytes 1179656 | tf_op jit(solution)/shard_map/ppermute | solution.py:68
  8.3 7.3 %collective-permute-start = (s32[4]{0:T(128)S(1)}, s32[4]{0:T(128)S(1)}, u32[]{:S(2)}, u32[]{:S(2)}) collective-permute-start(s32[4]{0:T(128)S(1)} %get-tuple-element.83), channel_id=1, source_target_pairs={{8,0},{16,8},{24,16},{9,1},{17,9},{25,17},{10,2},{18,10},{26,18},{... | collective-permute-start | bytes 56 | tf_op jit(solution)/shard_map/ppermute | solution.py:25
  10.9 7.2 %collective-permute-start.1 = (s32[4]{0:T(128)S(1)}, s32[4]{0:T(128)S(1)}, u32[]{:S(2)}, u32[]{:S(2)}) collective-permute-start(s32[4]{0:T(128)S(1)} %get-tuple-element.85), channel_id=1, source_target_pairs={{0,8},{8,16},{16,24},{1,9},{9,17},{17,25},{2,10},{10,18},{18,26},{... | collective-permute-start | bytes 56 | tf_op jit(solution)/shard_map/ppermute | solution.py:25
  13.9 20.8 %collective-permute-start.4 = (bf16[3,2,256,128]{3,2,1,0:T(8,128)(2,1)}, bf16[3,2,256,128]{3,2,1,0:T(8,128)(2,1)S(1)}, u32[]{:S(2)}, u32[]{:S(2)}) collective-permute-start(bf16[3,2,256,128]{3,2,1,0:T(8,128)(2,1)} %get-tuple-element.47), channel_id=1, source_target_pairs={{0,3},{1,2},{2,1},{3,0},{4,7},{5,6},{6,5},{7,4},{8,11},{9,10},{10,... | collective-permute-start | bytes 1179656 | tf_op jit(solution)/shard_map/ppermute | solution.py:68
  15.5 46.2 %collective-permute-start.5 = (bf16[3,2,256,128]{3,2,1,0:T(8,128)(2,1)}, bf16[3,2,256,128]{3,2,1,0:T(8,128)(2,1)S(1)}, u32[]{:S(2)}, u32[]{:S(2)}) collective-permute-start(bf16[3,2,256,128]{3,2,1,0:T(8,128)(2,1)} %get-tuple-element.48), channel_id=1, source_target_pairs={{0,4},{1,5},{2,6},{3,7},{4,0},{5,1},{6,2},{7,3},{8,12},{9,13},{10,... | collective-permute-start | bytes 1179656 | tf_op jit(solution)/shard_map/ppermute | solution.py:68
  18.1 52.0 %collective-permute-start.6 = (bf16[3,2,256,128]{3,2,1,0:T(8,128)(2,1)}, bf16[3,2,256,128]{3,2,1,0:T(8,128)(2,1)S(1)}, u32[]{:S(2)}, u32[]{:S(2)}) collective-permute-start(bf16[3,2,256,128]{3,2,1,0:T(8,128)(2,1)} %get-tuple-element.49), channel_id=1, source_target_pairs={{0,5},{1,4},{2,7},{3,6},{4,1},{5,0},{6,3},{7,2},{8,13},{9,12},{10,... | collective-permute-start | bytes 1179656 | tf_op jit(solution)/shard_map/ppermute | solution.py:68
  19.4 6.2 %copy-start.1 = (bf16[3,2,256,128]{3,2,1,0:T(8,128)(2,1)}, bf16[3,2,256,128]{3,2,1,0:T(8,128)(2,1)S(1)}, u32[]{:S(2)}) copy-start(bf16[3,2,256,128]{3,2,1,0:T(8,128)(2,1)S(1)} %collective-permute-done.2.refs_1_) | copy-start | bytes 1179652
  19.4 59.2 %collective-permute-start.7 = (bf16[3,2,256,128]{3,2,1,0:T(8,128)(2,1)}, bf16[3,2,256,128]{3,2,1,0:T(8,128)(2,1)S(1)}, u32[]{:S(2)}, u32[]{:S(2)}) collective-permute-start(bf16[3,2,256,128]{3,2,1,0:T(8,128)(2,1)} %get-tuple-element.50), channel_id=1, source_target_pairs={{0,6},{1,7},{2,4},{3,5},{4,2},{5,3},{6,0},{7,1},{8,14},{9,15},{10,... | collective-permute-start | bytes 1179656 | tf_op jit(solution)/shard_map/ppermute | solution.py:68
  21.0 4.7 %copy-start.2 = (bf16[3,2,256,128]{3,2,1,0:T(8,128)(2,1)}, bf16[3,2,256,128]{3,2,1,0:T(8,128)(2,1)S(1)}, u32[]{:S(2)}) copy-start(bf16[3,2,256,128]{3,2,1,0:T(8,128)(2,1)S(1)} %collective-permute-done.3.refs_2_) | copy-start | bytes 1179652
  21.0 66.5 %collective-permute-start.8 = (bf16[3,2,256,128]{3,2,1,0:T(8,128)(2,1)}, bf16[3,2,256,128]{3,2,1,0:T(8,128)(2,1)S(1)}, u32[]{:S(2)}, u32[]{:S(2)}) collective-permute-start(bf16[3,2,256,128]{3,2,1,0:T(8,128)(2,1)} %get-tuple-element.51), channel_id=1, source_target_pairs={{0,7},{1,6},{2,5},{3,4},{4,3},{5,2},{6,1},{7,0},{8,15},{9,14},{10,... | collective-permute-start | bytes 1179656 | tf_op jit(solution)/shard_map/ppermute | solution.py:68
  34.7 52.8 %copy-start.3 = (bf16[3,2,256,128]{3,2,1,0:T(8,128)(2,1)}, bf16[3,2,256,128]{3,2,1,0:T(8,128)(2,1)S(1)}, u32[]{:S(2)}) copy-start(bf16[3,2,256,128]{3,2,1,0:T(8,128)(2,1)S(1)} %collective-permute-done.4.refs_3_) | copy-start | bytes 1179652
  61.7 25.8 %copy-start.4 = (bf16[3,2,256,128]{3,2,1,0:T(8,128)(2,1)}, bf16[3,2,256,128]{3,2,1,0:T(8,128)(2,1)S(1)}, u32[]{:S(2)}) copy-start(bf16[3,2,256,128]{3,2,1,0:T(8,128)(2,1)S(1)} %collective-permute-done.5.refs_4_) | copy-start | bytes 1179652
  70.1 17.4 %copy-start.5 = (bf16[3,2,256,128]{3,2,1,0:T(8,128)(2,1)}, bf16[3,2,256,128]{3,2,1,0:T(8,128)(2,1)S(1)}, u32[]{:S(2)}) copy-start(bf16[3,2,256,128]{3,2,1,0:T(8,128)(2,1)S(1)} %collective-permute-done.6.refs_5_) | copy-start | bytes 1179652
  78.5 8.9 %copy-start.6 = (bf16[3,2,256,128]{3,2,1,0:T(8,128)(2,1)}, bf16[3,2,256,128]{3,2,1,0:T(8,128)(2,1)S(1)}, u32[]{:S(2)}) copy-start(bf16[3,2,256,128]{3,2,1,0:T(8,128)(2,1)S(1)} %collective-permute-done.7.refs_6_) | copy-start | bytes 1179652
  87.5 0.8 copy-start.7
  88.2 73.9 %all-to-all-start.1 = ((bf16[8,3,2,256,128]{4,3,2,1,0:T(8,128)(2,1)}), bf16[8,3,2,256,128]{4,3,2,1,0:T(8,128)(2,1)}, u32[]{:S(2)}, u32[]{:S(2)}) async-start(bf16[8,3,2,256,128]{4,3,2,1,0:T(8,128)(2,1)} %hold.1), calls=%async_computation.1 | async-start | bytes 6291456 | tf_op jit(solution)/shard_map/all_to_all | solution.py:63
  95.8 2.7 collective-permute-start.9
  97.2 3.6 %collective-permute-start.10 = (bf16[4,3,128,128]{3,2,1,0:T(8,128)(2,1)S(1)}, bf16[4,3,128,128]{3,2,1,0:T(8,128)(2,1)S(1)}, u32[]{:S(2)}, u32[]{:S(2)}) collective-permute-start(bf16[4,3,128,128]{3,2,1,0:T(8,128)(2,1)S(1)} %get-tuple-element.53), channel_id=1, source_target_pairs={{8,0},{16,8},{24,16},{9,1},{17,9},{25,17},{10,2},{18,10},{26,18},{... | collective-permute-start | bytes 1179656 | tf_op jit(solution)/shard_map/ppermute | solution.py:25
  137.2 10.2 %collective-permute-start.11 = (bf16[4,3,128,128]{3,2,1,0:T(8,128)(2,1)S(1)}, bf16[4,3,128,128]{3,2,1,0:T(8,128)(2,1)S(1)}, u32[]{:S(2)}, u32[]{:S(2)}) collective-permute-start(bf16[4,3,128,128]{3,2,1,0:T(8,128)(2,1)S(1)} %get-tuple-element.56), channel_id=1, source_target_pairs={{8,0},{16,8},{24,16},{9,1},{17,9},{25,17},{10,2},{18,10},{26,18},{... | collective-permute-start | bytes 1179656 | tf_op jit(solution)/shard_map/ppermute | solution.py:25
  138.5 10.2 %collective-permute-start.12 = (bf16[4,3,128,128]{3,2,1,0:T(8,128)(2,1)S(1)}, bf16[4,3,128,128]{3,2,1,0:T(8,128)(2,1)S(1)}, u32[]{:S(2)}, u32[]{:S(2)}) collective-permute-start(bf16[4,3,128,128]{3,2,1,0:T(8,128)(2,1)S(1)} %get-tuple-element.57), channel_id=1, source_target_pairs={{0,8},{8,16},{16,24},{1,9},{9,17},{17,25},{2,10},{10,18},{18,26},{... | collective-permute-start | bytes 1179656 | tf_op jit(solution)/shard_map/ppermute | solution.py:25
  162.1 95.9 %all-to-all-start = ((bf16[8,3,2,256,128]{4,3,2,1,0:T(8,128)(2,1)}), bf16[8,3,2,256,128]{4,3,2,1,0:T(8,128)(2,1)S(1)}, u32[]{:S(2)}, u32[]{:S(2)}) async-start(bf16[8,3,2,256,128]{4,3,2,1,0:T(8,128)(2,1)} %finish.2.refs_1_), calls=%async_computation | async-start | bytes 6291456 | tf_op jit(solution)/shard_map/all_to_all | solution.py:63
  171.4 2.6 collective-permute-start.13
  172.7 3.6 %collective-permute-start.14 = (bf16[4,3,128,128]{3,2,1,0:T(8,128)(2,1)S(1)}, bf16[4,3,128,128]{3,2,1,0:T(8,128)(2,1)S(1)}, u32[]{:S(2)}, u32[]{:S(2)}) collective-permute-start(bf16[4,3,128,128]{3,2,1,0:T(8,128)(2,1)S(1)} %get-tuple-element.59), channel_id=1, source_target_pairs={{8,0},{16,8},{24,16},{9,1},{17,9},{25,17},{10,2},{18,10},{26,18},{... | collective-permute-start | bytes 1179656 | tf_op jit(solution)/shard_map/ppermute | solution.py:25
  212.8 9.6 %collective-permute-start.15 = (bf16[4,3,128,128]{3,2,1,0:T(8,128)(2,1)S(1)}, bf16[4,3,128,128]{3,2,1,0:T(8,128)(2,1)S(1)}, u32[]{:S(2)}, u32[]{:S(2)}) collective-permute-start(bf16[4,3,128,128]{3,2,1,0:T(8,128)(2,1)S(1)} %get-tuple-element.62), channel_id=1, source_target_pairs={{8,0},{16,8},{24,16},{9,1},{17,9},{25,17},{10,2},{18,10},{26,18},{... | collective-permute-start | bytes 1179656 | tf_op jit(solution)/shard_map/ppermute | solution.py:25
  214.1 9.5 %collective-permute-start.16 = (bf16[4,3,128,128]{3,2,1,0:T(8,128)(2,1)S(1)}, bf16[4,3,128,128]{3,2,1,0:T(8,128)(2,1)S(1)}, u32[]{:S(2)}, u32[]{:S(2)}) collective-permute-start(bf16[4,3,128,128]{3,2,1,0:T(8,128)(2,1)S(1)} %get-tuple-element.63), channel_id=1, source_target_pairs={{0,8},{8,16},{16,24},{1,9},{9,17},{17,25},{2,10},{10,18},{18,26},{... | collective-permute-start | bytes 1179656 | tf_op jit(solution)/shard_map/ppermute | solution.py:25
  226.1 10.4 %collective-permute-start.17 = (bf16[3,2,256,128]{3,2,1,0:T(8,128)(2,1)}, bf16[3,2,256,128]{3,2,1,0:T(8,128)(2,1)S(1)}, u32[]{:S(2)}, u32[]{:S(2)}) collective-permute-start(bf16[3,2,256,128]{3,2,1,0:T(8,128)(2,1)} %get-tuple-element.65), channel_id=1, source_target_pairs={{0,1},{1,0},{2,3},{3,2},{4,5},{5,4},{6,7},{7,6},{8,9},{9,8},{10,11... | collective-permute-start | bytes 1179656 | tf_op jit(solution)/shard_map/ppermute | solution.py:68
  227.7 29.0 %collective-permute-start.18 = (bf16[3,2,256,128]{3,2,1,0:T(8,128)(2,1)}, bf16[3,2,256,128]{3,2,1,0:T(8,128)(2,1)S(1)}, u32[]{:S(2)}, u32[]{:S(2)}) collective-permute-start(bf16[3,2,256,128]{3,2,1,0:T(8,128)(2,1)} %get-tuple-element.66), channel_id=1, source_target_pairs={{0,2},{1,3},{2,0},{3,1},{4,6},{5,7},{6,4},{7,5},{8,10},{9,11},{10,... | collective-permute-start | bytes 1179656 | tf_op jit(solution)/shard_map/ppermute | solution.py:68
  228.2 40.2 %collective-permute-start.19 = (bf16[3,2,256,128]{3,2,1,0:T(8,128)(2,1)}, bf16[3,2,256,128]{3,2,1,0:T(8,128)(2,1)}, u32[]{:S(2)}, u32[]{:S(2)}) collective-permute-start(bf16[3,2,256,128]{3,2,1,0:T(8,128)(2,1)} %get-tuple-element.67), channel_id=1, source_target_pairs={{0,3},{1,2},{2,1},{3,0},{4,7},{5,6},{6,5},{7,4},{8,11},{9,10},{10,... | collective-permute-start | bytes 1179656 | tf_op jit(solution)/shard_map/ppermute | solution.py:68
  229.7 38.7 %collective-permute-start.20 = (bf16[3,2,256,128]{3,2,1,0:T(8,128)(2,1)}, bf16[3,2,256,128]{3,2,1,0:T(8,128)(2,1)}, u32[]{:S(2)}, u32[]{:S(2)}) collective-permute-start(bf16[3,2,256,128]{3,2,1,0:T(8,128)(2,1)} %get-tuple-element.68), channel_id=1, source_target_pairs={{0,4},{1,5},{2,6},{3,7},{4,0},{5,1},{6,2},{7,3},{8,12},{9,13},{10,... | collective-permute-start | bytes 1179656 | tf_op jit(solution)/shard_map/ppermute | solution.py:68
  231.8 56.4 %collective-permute-start.21 = (bf16[3,2,256,128]{3,2,1,0:T(8,128)(2,1)}, bf16[3,2,256,128]{3,2,1,0:T(8,128)(2,1)}, u32[]{:S(2)}, u32[]{:S(2)}) collective-permute-start(bf16[3,2,256,128]{3,2,1,0:T(8,128)(2,1)} %get-tuple-element.69), channel_id=1, source_target_pairs={{0,5},{1,4},{2,7},{3,6},{4,1},{5,0},{6,3},{7,2},{8,13},{9,12},{10,... | collective-permute-start | bytes 1179656 | tf_op jit(solution)/shard_map/ppermute | solution.py:68
  236.5 70.4 %copy-start.8 = (bf16[3,2,256,128]{3,2,1,0:T(8,128)(2,1)}, bf16[3,2,256,128]{3,2,1,0:T(8,128)(2,1)S(1)}, u32[]{:S(2)}) copy-start(bf16[3,2,256,128]{3,2,1,0:T(8,128)(2,1)S(1)} %collective-permute-done.17.refs_2_) | copy-start | bytes 1179652
  236.5 62.6 %collective-permute-start.22 = (bf16[3,2,256,128]{3,2,1,0:T(8,128)(2,1)}, bf16[3,2,256,128]{3,2,1,0:T(8,128)(2,1)}, u32[]{:S(2)}, u32[]{:S(2)}) collective-permute-start(bf16[3,2,256,128]{3,2,1,0:T(8,128)(2,1)} %get-tuple-element.70), channel_id=1, source_target_pairs={{0,6},{1,7},{2,4},{3,5},{4,2},{5,3},{6,0},{7,1},{8,14},{9,15},{10,... | collective-permute-start | bytes 1179656 | tf_op jit(solution)/shard_map/ppermute | solution.py:68
  256.7 0.7 copy-start.9
  257.4 49.5 %collective-permute-start.23 = (bf16[3,2,256,128]{3,2,1,0:T(8,128)(2,1)}, bf16[3,2,256,128]{3,2,1,0:T(8,128)(2,1)}, u32[]{:S(2)}, u32[]{:S(2)}) collective-permute-start(bf16[3,2,256,128]{3,2,1,0:T(8,128)(2,1)} %get-tuple-element.71), channel_id=1, source_target_pairs={{0,7},{1,6},{2,5},{3,4},{4,3},{5,2},{6,1},{7,0},{8,15},{9,14},{10,... | collective-permute-start | bytes 1179656 | tf_op jit(solution)/shard_map/ppermute | solution.py:68
  258.0 1.6 copy-start

commit v8 on v7

--- a/solution.py
+++ b/solution.py
@@ -28,7 +28,7 @@
 def part_of(messages, me, item):
     if len(messages) == 1:
         return messages[0].at[item], item
-    return messages[item], me[0] ^ item
+    return messages[item], me[0] ^ (len(messages) - 1 - item)
 
 
 def message_shape(messages):
@@ -63,9 +63,9 @@
         return [lax.all_to_all(messages[0], "seq", split_axis=0, concat_axis=0, tiled=True)]
     count = len(messages)
     received = list(messages)
-    for k in range(1, count):
-        pairs = [(i, i ^ k) for i in range(count)]
-        received[k] = lax.ppermute(messages[k], "seq", pairs)
+    for item in range(count - 1):
+        pairs = [(i, i ^ (count - 1 - item)) for i in range(count)]
+        received[item] = lax.ppermute(messages[item], "seq", pairs)
     return received
 
 
@@ -77,11 +77,11 @@
     sources = (key, value, query, d_out)
     aligned = apart and per_peer % LANES == 0
     at_once = aligned or not apart
-    order = range(peers - 1, -1, -1)
+    order = range(peers)
 
     def span(item):
         if aligned:
-            base, begin = pl.multiple_of((me[0] ^ item) * per_peer, LANES), first
+            base, begin = pl.multiple_of(part_of(messages, me, item)[1] * per_peer, LANES), first
         else:
             base, begin = 0, item * per_peer + first
         low = begin // LANES * LANES
@@ -509,7 +509,7 @@
                 ready[peer, head, 0, i * block_rows : (i + 1) * block_rows] = sums[
                     peer * each + i
                 ].astype(ready.dtype)
-        for item in range(peers - 1, -1, -1):
+        for item in range(peers):
             send(item, head).start()
     for head in range(heads):
         for item in range(peers):
@@ -589,7 +589,7 @@
             me, arrays, start, size, heads_here, peers, head_dim, chunk == 0, after
         )
         if chunk == 1:
-            packed = hold(packed, came[0][1:])
+            packed = hold(packed, came[0][:-1])
         came.append(exchange(packed))
     received = []
     outs = finished = ()

time: 312 us -> 312 us (level); the launches traced: 312 us -> 308 us
  waiting for transfers between devices: 147 us -> 138 us
  starting transfers between devices: 59.3 us -> 63 us
    ppermute x14, waiting for transfers between devices: 129 us -> 121 us  [exchange(): received[item] = lax.ppermute(messages[item], 'seq', pairs)]
    all_to_all x2, waiting for transfers between devices: 10.8 us -> 7.29 us  [exchange(): lax.all_to_all(messages[0], 'seq', split_axis=0, concat_axis=0, tiled=True)]
    ppermute x10, waiting for transfers between devices: 7.03 us -> 10.3 us  [from_behind(): return lax.ppermute(x, axis, pairs)]
  transfers between devices with their start and end apart: 26 -> 26, of which waited for: 16 -> 14; matrix products, arithmetic and copies ran while one was open for 1% -> 1% of each run, Pallas kernels for 29% -> 29%
where the time goes in v8:
time: 312 us; the launch traced here: 308 us
  waiting for transfers between devices  138 us (44%)
  Pallas kernels  98 us (31%)
  starting transfers between devices  63 us (20%)
  local copies, waits for them, and re-layouts  4.21 us (1%)
    ppermute x14, waiting for transfers between devices, exchange(): received[item] = lax.ppermute(messages[item], 'seq', pairs)  121 us
    pallas_call x2, Pallas kernels, attend(): pl.pallas_call(functools.partial(attend_kernel, block_rows=block_rows, he...  72.8 us
    ppermute x10, starting transfers between devices, from_behind(): return lax.ppermute(x, axis, pairs)  30.3 us
    ppermute x14, starting transfers between devices, exchange(): received[item] = lax.ppermute(messages[item], 'seq', pairs)  19.8 us
    all_to_all x2, starting transfers between devices, exchange(): lax.all_to_all(messages[0], 'seq', split_axis=0, concat_axis=0, tiled=True)  12.9 us
    ppermute x10, waiting for transfers between devices, from_behind(): return lax.ppermute(x, axis, pairs)  10.3 us
    pallas_call x2, Pallas kernels, unpack(): pl.pallas_call(functools.partial(unpack_kernel, chunk=chunk, peers=peers,...  7.92 us
    pallas_call x2, Pallas kernels, pack(): pl.pallas_call(functools.partial(pack_kernel, first=start * head_dim, hea...  7.8 us
  transfers between devices with their start and end apart: 26, of which 14 were waited for; matrix products, arithmetic and copies ran while one was open for 1% of the time, Pallas kernels for 29%

profile of v8, /device:TPU:8, one launch (start us, length us, event | category | flops | bytes accessed | tf_op | source)
XLA Modules:
  0.0 307.5 jit_solution(677596921665059150)
XLA Ops:
  0.6 3.9 %pack.2 = (bf16[3,2,256,128]{3,2,1,0:T(8,128)(2,1)}, bf16[3,2,256,128]{3,2,1,0:T(8,128)(2,1)}, bf16[3,2,256,128]{3,2,1,0:T(8,128)(2,1)}, bf16[3,2,256,128]{3,2,1...) custom-call(s32[1]{0:T(128)} %bitcast.me, ...), custom_call_target="tpu_custom_call" | custom-call | tf_op jit(solution)/shard_map/pack/pallas_call | solution.py:135
  4.6 2.6 collective-permute-start.2
  8.0 1.3 top_k.17
  9.3 1.3 collective-permute-start
  10.6 1.3 top_k.24
  11.9 3.0 collective-permute-start.1
  14.9 4.4 %collective-permute-start.4 = (bf16[3,2,256,128]{3,2,1,0:T(8,128)(2,1)}, bf16[3,2,256,128]{3,2,1,0:T(8,128)(2,1)S(1)}, u32[]{:S(2)}, u32[]{:S(2)}) collective-permute-start(bf16[3,2,256,128]{3,2,1,0:T(8,128)(2,1)} %get-tuple-element.46), channel_id=1, source_target_pairs={{0,5},{1,4},{2,7},{3,6},{4,1},{5,0},{6,3},{7,2},{8,13},{9,12},{10,... | collective-permute-start | bytes 1179656 | tf_op jit(solution)/shard_map/ppermute | solution.py:68
  19.5 1.6 collective-permute-start.6
  21.1 35.4 %collective-permute-done.2.refs_0_.refs_1_ = bf16[3,2,256,128]{3,2,1,0:T(8,128)(2,1)S(1)} collective-permute-done((bf16[3,2,256,128]{3,2,1,0:T(8,128)(2,1)}, bf16[3,2,256,128]{3,2,1,0:T(8,128)(2,1)S(1)}, u32[]{:S(2)}, u32[]{:S(2)}) %collective-permute-start.2) | collective-permute-done | bytes 393248 | tf_op jit(solution)/shard_map/ppermute | solution.py:68
  56.5 7.3 %collective-permute-done.3.refs_1_.refs_2_ = bf16[3,2,256,128]{3,2,1,0:T(8,128)(2,1)S(1)} collective-permute-done((bf16[3,2,256,128]{3,2,1,0:T(8,128)(2,1)}, bf16[3,2,256,128]{3,2,1,0:T(8,128)(2,1)S(1)}, u32[]{:S(2)}, u32[]{:S(2)}) %collective-permute-start.3) | collective-permute-done | bytes 393248 | tf_op jit(solution)/shard_map/ppermute | solution.py:68
  64.9 3.9 %pack.3.refs_0_ = bf16[8,3,2,256,128]{4,3,2,1,0:T(8,128)(2,1)} custom-call(s32[1]{0:T(128)} %bitcast.me, bf16[256,3072]{1,0:T(8,128)(2,1)} %query.3, bf16[256,3072]{1,0:T(8,128)(2,1)} %key.3, bf16[256,3072]{1,0:T(8,128)(2,1)} %value.3, bf16[256,3072]{1,0:T(8,128)(2,1)} %d_out.3, s32[8]{0:T(128)S(1)} %pad_add_fusion.asked.refs_0_, ...), custom_call_target="tpu_custom_call" | custom-call | tf_op jit(solution)/shard_map/pack/pallas_call | solution.py:135
  68.8 2.6 collective-permute-done.4.refs_2_.refs_3_
  71.4 7.3 %collective-permute-done.5.refs_3_.refs_4_ = bf16[3,2,256,128]{3,2,1,0:T(8,128)(2,1)S(1)} collective-permute-done((bf16[3,2,256,128]{3,2,1,0:T(8,128)(2,1)}, bf16[3,2,256,128]{3,2,1,0:T(8,128)(2,1)S(1)}, u32[]{:S(2)}, u32[]{:S(2)}) %collective-permute-start.5) | collective-permute-done | bytes 393248 | tf_op jit(solution)/shard_map/ppermute | solution.py:68
  78.7 1.6 collective-permute-done.7.refs_5_.refs_6_
  80.3 0.7 copy-done.6
  81.8 6.7 %all-to-all-start.1 = ((bf16[8,3,2,256,128]{4,3,2,1,0:T(8,128)(2,1)}), bf16[8,3,2,256,128]{4,3,2,1,0:T(8,128)(2,1)}, u32[]{:S(2)}, u32[]{:S(2)}) async-start(bf16[8,3,2,256,128]{4,3,2,1,0:T(8,128)(2,1)} %hold.1), calls=%async_computation.1 | async-start | bytes 6291456 | tf_op jit(solution)/shard_map/all_to_all | solution.py:63
  88.6 2.1 pick.2
  90.7 1.3 collective-permute-start.9
  92.0 1.3 collective-permute-start.10
  93.3 3.9 %collective-permute-done.10.came_next = bf16[4,3,128,128]{3,2,1,0:T(8,128)(2,1)S(1)} collective-permute-done((bf16[4,3,128,128]{3,2,1,0:T(8,128)(2,1)S(1)}, bf16[4,3,128,128]{3,2,1,0:T(8,128)(2,1)S(1)}, u32[]{:S(2)}, u32[]{:S(2)}) %collective-permute-start.10) | collective-permute-done | bytes 393248 | tf_op jit(solution)/shard_map/ppermute | solution.py:25
  97.3 36.4 %attend.2 = (bf16[8,3,256,128]{3,2,1,0:T(8,128)(2,1)S(1)}, f32[3,16,128,128]{3,2,1,0:T(8,128)S(1)}, bf16[4,3,128,128]{3,2,1,0:T(8,128)(2,1)S(1)}, bf16[4,3,128,128]{3,2,1,0:T(8,128)(2,1)S(1)}) custom-call(s32[1]{0:T(128)} %bitcast.me, s32[3,16,8]{2,1,0:T(8,128)S(1)} %get-tuple-element.81.lists, ...), custom_call_target="tpu_custom_call" | custom-call | tf_op jit(solution)/shard_map/attend/pallas_call | solution.py:459
  133.7 1.3 collective-permute-start.11
  135.0 9.1 %collective-permute-start.12 = (bf16[4,3,128,128]{3,2,1,0:T(8,128)(2,1)S(1)}, bf16[4,3,128,128]{3,2,1,0:T(8,128)(2,1)S(1)}, u32[]{:S(2)}, u32[]{:S(2)}) collective-permute-start(bf16[4,3,128,128]{3,2,1,0:T(8,128)(2,1)S(1)} %get-tuple-element.57), channel_id=1, source_target_pairs={{0,8},{8,16},{16,24},{1,9},{9,17},{17,25},{2,10},{10,18},{18,26},{... | collective-permute-start | bytes 1179656 | tf_op jit(solution)/shard_map/ppermute | solution.py:25
  144.1 1.3 collective-permute-done.12.earlier
  145.4 2.6 finish.2.refs_1_
  148.1 7.3 %all-to-all-done.1.refs_0_ = bf16[8,3,2,256,128]{4,3,2,1,0:T(8,128)(2,1)} async-done(((bf16[8,3,2,256,128]{4,3,2,1,0:T(8,128)(2,1)}), bf16[8,3,2,256,128]{4,3,2,1,0:T(8,128)(2,1)}, u32[]{:S(2)}, u32[]{:S(2)}) %all-to-all-start.1) | async-done | bytes 3145760 | tf_op jit(solution)/shard_map/all_to_all | solution.py:63
  155.4 6.2 %all-to-all-start = ((bf16[8,3,2,256,128]{4,3,2,1,0:T(8,128)(2,1)}), bf16[8,3,2,256,128]{4,3,2,1,0:T(8,128)(2,1)S(1)}, u32[]{:S(2)}, u32[]{:S(2)}) async-start(bf16[8,3,2,256,128]{4,3,2,1,0:T(8,128)(2,1)} %finish.2.refs_1_), calls=%async_computation | async-start | bytes 6291456 | tf_op jit(solution)/shard_map/all_to_all | solution.py:63
  161.5 2.1 pick.3
  163.7 1.4 collective-permute-start.13
  165.0 1.3 collective-permute-start.14
  166.4 4.0 %collective-permute-done.14.came_next = bf16[4,3,128,128]{3,2,1,0:T(8,128)(2,1)S(1)} collective-permute-done((bf16[4,3,128,128]{3,2,1,0:T(8,128)(2,1)S(1)}, bf16[4,3,128,128]{3,2,1,0:T(8,128)(2,1)S(1)}, u32[]{:S(2)}, u32[]{:S(2)}) %collective-permute-start.14) | collective-permute-done | bytes 393248 | tf_op jit(solution)/shard_map/ppermute | solution.py:25
  170.3 36.4 %attend.3 = (bf16[8,3,256,128]{3,2,1,0:T(8,128)(2,1)S(1)}, f32[3,16,128,128]{3,2,1,0:T(8,128)S(1)}, bf16[4,3,128,128]{3,2,1,0:T(8,128)(2,1)S(1)}, bf16[4,3,128,128]{3,2,1,0:T(8,128)(2,1)S(1)}) custom-call(s32[1]{0:T(128)} %bitcast.me, s32[3,16,8]{2,1,0:T(8,128)S(1)} %get-tuple-element.80.lists, ...), custom_call_target="tpu_custom_call" | custom-call | tf_op jit(solution)/shard_map/attend/pallas_call | solution.py:459
  206.7 1.3 collective-permute-start.15
  208.0 9.0 %collective-permute-start.16 = (bf16[4,3,128,128]{3,2,1,0:T(8,128)(2,1)S(1)}, bf16[4,3,128,128]{3,2,1,0:T(8,128)(2,1)S(1)}, u32[]{:S(2)}, u32[]{:S(2)}) collective-permute-start(bf16[4,3,128,128]{3,2,1,0:T(8,128)(2,1)S(1)} %get-tuple-element.63), channel_id=1, source_target_pairs={{0,8},{8,16},{16,24},{1,9},{9,17},{17,25},{2,10},{10,18},{18,26},{... | collective-permute-start | bytes 1179656 | tf_op jit(solution)/shard_map/ppermute | solution.py:25
  217.1 1.1 collective-permute-done.16.earlier
  218.2 2.6 finish.3
  220.8 2.4 collective-permute-start.17
  223.8 3.9 %collective-permute-start.19 = (bf16[3,2,256,128]{3,2,1,0:T(8,128)(2,1)}, bf16[3,2,256,128]{3,2,1,0:T(8,128)(2,1)}, u32[]{:S(2)}, u32[]{:S(2)}) collective-permute-start(bf16[3,2,256,128]{3,2,1,0:T(8,128)(2,1)} %get-tuple-element.66), channel_id=1, source_target_pairs={{0,5},{1,4},{2,7},{3,6},{4,1},{5,0},{6,3},{7,2},{8,13},{9,12},{10,... | collective-permute-start | bytes 1179656 | tf_op jit(solution)/shard_map/ppermute | solution.py:68
  227.9 2.0 collective-permute-start.21
  230.0 48.5 %collective-permute-done.17.refs_1_ = bf16[3,2,256,128]{3,2,1,0:T(8,128)(2,1)S(1)} collective-permute-done((bf16[3,2,256,128]{3,2,1,0:T(8,128)(2,1)}, bf16[3,2,256,128]{3,2,1,0:T(8,128)(2,1)S(1)}, u32[]{:S(2)}, u32[]{:S(2)}) %collective-permute-start.17) | collective-permute-done | bytes 393248 | tf_op jit(solution)/shard_map/ppermute | solution.py:68
  278.5 8.2 %collective-permute-done.18.refs_2_ = bf16[3,2,256,128]{3,2,1,0:T(8,128)(2,1)S(1)} collective-permute-done((bf16[3,2,256,128]{3,2,1,0:T(8,128)(2,1)}, bf16[3,2,256,128]{3,2,1,0:T(8,128)(2,1)S(1)}, u32[]{:S(2)}, u32[]{:S(2)}) %collective-permute-start.18) | collective-permute-done | bytes 393248 | tf_op jit(solution)/shard_map/ppermute | solution.py:68
  286.7 0.7 copy-done.9
  287.4 0.8 collective-permute-start.23
  288.2 1.6 copy-done
  289.8 3.0 unpack.2
  292.9 7.6 %collective-permute-done.20.refs_4_ = bf16[3,2,256,128]{3,2,1,0:T(8,128)(2,1)} collective-permute-done((bf16[3,2,256,128]{3,2,1,0:T(8,128)(2,1)}, bf16[3,2,256,128]{3,2,1,0:T(8,128)(2,1)}, u32[]{:S(2)}, u32[]{:S(2)}) %collective-permute-start.20) | collective-permute-done | bytes 393248 | tf_op jit(solution)/shard_map/ppermute | solution.py:68
  300.5 2.0 collective-permute-done.22.refs_6_
  302.5 4.9 %unpack.3 = (bf16[256,3072]{1,0:T(8,128)(2,1)}, bf16[256,3072]{1,0:T(8,128)(2,1)}, bf16[256,3072]{1,0:T(8,128)(2,1)}, bf16[256,3072]{1,0:T(8,128)(2,1)}) custom-call(s32[1]{0:T(128)} %bitcast.me, bf16[8,3,2,256,128]{4,3,2,1,0:T(8,128)(2,1)} %copy-done, ...), custom_call_target="tpu_custom_call", output_to_operand_aliasing={{0}: (10, {}), {1}: (11, {}), {2}: (12, {}), {3}: (13, {})} | custom-call | tf_op jit(solution)/shard_map/unpack/pallas_call | solution.py:241
  (55 shorter events, 3.6 us)
Async XLA Ops:
  0.6 7.0 %copy-start.10 = (s32[6,16,8]{1,2,0:T(8,128)S(1)}, s32[6,16,8]{1,2,0:T(8,128)}, u32[]{:S(2)}) copy-start(s32[6,16,8]{1,2,0:T(8,128)} %param.9) | copy-start | bytes 9220
  4.6 51.9 %collective-permute-start.2 = (bf16[3,2,256,128]{3,2,1,0:T(8,128)(2,1)}, bf16[3,2,256,128]{3,2,1,0:T(8,128)(2,1)S(1)}, u32[]{:S(2)}, u32[]{:S(2)}) collective-permute-start(bf16[3,2,256,128]{3,2,1,0:T(8,128)(2,1)} %get-tuple-element.44), channel_id=1, source_target_pairs={{0,7},{1,6},{2,5},{3,4},{4,3},{5,2},{6,1},{7,0},{8,15},{9,14},{10,... | collective-permute-start | bytes 1179656 | tf_op jit(solution)/shard_map/ppermute | solution.py:68
  7.1 56.7 %collective-permute-start.3 = (bf16[3,2,256,128]{3,2,1,0:T(8,128)(2,1)}, bf16[3,2,256,128]{3,2,1,0:T(8,128)(2,1)S(1)}, u32[]{:S(2)}, u32[]{:S(2)}) collective-permute-start(bf16[3,2,256,128]{3,2,1,0:T(8,128)(2,1)} %get-tuple-element.45), channel_id=1, source_target_pairs={{0,6},{1,7},{2,4},{3,5},{4,2},{5,3},{6,0},{7,1},{8,14},{9,15},{10,... | collective-permute-start | bytes 1179656 | tf_op jit(solution)/shard_map/ppermute | solution.py:68
  9.3 10.1 %collective-permute-start = (s32[4]{0:T(128)S(1)}, s32[4]{0:T(128)S(1)}, u32[]{:S(2)}, u32[]{:S(2)}) collective-permute-start(s32[4]{0:T(128)S(1)} %get-tuple-element.83), channel_id=1, source_target_pairs={{8,0},{16,8},{24,16},{9,1},{17,9},{25,17},{10,2},{18,10},{26,18},{... | collective-permute-start | bytes 56 | tf_op jit(solution)/shard_map/ppermute | solution.py:25
  11.9 7.6 %collective-permute-start.1 = (s32[4]{0:T(128)S(1)}, s32[4]{0:T(128)S(1)}, u32[]{:S(2)}, u32[]{:S(2)}) collective-permute-start(s32[4]{0:T(128)S(1)} %get-tuple-element.85), channel_id=1, source_target_pairs={{0,8},{8,16},{16,24},{1,9},{9,17},{17,25},{2,10},{10,18},{18,26},{... | collective-permute-start | bytes 56 | tf_op jit(solution)/shard_map/ppermute | solution.py:25
  14.9 56.5 %collective-permute-start.4 = (bf16[3,2,256,128]{3,2,1,0:T(8,128)(2,1)}, bf16[3,2,256,128]{3,2,1,0:T(8,128)(2,1)S(1)}, u32[]{:S(2)}, u32[]{:S(2)}) collective-permute-start(bf16[3,2,256,128]{3,2,1,0:T(8,128)(2,1)} %get-tuple-element.46), channel_id=1, source_target_pairs={{0,5},{1,4},{2,7},{3,6},{4,1},{5,0},{6,3},{7,2},{8,13},{9,12},{10,... | collective-permute-start | bytes 1179656 | tf_op jit(solution)/shard_map/ppermute | solution.py:68
  19.4 59.4 %collective-permute-start.5 = (bf16[3,2,256,128]{3,2,1,0:T(8,128)(2,1)}, bf16[3,2,256,128]{3,2,1,0:T(8,128)(2,1)S(1)}, u32[]{:S(2)}, u32[]{:S(2)}) collective-permute-start(bf16[3,2,256,128]{3,2,1,0:T(8,128)(2,1)} %get-tuple-element.47), channel_id=1, source_target_pairs={{0,4},{1,5},{2,6},{3,7},{4,0},{5,1},{6,2},{7,3},{8,12},{9,13},{10,... | collective-permute-start | bytes 1179656 | tf_op jit(solution)/shard_map/ppermute | solution.py:68
  19.5 59.2 %collective-permute-start.6 = (bf16[3,2,256,128]{3,2,1,0:T(8,128)(2,1)}, bf16[3,2,256,128]{3,2,1,0:T(8,128)(2,1)S(1)}, u32[]{:S(2)}, u32[]{:S(2)}) collective-permute-start(bf16[3,2,256,128]{3,2,1,0:T(8,128)(2,1)} %get-tuple-element.48), channel_id=1, source_target_pairs={{0,3},{1,2},{2,1},{3,0},{4,7},{5,6},{6,5},{7,4},{8,11},{9,10},{10,... | collective-permute-start | bytes 1179656 | tf_op jit(solution)/shard_map/ppermute | solution.py:68
  56.5 12.3 %copy-start.1 = (bf16[3,2,256,128]{3,2,1,0:T(8,128)(2,1)}, bf16[3,2,256,128]{3,2,1,0:T(8,128)(2,1)S(1)}, u32[]{:S(2)}) copy-start(bf16[3,2,256,128]{3,2,1,0:T(8,128)(2,1)S(1)} %collective-permute-done.2.refs_0_.refs_1_) | copy-start | bytes 1179652
  56.5 23.8 %collective-permute-start.7 = (bf16[3,2,256,128]{3,2,1,0:T(8,128)(2,1)}, bf16[3,2,256,128]{3,2,1,0:T(8,128)(2,1)S(1)}, u32[]{:S(2)}, u32[]{:S(2)}) collective-permute-start(bf16[3,2,256,128]{3,2,1,0:T(8,128)(2,1)} %get-tuple-element.49), channel_id=1, source_target_pairs={{0,2},{1,3},{2,0},{3,1},{4,6},{5,7},{6,4},{7,5},{8,10},{9,11},{10,... | collective-permute-start | bytes 1179656 | tf_op jit(solution)/shard_map/ppermute | solution.py:68
  63.8 4.9 %copy-start.2 = (bf16[3,2,256,128]{3,2,1,0:T(8,128)(2,1)}, bf16[3,2,256,128]{3,2,1,0:T(8,128)(2,1)S(1)}, u32[]{:S(2)}) copy-start(bf16[3,2,256,128]{3,2,1,0:T(8,128)(2,1)S(1)} %collective-permute-done.3.refs_1_.refs_2_) | copy-start | bytes 1179652
  63.8 16.5 %collective-permute-start.8 = (bf16[3,2,256,128]{3,2,1,0:T(8,128)(2,1)}, bf16[3,2,256,128]{3,2,1,0:T(8,128)(2,1)S(1)}, u32[]{:S(2)}, u32[]{:S(2)}) collective-permute-start(bf16[3,2,256,128]{3,2,1,0:T(8,128)(2,1)} %get-tuple-element.50), channel_id=1, source_target_pairs={{0,1},{1,0},{2,3},{3,2},{4,5},{5,4},{6,7},{7,6},{8,9},{9,8},{10,11... | collective-permute-start | bytes 1179656 | tf_op jit(solution)/shard_map/ppermute | solution.py:68
  71.4 8.9 %copy-start.3 = (bf16[3,2,256,128]{3,2,1,0:T(8,128)(2,1)}, bf16[3,2,256,128]{3,2,1,0:T(8,128)(2,1)S(1)}, u32[]{:S(2)}) copy-start(bf16[3,2,256,128]{3,2,1,0:T(8,128)(2,1)S(1)} %collective-permute-done.4.refs_2_.refs_3_) | copy-start | bytes 1179652
  78.7 1.6 copy-start.4
  78.7 1.6 copy-start.5
  80.3 0.8 copy-start.6
  81.1 0.7 copy-start.7
  81.8 73.5 %all-to-all-start.1 = ((bf16[8,3,2,256,128]{4,3,2,1,0:T(8,128)(2,1)}), bf16[8,3,2,256,128]{4,3,2,1,0:T(8,128)(2,1)}, u32[]{:S(2)}, u32[]{:S(2)}) async-start(bf16[8,3,2,256,128]{4,3,2,1,0:T(8,128)(2,1)} %hold.1), calls=%async_computation.1 | async-start | bytes 6291456 | tf_op jit(solution)/shard_map/all_to_all | solution.py:63
  90.7 2.6 collective-permute-start.9
  92.0 5.3 %collective-permute-start.10 = (bf16[4,3,128,128]{3,2,1,0:T(8,128)(2,1)S(1)}, bf16[4,3,128,128]{3,2,1,0:T(8,128)(2,1)S(1)}, u32[]{:S(2)}, u32[]{:S(2)}) collective-permute-start(bf16[4,3,128,128]{3,2,1,0:T(8,128)(2,1)S(1)} %get-tuple-element.53), channel_id=1, source_target_pairs={{8,0},{16,8},{24,16},{9,1},{17,9},{25,17},{10,2},{18,10},{26,18},{... | collective-permute-start | bytes 1179656 | tf_op jit(solution)/shard_map/ppermute | solution.py:25
  133.7 10.4 %collective-permute-start.11 = (bf16[4,3,128,128]{3,2,1,0:T(8,128)(2,1)S(1)}, bf16[4,3,128,128]{3,2,1,0:T(8,128)(2,1)S(1)}, u32[]{:S(2)}, u32[]{:S(2)}) collective-permute-start(bf16[4,3,128,128]{3,2,1,0:T(8,128)(2,1)S(1)} %get-tuple-element.56), channel_id=1, source_target_pairs={{8,0},{16,8},{24,16},{9,1},{17,9},{25,17},{10,2},{18,10},{26,18},{... | collective-permute-start | bytes 1179656 | tf_op jit(solution)/shard_map/ppermute | solution.py:25
  135.0 10.4 %collective-permute-start.12 = (bf16[4,3,128,128]{3,2,1,0:T(8,128)(2,1)S(1)}, bf16[4,3,128,128]{3,2,1,0:T(8,128)(2,1)S(1)}, u32[]{:S(2)}, u32[]{:S(2)}) collective-permute-start(bf16[4,3,128,128]{3,2,1,0:T(8,128)(2,1)S(1)} %get-tuple-element.57), channel_id=1, source_target_pairs={{0,8},{8,16},{16,24},{1,9},{9,17},{17,25},{2,10},{10,18},{18,26},{... | collective-permute-start | bytes 1179656 | tf_op jit(solution)/shard_map/ppermute | solution.py:25
  155.4 132.8 %all-to-all-start = ((bf16[8,3,2,256,128]{4,3,2,1,0:T(8,128)(2,1)}), bf16[8,3,2,256,128]{4,3,2,1,0:T(8,128)(2,1)S(1)}, u32[]{:S(2)}, u32[]{:S(2)}) async-start(bf16[8,3,2,256,128]{4,3,2,1,0:T(8,128)(2,1)} %finish.2.refs_1_), calls=%async_computation | async-start | bytes 6291456 | tf_op jit(solution)/shard_map/all_to_all | solution.py:63
  163.7 2.7 collective-permute-start.13
  165.0 5.3 %collective-permute-start.14 = (bf16[4,3,128,128]{3,2,1,0:T(8,128)(2,1)S(1)}, bf16[4,3,128,128]{3,2,1,0:T(8,128)(2,1)S(1)}, u32[]{:S(2)}, u32[]{:S(2)}) collective-permute-start(bf16[4,3,128,128]{3,2,1,0:T(8,128)(2,1)S(1)} %get-tuple-element.59), channel_id=1, source_target_pairs={{8,0},{16,8},{24,16},{9,1},{17,9},{25,17},{10,2},{18,10},{26,18},{... | collective-permute-start | bytes 1179656 | tf_op jit(solution)/shard_map/ppermute | solution.py:25
  206.7 10.3 %collective-permute-start.15 = (bf16[4,3,128,128]{3,2,1,0:T(8,128)(2,1)S(1)}, bf16[4,3,128,128]{3,2,1,0:T(8,128)(2,1)S(1)}, u32[]{:S(2)}, u32[]{:S(2)}) collective-permute-start(bf16[4,3,128,128]{3,2,1,0:T(8,128)(2,1)S(1)} %get-tuple-element.62), channel_id=1, source_target_pairs={{8,0},{16,8},{24,16},{9,1},{17,9},{25,17},{10,2},{18,10},{26,18},{... | collective-permute-start | bytes 1179656 | tf_op jit(solution)/shard_map/ppermute | solution.py:25
  208.0 10.1 %collective-permute-start.16 = (bf16[4,3,128,128]{3,2,1,0:T(8,128)(2,1)S(1)}, bf16[4,3,128,128]{3,2,1,0:T(8,128)(2,1)S(1)}, u32[]{:S(2)}, u32[]{:S(2)}) collective-permute-start(bf16[4,3,128,128]{3,2,1,0:T(8,128)(2,1)S(1)} %get-tuple-element.63), channel_id=1, source_target_pairs={{0,8},{8,16},{16,24},{1,9},{9,17},{17,25},{2,10},{10,18},{18,26},{... | collective-permute-start | bytes 1179656 | tf_op jit(solution)/shard_map/ppermute | solution.py:25
  220.8 57.7 %collective-permute-start.17 = (bf16[3,2,256,128]{3,2,1,0:T(8,128)(2,1)}, bf16[3,2,256,128]{3,2,1,0:T(8,128)(2,1)S(1)}, u32[]{:S(2)}, u32[]{:S(2)}) collective-permute-start(bf16[3,2,256,128]{3,2,1,0:T(8,128)(2,1)} %get-tuple-element.64), channel_id=1, source_target_pairs={{0,7},{1,6},{2,5},{3,4},{4,3},{5,2},{6,1},{7,0},{8,15},{9,14},{10,... | collective-permute-start | bytes 1179656 | tf_op jit(solution)/shard_map/ppermute | solution.py:68
  223.2 63.5 %collective-permute-start.18 = (bf16[3,2,256,128]{3,2,1,0:T(8,128)(2,1)}, bf16[3,2,256,128]{3,2,1,0:T(8,128)(2,1)S(1)}, u32[]{:S(2)}, u32[]{:S(2)}) collective-permute-start(bf16[3,2,256,128]{3,2,1,0:T(8,128)(2,1)} %get-tuple-element.65), channel_id=1, source_target_pairs={{0,6},{1,7},{2,4},{3,5},{4,2},{5,3},{6,0},{7,1},{8,14},{9,15},{10,... | collective-permute-start | bytes 1179656 | tf_op jit(solution)/shard_map/ppermute | solution.py:68
  223.8 69.1 %collective-permute-start.19 = (bf16[3,2,256,128]{3,2,1,0:T(8,128)(2,1)}, bf16[3,2,256,128]{3,2,1,0:T(8,128)(2,1)}, u32[]{:S(2)}, u32[]{:S(2)}) collective-permute-start(bf16[3,2,256,128]{3,2,1,0:T(8,128)(2,1)} %get-tuple-element.66), channel_id=1, source_target_pairs={{0,5},{1,4},{2,7},{3,6},{4,1},{5,0},{6,3},{7,2},{8,13},{9,12},{10,... | collective-permute-start | bytes 1179656 | tf_op jit(solution)/shard_map/ppermute | solution.py:68
  227.6 72.9 %collective-permute-start.20 = (bf16[3,2,256,128]{3,2,1,0:T(8,128)(2,1)}, bf16[3,2,256,128]{3,2,1,0:T(8,128)(2,1)}, u32[]{:S(2)}, u32[]{:S(2)}) collective-permute-start(bf16[3,2,256,128]{3,2,1,0:T(8,128)(2,1)} %get-tuple-element.67), channel_id=1, source_target_pairs={{0,4},{1,5},{2,6},{3,7},{4,0},{5,1},{6,2},{7,3},{8,12},{9,13},{10,... | collective-permute-start | bytes 1179656 | tf_op jit(solution)/shard_map/ppermute | solution.py:68
  227.9 72.6 %collective-permute-start.21 = (bf16[3,2,256,128]{3,2,1,0:T(8,128)(2,1)}, bf16[3,2,256,128]{3,2,1,0:T(8,128)(2,1)}, u32[]{:S(2)}, u32[]{:S(2)}) collective-permute-start(bf16[3,2,256,128]{3,2,1,0:T(8,128)(2,1)} %get-tuple-element.68), channel_id=1, source_target_pairs={{0,3},{1,2},{2,1},{3,0},{4,7},{5,6},{6,5},{7,4},{8,11},{9,10},{10,... | collective-permute-start | bytes 1179656 | tf_op jit(solution)/shard_map/ppermute | solution.py:68
  278.5 24.0 %copy-start.8 = (bf16[3,2,256,128]{3,2,1,0:T(8,128)(2,1)}, bf16[3,2,256,128]{3,2,1,0:T(8,128)(2,1)S(1)}, u32[]{:S(2)}) copy-start(bf16[3,2,256,128]{3,2,1,0:T(8,128)(2,1)S(1)} %collective-permute-done.17.refs_1_) | copy-start | bytes 1179652
  278.5 24.0 %collective-permute-start.22 = (bf16[3,2,256,128]{3,2,1,0:T(8,128)(2,1)}, bf16[3,2,256,128]{3,2,1,0:T(8,128)(2,1)}, u32[]{:S(2)}, u32[]{:S(2)}) collective-permute-start(bf16[3,2,256,128]{3,2,1,0:T(8,128)(2,1)} %get-tuple-element.69), channel_id=1, source_target_pairs={{0,2},{1,3},{2,0},{3,1},{4,6},{5,7},{6,4},{7,5},{8,10},{9,11},{10,... | collective-permute-start | bytes 1179656 | tf_op jit(solution)/shard_map/ppermute | solution.py:68
  286.7 0.7 copy-start.9
  287.4 15.1 %collective-permute-start.23 = (bf16[3,2,256,128]{3,2,1,0:T(8,128)(2,1)}, bf16[3,2,256,128]{3,2,1,0:T(8,128)(2,1)}, u32[]{:S(2)}, u32[]{:S(2)}) collective-permute-start(bf16[3,2,256,128]{3,2,1,0:T(8,128)(2,1)} %get-tuple-element.70), channel_id=1, source_target_pairs={{0,1},{1,0},{2,3},{3,2},{4,5},{5,4},{6,7},{7,6},{8,9},{9,8},{10,11... | collective-permute-start | bytes 1179656 | tf_op jit(solution)/shard_map/ppermute | solution.py:68
  288.2 1.6 copy-start

commit v9 on v8

--- a/solution.py
+++ b/solution.py
@@ -26,9 +26,12 @@
 
 
 def part_of(messages, me, item):
-    if len(messages) == 1:
+    far = len(messages) - 1
+    if far == 0:
         return messages[0].at[item], item
-    return messages[item], me[0] ^ (len(messages) - 1 - item)
+    if item < far:
+        return messages[item], me[0] ^ (2 * far - 1 - item)
+    return messages[far].at[item - far], lax.div(me[0], far) * far + item - far
 
 
 def message_shape(messages):
@@ -37,7 +40,8 @@
 
 def message_outs(peers, shape, dtype, apart):
     if apart:
-        return [pltpu.HBM(shape, dtype)] * peers
+        far = peers // 2
+        return [pltpu.HBM(shape, dtype)] * far + [pltpu.HBM((far,) + shape, dtype)]
     return [pltpu.HBM((peers,) + shape, dtype)]
 
 
@@ -59,20 +63,30 @@
 
 
 def exchange(messages):
-    if len(messages) == 1:
+    far = len(messages) - 1
+    if far == 0:
         return [lax.all_to_all(messages[0], "seq", split_axis=0, concat_axis=0, tiled=True)]
-    count = len(messages)
-    received = list(messages)
-    for item in range(count - 1):
-        pairs = [(i, i ^ (count - 1 - item)) for i in range(count)]
-        received[item] = lax.ppermute(messages[item], "seq", pairs)
-    return received
+    peers = range(2 * far)
+    received = [
+        lax.ppermute(messages[item], "seq", [(i, i ^ (2 * far - 1 - item)) for i in peers])
+        for item in range(far)
+    ]
+    halves = [list(peers[:far]), list(peers[far:])]
+    near = lax.all_to_all(
+        messages[far],
+        "seq",
+        split_axis=0,
+        concat_axis=0,
+        axis_index_groups=halves,
+        tiled=True,
+    )
+    return received + [near]
 
 
 def pack_kernel(
     me, query, key, value, d_out, *refs, first, heads, peers, apart, per_peer, head_dim
 ):
-    messages = refs[-4 - (peers if apart else 1) : -4]
+    messages = refs[-4 - (peers // 2 + 1 if apart else 1) : -4]
     stage, ready, in_sems, out_sems = refs[-4:]
     sources = (key, value, query, d_out)
     aligned = apart and per_peer % LANES == 0
@@ -589,7 +603,7 @@
             me, arrays, start, size, heads_here, peers, head_dim, chunk == 0, after
         )
         if chunk == 1:
-            packed = hold(packed, came[0][:-1])
+            packed = hold(packed, came[0][: peers // 4])
         came.append(exchange(packed))
     received = []
     outs = finished = ()

time: 312 us -> 390 us (1.25)
  waiting for transfers between devices: 138 us -> 209 us
  starting transfers between devices: 63 us -> 69.6 us
    ppermute x14 -> x8, waiting for transfers between devices: 121 us -> 196 us  [exchange(): lax.ppermute(messages[item], 'seq', [(i, i ^ 2 * far - 1 - item) for i in...]
    all_to_all x0 -> x2, starting transfers between devices: none -> 10 us  [exchange(): lax.all_to_all(messages[far], 'seq', split_axis=0, concat_axis=0, axis_in...]
    ppermute x14 -> x8, starting transfers between devices: 19.8 us -> 14.4 us  [exchange(): lax.ppermute(messages[item], 'seq', [(i, i ^ 2 * far - 1 - item) for i in...]
    ppermute x10, starting transfers between devices: 30.3 us -> 34.7 us  [from_behind(): return lax.ppermute(x, axis, pairs)]
    all_to_all x2, waiting for transfers between devices: 7.29 us -> 2.93 us  [exchange(): lax.all_to_all(messages[0], 'seq', split_axis=0, concat_axis=0, tiled=True)]
  transfers between devices with their start and end apart: 26 -> 22, of which waited for: 14 -> 13; matrix products, arithmetic and copies ran while one was open for 1% -> 1% of each run, Pallas kernels for 29% -> 23%
where the time goes in v9:
time: 390 us; the launch traced here: 387 us
  waiting for transfers between devices  209 us (54%)
  Pallas kernels  97.8 us (25%)
  starting transfers between devices  69.6 us (18%)
  local copies, waits for them, and re-layouts  7 us (2%)
    ppermute x8, waiting for transfers between devices, exchange(): lax.ppermute(messages[item], 'seq', [(i, i ^ 2 * far - 1 - item) for i in...  196 us
    pallas_call x2, Pallas kernels, attend(): pl.pallas_call(functools.partial(attend_kernel, block_rows=block_rows, he...  72.8 us
    ppermute x10, starting transfers between devices, from_behind(): return lax.ppermute(x, axis, pairs)  34.7 us
    ppermute x8, starting transfers between devices, exchange(): lax.ppermute(messages[item], 'seq', [(i, i ^ 2 * far - 1 - item) for i in...  14.4 us
    all_to_all x2, starting transfers between devices, exchange(): lax.all_to_all(messages[0], 'seq', split_axis=0, concat_axis=0, tiled=True)  10.5 us
    all_to_all x2, starting transfers between devices, exchange(): lax.all_to_all(messages[far], 'seq', split_axis=0, concat_axis=0, axis_in...  10 us
    ppermute x10, waiting for transfers between devices, from_behind(): return lax.ppermute(x, axis, pairs)  9.74 us
  transfers between devices with their start and end apart: 22, of which 13 were waited for; matrix products, arithmetic and copies ran while one was open for 1% of the time, Pallas kernels for 23%

profile of v9, /device:TPU:8, one launch (start us, length us, event | category | flops | bytes accessed | tf_op | source)
XLA Modules:
  0.0 387.4 jit_solution(6759729628090773389)
XLA Ops:
  0.6 3.9 %pack.2 = (bf16[3,2,256,128]{3,2,1,0:T(8,128)(2,1)}, bf16[3,2,256,128]{3,2,1,0:T(8,128)(2,1)}, bf16[3,2,256,128]{3,2,1,0:T(8,128)(2,1)}, bf16[3,2,256,128]{3,2,1,0:T(8,128)(2,1)}, bf16[4,3,2,256,128]{4,3,2,1,0:T(8,128)(2,1)}) custom-call(s32[1]{0:T(128)} %bitcast.me, bf16[256,3072]{1,0:T(8,128)(2,1)} %query.3, bf16[256,3072]{1,0:T(8,128)(2,1)} %key.3, ...), custom_call_target="tpu_custom_call" | custom-call | tf_op jit(solution)/shard_map/pack/pallas_call | solution.py:149
  4.6 4.4 %all-to-all-start = ((bf16[4,3,2,256,128]{4,3,2,1,0:T(8,128)(2,1)}), bf16[4,3,2,256,128]{4,3,2,1,0:T(8,128)(2,1)S(1)}, u32[]{:S(2)}, u32[]{:S(2)}) async-start(bf16[4,3,2,256,128]{4,3,2,1,0:T(8,128)(2,1)} %get-tuple-element.42), calls=%async_computation | async-start | bytes 3145728 | tf_op jit(solution)/shard_map/all_to_all | solution.py:75
  9.3 1.3 top_k.17
  10.6 1.3 collective-permute-start
  11.9 1.3 top_k.24
  13.2 3.0 collective-permute-start.1
  16.2 2.7 collective-permute-start.2
  19.6 3.9 %pack.3.refs_0_ = bf16[8,3,2,256,128]{4,3,2,1,0:T(8,128)(2,1)} custom-call(s32[1]{0:T(128)} %bitcast.me, bf16[256,3072]{1,0:T(8,128)(2,1)} %query.3, bf16[256,3072]{1,0:T(8,128)(2,1)} %key.3, bf16[256,3072]{1,0:T(8,128)(2,1)} %value.3, bf16[256,3072]{1,0:T(8,128)(2,1)} %d_out.3, s32[8]{0:T(128)S(1)} %pad_add_fusion.asked.refs_0_, ...), custom_call_target="tpu_custom_call" | custom-call | tf_op jit(solution)/shard_map/pack/pallas_call | solution.py:149
  23.5 21.9 %collective-permute-done.2.refs_0_.refs_1_ = bf16[3,2,256,128]{3,2,1,0:T(8,128)(2,1)S(1)} collective-permute-done((bf16[3,2,256,128]{3,2,1,0:T(8,128)(2,1)}, bf16[3,2,256,128]{3,2,1,0:T(8,128)(2,1)S(1)}, u32[]{:S(2)}, u32[]{:S(2)}) %collective-permute-start.2) | collective-permute-done | bytes 393248 | tf_op jit(solution)/shard_map/ppermute | solution.py:71
  45.4 9.2 %collective-permute-done.3.refs_1_.refs_2_ = bf16[3,2,256,128]{3,2,1,0:T(8,128)(2,1)S(1)} collective-permute-done((bf16[3,2,256,128]{3,2,1,0:T(8,128)(2,1)S(1)}, bf16[3,2,256,128]{3,2,1,0:T(8,128)(2,1)S(1)}, u32[]{:S(2)}, u32[]{:S(2)}) %collective-permute-start.3) | collective-permute-done | bytes 393248 | tf_op jit(solution)/shard_map/ppermute | solution.py:71
  54.5 0.7 copy-done.4
  55.3 1.1 copy-done.2
  56.4 4.4 %all-to-all-start.2 = ((bf16[8,3,2,256,128]{4,3,2,1,0:T(8,128)(2,1)}), bf16[8,3,2,256,128]{4,3,2,1,0:T(8,128)(2,1)S(1)}, u32[]{:S(2)}, u32[]{:S(2)}) async-start(bf16[8,3,2,256,128]{4,3,2,1,0:T(8,128)(2,1)} %hold.1), calls=%async_computation.2 | async-start | bytes 6291456 | tf_op jit(solution)/shard_map/all_to_all | solution.py:68
  60.8 3.3 collective-permute-start.4
  64.6 90.1 %collective-permute-done.4.refs_2_ = bf16[3,2,256,128]{3,2,1,0:T(8,128)(2,1)S(1)} collective-permute-done((bf16[3,2,256,128]{3,2,1,0:T(8,128)(2,1)}, bf16[3,2,256,128]{3,2,1,0:T(8,128)(2,1)S(1)}, u32[]{:S(2)}, u32[]{:S(2)}) %collective-permute-start.4) | collective-permute-done | bytes 393248 | tf_op jit(solution)/shard_map/ppermute | solution.py:71
  154.7 8.3 %collective-permute-done.5.refs_3_ = bf16[3,2,256,128]{3,2,1,0:T(8,128)(2,1)S(1)} collective-permute-done((bf16[3,2,256,128]{3,2,1,0:T(8,128)(2,1)}, bf16[3,2,256,128]{3,2,1,0:T(8,128)(2,1)S(1)}, u32[]{:S(2)}, u32[]{:S(2)}) %collective-permute-start.5) | collective-permute-done | bytes 393248 | tf_op jit(solution)/shard_map/ppermute | solution.py:71
  163.0 0.7 copy-done.6
  163.8 2.1 pick.2
  165.9 1.9 collective-permute-start.6
  167.9 1.3 collective-permute-start.7
  169.2 2.3 collective-permute-done.7.came_next
  171.5 36.4 %attend.2 = (bf16[8,3,256,128]{3,2,1,0:T(8,128)(2,1)S(1)}, f32[3,16,128,128]{3,2,1,0:T(8,128)S(1)}, bf16[4,3,128,128]{3,2,1,0:T(8,128)(2,1)S(1)}, bf16[4,3,128,128]{3,2,1,0:T(8,128)(2,1)S(1)}) custom-call(s32[1]{0:T(128)} %bitcast.me, s32[3,16,8]{2,1,0:T(8,128)S(1)} %get-tuple-element.69.lists, ...), custom_call_target="tpu_custom_call" | custom-call | tf_op jit(solution)/shard_map/attend/pallas_call | solution.py:473
  207.9 1.3 collective-permute-start.8
  209.2 8.0 %collective-permute-start.9 = (bf16[4,3,128,128]{3,2,1,0:T(8,128)(2,1)S(1)}, bf16[4,3,128,128]{3,2,1,0:T(8,128)(2,1)S(1)}, u32[]{:S(2)}, u32[]{:S(2)}) collective-permute-start(bf16[4,3,128,128]{3,2,1,0:T(8,128)(2,1)S(1)} %get-tuple-element.48), channel_id=1, source_target_pairs={{0,8},{8,16},{16,24},{1,9},{9,17},{17,25},{2,10},{10,18},{18,26},{... | collective-permute-start | bytes 1179656 | tf_op jit(solution)/shard_map/ppermute | solution.py:25
  217.2 1.3 collective-permute-done.9.earlier
  218.5 2.6 finish.2.refs_1_
  221.2 1.7 copy-done.1
  222.9 6.1 %all-to-all-start.1 = ((bf16[8,3,2,256,128]{4,3,2,1,0:T(8,128)(2,1)}), bf16[8,3,2,256,128]{4,3,2,1,0:T(8,128)(2,1)S(1)}, u32[]{:S(2)}, u32[]{:S(2)}) async-start(bf16[8,3,2,256,128]{4,3,2,1,0:T(8,128)(2,1)} %finish.2.refs_1_), calls=%async_computation.1 | async-start | bytes 6291456 | tf_op jit(solution)/shard_map/all_to_all | solution.py:68
  229.0 2.1 pick.3
  231.1 6.5 %collective-permute-start.10 = (bf16[4,3,128,128]{3,2,1,0:T(8,128)(2,1)S(1)}, bf16[4,3,128,128]{3,2,1,0:T(8,128)(2,1)S(1)}, u32[]{:S(2)}, u32[]{:S(2)}) collective-permute-start(bf16[4,3,128,128]{3,2,1,0:T(8,128)(2,1)S(1)} %get-tuple-element.49), channel_id=1, source_target_pairs={{0,8},{8,16},{16,24},{1,9},{9,17},{17,25},{2,10},{10,18},{18,26},{... | collective-permute-start | bytes 1179656 | tf_op jit(solution)/shard_map/ppermute | solution.py:25
  237.6 1.3 collective-permute-start.11
  238.9 4.8 %collective-permute-done.11.came_next = bf16[4,3,128,128]{3,2,1,0:T(8,128)(2,1)S(1)} collective-permute-done((bf16[4,3,128,128]{3,2,1,0:T(8,128)(2,1)S(1)}, bf16[4,3,128,128]{3,2,1,0:T(8,128)(2,1)S(1)}, u32[]{:S(2)}, u32[]{:S(2)}) %collective-permute-start.11) | collective-permute-done | bytes 393248 | tf_op jit(solution)/shard_map/ppermute | solution.py:25
  243.7 36.4 %attend.3 = (bf16[8,3,256,128]{3,2,1,0:T(8,128)(2,1)S(1)}, f32[3,16,128,128]{3,2,1,0:T(8,128)S(1)}, bf16[4,3,128,128]{3,2,1,0:T(8,128)(2,1)S(1)}, bf16[4,3,128,128]{3,2,1,0:T(8,128)(2,1)S(1)}) custom-call(s32[1]{0:T(128)} %bitcast.me, s32[3,16,8]{2,1,0:T(8,128)S(1)} %get-tuple-element.68.lists, ...), custom_call_target="tpu_custom_call" | custom-call | tf_op jit(solution)/shard_map/attend/pallas_call | solution.py:473
  280.1 1.3 collective-permute-start.12
  281.4 8.8 %collective-permute-start.13 = (bf16[4,3,128,128]{3,2,1,0:T(8,128)(2,1)S(1)}, bf16[4,3,128,128]{3,2,1,0:T(8,128)(2,1)S(1)}, u32[]{:S(2)}, u32[]{:S(2)}) collective-permute-start(bf16[4,3,128,128]{3,2,1,0:T(8,128)(2,1)S(1)} %get-tuple-element.54), channel_id=1, source_target_pairs={{0,8},{8,16},{16,24},{1,9},{9,17},{17,25},{2,10},{10,18},{18,26},{... | collective-permute-start | bytes 1179656 | tf_op jit(solution)/shard_map/ppermute | solution.py:25
  290.3 1.3 collective-permute-done.13.earlier
  291.6 2.6 finish.3
  294.2 2.9 all-to-all-done.1.refs_0_
  297.1 1.6 copy-done
  298.7 5.6 %all-to-all-start.3 = ((bf16[4,3,2,256,128]{4,3,2,1,0:T(8,128)(2,1)}), bf16[4,3,2,256,128]{4,3,2,1,0:T(8,128)(2,1)}, u32[]{:S(2)}, u32[]{:S(2)}) async-start(bf16[4,3,2,256,128]{4,3,2,1,0:T(8,128)(2,1)} %get-tuple-element.59), calls=%async_computation.3 | async-start | bytes 3145728 | tf_op jit(solution)/shard_map/all_to_all | solution.py:75
  304.4 2.4 collective-permute-start.14
  307.3 4.2 %collective-permute-start.16 = (bf16[3,2,256,128]{3,2,1,0:T(8,128)(2,1)}, bf16[3,2,256,128]{3,2,1,0:T(8,128)(2,1)S(1)}, u32[]{:S(2)}, u32[]{:S(2)}) collective-permute-start(bf16[3,2,256,128]{3,2,1,0:T(8,128)(2,1)} %get-tuple-element.57), channel_id=1, source_target_pairs={{0,5},{1,4},{2,7},{3,6},{4,1},{5,0},{6,3},{7,2},{8,13},{9,12},{10,... | collective-permute-start | bytes 1179656 | tf_op jit(solution)/shard_map/ppermute | solution.py:71
  312.0 3.0 unpack.2
  315.0 8.4 %collective-permute-done.14.refs_1_ = bf16[3,2,256,128]{3,2,1,0:T(8,128)(2,1)S(1)} collective-permute-done((bf16[3,2,256,128]{3,2,1,0:T(8,128)(2,1)}, bf16[3,2,256,128]{3,2,1,0:T(8,128)(2,1)S(1)}, u32[]{:S(2)}, u32[]{:S(2)}) %collective-permute-start.14) | collective-permute-done | bytes 393248 | tf_op jit(solution)/shard_map/ppermute | solution.py:71
  323.4 41.6 %collective-permute-done.15.refs_2_ = bf16[3,2,256,128]{3,2,1,0:T(8,128)(2,1)S(1)} collective-permute-done((bf16[3,2,256,128]{3,2,1,0:T(8,128)(2,1)}, bf16[3,2,256,128]{3,2,1,0:T(8,128)(2,1)S(1)}, u32[]{:S(2)}, u32[]{:S(2)}) %collective-permute-start.15) | collective-permute-done | bytes 393248 | tf_op jit(solution)/shard_map/ppermute | solution.py:71
  365.0 8.4 %collective-permute-done.16.refs_3_ = bf16[3,2,256,128]{3,2,1,0:T(8,128)(2,1)S(1)} collective-permute-done((bf16[3,2,256,128]{3,2,1,0:T(8,128)(2,1)}, bf16[3,2,256,128]{3,2,1,0:T(8,128)(2,1)S(1)}, u32[]{:S(2)}, u32[]{:S(2)}) %collective-permute-start.16) | collective-permute-done | bytes 393248 | tf_op jit(solution)/shard_map/ppermute | solution.py:71
  373.5 8.3 %collective-permute-done.17.refs_4_ = bf16[3,2,256,128]{3,2,1,0:T(8,128)(2,1)S(1)} collective-permute-done((bf16[3,2,256,128]{3,2,1,0:T(8,128)(2,1)S(1)}, bf16[3,2,256,128]{3,2,1,0:T(8,128)(2,1)S(1)}, u32[]{:S(2)}, u32[]{:S(2)}) %collective-permute-start.17) | collective-permute-done | bytes 393248 | tf_op jit(solution)/shard_map/ppermute | solution.py:71
  382.5 4.7 %unpack.3 = (bf16[256,3072]{1,0:T(8,128)(2,1)}, bf16[256,3072]{1,0:T(8,128)(2,1)}, bf16[256,3072]{1,0:T(8,128)(2,1)}, bf16[256,3072]{1,0:T(8,128)(2,1)}) custom-call(s32[1]{0:T(128)} %bitcast.me, bf16[8,3,2,256,128]{4,3,2,1,0:T(8,128)(2,1)} %copy-done, ...), custom_call_target="tpu_custom_call", output_to_operand_aliasing={{0}: (7, {}), {1}: (8, {}), {2}: (9, {}), {3}: (10, {})} | custom-call | tf_op jit(solution)/shard_map/unpack/pallas_call | solution.py:255
  (53 shorter events, 3.3 us)
Async XLA Ops:
  4.5 4.4 %copy-start.11 = (s32[6,16,8]{1,2,0:T(8,128)S(1)}, s32[6,16,8]{1,2,0:T(8,128)}, u32[]{:S(2)}) copy-start(s32[6,16,8]{1,2,0:T(8,128)} %param.9) | copy-start | bytes 9220
  4.5 14.3 %copy-start.12 = (bf16[3,2,256,128]{3,2,1,0:T(8,128)(2,1)S(1)}, bf16[3,2,256,128]{3,2,1,0:T(8,128)(2,1)}, u32[]{:S(2)}) copy-start(bf16[3,2,256,128]{3,2,1,0:T(8,128)(2,1)} %get-tuple-element.39) | copy-start | bytes 1179652
  4.6 50.7 %all-to-all-start = ((bf16[4,3,2,256,128]{4,3,2,1,0:T(8,128)(2,1)}), bf16[4,3,2,256,128]{4,3,2,1,0:T(8,128)(2,1)S(1)}, u32[]{:S(2)}, u32[]{:S(2)}) async-start(bf16[4,3,2,256,128]{4,3,2,1,0:T(8,128)(2,1)} %get-tuple-element.42), calls=%async_computation | async-start | bytes 3145728 | tf_op jit(solution)/shard_map/all_to_all | solution.py:75
  10.6 8.9 %collective-permute-start = (s32[4]{0:T(128)S(1)}, s32[4]{0:T(128)S(1)}, u32[]{:S(2)}, u32[]{:S(2)}) collective-permute-start(s32[4]{0:T(128)S(1)} %get-tuple-element.71), channel_id=1, source_target_pairs={{8,0},{16,8},{24,16},{9,1},{17,9},{25,17},{10,2},{18,10},{26,18},{... | collective-permute-start | bytes 56 | tf_op jit(solution)/shard_map/ppermute | solution.py:25
  13.2 6.3 %collective-permute-start.1 = (s32[4]{0:T(128)S(1)}, s32[4]{0:T(128)S(1)}, u32[]{:S(2)}, u32[]{:S(2)}) collective-permute-start(s32[4]{0:T(128)S(1)} %get-tuple-element.73), channel_id=1, source_target_pairs={{0,8},{8,16},{16,24},{1,9},{9,17},{17,25},{2,10},{10,18},{18,26},{... | collective-permute-start | bytes 56 | tf_op jit(solution)/shard_map/ppermute | solution.py:25
  16.2 29.2 %collective-permute-start.2 = (bf16[3,2,256,128]{3,2,1,0:T(8,128)(2,1)}, bf16[3,2,256,128]{3,2,1,0:T(8,128)(2,1)S(1)}, u32[]{:S(2)}, u32[]{:S(2)}) collective-permute-start(bf16[3,2,256,128]{3,2,1,0:T(8,128)(2,1)} %get-tuple-element.38), channel_id=1, source_target_pairs={{0,7},{1,6},{2,5},{3,4},{4,3},{5,2},{6,1},{7,0},{8,15},{9,14},{10,... | collective-permute-start | bytes 1179656 | tf_op jit(solution)/shard_map/ppermute | solution.py:71
  18.9 35.7 %collective-permute-start.3 = (bf16[3,2,256,128]{3,2,1,0:T(8,128)(2,1)S(1)}, bf16[3,2,256,128]{3,2,1,0:T(8,128)(2,1)S(1)}, u32[]{:S(2)}, u32[]{:S(2)}) collective-permute-start(bf16[3,2,256,128]{3,2,1,0:T(8,128)(2,1)S(1)} %copy-done.12), channel_id=1, source_target_pairs={{0,6},{1,7},{2,4},{3,5},{4,2},{5,3},{6,0},{7,1},{8,14},{9,15},{10,... | collective-permute-start | bytes 1179656 | tf_op jit(solution)/shard_map/ppermute | solution.py:71
  45.4 9.2 %copy-start.3 = (bf16[3,2,256,128]{3,2,1,0:T(8,128)(2,1)}, bf16[3,2,256,128]{3,2,1,0:T(8,128)(2,1)S(1)}, u32[]{:S(2)}) copy-start(bf16[3,2,256,128]{3,2,1,0:T(8,128)(2,1)S(1)} %collective-permute-done.2.refs_0_.refs_1_) | copy-start | bytes 1179652
  54.5 0.7 copy-start.4
  55.3 1.1 copy-start.2
  56.4 164.7 %all-to-all-start.2 = ((bf16[8,3,2,256,128]{4,3,2,1,0:T(8,128)(2,1)}), bf16[8,3,2,256,128]{4,3,2,1,0:T(8,128)(2,1)S(1)}, u32[]{:S(2)}, u32[]{:S(2)}) async-start(bf16[8,3,2,256,128]{4,3,2,1,0:T(8,128)(2,1)} %hold.1), calls=%async_computation.2 | async-start | bytes 6291456 | tf_op jit(solution)/shard_map/all_to_all | solution.py:68
  60.8 93.9 %collective-permute-start.4 = (bf16[3,2,256,128]{3,2,1,0:T(8,128)(2,1)}, bf16[3,2,256,128]{3,2,1,0:T(8,128)(2,1)S(1)}, u32[]{:S(2)}, u32[]{:S(2)}) collective-permute-start(bf16[3,2,256,128]{3,2,1,0:T(8,128)(2,1)} %get-tuple-element.40), channel_id=1, source_target_pairs={{0,5},{1,4},{2,7},{3,6},{4,1},{5,0},{6,3},{7,2},{8,13},{9,12},{10,... | collective-permute-start | bytes 1179656 | tf_op jit(solution)/shard_map/ppermute | solution.py:71
  64.1 99.0 %collective-permute-start.5 = (bf16[3,2,256,128]{3,2,1,0:T(8,128)(2,1)}, bf16[3,2,256,128]{3,2,1,0:T(8,128)(2,1)S(1)}, u32[]{:S(2)}, u32[]{:S(2)}) collective-permute-start(bf16[3,2,256,128]{3,2,1,0:T(8,128)(2,1)} %get-tuple-element.41), channel_id=1, source_target_pairs={{0,4},{1,5},{2,6},{3,7},{4,0},{5,1},{6,2},{7,3},{8,12},{9,13},{10,... | collective-permute-start | bytes 1179656 | tf_op jit(solution)/shard_map/ppermute | solution.py:71
  154.7 8.3 %copy-start.5 = (bf16[3,2,256,128]{3,2,1,0:T(8,128)(2,1)}, bf16[3,2,256,128]{3,2,1,0:T(8,128)(2,1)S(1)}, u32[]{:S(2)}) copy-start(bf16[3,2,256,128]{3,2,1,0:T(8,128)(2,1)S(1)} %collective-permute-done.4.refs_2_) | copy-start | bytes 1179652
  163.0 0.7 copy-start.6
  165.9 3.3 collective-permute-start.6
  167.9 3.6 collective-permute-start.7
  207.9 9.3 %collective-permute-start.8 = (bf16[4,3,128,128]{3,2,1,0:T(8,128)(2,1)S(1)}, bf16[4,3,128,128]{3,2,1,0:T(8,128)(2,1)S(1)}, u32[]{:S(2)}, u32[]{:S(2)}) collective-permute-start(bf16[4,3,128,128]{3,2,1,0:T(8,128)(2,1)S(1)} %get-tuple-element.47), channel_id=1, source_target_pairs={{8,0},{16,8},{24,16},{9,1},{17,9},{25,17},{10,2},{18,10},{26,18},{... | collective-permute-start | bytes 1179656 | tf_op jit(solution)/shard_map/ppermute | solution.py:25
  209.2 9.3 %collective-permute-start.9 = (bf16[4,3,128,128]{3,2,1,0:T(8,128)(2,1)S(1)}, bf16[4,3,128,128]{3,2,1,0:T(8,128)(2,1)S(1)}, u32[]{:S(2)}, u32[]{:S(2)}) collective-permute-start(bf16[4,3,128,128]{3,2,1,0:T(8,128)(2,1)S(1)} %get-tuple-element.48), channel_id=1, source_target_pairs={{0,8},{8,16},{16,24},{1,9},{9,17},{17,25},{2,10},{10,18},{18,26},{... | collective-permute-start | bytes 1179656 | tf_op jit(solution)/shard_map/ppermute | solution.py:25
  221.2 1.7 copy-start.1
  222.9 74.2 %all-to-all-start.1 = ((bf16[8,3,2,256,128]{4,3,2,1,0:T(8,128)(2,1)}), bf16[8,3,2,256,128]{4,3,2,1,0:T(8,128)(2,1)S(1)}, u32[]{:S(2)}, u32[]{:S(2)}) async-start(bf16[8,3,2,256,128]{4,3,2,1,0:T(8,128)(2,1)} %finish.2.refs_1_), calls=%async_computation.1 | async-start | bytes 6291456 | tf_op jit(solution)/shard_map/all_to_all | solution.py:68
  231.1 7.8 %collective-permute-start.10 = (bf16[4,3,128,128]{3,2,1,0:T(8,128)(2,1)S(1)}, bf16[4,3,128,128]{3,2,1,0:T(8,128)(2,1)S(1)}, u32[]{:S(2)}, u32[]{:S(2)}) collective-permute-start(bf16[4,3,128,128]{3,2,1,0:T(8,128)(2,1)S(1)} %get-tuple-element.49), channel_id=1, source_target_pairs={{0,8},{8,16},{16,24},{1,9},{9,17},{17,25},{2,10},{10,18},{18,26},{... | collective-permute-start | bytes 1179656 | tf_op jit(solution)/shard_map/ppermute | solution.py:25
  237.6 6.1 %collective-permute-start.11 = (bf16[4,3,128,128]{3,2,1,0:T(8,128)(2,1)S(1)}, bf16[4,3,128,128]{3,2,1,0:T(8,128)(2,1)S(1)}, u32[]{:S(2)}, u32[]{:S(2)}) collective-permute-start(bf16[4,3,128,128]{3,2,1,0:T(8,128)(2,1)S(1)} %get-tuple-element.50), channel_id=1, source_target_pairs={{8,0},{16,8},{24,16},{9,1},{17,9},{25,17},{10,2},{18,10},{26,18},{... | collective-permute-start | bytes 1179656 | tf_op jit(solution)/shard_map/ppermute | solution.py:25
  280.1 10.1 %collective-permute-start.12 = (bf16[4,3,128,128]{3,2,1,0:T(8,128)(2,1)S(1)}, bf16[4,3,128,128]{3,2,1,0:T(8,128)(2,1)S(1)}, u32[]{:S(2)}, u32[]{:S(2)}) collective-permute-start(bf16[4,3,128,128]{3,2,1,0:T(8,128)(2,1)S(1)} %get-tuple-element.53), channel_id=1, source_target_pairs={{8,0},{16,8},{24,16},{9,1},{17,9},{25,17},{10,2},{18,10},{26,18},{... | collective-permute-start | bytes 1179656 | tf_op jit(solution)/shard_map/ppermute | solution.py:25
  281.4 10.1 %collective-permute-start.13 = (bf16[4,3,128,128]{3,2,1,0:T(8,128)(2,1)S(1)}, bf16[4,3,128,128]{3,2,1,0:T(8,128)(2,1)S(1)}, u32[]{:S(2)}, u32[]{:S(2)}) collective-permute-start(bf16[4,3,128,128]{3,2,1,0:T(8,128)(2,1)S(1)} %get-tuple-element.54), channel_id=1, source_target_pairs={{0,8},{8,16},{16,24},{1,9},{9,17},{17,25},{2,10},{10,18},{18,26},{... | collective-permute-start | bytes 1179656 | tf_op jit(solution)/shard_map/ppermute | solution.py:25
  297.1 1.6 copy-start
  297.1 14.4 %copy-start.13 = (bf16[3,2,256,128]{3,2,1,0:T(8,128)(2,1)S(1)}, bf16[3,2,256,128]{3,2,1,0:T(8,128)(2,1)}, u32[]{:S(2)}) copy-start(bf16[3,2,256,128]{3,2,1,0:T(8,128)(2,1)} %get-tuple-element.58) | copy-start | bytes 1179652
  298.7 83.1 %all-to-all-start.3 = ((bf16[4,3,2,256,128]{4,3,2,1,0:T(8,128)(2,1)}), bf16[4,3,2,256,128]{4,3,2,1,0:T(8,128)(2,1)}, u32[]{:S(2)}, u32[]{:S(2)}) async-start(bf16[4,3,2,256,128]{4,3,2,1,0:T(8,128)(2,1)} %get-tuple-element.59), calls=%async_computation.3 | async-start | bytes 3145728 | tf_op jit(solution)/shard_map/all_to_all | solution.py:75
  304.4 19.0 %collective-permute-start.14 = (bf16[3,2,256,128]{3,2,1,0:T(8,128)(2,1)}, bf16[3,2,256,128]{3,2,1,0:T(8,128)(2,1)S(1)}, u32[]{:S(2)}, u32[]{:S(2)}) collective-permute-start(bf16[3,2,256,128]{3,2,1,0:T(8,128)(2,1)} %get-tuple-element.55), channel_id=1, source_target_pairs={{0,7},{1,6},{2,5},{3,4},{4,3},{5,2},{6,1},{7,0},{8,15},{9,14},{10,... | collective-permute-start | bytes 1179656 | tf_op jit(solution)/shard_map/ppermute | solution.py:71
  306.8 58.2 %collective-permute-start.15 = (bf16[3,2,256,128]{3,2,1,0:T(8,128)(2,1)}, bf16[3,2,256,128]{3,2,1,0:T(8,128)(2,1)S(1)}, u32[]{:S(2)}, u32[]{:S(2)}) collective-permute-start(bf16[3,2,256,128]{3,2,1,0:T(8,128)(2,1)} %get-tuple-element.56), channel_id=1, source_target_pairs={{0,6},{1,7},{2,4},{3,5},{4,2},{5,3},{6,0},{7,1},{8,14},{9,15},{10,... | collective-permute-start | bytes 1179656 | tf_op jit(solution)/shard_map/ppermute | solution.py:71
  307.3 66.2 %collective-permute-start.16 = (bf16[3,2,256,128]{3,2,1,0:T(8,128)(2,1)}, bf16[3,2,256,128]{3,2,1,0:T(8,128)(2,1)S(1)}, u32[]{:S(2)}, u32[]{:S(2)}) collective-permute-start(bf16[3,2,256,128]{3,2,1,0:T(8,128)(2,1)} %get-tuple-element.57), channel_id=1, source_target_pairs={{0,5},{1,4},{2,7},{3,6},{4,1},{5,0},{6,3},{7,2},{8,13},{9,12},{10,... | collective-permute-start | bytes 1179656 | tf_op jit(solution)/shard_map/ppermute | solution.py:71
  311.5 70.2 %collective-permute-start.17 = (bf16[3,2,256,128]{3,2,1,0:T(8,128)(2,1)S(1)}, bf16[3,2,256,128]{3,2,1,0:T(8,128)(2,1)S(1)}, u32[]{:S(2)}, u32[]{:S(2)}) collective-permute-start(bf16[3,2,256,128]{3,2,1,0:T(8,128)(2,1)S(1)} %copy-done.13), channel_id=1, source_target_pairs={{0,4},{1,5},{2,6},{3,7},{4,0},{5,1},{6,2},{7,3},{8,12},{9,13},{10,... | collective-permute-start | bytes 1179656 | tf_op jit(solution)/shard_map/ppermute | solution.py:71
  323.4 58.4 %copy-start.7 = (bf16[3,2,256,128]{3,2,1,0:T(8,128)(2,1)}, bf16[3,2,256,128]{3,2,1,0:T(8,128)(2,1)S(1)}, u32[]{:S(2)}) copy-start(bf16[3,2,256,128]{3,2,1,0:T(8,128)(2,1)S(1)} %collective-permute-done.14.refs_1_) | copy-start | bytes 1179652
  365.0 16.8 %copy-start.8 = (bf16[3,2,256,128]{3,2,1,0:T(8,128)(2,1)}, bf16[3,2,256,128]{3,2,1,0:T(8,128)(2,1)S(1)}, u32[]{:S(2)}) copy-start(bf16[3,2,256,128]{3,2,1,0:T(8,128)(2,1)S(1)} %collective-permute-done.15.refs_2_) | copy-start | bytes 1179652
  373.5 8.3 %copy-start.9 = (bf16[3,2,256,128]{3,2,1,0:T(8,128)(2,1)}, bf16[3,2,256,128]{3,2,1,0:T(8,128)(2,1)S(1)}, u32[]{:S(2)}) copy-start(bf16[3,2,256,128]{3,2,1,0:T(8,128)(2,1)S(1)} %collective-permute-done.16.refs_3_) | copy-start | bytes 1179652
  381.8 0.7 copy-start.10

commit v10 on v8

--- a/solution.py
+++ b/solution.py
@@ -17,6 +17,10 @@
 
 def in_hbm(x):
     return pltpu.with_memory_space_constraint(x, pltpu.HBM)
+
+
+def in_vmem(x):
+    return pltpu.with_memory_space_constraint(x, pltpu.VMEM)
 
 
 def from_behind(x, axis, by):
@@ -70,18 +74,23 @@
 
 
 def pack_kernel(
-    me, query, key, value, d_out, *refs, first, heads, peers, apart, per_peer, head_dim
+    me, query, key, value, d_out, *refs, first, heads, items, apart, per_peer, head_dim
 ):
-    messages = refs[-4 - (peers if apart else 1) : -4]
+    messages = refs[-4 - (len(items) if apart else 1) : -4]
     stage, ready, in_sems, out_sems = refs[-4:]
     sources = (key, value, query, d_out)
     aligned = apart and per_peer % LANES == 0
     at_once = aligned or not apart
-    order = range(peers)
+    peers = stage.shape[1]
+
+    def place_of(item):
+        if apart:
+            return messages[item - items[0]], me[0] ^ (peers - 1 - item)
+        return messages[0].at[item], item
 
     def span(item):
         if aligned:
-            base, begin = pl.multiple_of(part_of(messages, me, item)[1] * per_peer, LANES), first
+            base, begin = pl.multiple_of(place_of(item)[1] * per_peer, LANES), first
         else:
             base, begin = 0, item * per_peer + first
         low = begin // LANES * LANES
@@ -97,15 +106,16 @@
         )
 
     def send(item):
-        target, peer = part_of(messages, me, item)
+        target, peer = place_of(item)
         return pltpu.make_async_copy(
             ready.at[item if aligned else peer], target, out_sems.at[item]
         )
 
-    for item in order:
+    made = items if at_once else range(peers)
+    for item in made:
         for i in range(4):
             fetch(item, i).start()
-    for item in order:
+    for item in made:
         for i in range(4):
             fetch(item, i).wait()
         at = span(item)[2]
@@ -119,9 +129,9 @@
         if at_once:
             send(item).start()
     if not at_once:
-        for item in order:
+        for item in items:
             send(item).start()
-    for item in order:
+    for item in items:
         send(item).wait()
 
 
@@ -137,7 +147,7 @@
             pack_kernel,
             first=start * head_dim,
             heads=heads,
-            peers=peers,
+            items=range(peers),
             apart=apart,
             per_peer=heads_here * head_dim,
             head_dim=head_dim,
@@ -263,54 +273,124 @@
     )(me, *[in_hbm(x) for x in (*flat, *earlier)])
 
 
-def pick_kernel(me, asked, *refs, count, block_rows):
-    for_next, for_prev, stage, sems = refs[-4:]
-    peers, _, rows, _ = stage.shape
-    each = rows // block_rows
-
-    def fetch(item):
+def pick_kernel(me, asked, *refs, count):
+    for_next, for_prev, table, sems = refs[-4:]
+    heads, window, block_rows, _ = table.shape
+    peers, each = sems.shape
+
+    def fetch(item, i):
         source, peer = part_of(refs[:count], me, item)
-        return pltpu.make_async_copy(source.at[:, 0], stage.at[peer], sems.at[item])
+        rows = pl.ds(i * block_rows, block_rows)
+        return pltpu.make_async_copy(
+            source.at[:, 0, rows], table.at[:, CROSS + peer * each + i], sems.at[item, i]
+        )
 
     for item in range(peers):
-        fetch(item).start()
+        for i in range(each):
+            fetch(item, i).start()
     for item in range(peers):
-        fetch(item).wait()
-    for i in range(2 * CROSS):
-        target = for_next if i < CROSS else for_prev
-        peer = lax.div(asked[i], each)
-        start = pl.multiple_of(lax.rem(asked[i], each) * block_rows, block_rows)
-        target[i % CROSS] = stage[peer, :, pl.ds(start, block_rows)]
+        for i in range(each):
+            fetch(item, i).wait()
+    for i in range(CROSS):
+        for_next[i] = table[:, CROSS + asked[i]]
+        for_prev[i] = table[:, CROSS + asked[CROSS + i]]
 
 
 def pick(me, messages, asked, block_rows, after):
     heads, _, rows, lanes = message_shape(messages)
     dtype = messages[0].dtype
     peers = lax.axis_size("seq")
+    each = rows // block_rows
+    window = peers * each + 2 * CROSS
     picked = jax.ShapeDtypeStruct((CROSS, heads, block_rows, lanes), dtype)
     return pl.pallas_call(
-        functools.partial(pick_kernel, count=len(messages), block_rows=block_rows),
+        functools.partial(pick_kernel, count=len(messages)),
         in_specs=[pl.BlockSpec(memory_space=pltpu.SMEM)] * 2
         + [pl.BlockSpec(memory_space=pltpu.HBM)] * (len(messages) + len(after)),
-        out_specs=[pl.BlockSpec(memory_space=pltpu.VMEM)] * 2,
-        out_shape=[picked, picked],
-        scratch_shapes=[
-            pltpu.VMEM((peers, heads, rows, lanes), dtype),
-            pltpu.SemaphoreType.DMA((peers,)),
-        ],
+        out_specs=[pl.BlockSpec(memory_space=pltpu.VMEM)] * 3,
+        out_shape=[picked, picked, pltpu.VMEM((heads, window, block_rows, lanes), dtype)],
+        scratch_shapes=[pltpu.SemaphoreType.DMA((peers, each))],
         compiler_params=pltpu.CompilerParams(vmem_limit_bytes=SMALL_VMEM),
         name="pick",
     )(me, asked, *[in_hbm(x) for x in (*messages, *after)])
 
 
-def attend_kernel(me, lists, came_prev, came_next, *refs, block_rows, head_dim, per_list):
-    messages = refs[:-13]
-    back, own, to_prev, to_next = refs[-13:-9]
-    message, table, turned, sums, both_even, both_odd, low_even, low_odd, sems = refs[-9:]
-    peers, heads, _, rows, lanes = message.shape
+def prepare_kernel(me, table, *refs, peers):
+    messages = refs[:-4]
+    turned, pairs, sums, sems = refs[-4:]
+    heads, window, _, _ = table.shape
+
+    def fetch(item):
+        source, peer = part_of(messages, me, item)
+        return pltpu.make_async_copy(source.at[:, 1], pairs.at[peer], sems.at[item])
+
+    for item in range(peers):
+        fetch(item).start()
+    for head in range(heads):
+
+        def clear(i, carry):
+            sums[head, i] = jnp.zeros(sums.shape[2:], sums.dtype)
+            return carry
+
+        def turn(i, carry):
+            turned[head, i] = table[head, i].T
+            return carry
+
+        lax.fori_loop(0, window, clear, 0)
+        lax.fori_loop(CROSS, window - CROSS, turn, 0)
+    for item in range(peers):
+        fetch(item).wait()
+
+
+def prepare(me, messages, table):
+    heads, _, rows, lanes = message_shape(messages)
+    _, window, block_rows, _ = table.shape
+    dtype = messages[0].dtype
+    peers = lax.axis_size("seq")
+    inside = pl.BlockSpec(memory_space=pltpu.VMEM)
+    return pl.pallas_call(
+        functools.partial(prepare_kernel, peers=peers),
+        in_specs=[pl.BlockSpec(memory_space=pltpu.SMEM), inside]
+        + [pl.BlockSpec(memory_space=pltpu.HBM)] * len(messages),
+        out_specs=[inside] * 3,
+        out_shape=[
+            pltpu.VMEM((heads, window, lanes, block_rows), dtype),
+            pltpu.VMEM((peers, heads, rows, lanes), dtype),
+            pltpu.VMEM((heads, window, block_rows, lanes), jnp.float32),
+        ],
+        scratch_shapes=[pltpu.SemaphoreType.DMA((peers,))],
+        compiler_params=pltpu.CompilerParams(vmem_limit_bytes=SMALL_VMEM),
+        name="prepare",
+    )(me, in_vmem(table), *[in_hbm(x) for x in messages])
+
+
+def attend_kernel(
+    lists,
+    came_prev,
+    came_next,
+    pairs,
+    table_in,
+    turned_in,
+    sums_in,
+    back,
+    to_prev,
+    to_next,
+    table,
+    turned,
+    sums,
+    both_even,
+    both_odd,
+    low_even,
+    low_odd,
+    *,
+    head_dim,
+    per_list,
+):
+    del table_in, turned_in, sums_in
+    peers, heads, rows, lanes = pairs.shape
+    _, window, block_rows, _ = table.shape
     each = rows // block_rows
     blocks = peers * each
-    window = blocks + 2 * CROSS
     units = heads * blocks
     keys = per_list * block_rows
     scaling = head_dim ** (-0.5)
@@ -319,34 +399,12 @@
     low = (low_even, low_odd)
     step_rows = 64
 
-    def fetch(item):
-        source, peer = part_of(messages, me, item)
-        return pltpu.make_async_copy(source, message.at[peer], sems.at[item])
-
-    for item in range(peers):
-        fetch(item).start()
-    for item in range(peers):
-        fetch(item).wait()
     for head in range(heads):
         for i in range(CROSS):
             table[head, i] = came_prev[i, head]
             table[head, CROSS + blocks + i] = came_next[i, head]
-
-        def fill(peer, carry):
-            for i in range(each):
-                table[head, CROSS + peer * each + i] = message[
-                    peer, head, 0, i * block_rows : (i + 1) * block_rows
-                ]
-            return carry
-
-        lax.fori_loop(0, peers, fill, 0)
-
-        def turn(i, carry):
-            turned[head, i] = table[head, i].T
-            sums[head, i] = jnp.zeros(sums.shape[2:], sums.dtype)
-            return carry
-
-        lax.fori_loop(0, window, turn, 0)
+            turned[head, i] = came_prev[i, head].T
+            turned[head, CROSS + blocks + i] = came_next[i, head].T
 
     left = lax.broadcasted_iota(jnp.int32, (block_rows, lanes), 1) < head_dim
 
@@ -359,7 +417,7 @@
         return head, ids, peer, pl.ds(start, block_rows)
 
     def apart_of(head, peer, here):
-        query_grad = message[peer, head, 1, here]
+        query_grad = pairs[peer, head, here]
         nothing = jnp.zeros_like(query_grad)
         return jnp.concatenate(
             [jnp.where(left, query_grad, nothing), jnp.where(left, nothing, query_grad)],
@@ -437,59 +495,42 @@
             to_prev[i, head] = (sums[head, i] * factor).astype(to_prev.dtype)
             to_next[i, head] = (sums[head, CROSS + blocks + i] * factor).astype(to_next.dtype)
 
-        def finish(i, carry):
-            own[head, i] = sums[head, CROSS + i] * factor
-            return carry
-
-        lax.fori_loop(0, blocks, finish, 0)
-
-
-def attend(me, messages, came_prev, came_next, lists, block_rows):
-    shape = message_shape(messages)
-    heads, _, rows, lanes = shape
-    dtype = messages[0].dtype
-    peers = lax.axis_size("seq")
+
+def attend(lists, came_prev, came_next, pairs, table, turned, sums):
+    _, _, block_rows, lanes = came_prev.shape
+    dtype = pairs.dtype
     per_list = lists.shape[-1]
     keys = per_list * block_rows
-    blocks = peers * rows // block_rows
-    window = blocks + 2 * CROSS
     inside = pl.BlockSpec(memory_space=pltpu.VMEM)
-    scalars = pl.BlockSpec(memory_space=pltpu.SMEM)
     cross_shape = jax.ShapeDtypeStruct(came_prev.shape, dtype)
+    kept = (table, turned, sums)
     return pl.pallas_call(
-        functools.partial(
-            attend_kernel, block_rows=block_rows, head_dim=lanes // 2, per_list=per_list
-        ),
-        in_specs=[scalars, scalars, inside, inside]
-        + [pl.BlockSpec(memory_space=pltpu.HBM)] * len(messages),
-        out_specs=[inside] * 4,
-        out_shape=[
-            pltpu.VMEM((peers, heads, rows, lanes), dtype),
-            pltpu.VMEM((heads, blocks, block_rows, lanes), jnp.float32),
-            cross_shape,
-            cross_shape,
-        ],
+        functools.partial(attend_kernel, head_dim=lanes // 2, per_list=per_list),
+        in_specs=[pl.BlockSpec(memory_space=pltpu.SMEM)] + [inside] * 6,
+        out_specs=[inside] * 6,
+        out_shape=[pltpu.VMEM(pairs.shape, dtype), cross_shape, cross_shape]
+        + [pltpu.VMEM(x.shape, x.dtype) for x in kept],
+        input_output_aliases={4: 3, 5: 4, 6: 5},
         scratch_shapes=[
-            pltpu.VMEM((peers,) + shape, dtype),
-            pltpu.VMEM((heads, window, block_rows, lanes), dtype),
-            pltpu.VMEM((heads, window, lanes, block_rows), dtype),
-            pltpu.VMEM((heads, window, block_rows, lanes), jnp.float32),
             pltpu.VMEM((keys, 2 * block_rows), jnp.float32),
             pltpu.VMEM((keys, 2 * block_rows), jnp.float32),
             pltpu.VMEM((keys, 2 * block_rows), dtype),
             pltpu.VMEM((keys, 2 * block_rows), dtype),
-            pltpu.SemaphoreType.DMA((peers,)),
         ],
-        compiler_params=pltpu.CompilerParams(vmem_limit_bytes=LARGE_VMEM),
+        compiler_params=pltpu.CompilerParams(vmem_limit_bytes=SMALL_VMEM),
         name="attend",
-    )(me, lists, came_prev, came_next, *[in_hbm(x) for x in messages])
-
-
-def finish_kernel(me, asked, back, own, later, earlier, *refs, block_rows):
+    )(lists, came_prev, came_next, *[in_vmem(x) for x in (pairs, *kept)])
+
+
+def finish_kernel(me, asked, back, kept, later, earlier, *refs, block_rows):
     messages = refs[:-3]
     sums, ready, sems = refs[-3:]
-    peers, heads, _, rows, _ = ready.shape
+    peers, heads, _, rows, lanes = ready.shape
     each = rows // block_rows
+    blocks = peers * each
+    head_dim = lanes // 2
+    left = lax.broadcasted_iota(jnp.int32, (block_rows, lanes), 1) < head_dim
+    factor = jnp.where(left, head_dim ** (-0.5), 1.0)
 
     def send(item, head):
         target, peer = part_of(messages, me, item)
@@ -498,7 +539,7 @@
         )
 
     for head in range(heads):
-        sums[...] = own[head]
+        sums[...] = kept[head, CROSS : CROSS + blocks] * factor
         for i in range(CROSS):
             sums[asked[i]] += later[i, head].astype(jnp.float32)
         for i in range(CROSS):
@@ -516,9 +557,10 @@
             send(item, head).wait()
 
 
-def finish(me, back, own, later, earlier, asked, apart):
+def finish(me, back, kept, later, earlier, asked, apart):
     peers, heads, rows, lanes = back.shape
-    _, blocks, block_rows, _ = own.shape
+    _, window, block_rows, _ = kept.shape
+    blocks = window - 2 * CROSS
     inside = pl.BlockSpec(memory_space=pltpu.VMEM)
     scalars = pl.BlockSpec(memory_space=pltpu.SMEM)
     shape = (heads, 2, rows, lanes)
@@ -538,8 +580,8 @@
     )(
         me,
         asked,
-        pltpu.with_memory_space_constraint(back, pltpu.VMEM),
-        pltpu.with_memory_space_constraint(own, pltpu.VMEM),
+        in_vmem(back),
+        in_vmem(kept),
         later,
         earlier,
     )
@@ -594,15 +636,17 @@
     received = []
     outs = finished = ()
     for chunk, (messages, start, size) in enumerate(zip(came, starts, sizes)):
-        for_next, for_prev = pick(me, messages, asked, block_rows, finished[:1])
+        for_next, for_prev, table = pick(me, messages, asked, block_rows, finished[:1])
         came_prev = from_behind(for_next, "slab", 1)
         came_next = from_behind(for_prev, "slab", -1)
-        back, own, to_prev, to_next = attend(
-            me, messages, came_prev, came_next, local_ids[start : start + size], block_rows
+        turned, pairs, sums = prepare(me, messages, table)
+        lists = local_ids[start : start + size]
+        back, to_prev, to_next, _, _, kept = attend(
+            lists, came_prev, came_next, pairs, table, turned, sums
         )
         later = from_behind(to_prev, "slab", -1)
         earlier = from_behind(to_next, "slab", 1)
-        finished = finish(me, back, own, later, earlier, asked, chunk == last)
+        finished = finish(me, back, kept, later, earlier, asked, chunk == last)
         received.append(exchange(finished))
         outs = unpack(me, received, starts, heads_here, outs)
     return tuple(outs)

time: 312 us -> 309 us (level)
  waiting for transfers between devices: 138 us -> 146 us
  Pallas kernels: 98 us -> 91.1 us
  starting transfers between devices: 63 us -> 58.6 us
    all_to_all x2, waiting for transfers between devices: 7.29 us -> 17.6 us  [exchange(): lax.all_to_all(messages[0], 'seq', split_axis=0, concat_axis=0, tiled=True)]
    ppermute x10, waiting for transfers between devices: 10.3 us -> 2.5 us  [from_behind(): return lax.ppermute(x, axis, pairs)]
    pallas_call x4 -> x6, Pallas kernels: 77.1 us -> 70.2 us  [the longest x2 58 us: attend(): pl.pallas_call(functools.partial(attend_kernel, head_dim=lanes // 2, per_...]
    ppermute x14, waiting for transfers between devices: 121 us -> 126 us  [exchange(): received[item] = lax.ppermute(messages[item], 'seq', pairs)]
    ppermute x10, starting transfers between devices: 30.3 us -> 25.5 us  [from_behind(): return lax.ppermute(x, axis, pairs)]
  transfers between devices with their start and end apart: 26 -> 26, of which waited for: 14 -> 13; matrix products, arithmetic and copies ran while one was open for 1% -> 1% of each run, Pallas kernels for 29% -> 27%
where the time goes in v10:
time: 309 us; the launch traced here: 304 us
  waiting for transfers between devices  146 us (47%)
  Pallas kernels  91.1 us (29%)
  starting transfers between devices  58.6 us (19%)
  local copies, waits for them, and re-layouts  4.2 us (1%)
    ppermute x14, waiting for transfers between devices, exchange(): received[item] = lax.ppermute(messages[item], 'seq', pairs)  126 us
    pallas_call x2, Pallas kernels, attend(): pl.pallas_call(functools.partial(attend_kernel, head_dim=lanes // 2, per_...  58 us
    ppermute x10, starting transfers between devices, from_behind(): return lax.ppermute(x, axis, pairs)  25.5 us
    ppermute x14, starting transfers between devices, exchange(): received[item] = lax.ppermute(messages[item], 'seq', pairs)  20.2 us
    all_to_all x2, waiting for transfers between devices, exchange(): lax.all_to_all(messages[0], 'seq', split_axis=0, concat_axis=0, tiled=True)  17.6 us
    all_to_all x2, starting transfers between devices, exchange(): lax.all_to_all(messages[0], 'seq', split_axis=0, concat_axis=0, tiled=True)  12.9 us
    pallas_call x2, Pallas kernels, unpack(): pl.pallas_call(functools.partial(unpack_kernel, chunk=chunk, peers=peers,...  7.92 us
    pallas_call x2, Pallas kernels, prepare(): pl.pallas_call(functools.partial(prepare_kernel, peers=peers), in_specs=[...  7.79 us
  transfers between devices with their start and end apart: 26, of which 13 were waited for; matrix products, arithmetic and copies ran while one was open for 1% of the time, Pallas kernels for 27%

profile of v10, /device:TPU:8, one launch (start us, length us, event | category | flops | bytes accessed | tf_op | source)
XLA Modules:
  0.0 304.1 jit_solution(6924566626563214185)
XLA Ops:
  0.6 3.9 %pack.2 = (bf16[3,2,256,128]{3,2,1,0:T(8,128)(2,1)}, bf16[3,2,256,128]{3,2,1,0:T(8,128)(2,1)}, bf16[3,2,256,128]{3,2,1,0:T(8,128)(2,1)}, bf16[3,2,256,128]{3,2,1...) custom-call(s32[1]{0:T(128)} %bitcast.me, ...), custom_call_target="tpu_custom_call" | custom-call | tf_op jit(solution)/shard_map/pack/pallas_call | solution.py:145
  4.6 2.6 collective-permute-start.2
  8.0 1.3 top_k.24
  9.3 1.3 collective-permute-start.1
  10.6 1.3 top_k.17
  11.9 1.3 collective-permute-start
  13.2 4.4 %collective-permute-start.4 = (bf16[3,2,256,128]{3,2,1,0:T(8,128)(2,1)}, bf16[3,2,256,128]{3,2,1,0:T(8,128)(2,1)S(1)}, u32[]{:S(2)}, u32[]{:S(2)}) collective-permute-start(bf16[3,2,256,128]{3,2,1,0:T(8,128)(2,1)} %get-tuple-element.54), channel_id=1, source_target_pairs={{0,5},{1,4},{2,7},{3,6},{4,1},{5,0},{6,3},{7,2},{8,13},{9,12},{10,... | collective-permute-start | bytes 1179656 | tf_op jit(solution)/shard_map/ppermute | solution.py:72
  17.7 1.6 collective-permute-start.6
  19.3 37.2 %collective-permute-done.2.refs_0_.refs_1_ = bf16[3,2,256,128]{3,2,1,0:T(8,128)(2,1)S(1)} collective-permute-done((bf16[3,2,256,128]{3,2,1,0:T(8,128)(2,1)}, bf16[3,2,256,128]{3,2,1,0:T(8,128)(2,1)S(1)}, u32[]{:S(2)}, u32[]{:S(2)}) %collective-permute-start.2) | collective-permute-done | bytes 393248 | tf_op jit(solution)/shard_map/ppermute | solution.py:72
  56.5 7.3 %collective-permute-done.3.refs_1_.refs_2_ = bf16[3,2,256,128]{3,2,1,0:T(8,128)(2,1)S(1)} collective-permute-done((bf16[3,2,256,128]{3,2,1,0:T(8,128)(2,1)}, bf16[3,2,256,128]{3,2,1,0:T(8,128)(2,1)S(1)}, u32[]{:S(2)}, u32[]{:S(2)}) %collective-permute-start.3) | collective-permute-done | bytes 393248 | tf_op jit(solution)/shard_map/ppermute | solution.py:72
  64.9 3.9 %pack.3.refs_0_ = bf16[8,3,2,256,128]{4,3,2,1,0:T(8,128)(2,1)} custom-call(s32[1]{0:T(128)} %bitcast.me, bf16[256,3072]{1,0:T(8,128)(2,1)} %query.3, bf16[256,3072]{1,0:T(8,128)(2,1)} %key.3, bf16[256,3072]{1,0:T(8,128)(2,1)} %value.3, bf16[256,3072]{1,0:T(8,128)(2,1)} %d_out.3, s32[8]{0:T(128)S(1)} %pad_add_fusion.asked.refs_0_, ...), custom_call_target="tpu_custom_call" | custom-call | tf_op jit(solution)/shard_map/pack/pallas_call | solution.py:145
  68.8 2.6 collective-permute-done.4.refs_2_.refs_3_
  71.4 7.3 %collective-permute-done.5.refs_3_.refs_4_ = bf16[3,2,256,128]{3,2,1,0:T(8,128)(2,1)S(1)} collective-permute-done((bf16[3,2,256,128]{3,2,1,0:T(8,128)(2,1)}, bf16[3,2,256,128]{3,2,1,0:T(8,128)(2,1)S(1)}, u32[]{:S(2)}, u32[]{:S(2)}) %collective-permute-start.5) | collective-permute-done | bytes 393248 | tf_op jit(solution)/shard_map/ppermute | solution.py:72
  78.7 1.6 collective-permute-done.7.refs_5_.refs_6_
  80.3 0.7 copy-done.6
  81.8 6.7 %all-to-all-start.1 = ((bf16[8,3,2,256,128]{4,3,2,1,0:T(8,128)(2,1)}), bf16[8,3,2,256,128]{4,3,2,1,0:T(8,128)(2,1)}, u32[]{:S(2)}, u32[]{:S(2)}) async-start(bf16[8,3,2,256,128]{4,3,2,1,0:T(8,128)(2,1)} %hold.1), calls=%async_computation.1 | async-start | bytes 6291456 | tf_op jit(solution)/shard_map/all_to_all | solution.py:67
  88.5 2.2 pick.2
  90.7 1.3 collective-permute-start.10
  92.0 3.1 %collective-permute-start.9 = (bf16[4,3,128,128]{3,2,1,0:T(8,128)(2,1)S(1)}, bf16[4,3,128,128]{3,2,1,0:T(8,128)(2,1)S(1)}, u32[]{:S(2)}, u32[]{:S(2)}) collective-permute-start(bf16[4,3,128,128]{3,2,1,0:T(8,128)(2,1)S(1)} %get-tuple-element.60), channel_id=1, source_target_pairs={{0,8},{8,16},{16,24},{1,9},{9,17},{17,25},{2,10},{10,18},{18,26},{... | collective-permute-start | bytes 1179656 | tf_op jit(solution)/shard_map/ppermute | solution.py:29
  95.1 3.9 %prepare.2 = (bf16[3,24,128,128]{3,2,1,0:T(8,128)(2,1)S(1)}, bf16[8,3,256,128]{3,2,1,0:T(8,128)(2,1)S(1)}, f32[3,24,128,128]{3,2,1,0:T(8,128)S(1)}) custom-call(s32[1]{0:T(128)} %bitcast.me, bf16[3,24,128,128]{3,2,1,0:T(8,128)(2,1)S(1)} %get-tuple-element.62.table.table_in, bf16[3,2,256,128]{3,2,1,0:T(8,128)(2,1)} %copy-done.1, ...), custom_call_target="tpu_custom_call" | custom-call | tf_op jit(solution)/shard_map/prepare/pallas_call | solution.py:351
  99.0 29.1 %attend.2 = (bf16[8,3,256,128]{3,2,1,0:T(8,128)(2,1)S(1)}, bf16[4,3,128,128]{3,2,1,0:T(8,128)(2,1)S(1)}, bf16[4,3,128,128]{3,2,1,0:T(8,128)(2,1)S(1)}, bf16[3,24...) custom-call(s32[3,16,8]{2,1,0:T(8,128)S(1)} %get-tuple-element.97.li, ...), custom_call_target="tpu_custom_call", output_to_operand_aliasing={{3}: (4, {}), {4}: (5, {}), {5}: (6, {})} | custom-call | tf_op jit(solution)/shard_map/attend/pallas_call | solution.py:507
  128.1 1.3 collective-permute-start.11
  129.4 4.3 %collective-permute-start.12 = (bf16[4,3,128,128]{3,2,1,0:T(8,128)(2,1)S(1)}, bf16[4,3,128,128]{3,2,1,0:T(8,128)(2,1)S(1)}, u32[]{:S(2)}, u32[]{:S(2)}) collective-permute-start(bf16[4,3,128,128]{3,2,1,0:T(8,128)(2,1)S(1)} %get-tuple-element.69), channel_id=1, source_target_pairs={{0,8},{8,16},{16,24},{1,9},{9,17},{17,25},{2,10},{10,18},{18,26},{... | collective-permute-start | bytes 1179656 | tf_op jit(solution)/shard_map/ppermute | solution.py:29
  133.8 1.3 collective-permute-done.12.earlier
  135.1 2.6 finish.2.refs_1_
  137.7 17.6 %all-to-all-done.1.refs_0_ = bf16[8,3,2,256,128]{4,3,2,1,0:T(8,128)(2,1)} async-done(((bf16[8,3,2,256,128]{4,3,2,1,0:T(8,128)(2,1)}), bf16[8,3,2,256,128]{4,3,2,1,0:T(8,128)(2,1)}, u32[]{:S(2)}, u32[]{:S(2)}) %all-to-all-start.1) | async-done | bytes 3145760 | tf_op jit(solution)/shard_map/all_to_all | solution.py:67
  155.3 6.2 %all-to-all-start = ((bf16[8,3,2,256,128]{4,3,2,1,0:T(8,128)(2,1)}), bf16[8,3,2,256,128]{4,3,2,1,0:T(8,128)(2,1)S(1)}, u32[]{:S(2)}, u32[]{:S(2)}) async-start(bf16[8,3,2,256,128]{4,3,2,1,0:T(8,128)(2,1)} %finish.2.refs_1_), calls=%async_computation | async-start | bytes 6291456 | tf_op jit(solution)/shard_map/all_to_all | solution.py:67
  161.5 2.2 pick.3
  163.7 1.4 collective-permute-start.13
  165.1 1.3 collective-permute-start.14
  166.4 3.9 %prepare.3 = (bf16[3,24,128,128]{3,2,1,0:T(8,128)(2,1)S(1)}, bf16[8,3,256,128]{3,2,1,0:T(8,128)(2,1)S(1)}, f32[3,24,128,128]{3,2,1,0:T(8,128)S(1)}) custom-call(s32[1]{0:T(128)} %bitcast.me, bf16[3,24,128,128]{3,2,1,0:T(8,128)(2,1)S(1)} %get-tuple-element.72.table.table_in, bf16[8,3,2,256,128]{4,3,2,1,0:T(8,128)(2,1)} %all-to-all-done.1.refs_0_), custom_call_target="tpu_custom_call" | custom-call | tf_op jit(solution)/shard_map/prepare/pallas_call | solution.py:351
  170.4 28.9 %attend.3 = (bf16[8,3,256,128]{3,2,1,0:T(8,128)(2,1)S(1)}, bf16[4,3,128,128]{3,2,1,0:T(8,128)(2,1)S(1)}, bf16[4,3,128,128]{3,2,1,0:T(8,128)(2,1)S(1)}, bf16[3,24...) custom-call(s32[3,16,8]{2,1,0:T(8,128)S(1)} %get-tuple-element.96.li, ...), custom_call_target="tpu_custom_call", output_to_operand_aliasing={{3}: (4, {}), {4}: (5, {}), {5}: (6, {})} | custom-call | tf_op jit(solution)/shard_map/attend/pallas_call | solution.py:507
  199.3 1.3 collective-permute-start.15
  200.6 9.0 %collective-permute-start.16 = (bf16[4,3,128,128]{3,2,1,0:T(8,128)(2,1)S(1)}, bf16[4,3,128,128]{3,2,1,0:T(8,128)(2,1)S(1)}, u32[]{:S(2)}, u32[]{:S(2)}) collective-permute-start(bf16[4,3,128,128]{3,2,1,0:T(8,128)(2,1)S(1)} %get-tuple-element.79), channel_id=1, source_target_pairs={{0,8},{8,16},{16,24},{1,9},{9,17},{17,25},{2,10},{10,18},{18,26},{... | collective-permute-start | bytes 1179656 | tf_op jit(solution)/shard_map/ppermute | solution.py:29
  209.6 1.1 collective-permute-done.16.earlier
  210.7 2.6 finish.3
  213.4 2.4 collective-permute-start.17
  216.3 3.9 %collective-permute-start.19 = (bf16[3,2,256,128]{3,2,1,0:T(8,128)(2,1)}, bf16[3,2,256,128]{3,2,1,0:T(8,128)(2,1)}, u32[]{:S(2)}, u32[]{:S(2)}) collective-permute-start(bf16[3,2,256,128]{3,2,1,0:T(8,128)(2,1)} %get-tuple-element.82), channel_id=1, source_target_pairs={{0,5},{1,4},{2,7},{3,6},{4,1},{5,0},{6,3},{7,2},{8,13},{9,12},{10,... | collective-permute-start | bytes 1179656 | tf_op jit(solution)/shard_map/ppermute | solution.py:72
  220.5 2.0 collective-permute-start.21
  222.5 52.5 %collective-permute-done.17.refs_1_ = bf16[3,2,256,128]{3,2,1,0:T(8,128)(2,1)S(1)} collective-permute-done((bf16[3,2,256,128]{3,2,1,0:T(8,128)(2,1)}, bf16[3,2,256,128]{3,2,1,0:T(8,128)(2,1)S(1)}, u32[]{:S(2)}, u32[]{:S(2)}) %collective-permute-start.17) | collective-permute-done | bytes 393248 | tf_op jit(solution)/shard_map/ppermute | solution.py:72
  275.0 7.8 %collective-permute-done.18.refs_2_ = bf16[3,2,256,128]{3,2,1,0:T(8,128)(2,1)S(1)} collective-permute-done((bf16[3,2,256,128]{3,2,1,0:T(8,128)(2,1)}, bf16[3,2,256,128]{3,2,1,0:T(8,128)(2,1)S(1)}, u32[]{:S(2)}, u32[]{:S(2)}) %collective-permute-start.18) | collective-permute-done | bytes 393248 | tf_op jit(solution)/shard_map/ppermute | solution.py:72
  282.8 0.7 copy-done.9
  283.5 1.2 collective-permute-start.23
  284.7 1.6 copy-done
  286.4 3.0 %unpack.2 = (bf16[256,3072]{1,0:T(8,128)(2,1)}, bf16[256,3072]{1,0:T(8,128)(2,1)}, bf16[256,3072]{1,0:T(8,128)(2,1)}, bf16[256,3072]{1,0:T(8,128)(2,1)}) custom-call(s32[1]{0:T(128)} %bitcast.me, bf16[8,3,2,256,128]{4,3,2,1,0:T(8,128)(2,1)} %copy-done), custom_call_target="tpu_custom_call" | custom-call | tf_op jit(solution)/shard_map/unpack/pallas_call | solution.py:251
  289.4 8.0 %collective-permute-done.20.refs_4_ = bf16[3,2,256,128]{3,2,1,0:T(8,128)(2,1)} collective-permute-done((bf16[3,2,256,128]{3,2,1,0:T(8,128)(2,1)}, bf16[3,2,256,128]{3,2,1,0:T(8,128)(2,1)}, u32[]{:S(2)}, u32[]{:S(2)}) %collective-permute-start.20) | collective-permute-done | bytes 393248 | tf_op jit(solution)/shard_map/ppermute | solution.py:72
  297.4 1.6 collective-permute-done.22.refs_6_
  299.0 4.9 %unpack.3 = (bf16[256,3072]{1,0:T(8,128)(2,1)}, bf16[256,3072]{1,0:T(8,128)(2,1)}, bf16[256,3072]{1,0:T(8,128)(2,1)}, bf16[256,3072]{1,0:T(8,128)(2,1)}) custom-call(s32[1]{0:T(128)} %bitcast.me, bf16[8,3,2,256,128]{4,3,2,1,0:T(8,128)(2,1)} %copy-done, ...), custom_call_target="tpu_custom_call", output_to_operand_aliasing={{0}: (10, {}), {1}: (11, {}), {2}: (12, {}), {3}: (13, {})} | custom-call | tf_op jit(solution)/shard_map/unpack/pallas_call | solution.py:251
  (57 shorter events, 3.7 us)
Async XLA Ops:
  0.6 6.9 %copy-start.10 = (s32[6,16,8]{1,2,0:T(8,128)S(1)}, s32[6,16,8]{1,2,0:T(8,128)}, u32[]{:S(2)}) copy-start(s32[6,16,8]{1,2,0:T(8,128)} %param.9) | copy-start | bytes 9220
  4.6 51.9 %collective-permute-start.2 = (bf16[3,2,256,128]{3,2,1,0:T(8,128)(2,1)}, bf16[3,2,256,128]{3,2,1,0:T(8,128)(2,1)S(1)}, u32[]{:S(2)}, u32[]{:S(2)}) collective-permute-start(bf16[3,2,256,128]{3,2,1,0:T(8,128)(2,1)} %get-tuple-element.52), channel_id=1, source_target_pairs={{0,7},{1,6},{2,5},{3,4},{4,3},{5,2},{6,1},{7,0},{8,15},{9,14},{10,... | collective-permute-start | bytes 1179656 | tf_op jit(solution)/shard_map/ppermute | solution.py:72
  7.1 56.7 %collective-permute-start.3 = (bf16[3,2,256,128]{3,2,1,0:T(8,128)(2,1)}, bf16[3,2,256,128]{3,2,1,0:T(8,128)(2,1)S(1)}, u32[]{:S(2)}, u32[]{:S(2)}) collective-permute-start(bf16[3,2,256,128]{3,2,1,0:T(8,128)(2,1)} %get-tuple-element.53), channel_id=1, source_target_pairs={{0,6},{1,7},{2,4},{3,5},{4,2},{5,3},{6,0},{7,1},{8,14},{9,15},{10,... | collective-permute-start | bytes 1179656 | tf_op jit(solution)/shard_map/ppermute | solution.py:72
  9.3 8.3 %collective-permute-start.1 = (s32[4]{0:T(128)S(1)}, s32[4]{0:T(128)S(1)}, u32[]{:S(2)}, u32[]{:S(2)}) collective-permute-start(s32[4]{0:T(128)S(1)} %get-tuple-element.101), channel_id=1, source_target_pairs={{0,8},{8,16},{16,24},{1,9},{9,17},{17,25},{2,10},{10,18},{18,26},{... | collective-permute-start | bytes 56 | tf_op jit(solution)/shard_map/ppermute | solution.py:29
  11.9 5.8 %collective-permute-start = (s32[4]{0:T(128)S(1)}, s32[4]{0:T(128)S(1)}, u32[]{:S(2)}, u32[]{:S(2)}) collective-permute-start(s32[4]{0:T(128)S(1)} %get-tuple-element.99), channel_id=1, source_target_pairs={{8,0},{16,8},{24,16},{9,1},{17,9},{25,17},{10,2},{18,10},{26,18},{... | collective-permute-start | bytes 56 | tf_op jit(solution)/shard_map/ppermute | solution.py:29
  13.2 58.2 %collective-permute-start.4 = (bf16[3,2,256,128]{3,2,1,0:T(8,128)(2,1)}, bf16[3,2,256,128]{3,2,1,0:T(8,128)(2,1)S(1)}, u32[]{:S(2)}, u32[]{:S(2)}) collective-permute-start(bf16[3,2,256,128]{3,2,1,0:T(8,128)(2,1)} %get-tuple-element.54), channel_id=1, source_target_pairs={{0,5},{1,4},{2,7},{3,6},{4,1},{5,0},{6,3},{7,2},{8,13},{9,12},{10,... | collective-permute-start | bytes 1179656 | tf_op jit(solution)/shard_map/ppermute | solution.py:72
  17.6 61.1 %collective-permute-start.5 = (bf16[3,2,256,128]{3,2,1,0:T(8,128)(2,1)}, bf16[3,2,256,128]{3,2,1,0:T(8,128)(2,1)S(1)}, u32[]{:S(2)}, u32[]{:S(2)}) collective-permute-start(bf16[3,2,256,128]{3,2,1,0:T(8,128)(2,1)} %get-tuple-element.55), channel_id=1, source_target_pairs={{0,4},{1,5},{2,6},{3,7},{4,0},{5,1},{6,2},{7,3},{8,12},{9,13},{10,... | collective-permute-start | bytes 1179656 | tf_op jit(solution)/shard_map/ppermute | solution.py:72
  17.7 61.0 %collective-permute-start.6 = (bf16[3,2,256,128]{3,2,1,0:T(8,128)(2,1)}, bf16[3,2,256,128]{3,2,1,0:T(8,128)(2,1)S(1)}, u32[]{:S(2)}, u32[]{:S(2)}) collective-permute-start(bf16[3,2,256,128]{3,2,1,0:T(8,128)(2,1)} %get-tuple-element.56), channel_id=1, source_target_pairs={{0,3},{1,2},{2,1},{3,0},{4,7},{5,6},{6,5},{7,4},{8,11},{9,10},{10,... | collective-permute-start | bytes 1179656 | tf_op jit(solution)/shard_map/ppermute | solution.py:72
  56.5 12.3 %copy-start.1 = (bf16[3,2,256,128]{3,2,1,0:T(8,128)(2,1)}, bf16[3,2,256,128]{3,2,1,0:T(8,128)(2,1)S(1)}, u32[]{:S(2)}) copy-start(bf16[3,2,256,128]{3,2,1,0:T(8,128)(2,1)S(1)} %collective-permute-done.2.refs_0_.refs_1_) | copy-start | bytes 1179652
  56.5 23.8 %collective-permute-start.7 = (bf16[3,2,256,128]{3,2,1,0:T(8,128)(2,1)}, bf16[3,2,256,128]{3,2,1,0:T(8,128)(2,1)S(1)}, u32[]{:S(2)}, u32[]{:S(2)}) collective-permute-start(bf16[3,2,256,128]{3,2,1,0:T(8,128)(2,1)} %get-tuple-element.57), channel_id=1, source_target_pairs={{0,2},{1,3},{2,0},{3,1},{4,6},{5,7},{6,4},{7,5},{8,10},{9,11},{10,... | collective-permute-start | bytes 1179656 | tf_op jit(solution)/shard_map/ppermute | solution.py:72
  63.8 4.9 %copy-start.2 = (bf16[3,2,256,128]{3,2,1,0:T(8,128)(2,1)}, bf16[3,2,256,128]{3,2,1,0:T(8,128)(2,1)S(1)}, u32[]{:S(2)}) copy-start(bf16[3,2,256,128]{3,2,1,0:T(8,128)(2,1)S(1)} %collective-permute-done.3.refs_1_.refs_2_) | copy-start | bytes 1179652
  63.8 16.5 %collective-permute-start.8 = (bf16[3,2,256,128]{3,2,1,0:T(8,128)(2,1)}, bf16[3,2,256,128]{3,2,1,0:T(8,128)(2,1)S(1)}, u32[]{:S(2)}, u32[]{:S(2)}) collective-permute-start(bf16[3,2,256,128]{3,2,1,0:T(8,128)(2,1)} %get-tuple-element.58), channel_id=1, source_target_pairs={{0,1},{1,0},{2,3},{3,2},{4,5},{5,4},{6,7},{7,6},{8,9},{9,8},{10,11... | collective-permute-start | bytes 1179656 | tf_op jit(solution)/shard_map/ppermute | solution.py:72
  71.4 8.9 %copy-start.3 = (bf16[3,2,256,128]{3,2,1,0:T(8,128)(2,1)}, bf16[3,2,256,128]{3,2,1,0:T(8,128)(2,1)S(1)}, u32[]{:S(2)}) copy-start(bf16[3,2,256,128]{3,2,1,0:T(8,128)(2,1)S(1)} %collective-permute-done.4.refs_2_.refs_3_) | copy-start | bytes 1179652
  78.7 1.6 copy-start.4
  78.7 1.6 copy-start.5
  80.3 0.8 copy-start.6
  81.1 0.7 copy-start.7
  81.8 73.5 %all-to-all-start.1 = ((bf16[8,3,2,256,128]{4,3,2,1,0:T(8,128)(2,1)}), bf16[8,3,2,256,128]{4,3,2,1,0:T(8,128)(2,1)}, u32[]{:S(2)}, u32[]{:S(2)}) async-start(bf16[8,3,2,256,128]{4,3,2,1,0:T(8,128)(2,1)} %hold.1), calls=%async_computation.1 | async-start | bytes 6291456 | tf_op jit(solution)/shard_map/all_to_all | solution.py:67
  90.7 8.3 %collective-permute-start.10 = (bf16[4,3,128,128]{3,2,1,0:T(8,128)(2,1)S(1)}, bf16[4,3,128,128]{3,2,1,0:T(8,128)(2,1)S(1)}, u32[]{:S(2)}, u32[]{:S(2)}) collective-permute-start(bf16[4,3,128,128]{3,2,1,0:T(8,128)(2,1)S(1)} %get-tuple-element.61), channel_id=1, source_target_pairs={{8,0},{16,8},{24,16},{9,1},{17,9},{25,17},{10,2},{18,10},{26,18},{... | collective-permute-start | bytes 1179656 | tf_op jit(solution)/shard_map/ppermute | solution.py:29
  92.0 7.0 %collective-permute-start.9 = (bf16[4,3,128,128]{3,2,1,0:T(8,128)(2,1)S(1)}, bf16[4,3,128,128]{3,2,1,0:T(8,128)(2,1)S(1)}, u32[]{:S(2)}, u32[]{:S(2)}) collective-permute-start(bf16[4,3,128,128]{3,2,1,0:T(8,128)(2,1)S(1)} %get-tuple-element.60), channel_id=1, source_target_pairs={{0,8},{8,16},{16,24},{1,9},{9,17},{17,25},{2,10},{10,18},{18,26},{... | collective-permute-start | bytes 1179656 | tf_op jit(solution)/shard_map/ppermute | solution.py:29
  128.1 5.6 %collective-permute-start.11 = (bf16[4,3,128,128]{3,2,1,0:T(8,128)(2,1)S(1)}, bf16[4,3,128,128]{3,2,1,0:T(8,128)(2,1)S(1)}, u32[]{:S(2)}, u32[]{:S(2)}) collective-permute-start(bf16[4,3,128,128]{3,2,1,0:T(8,128)(2,1)S(1)} %get-tuple-element.68), channel_id=1, source_target_pairs={{8,0},{16,8},{24,16},{9,1},{17,9},{25,17},{10,2},{18,10},{26,18},{... | collective-permute-start | bytes 1179656 | tf_op jit(solution)/shard_map/ppermute | solution.py:29
  129.4 5.7 %collective-permute-start.12 = (bf16[4,3,128,128]{3,2,1,0:T(8,128)(2,1)S(1)}, bf16[4,3,128,128]{3,2,1,0:T(8,128)(2,1)S(1)}, u32[]{:S(2)}, u32[]{:S(2)}) collective-permute-start(bf16[4,3,128,128]{3,2,1,0:T(8,128)(2,1)S(1)} %get-tuple-element.69), channel_id=1, source_target_pairs={{0,8},{8,16},{16,24},{1,9},{9,17},{17,25},{2,10},{10,18},{18,26},{... | collective-permute-start | bytes 1179656 | tf_op jit(solution)/shard_map/ppermute | solution.py:29
  155.3 129.4 %all-to-all-start = ((bf16[8,3,2,256,128]{4,3,2,1,0:T(8,128)(2,1)}), bf16[8,3,2,256,128]{4,3,2,1,0:T(8,128)(2,1)S(1)}, u32[]{:S(2)}, u32[]{:S(2)}) async-start(bf16[8,3,2,256,128]{4,3,2,1,0:T(8,128)(2,1)} %finish.2.refs_1_), calls=%async_computation | async-start | bytes 6291456 | tf_op jit(solution)/shard_map/all_to_all | solution.py:67
  163.7 6.6 %collective-permute-start.13 = (bf16[4,3,128,128]{3,2,1,0:T(8,128)(2,1)S(1)}, bf16[4,3,128,128]{3,2,1,0:T(8,128)(2,1)S(1)}, u32[]{:S(2)}, u32[]{:S(2)}) collective-permute-start(bf16[4,3,128,128]{3,2,1,0:T(8,128)(2,1)S(1)} %get-tuple-element.70), channel_id=1, source_target_pairs={{0,8},{8,16},{16,24},{1,9},{9,17},{17,25},{2,10},{10,18},{18,26},{... | collective-permute-start | bytes 1179656 | tf_op jit(solution)/shard_map/ppermute | solution.py:29
  165.1 5.3 %collective-permute-start.14 = (bf16[4,3,128,128]{3,2,1,0:T(8,128)(2,1)S(1)}, bf16[4,3,128,128]{3,2,1,0:T(8,128)(2,1)S(1)}, u32[]{:S(2)}, u32[]{:S(2)}) collective-permute-start(bf16[4,3,128,128]{3,2,1,0:T(8,128)(2,1)S(1)} %get-tuple-element.71), channel_id=1, source_target_pairs={{8,0},{16,8},{24,16},{9,1},{17,9},{25,17},{10,2},{18,10},{26,18},{... | collective-permute-start | bytes 1179656 | tf_op jit(solution)/shard_map/ppermute | solution.py:29
  199.3 10.3 %collective-permute-start.15 = (bf16[4,3,128,128]{3,2,1,0:T(8,128)(2,1)S(1)}, bf16[4,3,128,128]{3,2,1,0:T(8,128)(2,1)S(1)}, u32[]{:S(2)}, u32[]{:S(2)}) collective-permute-start(bf16[4,3,128,128]{3,2,1,0:T(8,128)(2,1)S(1)} %get-tuple-element.78), channel_id=1, source_target_pairs={{8,0},{16,8},{24,16},{9,1},{17,9},{25,17},{10,2},{18,10},{26,18},{... | collective-permute-start | bytes 1179656 | tf_op jit(solution)/shard_map/ppermute | solution.py:29
  200.6 10.1 %collective-permute-start.16 = (bf16[4,3,128,128]{3,2,1,0:T(8,128)(2,1)S(1)}, bf16[4,3,128,128]{3,2,1,0:T(8,128)(2,1)S(1)}, u32[]{:S(2)}, u32[]{:S(2)}) collective-permute-start(bf16[4,3,128,128]{3,2,1,0:T(8,128)(2,1)S(1)} %get-tuple-element.79), channel_id=1, source_target_pairs={{0,8},{8,16},{16,24},{1,9},{9,17},{17,25},{2,10},{10,18},{18,26},{... | collective-permute-start | bytes 1179656 | tf_op jit(solution)/shard_map/ppermute | solution.py:29
  213.4 61.6 %collective-permute-start.17 = (bf16[3,2,256,128]{3,2,1,0:T(8,128)(2,1)}, bf16[3,2,256,128]{3,2,1,0:T(8,128)(2,1)S(1)}, u32[]{:S(2)}, u32[]{:S(2)}) collective-permute-start(bf16[3,2,256,128]{3,2,1,0:T(8,128)(2,1)} %get-tuple-element.80), channel_id=1, source_target_pairs={{0,7},{1,6},{2,5},{3,4},{4,3},{5,2},{6,1},{7,0},{8,15},{9,14},{10,... | collective-permute-start | bytes 1179656 | tf_op jit(solution)/shard_map/ppermute | solution.py:72
  215.8 67.0 %collective-permute-start.18 = (bf16[3,2,256,128]{3,2,1,0:T(8,128)(2,1)}, bf16[3,2,256,128]{3,2,1,0:T(8,128)(2,1)S(1)}, u32[]{:S(2)}, u32[]{:S(2)}) collective-permute-start(bf16[3,2,256,128]{3,2,1,0:T(8,128)(2,1)} %get-tuple-element.81), channel_id=1, source_target_pairs={{0,6},{1,7},{2,4},{3,5},{4,2},{5,3},{6,0},{7,1},{8,14},{9,15},{10,... | collective-permute-start | bytes 1179656 | tf_op jit(solution)/shard_map/ppermute | solution.py:72
  216.3 73.1 %collective-permute-start.19 = (bf16[3,2,256,128]{3,2,1,0:T(8,128)(2,1)}, bf16[3,2,256,128]{3,2,1,0:T(8,128)(2,1)}, u32[]{:S(2)}, u32[]{:S(2)}) collective-permute-start(bf16[3,2,256,128]{3,2,1,0:T(8,128)(2,1)} %get-tuple-element.82), channel_id=1, source_target_pairs={{0,5},{1,4},{2,7},{3,6},{4,1},{5,0},{6,3},{7,2},{8,13},{9,12},{10,... | collective-permute-start | bytes 1179656 | tf_op jit(solution)/shard_map/ppermute | solution.py:72
  220.2 77.2 %collective-permute-start.20 = (bf16[3,2,256,128]{3,2,1,0:T(8,128)(2,1)}, bf16[3,2,256,128]{3,2,1,0:T(8,128)(2,1)}, u32[]{:S(2)}, u32[]{:S(2)}) collective-permute-start(bf16[3,2,256,128]{3,2,1,0:T(8,128)(2,1)} %get-tuple-element.83), channel_id=1, source_target_pairs={{0,4},{1,5},{2,6},{3,7},{4,0},{5,1},{6,2},{7,3},{8,12},{9,13},{10,... | collective-permute-start | bytes 1179656 | tf_op jit(solution)/shard_map/ppermute | solution.py:72
  220.5 76.9 %collective-permute-start.21 = (bf16[3,2,256,128]{3,2,1,0:T(8,128)(2,1)}, bf16[3,2,256,128]{3,2,1,0:T(8,128)(2,1)}, u32[]{:S(2)}, u32[]{:S(2)}) collective-permute-start(bf16[3,2,256,128]{3,2,1,0:T(8,128)(2,1)} %get-tuple-element.84), channel_id=1, source_target_pairs={{0,3},{1,2},{2,1},{3,0},{4,7},{5,6},{6,5},{7,4},{8,11},{9,10},{10,... | collective-permute-start | bytes 1179656 | tf_op jit(solution)/shard_map/ppermute | solution.py:72
  275.0 24.0 %copy-start.8 = (bf16[3,2,256,128]{3,2,1,0:T(8,128)(2,1)}, bf16[3,2,256,128]{3,2,1,0:T(8,128)(2,1)S(1)}, u32[]{:S(2)}) copy-start(bf16[3,2,256,128]{3,2,1,0:T(8,128)(2,1)S(1)} %collective-permute-done.17.refs_1_) | copy-start | bytes 1179652
  275.0 24.0 %collective-permute-start.22 = (bf16[3,2,256,128]{3,2,1,0:T(8,128)(2,1)}, bf16[3,2,256,128]{3,2,1,0:T(8,128)(2,1)}, u32[]{:S(2)}, u32[]{:S(2)}) collective-permute-start(bf16[3,2,256,128]{3,2,1,0:T(8,128)(2,1)} %get-tuple-element.85), channel_id=1, source_target_pairs={{0,2},{1,3},{2,0},{3,1},{4,6},{5,7},{6,4},{7,5},{8,10},{9,11},{10,... | collective-permute-start | bytes 1179656 | tf_op jit(solution)/shard_map/ppermute | solution.py:72
  282.8 0.7 copy-start.9
  283.5 15.5 %collective-permute-start.23 = (bf16[3,2,256,128]{3,2,1,0:T(8,128)(2,1)}, bf16[3,2,256,128]{3,2,1,0:T(8,128)(2,1)}, u32[]{:S(2)}, u32[]{:S(2)}) collective-permute-start(bf16[3,2,256,128]{3,2,1,0:T(8,128)(2,1)} %get-tuple-element.86), channel_id=1, source_target_pairs={{0,1},{1,0},{2,3},{3,2},{4,5},{5,4},{6,7},{7,6},{8,9},{9,8},{10,11... | collective-permute-start | bytes 1179656 | tf_op jit(solution)/shard_map/ppermute | solution.py:72
  284.7 1.6 copy-start

commit v11 on v10

--- a/solution.py
+++ b/solution.py
@@ -270,6 +270,108 @@
         ],
         compiler_params=pltpu.CompilerParams(vmem_limit_bytes=SMALL_VMEM),
         name="unpack",
+    )(me, *[in_hbm(x) for x in (*flat, *earlier)])
+
+
+def unpack_items_kernel(me, *refs, items, peers, counts, joint, earlier, jobs, per_peer):
+    ends = [sum(counts[: c + 1]) for c in range(len(counts))]
+    groups = [refs[end - count : end] for end, count in zip(ends, counts)]
+    outs = refs[ends[-1] + earlier :][:4]
+    stages = refs[-3 - len(counts) : -3]
+    ready, in_sems, out_sems = refs[-3:]
+    head_dim = ready.shape[-1] // 2
+    used = [
+        sorted({head for job in jobs for which, head in job[1:] if which == c})
+        for c in range(len(counts))
+    ]
+
+    def peer_of(j):
+        return me[0] ^ (peers - 1 - items[j])
+
+    def fetch(which, j):
+        group = groups[which]
+        source = group[0].at[peer_of(j)] if joint[which] else group[j]
+        some = pl.ds(used[which][0], used[which][-1] - used[which][0] + 1)
+        return pltpu.make_async_copy(
+            source.at[some], stages[which].at[j, some], in_sems.at[which, j]
+        )
+
+    def send(j, job, i):
+        first = pl.multiple_of(peer_of(j) * per_peer, LANES) + jobs[job][0] * LANES
+        return pltpu.make_async_copy(
+            ready.at[j, i, job], outs[i].at[:, pl.ds(first, LANES)], out_sems.at[j, i, job]
+        )
+
+    steps = [(j, which) for j in range(len(items)) for which in range(len(counts))]
+    steps = [(j, which) for j, which in steps if used[which]]
+    for j, which in steps:
+        fetch(which, j).start()
+    for j in range(len(items)):
+        for at, which in steps:
+            if at == j:
+                fetch(which, j).wait()
+        for job, (_, left, right) in enumerate(jobs):
+            sides = [stages[which][j, head] for which, head in (left, right)]
+            for i, (kind, at) in enumerate(((1, head_dim), (1, 0), (0, 0), (0, head_dim))):
+                ready[j, i, job] = jnp.concatenate(
+                    [side[kind, :, at : at + head_dim] for side in sides], axis=1
+                )
+                send(j, job, i).start()
+    for j in range(len(items)):
+        for job in range(len(jobs)):
+            for i in range(4):
+                send(j, job, i).wait()
+
+
+def unpack_items(me, messages, starts, heads_here, items, earlier):
+    chunk = len(messages) - 1
+    peers = lax.axis_size("seq")
+    _, _, rows, pair_dim = message_shape(messages[0])
+    head_dim = pair_dim // 2
+    per_peer = heads_here * head_dim
+    dtype = messages[0][0].dtype
+
+    def place_of(head):
+        which = max(c for c, start in enumerate(starts) if start <= head)
+        return which, head - starts[which]
+
+    jobs = []
+    for tile in range(per_peer // LANES):
+        left, right = place_of(2 * tile), place_of(2 * tile + 1)
+        if max(left[0], right[0]) == chunk:
+            jobs.append((tile, left, right))
+    groups = [
+        list(group) if len(group) == 1 else [group[item] for item in items]
+        for group in messages
+    ]
+    flat = [x for group in groups for x in group]
+    anywhere = pl.BlockSpec(memory_space=pltpu.HBM)
+    return pl.pallas_call(
+        functools.partial(
+            unpack_items_kernel,
+            items=items,
+            peers=peers,
+            counts=[len(group) for group in groups],
+            joint=[len(group) == 1 for group in messages],
+            earlier=len(earlier),
+            jobs=jobs,
+            per_peer=per_peer,
+        ),
+        in_specs=[pl.BlockSpec(memory_space=pltpu.SMEM)]
+        + [anywhere] * (len(flat) + len(earlier)),
+        out_specs=[anywhere] * 4,
+        out_shape=[pltpu.HBM((rows, peers * per_peer), dtype)] * 4,
+        input_output_aliases={1 + len(flat) + i: i for i in range(len(earlier))},
+        scratch_shapes=[
+            pltpu.VMEM((len(items),) + message_shape(m), dtype) for m in messages
+        ]
+        + [
+            pltpu.VMEM((len(items), 4, len(jobs), rows, LANES), dtype),
+            pltpu.SemaphoreType.DMA((chunk + 1, len(items))),
+            pltpu.SemaphoreType.DMA((len(items), 4, len(jobs))),
+        ],
+        compiler_params=pltpu.CompilerParams(vmem_limit_bytes=SMALL_VMEM),
+        name="unpack_items",
     )(me, *[in_hbm(x) for x in (*flat, *earlier)])
 
 
@@ -648,7 +750,17 @@
         earlier = from_behind(to_next, "slab", 1)
         finished = finish(me, back, kept, later, earlier, asked, chunk == last)
         received.append(exchange(finished))
-        outs = unpack(me, received, starts, heads_here, outs)
+        if chunk == last and heads_here * head_dim % LANES == 0:
+            half = peers // 2
+            parts = (
+                [peers - 1, *range(half // 2)],
+                [*range(half // 2, half - 1), *range(half, peers - 1)],
+                [half - 1],
+            )
+            for items in parts:
+                outs = unpack_items(me, received, starts, heads_here, items, outs)
+        else:
+            outs = unpack(me, received, starts, heads_here, outs)
     return tuple(outs)
 
 

time: 309 us -> 307 us (level)
  the two profiles are of different devices: /device:TPU:8 before, /device:TPU:2 now
where the time goes in v11:
time: 307 us; the launch traced here: 306 us
  starting transfers between devices  140 us (46%)
  Pallas kernels  93.8 us (31%)
  waiting for transfers between devices  63.9 us (21%)
  local copies, waits for them, and re-layouts  4.96 us (2%)
    ppermute x14, starting transfers between devices, exchange(): received[item] = lax.ppermute(messages[item], 'seq', pairs)  105 us
    pallas_call x2, Pallas kernels, attend(): pl.pallas_call(functools.partial(attend_kernel, head_dim=lanes // 2, per_...  58 us
    ppermute x14, waiting for transfers between devices, exchange(): received[item] = lax.ppermute(messages[item], 'seq', pairs)  41.8 us
    ppermute x10, starting transfers between devices, from_behind(): return lax.ppermute(x, axis, pairs)  25.7 us
    all_to_all x2, waiting for transfers between devices, exchange(): lax.all_to_all(messages[0], 'seq', split_axis=0, concat_axis=0, tiled=True)  19.6 us
    all_to_all x2, starting transfers between devices, exchange(): lax.all_to_all(messages[0], 'seq', split_axis=0, concat_axis=0, tiled=True)  8.98 us
    pallas_call x2, Pallas kernels, prepare(): pl.pallas_call(functools.partial(prepare_kernel, peers=peers), in_specs=[...  7.79 us
    pallas_call x2, Pallas kernels, pack(): pl.pallas_call(functools.partial(pack_kernel, first=start * head_dim, hea...  7.79 us
  transfers between devices with their start and end apart: 26, of which 12 were waited for; matrix products, arithmetic and copies ran while one was open for 1% of the time, Pallas kernels for 29%

profile of v11, /device:TPU:2, one launch (start us, length us, event | category | flops | bytes accessed | tf_op | source)
XLA Modules:
  0.0 306.5 jit_solution(5393359783850696081)
XLA Ops:
  0.6 3.9 %pack.2 = (bf16[3,2,256,128]{3,2,1,0:T(8,128)(2,1)}, bf16[3,2,256,128]{3,2,1,0:T(8,128)(2,1)}, bf16[3,2,256,128]{3,2,1,0:T(8,128)(2,1)}, bf16[3,2,256,128]{3,2,1...) custom-call(s32[1]{0:T(128)} %bitcast.me, ...), custom_call_target="tpu_custom_call" | custom-call | tf_op jit(solution)/shard_map/pack/pallas_call | solution.py:145
  4.6 3.6 %collective-permute-start.2 = (bf16[3,2,256,128]{3,2,1,0:T(8,128)(2,1)}, bf16[3,2,256,128]{3,2,1,0:T(8,128)(2,1)S(1)}, u32[]{:S(2)}, u32[]{:S(2)}) collective-permute-start(bf16[3,2,256,128]{3,2,1,0:T(8,128)(2,1)} %get-tuple-element.60), channel_id=1, source_target_pairs={{0,7},{1,6},{2,5},{3,4},{4,3},{5,2},{6,1},{7,0},{8,15},{9,14},{10,... | collective-permute-start | bytes 1179656 | tf_op jit(solution)/shard_map/ppermute | solution.py:72
  8.7 1.3 top_k.24
  10.0 1.4 collective-permute-start.1
  11.5 1.3 top_k.17
  12.8 1.3 collective-permute-start
  14.1 1.7 collective-permute-start.4
  15.9 2.1 collective-permute-start.5
  18.0 1.3 collective-permute-start.6
  19.6 38.4 %collective-permute-start.7 = (bf16[3,2,256,128]{3,2,1,0:T(8,128)(2,1)}, bf16[3,2,256,128]{3,2,1,0:T(8,128)(2,1)S(1)}, u32[]{:S(2)}, u32[]{:S(2)}) collective-permute-start(bf16[3,2,256,128]{3,2,1,0:T(8,128)(2,1)} %get-tuple-element.65), channel_id=1, source_target_pairs={{0,2},{1,3},{2,0},{3,1},{4,6},{5,7},{6,4},{7,5},{8,10},{9,11},{10,... | collective-permute-start | bytes 1179656 | tf_op jit(solution)/shard_map/ppermute | solution.py:72
  59.0 3.9 %pack.3.refs_0_ = bf16[8,3,2,256,128]{4,3,2,1,0:T(8,128)(2,1)} custom-call(s32[1]{0:T(128)} %bitcast.me, bf16[256,3072]{1,0:T(8,128)(2,1)} %query.3, bf16[256,3072]{1,0:T(8,128)(2,1)} %key.3, bf16[256,3072]{1,0:T(8,128)(2,1)} %value.3, bf16[256,3072]{1,0:T(8,128)(2,1)} %d_out.3, s32[8]{0:T(128)S(1)} %pad_add_fusion.asked.refs_0_, ...), custom_call_target="tpu_custom_call" | custom-call | tf_op jit(solution)/shard_map/pack/pallas_call | solution.py:145
  62.9 10.5 %collective-permute-done.4.refs_2_.refs_3_ = bf16[3,2,256,128]{3,2,1,0:T(8,128)(2,1)S(1)} collective-permute-done((bf16[3,2,256,128]{3,2,1,0:T(8,128)(2,1)}, bf16[3,2,256,128]{3,2,1,0:T(8,128)(2,1)S(1)}, u32[]{:S(2)}, u32[]{:S(2)}) %collective-permute-start.4) | collective-permute-done | bytes 393248 | tf_op jit(solution)/shard_map/ppermute | solution.py:72
  73.4 6.7 %collective-permute-done.5.refs_3_.refs_4_ = bf16[3,2,256,128]{3,2,1,0:T(8,128)(2,1)S(1)} collective-permute-done((bf16[3,2,256,128]{3,2,1,0:T(8,128)(2,1)}, bf16[3,2,256,128]{3,2,1,0:T(8,128)(2,1)S(1)}, u32[]{:S(2)}, u32[]{:S(2)}) %collective-permute-start.5) | collective-permute-done | bytes 393248 | tf_op jit(solution)/shard_map/ppermute | solution.py:72
  80.0 2.3 collective-permute-done.7.refs_5_.refs_6_
  83.8 4.8 %all-to-all-start.1 = ((bf16[8,3,2,256,128]{4,3,2,1,0:T(8,128)(2,1)}), bf16[8,3,2,256,128]{4,3,2,1,0:T(8,128)(2,1)}, u32[]{:S(2)}, u32[]{:S(2)}) async-start(bf16[8,3,2,256,128]{4,3,2,1,0:T(8,128)(2,1)} %hold.1), calls=%async_computation.1 | async-start | bytes 6291456 | tf_op jit(solution)/shard_map/all_to_all | solution.py:67
  88.6 2.2 pick.2
  90.8 1.3 collective-permute-start.10
  92.1 3.1 collective-permute-start.9
  95.2 3.9 %prepare.2 = (bf16[3,24,128,128]{3,2,1,0:T(8,128)(2,1)S(1)}, bf16[8,3,256,128]{3,2,1,0:T(8,128)(2,1)S(1)}, f32[3,24,128,128]{3,2,1,0:T(8,128)S(1)}) custom-call(s32[1]{0:T(128)} %bitcast.me, bf16[3,24,128,128]{3,2,1,0:T(8,128)(2,1)S(1)} %get-tuple-element.70.table.table_in, bf16[3,2,256,128]{3,2,1,0:T(8,128)(2,1)} %copy-done.1, ...), custom_call_target="tpu_custom_call" | custom-call | tf_op jit(solution)/shard_map/prepare/pallas_call | solution.py:453
  99.1 29.1 %attend.2 = (bf16[8,3,256,128]{3,2,1,0:T(8,128)(2,1)S(1)}, bf16[4,3,128,128]{3,2,1,0:T(8,128)(2,1)S(1)}, bf16[4,3,128,128]{3,2,1,0:T(8,128)(2,1)S(1)}, bf16[3,24...) custom-call(s32[3,16,8]{2,1,0:T(8,128)S(1)} %get-tuple-element.113.l, ...), custom_call_target="tpu_custom_call", output_to_operand_aliasing={{3}: (4, {}), {4}: (5, {}), {5}: (6, {})} | custom-call | tf_op jit(solution)/shard_map/attend/pallas_call | solution.py:609
  128.2 1.3 collective-permute-start.11
  129.5 4.3 %collective-permute-start.12 = (bf16[4,3,128,128]{3,2,1,0:T(8,128)(2,1)S(1)}, bf16[4,3,128,128]{3,2,1,0:T(8,128)(2,1)S(1)}, u32[]{:S(2)}, u32[]{:S(2)}) collective-permute-start(bf16[4,3,128,128]{3,2,1,0:T(8,128)(2,1)S(1)} %get-tuple-element.77), channel_id=1, source_target_pairs={{0,8},{8,16},{16,24},{1,9},{9,17},{17,25},{2,10},{10,18},{18,26},{... | collective-permute-start | bytes 1179656 | tf_op jit(solution)/shard_map/ppermute | solution.py:29
  133.9 1.3 collective-permute-done.12.earlier
  135.2 2.6 finish.2.refs_1_
  137.8 19.6 %all-to-all-done.1.refs_0_ = bf16[8,3,2,256,128]{4,3,2,1,0:T(8,128)(2,1)} async-done(((bf16[8,3,2,256,128]{4,3,2,1,0:T(8,128)(2,1)}), bf16[8,3,2,256,128]{4,3,2,1,0:T(8,128)(2,1)}, u32[]{:S(2)}, u32[]{:S(2)}) %all-to-all-start.1) | async-done | bytes 3145760 | tf_op jit(solution)/shard_map/all_to_all | solution.py:67
  157.4 4.2 %all-to-all-start = ((bf16[8,3,2,256,128]{4,3,2,1,0:T(8,128)(2,1)}), bf16[8,3,2,256,128]{4,3,2,1,0:T(8,128)(2,1)S(1)}, u32[]{:S(2)}, u32[]{:S(2)}) async-start(bf16[8,3,2,256,128]{4,3,2,1,0:T(8,128)(2,1)} %finish.2.refs_1_), calls=%async_computation | async-start | bytes 6291456 | tf_op jit(solution)/shard_map/all_to_all | solution.py:67
  161.6 2.2 pick.3
  163.8 1.4 collective-permute-start.13
  165.2 1.3 collective-permute-start.14
  166.5 3.9 %prepare.3 = (bf16[3,24,128,128]{3,2,1,0:T(8,128)(2,1)S(1)}, bf16[8,3,256,128]{3,2,1,0:T(8,128)(2,1)S(1)}, f32[3,24,128,128]{3,2,1,0:T(8,128)S(1)}) custom-call(s32[1]{0:T(128)} %bitcast.me, bf16[3,24,128,128]{3,2,1,0:T(8,128)(2,1)S(1)} %get-tuple-element.80.table.table_in, bf16[8,3,2,256,128]{4,3,2,1,0:T(8,128)(2,1)} %all-to-all-done.1.refs_0_), custom_call_target="tpu_custom_call" | custom-call | tf_op jit(solution)/shard_map/prepare/pallas_call | solution.py:453
  170.5 28.9 %attend.3 = (bf16[8,3,256,128]{3,2,1,0:T(8,128)(2,1)S(1)}, bf16[4,3,128,128]{3,2,1,0:T(8,128)(2,1)S(1)}, bf16[4,3,128,128]{3,2,1,0:T(8,128)(2,1)S(1)}, bf16[3,24...) custom-call(s32[3,16,8]{2,1,0:T(8,128)S(1)} %get-tuple-element.112.l, ...), custom_call_target="tpu_custom_call", output_to_operand_aliasing={{3}: (4, {}), {4}: (5, {}), {5}: (6, {})} | custom-call | tf_op jit(solution)/shard_map/attend/pallas_call | solution.py:609
  199.4 1.3 collective-permute-start.15
  200.7 9.0 %collective-permute-start.16 = (bf16[4,3,128,128]{3,2,1,0:T(8,128)(2,1)S(1)}, bf16[4,3,128,128]{3,2,1,0:T(8,128)(2,1)S(1)}, u32[]{:S(2)}, u32[]{:S(2)}) collective-permute-start(bf16[4,3,128,128]{3,2,1,0:T(8,128)(2,1)S(1)} %get-tuple-element.87), channel_id=1, source_target_pairs={{0,8},{8,16},{16,24},{1,9},{9,17},{17,25},{2,10},{10,18},{18,26},{... | collective-permute-start | bytes 1179656 | tf_op jit(solution)/shard_map/ppermute | solution.py:29
  209.7 1.1 collective-permute-done.16.earlier
  210.8 2.6 finish.3
  213.4 3.0 collective-permute-start.22
  216.8 1.9 collective-permute-start.18
  218.8 3.0 collective-permute-start.19
  222.1 2.4 collective-permute-done.22.refs_2_
  224.4 6.8 %collective-permute-done.23.refs_3_ = bf16[3,2,256,128]{3,2,1,0:T(8,128)(2,1)S(1)} collective-permute-done((bf16[3,2,256,128]{3,2,1,0:T(8,128)(2,1)}, bf16[3,2,256,128]{3,2,1,0:T(8,128)(2,1)S(1)}, u32[]{:S(2)}, u32[]{:S(2)}) %collective-permute-start.23) | collective-permute-done | bytes 393248 | tf_op jit(solution)/shard_map/ppermute | solution.py:72
  232.0 48.4 %collective-permute-start.17 = (bf16[3,2,256,128]{3,2,1,0:T(8,128)(2,1)}, bf16[3,2,256,128]{3,2,1,0:T(8,128)(2,1)}, u32[]{:S(2)}, u32[]{:S(2)}) collective-permute-start(bf16[3,2,256,128]{3,2,1,0:T(8,128)(2,1)} %get-tuple-element.88), channel_id=1, source_target_pairs={{0,4},{1,5},{2,6},{3,7},{4,0},{5,1},{6,2},{7,3},{8,12},{9,13},{10,... | collective-permute-start | bytes 1179656 | tf_op jit(solution)/shard_map/ppermute | solution.py:72
  280.4 1.6 copy-done
  282.0 3.0 unpack.1
  285.1 2.6 unpack_items.3
  287.7 4.6 %collective-permute-done.18.refs_1_ = bf16[3,2,256,128]{3,2,1,0:T(8,128)(2,1)S(1)} collective-permute-done((bf16[3,2,256,128]{3,2,1,0:T(8,128)(2,1)}, bf16[3,2,256,128]{3,2,1,0:T(8,128)(2,1)S(1)}, u32[]{:S(2)}, u32[]{:S(2)}) %collective-permute-start.18) | collective-permute-done | bytes 393248 | tf_op jit(solution)/shard_map/ppermute | solution.py:72
  293.1 2.9 unpack_items.4
  296.0 8.3 %collective-permute-done.17.refs_1_ = bf16[3,2,256,128]{3,2,1,0:T(8,128)(2,1)} collective-permute-done((bf16[3,2,256,128]{3,2,1,0:T(8,128)(2,1)}, bf16[3,2,256,128]{3,2,1,0:T(8,128)(2,1)}, u32[]{:S(2)}, u32[]{:S(2)}) %collective-permute-start.17) | collective-permute-done | bytes 393248 | tf_op jit(solution)/shard_map/ppermute | solution.py:72
  304.3 2.0 unpack_items.5
  (61 shorter events, 5.6 us)
Async XLA Ops:
  0.6 7.7 %copy-start.11 = (s32[6,16,8]{1,2,0:T(8,128)S(1)}, s32[6,16,8]{1,2,0:T(8,128)}, u32[]{:S(2)}) copy-start(s32[6,16,8]{1,2,0:T(8,128)} %param.9) | copy-start | bytes 9220
  4.6 15.0 %collective-permute-start.2 = (bf16[3,2,256,128]{3,2,1,0:T(8,128)(2,1)}, bf16[3,2,256,128]{3,2,1,0:T(8,128)(2,1)S(1)}, u32[]{:S(2)}, u32[]{:S(2)}) collective-permute-start(bf16[3,2,256,128]{3,2,1,0:T(8,128)(2,1)} %get-tuple-element.60), channel_id=1, source_target_pairs={{0,7},{1,6},{2,5},{3,4},{4,3},{5,2},{6,1},{7,0},{8,15},{9,14},{10,... | collective-permute-start | bytes 1179656 | tf_op jit(solution)/shard_map/ppermute | solution.py:72
  8.2 49.8 %collective-permute-start.3 = (bf16[3,2,256,128]{3,2,1,0:T(8,128)(2,1)}, bf16[3,2,256,128]{3,2,1,0:T(8,128)(2,1)S(1)}, u32[]{:S(2)}, u32[]{:S(2)}) collective-permute-start(bf16[3,2,256,128]{3,2,1,0:T(8,128)(2,1)} %get-tuple-element.61), channel_id=1, source_target_pairs={{0,6},{1,7},{2,4},{3,5},{4,2},{5,3},{6,0},{7,1},{8,14},{9,15},{10,... | collective-permute-start | bytes 1179656 | tf_op jit(solution)/shard_map/ppermute | solution.py:72
  10.0 5.8 %collective-permute-start.1 = (s32[4]{0:T(128)S(1)}, s32[4]{0:T(128)S(1)}, u32[]{:S(2)}, u32[]{:S(2)}) collective-permute-start(s32[4]{0:T(128)S(1)} %get-tuple-element.117), channel_id=1, source_target_pairs={{0,8},{8,16},{16,24},{1,9},{9,17},{17,25},{2,10},{10,18},{18,26},{... | collective-permute-start | bytes 56 | tf_op jit(solution)/shard_map/ppermute | solution.py:29
  12.8 5.2 %collective-permute-start = (s32[4]{0:T(128)S(1)}, s32[4]{0:T(128)S(1)}, u32[]{:S(2)}, u32[]{:S(2)}) collective-permute-start(s32[4]{0:T(128)S(1)} %get-tuple-element.115), channel_id=1, source_target_pairs={{8,0},{16,8},{24,16},{9,1},{17,9},{25,17},{10,2},{18,10},{26,18},{... | collective-permute-start | bytes 56 | tf_op jit(solution)/shard_map/ppermute | solution.py:29
  14.1 59.2 %collective-permute-start.4 = (bf16[3,2,256,128]{3,2,1,0:T(8,128)(2,1)}, bf16[3,2,256,128]{3,2,1,0:T(8,128)(2,1)S(1)}, u32[]{:S(2)}, u32[]{:S(2)}) collective-permute-start(bf16[3,2,256,128]{3,2,1,0:T(8,128)(2,1)} %get-tuple-element.62), channel_id=1, source_target_pairs={{0,5},{1,4},{2,7},{3,6},{4,1},{5,0},{6,3},{7,2},{8,13},{9,12},{10,... | collective-permute-start | bytes 1179656 | tf_op jit(solution)/shard_map/ppermute | solution.py:72
  15.9 64.2 %collective-permute-start.5 = (bf16[3,2,256,128]{3,2,1,0:T(8,128)(2,1)}, bf16[3,2,256,128]{3,2,1,0:T(8,128)(2,1)S(1)}, u32[]{:S(2)}, u32[]{:S(2)}) collective-permute-start(bf16[3,2,256,128]{3,2,1,0:T(8,128)(2,1)} %get-tuple-element.63), channel_id=1, source_target_pairs={{0,4},{1,5},{2,6},{3,7},{4,0},{5,1},{6,2},{7,3},{8,12},{9,13},{10,... | collective-permute-start | bytes 1179656 | tf_op jit(solution)/shard_map/ppermute | solution.py:72
  18.0 62.0 %collective-permute-start.6 = (bf16[3,2,256,128]{3,2,1,0:T(8,128)(2,1)}, bf16[3,2,256,128]{3,2,1,0:T(8,128)(2,1)S(1)}, u32[]{:S(2)}, u32[]{:S(2)}) collective-permute-start(bf16[3,2,256,128]{3,2,1,0:T(8,128)(2,1)} %get-tuple-element.64), channel_id=1, source_target_pairs={{0,3},{1,2},{2,1},{3,0},{4,7},{5,6},{6,5},{7,4},{8,11},{9,10},{10,... | collective-permute-start | bytes 1179656 | tf_op jit(solution)/shard_map/ppermute | solution.py:72
  19.6 43.3 %copy-start.1 = (bf16[3,2,256,128]{3,2,1,0:T(8,128)(2,1)}, bf16[3,2,256,128]{3,2,1,0:T(8,128)(2,1)S(1)}, u32[]{:S(2)}) copy-start(bf16[3,2,256,128]{3,2,1,0:T(8,128)(2,1)S(1)} %collective-permute-done.2.refs_0_.refs_1_) | copy-start | bytes 1179652
  19.6 62.7 %collective-permute-start.7 = (bf16[3,2,256,128]{3,2,1,0:T(8,128)(2,1)}, bf16[3,2,256,128]{3,2,1,0:T(8,128)(2,1)S(1)}, u32[]{:S(2)}, u32[]{:S(2)}) collective-permute-start(bf16[3,2,256,128]{3,2,1,0:T(8,128)(2,1)} %get-tuple-element.65), channel_id=1, source_target_pairs={{0,2},{1,3},{2,0},{3,1},{4,6},{5,7},{6,4},{7,5},{8,10},{9,11},{10,... | collective-permute-start | bytes 1179656 | tf_op jit(solution)/shard_map/ppermute | solution.py:72
  58.0 4.9 %copy-start.2 = (bf16[3,2,256,128]{3,2,1,0:T(8,128)(2,1)}, bf16[3,2,256,128]{3,2,1,0:T(8,128)(2,1)S(1)}, u32[]{:S(2)}) copy-start(bf16[3,2,256,128]{3,2,1,0:T(8,128)(2,1)S(1)} %collective-permute-done.3.refs_1_.refs_2_) | copy-start | bytes 1179652
  58.0 24.3 %collective-permute-start.8 = (bf16[3,2,256,128]{3,2,1,0:T(8,128)(2,1)}, bf16[3,2,256,128]{3,2,1,0:T(8,128)(2,1)S(1)}, u32[]{:S(2)}, u32[]{:S(2)}) collective-permute-start(bf16[3,2,256,128]{3,2,1,0:T(8,128)(2,1)} %get-tuple-element.66), channel_id=1, source_target_pairs={{0,1},{1,0},{2,3},{3,2},{4,5},{5,4},{6,7},{7,6},{8,9},{9,8},{10,11... | collective-permute-start | bytes 1179656 | tf_op jit(solution)/shard_map/ppermute | solution.py:72
  73.4 8.9 %copy-start.3 = (bf16[3,2,256,128]{3,2,1,0:T(8,128)(2,1)}, bf16[3,2,256,128]{3,2,1,0:T(8,128)(2,1)S(1)}, u32[]{:S(2)}) copy-start(bf16[3,2,256,128]{3,2,1,0:T(8,128)(2,1)S(1)} %collective-permute-done.4.refs_2_.refs_3_) | copy-start | bytes 1179652
  80.0 2.3 copy-start.4
  80.0 2.3 copy-start.5
  82.3 0.8 copy-start.6
  83.0 0.8 copy-start.7
  83.8 73.6 %all-to-all-start.1 = ((bf16[8,3,2,256,128]{4,3,2,1,0:T(8,128)(2,1)}), bf16[8,3,2,256,128]{4,3,2,1,0:T(8,128)(2,1)}, u32[]{:S(2)}, u32[]{:S(2)}) async-start(bf16[8,3,2,256,128]{4,3,2,1,0:T(8,128)(2,1)} %hold.1), calls=%async_computation.1 | async-start | bytes 6291456 | tf_op jit(solution)/shard_map/all_to_all | solution.py:67
  90.8 8.3 %collective-permute-start.10 = (bf16[4,3,128,128]{3,2,1,0:T(8,128)(2,1)S(1)}, bf16[4,3,128,128]{3,2,1,0:T(8,128)(2,1)S(1)}, u32[]{:S(2)}, u32[]{:S(2)}) collective-permute-start(bf16[4,3,128,128]{3,2,1,0:T(8,128)(2,1)S(1)} %get-tuple-element.69), channel_id=1, source_target_pairs={{8,0},{16,8},{24,16},{9,1},{17,9},{25,17},{10,2},{18,10},{26,18},{... | collective-permute-start | bytes 1179656 | tf_op jit(solution)/shard_map/ppermute | solution.py:29
  92.1 7.0 %collective-permute-start.9 = (bf16[4,3,128,128]{3,2,1,0:T(8,128)(2,1)S(1)}, bf16[4,3,128,128]{3,2,1,0:T(8,128)(2,1)S(1)}, u32[]{:S(2)}, u32[]{:S(2)}) collective-permute-start(bf16[4,3,128,128]{3,2,1,0:T(8,128)(2,1)S(1)} %get-tuple-element.68), channel_id=1, source_target_pairs={{0,8},{8,16},{16,24},{1,9},{9,17},{17,25},{2,10},{10,18},{18,26},{... | collective-permute-start | bytes 1179656 | tf_op jit(solution)/shard_map/ppermute | solution.py:29
  128.2 5.6 %collective-permute-start.11 = (bf16[4,3,128,128]{3,2,1,0:T(8,128)(2,1)S(1)}, bf16[4,3,128,128]{3,2,1,0:T(8,128)(2,1)S(1)}, u32[]{:S(2)}, u32[]{:S(2)}) collective-permute-start(bf16[4,3,128,128]{3,2,1,0:T(8,128)(2,1)S(1)} %get-tuple-element.76), channel_id=1, source_target_pairs={{8,0},{16,8},{24,16},{9,1},{17,9},{25,17},{10,2},{18,10},{26,18},{... | collective-permute-start | bytes 1179656 | tf_op jit(solution)/shard_map/ppermute | solution.py:29
  129.5 5.6 %collective-permute-start.12 = (bf16[4,3,128,128]{3,2,1,0:T(8,128)(2,1)S(1)}, bf16[4,3,128,128]{3,2,1,0:T(8,128)(2,1)S(1)}, u32[]{:S(2)}, u32[]{:S(2)}) collective-permute-start(bf16[4,3,128,128]{3,2,1,0:T(8,128)(2,1)S(1)} %get-tuple-element.77), channel_id=1, source_target_pairs={{0,8},{8,16},{16,24},{1,9},{9,17},{17,25},{2,10},{10,18},{18,26},{... | collective-permute-start | bytes 1179656 | tf_op jit(solution)/shard_map/ppermute | solution.py:29
  157.4 122.9 %all-to-all-start = ((bf16[8,3,2,256,128]{4,3,2,1,0:T(8,128)(2,1)}), bf16[8,3,2,256,128]{4,3,2,1,0:T(8,128)(2,1)S(1)}, u32[]{:S(2)}, u32[]{:S(2)}) async-start(bf16[8,3,2,256,128]{4,3,2,1,0:T(8,128)(2,1)} %finish.2.refs_1_), calls=%async_computation | async-start | bytes 6291456 | tf_op jit(solution)/shard_map/all_to_all | solution.py:67
  163.8 6.6 %collective-permute-start.13 = (bf16[4,3,128,128]{3,2,1,0:T(8,128)(2,1)S(1)}, bf16[4,3,128,128]{3,2,1,0:T(8,128)(2,1)S(1)}, u32[]{:S(2)}, u32[]{:S(2)}) collective-permute-start(bf16[4,3,128,128]{3,2,1,0:T(8,128)(2,1)S(1)} %get-tuple-element.78), channel_id=1, source_target_pairs={{0,8},{8,16},{16,24},{1,9},{9,17},{17,25},{2,10},{10,18},{18,26},{... | collective-permute-start | bytes 1179656 | tf_op jit(solution)/shard_map/ppermute | solution.py:29
  165.2 5.3 %collective-permute-start.14 = (bf16[4,3,128,128]{3,2,1,0:T(8,128)(2,1)S(1)}, bf16[4,3,128,128]{3,2,1,0:T(8,128)(2,1)S(1)}, u32[]{:S(2)}, u32[]{:S(2)}) collective-permute-start(bf16[4,3,128,128]{3,2,1,0:T(8,128)(2,1)S(1)} %get-tuple-element.79), channel_id=1, source_target_pairs={{8,0},{16,8},{24,16},{9,1},{17,9},{25,17},{10,2},{18,10},{26,18},{... | collective-permute-start | bytes 1179656 | tf_op jit(solution)/shard_map/ppermute | solution.py:29
  199.4 10.3 %collective-permute-start.15 = (bf16[4,3,128,128]{3,2,1,0:T(8,128)(2,1)S(1)}, bf16[4,3,128,128]{3,2,1,0:T(8,128)(2,1)S(1)}, u32[]{:S(2)}, u32[]{:S(2)}) collective-permute-start(bf16[4,3,128,128]{3,2,1,0:T(8,128)(2,1)S(1)} %get-tuple-element.86), channel_id=1, source_target_pairs={{8,0},{16,8},{24,16},{9,1},{17,9},{25,17},{10,2},{18,10},{26,18},{... | collective-permute-start | bytes 1179656 | tf_op jit(solution)/shard_map/ppermute | solution.py:29
  200.7 10.1 %collective-permute-start.16 = (bf16[4,3,128,128]{3,2,1,0:T(8,128)(2,1)S(1)}, bf16[4,3,128,128]{3,2,1,0:T(8,128)(2,1)S(1)}, u32[]{:S(2)}, u32[]{:S(2)}) collective-permute-start(bf16[4,3,128,128]{3,2,1,0:T(8,128)(2,1)S(1)} %get-tuple-element.87), channel_id=1, source_target_pairs={{0,8},{8,16},{16,24},{1,9},{9,17},{17,25},{2,10},{10,18},{18,26},{... | collective-permute-start | bytes 1179656 | tf_op jit(solution)/shard_map/ppermute | solution.py:29
  213.4 11.0 %collective-permute-start.22 = (bf16[3,2,256,128]{3,2,1,0:T(8,128)(2,1)}, bf16[3,2,256,128]{3,2,1,0:T(8,128)(2,1)S(1)}, u32[]{:S(2)}, u32[]{:S(2)}) collective-permute-start(bf16[3,2,256,128]{3,2,1,0:T(8,128)(2,1)} %get-tuple-element.94), channel_id=1, source_target_pairs={{0,7},{1,6},{2,5},{3,4},{4,3},{5,2},{6,1},{7,0},{8,15},{9,14},{10,... | collective-permute-start | bytes 1179656 | tf_op jit(solution)/shard_map/ppermute | solution.py:72
  216.5 14.7 %collective-permute-start.23 = (bf16[3,2,256,128]{3,2,1,0:T(8,128)(2,1)}, bf16[3,2,256,128]{3,2,1,0:T(8,128)(2,1)S(1)}, u32[]{:S(2)}, u32[]{:S(2)}) collective-permute-start(bf16[3,2,256,128]{3,2,1,0:T(8,128)(2,1)} %get-tuple-element.95), channel_id=1, source_target_pairs={{0,6},{1,7},{2,4},{3,5},{4,2},{5,3},{6,0},{7,1},{8,14},{9,15},{10,... | collective-permute-start | bytes 1179656 | tf_op jit(solution)/shard_map/ppermute | solution.py:72
  216.8 75.5 %collective-permute-start.18 = (bf16[3,2,256,128]{3,2,1,0:T(8,128)(2,1)}, bf16[3,2,256,128]{3,2,1,0:T(8,128)(2,1)S(1)}, u32[]{:S(2)}, u32[]{:S(2)}) collective-permute-start(bf16[3,2,256,128]{3,2,1,0:T(8,128)(2,1)} %get-tuple-element.89), channel_id=1, source_target_pairs={{0,5},{1,4},{2,7},{3,6},{4,1},{5,0},{6,3},{7,2},{8,13},{9,12},{10,... | collective-permute-start | bytes 1179656 | tf_op jit(solution)/shard_map/ppermute | solution.py:72
  218.8 73.5 %collective-permute-start.19 = (bf16[3,2,256,128]{3,2,1,0:T(8,128)(2,1)}, bf16[3,2,256,128]{3,2,1,0:T(8,128)(2,1)}, u32[]{:S(2)}, u32[]{:S(2)}) collective-permute-start(bf16[3,2,256,128]{3,2,1,0:T(8,128)(2,1)} %get-tuple-element.90), channel_id=1, source_target_pairs={{0,3},{1,2},{2,1},{3,0},{4,7},{5,6},{6,5},{7,4},{8,11},{9,10},{10,... | collective-permute-start | bytes 1179656 | tf_op jit(solution)/shard_map/ppermute | solution.py:72
  221.8 70.5 %collective-permute-start.20 = (bf16[3,2,256,128]{3,2,1,0:T(8,128)(2,1)}, bf16[3,2,256,128]{3,2,1,0:T(8,128)(2,1)}, u32[]{:S(2)}, u32[]{:S(2)}) collective-permute-start(bf16[3,2,256,128]{3,2,1,0:T(8,128)(2,1)} %get-tuple-element.91), channel_id=1, source_target_pairs={{0,2},{1,3},{2,0},{3,1},{4,6},{5,7},{6,4},{7,5},{8,10},{9,11},{10,... | collective-permute-start | bytes 1179656 | tf_op jit(solution)/shard_map/ppermute | solution.py:72
  224.4 6.8 %copy-start.9 = (bf16[3,2,256,128]{3,2,1,0:T(8,128)(2,1)}, bf16[3,2,256,128]{3,2,1,0:T(8,128)(2,1)S(1)}, u32[]{:S(2)}) copy-start(bf16[3,2,256,128]{3,2,1,0:T(8,128)(2,1)S(1)} %collective-permute-done.22.refs_2_) | copy-start | bytes 1179652
  224.4 67.9 %collective-permute-start.21 = (bf16[3,2,256,128]{3,2,1,0:T(8,128)(2,1)}, bf16[3,2,256,128]{3,2,1,0:T(8,128)(2,1)}, u32[]{:S(2)}, u32[]{:S(2)}) collective-permute-start(bf16[3,2,256,128]{3,2,1,0:T(8,128)(2,1)} %get-tuple-element.92), channel_id=1, source_target_pairs={{0,1},{1,0},{2,3},{3,2},{4,5},{5,4},{6,7},{7,6},{8,9},{9,8},{10,11... | collective-permute-start | bytes 1179656 | tf_op jit(solution)/shard_map/ppermute | solution.py:72
  231.2 0.8 copy-start.10
  232.0 72.3 %collective-permute-start.17 = (bf16[3,2,256,128]{3,2,1,0:T(8,128)(2,1)}, bf16[3,2,256,128]{3,2,1,0:T(8,128)(2,1)}, u32[]{:S(2)}, u32[]{:S(2)}) collective-permute-start(bf16[3,2,256,128]{3,2,1,0:T(8,128)(2,1)} %get-tuple-element.88), channel_id=1, source_target_pairs={{0,4},{1,5},{2,6},{3,7},{4,0},{5,1},{6,2},{7,3},{8,12},{9,13},{10,... | collective-permute-start | bytes 1179656 | tf_op jit(solution)/shard_map/ppermute | solution.py:72
  280.4 1.6 copy-start
  292.3 0.8 copy-start.8

commit v12 on v11

--- a/solution.py
+++ b/solution.py
@@ -43,23 +43,6 @@
     if apart:
         return [pltpu.HBM(shape, dtype)] * peers
     return [pltpu.HBM((peers,) + shape, dtype)]
-
-
-def hold_kernel(*refs):
-    del refs
-
-
-def hold(arrays, after):
-    count = len(arrays)
-    anywhere = pl.BlockSpec(memory_space=pltpu.HBM)
-    return pl.pallas_call(
-        hold_kernel,
-        in_specs=[anywhere] * (count + len(after)),
-        out_specs=[anywhere] * count,
-        out_shape=[pltpu.HBM(x.shape, x.dtype) for x in arrays],
-        input_output_aliases={i: i for i in range(count)},
-        name="hold",
-    )(*[in_hbm(x) for x in (*arrays, *after)])
 
 
 def exchange(messages):
@@ -73,99 +56,73 @@
     return received
 
 
-def pack_kernel(
-    me, query, key, value, d_out, *refs, first, heads, items, apart, per_peer, head_dim
-):
-    messages = refs[-4 - (len(items) if apart else 1) : -4]
-    stage, ready, in_sems, out_sems = refs[-4:]
+def pack_kernel(query, key, value, d_out, *refs, first, heads, per_peer, head_dim):
+    message, stage, ready, in_sems, out_sems = refs[-5:]
     sources = (key, value, query, d_out)
-    aligned = apart and per_peer % LANES == 0
-    at_once = aligned or not apart
-    peers = stage.shape[1]
-
-    def place_of(item):
-        if apart:
-            return messages[item - items[0]], me[0] ^ (peers - 1 - item)
-        return messages[0].at[item], item
-
-    def span(item):
-        if aligned:
-            base, begin = pl.multiple_of(place_of(item)[1] * per_peer, LANES), first
-        else:
-            base, begin = 0, item * per_peer + first
+    peers = message.shape[0]
+
+    def span(peer):
+        begin = peer * per_peer + first
         low = begin // LANES * LANES
         high = -(-(begin + heads * head_dim) // LANES) * LANES
-        return base + low, high - low, begin - low
-
-    def fetch(item, i):
-        low, width, _ = span(item)
+        return low, high - low, begin - low
+
+    def fetch(peer, i):
+        low, width, _ = span(peer)
         return pltpu.make_async_copy(
             sources[i].at[:, pl.ds(low, width)],
-            stage.at[i, item, :, pl.ds(0, width)],
-            in_sems.at[i, item],
-        )
-
-    def send(item):
-        target, peer = place_of(item)
-        return pltpu.make_async_copy(
-            ready.at[item if aligned else peer], target, out_sems.at[item]
-        )
-
-    made = items if at_once else range(peers)
-    for item in made:
+            stage.at[i, peer, :, pl.ds(0, width)],
+            in_sems.at[i, peer],
+        )
+
+    def send(peer):
+        return pltpu.make_async_copy(ready.at[peer], message.at[peer], out_sems.at[peer])
+
+    for peer in range(peers):
         for i in range(4):
-            fetch(item, i).start()
-    for item in made:
+            fetch(peer, i).start()
+    for peer in range(peers):
         for i in range(4):
-            fetch(item, i).wait()
-        at = span(item)[2]
+            fetch(peer, i).wait()
+        at = span(peer)[2]
         for head in range(heads):
             lanes = slice(at + head * head_dim, at + (head + 1) * head_dim)
             for kind in range(2):
-                ready[item, head, kind] = jnp.concatenate(
-                    [stage[2 * kind, item, :, lanes], stage[2 * kind + 1, item, :, lanes]],
+                ready[peer, head, kind] = jnp.concatenate(
+                    [stage[2 * kind, peer, :, lanes], stage[2 * kind + 1, peer, :, lanes]],
                     axis=1,
                 )
-        if at_once:
-            send(item).start()
-    if not at_once:
-        for item in items:
-            send(item).start()
-    for item in items:
-        send(item).wait()
-
-
-def pack(me, arrays, start, heads, heads_here, peers, head_dim, apart, after):
+        send(peer).start()
+    for peer in range(peers):
+        send(peer).wait()
+
+
+def pack(arrays, start, heads, heads_here, peers, head_dim, after):
     rows = arrays[0].shape[0]
     dtype = arrays[0].dtype
-    shape = (heads, 2, rows, 2 * head_dim)
+    shape = (peers, heads, 2, rows, 2 * head_dim)
     width = (-(-heads * head_dim // LANES) + 1) * LANES
     anywhere = pl.BlockSpec(memory_space=pltpu.HBM)
-    outs = message_outs(peers, shape, dtype, apart)
     return pl.pallas_call(
         functools.partial(
             pack_kernel,
             first=start * head_dim,
             heads=heads,
-            items=range(peers),
-            apart=apart,
             per_peer=heads_here * head_dim,
             head_dim=head_dim,
         ),
-        in_specs=[pl.BlockSpec(memory_space=pltpu.SMEM)]
-        + [anywhere] * 4
-        + [pl.BlockSpec(memory_space=pl.ANY)] * len(after),
-        out_specs=[anywhere] * len(outs),
-        out_shape=outs,
+        in_specs=[anywhere] * 4 + [pl.BlockSpec(memory_space=pl.ANY)] * len(after),
+        out_specs=[anywhere],
+        out_shape=[pltpu.HBM(shape, dtype)],
         scratch_shapes=[
             pltpu.VMEM((4, peers, rows, width), dtype),
-            pltpu.VMEM((peers,) + shape, dtype),
+            pltpu.VMEM(shape, dtype),
             pltpu.SemaphoreType.DMA((4, peers)),
             pltpu.SemaphoreType.DMA((peers,)),
         ],
         compiler_params=pltpu.CompilerParams(vmem_limit_bytes=SMALL_VMEM),
         name="pack",
-    )(me, *[in_hbm(x) for x in arrays], *after)
+    )(*[in_hbm(x) for x in arrays], *after)
 
 
 def unpack_kernel(me, *refs, chunk, peers, counts, earlier, jobs):
@@ -729,11 +686,7 @@
     came = []
     for chunk, (start, size) in enumerate(zip(starts, sizes)):
         after = (asked, local_ids) if came else ()
-        packed = pack(
-            me, arrays, start, size, heads_here, peers, head_dim, chunk == 0, after
-        )
-        if chunk == 1:
-            packed = hold(packed, came[0][:-1])
+        packed = pack(arrays, start, size, heads_here, peers, head_dim, after)
         came.append(exchange(packed))
     received = []
     outs = finished = ()
@@ -754,8 +707,8 @@
             half = peers // 2
             parts = (
                 [peers - 1, *range(half // 2)],
-                [*range(half // 2, half - 1), *range(half, peers - 1)],
-                [half - 1],
+                list(range(half // 2, half)),
+                list(range(half, peers - 1)),
             )
             for items in parts:
                 outs = unpack_items(me, received, starts, heads_here, items, outs)

time: 307 us -> 307 us (level)
  the two profiles are of different devices: /device:TPU:2 before, /device:TPU:8 now
where the time goes in v12:
time: 307 us; the launch traced here: 303 us
  waiting for transfers between devices  142 us (46%)
  Pallas kernels  94.3 us (31%)
  starting transfers between devices  58.1 us (19%)
  local copies, waits for them, and re-layouts  4.37 us (1%)
    all_to_all x3, waiting for transfers between devices, exchange(): lax.all_to_all(messages[0], 'seq', split_axis=0, concat_axis=0, tiled=True)  70.3 us
    ppermute x7, waiting for transfers between devices, exchange(): received[item] = lax.ppermute(messages[item], 'seq', pairs)  65.6 us
    pallas_call x2, Pallas kernels, attend(): pl.pallas_call(functools.partial(attend_kernel, head_dim=lanes // 2, per_...  58.5 us
    ppermute x10, starting transfers between devices, from_behind(): return lax.ppermute(x, axis, pairs)  28.4 us
    all_to_all x3, starting transfers between devices, exchange(): lax.all_to_all(messages[0], 'seq', split_axis=0, concat_axis=0, tiled=True)  19.3 us
    ppermute x7, starting transfers between devices, exchange(): received[item] = lax.ppermute(messages[item], 'seq', pairs)  10.4 us
    pallas_call x2, Pallas kernels, pack(): pl.pallas_call(functools.partial(pack_kernel, first=start * head_dim, hea...  7.81 us
    pallas_call x2, Pallas kernels, prepare(): pl.pallas_call(functools.partial(prepare_kernel, peers=peers), in_specs=[...  7.78 us
  transfers between devices with their start and end apart: 20, of which 10 were waited for; matrix products, arithmetic and copies ran while one was open for 1% of the time, Pallas kernels for 29%

profile of v12, /device:TPU:8, one launch (start us, length us, event | category | flops | bytes accessed | tf_op | source)
XLA Modules:
  0.0 302.5 jit_solution(16164815516279344300)
XLA Ops:
  0.6 3.9 %pack.2 = bf16[8,3,2,256,128]{4,3,2,1,0:T(8,128)(2,1)} custom-call(bf16[256,3072]{1,0:T(8,128)(2,1)} %query.3, bf16[256,3072]{1,0:T(8,128)(2,1)} %key.3, bf16[256,3072]{1,0:T(8,128)(2,1)} %value.3, bf16[256,3072]{1,0:T(8,128)(2,1)} %d_out.3), custom_call_target="tpu_custom_call" | custom-call | tf_op jit(solution)/shard_map/pack/pallas_call | solution.py:106
  4.6 6.3 %all-to-all-start = ((bf16[8,3,2,256,128]{4,3,2,1,0:T(8,128)(2,1)}), bf16[8,3,2,256,128]{4,3,2,1,0:T(8,128)(2,1)S(1)}, u32[]{:S(2)}, u32[]{:S(2)}) async-start(bf16[8,3,2,256,128]{4,3,2,1,0:T(8,128)(2,1)} %pack.2), calls=%async_computation | async-start | bytes 6291456 | tf_op jit(solution)/shard_map/all_to_all | solution.py:50
  11.0 0.2 compare_reduce_fusion.1
  11.2 1.2 top_k.24
  12.5 1.3 collective-permute-start.1
  13.8 1.2 top_k.17
  15.0 1.3 collective-permute-start
  16.6 3.2 %collective-permute-done = s32[4]{0:T(128)S(1)} collective-permute-done((s32[4]{0:T(128)S(1)}, s32[4]{0:T(128)S(1)}, u32[]{:S(2)}, u32[]{:S(2)}) %collective-permute-start) | collective-permute-done | bytes 48 | tf_op jit(solution)/shard_map/ppermute | solution.py:29
  19.9 3.9 %pack.3 = bf16[8,3,2,256,128]{4,3,2,1,0:T(8,128)(2,1)} custom-call(bf16[256,3072]{1,0:T(8,128)(2,1)} %query.3, bf16[256,3072]{1,0:T(8,128)(2,1)} %key.3, bf16[256,3072]{1,0:T(8,128)(2,1)} %value.3, bf16[256,3072]{1,0:T(8,128)(2,1)} %d_out.3, s32[8]{0:T(128)S(1)} %pad_add_fusion.asked.refs_0_, s32[6,16,8]{2,1,0:T(8,128)S(1)} %select_select_fusion.refs_1_), custom_call_target="tpu_custom_call" | custom-call | tf_op jit(solution)/shard_map/pack/pallas_call | solution.py:106
  23.8 55.3 %all-to-all-done.refs_0_ = bf16[8,3,2,256,128]{4,3,2,1,0:T(8,128)(2,1)S(1)} async-done(((bf16[8,3,2,256,128]{4,3,2,1,0:T(8,128)(2,1)}), bf16[8,3,2,256,128]{4,3,2,1,0:T(8,128)(2,1)S(1)}, u32[]{:S(2)}, u32[]{:S(2)}) %all-to-all-start) | async-done | bytes 3145760 | tf_op jit(solution)/shard_map/all_to_all | solution.py:50
  79.1 1.6 copy-done.1
  80.7 6.8 %all-to-all-start.2 = ((bf16[8,3,2,256,128]{4,3,2,1,0:T(8,128)(2,1)}), bf16[8,3,2,256,128]{4,3,2,1,0:T(8,128)(2,1)}, u32[]{:S(2)}, u32[]{:S(2)}) async-start(bf16[8,3,2,256,128]{4,3,2,1,0:T(8,128)(2,1)} %pack.3), calls=%async_computation.2 | async-start | bytes 6291456 | tf_op jit(solution)/shard_map/all_to_all | solution.py:50
  87.5 2.2 pick.2
  89.7 1.3 collective-permute-start.2
  91.1 1.3 collective-permute-start.3
  92.4 3.9 %prepare.2 = (bf16[3,24,128,128]{3,2,1,0:T(8,128)(2,1)S(1)}, bf16[8,3,256,128]{3,2,1,0:T(8,128)(2,1)S(1)}, f32[3,24,128,128]{3,2,1,0:T(8,128)S(1)}) custom-call(s32[1]{0:T(128)} %bitcast.me, bf16[3,24,128,128]{3,2,1,0:T(8,128)(2,1)S(1)} %get-tuple-element.54.table.table_in, bf16[8,3,2,256,128]{4,3,2,1,0:T(8,128)(2,1)} %copy-done.1), custom_call_target="tpu_custom_call" | custom-call | tf_op jit(solution)/shard_map/prepare/pallas_call | solution.py:410
  96.3 0.1 collective-permute-done.3.came_next
  96.4 29.6 %attend.2 = (bf16[8,3,256,128]{3,2,1,0:T(8,128)(2,1)S(1)}, bf16[4,3,128,128]{3,2,1,0:T(8,128)(2,1)S(1)}, bf16[4,3,128,128]{3,2,1,0:T(8,128)(2,1)S(1)}, bf16[3,24...) custom-call(s32[3,16,8]{2,1,0:T(8,128)S(1)} %get-tuple-element.97.li, ...), custom_call_target="tpu_custom_call", output_to_operand_aliasing={{3}: (4, {}), {4}: (5, {}), {5}: (6, {})} | custom-call | tf_op jit(solution)/shard_map/attend/pallas_call | solution.py:566
  126.0 1.3 collective-permute-start.4
  127.3 8.9 %collective-permute-start.5 = (bf16[4,3,128,128]{3,2,1,0:T(8,128)(2,1)S(1)}, bf16[4,3,128,128]{3,2,1,0:T(8,128)(2,1)S(1)}, u32[]{:S(2)}, u32[]{:S(2)}) collective-permute-start(bf16[4,3,128,128]{3,2,1,0:T(8,128)(2,1)S(1)} %get-tuple-element.61), channel_id=1, source_target_pairs={{0,8},{8,16},{16,24},{1,9},{9,17},{17,25},{2,10},{10,18},{18,26},{... | collective-permute-start | bytes 1179656 | tf_op jit(solution)/shard_map/ppermute | solution.py:29
  136.3 1.3 collective-permute-done.5.earlier
  137.6 2.6 finish.2.refs_1_
  140.2 15.0 %all-to-all-done.2.refs_0_ = bf16[8,3,2,256,128]{4,3,2,1,0:T(8,128)(2,1)} async-done(((bf16[8,3,2,256,128]{4,3,2,1,0:T(8,128)(2,1)}), bf16[8,3,2,256,128]{4,3,2,1,0:T(8,128)(2,1)}, u32[]{:S(2)}, u32[]{:S(2)}) %all-to-all-start.2) | async-done | bytes 3145760 | tf_op jit(solution)/shard_map/all_to_all | solution.py:50
  155.3 6.2 %all-to-all-start.1 = ((bf16[8,3,2,256,128]{4,3,2,1,0:T(8,128)(2,1)}), bf16[8,3,2,256,128]{4,3,2,1,0:T(8,128)(2,1)S(1)}, u32[]{:S(2)}, u32[]{:S(2)}) async-start(bf16[8,3,2,256,128]{4,3,2,1,0:T(8,128)(2,1)} %finish.2.refs_1_), calls=%async_computation.1 | async-start | bytes 6291456 | tf_op jit(solution)/shard_map/all_to_all | solution.py:50
  161.5 2.2 pick.3
  163.7 1.4 collective-permute-start.6
  165.0 1.3 collective-permute-start.7
  166.3 3.9 %prepare.3 = (bf16[3,24,128,128]{3,2,1,0:T(8,128)(2,1)S(1)}, bf16[8,3,256,128]{3,2,1,0:T(8,128)(2,1)S(1)}, f32[3,24,128,128]{3,2,1,0:T(8,128)S(1)}) custom-call(s32[1]{0:T(128)} %bitcast.me, bf16[3,24,128,128]{3,2,1,0:T(8,128)(2,1)S(1)} %get-tuple-element.64.table.table_in, bf16[8,3,2,256,128]{4,3,2,1,0:T(8,128)(2,1)} %all-to-all-done.2.refs_0_), custom_call_target="tpu_custom_call" | custom-call | tf_op jit(solution)/shard_map/prepare/pallas_call | solution.py:410
  170.3 28.9 %attend.3 = (bf16[8,3,256,128]{3,2,1,0:T(8,128)(2,1)S(1)}, bf16[4,3,128,128]{3,2,1,0:T(8,128)(2,1)S(1)}, bf16[4,3,128,128]{3,2,1,0:T(8,128)(2,1)S(1)}, bf16[3,24...) custom-call(s32[3,16,8]{2,1,0:T(8,128)S(1)} %get-tuple-element.96.li, ...), custom_call_target="tpu_custom_call", output_to_operand_aliasing={{3}: (4, {}), {4}: (5, {}), {5}: (6, {})} | custom-call | tf_op jit(solution)/shard_map/attend/pallas_call | solution.py:566
  199.2 1.3 collective-permute-start.8
  200.5 9.0 %collective-permute-start.9 = (bf16[4,3,128,128]{3,2,1,0:T(8,128)(2,1)S(1)}, bf16[4,3,128,128]{3,2,1,0:T(8,128)(2,1)S(1)}, u32[]{:S(2)}, u32[]{:S(2)}) collective-permute-start(bf16[4,3,128,128]{3,2,1,0:T(8,128)(2,1)S(1)} %get-tuple-element.71), channel_id=1, source_target_pairs={{0,8},{8,16},{16,24},{1,9},{9,17},{17,25},{2,10},{10,18},{18,26},{... | collective-permute-start | bytes 1179656 | tf_op jit(solution)/shard_map/ppermute | solution.py:29
  209.6 1.1 collective-permute-done.9.earlier
  210.7 2.6 finish.3
  213.3 2.4 collective-permute-start.15
  215.7 0.6 collective-permute-start.16
  216.3 3.9 %collective-permute-start.13 = (bf16[3,2,256,128]{3,2,1,0:T(8,128)(2,1)}, bf16[3,2,256,128]{3,2,1,0:T(8,128)(2,1)S(1)}, u32[]{:S(2)}, u32[]{:S(2)}) collective-permute-start(bf16[3,2,256,128]{3,2,1,0:T(8,128)(2,1)} %get-tuple-element.75), channel_id=1, source_target_pairs={{0,5},{1,4},{2,7},{3,6},{4,1},{5,0},{6,3},{7,2},{8,13},{9,12},{10,... | collective-permute-start | bytes 1179656 | tf_op jit(solution)/shard_map/ppermute | solution.py:55
  220.2 0.3 collective-permute-start.14
  220.5 2.0 collective-permute-start.10
  222.5 52.5 %collective-permute-done.15.refs_2_ = bf16[3,2,256,128]{3,2,1,0:T(8,128)(2,1)S(1)} collective-permute-done((bf16[3,2,256,128]{3,2,1,0:T(8,128)(2,1)}, bf16[3,2,256,128]{3,2,1,0:T(8,128)(2,1)S(1)}, u32[]{:S(2)}, u32[]{:S(2)}) %collective-permute-start.15) | collective-permute-done | bytes 393248 | tf_op jit(solution)/shard_map/ppermute | solution.py:55
  275.0 7.8 %collective-permute-done.16.refs_3_ = bf16[3,2,256,128]{3,2,1,0:T(8,128)(2,1)S(1)} collective-permute-done((bf16[3,2,256,128]{3,2,1,0:T(8,128)(2,1)}, bf16[3,2,256,128]{3,2,1,0:T(8,128)(2,1)S(1)}, u32[]{:S(2)}, u32[]{:S(2)}) %collective-permute-start.16) | collective-permute-done | bytes 393248 | tf_op jit(solution)/shard_map/ppermute | solution.py:55
  282.7 0.7 copy-done.4
  283.4 1.2 collective-permute-start.12
  284.7 1.6 copy-done
  286.3 3.0 %unpack.1 = (bf16[256,3072]{1,0:T(8,128)(2,1)}, bf16[256,3072]{1,0:T(8,128)(2,1)}, bf16[256,3072]{1,0:T(8,128)(2,1)}, bf16[256,3072]{1,0:T(8,128)(2,1)}) custom-call(s32[1]{0:T(128)} %bitcast.me, bf16[8,3,2,256,128]{4,3,2,1,0:T(8,128)(2,1)} %copy-done), custom_call_target="tpu_custom_call" | custom-call | tf_op jit(solution)/shard_map/unpack/pallas_call | solution.py:208
  289.4 2.6 unpack_items.3
  292.0 5.4 %collective-permute-done.14.refs_2_ = bf16[3,2,256,128]{3,2,1,0:T(8,128)(2,1)} collective-permute-done((bf16[3,2,256,128]{3,2,1,0:T(8,128)(2,1)}, bf16[3,2,256,128]{3,2,1,0:T(8,128)(2,1)}, u32[]{:S(2)}, u32[]{:S(2)}) %collective-permute-start.14) | collective-permute-done | bytes 393248 | tf_op jit(solution)/shard_map/ppermute | solution.py:55
  297.4 2.3 unpack_items.4
  299.7 2.6 unpack_items.5
  (36 shorter events, 0.6 us)
Async XLA Ops:
  4.5 6.3 %copy-start.5 = (s32[6,16,8]{1,2,0:T(8,128)S(1)}, s32[6,16,8]{1,2,0:T(8,128)}, u32[]{:S(2)}) copy-start(s32[6,16,8]{1,2,0:T(8,128)} %param.9) | copy-start | bytes 9220
  4.6 74.5 %all-to-all-start = ((bf16[8,3,2,256,128]{4,3,2,1,0:T(8,128)(2,1)}), bf16[8,3,2,256,128]{4,3,2,1,0:T(8,128)(2,1)S(1)}, u32[]{:S(2)}, u32[]{:S(2)}) async-start(bf16[8,3,2,256,128]{4,3,2,1,0:T(8,128)(2,1)} %pack.2), calls=%async_computation | async-start | bytes 6291456 | tf_op jit(solution)/shard_map/all_to_all | solution.py:50
  12.5 4.1 %collective-permute-start.1 = (s32[4]{0:T(128)S(1)}, s32[4]{0:T(128)S(1)}, u32[]{:S(2)}, u32[]{:S(2)}) collective-permute-start(s32[4]{0:T(128)S(1)} %get-tuple-element.101), channel_id=1, source_target_pairs={{0,8},{8,16},{16,24},{1,9},{9,17},{17,25},{2,10},{10,18},{18,26},{... | collective-permute-start | bytes 56 | tf_op jit(solution)/shard_map/ppermute | solution.py:29
  15.0 4.8 %collective-permute-start = (s32[4]{0:T(128)S(1)}, s32[4]{0:T(128)S(1)}, u32[]{:S(2)}, u32[]{:S(2)}) collective-permute-start(s32[4]{0:T(128)S(1)} %get-tuple-element.99), channel_id=1, source_target_pairs={{8,0},{16,8},{24,16},{9,1},{17,9},{25,17},{10,2},{18,10},{26,18},{... | collective-permute-start | bytes 56 | tf_op jit(solution)/shard_map/ppermute | solution.py:29
  79.1 1.7 copy-start.1
  80.7 74.5 %all-to-all-start.2 = ((bf16[8,3,2,256,128]{4,3,2,1,0:T(8,128)(2,1)}), bf16[8,3,2,256,128]{4,3,2,1,0:T(8,128)(2,1)}, u32[]{:S(2)}, u32[]{:S(2)}) async-start(bf16[8,3,2,256,128]{4,3,2,1,0:T(8,128)(2,1)} %pack.3), calls=%async_computation.2 | async-start | bytes 6291456 | tf_op jit(solution)/shard_map/all_to_all | solution.py:50
  89.7 6.5 %collective-permute-start.2 = (bf16[4,3,128,128]{3,2,1,0:T(8,128)(2,1)S(1)}, bf16[4,3,128,128]{3,2,1,0:T(8,128)(2,1)S(1)}, u32[]{:S(2)}, u32[]{:S(2)}) collective-permute-start(bf16[4,3,128,128]{3,2,1,0:T(8,128)(2,1)S(1)} %get-tuple-element.52), channel_id=1, source_target_pairs={{0,8},{8,16},{16,24},{1,9},{9,17},{17,25},{2,10},{10,18},{18,26},{... | collective-permute-start | bytes 1179656 | tf_op jit(solution)/shard_map/ppermute | solution.py:29
  91.1 5.3 %collective-permute-start.3 = (bf16[4,3,128,128]{3,2,1,0:T(8,128)(2,1)S(1)}, bf16[4,3,128,128]{3,2,1,0:T(8,128)(2,1)S(1)}, u32[]{:S(2)}, u32[]{:S(2)}) collective-permute-start(bf16[4,3,128,128]{3,2,1,0:T(8,128)(2,1)S(1)} %get-tuple-element.53), channel_id=1, source_target_pairs={{8,0},{16,8},{24,16},{9,1},{17,9},{25,17},{10,2},{18,10},{26,18},{... | collective-permute-start | bytes 1179656 | tf_op jit(solution)/shard_map/ppermute | solution.py:29
  126.0 10.2 %collective-permute-start.4 = (bf16[4,3,128,128]{3,2,1,0:T(8,128)(2,1)S(1)}, bf16[4,3,128,128]{3,2,1,0:T(8,128)(2,1)S(1)}, u32[]{:S(2)}, u32[]{:S(2)}) collective-permute-start(bf16[4,3,128,128]{3,2,1,0:T(8,128)(2,1)S(1)} %get-tuple-element.60), channel_id=1, source_target_pairs={{8,0},{16,8},{24,16},{9,1},{17,9},{25,17},{10,2},{18,10},{26,18},{... | collective-permute-start | bytes 1179656 | tf_op jit(solution)/shard_map/ppermute | solution.py:29
  127.3 10.3 %collective-permute-start.5 = (bf16[4,3,128,128]{3,2,1,0:T(8,128)(2,1)S(1)}, bf16[4,3,128,128]{3,2,1,0:T(8,128)(2,1)S(1)}, u32[]{:S(2)}, u32[]{:S(2)}) collective-permute-start(bf16[4,3,128,128]{3,2,1,0:T(8,128)(2,1)S(1)} %get-tuple-element.61), channel_id=1, source_target_pairs={{0,8},{8,16},{16,24},{1,9},{9,17},{17,25},{2,10},{10,18},{18,26},{... | collective-permute-start | bytes 1179656 | tf_op jit(solution)/shard_map/ppermute | solution.py:29
  155.3 129.4 %all-to-all-start.1 = ((bf16[8,3,2,256,128]{4,3,2,1,0:T(8,128)(2,1)}), bf16[8,3,2,256,128]{4,3,2,1,0:T(8,128)(2,1)S(1)}, u32[]{:S(2)}, u32[]{:S(2)}) async-start(bf16[8,3,2,256,128]{4,3,2,1,0:T(8,128)(2,1)} %finish.2.refs_1_), calls=%async_computation.1 | async-start | bytes 6291456 | tf_op jit(solution)/shard_map/all_to_all | solution.py:50
  163.7 6.6 %collective-permute-start.6 = (bf16[4,3,128,128]{3,2,1,0:T(8,128)(2,1)S(1)}, bf16[4,3,128,128]{3,2,1,0:T(8,128)(2,1)S(1)}, u32[]{:S(2)}, u32[]{:S(2)}) collective-permute-start(bf16[4,3,128,128]{3,2,1,0:T(8,128)(2,1)S(1)} %get-tuple-element.62), channel_id=1, source_target_pairs={{0,8},{8,16},{16,24},{1,9},{9,17},{17,25},{2,10},{10,18},{18,26},{... | collective-permute-start | bytes 1179656 | tf_op jit(solution)/shard_map/ppermute | solution.py:29
  165.0 5.3 %collective-permute-start.7 = (bf16[4,3,128,128]{3,2,1,0:T(8,128)(2,1)S(1)}, bf16[4,3,128,128]{3,2,1,0:T(8,128)(2,1)S(1)}, u32[]{:S(2)}, u32[]{:S(2)}) collective-permute-start(bf16[4,3,128,128]{3,2,1,0:T(8,128)(2,1)S(1)} %get-tuple-element.63), channel_id=1, source_target_pairs={{8,0},{16,8},{24,16},{9,1},{17,9},{25,17},{10,2},{18,10},{26,18},{... | collective-permute-start | bytes 1179656 | tf_op jit(solution)/shard_map/ppermute | solution.py:29
  199.2 10.3 %collective-permute-start.8 = (bf16[4,3,128,128]{3,2,1,0:T(8,128)(2,1)S(1)}, bf16[4,3,128,128]{3,2,1,0:T(8,128)(2,1)S(1)}, u32[]{:S(2)}, u32[]{:S(2)}) collective-permute-start(bf16[4,3,128,128]{3,2,1,0:T(8,128)(2,1)S(1)} %get-tuple-element.70), channel_id=1, source_target_pairs={{8,0},{16,8},{24,16},{9,1},{17,9},{25,17},{10,2},{18,10},{26,18},{... | collective-permute-start | bytes 1179656 | tf_op jit(solution)/shard_map/ppermute | solution.py:29
  200.5 10.1 %collective-permute-start.9 = (bf16[4,3,128,128]{3,2,1,0:T(8,128)(2,1)S(1)}, bf16[4,3,128,128]{3,2,1,0:T(8,128)(2,1)S(1)}, u32[]{:S(2)}, u32[]{:S(2)}) collective-permute-start(bf16[4,3,128,128]{3,2,1,0:T(8,128)(2,1)S(1)} %get-tuple-element.71), channel_id=1, source_target_pairs={{0,8},{8,16},{16,24},{1,9},{9,17},{17,25},{2,10},{10,18},{18,26},{... | collective-permute-start | bytes 1179656 | tf_op jit(solution)/shard_map/ppermute | solution.py:29
  213.3 61.7 %collective-permute-start.15 = (bf16[3,2,256,128]{3,2,1,0:T(8,128)(2,1)}, bf16[3,2,256,128]{3,2,1,0:T(8,128)(2,1)S(1)}, u32[]{:S(2)}, u32[]{:S(2)}) collective-permute-start(bf16[3,2,256,128]{3,2,1,0:T(8,128)(2,1)} %get-tuple-element.78), channel_id=1, source_target_pairs={{0,7},{1,6},{2,5},{3,4},{4,3},{5,2},{6,1},{7,0},{8,15},{9,14},{10,... | collective-permute-start | bytes 1179656 | tf_op jit(solution)/shard_map/ppermute | solution.py:55
  215.7 67.0 %collective-permute-start.16 = (bf16[3,2,256,128]{3,2,1,0:T(8,128)(2,1)}, bf16[3,2,256,128]{3,2,1,0:T(8,128)(2,1)S(1)}, u32[]{:S(2)}, u32[]{:S(2)}) collective-permute-start(bf16[3,2,256,128]{3,2,1,0:T(8,128)(2,1)} %get-tuple-element.79), channel_id=1, source_target_pairs={{0,6},{1,7},{2,4},{3,5},{4,2},{5,3},{6,0},{7,1},{8,14},{9,15},{10,... | collective-permute-start | bytes 1179656 | tf_op jit(solution)/shard_map/ppermute | solution.py:55
  216.3 75.7 %collective-permute-start.13 = (bf16[3,2,256,128]{3,2,1,0:T(8,128)(2,1)}, bf16[3,2,256,128]{3,2,1,0:T(8,128)(2,1)S(1)}, u32[]{:S(2)}, u32[]{:S(2)}) collective-permute-start(bf16[3,2,256,128]{3,2,1,0:T(8,128)(2,1)} %get-tuple-element.75), channel_id=1, source_target_pairs={{0,5},{1,4},{2,7},{3,6},{4,1},{5,0},{6,3},{7,2},{8,13},{9,12},{10,... | collective-permute-start | bytes 1179656 | tf_op jit(solution)/shard_map/ppermute | solution.py:55
  220.2 77.2 %collective-permute-start.14 = (bf16[3,2,256,128]{3,2,1,0:T(8,128)(2,1)}, bf16[3,2,256,128]{3,2,1,0:T(8,128)(2,1)}, u32[]{:S(2)}, u32[]{:S(2)}) collective-permute-start(bf16[3,2,256,128]{3,2,1,0:T(8,128)(2,1)} %get-tuple-element.76), channel_id=1, source_target_pairs={{0,4},{1,5},{2,6},{3,7},{4,0},{5,1},{6,2},{7,3},{8,12},{9,13},{10,... | collective-permute-start | bytes 1179656 | tf_op jit(solution)/shard_map/ppermute | solution.py:55
  220.5 79.3 %collective-permute-start.10 = (bf16[3,2,256,128]{3,2,1,0:T(8,128)(2,1)}, bf16[3,2,256,128]{3,2,1,0:T(8,128)(2,1)}, u32[]{:S(2)}, u32[]{:S(2)}) collective-permute-start(bf16[3,2,256,128]{3,2,1,0:T(8,128)(2,1)} %get-tuple-element.72), channel_id=1, source_target_pairs={{0,3},{1,2},{2,1},{3,0},{4,7},{5,6},{6,5},{7,4},{8,11},{9,10},{10,... | collective-permute-start | bytes 1179656 | tf_op jit(solution)/shard_map/ppermute | solution.py:55
  275.0 7.8 %copy-start.3 = (bf16[3,2,256,128]{3,2,1,0:T(8,128)(2,1)}, bf16[3,2,256,128]{3,2,1,0:T(8,128)(2,1)S(1)}, u32[]{:S(2)}) copy-start(bf16[3,2,256,128]{3,2,1,0:T(8,128)(2,1)S(1)} %collective-permute-done.15.refs_2_) | copy-start | bytes 1179652
  275.0 24.8 %collective-permute-start.11 = (bf16[3,2,256,128]{3,2,1,0:T(8,128)(2,1)}, bf16[3,2,256,128]{3,2,1,0:T(8,128)(2,1)}, u32[]{:S(2)}, u32[]{:S(2)}) collective-permute-start(bf16[3,2,256,128]{3,2,1,0:T(8,128)(2,1)} %get-tuple-element.73), channel_id=1, source_target_pairs={{0,2},{1,3},{2,0},{3,1},{4,6},{5,7},{6,4},{7,5},{8,10},{9,11},{10,... | collective-permute-start | bytes 1179656 | tf_op jit(solution)/shard_map/ppermute | solution.py:55
  282.7 0.7 copy-start.4
  283.4 16.3 %collective-permute-start.12 = (bf16[3,2,256,128]{3,2,1,0:T(8,128)(2,1)}, bf16[3,2,256,128]{3,2,1,0:T(8,128)(2,1)}, u32[]{:S(2)}, u32[]{:S(2)}) collective-permute-start(bf16[3,2,256,128]{3,2,1,0:T(8,128)(2,1)} %get-tuple-element.74), channel_id=1, source_target_pairs={{0,1},{1,0},{2,3},{3,2},{4,5},{5,4},{6,7},{7,6},{8,9},{9,8},{10,11... | collective-permute-start | bytes 1179656 | tf_op jit(solution)/shard_map/ppermute | solution.py:55
  284.7 1.7 copy-start
  292.0 5.4 %copy-start.2 = (bf16[3,2,256,128]{3,2,1,0:T(8,128)(2,1)}, bf16[3,2,256,128]{3,2,1,0:T(8,128)(2,1)S(1)}, u32[]{:S(2)}) copy-start(bf16[3,2,256,128]{3,2,1,0:T(8,128)(2,1)S(1)} %collective-permute-done.13.refs_1_) | copy-start | bytes 1179652

commit v13 on v12

--- a/solution.py
+++ b/solution.py
@@ -215,7 +215,8 @@
             jobs=jobs,
         ),
         in_specs=[pl.BlockSpec(memory_space=pltpu.SMEM)]
-        + [anywhere] * (len(flat) + len(earlier)),
+        + [pl.BlockSpec(memory_space=pl.ANY)] * len(flat)
+        + [anywhere] * len(earlier),
         out_specs=[anywhere] * 4,
         out_shape=[pltpu.HBM((rows, columns), dtype)] * 4,
         input_output_aliases={1 + len(flat) + i: i for i in range(len(earlier))},
@@ -227,7 +228,7 @@
         ],
         compiler_params=pltpu.CompilerParams(vmem_limit_bytes=SMALL_VMEM),
         name="unpack",
-    )(me, *[in_hbm(x) for x in (*flat, *earlier)])
+    )(me, *flat, *[in_hbm(x) for x in earlier])
 
 
 def unpack_items_kernel(me, *refs, items, peers, counts, joint, earlier, jobs, per_peer):
@@ -315,7 +316,8 @@
             per_peer=per_peer,
         ),
         in_specs=[pl.BlockSpec(memory_space=pltpu.SMEM)]
-        + [anywhere] * (len(flat) + len(earlier)),
+        + [pl.BlockSpec(memory_space=pl.ANY)] * len(flat)
+        + [anywhere] * len(earlier),
         out_specs=[anywhere] * 4,
         out_shape=[pltpu.HBM((rows, peers * per_peer), dtype)] * 4,
         input_output_aliases={1 + len(flat) + i: i for i in range(len(earlier))},
@@ -329,7 +331,7 @@
         ],
         compiler_params=pltpu.CompilerParams(vmem_limit_bytes=SMALL_VMEM),
         name="unpack_items",
-    )(me, *[in_hbm(x) for x in (*flat, *earlier)])
+    )(me, *flat, *[in_hbm(x) for x in earlier])
 
 
 def pick_kernel(me, asked, *refs, count):
@@ -365,13 +367,13 @@
     return pl.pallas_call(
         functools.partial(pick_kernel, count=len(messages)),
         in_specs=[pl.BlockSpec(memory_space=pltpu.SMEM)] * 2
-        + [pl.BlockSpec(memory_space=pltpu.HBM)] * (len(messages) + len(after)),
+        + [pl.BlockSpec(memory_space=pl.ANY)] * (len(messages) + len(after)),
         out_specs=[pl.BlockSpec(memory_space=pltpu.VMEM)] * 3,
         out_shape=[picked, picked, pltpu.VMEM((heads, window, block_rows, lanes), dtype)],
         scratch_shapes=[pltpu.SemaphoreType.DMA((peers, each))],
         compiler_params=pltpu.CompilerParams(vmem_limit_bytes=SMALL_VMEM),
         name="pick",
-    )(me, asked, *[in_hbm(x) for x in (*messages, *after)])
+    )(me, asked, *messages, *[in_hbm(x) for x in after])
 
 
 def prepare_kernel(me, table, *refs, peers):
@@ -410,7 +412,7 @@
     return pl.pallas_call(
         functools.partial(prepare_kernel, peers=peers),
         in_specs=[pl.BlockSpec(memory_space=pltpu.SMEM), inside]
-        + [pl.BlockSpec(memory_space=pltpu.HBM)] * len(messages),
+        + [pl.BlockSpec(memory_space=pl.ANY)] * len(messages),
         out_specs=[inside] * 3,
         out_shape=[
             pltpu.VMEM((heads, window, lanes, block_rows), dtype),
@@ -420,7 +422,7 @@
         scratch_shapes=[pltpu.SemaphoreType.DMA((peers,))],
         compiler_params=pltpu.CompilerParams(vmem_limit_bytes=SMALL_VMEM),
         name="prepare",
-    )(me, in_vmem(table), *[in_hbm(x) for x in messages])
+    )(me, in_vmem(table), *messages)
 
 
 def attend_kernel(
@@ -681,7 +683,6 @@
     )
 
     me = lax.axis_index("seq").astype(jnp.int32).reshape(1)
-    me = lax.axis_index("seq").astype(jnp.int32).reshape(1)
     last = chunks - 1
     came = []
     for chunk, (start, size) in enumerate(zip(starts, sizes)):
@@ -707,8 +708,8 @@
             half = peers // 2
             parts = (
                 [peers - 1, *range(half // 2)],
-                list(range(half // 2, half)),
-                list(range(half, peers - 1)),
+                list(range(half // 2, half - 1)),
+                list(range(half - 1, peers - 1)),
             )
             for items in parts:
                 outs = unpack_items(me, received, starts, heads_here, items, outs)

time: 307 us -> 306 us (level)
  no operation moved by 1% of the time
where the time goes in v13:
time: 306 us; the launch traced here: 301 us
  waiting for transfers between devices  144 us (47%)
  Pallas kernels  93.6 us (31%)
  starting transfers between devices  57.5 us (19%)
    all_to_all x3, waiting for transfers between devices, exchange(): lax.all_to_all(messages[0], 'seq', split_axis=0, concat_axis=0, tiled=True)  71.3 us
    ppermute x7, waiting for transfers between devices, exchange(): received[item] = lax.ppermute(messages[item], 'seq', pairs)  67.5 us
    pallas_call x2, Pallas kernels, attend(): pl.pallas_call(functools.partial(attend_kernel, head_dim=lanes // 2, per_...  58.3 us
    ppermute x10, starting transfers between devices, from_behind(): return lax.ppermute(x, axis, pairs)  27.8 us
    all_to_all x3, starting transfers between devices, exchange(): lax.all_to_all(messages[0], 'seq', split_axis=0, concat_axis=0, tiled=True)  19.3 us
    ppermute x7, starting transfers between devices, exchange(): received[item] = lax.ppermute(messages[item], 'seq', pairs)  10.4 us
    pallas_call x2, Pallas kernels, prepare(): pl.pallas_call(functools.partial(prepare_kernel, peers=peers), in_specs=[...  8.45 us
    pallas_call x3, Pallas kernels, unpack_items(): pl.pallas_call(functools.partial(unpack_items_kernel, items=items, peers=...  7.9 us
  transfers between devices with their start and end apart: 20, of which 10 were waited for; matrix products, arithmetic and copies ran while one was open for 1% of the time, Pallas kernels for 29%

profile of v13, /device:TPU:8, one launch (start us, length us, event | category | flops | bytes accessed | tf_op | source)
XLA Modules:
  0.0 301.4 jit_solution(15145090056118779883)
XLA Ops:
  0.6 3.9 %pack.2 = bf16[8,3,2,256,128]{4,3,2,1,0:T(8,128)(2,1)} custom-call(bf16[256,3072]{1,0:T(8,128)(2,1)} %query.3, bf16[256,3072]{1,0:T(8,128)(2,1)} %key.3, bf16[256,3072]{1,0:T(8,128)(2,1)} %value.3, bf16[256,3072]{1,0:T(8,128)(2,1)} %d_out.3), custom_call_target="tpu_custom_call" | custom-call | tf_op jit(solution)/shard_map/pack/pallas_call | solution.py:106
  4.6 6.3 %all-to-all-start = ((bf16[8,3,2,256,128]{4,3,2,1,0:T(8,128)(2,1)}), bf16[8,3,2,256,128]{4,3,2,1,0:T(8,128)(2,1)S(1)}, u32[]{:S(2)}, u32[]{:S(2)}) async-start(bf16[8,3,2,256,128]{4,3,2,1,0:T(8,128)(2,1)} %pack.2), calls=%async_computation | async-start | bytes 6291456 | tf_op jit(solution)/shard_map/all_to_all | solution.py:50
  10.9 0.1 eq.22
  11.0 0.2 compare_reduce_fusion.1
  11.2 1.2 top_k.24
  12.5 1.3 collective-permute-start.1
  13.8 1.2 top_k.17
  15.0 1.3 collective-permute-start
  16.6 3.2 %collective-permute-done = s32[4]{0:T(128)S(1)} collective-permute-done((s32[4]{0:T(128)S(1)}, s32[4]{0:T(128)S(1)}, u32[]{:S(2)}, u32[]{:S(2)}) %collective-permute-start) | collective-permute-done | bytes 48 | tf_op jit(solution)/shard_map/ppermute | solution.py:29
  19.9 3.9 %pack.3 = bf16[8,3,2,256,128]{4,3,2,1,0:T(8,128)(2,1)} custom-call(bf16[256,3072]{1,0:T(8,128)(2,1)} %query.3, bf16[256,3072]{1,0:T(8,128)(2,1)} %key.3, bf16[256,3072]{1,0:T(8,128)(2,1)} %value.3, bf16[256,3072]{1,0:T(8,128)(2,1)} %d_out.3, s32[8]{0:T(128)S(1)} %pad_add_fusion.asked.refs_0_, s32[6,16,8]{2,1,0:T(8,128)S(1)} %select_select_fusion.refs_1_), custom_call_target="tpu_custom_call" | custom-call | tf_op jit(solution)/shard_map/pack/pallas_call | solution.py:106
  23.8 55.3 %all-to-all-done.refs_0_ = bf16[8,3,2,256,128]{4,3,2,1,0:T(8,128)(2,1)S(1)} async-done(((bf16[8,3,2,256,128]{4,3,2,1,0:T(8,128)(2,1)}), bf16[8,3,2,256,128]{4,3,2,1,0:T(8,128)(2,1)S(1)}, u32[]{:S(2)}, u32[]{:S(2)}) %all-to-all-start) | async-done | bytes 3145760 | tf_op jit(solution)/shard_map/all_to_all | solution.py:50
  79.1 6.8 %all-to-all-start.2 = ((bf16[8,3,2,256,128]{4,3,2,1,0:T(8,128)(2,1)}), bf16[8,3,2,256,128]{4,3,2,1,0:T(8,128)(2,1)}, u32[]{:S(2)}, u32[]{:S(2)}) async-start(bf16[8,3,2,256,128]{4,3,2,1,0:T(8,128)(2,1)} %pack.3), calls=%async_computation.2 | async-start | bytes 6291456 | tf_op jit(solution)/shard_map/all_to_all | solution.py:50
  85.9 1.4 pick.2
  87.3 1.3 collective-permute-start.2
  88.7 1.3 collective-permute-start.3
  90.0 4.6 %prepare.2 = (bf16[3,24,128,128]{3,2,1,0:T(8,128)(2,1)S(1)}, bf16[8,3,256,128]{3,2,1,0:T(8,128)(2,1)S(1)}, f32[3,24,128,128]{3,2,1,0:T(8,128)S(1)}) custom-call(s32[1]{0:T(128)} %bitcast.me, bf16[3,24,128,128]{3,2,1,0:T(8,128)(2,1)S(1)} %get-tuple-element.54.table.table_in, bf16[8,3,2,256,128]{4,3,2,1,0:T(8,128)(2,1)S(1)} %all-to-all-done.refs_0_), custom_call_target="tpu_custom_call" | custom-call | tf_op jit(solution)/shard_map/prepare/pallas_call | solution.py:412
  94.6 29.4 %attend.2 = (bf16[8,3,256,128]{3,2,1,0:T(8,128)(2,1)S(1)}, bf16[4,3,128,128]{3,2,1,0:T(8,128)(2,1)S(1)}, bf16[4,3,128,128]{3,2,1,0:T(8,128)(2,1)S(1)}, bf16[3,24...) custom-call(s32[3,16,8]{2,1,0:T(8,128)S(1)} %get-tuple-element.97.li, ...), custom_call_target="tpu_custom_call", output_to_operand_aliasing={{3}: (4, {}), {4}: (5, {}), {5}: (6, {})} | custom-call | tf_op jit(solution)/shard_map/attend/pallas_call | solution.py:568
  124.0 1.3 collective-permute-start.4
  125.3 8.4 %collective-permute-start.5 = (bf16[4,3,128,128]{3,2,1,0:T(8,128)(2,1)S(1)}, bf16[4,3,128,128]{3,2,1,0:T(8,128)(2,1)S(1)}, u32[]{:S(2)}, u32[]{:S(2)}) collective-permute-start(bf16[4,3,128,128]{3,2,1,0:T(8,128)(2,1)S(1)} %get-tuple-element.61), channel_id=1, source_target_pairs={{0,8},{8,16},{16,24},{1,9},{9,17},{17,25},{2,10},{10,18},{18,26},{... | collective-permute-start | bytes 1179656 | tf_op jit(solution)/shard_map/ppermute | solution.py:29
  133.7 1.3 collective-permute-done.5.earlier
  135.0 2.6 finish.2.refs_1_
  137.6 16.0 %all-to-all-done.2.refs_0_ = bf16[8,3,2,256,128]{4,3,2,1,0:T(8,128)(2,1)} async-done(((bf16[8,3,2,256,128]{4,3,2,1,0:T(8,128)(2,1)}), bf16[8,3,2,256,128]{4,3,2,1,0:T(8,128)(2,1)}, u32[]{:S(2)}, u32[]{:S(2)}) %all-to-all-start.2) | async-done | bytes 3145760 | tf_op jit(solution)/shard_map/all_to_all | solution.py:50
  153.6 6.2 %all-to-all-start.1 = ((bf16[8,3,2,256,128]{4,3,2,1,0:T(8,128)(2,1)}), bf16[8,3,2,256,128]{4,3,2,1,0:T(8,128)(2,1)S(1)}, u32[]{:S(2)}, u32[]{:S(2)}) async-start(bf16[8,3,2,256,128]{4,3,2,1,0:T(8,128)(2,1)} %finish.2.refs_1_), calls=%async_computation.1 | async-start | bytes 6291456 | tf_op jit(solution)/shard_map/all_to_all | solution.py:50
  159.8 2.2 pick.3
  162.0 1.4 collective-permute-start.6
  163.4 1.3 collective-permute-start.7
  164.7 3.9 %prepare.3 = (bf16[3,24,128,128]{3,2,1,0:T(8,128)(2,1)S(1)}, bf16[8,3,256,128]{3,2,1,0:T(8,128)(2,1)S(1)}, f32[3,24,128,128]{3,2,1,0:T(8,128)S(1)}) custom-call(s32[1]{0:T(128)} %bitcast.me, bf16[3,24,128,128]{3,2,1,0:T(8,128)(2,1)S(1)} %get-tuple-element.64.table.table_in, bf16[8,3,2,256,128]{4,3,2,1,0:T(8,128)(2,1)} %all-to-all-done.2.refs_0_), custom_call_target="tpu_custom_call" | custom-call | tf_op jit(solution)/shard_map/prepare/pallas_call | solution.py:412
  168.7 28.9 %attend.3 = (bf16[8,3,256,128]{3,2,1,0:T(8,128)(2,1)S(1)}, bf16[4,3,128,128]{3,2,1,0:T(8,128)(2,1)S(1)}, bf16[4,3,128,128]{3,2,1,0:T(8,128)(2,1)S(1)}, bf16[3,24...) custom-call(s32[3,16,8]{2,1,0:T(8,128)S(1)} %get-tuple-element.96.li, ...), custom_call_target="tpu_custom_call", output_to_operand_aliasing={{3}: (4, {}), {4}: (5, {}), {5}: (6, {})} | custom-call | tf_op jit(solution)/shard_map/attend/pallas_call | solution.py:568
  197.6 1.3 collective-permute-start.8
  198.9 9.0 %collective-permute-start.9 = (bf16[4,3,128,128]{3,2,1,0:T(8,128)(2,1)S(1)}, bf16[4,3,128,128]{3,2,1,0:T(8,128)(2,1)S(1)}, u32[]{:S(2)}, u32[]{:S(2)}) collective-permute-start(bf16[4,3,128,128]{3,2,1,0:T(8,128)(2,1)S(1)} %get-tuple-element.71), channel_id=1, source_target_pairs={{0,8},{8,16},{16,24},{1,9},{9,17},{17,25},{2,10},{10,18},{18,26},{... | collective-permute-start | bytes 1179656 | tf_op jit(solution)/shard_map/ppermute | solution.py:29
  207.9 1.1 collective-permute-done.9.earlier
  209.0 2.6 finish.3
  211.6 2.4 collective-permute-start.15
  214.1 0.6 collective-permute-start.16
  214.6 3.9 %collective-permute-start.14 = (bf16[3,2,256,128]{3,2,1,0:T(8,128)(2,1)}, bf16[3,2,256,128]{3,2,1,0:T(8,128)(2,1)}, u32[]{:S(2)}, u32[]{:S(2)}) collective-permute-start(bf16[3,2,256,128]{3,2,1,0:T(8,128)(2,1)} %get-tuple-element.76), channel_id=1, source_target_pairs={{0,5},{1,4},{2,7},{3,6},{4,1},{5,0},{6,3},{7,2},{8,13},{9,12},{10,... | collective-permute-start | bytes 1179656 | tf_op jit(solution)/shard_map/ppermute | solution.py:55
  218.5 0.3 collective-permute-start.10
  218.8 2.0 collective-permute-start.11
  220.8 52.5 %collective-permute-done.15.refs_2_ = bf16[3,2,256,128]{3,2,1,0:T(8,128)(2,1)S(1)} collective-permute-done((bf16[3,2,256,128]{3,2,1,0:T(8,128)(2,1)}, bf16[3,2,256,128]{3,2,1,0:T(8,128)(2,1)S(1)}, u32[]{:S(2)}, u32[]{:S(2)}) %collective-permute-start.15) | collective-permute-done | bytes 393248 | tf_op jit(solution)/shard_map/ppermute | solution.py:55
  273.3 0.7 copy-done.1
  274.0 7.0 %collective-permute-done.16.refs_3_ = bf16[3,2,256,128]{3,2,1,0:T(8,128)(2,1)S(1)} collective-permute-done((bf16[3,2,256,128]{3,2,1,0:T(8,128)(2,1)}, bf16[3,2,256,128]{3,2,1,0:T(8,128)(2,1)S(1)}, u32[]{:S(2)}, u32[]{:S(2)}) %collective-permute-start.16) | collective-permute-done | bytes 393248 | tf_op jit(solution)/shard_map/ppermute | solution.py:55
  281.1 0.7 copy-done.3
  281.8 1.2 collective-permute-start.13
  283.0 2.2 unpack.1
  285.3 2.6 unpack_items.3
  288.0 2.1 unpack_items.4
  290.1 5.6 %collective-permute-done.10.refs_1_ = bf16[3,2,256,128]{3,2,1,0:T(8,128)(2,1)S(1)} collective-permute-done((bf16[3,2,256,128]{3,2,1,0:T(8,128)(2,1)}, bf16[3,2,256,128]{3,2,1,0:T(8,128)(2,1)S(1)}, u32[]{:S(2)}, u32[]{:S(2)}) %collective-permute-start.10) | collective-permute-done | bytes 393248 | tf_op jit(solution)/shard_map/ppermute | solution.py:55
  295.7 2.3 collective-permute-done.12.refs_3_
  298.1 3.1 %unpack_items.5 = (bf16[256,3072]{1,0:T(8,128)(2,1)}, bf16[256,3072]{1,0:T(8,128)(2,1)}, bf16[256,3072]{1,0:T(8,128)(2,1)}, bf16[256,3072]{1,0:T(8,128)(2,1)}) custom-call(s32[1]{0:T(128)} %bitcast.me, bf16[8,3,2,256,128]{4,3,2,1,0:T(8,128)(2,1)S(1)} %all-to-all-done.1.refs_0_, ...), custom_call_target="tpu_custom_call", output_to_operand_aliasing={{0}: (6, {}), {1}: (7, {}), {2}: (8, {}), {3}: (9, {})} | custom-call | tf_op jit(solution)/shard_map/unpack_items/pallas_call | solution.py:307
  (36 shorter events, 0.6 us)
Async XLA Ops:
  4.5 6.3 %copy-start.5 = (s32[6,16,8]{1,2,0:T(8,128)S(1)}, s32[6,16,8]{1,2,0:T(8,128)}, u32[]{:S(2)}) copy-start(s32[6,16,8]{1,2,0:T(8,128)} %param.9) | copy-start | bytes 9220
  4.6 74.5 %all-to-all-start = ((bf16[8,3,2,256,128]{4,3,2,1,0:T(8,128)(2,1)}), bf16[8,3,2,256,128]{4,3,2,1,0:T(8,128)(2,1)S(1)}, u32[]{:S(2)}, u32[]{:S(2)}) async-start(bf16[8,3,2,256,128]{4,3,2,1,0:T(8,128)(2,1)} %pack.2), calls=%async_computation | async-start | bytes 6291456 | tf_op jit(solution)/shard_map/all_to_all | solution.py:50
  12.5 4.1 %collective-permute-start.1 = (s32[4]{0:T(128)S(1)}, s32[4]{0:T(128)S(1)}, u32[]{:S(2)}, u32[]{:S(2)}) collective-permute-start(s32[4]{0:T(128)S(1)} %get-tuple-element.101), channel_id=1, source_target_pairs={{0,8},{8,16},{16,24},{1,9},{9,17},{17,25},{2,10},{10,18},{18,26},{... | collective-permute-start | bytes 56 | tf_op jit(solution)/shard_map/ppermute | solution.py:29
  15.0 4.8 %collective-permute-start = (s32[4]{0:T(128)S(1)}, s32[4]{0:T(128)S(1)}, u32[]{:S(2)}, u32[]{:S(2)}) collective-permute-start(s32[4]{0:T(128)S(1)} %get-tuple-element.99), channel_id=1, source_target_pairs={{8,0},{16,8},{24,16},{9,1},{17,9},{25,17},{10,2},{18,10},{26,18},{... | collective-permute-start | bytes 56 | tf_op jit(solution)/shard_map/ppermute | solution.py:29
  79.1 74.5 %all-to-all-start.2 = ((bf16[8,3,2,256,128]{4,3,2,1,0:T(8,128)(2,1)}), bf16[8,3,2,256,128]{4,3,2,1,0:T(8,128)(2,1)}, u32[]{:S(2)}, u32[]{:S(2)}) async-start(bf16[8,3,2,256,128]{4,3,2,1,0:T(8,128)(2,1)} %pack.3), calls=%async_computation.2 | async-start | bytes 6291456 | tf_op jit(solution)/shard_map/all_to_all | solution.py:50
  87.3 7.2 %collective-permute-start.2 = (bf16[4,3,128,128]{3,2,1,0:T(8,128)(2,1)S(1)}, bf16[4,3,128,128]{3,2,1,0:T(8,128)(2,1)S(1)}, u32[]{:S(2)}, u32[]{:S(2)}) collective-permute-start(bf16[4,3,128,128]{3,2,1,0:T(8,128)(2,1)S(1)} %get-tuple-element.52), channel_id=1, source_target_pairs={{0,8},{8,16},{16,24},{1,9},{9,17},{17,25},{2,10},{10,18},{18,26},{... | collective-permute-start | bytes 1179656 | tf_op jit(solution)/shard_map/ppermute | solution.py:29
  88.7 5.9 %collective-permute-start.3 = (bf16[4,3,128,128]{3,2,1,0:T(8,128)(2,1)S(1)}, bf16[4,3,128,128]{3,2,1,0:T(8,128)(2,1)S(1)}, u32[]{:S(2)}, u32[]{:S(2)}) collective-permute-start(bf16[4,3,128,128]{3,2,1,0:T(8,128)(2,1)S(1)} %get-tuple-element.53), channel_id=1, source_target_pairs={{8,0},{16,8},{24,16},{9,1},{17,9},{25,17},{10,2},{18,10},{26,18},{... | collective-permute-start | bytes 1179656 | tf_op jit(solution)/shard_map/ppermute | solution.py:29
  124.0 9.7 %collective-permute-start.4 = (bf16[4,3,128,128]{3,2,1,0:T(8,128)(2,1)S(1)}, bf16[4,3,128,128]{3,2,1,0:T(8,128)(2,1)S(1)}, u32[]{:S(2)}, u32[]{:S(2)}) collective-permute-start(bf16[4,3,128,128]{3,2,1,0:T(8,128)(2,1)S(1)} %get-tuple-element.60), channel_id=1, source_target_pairs={{8,0},{16,8},{24,16},{9,1},{17,9},{25,17},{10,2},{18,10},{26,18},{... | collective-permute-start | bytes 1179656 | tf_op jit(solution)/shard_map/ppermute | solution.py:29
  125.3 9.7 %collective-permute-start.5 = (bf16[4,3,128,128]{3,2,1,0:T(8,128)(2,1)S(1)}, bf16[4,3,128,128]{3,2,1,0:T(8,128)(2,1)S(1)}, u32[]{:S(2)}, u32[]{:S(2)}) collective-permute-start(bf16[4,3,128,128]{3,2,1,0:T(8,128)(2,1)S(1)} %get-tuple-element.61), channel_id=1, source_target_pairs={{0,8},{8,16},{16,24},{1,9},{9,17},{17,25},{2,10},{10,18},{18,26},{... | collective-permute-start | bytes 1179656 | tf_op jit(solution)/shard_map/ppermute | solution.py:29
  153.6 129.4 %all-to-all-start.1 = ((bf16[8,3,2,256,128]{4,3,2,1,0:T(8,128)(2,1)}), bf16[8,3,2,256,128]{4,3,2,1,0:T(8,128)(2,1)S(1)}, u32[]{:S(2)}, u32[]{:S(2)}) async-start(bf16[8,3,2,256,128]{4,3,2,1,0:T(8,128)(2,1)} %finish.2.refs_1_), calls=%async_computation.1 | async-start | bytes 6291456 | tf_op jit(solution)/shard_map/all_to_all | solution.py:50
  162.0 6.6 %collective-permute-start.6 = (bf16[4,3,128,128]{3,2,1,0:T(8,128)(2,1)S(1)}, bf16[4,3,128,128]{3,2,1,0:T(8,128)(2,1)S(1)}, u32[]{:S(2)}, u32[]{:S(2)}) collective-permute-start(bf16[4,3,128,128]{3,2,1,0:T(8,128)(2,1)S(1)} %get-tuple-element.62), channel_id=1, source_target_pairs={{0,8},{8,16},{16,24},{1,9},{9,17},{17,25},{2,10},{10,18},{18,26},{... | collective-permute-start | bytes 1179656 | tf_op jit(solution)/shard_map/ppermute | solution.py:29
  163.4 5.3 %collective-permute-start.7 = (bf16[4,3,128,128]{3,2,1,0:T(8,128)(2,1)S(1)}, bf16[4,3,128,128]{3,2,1,0:T(8,128)(2,1)S(1)}, u32[]{:S(2)}, u32[]{:S(2)}) collective-permute-start(bf16[4,3,128,128]{3,2,1,0:T(8,128)(2,1)S(1)} %get-tuple-element.63), channel_id=1, source_target_pairs={{8,0},{16,8},{24,16},{9,1},{17,9},{25,17},{10,2},{18,10},{26,18},{... | collective-permute-start | bytes 1179656 | tf_op jit(solution)/shard_map/ppermute | solution.py:29
  197.6 10.3 %collective-permute-start.8 = (bf16[4,3,128,128]{3,2,1,0:T(8,128)(2,1)S(1)}, bf16[4,3,128,128]{3,2,1,0:T(8,128)(2,1)S(1)}, u32[]{:S(2)}, u32[]{:S(2)}) collective-permute-start(bf16[4,3,128,128]{3,2,1,0:T(8,128)(2,1)S(1)} %get-tuple-element.70), channel_id=1, source_target_pairs={{8,0},{16,8},{24,16},{9,1},{17,9},{25,17},{10,2},{18,10},{26,18},{... | collective-permute-start | bytes 1179656 | tf_op jit(solution)/shard_map/ppermute | solution.py:29
  198.9 10.1 %collective-permute-start.9 = (bf16[4,3,128,128]{3,2,1,0:T(8,128)(2,1)S(1)}, bf16[4,3,128,128]{3,2,1,0:T(8,128)(2,1)S(1)}, u32[]{:S(2)}, u32[]{:S(2)}) collective-permute-start(bf16[4,3,128,128]{3,2,1,0:T(8,128)(2,1)S(1)} %get-tuple-element.71), channel_id=1, source_target_pairs={{0,8},{8,16},{16,24},{1,9},{9,17},{17,25},{2,10},{10,18},{18,26},{... | collective-permute-start | bytes 1179656 | tf_op jit(solution)/shard_map/ppermute | solution.py:29
  211.6 61.7 %collective-permute-start.15 = (bf16[3,2,256,128]{3,2,1,0:T(8,128)(2,1)}, bf16[3,2,256,128]{3,2,1,0:T(8,128)(2,1)S(1)}, u32[]{:S(2)}, u32[]{:S(2)}) collective-permute-start(bf16[3,2,256,128]{3,2,1,0:T(8,128)(2,1)} %get-tuple-element.78), channel_id=1, source_target_pairs={{0,7},{1,6},{2,5},{3,4},{4,3},{5,2},{6,1},{7,0},{8,15},{9,14},{10,... | collective-permute-start | bytes 1179656 | tf_op jit(solution)/shard_map/ppermute | solution.py:55
  214.1 67.0 %collective-permute-start.16 = (bf16[3,2,256,128]{3,2,1,0:T(8,128)(2,1)}, bf16[3,2,256,128]{3,2,1,0:T(8,128)(2,1)S(1)}, u32[]{:S(2)}, u32[]{:S(2)}) collective-permute-start(bf16[3,2,256,128]{3,2,1,0:T(8,128)(2,1)} %get-tuple-element.79), channel_id=1, source_target_pairs={{0,6},{1,7},{2,4},{3,5},{4,2},{5,3},{6,0},{7,1},{8,14},{9,15},{10,... | collective-permute-start | bytes 1179656 | tf_op jit(solution)/shard_map/ppermute | solution.py:55
  214.6 73.3 %collective-permute-start.14 = (bf16[3,2,256,128]{3,2,1,0:T(8,128)(2,1)}, bf16[3,2,256,128]{3,2,1,0:T(8,128)(2,1)}, u32[]{:S(2)}, u32[]{:S(2)}) collective-permute-start(bf16[3,2,256,128]{3,2,1,0:T(8,128)(2,1)} %get-tuple-element.76), channel_id=1, source_target_pairs={{0,5},{1,4},{2,7},{3,6},{4,1},{5,0},{6,3},{7,2},{8,13},{9,12},{10,... | collective-permute-start | bytes 1179656 | tf_op jit(solution)/shard_map/ppermute | solution.py:55
  218.5 77.2 %collective-permute-start.10 = (bf16[3,2,256,128]{3,2,1,0:T(8,128)(2,1)}, bf16[3,2,256,128]{3,2,1,0:T(8,128)(2,1)S(1)}, u32[]{:S(2)}, u32[]{:S(2)}) collective-permute-start(bf16[3,2,256,128]{3,2,1,0:T(8,128)(2,1)} %get-tuple-element.72), channel_id=1, source_target_pairs={{0,4},{1,5},{2,6},{3,7},{4,0},{5,1},{6,2},{7,3},{8,12},{9,13},{10,... | collective-permute-start | bytes 1179656 | tf_op jit(solution)/shard_map/ppermute | solution.py:55
  218.8 76.9 %collective-permute-start.11 = (bf16[3,2,256,128]{3,2,1,0:T(8,128)(2,1)}, bf16[3,2,256,128]{3,2,1,0:T(8,128)(2,1)}, u32[]{:S(2)}, u32[]{:S(2)}) collective-permute-start(bf16[3,2,256,128]{3,2,1,0:T(8,128)(2,1)} %get-tuple-element.73), channel_id=1, source_target_pairs={{0,3},{1,2},{2,1},{3,0},{4,7},{5,6},{6,5},{7,4},{8,11},{9,10},{10,... | collective-permute-start | bytes 1179656 | tf_op jit(solution)/shard_map/ppermute | solution.py:55
  273.3 0.7 copy-start.1
  274.0 24.0 %collective-permute-start.12 = (bf16[3,2,256,128]{3,2,1,0:T(8,128)(2,1)}, bf16[3,2,256,128]{3,2,1,0:T(8,128)(2,1)}, u32[]{:S(2)}, u32[]{:S(2)}) collective-permute-start(bf16[3,2,256,128]{3,2,1,0:T(8,128)(2,1)} %get-tuple-element.74), channel_id=1, source_target_pairs={{0,2},{1,3},{2,0},{3,1},{4,6},{5,7},{6,4},{7,5},{8,10},{9,11},{10,... | collective-permute-start | bytes 1179656 | tf_op jit(solution)/shard_map/ppermute | solution.py:55
  281.1 0.7 copy-start.3
  281.8 16.3 %collective-permute-start.13 = (bf16[3,2,256,128]{3,2,1,0:T(8,128)(2,1)}, bf16[3,2,256,128]{3,2,1,0:T(8,128)(2,1)}, u32[]{:S(2)}, u32[]{:S(2)}) collective-permute-start(bf16[3,2,256,128]{3,2,1,0:T(8,128)(2,1)} %get-tuple-element.75), channel_id=1, source_target_pairs={{0,1},{1,0},{2,3},{3,2},{4,5},{5,4},{6,7},{7,6},{8,9},{9,8},{10,11... | collective-permute-start | bytes 1179656 | tf_op jit(solution)/shard_map/ppermute | solution.py:55
  283.0 2.3 copy-start
  283.0 2.3 copy-start.2
  283.0 2.3 copy-start.4

commit v14 on v13

--- a/solution.py
+++ b/solution.py
@@ -706,10 +706,11 @@
         received.append(exchange(finished))
         if chunk == last and heads_here * head_dim % LANES == 0:
             half = peers // 2
+            near = list(range(peers - 2, half - 1, -1))
             parts = (
-                [peers - 1, *range(half // 2)],
-                list(range(half // 2, half - 1)),
-                list(range(half - 1, peers - 1)),
+                [peers - 1, *near[::2]],
+                list(range(half // 2)),
+                [*range(half // 2, half), *near[1::2]],
             )
             for items in parts:
                 outs = unpack_items(me, received, starts, heads_here, items, outs)

time: 306 us -> 304 us (level)
    ppermute x7, waiting for transfers between devices: 67.5 us -> 55.6 us  [exchange(): received[item] = lax.ppermute(messages[item], 'seq', pairs)]
    all_to_all x3, waiting for transfers between devices: 71.3 us -> 81.7 us  [exchange(): lax.all_to_all(messages[0], 'seq', split_axis=0, concat_axis=0, tiled=True)]
  transfers between devices with their start and end apart: 20 -> 20, of which waited for: 10 -> 13; matrix products, arithmetic and copies ran while one was open for 1% -> 1% of each run, Pallas kernels for 29% -> 29%
where the time goes in v14:
time: 304 us; the launch traced here: 299 us
  waiting for transfers between devices  143 us (47%)
  Pallas kernels  93.6 us (31%)
  starting transfers between devices  56.3 us (19%)
    all_to_all x3, waiting for transfers between devices, exchange(): lax.all_to_all(messages[0], 'seq', split_axis=0, concat_axis=0, tiled=True)  81.7 us
    pallas_call x2, Pallas kernels, attend(): pl.pallas_call(functools.partial(attend_kernel, head_dim=lanes // 2, per_...  58.3 us
    ppermute x7, waiting for transfers between devices, exchange(): received[item] = lax.ppermute(messages[item], 'seq', pairs)  55.6 us
    ppermute x10, starting transfers between devices, from_behind(): return lax.ppermute(x, axis, pairs)  27.8 us
    all_to_all x3, starting transfers between devices, exchange(): lax.all_to_all(messages[0], 'seq', split_axis=0, concat_axis=0, tiled=True)  19.3 us
    ppermute x7, starting transfers between devices, exchange(): received[item] = lax.ppermute(messages[item], 'seq', pairs)  9.18 us
    pallas_call x2, Pallas kernels, prepare(): pl.pallas_call(functools.partial(prepare_kernel, peers=peers), in_specs=[...  8.45 us
    pallas_call x3, Pallas kernels, unpack_items(): pl.pallas_call(functools.partial(unpack_items_kernel, items=items, peers=...  7.86 us
  transfers between devices with their start and end apart: 20, of which 13 were waited for; matrix products, arithmetic and copies ran while one was open for 1% of the time, Pallas kernels for 29%

profile of v14, /device:TPU:8, one launch (start us, length us, event | category | flops | bytes accessed | tf_op | source)
XLA Modules:
  0.0 298.6 jit_solution(17204176367117223491)
XLA Ops:
  0.6 3.9 %pack.2 = bf16[8,3,2,256,128]{4,3,2,1,0:T(8,128)(2,1)} custom-call(bf16[256,3072]{1,0:T(8,128)(2,1)} %query.3, bf16[256,3072]{1,0:T(8,128)(2,1)} %key.3, bf16[256,3072]{1,0:T(8,128)(2,1)} %value.3, bf16[256,3072]{1,0:T(8,128)(2,1)} %d_out.3), custom_call_target="tpu_custom_call" | custom-call | tf_op jit(solution)/shard_map/pack/pallas_call | solution.py:106
  4.6 6.3 %all-to-all-start = ((bf16[8,3,2,256,128]{4,3,2,1,0:T(8,128)(2,1)}), bf16[8,3,2,256,128]{4,3,2,1,0:T(8,128)(2,1)S(1)}, u32[]{:S(2)}, u32[]{:S(2)}) async-start(bf16[8,3,2,256,128]{4,3,2,1,0:T(8,128)(2,1)} %pack.2), calls=%async_computation | async-start | bytes 6291456 | tf_op jit(solution)/shard_map/all_to_all | solution.py:50
  10.9 0.1 eq.22
  11.0 0.2 compare_reduce_fusion.1
  11.2 1.2 top_k.24
  12.5 1.3 collective-permute-start.1
  13.8 1.2 top_k.17
  15.0 1.3 collective-permute-start
  16.6 3.2 %collective-permute-done = s32[4]{0:T(128)S(1)} collective-permute-done((s32[4]{0:T(128)S(1)}, s32[4]{0:T(128)S(1)}, u32[]{:S(2)}, u32[]{:S(2)}) %collective-permute-start) | collective-permute-done | bytes 48 | tf_op jit(solution)/shard_map/ppermute | solution.py:29
  19.9 3.9 %pack.3 = bf16[8,3,2,256,128]{4,3,2,1,0:T(8,128)(2,1)} custom-call(bf16[256,3072]{1,0:T(8,128)(2,1)} %query.3, bf16[256,3072]{1,0:T(8,128)(2,1)} %key.3, bf16[256,3072]{1,0:T(8,128)(2,1)} %value.3, bf16[256,3072]{1,0:T(8,128)(2,1)} %d_out.3, s32[8]{0:T(128)S(1)} %pad_add_fusion.asked.refs_0_, s32[6,16,8]{2,1,0:T(8,128)S(1)} %select_select_fusion.refs_1_), custom_call_target="tpu_custom_call" | custom-call | tf_op jit(solution)/shard_map/pack/pallas_call | solution.py:106
  23.8 55.3 %all-to-all-done.refs_0_ = bf16[8,3,2,256,128]{4,3,2,1,0:T(8,128)(2,1)S(1)} async-done(((bf16[8,3,2,256,128]{4,3,2,1,0:T(8,128)(2,1)}), bf16[8,3,2,256,128]{4,3,2,1,0:T(8,128)(2,1)S(1)}, u32[]{:S(2)}, u32[]{:S(2)}) %all-to-all-start) | async-done | bytes 3145760 | tf_op jit(solution)/shard_map/all_to_all | solution.py:50
  79.1 6.8 %all-to-all-start.2 = ((bf16[8,3,2,256,128]{4,3,2,1,0:T(8,128)(2,1)}), bf16[8,3,2,256,128]{4,3,2,1,0:T(8,128)(2,1)}, u32[]{:S(2)}, u32[]{:S(2)}) async-start(bf16[8,3,2,256,128]{4,3,2,1,0:T(8,128)(2,1)} %pack.3), calls=%async_computation.2 | async-start | bytes 6291456 | tf_op jit(solution)/shard_map/all_to_all | solution.py:50
  85.9 1.4 pick.2
  87.3 1.3 collective-permute-start.2
  88.7 1.3 collective-permute-start.3
  90.0 4.6 %prepare.2 = (bf16[3,24,128,128]{3,2,1,0:T(8,128)(2,1)S(1)}, bf16[8,3,256,128]{3,2,1,0:T(8,128)(2,1)S(1)}, f32[3,24,128,128]{3,2,1,0:T(8,128)S(1)}) custom-call(s32[1]{0:T(128)} %bitcast.me, bf16[3,24,128,128]{3,2,1,0:T(8,128)(2,1)S(1)} %get-tuple-element.54.table.table_in, bf16[8,3,2,256,128]{4,3,2,1,0:T(8,128)(2,1)S(1)} %all-to-all-done.refs_0_), custom_call_target="tpu_custom_call" | custom-call | tf_op jit(solution)/shard_map/prepare/pallas_call | solution.py:412
  94.6 29.4 %attend.2 = (bf16[8,3,256,128]{3,2,1,0:T(8,128)(2,1)S(1)}, bf16[4,3,128,128]{3,2,1,0:T(8,128)(2,1)S(1)}, bf16[4,3,128,128]{3,2,1,0:T(8,128)(2,1)S(1)}, bf16[3,24...) custom-call(s32[3,16,8]{2,1,0:T(8,128)S(1)} %get-tuple-element.97.li, ...), custom_call_target="tpu_custom_call", output_to_operand_aliasing={{3}: (4, {}), {4}: (5, {}), {5}: (6, {})} | custom-call | tf_op jit(solution)/shard_map/attend/pallas_call | solution.py:568
  124.0 1.3 collective-permute-start.4
  125.3 8.4 %collective-permute-start.5 = (bf16[4,3,128,128]{3,2,1,0:T(8,128)(2,1)S(1)}, bf16[4,3,128,128]{3,2,1,0:T(8,128)(2,1)S(1)}, u32[]{:S(2)}, u32[]{:S(2)}) collective-permute-start(bf16[4,3,128,128]{3,2,1,0:T(8,128)(2,1)S(1)} %get-tuple-element.61), channel_id=1, source_target_pairs={{0,8},{8,16},{16,24},{1,9},{9,17},{17,25},{2,10},{10,18},{18,26},{... | collective-permute-start | bytes 1179656 | tf_op jit(solution)/shard_map/ppermute | solution.py:29
  133.7 1.3 collective-permute-done.5.earlier
  135.0 2.6 finish.2.refs_1_
  137.6 16.0 %all-to-all-done.2.refs_0_ = bf16[8,3,2,256,128]{4,3,2,1,0:T(8,128)(2,1)} async-done(((bf16[8,3,2,256,128]{4,3,2,1,0:T(8,128)(2,1)}), bf16[8,3,2,256,128]{4,3,2,1,0:T(8,128)(2,1)}, u32[]{:S(2)}, u32[]{:S(2)}) %all-to-all-start.2) | async-done | bytes 3145760 | tf_op jit(solution)/shard_map/all_to_all | solution.py:50
  153.6 6.2 %all-to-all-start.1 = ((bf16[8,3,2,256,128]{4,3,2,1,0:T(8,128)(2,1)}), bf16[8,3,2,256,128]{4,3,2,1,0:T(8,128)(2,1)S(1)}, u32[]{:S(2)}, u32[]{:S(2)}) async-start(bf16[8,3,2,256,128]{4,3,2,1,0:T(8,128)(2,1)} %finish.2.refs_1_), calls=%async_computation.1 | async-start | bytes 6291456 | tf_op jit(solution)/shard_map/all_to_all | solution.py:50
  159.8 2.2 pick.3
  162.0 1.4 collective-permute-start.6
  163.4 1.3 collective-permute-start.7
  164.7 3.9 %prepare.3 = (bf16[3,24,128,128]{3,2,1,0:T(8,128)(2,1)S(1)}, bf16[8,3,256,128]{3,2,1,0:T(8,128)(2,1)S(1)}, f32[3,24,128,128]{3,2,1,0:T(8,128)S(1)}) custom-call(s32[1]{0:T(128)} %bitcast.me, bf16[3,24,128,128]{3,2,1,0:T(8,128)(2,1)S(1)} %get-tuple-element.64.table.table_in, bf16[8,3,2,256,128]{4,3,2,1,0:T(8,128)(2,1)} %all-to-all-done.2.refs_0_), custom_call_target="tpu_custom_call" | custom-call | tf_op jit(solution)/shard_map/prepare/pallas_call | solution.py:412
  168.7 28.9 %attend.3 = (bf16[8,3,256,128]{3,2,1,0:T(8,128)(2,1)S(1)}, bf16[4,3,128,128]{3,2,1,0:T(8,128)(2,1)S(1)}, bf16[4,3,128,128]{3,2,1,0:T(8,128)(2,1)S(1)}, bf16[3,24...) custom-call(s32[3,16,8]{2,1,0:T(8,128)S(1)} %get-tuple-element.96.li, ...), custom_call_target="tpu_custom_call", output_to_operand_aliasing={{3}: (4, {}), {4}: (5, {}), {5}: (6, {})} | custom-call | tf_op jit(solution)/shard_map/attend/pallas_call | solution.py:568
  197.6 1.3 collective-permute-start.8
  198.9 9.0 %collective-permute-start.9 = (bf16[4,3,128,128]{3,2,1,0:T(8,128)(2,1)S(1)}, bf16[4,3,128,128]{3,2,1,0:T(8,128)(2,1)S(1)}, u32[]{:S(2)}, u32[]{:S(2)}) collective-permute-start(bf16[4,3,128,128]{3,2,1,0:T(8,128)(2,1)S(1)} %get-tuple-element.71), channel_id=1, source_target_pairs={{0,8},{8,16},{16,24},{1,9},{9,17},{17,25},{2,10},{10,18},{18,26},{... | collective-permute-start | bytes 1179656 | tf_op jit(solution)/shard_map/ppermute | solution.py:29
  207.9 1.1 collective-permute-done.9.earlier
  209.0 2.6 finish.3
  211.6 1.5 collective-permute-start.15
  213.3 3.7 %collective-permute-start.13 = (bf16[3,2,256,128]{3,2,1,0:T(8,128)(2,1)}, bf16[3,2,256,128]{3,2,1,0:T(8,128)(2,1)S(1)}, u32[]{:S(2)}, u32[]{:S(2)}) collective-permute-start(bf16[3,2,256,128]{3,2,1,0:T(8,128)(2,1)} %get-tuple-element.75), channel_id=1, source_target_pairs={{0,7},{1,6},{2,5},{3,4},{4,3},{5,2},{6,1},{7,0},{8,15},{9,14},{10,... | collective-permute-start | bytes 1179656 | tf_op jit(solution)/shard_map/ppermute | solution.py:55
  217.0 3.8 %collective-permute-start.10 = (bf16[3,2,256,128]{3,2,1,0:T(8,128)(2,1)}, bf16[3,2,256,128]{3,2,1,0:T(8,128)(2,1)}, u32[]{:S(2)}, u32[]{:S(2)}) collective-permute-start(bf16[3,2,256,128]{3,2,1,0:T(8,128)(2,1)} %get-tuple-element.72), channel_id=1, source_target_pairs={{0,5},{1,4},{2,7},{3,6},{4,1},{5,0},{6,3},{7,2},{8,13},{9,12},{10,... | collective-permute-start | bytes 1179656 | tf_op jit(solution)/shard_map/ppermute | solution.py:55
  220.8 17.6 %collective-permute-done.15.refs_2_ = bf16[3,2,256,128]{3,2,1,0:T(8,128)(2,1)S(1)} collective-permute-done((bf16[3,2,256,128]{3,2,1,0:T(8,128)(2,1)}, bf16[3,2,256,128]{3,2,1,0:T(8,128)(2,1)S(1)}, u32[]{:S(2)}, u32[]{:S(2)}) %collective-permute-start.15) | collective-permute-done | bytes 393248 | tf_op jit(solution)/shard_map/ppermute | solution.py:55
  238.5 0.7 copy-done.1
  239.2 11.4 %collective-permute-done.16.refs_3_ = bf16[3,2,256,128]{3,2,1,0:T(8,128)(2,1)S(1)} collective-permute-done((bf16[3,2,256,128]{3,2,1,0:T(8,128)(2,1)}, bf16[3,2,256,128]{3,2,1,0:T(8,128)(2,1)S(1)}, u32[]{:S(2)}, u32[]{:S(2)}) %collective-permute-start.16) | collective-permute-done | bytes 393248 | tf_op jit(solution)/shard_map/ppermute | solution.py:55
  250.7 0.7 copy-done.3
  251.4 10.4 %all-to-all-done.1.refs_0_ = bf16[8,3,2,256,128]{4,3,2,1,0:T(8,128)(2,1)S(1)} async-done(((bf16[8,3,2,256,128]{4,3,2,1,0:T(8,128)(2,1)}), bf16[8,3,2,256,128]{4,3,2,1,0:T(8,128)(2,1)S(1)}, u32[]{:S(2)}, u32[]{:S(2)}) %all-to-all-start.1) | async-done | bytes 3145760 | tf_op jit(solution)/shard_map/all_to_all | solution.py:50
  261.8 2.2 unpack.1
  264.1 2.6 unpack_items.3
  266.7 8.6 %collective-permute-done.13.refs_1_ = bf16[3,2,256,128]{3,2,1,0:T(8,128)(2,1)S(1)} collective-permute-done((bf16[3,2,256,128]{3,2,1,0:T(8,128)(2,1)}, bf16[3,2,256,128]{3,2,1,0:T(8,128)(2,1)S(1)}, u32[]{:S(2)}, u32[]{:S(2)}) %collective-permute-start.13) | collective-permute-done | bytes 393248 | tf_op jit(solution)/shard_map/ppermute | solution.py:55
  275.3 5.9 %collective-permute-done.14.refs_2_ = bf16[3,2,256,128]{3,2,1,0:T(8,128)(2,1)} collective-permute-done((bf16[3,2,256,128]{3,2,1,0:T(8,128)(2,1)}, bf16[3,2,256,128]{3,2,1,0:T(8,128)(2,1)}, u32[]{:S(2)}, u32[]{:S(2)}) %collective-permute-start.14) | collective-permute-done | bytes 393248 | tf_op jit(solution)/shard_map/ppermute | solution.py:55
  281.2 2.6 unpack_items.4
  283.8 3.6 %collective-permute-done.10.refs_1_ = bf16[3,2,256,128]{3,2,1,0:T(8,128)(2,1)} collective-permute-done((bf16[3,2,256,128]{3,2,1,0:T(8,128)(2,1)}, bf16[3,2,256,128]{3,2,1,0:T(8,128)(2,1)}, u32[]{:S(2)}, u32[]{:S(2)}) %collective-permute-start.10) | collective-permute-done | bytes 393248 | tf_op jit(solution)/shard_map/ppermute | solution.py:55
  287.4 8.3 %collective-permute-done.11.refs_2_ = bf16[3,2,256,128]{3,2,1,0:T(8,128)(2,1)} collective-permute-done((bf16[3,2,256,128]{3,2,1,0:T(8,128)(2,1)}, bf16[3,2,256,128]{3,2,1,0:T(8,128)(2,1)}, u32[]{:S(2)}, u32[]{:S(2)}) %collective-permute-start.11) | collective-permute-done | bytes 393248 | tf_op jit(solution)/shard_map/ppermute | solution.py:55
  295.7 2.7 unpack_items.5
  (36 shorter events, 0.6 us)
Async XLA Ops:
  4.5 6.3 %copy-start.5 = (s32[6,16,8]{1,2,0:T(8,128)S(1)}, s32[6,16,8]{1,2,0:T(8,128)}, u32[]{:S(2)}) copy-start(s32[6,16,8]{1,2,0:T(8,128)} %param.9) | copy-start | bytes 9220
  4.6 74.5 %all-to-all-start = ((bf16[8,3,2,256,128]{4,3,2,1,0:T(8,128)(2,1)}), bf16[8,3,2,256,128]{4,3,2,1,0:T(8,128)(2,1)S(1)}, u32[]{:S(2)}, u32[]{:S(2)}) async-start(bf16[8,3,2,256,128]{4,3,2,1,0:T(8,128)(2,1)} %pack.2), calls=%async_computation | async-start | bytes 6291456 | tf_op jit(solution)/shard_map/all_to_all | solution.py:50
  12.5 4.1 %collective-permute-start.1 = (s32[4]{0:T(128)S(1)}, s32[4]{0:T(128)S(1)}, u32[]{:S(2)}, u32[]{:S(2)}) collective-permute-start(s32[4]{0:T(128)S(1)} %get-tuple-element.101), channel_id=1, source_target_pairs={{0,8},{8,16},{16,24},{1,9},{9,17},{17,25},{2,10},{10,18},{18,26},{... | collective-permute-start | bytes 56 | tf_op jit(solution)/shard_map/ppermute | solution.py:29
  15.0 4.8 %collective-permute-start = (s32[4]{0:T(128)S(1)}, s32[4]{0:T(128)S(1)}, u32[]{:S(2)}, u32[]{:S(2)}) collective-permute-start(s32[4]{0:T(128)S(1)} %get-tuple-element.99), channel_id=1, source_target_pairs={{8,0},{16,8},{24,16},{9,1},{17,9},{25,17},{10,2},{18,10},{26,18},{... | collective-permute-start | bytes 56 | tf_op jit(solution)/shard_map/ppermute | solution.py:29
  79.1 74.5 %all-to-all-start.2 = ((bf16[8,3,2,256,128]{4,3,2,1,0:T(8,128)(2,1)}), bf16[8,3,2,256,128]{4,3,2,1,0:T(8,128)(2,1)}, u32[]{:S(2)}, u32[]{:S(2)}) async-start(bf16[8,3,2,256,128]{4,3,2,1,0:T(8,128)(2,1)} %pack.3), calls=%async_computation.2 | async-start | bytes 6291456 | tf_op jit(solution)/shard_map/all_to_all | solution.py:50
  87.3 7.2 %collective-permute-start.2 = (bf16[4,3,128,128]{3,2,1,0:T(8,128)(2,1)S(1)}, bf16[4,3,128,128]{3,2,1,0:T(8,128)(2,1)S(1)}, u32[]{:S(2)}, u32[]{:S(2)}) collective-permute-start(bf16[4,3,128,128]{3,2,1,0:T(8,128)(2,1)S(1)} %get-tuple-element.52), channel_id=1, source_target_pairs={{0,8},{8,16},{16,24},{1,9},{9,17},{17,25},{2,10},{10,18},{18,26},{... | collective-permute-start | bytes 1179656 | tf_op jit(solution)/shard_map/ppermute | solution.py:29
  88.7 5.9 %collective-permute-start.3 = (bf16[4,3,128,128]{3,2,1,0:T(8,128)(2,1)S(1)}, bf16[4,3,128,128]{3,2,1,0:T(8,128)(2,1)S(1)}, u32[]{:S(2)}, u32[]{:S(2)}) collective-permute-start(bf16[4,3,128,128]{3,2,1,0:T(8,128)(2,1)S(1)} %get-tuple-element.53), channel_id=1, source_target_pairs={{8,0},{16,8},{24,16},{9,1},{17,9},{25,17},{10,2},{18,10},{26,18},{... | collective-permute-start | bytes 1179656 | tf_op jit(solution)/shard_map/ppermute | solution.py:29
  124.0 9.7 %collective-permute-start.4 = (bf16[4,3,128,128]{3,2,1,0:T(8,128)(2,1)S(1)}, bf16[4,3,128,128]{3,2,1,0:T(8,128)(2,1)S(1)}, u32[]{:S(2)}, u32[]{:S(2)}) collective-permute-start(bf16[4,3,128,128]{3,2,1,0:T(8,128)(2,1)S(1)} %get-tuple-element.60), channel_id=1, source_target_pairs={{8,0},{16,8},{24,16},{9,1},{17,9},{25,17},{10,2},{18,10},{26,18},{... | collective-permute-start | bytes 1179656 | tf_op jit(solution)/shard_map/ppermute | solution.py:29
  125.3 9.7 %collective-permute-start.5 = (bf16[4,3,128,128]{3,2,1,0:T(8,128)(2,1)S(1)}, bf16[4,3,128,128]{3,2,1,0:T(8,128)(2,1)S(1)}, u32[]{:S(2)}, u32[]{:S(2)}) collective-permute-start(bf16[4,3,128,128]{3,2,1,0:T(8,128)(2,1)S(1)} %get-tuple-element.61), channel_id=1, source_target_pairs={{0,8},{8,16},{16,24},{1,9},{9,17},{17,25},{2,10},{10,18},{18,26},{... | collective-permute-start | bytes 1179656 | tf_op jit(solution)/shard_map/ppermute | solution.py:29
  153.6 108.2 %all-to-all-start.1 = ((bf16[8,3,2,256,128]{4,3,2,1,0:T(8,128)(2,1)}), bf16[8,3,2,256,128]{4,3,2,1,0:T(8,128)(2,1)S(1)}, u32[]{:S(2)}, u32[]{:S(2)}) async-start(bf16[8,3,2,256,128]{4,3,2,1,0:T(8,128)(2,1)} %finish.2.refs_1_), calls=%async_computation.1 | async-start | bytes 6291456 | tf_op jit(solution)/shard_map/all_to_all | solution.py:50
  162.0 6.6 %collective-permute-start.6 = (bf16[4,3,128,128]{3,2,1,0:T(8,128)(2,1)S(1)}, bf16[4,3,128,128]{3,2,1,0:T(8,128)(2,1)S(1)}, u32[]{:S(2)}, u32[]{:S(2)}) collective-permute-start(bf16[4,3,128,128]{3,2,1,0:T(8,128)(2,1)S(1)} %get-tuple-element.62), channel_id=1, source_target_pairs={{0,8},{8,16},{16,24},{1,9},{9,17},{17,25},{2,10},{10,18},{18,26},{... | collective-permute-start | bytes 1179656 | tf_op jit(solution)/shard_map/ppermute | solution.py:29
  163.4 5.3 %collective-permute-start.7 = (bf16[4,3,128,128]{3,2,1,0:T(8,128)(2,1)S(1)}, bf16[4,3,128,128]{3,2,1,0:T(8,128)(2,1)S(1)}, u32[]{:S(2)}, u32[]{:S(2)}) collective-permute-start(bf16[4,3,128,128]{3,2,1,0:T(8,128)(2,1)S(1)} %get-tuple-element.63), channel_id=1, source_target_pairs={{8,0},{16,8},{24,16},{9,1},{17,9},{25,17},{10,2},{18,10},{26,18},{... | collective-permute-start | bytes 1179656 | tf_op jit(solution)/shard_map/ppermute | solution.py:29
  197.6 10.3 %collective-permute-start.8 = (bf16[4,3,128,128]{3,2,1,0:T(8,128)(2,1)S(1)}, bf16[4,3,128,128]{3,2,1,0:T(8,128)(2,1)S(1)}, u32[]{:S(2)}, u32[]{:S(2)}) collective-permute-start(bf16[4,3,128,128]{3,2,1,0:T(8,128)(2,1)S(1)} %get-tuple-element.70), channel_id=1, source_target_pairs={{8,0},{16,8},{24,16},{9,1},{17,9},{25,17},{10,2},{18,10},{26,18},{... | collective-permute-start | bytes 1179656 | tf_op jit(solution)/shard_map/ppermute | solution.py:29
  198.9 10.1 %collective-permute-start.9 = (bf16[4,3,128,128]{3,2,1,0:T(8,128)(2,1)S(1)}, bf16[4,3,128,128]{3,2,1,0:T(8,128)(2,1)S(1)}, u32[]{:S(2)}, u32[]{:S(2)}) collective-permute-start(bf16[4,3,128,128]{3,2,1,0:T(8,128)(2,1)S(1)} %get-tuple-element.71), channel_id=1, source_target_pairs={{0,8},{8,16},{16,24},{1,9},{9,17},{17,25},{2,10},{10,18},{18,26},{... | collective-permute-start | bytes 1179656 | tf_op jit(solution)/shard_map/ppermute | solution.py:29
  211.6 26.8 %collective-permute-start.15 = (bf16[3,2,256,128]{3,2,1,0:T(8,128)(2,1)}, bf16[3,2,256,128]{3,2,1,0:T(8,128)(2,1)S(1)}, u32[]{:S(2)}, u32[]{:S(2)}) collective-permute-start(bf16[3,2,256,128]{3,2,1,0:T(8,128)(2,1)} %get-tuple-element.78), channel_id=1, source_target_pairs={{0,1},{1,0},{2,3},{3,2},{4,5},{5,4},{6,7},{7,6},{8,9},{9,8},{10,11... | collective-permute-start | bytes 1179656 | tf_op jit(solution)/shard_map/ppermute | solution.py:55
  213.2 37.5 %collective-permute-start.16 = (bf16[3,2,256,128]{3,2,1,0:T(8,128)(2,1)}, bf16[3,2,256,128]{3,2,1,0:T(8,128)(2,1)S(1)}, u32[]{:S(2)}, u32[]{:S(2)}) collective-permute-start(bf16[3,2,256,128]{3,2,1,0:T(8,128)(2,1)} %get-tuple-element.79), channel_id=1, source_target_pairs={{0,3},{1,2},{2,1},{3,0},{4,7},{5,6},{6,5},{7,4},{8,11},{9,10},{10,... | collective-permute-start | bytes 1179656 | tf_op jit(solution)/shard_map/ppermute | solution.py:55
  213.3 62.0 %collective-permute-start.13 = (bf16[3,2,256,128]{3,2,1,0:T(8,128)(2,1)}, bf16[3,2,256,128]{3,2,1,0:T(8,128)(2,1)S(1)}, u32[]{:S(2)}, u32[]{:S(2)}) collective-permute-start(bf16[3,2,256,128]{3,2,1,0:T(8,128)(2,1)} %get-tuple-element.75), channel_id=1, source_target_pairs={{0,7},{1,6},{2,5},{3,4},{4,3},{5,2},{6,1},{7,0},{8,15},{9,14},{10,... | collective-permute-start | bytes 1179656 | tf_op jit(solution)/shard_map/ppermute | solution.py:55
  217.0 64.2 %collective-permute-start.14 = (bf16[3,2,256,128]{3,2,1,0:T(8,128)(2,1)}, bf16[3,2,256,128]{3,2,1,0:T(8,128)(2,1)}, u32[]{:S(2)}, u32[]{:S(2)}) collective-permute-start(bf16[3,2,256,128]{3,2,1,0:T(8,128)(2,1)} %get-tuple-element.76), channel_id=1, source_target_pairs={{0,6},{1,7},{2,4},{3,5},{4,2},{5,3},{6,0},{7,1},{8,14},{9,15},{10,... | collective-permute-start | bytes 1179656 | tf_op jit(solution)/shard_map/ppermute | solution.py:55
  217.0 70.4 %collective-permute-start.10 = (bf16[3,2,256,128]{3,2,1,0:T(8,128)(2,1)}, bf16[3,2,256,128]{3,2,1,0:T(8,128)(2,1)}, u32[]{:S(2)}, u32[]{:S(2)}) collective-permute-start(bf16[3,2,256,128]{3,2,1,0:T(8,128)(2,1)} %get-tuple-element.72), channel_id=1, source_target_pairs={{0,5},{1,4},{2,7},{3,6},{4,1},{5,0},{6,3},{7,2},{8,13},{9,12},{10,... | collective-permute-start | bytes 1179656 | tf_op jit(solution)/shard_map/ppermute | solution.py:55
  238.5 0.7 copy-start.1
  239.2 56.5 %collective-permute-start.11 = (bf16[3,2,256,128]{3,2,1,0:T(8,128)(2,1)}, bf16[3,2,256,128]{3,2,1,0:T(8,128)(2,1)}, u32[]{:S(2)}, u32[]{:S(2)}) collective-permute-start(bf16[3,2,256,128]{3,2,1,0:T(8,128)(2,1)} %get-tuple-element.73), channel_id=1, source_target_pairs={{0,4},{1,5},{2,6},{3,7},{4,0},{5,1},{6,2},{7,3},{8,12},{9,13},{10,... | collective-permute-start | bytes 1179656 | tf_op jit(solution)/shard_map/ppermute | solution.py:55
  250.7 0.7 copy-start.3
  251.4 44.3 %collective-permute-start.12 = (bf16[3,2,256,128]{3,2,1,0:T(8,128)(2,1)}, bf16[3,2,256,128]{3,2,1,0:T(8,128)(2,1)}, u32[]{:S(2)}, u32[]{:S(2)}) collective-permute-start(bf16[3,2,256,128]{3,2,1,0:T(8,128)(2,1)} %get-tuple-element.74), channel_id=1, source_target_pairs={{0,2},{1,3},{2,0},{3,1},{4,6},{5,7},{6,4},{7,5},{8,10},{9,11},{10,... | collective-permute-start | bytes 1179656 | tf_op jit(solution)/shard_map/ppermute | solution.py:55
  261.8 2.3 copy-start
  261.8 2.3 copy-start.2
  261.8 2.3 copy-start.4

commit v15 on v14

--- a/solution.py
+++ b/solution.py
@@ -29,30 +29,57 @@
     return lax.ppermute(x, axis, pairs)
 
 
-def part_of(messages, me, item):
-    if len(messages) == 1:
+JOINT, APART, PAIRED = "joint", "apart", "paired"
+
+
+def form_of(messages, peers):
+    return {1: JOINT, peers: APART}.get(len(messages), PAIRED)
+
+
+def part_of(messages, me, item, peers):
+    form, half = form_of(messages, peers), peers // 2
+    if form == JOINT:
         return messages[0].at[item], item
-    return messages[item], me[0] ^ (len(messages) - 1 - item)
+    if form == PAIRED and item >= half:
+        return messages[half].at[item - half], lax.div(me[0], half) * half + item - half
+    part = messages[item]
+    if len(part.shape) == 5:
+        part = part.at[1 - lax.div(me[0], half)]
+    return part, me[0] ^ (peers - 1 - item)
 
 
 def message_shape(messages):
     return messages[0].shape[-4:]
 
 
-def message_outs(peers, shape, dtype, apart):
-    if apart:
+def message_outs(peers, shape, dtype, form):
+    if form == JOINT:
+        return [pltpu.HBM((peers,) + shape, dtype)]
+    if form == APART:
         return [pltpu.HBM(shape, dtype)] * peers
-    return [pltpu.HBM((peers,) + shape, dtype)]
+    half = peers // 2
+    return [pltpu.HBM(shape, dtype)] * half + [pltpu.HBM((half,) + shape, dtype)]
 
 
 def exchange(messages):
-    if len(messages) == 1:
-        return [lax.all_to_all(messages[0], "seq", split_axis=0, concat_axis=0, tiled=True)]
-    count = len(messages)
+    peers = lax.axis_size("seq")
+    form, half = form_of(messages, peers), peers // 2
+    swap = functools.partial(
+        lax.all_to_all, axis_name="seq", split_axis=0, concat_axis=0, tiled=True
+    )
+    if form == JOINT:
+        return [swap(messages[0])]
     received = list(messages)
-    for item in range(count - 1):
-        pairs = [(i, i ^ (count - 1 - item)) for i in range(count)]
-        received[item] = lax.ppermute(messages[item], "seq", pairs)
+    if form == APART:
+        for item in range(peers - 1):
+            pairs = [(i, i ^ (peers - 1 - item)) for i in range(peers)]
+            received[item] = lax.ppermute(messages[item], "seq", pairs)
+        return received
+    for item in range(half):
+        pairs = [[i, i ^ (peers - 1 - item)] for i in range(half)]
+        received[item] = lax.all_gather(messages[item], "seq", axis_index_groups=pairs)
+    halves = [list(range(half)), list(range(half, peers))]
+    received[half] = swap(messages[half], axis_index_groups=halves)
     return received
 
 
@@ -142,7 +169,7 @@
     def fetch(which, item, slot=None):
         heads = heads_used[which]
         some = pl.ds(heads[0], heads[-1] - heads[0] + 1)
-        source, peer = part_of(groups[which], me, item)
+        source, peer = part_of(groups[which], me, item, peers)
         slot = peer if slot is None else slot
         return pltpu.make_async_copy(
             source.at[some], stages[which].at[slot, some], in_sems.at[which, slot]
@@ -231,7 +258,7 @@
     )(me, *flat, *[in_hbm(x) for x in earlier])
 
 
-def unpack_items_kernel(me, *refs, items, peers, counts, joint, earlier, jobs, per_peer):
+def unpack_items_kernel(me, *refs, items, peers, counts, forms, earlier, jobs, per_peer):
     ends = [sum(counts[: c + 1]) for c in range(len(counts))]
     groups = [refs[end - count : end] for end, count in zip(ends, counts)]
     outs = refs[ends[-1] + earlier :][:4]
@@ -246,9 +273,18 @@
     def peer_of(j):
         return me[0] ^ (peers - 1 - items[j])
 
+    def source_of(group, form, j):
+        half = peers // 2
+        if form == JOINT:
+            return group[0].at[peer_of(j)]
+        if form == APART:
+            return group[j]
+        if items[j] < half:
+            return group[items[j]].at[1 - lax.div(me[0], half)]
+        return group[half].at[lax.rem(peer_of(j), half)]
+
     def fetch(which, j):
-        group = groups[which]
-        source = group[0].at[peer_of(j)] if joint[which] else group[j]
+        source = source_of(groups[which], forms[which], j)
         some = pl.ds(used[which][0], used[which][-1] - used[which][0] + 1)
         return pltpu.make_async_copy(
             source.at[some], stages[which].at[j, some], in_sems.at[which, j]
@@ -298,9 +334,10 @@
         left, right = place_of(2 * tile), place_of(2 * tile + 1)
         if max(left[0], right[0]) == chunk:
             jobs.append((tile, left, right))
+    forms = [form_of(group, peers) for group in messages]
     groups = [
-        list(group) if len(group) == 1 else [group[item] for item in items]
-        for group in messages
+        [group[item] for item in items] if form == APART else list(group)
+        for group, form in zip(messages, forms)
     ]
     flat = [x for group in groups for x in group]
     anywhere = pl.BlockSpec(memory_space=pltpu.HBM)
@@ -310,7 +347,7 @@
             items=items,
             peers=peers,
             counts=[len(group) for group in groups],
-            joint=[len(group) == 1 for group in messages],
+            forms=forms,
             earlier=len(earlier),
             jobs=jobs,
             per_peer=per_peer,
@@ -340,7 +377,7 @@
     peers, each = sems.shape
 
     def fetch(item, i):
-        source, peer = part_of(refs[:count], me, item)
+        source, peer = part_of(refs[:count], me, item, peers)
         rows = pl.ds(i * block_rows, block_rows)
         return pltpu.make_async_copy(
             source.at[:, 0, rows], table.at[:, CROSS + peer * each + i], sems.at[item, i]
@@ -382,7 +419,7 @@
     heads, window, _, _ = table.shape
 
     def fetch(item):
-        source, peer = part_of(messages, me, item)
+        source, peer = part_of(messages, me, item, peers)
         return pltpu.make_async_copy(source.at[:, 1], pairs.at[peer], sems.at[item])
 
     for item in range(peers):
@@ -594,7 +631,7 @@
     factor = jnp.where(left, head_dim ** (-0.5), 1.0)
 
     def send(item, head):
-        target, peer = part_of(messages, me, item)
+        target, peer = part_of(messages, me, item, peers)
         return pltpu.make_async_copy(
             ready.at[peer, head], target.at[head], sems.at[item, head]
         )
@@ -618,14 +655,14 @@
             send(item, head).wait()
 
 
-def finish(me, back, kept, later, earlier, asked, apart):
+def finish(me, back, kept, later, earlier, asked, form):
     peers, heads, rows, lanes = back.shape
     _, window, block_rows, _ = kept.shape
     blocks = window - 2 * CROSS
     inside = pl.BlockSpec(memory_space=pltpu.VMEM)
     scalars = pl.BlockSpec(memory_space=pltpu.SMEM)
     shape = (heads, 2, rows, lanes)
-    outs = message_outs(peers, shape, back.dtype, apart)
+    outs = message_outs(peers, shape, back.dtype, form)
     return pl.pallas_call(
         functools.partial(finish_kernel, block_rows=block_rows),
         in_specs=[scalars, scalars] + [inside] * 4,
@@ -702,7 +739,8 @@
         )
         later = from_behind(to_prev, "slab", -1)
         earlier = from_behind(to_next, "slab", 1)
-        finished = finish(me, back, kept, later, earlier, asked, chunk == last)
+        form = APART if chunk == last else PAIRED
+        finished = finish(me, back, kept, later, earlier, asked, form)
         received.append(exchange(finished))
         if chunk == last and heads_here * head_dim % LANES == 0:
             half = peers // 2

time: 304 us -> 379 us (1.25)
  blocking collectives: 0 us -> 124 us
  waiting for transfers between devices: 143 us -> 75 us
  starting transfers between devices: 56.3 us -> 73.9 us
    all_gather x0 -> x4, blocking collectives: none -> 124 us  [exchange(): lax.all_gather(messages[item], 'seq', axis_index_groups=pairs)]
    ppermute x7, waiting for transfers between devices: 55.6 us -> 0.02 us  [exchange(): received[item] = lax.ppermute(messages[item], 'seq', pairs)]
    ppermute x7, starting transfers between devices: 9.18 us -> 25.4 us  [exchange(): received[item] = lax.ppermute(messages[item], 'seq', pairs)]
    all_to_all x3, waiting for transfers between devices: 81.7 us -> 71.8 us  [the longest x2 71.8 us: exchange(): return [swap(messages[0])]]
  transfers between devices with their start and end apart: 20 -> 20, of which waited for: 13 -> 6; matrix products, arithmetic and copies ran while one was open for 1% -> 1% of each run, Pallas kernels for 29% -> 24%
where the time goes in v15:
time: 379 us; the launch traced here: 375 us
  blocking collectives  124 us (33%)
  Pallas kernels  95.4 us (25%)
  waiting for transfers between devices  75 us (20%)
  starting transfers between devices  73.9 us (19%)
    all_gather x4, blocking collectives, exchange(): lax.all_gather(messages[item], 'seq', axis_index_groups=pairs)  124 us
    all_to_all x2, waiting for transfers between devices, exchange(): return [swap(messages[0])]  71.8 us
    pallas_call x2, Pallas kernels, attend(): pl.pallas_call(functools.partial(attend_kernel, head_dim=lanes // 2, per_...  60 us
    ppermute x10, starting transfers between devices, from_behind(): return lax.ppermute(x, axis, pairs)  29.3 us
    ppermute x7, starting transfers between devices, exchange(): received[item] = lax.ppermute(messages[item], 'seq', pairs)  25.4 us
    all_to_all x2, starting transfers between devices, exchange(): return [swap(messages[0])]  13 us
    pallas_call x2, Pallas kernels, prepare(): pl.pallas_call(functools.partial(prepare_kernel, peers=peers), in_specs=[...  8.45 us
    pallas_call x3, Pallas kernels, unpack_items(): pl.pallas_call(functools.partial(unpack_items_kernel, items=items, peers=...  7.96 us
  transfers between devices with their start and end apart: 20, of which 6 were waited for; matrix products, arithmetic and copies ran while one was open for 1% of the time, Pallas kernels for 24%

profile of v15, /device:TPU:8, one launch (start us, length us, event | category | flops | bytes accessed | tf_op | source)
XLA Modules:
  0.0 375.3 jit_solution(3953700580742152844)
XLA Ops:
  0.6 3.9 %pack.2 = bf16[8,3,2,256,128]{4,3,2,1,0:T(8,128)(2,1)} custom-call(bf16[256,3072]{1,0:T(8,128)(2,1)} %query.3, bf16[256,3072]{1,0:T(8,128)(2,1)} %key.3, bf16[256,3072]{1,0:T(8,128)(2,1)} %value.3, bf16[256,3072]{1,0:T(8,128)(2,1)} %d_out.3), custom_call_target="tpu_custom_call" | custom-call | tf_op jit(solution)/shard_map/pack/pallas_call | solution.py:133
  4.6 6.3 %all-to-all-start = ((bf16[8,3,2,256,128]{4,3,2,1,0:T(8,128)(2,1)}), bf16[8,3,2,256,128]{4,3,2,1,0:T(8,128)(2,1)S(1)}, u32[]{:S(2)}, u32[]{:S(2)}) async-start(bf16[8,3,2,256,128]{4,3,2,1,0:T(8,128)(2,1)} %pack.2), calls=%async_computation | async-start | bytes 6291456 | tf_op jit(solution)/shard_map/all_to_all | solution.py:71
  10.9 0.1 eq.22
  11.0 0.2 compare_reduce_fusion.1
  11.2 1.2 top_k.17
  12.5 1.3 collective-permute-start
  13.8 1.2 top_k.24
  15.0 3.0 collective-permute-start.1
  18.3 0.5 collective-permute-done.1
  18.9 3.9 %pack.3 = bf16[8,3,2,256,128]{4,3,2,1,0:T(8,128)(2,1)} custom-call(bf16[256,3072]{1,0:T(8,128)(2,1)} %query.3, bf16[256,3072]{1,0:T(8,128)(2,1)} %key.3, bf16[256,3072]{1,0:T(8,128)(2,1)} %value.3, bf16[256,3072]{1,0:T(8,128)(2,1)} %d_out.3, s32[8]{0:T(128)S(1)} %pad_add_fusion.asked.refs_0_, s32[6,16,8]{2,1,0:T(8,128)S(1)} %select_select_fusion.refs_1_), custom_call_target="tpu_custom_call" | custom-call | tf_op jit(solution)/shard_map/pack/pallas_call | solution.py:133
  22.8 56.2 %all-to-all-done.refs_0_ = bf16[8,3,2,256,128]{4,3,2,1,0:T(8,128)(2,1)S(1)} async-done(((bf16[8,3,2,256,128]{4,3,2,1,0:T(8,128)(2,1)}), bf16[8,3,2,256,128]{4,3,2,1,0:T(8,128)(2,1)S(1)}, u32[]{:S(2)}, u32[]{:S(2)}) %all-to-all-start) | async-done | bytes 3145760 | tf_op jit(solution)/shard_map/all_to_all | solution.py:71
  79.1 6.8 %all-to-all-start.2 = ((bf16[8,3,2,256,128]{4,3,2,1,0:T(8,128)(2,1)}), bf16[8,3,2,256,128]{4,3,2,1,0:T(8,128)(2,1)}, u32[]{:S(2)}, u32[]{:S(2)}) async-start(bf16[8,3,2,256,128]{4,3,2,1,0:T(8,128)(2,1)} %pack.3), calls=%async_computation.2 | async-start | bytes 6291456 | tf_op jit(solution)/shard_map/all_to_all | solution.py:71
  85.8 1.4 pick.2
  87.3 1.3 collective-permute-start.2
  88.6 1.3 collective-permute-start.3
  89.9 4.6 %prepare.2 = (bf16[3,24,128,128]{3,2,1,0:T(8,128)(2,1)S(1)}, bf16[8,3,256,128]{3,2,1,0:T(8,128)(2,1)S(1)}, f32[3,24,128,128]{3,2,1,0:T(8,128)S(1)}) custom-call(s32[1]{0:T(128)} %bitcast.me, bf16[3,24,128,128]{3,2,1,0:T(8,128)(2,1)S(1)} %get-tuple-element.59.table.table_in, bf16[8,3,2,256,128]{4,3,2,1,0:T(8,128)(2,1)S(1)} %all-to-all-done.refs_0_), custom_call_target="tpu_custom_call" | custom-call | tf_op jit(solution)/shard_map/prepare/pallas_call | solution.py:449
  94.5 29.9 %attend.2 = (bf16[8,3,256,128]{3,2,1,0:T(8,128)(2,1)S(1)}, bf16[4,3,128,128]{3,2,1,0:T(8,128)(2,1)S(1)}, bf16[4,3,128,128]{3,2,1,0:T(8,128)(2,1)S(1)}, bf16[3,24...) custom-call(s32[3,16,8]{2,1,0:T(8,128)S(1)} %get-tuple-element.107.l, ...), custom_call_target="tpu_custom_call", output_to_operand_aliasing={{3}: (4, {}), {4}: (5, {}), {5}: (6, {})} | custom-call | tf_op jit(solution)/shard_map/attend/pallas_call | solution.py:605
  124.4 1.3 collective-permute-start.4
  125.7 8.4 %collective-permute-start.5 = (bf16[4,3,128,128]{3,2,1,0:T(8,128)(2,1)S(1)}, bf16[4,3,128,128]{3,2,1,0:T(8,128)(2,1)S(1)}, u32[]{:S(2)}, u32[]{:S(2)}) collective-permute-start(bf16[4,3,128,128]{3,2,1,0:T(8,128)(2,1)S(1)} %get-tuple-element.66), channel_id=1, source_target_pairs={{0,8},{8,16},{16,24},{1,9},{9,17},{17,25},{2,10},{10,18},{18,26},{... | collective-permute-start | bytes 1179656 | tf_op jit(solution)/shard_map/ppermute | solution.py:29
  134.1 1.3 collective-permute-done.5.earlier
  135.4 2.6 finish.2
  138.1 15.5 %all-to-all-done.2.refs_0_ = bf16[8,3,2,256,128]{4,3,2,1,0:T(8,128)(2,1)} async-done(((bf16[8,3,2,256,128]{4,3,2,1,0:T(8,128)(2,1)}), bf16[8,3,2,256,128]{4,3,2,1,0:T(8,128)(2,1)}, u32[]{:S(2)}, u32[]{:S(2)}) %all-to-all-start.2) | async-done | bytes 3145760 | tf_op jit(solution)/shard_map/all_to_all | solution.py:71
  153.6 6.1 %all-to-all-start.1 = ((bf16[4,3,2,256,128]{4,3,2,1,0:T(8,128)(2,1)}), bf16[4,3,2,256,128]{4,3,2,1,0:T(8,128)(2,1)S(1)}, u32[]{:S(2)}, u32[]{:S(2)}) async-start(bf16[4,3,2,256,128]{4,3,2,1,0:T(8,128)(2,1)} %get-tuple-element.71), calls=%async_computation.1 | async-start | bytes 3145728 | tf_op jit(solution)/shard_map/all_to_all | solution.py:82
  159.7 2.2 pick.3
  161.9 1.3 collective-permute-start.6
  163.2 1.3 collective-permute-start.7
  164.5 3.9 %prepare.3 = (bf16[3,24,128,128]{3,2,1,0:T(8,128)(2,1)S(1)}, bf16[8,3,256,128]{3,2,1,0:T(8,128)(2,1)S(1)}, f32[3,24,128,128]{3,2,1,0:T(8,128)S(1)}) custom-call(s32[1]{0:T(128)} %bitcast.me, bf16[3,24,128,128]{3,2,1,0:T(8,128)(2,1)S(1)} %get-tuple-element.74.table.table_in, bf16[8,3,2,256,128]{4,3,2,1,0:T(8,128)(2,1)} %all-to-all-done.2.refs_0_), custom_call_target="tpu_custom_call" | custom-call | tf_op jit(solution)/shard_map/prepare/pallas_call | solution.py:449
  168.4 0.1 collective-permute-done.7.came_next
  168.6 30.1 %attend.3 = (bf16[8,3,256,128]{3,2,1,0:T(8,128)(2,1)S(1)}, bf16[4,3,128,128]{3,2,1,0:T(8,128)(2,1)S(1)}, bf16[4,3,128,128]{3,2,1,0:T(8,128)(2,1)S(1)}, bf16[3,24...) custom-call(s32[3,16,8]{2,1,0:T(8,128)S(1)} %get-tuple-element.106.l, ...), custom_call_target="tpu_custom_call", output_to_operand_aliasing={{3}: (4, {}), {4}: (5, {}), {5}: (6, {})} | custom-call | tf_op jit(solution)/shard_map/attend/pallas_call | solution.py:605
  198.6 1.3 collective-permute-start.8
  199.9 8.8 %collective-permute-start.9 = (bf16[4,3,128,128]{3,2,1,0:T(8,128)(2,1)S(1)}, bf16[4,3,128,128]{3,2,1,0:T(8,128)(2,1)S(1)}, u32[]{:S(2)}, u32[]{:S(2)}) collective-permute-start(bf16[4,3,128,128]{3,2,1,0:T(8,128)(2,1)S(1)} %get-tuple-element.81), channel_id=1, source_target_pairs={{0,8},{8,16},{16,24},{1,9},{9,17},{17,25},{2,10},{10,18},{18,26},{... | collective-permute-start | bytes 1179656 | tf_op jit(solution)/shard_map/ppermute | solution.py:29
  208.8 1.3 collective-permute-done.9.earlier
  210.1 2.7 finish.3
  212.8 1.5 collective-permute-start.15
  214.4 17.3 %all-gather = bf16[6,2,256,128]{3,2,1,0:T(8,128)(2,1)S(1)} all-gather(bf16[3,2,256,128]{3,2,1,0:T(8,128)(2,1)S(1)} %copy-done.8), channel_id=2, replica_groups={{0,7},{1,6},{2,5},{3,4},{8,15},{9,14},{10,13},{11,12},{16,23},{17,22},{..., dimensions={0}, use_global_device_ids=true | all-gather | bytes 1179648 | tf_op jit(solution)/shard_map/all_gather | solution.py:80
  231.7 10.2 %all-gather.1 = bf16[6,2,256,128]{3,2,1,0:T(8,128)(2,1)S(1)} all-gather(bf16[3,2,256,128]{3,2,1,0:T(8,128)(2,1)S(1)} %copy-done.11), channel_id=3, replica_groups={{0,6},{1,7},{2,4},{3,5},{8,14},{9,15},{10,12},{11,13},{16,22},{17,23},{..., dimensions={0}, use_global_device_ids=true | all-gather | bytes 1179648 | tf_op jit(solution)/shard_map/all_gather | solution.py:80
  241.8 7.8 %collective-permute-start.10 = (bf16[3,2,256,128]{3,2,1,0:T(8,128)(2,1)}, bf16[3,2,256,128]{3,2,1,0:T(8,128)(2,1)S(1)}, u32[]{:S(2)}, u32[]{:S(2)}) collective-permute-start(bf16[3,2,256,128]{3,2,1,0:T(8,128)(2,1)} %get-tuple-element.82), channel_id=1, source_target_pairs={{0,5},{1,4},{2,7},{3,6},{4,1},{5,0},{6,3},{7,2},{8,13},{9,12},{10,... | collective-permute-start | bytes 1179656 | tf_op jit(solution)/shard_map/ppermute | solution.py:76
  249.7 13.4 %collective-permute-start.11 = (bf16[3,2,256,128]{3,2,1,0:T(8,128)(2,1)}, bf16[3,2,256,128]{3,2,1,0:T(8,128)(2,1)}, u32[]{:S(2)}, u32[]{:S(2)}) collective-permute-start(bf16[3,2,256,128]{3,2,1,0:T(8,128)(2,1)} %get-tuple-element.83), channel_id=1, source_target_pairs={{0,4},{1,5},{2,6},{3,7},{4,0},{5,1},{6,2},{7,3},{8,12},{9,13},{10,... | collective-permute-start | bytes 1179656 | tf_op jit(solution)/shard_map/ppermute | solution.py:76
  263.1 0.5 collective-permute-start.12
  263.6 2.0 collective-permute-start.14
  265.6 74.3 %all-gather.2 = bf16[6,2,256,128]{3,2,1,0:T(8,128)(2,1)} all-gather(bf16[3,2,256,128]{3,2,1,0:T(8,128)(2,1)S(1)} %copy-done.10), channel_id=4, replica_groups={{0,5},{1,4},{2,7},{3,6},{8,13},{9,12},{10,15},{11,14},{16,21},{17,20},{..., dimensions={0}, use_global_device_ids=true | all-gather | bytes 1179648 | tf_op jit(solution)/shard_map/all_gather | solution.py:80
  340.0 22.5 %all-gather.3 = bf16[6,2,256,128]{3,2,1,0:T(8,128)(2,1)} all-gather(bf16[3,2,256,128]{3,2,1,0:T(8,128)(2,1)S(1)} %copy-done.9), channel_id=5, replica_groups={{0,4},{1,5},{2,6},{3,7},{8,12},{9,13},{10,14},{11,15},{16,20},{17,21},{..., dimensions={0}, use_global_device_ids=true | all-gather | bytes 1179648 | tf_op jit(solution)/shard_map/all_gather | solution.py:80
  362.5 1.1 copy-done
  363.6 1.1 copy-done.2
  364.7 2.3 unpack.1
  367.1 2.6 unpack_items.3
  369.8 2.4 unpack_items.4
  372.2 2.9 unpack_items.5
  (54 shorter events, 0.6 us)
Async XLA Ops:
  4.5 6.3 %copy-start.12 = (s32[6,16,8]{1,2,0:T(8,128)S(1)}, s32[6,16,8]{1,2,0:T(8,128)}, u32[]{:S(2)}) copy-start(s32[6,16,8]{1,2,0:T(8,128)} %param.9) | copy-start | bytes 9220
  4.6 74.5 %all-to-all-start = ((bf16[8,3,2,256,128]{4,3,2,1,0:T(8,128)(2,1)}), bf16[8,3,2,256,128]{4,3,2,1,0:T(8,128)(2,1)S(1)}, u32[]{:S(2)}, u32[]{:S(2)}) async-start(bf16[8,3,2,256,128]{4,3,2,1,0:T(8,128)(2,1)} %pack.2), calls=%async_computation | async-start | bytes 6291456 | tf_op jit(solution)/shard_map/all_to_all | solution.py:71
  12.5 5.9 %collective-permute-start = (s32[4]{0:T(128)S(1)}, s32[4]{0:T(128)S(1)}, u32[]{:S(2)}, u32[]{:S(2)}) collective-permute-start(s32[4]{0:T(128)S(1)} %get-tuple-element.109), channel_id=1, source_target_pairs={{8,0},{16,8},{24,16},{9,1},{17,9},{25,17},{10,2},{18,10},{26,18},{... | collective-permute-start | bytes 56 | tf_op jit(solution)/shard_map/ppermute | solution.py:29
  15.0 3.8 %collective-permute-start.1 = (s32[4]{0:T(128)S(1)}, s32[4]{0:T(128)S(1)}, u32[]{:S(2)}, u32[]{:S(2)}) collective-permute-start(s32[4]{0:T(128)S(1)} %get-tuple-element.111), channel_id=1, source_target_pairs={{0,8},{8,16},{16,24},{1,9},{9,17},{17,25},{2,10},{10,18},{18,26},{... | collective-permute-start | bytes 56 | tf_op jit(solution)/shard_map/ppermute | solution.py:29
  79.1 74.5 %all-to-all-start.2 = ((bf16[8,3,2,256,128]{4,3,2,1,0:T(8,128)(2,1)}), bf16[8,3,2,256,128]{4,3,2,1,0:T(8,128)(2,1)}, u32[]{:S(2)}, u32[]{:S(2)}) async-start(bf16[8,3,2,256,128]{4,3,2,1,0:T(8,128)(2,1)} %pack.3), calls=%async_computation.2 | async-start | bytes 6291456 | tf_op jit(solution)/shard_map/all_to_all | solution.py:71
  87.3 7.2 %collective-permute-start.2 = (bf16[4,3,128,128]{3,2,1,0:T(8,128)(2,1)S(1)}, bf16[4,3,128,128]{3,2,1,0:T(8,128)(2,1)S(1)}, u32[]{:S(2)}, u32[]{:S(2)}) collective-permute-start(bf16[4,3,128,128]{3,2,1,0:T(8,128)(2,1)S(1)} %get-tuple-element.57), channel_id=1, source_target_pairs={{0,8},{8,16},{16,24},{1,9},{9,17},{17,25},{2,10},{10,18},{18,26},{... | collective-permute-start | bytes 1179656 | tf_op jit(solution)/shard_map/ppermute | solution.py:29
  88.6 5.9 %collective-permute-start.3 = (bf16[4,3,128,128]{3,2,1,0:T(8,128)(2,1)S(1)}, bf16[4,3,128,128]{3,2,1,0:T(8,128)(2,1)S(1)}, u32[]{:S(2)}, u32[]{:S(2)}) collective-permute-start(bf16[4,3,128,128]{3,2,1,0:T(8,128)(2,1)S(1)} %get-tuple-element.58), channel_id=1, source_target_pairs={{8,0},{16,8},{24,16},{9,1},{17,9},{25,17},{10,2},{18,10},{26,18},{... | collective-permute-start | bytes 1179656 | tf_op jit(solution)/shard_map/ppermute | solution.py:29
  124.4 9.7 %collective-permute-start.4 = (bf16[4,3,128,128]{3,2,1,0:T(8,128)(2,1)S(1)}, bf16[4,3,128,128]{3,2,1,0:T(8,128)(2,1)S(1)}, u32[]{:S(2)}, u32[]{:S(2)}) collective-permute-start(bf16[4,3,128,128]{3,2,1,0:T(8,128)(2,1)S(1)} %get-tuple-element.65), channel_id=1, source_target_pairs={{8,0},{16,8},{24,16},{9,1},{17,9},{25,17},{10,2},{18,10},{26,18},{... | collective-permute-start | bytes 1179656 | tf_op jit(solution)/shard_map/ppermute | solution.py:29
  125.7 9.7 %collective-permute-start.5 = (bf16[4,3,128,128]{3,2,1,0:T(8,128)(2,1)S(1)}, bf16[4,3,128,128]{3,2,1,0:T(8,128)(2,1)S(1)}, u32[]{:S(2)}, u32[]{:S(2)}) collective-permute-start(bf16[4,3,128,128]{3,2,1,0:T(8,128)(2,1)S(1)} %get-tuple-element.66), channel_id=1, source_target_pairs={{0,8},{8,16},{16,24},{1,9},{9,17},{17,25},{2,10},{10,18},{18,26},{... | collective-permute-start | bytes 1179656 | tf_op jit(solution)/shard_map/ppermute | solution.py:29
  153.6 208.9 %all-to-all-start.1 = ((bf16[4,3,2,256,128]{4,3,2,1,0:T(8,128)(2,1)}), bf16[4,3,2,256,128]{4,3,2,1,0:T(8,128)(2,1)S(1)}, u32[]{:S(2)}, u32[]{:S(2)}) async-start(bf16[4,3,2,256,128]{4,3,2,1,0:T(8,128)(2,1)} %get-tuple-element.71), calls=%async_computation.1 | async-start | bytes 3145728 | tf_op jit(solution)/shard_map/all_to_all | solution.py:82
  161.9 6.5 %collective-permute-start.6 = (bf16[4,3,128,128]{3,2,1,0:T(8,128)(2,1)S(1)}, bf16[4,3,128,128]{3,2,1,0:T(8,128)(2,1)S(1)}, u32[]{:S(2)}, u32[]{:S(2)}) collective-permute-start(bf16[4,3,128,128]{3,2,1,0:T(8,128)(2,1)S(1)} %get-tuple-element.72), channel_id=1, source_target_pairs={{0,8},{8,16},{16,24},{1,9},{9,17},{17,25},{2,10},{10,18},{18,26},{... | collective-permute-start | bytes 1179656 | tf_op jit(solution)/shard_map/ppermute | solution.py:29
  163.2 5.3 %collective-permute-start.7 = (bf16[4,3,128,128]{3,2,1,0:T(8,128)(2,1)S(1)}, bf16[4,3,128,128]{3,2,1,0:T(8,128)(2,1)S(1)}, u32[]{:S(2)}, u32[]{:S(2)}) collective-permute-start(bf16[4,3,128,128]{3,2,1,0:T(8,128)(2,1)S(1)} %get-tuple-element.73), channel_id=1, source_target_pairs={{8,0},{16,8},{24,16},{9,1},{17,9},{25,17},{10,2},{18,10},{26,18},{... | collective-permute-start | bytes 1179656 | tf_op jit(solution)/shard_map/ppermute | solution.py:29
  198.6 10.1 %collective-permute-start.8 = (bf16[4,3,128,128]{3,2,1,0:T(8,128)(2,1)S(1)}, bf16[4,3,128,128]{3,2,1,0:T(8,128)(2,1)S(1)}, u32[]{:S(2)}, u32[]{:S(2)}) collective-permute-start(bf16[4,3,128,128]{3,2,1,0:T(8,128)(2,1)S(1)} %get-tuple-element.80), channel_id=1, source_target_pairs={{8,0},{16,8},{24,16},{9,1},{17,9},{25,17},{10,2},{18,10},{26,18},{... | collective-permute-start | bytes 1179656 | tf_op jit(solution)/shard_map/ppermute | solution.py:29
  199.9 10.1 %collective-permute-start.9 = (bf16[4,3,128,128]{3,2,1,0:T(8,128)(2,1)S(1)}, bf16[4,3,128,128]{3,2,1,0:T(8,128)(2,1)S(1)}, u32[]{:S(2)}, u32[]{:S(2)}) collective-permute-start(bf16[4,3,128,128]{3,2,1,0:T(8,128)(2,1)S(1)} %get-tuple-element.81), channel_id=1, source_target_pairs={{0,8},{8,16},{16,24},{1,9},{9,17},{17,25},{2,10},{10,18},{18,26},{... | collective-permute-start | bytes 1179656 | tf_op jit(solution)/shard_map/ppermute | solution.py:29
  210.1 4.3 %copy-start.8 = (bf16[3,2,256,128]{3,2,1,0:T(8,128)(2,1)S(1)}, bf16[3,2,256,128]{3,2,1,0:T(8,128)(2,1)}, u32[]{:S(2)}) copy-start(bf16[3,2,256,128]{3,2,1,0:T(8,128)(2,1)} %get-tuple-element.67.refs_1_) | copy-start | bytes 1179652
  210.1 21.6 %copy-start.11 = (bf16[3,2,256,128]{3,2,1,0:T(8,128)(2,1)S(1)}, bf16[3,2,256,128]{3,2,1,0:T(8,128)(2,1)}, u32[]{:S(2)}) copy-start(bf16[3,2,256,128]{3,2,1,0:T(8,128)(2,1)} %get-tuple-element.68) | copy-start | bytes 1179652
  212.8 52.9 %copy-start.10 = (bf16[3,2,256,128]{3,2,1,0:T(8,128)(2,1)S(1)}, bf16[3,2,256,128]{3,2,1,0:T(8,128)(2,1)}, u32[]{:S(2)}) copy-start(bf16[3,2,256,128]{3,2,1,0:T(8,128)(2,1)} %get-tuple-element.69) | copy-start | bytes 1179652
  212.8 50.8 %collective-permute-start.15 = (bf16[3,2,256,128]{3,2,1,0:T(8,128)(2,1)}, bf16[3,2,256,128]{3,2,1,0:T(8,128)(2,1)S(1)}, u32[]{:S(2)}, u32[]{:S(2)}) collective-permute-start(bf16[3,2,256,128]{3,2,1,0:T(8,128)(2,1)} %get-tuple-element.88), channel_id=1, source_target_pairs={{0,1},{1,0},{2,3},{3,2},{4,5},{5,4},{6,7},{7,6},{8,9},{9,8},{10,11... | collective-permute-start | bytes 1179656 | tf_op jit(solution)/shard_map/ppermute | solution.py:76
  214.3 125.7 %copy-start.9 = (bf16[3,2,256,128]{3,2,1,0:T(8,128)(2,1)S(1)}, bf16[3,2,256,128]{3,2,1,0:T(8,128)(2,1)}, u32[]{:S(2)}) copy-start(bf16[3,2,256,128]{3,2,1,0:T(8,128)(2,1)} %get-tuple-element.70) | copy-start | bytes 1179652
  214.3 49.3 %collective-permute-start.16 = (bf16[3,2,256,128]{3,2,1,0:T(8,128)(2,1)}, bf16[3,2,256,128]{3,2,1,0:T(8,128)(2,1)S(1)}, u32[]{:S(2)}, u32[]{:S(2)}) collective-permute-start(bf16[3,2,256,128]{3,2,1,0:T(8,128)(2,1)} %get-tuple-element.89), channel_id=1, source_target_pairs={{0,3},{1,2},{2,1},{3,0},{4,7},{5,6},{6,5},{7,4},{8,11},{9,10},{10,... | collective-permute-start | bytes 1179656 | tf_op jit(solution)/shard_map/ppermute | solution.py:76
  241.8 130.3 %collective-permute-start.10 = (bf16[3,2,256,128]{3,2,1,0:T(8,128)(2,1)}, bf16[3,2,256,128]{3,2,1,0:T(8,128)(2,1)S(1)}, u32[]{:S(2)}, u32[]{:S(2)}) collective-permute-start(bf16[3,2,256,128]{3,2,1,0:T(8,128)(2,1)} %get-tuple-element.82), channel_id=1, source_target_pairs={{0,5},{1,4},{2,7},{3,6},{4,1},{5,0},{6,3},{7,2},{8,13},{9,12},{10,... | collective-permute-start | bytes 1179656 | tf_op jit(solution)/shard_map/ppermute | solution.py:76
  249.7 122.5 %collective-permute-start.11 = (bf16[3,2,256,128]{3,2,1,0:T(8,128)(2,1)}, bf16[3,2,256,128]{3,2,1,0:T(8,128)(2,1)}, u32[]{:S(2)}, u32[]{:S(2)}) collective-permute-start(bf16[3,2,256,128]{3,2,1,0:T(8,128)(2,1)} %get-tuple-element.83), channel_id=1, source_target_pairs={{0,4},{1,5},{2,6},{3,7},{4,0},{5,1},{6,2},{7,3},{8,12},{9,13},{10,... | collective-permute-start | bytes 1179656 | tf_op jit(solution)/shard_map/ppermute | solution.py:76
  263.1 109.1 %collective-permute-start.12 = (bf16[3,2,256,128]{3,2,1,0:T(8,128)(2,1)}, bf16[3,2,256,128]{3,2,1,0:T(8,128)(2,1)}, u32[]{:S(2)}, u32[]{:S(2)}) collective-permute-start(bf16[3,2,256,128]{3,2,1,0:T(8,128)(2,1)} %get-tuple-element.84), channel_id=1, source_target_pairs={{0,2},{1,3},{2,0},{3,1},{4,6},{5,7},{6,4},{7,5},{8,10},{9,11},{10,... | collective-permute-start | bytes 1179656 | tf_op jit(solution)/shard_map/ppermute | solution.py:76
  263.6 76.4 %copy-start.4 = (bf16[3,2,256,128]{3,2,1,0:T(8,128)(2,1)}, bf16[3,2,256,128]{3,2,1,0:T(8,128)(2,1)S(1)}, u32[]{:S(2)}) copy-start(bf16[3,2,256,128]{3,2,1,0:T(8,128)(2,1)S(1)} %collective-permute-done.15.refs_6_) | copy-start | bytes 1179652
  263.6 106.1 %collective-permute-start.13 = (bf16[3,2,256,128]{3,2,1,0:T(8,128)(2,1)}, bf16[3,2,256,128]{3,2,1,0:T(8,128)(2,1)}, u32[]{:S(2)}, u32[]{:S(2)}) collective-permute-start(bf16[3,2,256,128]{3,2,1,0:T(8,128)(2,1)} %get-tuple-element.85), channel_id=1, source_target_pairs={{0,7},{1,6},{2,5},{3,4},{4,3},{5,2},{6,1},{7,0},{8,15},{9,14},{10,... | collective-permute-start | bytes 1179656 | tf_op jit(solution)/shard_map/ppermute | solution.py:76
  263.6 76.4 %copy-start.6 = (bf16[3,2,256,128]{3,2,1,0:T(8,128)(2,1)}, bf16[3,2,256,128]{3,2,1,0:T(8,128)(2,1)S(1)}, u32[]{:S(2)}) copy-start(bf16[3,2,256,128]{3,2,1,0:T(8,128)(2,1)S(1)} %collective-permute-done.16.refs_7_) | copy-start | bytes 1179652
  263.6 106.1 %collective-permute-start.14 = (bf16[3,2,256,128]{3,2,1,0:T(8,128)(2,1)}, bf16[3,2,256,128]{3,2,1,0:T(8,128)(2,1)}, u32[]{:S(2)}, u32[]{:S(2)}) collective-permute-start(bf16[3,2,256,128]{3,2,1,0:T(8,128)(2,1)} %get-tuple-element.86), channel_id=1, source_target_pairs={{0,6},{1,7},{2,4},{3,5},{4,2},{5,3},{6,0},{7,1},{8,14},{9,15},{10,... | collective-permute-start | bytes 1179656 | tf_op jit(solution)/shard_map/ppermute | solution.py:76
  362.5 1.1 copy-start
  363.6 1.1 copy-start.2
  364.7 2.3 copy-start.1
  364.7 2.3 copy-start.3
  364.7 2.3 copy-start.5
  364.7 2.4 copy-start.7

commit v16 on v11

--- a/solution.py
+++ b/solution.py
@@ -51,26 +51,32 @@
 
 def hold(arrays, after):
     count = len(arrays)
-    anywhere = pl.BlockSpec(memory_space=pltpu.HBM)
-    return pl.pallas_call(
+    anywhere = pl.BlockSpec(memory_space=pl.ANY)
+    held = pl.pallas_call(
         hold_kernel,
         in_specs=[anywhere] * (count + len(after)),
         out_specs=[anywhere] * count,
-        out_shape=[pltpu.HBM(x.shape, x.dtype) for x in arrays],
+        out_shape=[jax.ShapeDtypeStruct(x.shape, x.dtype) for x in arrays],
         input_output_aliases={i: i for i in range(count)},
         name="hold",
-    )(*[in_hbm(x) for x in (*arrays, *after)])
+    )(*arrays, *after)
+    return list(held)
+
+
+def swap(messages, first, last):
+    count = len(messages)
+    return [
+        lax.ppermute(
+            messages[item], "seq", [(i, i ^ (count - 1 - item)) for i in range(count)]
+        )
+        for item in range(first, last)
+    ]
 
 
 def exchange(messages):
     if len(messages) == 1:
         return [lax.all_to_all(messages[0], "seq", split_axis=0, concat_axis=0, tiled=True)]
-    count = len(messages)
-    received = list(messages)
-    for item in range(count - 1):
-        pairs = [(i, i ^ (count - 1 - item)) for i in range(count)]
-        received[item] = lax.ppermute(messages[item], "seq", pairs)
-    return received
+    return swap(messages, 0, len(messages) - 1) + list(messages[-1:])
 
 
 def pack_kernel(
@@ -258,7 +264,8 @@
             jobs=jobs,
         ),
         in_specs=[pl.BlockSpec(memory_space=pltpu.SMEM)]
-        + [anywhere] * (len(flat) + len(earlier)),
+        + [pl.BlockSpec(memory_space=pl.ANY)] * len(flat)
+        + [anywhere] * len(earlier),
         out_specs=[anywhere] * 4,
         out_shape=[pltpu.HBM((rows, columns), dtype)] * 4,
         input_output_aliases={1 + len(flat) + i: i for i in range(len(earlier))},
@@ -270,7 +277,7 @@
         ],
         compiler_params=pltpu.CompilerParams(vmem_limit_bytes=SMALL_VMEM),
         name="unpack",
-    )(me, *[in_hbm(x) for x in (*flat, *earlier)])
+    )(me, *flat, *[in_hbm(x) for x in earlier])
 
 
 def unpack_items_kernel(me, *refs, items, peers, counts, joint, earlier, jobs, per_peer):
@@ -358,7 +365,8 @@
             per_peer=per_peer,
         ),
         in_specs=[pl.BlockSpec(memory_space=pltpu.SMEM)]
-        + [anywhere] * (len(flat) + len(earlier)),
+        + [pl.BlockSpec(memory_space=pl.ANY)] * len(flat)
+        + [anywhere] * len(earlier),
         out_specs=[anywhere] * 4,
         out_shape=[pltpu.HBM((rows, peers * per_peer), dtype)] * 4,
         input_output_aliases={1 + len(flat) + i: i for i in range(len(earlier))},
@@ -372,16 +380,17 @@
         ],
         compiler_params=pltpu.CompilerParams(vmem_limit_bytes=SMALL_VMEM),
         name="unpack_items",
-    )(me, *[in_hbm(x) for x in (*flat, *earlier)])
-
-
-def pick_kernel(me, asked, *refs, count):
+    )(me, *flat, *[in_hbm(x) for x in earlier])
+
+
+def pick_kernel(me, asked, *refs, order):
+    messages = [refs[order.index(item)] for item in range(len(order))]
     for_next, for_prev, table, sems = refs[-4:]
     heads, window, block_rows, _ = table.shape
     peers, each = sems.shape
 
     def fetch(item, i):
-        source, peer = part_of(refs[:count], me, item)
+        source, peer = part_of(messages, me, item)
         rows = pl.ds(i * block_rows, block_rows)
         return pltpu.make_async_copy(
             source.at[:, 0, rows], table.at[:, CROSS + peer * each + i], sems.at[item, i]
@@ -398,7 +407,7 @@
         for_prev[i] = table[:, CROSS + asked[CROSS + i]]
 
 
-def pick(me, messages, asked, block_rows, after):
+def pick(me, messages, asked, block_rows, order, after):
     heads, _, rows, lanes = message_shape(messages)
     dtype = messages[0].dtype
     peers = lax.axis_size("seq")
@@ -406,15 +415,15 @@
     window = peers * each + 2 * CROSS
     picked = jax.ShapeDtypeStruct((CROSS, heads, block_rows, lanes), dtype)
     return pl.pallas_call(
-        functools.partial(pick_kernel, count=len(messages)),
+        functools.partial(pick_kernel, order=order),
         in_specs=[pl.BlockSpec(memory_space=pltpu.SMEM)] * 2
-        + [pl.BlockSpec(memory_space=pltpu.HBM)] * (len(messages) + len(after)),
+        + [pl.BlockSpec(memory_space=pl.ANY)] * (len(messages) + len(after)),
         out_specs=[pl.BlockSpec(memory_space=pltpu.VMEM)] * 3,
         out_shape=[picked, picked, pltpu.VMEM((heads, window, block_rows, lanes), dtype)],
         scratch_shapes=[pltpu.SemaphoreType.DMA((peers, each))],
         compiler_params=pltpu.CompilerParams(vmem_limit_bytes=SMALL_VMEM),
         name="pick",
-    )(me, asked, *[in_hbm(x) for x in (*messages, *after)])
+    )(me, asked, *[messages[item] for item in order], *[in_hbm(x) for x in after])
 
 
 def prepare_kernel(me, table, *refs, peers):
@@ -453,7 +462,7 @@
     return pl.pallas_call(
         functools.partial(prepare_kernel, peers=peers),
         in_specs=[pl.BlockSpec(memory_space=pltpu.SMEM), inside]
-        + [pl.BlockSpec(memory_space=pltpu.HBM)] * len(messages),
+        + [pl.BlockSpec(memory_space=pl.ANY)] * len(messages),
         out_specs=[inside] * 3,
         out_shape=[
             pltpu.VMEM((heads, window, lanes, block_rows), dtype),
@@ -463,7 +472,7 @@
         scratch_shapes=[pltpu.SemaphoreType.DMA((peers,))],
         compiler_params=pltpu.CompilerParams(vmem_limit_bytes=SMALL_VMEM),
         name="prepare",
-    )(me, in_vmem(table), *[in_hbm(x) for x in messages])
+    )(me, in_vmem(table), *messages)
 
 
 def attend_kernel(
@@ -724,21 +733,27 @@
     )
 
     me = lax.axis_index("seq").astype(jnp.int32).reshape(1)
-    me = lax.axis_index("seq").astype(jnp.int32).reshape(1)
     last = chunks - 1
+    half = peers // 2
+    near = list(range(peers - 2, half - 1, -1))
+    parts = (near[::2], list(range(half // 2)), [*range(half // 2, half), *near[1::2]])
     came = []
     for chunk, (start, size) in enumerate(zip(starts, sizes)):
         after = (asked, local_ids) if came else ()
-        packed = pack(
-            me, arrays, start, size, heads_here, peers, head_dim, chunk == 0, after
+        packed = list(
+            pack(me, arrays, start, size, heads_here, peers, head_dim, chunk == 0, after)
         )
         if chunk == 1:
-            packed = hold(packed, came[0][:-1])
+            packed = hold(packed, [came[0][item] for part in parts for item in part])
         came.append(exchange(packed))
     received = []
     outs = finished = ()
     for chunk, (messages, start, size) in enumerate(zip(came, starts, sizes)):
-        for_next, for_prev, table = pick(me, messages, asked, block_rows, finished[:1])
+        order = [item for part in parts for item in part] + [peers - 1]
+        order = order if len(messages) > 1 else [0]
+        for_next, for_prev, table = pick(
+            me, messages, asked, block_rows, order, finished[:1]
+        )
         came_prev = from_behind(for_next, "slab", 1)
         came_next = from_behind(for_prev, "slab", -1)
         turned, pairs, sums = prepare(me, messages, table)
@@ -751,13 +766,7 @@
         finished = finish(me, back, kept, later, earlier, asked, chunk == last)
         received.append(exchange(finished))
         if chunk == last and heads_here * head_dim % LANES == 0:
-            half = peers // 2
-            parts = (
-                [peers - 1, *range(half // 2)],
-                [*range(half // 2, half - 1), *range(half, peers - 1)],
-                [half - 1],
-            )
-            for items in parts:
+            for items in ([peers - 1, *parts[0]], *parts[1:]):
                 outs = unpack_items(me, received, starts, heads_here, items, outs)
         else:
             outs = unpack(me, received, starts, heads_here, outs)

time: 307 us -> 312 us (1.016)
  the two profiles are of different devices: /device:TPU:2 before, /device:TPU:8 now
where the time goes in v16:
time: 312 us; the launch traced here: 307 us
  waiting for transfers between devices  128 us (41%)
  Pallas kernels  93.5 us (30%)
  starting transfers between devices  66.5 us (21%)
  local copies, waits for them, and re-layouts  14.6 us (5%)
    ppermute x14, waiting for transfers between devices, swap(): lax.ppermute(messages[item], 'seq', [(i, i ^ count - 1 - item) for i in r...  107 us
    pallas_call x2, Pallas kernels, attend(): pl.pallas_call(functools.partial(attend_kernel, head_dim=lanes // 2, per_...  58.3 us
    ppermute x14, starting transfers between devices, swap(): lax.ppermute(messages[item], 'seq', [(i, i ^ count - 1 - item) for i in r...  28.1 us
    ppermute x10, starting transfers between devices, from_behind(): return lax.ppermute(x, axis, pairs)  26.2 us
    all_to_all x2, waiting for transfers between devices, exchange(): lax.all_to_all(messages[0], 'seq', split_axis=0, concat_axis=0, tiled=True)  18.9 us
    unnamed x55, local copies, waits for them, and re-layouts  13.7 us
    all_to_all x2, starting transfers between devices, exchange(): lax.all_to_all(messages[0], 'seq', split_axis=0, concat_axis=0, tiled=True)  12.2 us
    pallas_call x2, Pallas kernels, prepare(): pl.pallas_call(functools.partial(prepare_kernel, peers=peers), in_specs=[...  9.13 us
  transfers between devices with their start and end apart: 26, of which 15 were waited for; matrix products, arithmetic and copies ran while one was open for 1% of the time, Pallas kernels for 28%

profile of v16, /device:TPU:8, one launch (start us, length us, event | category | flops | bytes accessed | tf_op | source)
XLA Modules:
  0.0 307.0 jit_solution(16331302911622379038)
XLA Ops:
  0.6 3.9 %pack.2 = (bf16[3,2,256,128]{3,2,1,0:T(8,128)(2,1)}, bf16[3,2,256,128]{3,2,1,0:T(8,128)(2,1)}, bf16[3,2,256,128]{3,2,1,0:T(8,128)(2,1)}, bf16[3,2,256,128]{3,2,1...) custom-call(s32[1]{0:T(128)} %bitcast.me, ...), custom_call_target="tpu_custom_call" | custom-call | tf_op jit(solution)/shard_map/pack/pallas_call | solution.py:151
  4.5 1.6 collective-permute-start.2
  7.7 1.4 collective-permute-start.1
  11.7 3.9 %collective-permute-start.4 = (bf16[3,2,256,128]{3,2,1,0:T(8,128)(2,1)}, bf16[3,2,256,128]{3,2,1,0:T(8,128)(2,1)S(1)}, u32[]{:S(2)}, u32[]{:S(2)}) collective-permute-start(bf16[3,2,256,128]{3,2,1,0:T(8,128)(2,1)} %get-tuple-element.62), channel_id=1, source_target_pairs={{0,7},{1,6},{2,5},{3,4},{4,3},{5,2},{6,1},{7,0},{8,15},{9,14},{10,... | collective-permute-start | bytes 1179656 | tf_op jit(solution)/shard_map/ppermute | solution.py:69
  15.7 3.7 %collective-permute-start.6 = (bf16[3,2,256,128]{3,2,1,0:T(8,128)(2,1)}, bf16[3,2,256,128]{3,2,1,0:T(8,128)(2,1)S(1)}, u32[]{:S(2)}, u32[]{:S(2)}) collective-permute-start(bf16[3,2,256,128]{3,2,1,0:T(8,128)(2,1)} %get-tuple-element.64), channel_id=1, source_target_pairs={{0,5},{1,4},{2,7},{3,6},{4,1},{5,0},{6,3},{7,2},{8,13},{9,12},{10,... | collective-permute-start | bytes 1179656 | tf_op jit(solution)/shard_map/ppermute | solution.py:69
  19.3 6.1 %collective-permute-done.2.refs_0_.refs_6_.refs_1_ = bf16[3,2,256,128]{3,2,1,0:T(8,128)(2,1)S(1)} collective-permute-done((bf16[3,2,256,128]{3,2,1,0:T(8,128)(2,1)}, bf16[3,2,256,128]{3,2,1,0:T(8,128)(2,1)S(1)}, u32[]{:S(2)}, u32[]{:S(2)}) %collective-permute-start.2) | collective-permute-done | bytes 393248 | tf_op jit(solution)/shard_map/ppermute | solution.py:69
  25.4 9.7 %collective-permute-start.7 = (bf16[3,2,256,128]{3,2,1,0:T(8,128)(2,1)}, bf16[3,2,256,128]{3,2,1,0:T(8,128)(2,1)S(1)}, u32[]{:S(2)}, u32[]{:S(2)}) collective-permute-start(bf16[3,2,256,128]{3,2,1,0:T(8,128)(2,1)} %get-tuple-element.65), channel_id=1, source_target_pairs={{0,4},{1,5},{2,6},{3,7},{4,0},{5,1},{6,2},{7,3},{8,12},{9,13},{10,... | collective-permute-start | bytes 1179656 | tf_op jit(solution)/shard_map/ppermute | solution.py:69
  35.5 3.9 %pack.3.refs_0_ = bf16[8,3,2,256,128]{4,3,2,1,0:T(8,128)(2,1)} custom-call(s32[1]{0:T(128)} %bitcast.me, bf16[256,3072]{1,0:T(8,128)(2,1)} %query.3, bf16[256,3072]{1,0:T(8,128)(2,1)} %key.3, bf16[256,3072]{1,0:T(8,128)(2,1)} %value.3, bf16[256,3072]{1,0:T(8,128)(2,1)} %d_out.3, s32[8]{0:T(128)S(1)} %pad_add_fusion.asked.refs_0_, ...), custom_call_target="tpu_custom_call" | custom-call | tf_op jit(solution)/shard_map/pack/pallas_call | solution.py:151
  39.4 19.0 %collective-permute-done.4.refs_2_.refs_0_.refs_3_ = bf16[3,2,256,128]{3,2,1,0:T(8,128)(2,1)S(1)} collective-permute-done((bf16[3,2,256,128]{3,2,1,0:T(8,128)(2,1)}, bf16[3,2,256,128]{3,2,1,0:T(8,128)(2,1)S(1)}, u32[]{:S(2)}, u32[]{:S(2)}) %collective-permute-start.4) | collective-permute-done | bytes 393248 | tf_op jit(solution)/shard_map/ppermute | solution.py:69
  58.4 8.2 %collective-permute-done.5.refs_3_.refs_1_.refs_4_ = bf16[3,2,256,128]{3,2,1,0:T(8,128)(2,1)S(1)} collective-permute-done((bf16[3,2,256,128]{3,2,1,0:T(8,128)(2,1)}, bf16[3,2,256,128]{3,2,1,0:T(8,128)(2,1)S(1)}, u32[]{:S(2)}, u32[]{:S(2)}) %collective-permute-start.5) | collective-permute-done | bytes 393248 | tf_op jit(solution)/shard_map/ppermute | solution.py:69
  66.7 8.4 %collective-permute-done.6.refs_4_.refs_2_.refs_5_ = bf16[3,2,256,128]{3,2,1,0:T(8,128)(2,1)S(1)} collective-permute-done((bf16[3,2,256,128]{3,2,1,0:T(8,128)(2,1)}, bf16[3,2,256,128]{3,2,1,0:T(8,128)(2,1)S(1)}, u32[]{:S(2)}, u32[]{:S(2)}) %collective-permute-start.6) | collective-permute-done | bytes 393248 | tf_op jit(solution)/shard_map/ppermute | solution.py:69
  75.1 8.4 %collective-permute-done.7.refs_5_.refs_3_.refs_6_ = bf16[3,2,256,128]{3,2,1,0:T(8,128)(2,1)S(1)} collective-permute-done((bf16[3,2,256,128]{3,2,1,0:T(8,128)(2,1)}, bf16[3,2,256,128]{3,2,1,0:T(8,128)(2,1)S(1)}, u32[]{:S(2)}, u32[]{:S(2)}) %collective-permute-start.7) | collective-permute-done | bytes 393248 | tf_op jit(solution)/shard_map/ppermute | solution.py:69
  85.0 6.1 %all-to-all-start.1 = ((bf16[8,3,2,256,128]{4,3,2,1,0:T(8,128)(2,1)}), bf16[8,3,2,256,128]{4,3,2,1,0:T(8,128)(2,1)S(1)}, u32[]{:S(2)}, u32[]{:S(2)}) async-start(bf16[8,3,2,256,128]{4,3,2,1,0:T(8,128)(2,1)} %hold.1), calls=%async_computation.1 | async-start | bytes 6291456 | tf_op jit(solution)/shard_map/all_to_all | solution.py:78
  98.1 1.5 pick.2
  99.7 1.3 collective-permute-start.10
  101.0 3.1 collective-permute-start.9
  104.6 4.6 %prepare.2 = (bf16[3,24,128,128]{3,2,1,0:T(8,128)(2,1)S(1)}, bf16[8,3,256,128]{3,2,1,0:T(8,128)(2,1)S(1)}, f32[3,24,128,128]{3,2,1,0:T(8,128)S(1)}) custom-call(s32[1]{0:T(128)} %bitcast.me, bf16[3,24,128,128]{3,2,1,0:T(8,128)(2,1)S(1)} %get-tuple-element.70.table.table_in, bf16[3,2,256,128]{3,2,1,0:T(8,128)(2,1)S(1)} %copy-done.8, ...), custom_call_target="tpu_custom_call" | custom-call | tf_op jit(solution)/shard_map/prepare/pallas_call | solution.py:462
  109.2 29.4 %attend.2 = (bf16[8,3,256,128]{3,2,1,0:T(8,128)(2,1)S(1)}, bf16[4,3,128,128]{3,2,1,0:T(8,128)(2,1)S(1)}, bf16[4,3,128,128]{3,2,1,0:T(8,128)(2,1)S(1)}, bf16[3,24...) custom-call(s32[3,16,8]{2,1,0:T(8,128)S(1)} %get-tuple-element.113.l, ...), custom_call_target="tpu_custom_call", output_to_operand_aliasing={{3}: (4, {}), {4}: (5, {}), {5}: (6, {})} | custom-call | tf_op jit(solution)/shard_map/attend/pallas_call | solution.py:618
  138.7 1.3 collective-permute-start.11
  140.0 5.4 %collective-permute-start.12 = (bf16[4,3,128,128]{3,2,1,0:T(8,128)(2,1)S(1)}, bf16[4,3,128,128]{3,2,1,0:T(8,128)(2,1)S(1)}, u32[]{:S(2)}, u32[]{:S(2)}) collective-permute-start(bf16[4,3,128,128]{3,2,1,0:T(8,128)(2,1)S(1)} %get-tuple-element.77), channel_id=1, source_target_pairs={{0,8},{8,16},{16,24},{1,9},{9,17},{17,25},{2,10},{10,18},{18,26},{... | collective-permute-start | bytes 1179656 | tf_op jit(solution)/shard_map/ppermute | solution.py:29
  145.4 1.3 collective-permute-done.12.earlier
  146.7 2.6 finish.2.refs_1_
  149.3 11.0 %all-to-all-done.1.refs_0_ = bf16[8,3,2,256,128]{4,3,2,1,0:T(8,128)(2,1)S(1)} async-done(((bf16[8,3,2,256,128]{4,3,2,1,0:T(8,128)(2,1)}), bf16[8,3,2,256,128]{4,3,2,1,0:T(8,128)(2,1)S(1)}, u32[]{:S(2)}, u32[]{:S(2)}) %all-to-all-start.1) | async-done | bytes 3145760 | tf_op jit(solution)/shard_map/all_to_all | solution.py:78
  160.4 1.7 copy-done
  162.1 6.1 %all-to-all-start = ((bf16[8,3,2,256,128]{4,3,2,1,0:T(8,128)(2,1)}), bf16[8,3,2,256,128]{4,3,2,1,0:T(8,128)(2,1)S(1)}, u32[]{:S(2)}, u32[]{:S(2)}) async-start(bf16[8,3,2,256,128]{4,3,2,1,0:T(8,128)(2,1)} %finish.2.refs_1_), calls=%async_computation | async-start | bytes 6291456 | tf_op jit(solution)/shard_map/all_to_all | solution.py:78
  168.2 1.9 copy-done.1
  170.0 1.4 pick.3
  171.5 1.4 collective-permute-start.13
  172.9 1.3 collective-permute-start.14
  174.3 4.6 %prepare.3 = (bf16[3,24,128,128]{3,2,1,0:T(8,128)(2,1)S(1)}, bf16[8,3,256,128]{3,2,1,0:T(8,128)(2,1)S(1)}, f32[3,24,128,128]{3,2,1,0:T(8,128)S(1)}) custom-call(s32[1]{0:T(128)} %bitcast.me, bf16[3,24,128,128]{3,2,1,0:T(8,128)(2,1)S(1)} %get-tuple-element.80.table.table_in, bf16[8,3,2,256,128]{4,3,2,1,0:T(8,128)(2,1)S(1)} %copy-done.2), custom_call_target="tpu_custom_call" | custom-call | tf_op jit(solution)/shard_map/prepare/pallas_call | solution.py:462
  178.9 28.9 %attend.3 = (bf16[8,3,256,128]{3,2,1,0:T(8,128)(2,1)S(1)}, bf16[4,3,128,128]{3,2,1,0:T(8,128)(2,1)S(1)}, bf16[4,3,128,128]{3,2,1,0:T(8,128)(2,1)S(1)}, bf16[3,24...) custom-call(s32[3,16,8]{2,1,0:T(8,128)S(1)} %copy-done.25, ...), custom_call_target="tpu_custom_call", output_to_operand_aliasing={{3}: (4, {}), {4}: (5, {}), {5}: (6, {})} | custom-call | tf_op jit(solution)/shard_map/attend/pallas_call | solution.py:618
  207.8 1.3 collective-permute-start.15
  209.1 8.4 %collective-permute-start.16 = (bf16[4,3,128,128]{3,2,1,0:T(8,128)(2,1)S(1)}, bf16[4,3,128,128]{3,2,1,0:T(8,128)(2,1)S(1)}, u32[]{:S(2)}, u32[]{:S(2)}) collective-permute-start(bf16[4,3,128,128]{3,2,1,0:T(8,128)(2,1)S(1)} %get-tuple-element.87), channel_id=1, source_target_pairs={{0,8},{8,16},{16,24},{1,9},{9,17},{17,25},{2,10},{10,18},{18,26},{... | collective-permute-start | bytes 1179656 | tf_op jit(solution)/shard_map/ppermute | solution.py:29
  218.6 2.6 finish.3
  221.3 1.5 collective-permute-start.22
  222.9 3.8 %collective-permute-start.20 = (bf16[3,2,256,128]{3,2,1,0:T(8,128)(2,1)}, bf16[3,2,256,128]{3,2,1,0:T(8,128)(2,1)S(1)}, u32[]{:S(2)}, u32[]{:S(2)}) collective-permute-start(bf16[3,2,256,128]{3,2,1,0:T(8,128)(2,1)} %get-tuple-element.91), channel_id=1, source_target_pairs={{0,7},{1,6},{2,5},{3,4},{4,3},{5,2},{6,1},{7,0},{8,15},{9,14},{10,... | collective-permute-start | bytes 1179656 | tf_op jit(solution)/shard_map/ppermute | solution.py:69
  226.6 3.8 %collective-permute-start.17 = (bf16[3,2,256,128]{3,2,1,0:T(8,128)(2,1)}, bf16[3,2,256,128]{3,2,1,0:T(8,128)(2,1)}, u32[]{:S(2)}, u32[]{:S(2)}) collective-permute-start(bf16[3,2,256,128]{3,2,1,0:T(8,128)(2,1)} %get-tuple-element.88), channel_id=1, source_target_pairs={{0,5},{1,4},{2,7},{3,6},{4,1},{5,0},{6,3},{7,2},{8,13},{9,12},{10,... | collective-permute-start | bytes 1179656 | tf_op jit(solution)/shard_map/ppermute | solution.py:69
  230.4 16.6 %collective-permute-done.22.refs_2_ = bf16[3,2,256,128]{3,2,1,0:T(8,128)(2,1)S(1)} collective-permute-done((bf16[3,2,256,128]{3,2,1,0:T(8,128)(2,1)}, bf16[3,2,256,128]{3,2,1,0:T(8,128)(2,1)S(1)}, u32[]{:S(2)}, u32[]{:S(2)}) %collective-permute-start.22) | collective-permute-done | bytes 393248 | tf_op jit(solution)/shard_map/ppermute | solution.py:69
  247.8 12.5 %collective-permute-done.23.refs_3_ = bf16[3,2,256,128]{3,2,1,0:T(8,128)(2,1)S(1)} collective-permute-done((bf16[3,2,256,128]{3,2,1,0:T(8,128)(2,1)}, bf16[3,2,256,128]{3,2,1,0:T(8,128)(2,1)S(1)}, u32[]{:S(2)}, u32[]{:S(2)}) %collective-permute-start.23) | collective-permute-done | bytes 393248 | tf_op jit(solution)/shard_map/ppermute | solution.py:69
  261.1 7.9 %all-to-all-done.refs_0_ = bf16[8,3,2,256,128]{4,3,2,1,0:T(8,128)(2,1)S(1)} async-done(((bf16[8,3,2,256,128]{4,3,2,1,0:T(8,128)(2,1)}), bf16[8,3,2,256,128]{4,3,2,1,0:T(8,128)(2,1)S(1)}, u32[]{:S(2)}, u32[]{:S(2)}) %all-to-all-start) | async-done | bytes 3145760 | tf_op jit(solution)/shard_map/all_to_all | solution.py:78
  269.0 2.2 unpack.1
  271.2 2.6 unpack_items.3
  273.9 8.6 %collective-permute-done.20.refs_1_ = bf16[3,2,256,128]{3,2,1,0:T(8,128)(2,1)S(1)} collective-permute-done((bf16[3,2,256,128]{3,2,1,0:T(8,128)(2,1)}, bf16[3,2,256,128]{3,2,1,0:T(8,128)(2,1)S(1)}, u32[]{:S(2)}, u32[]{:S(2)}) %collective-permute-start.20) | collective-permute-done | bytes 393248 | tf_op jit(solution)/shard_map/ppermute | solution.py:69
  282.5 7.1 %collective-permute-done.21.refs_2_ = bf16[3,2,256,128]{3,2,1,0:T(8,128)(2,1)} collective-permute-done((bf16[3,2,256,128]{3,2,1,0:T(8,128)(2,1)}, bf16[3,2,256,128]{3,2,1,0:T(8,128)(2,1)}, u32[]{:S(2)}, u32[]{:S(2)}) %collective-permute-start.21) | collective-permute-done | bytes 393248 | tf_op jit(solution)/shard_map/ppermute | solution.py:69
  289.5 2.6 unpack_items.4
  292.1 3.7 %collective-permute-done.17.refs_1_ = bf16[3,2,256,128]{3,2,1,0:T(8,128)(2,1)} collective-permute-done((bf16[3,2,256,128]{3,2,1,0:T(8,128)(2,1)}, bf16[3,2,256,128]{3,2,1,0:T(8,128)(2,1)}, u32[]{:S(2)}, u32[]{:S(2)}) %collective-permute-start.17) | collective-permute-done | bytes 393248 | tf_op jit(solution)/shard_map/ppermute | solution.py:69
  295.8 8.3 %collective-permute-done.18.refs_2_ = bf16[3,2,256,128]{3,2,1,0:T(8,128)(2,1)} collective-permute-done((bf16[3,2,256,128]{3,2,1,0:T(8,128)(2,1)}, bf16[3,2,256,128]{3,2,1,0:T(8,128)(2,1)}, u32[]{:S(2)}, u32[]{:S(2)}) %collective-permute-start.18) | collective-permute-done | bytes 393248 | tf_op jit(solution)/shard_map/ppermute | solution.py:69
  304.1 2.7 unpack_items.5
  (91 shorter events, 16.3 us)
Async XLA Ops:
  0.6 5.5 %copy-start.26 = (s32[6,16,8]{1,2,0:T(8,128)S(1)}, s32[6,16,8]{1,2,0:T(8,128)}, u32[]{:S(2)}) copy-start(s32[6,16,8]{1,2,0:T(8,128)} %param.9) | copy-start | bytes 9220
  4.5 20.9 %collective-permute-start.2 = (bf16[3,2,256,128]{3,2,1,0:T(8,128)(2,1)}, bf16[3,2,256,128]{3,2,1,0:T(8,128)(2,1)S(1)}, u32[]{:S(2)}, u32[]{:S(2)}) collective-permute-start(bf16[3,2,256,128]{3,2,1,0:T(8,128)(2,1)} %get-tuple-element.60), channel_id=1, source_target_pairs={{0,1},{1,0},{2,3},{3,2},{4,5},{5,4},{6,7},{7,6},{8,9},{9,8},{10,11... | collective-permute-start | bytes 1179656 | tf_op jit(solution)/shard_map/ppermute | solution.py:69
  6.1 29.0 %collective-permute-start.3 = (bf16[3,2,256,128]{3,2,1,0:T(8,128)(2,1)}, bf16[3,2,256,128]{3,2,1,0:T(8,128)(2,1)S(1)}, u32[]{:S(2)}, u32[]{:S(2)}) collective-permute-start(bf16[3,2,256,128]{3,2,1,0:T(8,128)(2,1)} %get-tuple-element.61), channel_id=1, source_target_pairs={{0,3},{1,2},{2,1},{3,0},{4,7},{5,6},{6,5},{7,4},{8,11},{9,10},{10,... | collective-permute-start | bytes 1179656 | tf_op jit(solution)/shard_map/ppermute | solution.py:69
  7.7 7.9 %collective-permute-start.1 = (s32[4]{0:T(128)S(1)}, s32[4]{0:T(128)S(1)}, u32[]{:S(2)}, u32[]{:S(2)}) collective-permute-start(s32[4]{0:T(128)S(1)} %get-tuple-element.117), channel_id=1, source_target_pairs={{0,8},{8,16},{16,24},{1,9},{9,17},{17,25},{2,10},{10,18},{18,26},{... | collective-permute-start | bytes 56 | tf_op jit(solution)/shard_map/ppermute | solution.py:29
  10.4 5.2 %collective-permute-start = (s32[4]{0:T(128)S(1)}, s32[4]{0:T(128)S(1)}, u32[]{:S(2)}, u32[]{:S(2)}) collective-permute-start(s32[4]{0:T(128)S(1)} %get-tuple-element.115), channel_id=1, source_target_pairs={{8,0},{16,8},{24,16},{9,1},{17,9},{25,17},{10,2},{18,10},{26,18},{... | collective-permute-start | bytes 56 | tf_op jit(solution)/shard_map/ppermute | solution.py:29
  11.7 46.7 %collective-permute-start.4 = (bf16[3,2,256,128]{3,2,1,0:T(8,128)(2,1)}, bf16[3,2,256,128]{3,2,1,0:T(8,128)(2,1)S(1)}, u32[]{:S(2)}, u32[]{:S(2)}) collective-permute-start(bf16[3,2,256,128]{3,2,1,0:T(8,128)(2,1)} %get-tuple-element.62), channel_id=1, source_target_pairs={{0,7},{1,6},{2,5},{3,4},{4,3},{5,2},{6,1},{7,0},{8,15},{9,14},{10,... | collective-permute-start | bytes 1179656 | tf_op jit(solution)/shard_map/ppermute | solution.py:69
  15.7 51.0 %collective-permute-start.5 = (bf16[3,2,256,128]{3,2,1,0:T(8,128)(2,1)}, bf16[3,2,256,128]{3,2,1,0:T(8,128)(2,1)S(1)}, u32[]{:S(2)}, u32[]{:S(2)}) collective-permute-start(bf16[3,2,256,128]{3,2,1,0:T(8,128)(2,1)} %get-tuple-element.63), channel_id=1, source_target_pairs={{0,6},{1,7},{2,4},{3,5},{4,2},{5,3},{6,0},{7,1},{8,14},{9,15},{10,... | collective-permute-start | bytes 1179656 | tf_op jit(solution)/shard_map/ppermute | solution.py:69
  15.7 59.4 %collective-permute-start.6 = (bf16[3,2,256,128]{3,2,1,0:T(8,128)(2,1)}, bf16[3,2,256,128]{3,2,1,0:T(8,128)(2,1)S(1)}, u32[]{:S(2)}, u32[]{:S(2)}) collective-permute-start(bf16[3,2,256,128]{3,2,1,0:T(8,128)(2,1)} %get-tuple-element.64), channel_id=1, source_target_pairs={{0,5},{1,4},{2,7},{3,6},{4,1},{5,0},{6,3},{7,2},{8,13},{9,12},{10,... | collective-permute-start | bytes 1179656 | tf_op jit(solution)/shard_map/ppermute | solution.py:69
  25.4 14.0 %copy-start.3 = (bf16[3,2,256,128]{3,2,1,0:T(8,128)(2,1)}, bf16[3,2,256,128]{3,2,1,0:T(8,128)(2,1)S(1)}, u32[]{:S(2)}) copy-start(bf16[3,2,256,128]{3,2,1,0:T(8,128)(2,1)S(1)} %collective-permute-done.2.refs_0_.refs_6_.refs_1_) | copy-start | bytes 1179652
  25.4 58.1 %collective-permute-start.7 = (bf16[3,2,256,128]{3,2,1,0:T(8,128)(2,1)}, bf16[3,2,256,128]{3,2,1,0:T(8,128)(2,1)S(1)}, u32[]{:S(2)}, u32[]{:S(2)}) collective-permute-start(bf16[3,2,256,128]{3,2,1,0:T(8,128)(2,1)} %get-tuple-element.65), channel_id=1, source_target_pairs={{0,4},{1,5},{2,6},{3,7},{4,0},{5,1},{6,2},{7,3},{8,12},{9,13},{10,... | collective-permute-start | bytes 1179656 | tf_op jit(solution)/shard_map/ppermute | solution.py:69
  35.1 4.3 %copy-start.5 = (bf16[3,2,256,128]{3,2,1,0:T(8,128)(2,1)}, bf16[3,2,256,128]{3,2,1,0:T(8,128)(2,1)S(1)}, u32[]{:S(2)}) copy-start(bf16[3,2,256,128]{3,2,1,0:T(8,128)(2,1)S(1)} %collective-permute-done.3.refs_1_.refs_4_.refs_2_) | copy-start | bytes 1179652
  35.1 48.4 %collective-permute-start.8 = (bf16[3,2,256,128]{3,2,1,0:T(8,128)(2,1)}, bf16[3,2,256,128]{3,2,1,0:T(8,128)(2,1)S(1)}, u32[]{:S(2)}, u32[]{:S(2)}) collective-permute-start(bf16[3,2,256,128]{3,2,1,0:T(8,128)(2,1)} %get-tuple-element.66), channel_id=1, source_target_pairs={{0,2},{1,3},{2,0},{3,1},{4,6},{5,7},{6,4},{7,5},{8,10},{9,11},{10,... | collective-permute-start | bytes 1179656 | tf_op jit(solution)/shard_map/ppermute | solution.py:69
  35.4 4.0 %copy-start.18 = (s32[6,16,8]{2,1,0:T(8,128)}, s32[6,16,8]{2,1,0:T(8,128)S(1)}, u32[]{:S(2)}) copy-start(s32[6,16,8]{2,1,0:T(8,128)S(1)} %select_select_fusion.refs_1_) | copy-start | bytes 9220
  58.4 25.1 %copy-start.7 = (bf16[3,2,256,128]{3,2,1,0:T(8,128)(2,1)}, bf16[3,2,256,128]{3,2,1,0:T(8,128)(2,1)S(1)}, u32[]{:S(2)}) copy-start(bf16[3,2,256,128]{3,2,1,0:T(8,128)(2,1)S(1)} %collective-permute-done.4.refs_2_.refs_0_.refs_3_) | copy-start | bytes 1179652
  66.7 16.9 %copy-start.9 = (bf16[3,2,256,128]{3,2,1,0:T(8,128)(2,1)}, bf16[3,2,256,128]{3,2,1,0:T(8,128)(2,1)S(1)}, u32[]{:S(2)}) copy-start(bf16[3,2,256,128]{3,2,1,0:T(8,128)(2,1)S(1)} %collective-permute-done.5.refs_3_.refs_1_.refs_4_) | copy-start | bytes 1179652
  75.1 8.4 %copy-start.11 = (bf16[3,2,256,128]{3,2,1,0:T(8,128)(2,1)}, bf16[3,2,256,128]{3,2,1,0:T(8,128)(2,1)S(1)}, u32[]{:S(2)}) copy-start(bf16[3,2,256,128]{3,2,1,0:T(8,128)(2,1)S(1)} %collective-permute-done.6.refs_4_.refs_2_.refs_5_) | copy-start | bytes 1179652
  85.0 6.1 %copy-start.4 = (bf16[3,2,256,128]{3,2,1,0:T(8,128)(2,1)S(1)}, bf16[3,2,256,128]{3,2,1,0:T(8,128)(2,1)}, u32[]{:S(2)}) copy-start(bf16[3,2,256,128]{3,2,1,0:T(8,128)(2,1)} %copy-done.3) | copy-start | bytes 1179652
  85.0 75.3 %all-to-all-start.1 = ((bf16[8,3,2,256,128]{4,3,2,1,0:T(8,128)(2,1)}), bf16[8,3,2,256,128]{4,3,2,1,0:T(8,128)(2,1)S(1)}, u32[]{:S(2)}, u32[]{:S(2)}) async-start(bf16[8,3,2,256,128]{4,3,2,1,0:T(8,128)(2,1)} %hold.1), calls=%async_computation.1 | async-start | bytes 6291456 | tf_op jit(solution)/shard_map/all_to_all | solution.py:78
  91.2 1.0 copy-start.6
  92.2 1.0 copy-start.8
  93.2 1.0 copy-start.10
  94.2 1.0 copy-start.12
  96.2 1.0 copy-start.16
  97.1 1.0 copy-start.17
  98.1 5.9 %copy-start.19 = (s32[6,16,8]{2,1,0:T(8,128)S(1)}, s32[6,16,8]{2,1,0:T(8,128)}, u32[]{:S(2)}) copy-start(s32[6,16,8]{2,1,0:T(8,128)} %copy-done.18) | copy-start | bytes 9220
  99.7 9.6 %collective-permute-start.10 = (bf16[4,3,128,128]{3,2,1,0:T(8,128)(2,1)S(1)}, bf16[4,3,128,128]{3,2,1,0:T(8,128)(2,1)S(1)}, u32[]{:S(2)}, u32[]{:S(2)}) collective-permute-start(bf16[4,3,128,128]{3,2,1,0:T(8,128)(2,1)S(1)} %get-tuple-element.69), channel_id=1, source_target_pairs={{8,0},{16,8},{24,16},{9,1},{17,9},{25,17},{10,2},{18,10},{26,18},{... | collective-permute-start | bytes 1179656 | tf_op jit(solution)/shard_map/ppermute | solution.py:29
  101.0 8.3 %collective-permute-start.9 = (bf16[4,3,128,128]{3,2,1,0:T(8,128)(2,1)S(1)}, bf16[4,3,128,128]{3,2,1,0:T(8,128)(2,1)S(1)}, u32[]{:S(2)}, u32[]{:S(2)}) collective-permute-start(bf16[4,3,128,128]{3,2,1,0:T(8,128)(2,1)S(1)} %get-tuple-element.68), channel_id=1, source_target_pairs={{0,8},{8,16},{16,24},{1,9},{9,17},{17,25},{2,10},{10,18},{18,26},{... | collective-permute-start | bytes 1179656 | tf_op jit(solution)/shard_map/ppermute | solution.py:29
  138.7 6.7 %collective-permute-start.11 = (bf16[4,3,128,128]{3,2,1,0:T(8,128)(2,1)S(1)}, bf16[4,3,128,128]{3,2,1,0:T(8,128)(2,1)S(1)}, u32[]{:S(2)}, u32[]{:S(2)}) collective-permute-start(bf16[4,3,128,128]{3,2,1,0:T(8,128)(2,1)S(1)} %get-tuple-element.76), channel_id=1, source_target_pairs={{8,0},{16,8},{24,16},{9,1},{17,9},{25,17},{10,2},{18,10},{26,18},{... | collective-permute-start | bytes 1179656 | tf_op jit(solution)/shard_map/ppermute | solution.py:29
  140.0 6.7 %collective-permute-start.12 = (bf16[4,3,128,128]{3,2,1,0:T(8,128)(2,1)S(1)}, bf16[4,3,128,128]{3,2,1,0:T(8,128)(2,1)S(1)}, u32[]{:S(2)}, u32[]{:S(2)}) collective-permute-start(bf16[4,3,128,128]{3,2,1,0:T(8,128)(2,1)S(1)} %get-tuple-element.77), channel_id=1, source_target_pairs={{0,8},{8,16},{16,24},{1,9},{9,17},{17,25},{2,10},{10,18},{18,26},{... | collective-permute-start | bytes 1179656 | tf_op jit(solution)/shard_map/ppermute | solution.py:29
  160.4 1.7 copy-start
  162.1 106.9 %all-to-all-start = ((bf16[8,3,2,256,128]{4,3,2,1,0:T(8,128)(2,1)}), bf16[8,3,2,256,128]{4,3,2,1,0:T(8,128)(2,1)S(1)}, u32[]{:S(2)}, u32[]{:S(2)}) async-start(bf16[8,3,2,256,128]{4,3,2,1,0:T(8,128)(2,1)} %finish.2.refs_1_), calls=%async_computation | async-start | bytes 6291456 | tf_op jit(solution)/shard_map/all_to_all | solution.py:78
  168.2 1.9 copy-start.1
  170.0 4.2 %copy-start.2 = (bf16[8,3,2,256,128]{4,3,2,1,0:T(8,128)(2,1)S(1)}, bf16[8,3,2,256,128]{4,3,2,1,0:T(8,128)(2,1)}, u32[]{:S(2)}) copy-start(bf16[8,3,2,256,128]{4,3,2,1,0:T(8,128)(2,1)} %copy-done) | copy-start | bytes 9437188
  171.5 7.3 %collective-permute-start.13 = (bf16[4,3,128,128]{3,2,1,0:T(8,128)(2,1)S(1)}, bf16[4,3,128,128]{3,2,1,0:T(8,128)(2,1)S(1)}, u32[]{:S(2)}, u32[]{:S(2)}) collective-permute-start(bf16[4,3,128,128]{3,2,1,0:T(8,128)(2,1)S(1)} %get-tuple-element.78), channel_id=1, source_target_pairs={{0,8},{8,16},{16,24},{1,9},{9,17},{17,25},{2,10},{10,18},{18,26},{... | collective-permute-start | bytes 1179656 | tf_op jit(solution)/shard_map/ppermute | solution.py:29
  172.9 5.9 %collective-permute-start.14 = (bf16[4,3,128,128]{3,2,1,0:T(8,128)(2,1)S(1)}, bf16[4,3,128,128]{3,2,1,0:T(8,128)(2,1)S(1)}, u32[]{:S(2)}, u32[]{:S(2)}) collective-permute-start(bf16[4,3,128,128]{3,2,1,0:T(8,128)(2,1)S(1)} %get-tuple-element.79), channel_id=1, source_target_pairs={{8,0},{16,8},{24,16},{9,1},{17,9},{25,17},{10,2},{18,10},{26,18},{... | collective-permute-start | bytes 1179656 | tf_op jit(solution)/shard_map/ppermute | solution.py:29
  174.2 4.6 %copy-start.25 = (s32[3,16,8]{2,1,0:T(8,128)S(1)}, s32[3,16,8]{2,1,0:T(8,128)}, u32[]{:S(2)}) copy-start(s32[3,16,8]{2,1,0:T(8,128)} %get-tuple-element.112.lists) | copy-start | bytes 4612
  207.8 9.7 %collective-permute-start.15 = (bf16[4,3,128,128]{3,2,1,0:T(8,128)(2,1)S(1)}, bf16[4,3,128,128]{3,2,1,0:T(8,128)(2,1)S(1)}, u32[]{:S(2)}, u32[]{:S(2)}) collective-permute-start(bf16[4,3,128,128]{3,2,1,0:T(8,128)(2,1)S(1)} %get-tuple-element.86), channel_id=1, source_target_pairs={{8,0},{16,8},{24,16},{9,1},{17,9},{25,17},{10,2},{18,10},{26,18},{... | collective-permute-start | bytes 1179656 | tf_op jit(solution)/shard_map/ppermute | solution.py:29
  209.1 9.6 %collective-permute-start.16 = (bf16[4,3,128,128]{3,2,1,0:T(8,128)(2,1)S(1)}, bf16[4,3,128,128]{3,2,1,0:T(8,128)(2,1)S(1)}, u32[]{:S(2)}, u32[]{:S(2)}) collective-permute-start(bf16[4,3,128,128]{3,2,1,0:T(8,128)(2,1)S(1)} %get-tuple-element.87), channel_id=1, source_target_pairs={{0,8},{8,16},{16,24},{1,9},{9,17},{17,25},{2,10},{10,18},{18,26},{... | collective-permute-start | bytes 1179656 | tf_op jit(solution)/shard_map/ppermute | solution.py:29
  221.3 25.8 %collective-permute-start.22 = (bf16[3,2,256,128]{3,2,1,0:T(8,128)(2,1)}, bf16[3,2,256,128]{3,2,1,0:T(8,128)(2,1)S(1)}, u32[]{:S(2)}, u32[]{:S(2)}) collective-permute-start(bf16[3,2,256,128]{3,2,1,0:T(8,128)(2,1)} %get-tuple-element.94), channel_id=1, source_target_pairs={{0,1},{1,0},{2,3},{3,2},{4,5},{5,4},{6,7},{7,6},{8,9},{9,8},{10,11... | collective-permute-start | bytes 1179656 | tf_op jit(solution)/shard_map/ppermute | solution.py:69
  222.8 37.5 %collective-permute-start.23 = (bf16[3,2,256,128]{3,2,1,0:T(8,128)(2,1)}, bf16[3,2,256,128]{3,2,1,0:T(8,128)(2,1)S(1)}, u32[]{:S(2)}, u32[]{:S(2)}) collective-permute-start(bf16[3,2,256,128]{3,2,1,0:T(8,128)(2,1)} %get-tuple-element.95), channel_id=1, source_target_pairs={{0,3},{1,2},{2,1},{3,0},{4,7},{5,6},{6,5},{7,4},{8,11},{9,10},{10,... | collective-permute-start | bytes 1179656 | tf_op jit(solution)/shard_map/ppermute | solution.py:69
  222.9 59.6 %collective-permute-start.20 = (bf16[3,2,256,128]{3,2,1,0:T(8,128)(2,1)}, bf16[3,2,256,128]{3,2,1,0:T(8,128)(2,1)S(1)}, u32[]{:S(2)}, u32[]{:S(2)}) collective-permute-start(bf16[3,2,256,128]{3,2,1,0:T(8,128)(2,1)} %get-tuple-element.91), channel_id=1, source_target_pairs={{0,7},{1,6},{2,5},{3,4},{4,3},{5,2},{6,1},{7,0},{8,15},{9,14},{10,... | collective-permute-start | bytes 1179656 | tf_op jit(solution)/shard_map/ppermute | solution.py:69
  226.6 62.9 %collective-permute-start.21 = (bf16[3,2,256,128]{3,2,1,0:T(8,128)(2,1)}, bf16[3,2,256,128]{3,2,1,0:T(8,128)(2,1)}, u32[]{:S(2)}, u32[]{:S(2)}) collective-permute-start(bf16[3,2,256,128]{3,2,1,0:T(8,128)(2,1)} %get-tuple-element.92), channel_id=1, source_target_pairs={{0,6},{1,7},{2,4},{3,5},{4,2},{5,3},{6,0},{7,1},{8,14},{9,15},{10,... | collective-permute-start | bytes 1179656 | tf_op jit(solution)/shard_map/ppermute | solution.py:69
  226.6 69.2 %collective-permute-start.17 = (bf16[3,2,256,128]{3,2,1,0:T(8,128)(2,1)}, bf16[3,2,256,128]{3,2,1,0:T(8,128)(2,1)}, u32[]{:S(2)}, u32[]{:S(2)}) collective-permute-start(bf16[3,2,256,128]{3,2,1,0:T(8,128)(2,1)} %get-tuple-element.88), channel_id=1, source_target_pairs={{0,5},{1,4},{2,7},{3,6},{4,1},{5,0},{6,3},{7,2},{8,13},{9,12},{10,... | collective-permute-start | bytes 1179656 | tf_op jit(solution)/shard_map/ppermute | solution.py:69
  247.8 56.3 %collective-permute-start.18 = (bf16[3,2,256,128]{3,2,1,0:T(8,128)(2,1)}, bf16[3,2,256,128]{3,2,1,0:T(8,128)(2,1)}, u32[]{:S(2)}, u32[]{:S(2)}) collective-permute-start(bf16[3,2,256,128]{3,2,1,0:T(8,128)(2,1)} %get-tuple-element.89), channel_id=1, source_target_pairs={{0,4},{1,5},{2,6},{3,7},{4,0},{5,1},{6,2},{7,3},{8,12},{9,13},{10,... | collective-permute-start | bytes 1179656 | tf_op jit(solution)/shard_map/ppermute | solution.py:69
  261.1 43.1 %collective-permute-start.19 = (bf16[3,2,256,128]{3,2,1,0:T(8,128)(2,1)}, bf16[3,2,256,128]{3,2,1,0:T(8,128)(2,1)}, u32[]{:S(2)}, u32[]{:S(2)}) collective-permute-start(bf16[3,2,256,128]{3,2,1,0:T(8,128)(2,1)} %get-tuple-element.90), channel_id=1, source_target_pairs={{0,2},{1,3},{2,0},{3,1},{4,6},{5,7},{6,4},{7,5},{8,10},{9,11},{10,... | collective-permute-start | bytes 1179656 | tf_op jit(solution)/shard_map/ppermute | solution.py:69
  269.0 2.3 copy-start.20
  269.0 2.3 copy-start.22
  269.0 2.3 copy-start.24
  (5 other events, 4.1 us)

commit v17 on v14

--- a/solution.py
+++ b/solution.py
@@ -56,6 +56,13 @@
     return received
 
 
+def join(left, right, head_dim, half):
+    first = lax.broadcasted_iota(jnp.int32, left.shape, 1) < head_dim
+    if half == 0:
+        return jnp.where(first, left, pltpu.roll(right, head_dim, 1))
+    return jnp.where(first, pltpu.roll(left, head_dim, 1), right)
+
+
 def pack_kernel(query, key, value, d_out, *refs, first, heads, per_peer, head_dim):
     message, stage, ready, in_sems, out_sems = refs[-5:]
     sources = (key, value, query, d_out)
@@ -86,11 +93,14 @@
             fetch(peer, i).wait()
         at = span(peer)[2]
         for head in range(heads):
-            lanes = slice(at + head * head_dim, at + (head + 1) * head_dim)
+            tile, inside = divmod(at + head * head_dim, LANES)
+            lanes = slice(tile * LANES, (tile + 1) * LANES)
             for kind in range(2):
-                ready[peer, head, kind] = jnp.concatenate(
-                    [stage[2 * kind, peer, :, lanes], stage[2 * kind + 1, peer, :, lanes]],
-                    axis=1,
+                ready[peer, head, kind] = join(
+                    stage[2 * kind, peer, :, lanes],
+                    stage[2 * kind + 1, peer, :, lanes],
+                    head_dim,
+                    inside // head_dim,
                 )
         send(peer).start()
     for peer in range(peers):
@@ -170,10 +180,8 @@
         for which, peer, _ in (left, right):
             wait_for(which, peer)
         sides = [stages[which][peer, head] for which, peer, head in (left, right)]
-        for i, (kind, at) in enumerate(((1, head_dim), (1, 0), (0, 0), (0, head_dim))):
-            ready[i, job] = jnp.concatenate(
-                [side[kind, :, at : at + head_dim] for side in sides], axis=1
-            )
+        for i, (kind, half) in enumerate(((1, 1), (1, 0), (0, 0), (0, 1))):
+            ready[i, job] = join(sides[0][kind], sides[1][kind], head_dim, half)
             send(job, i).start()
     for which in chunks_used:
         for peer in range(peers):
@@ -270,10 +278,8 @@
                 fetch(which, j).wait()
         for job, (_, left, right) in enumerate(jobs):
             sides = [stages[which][j, head] for which, head in (left, right)]
-            for i, (kind, at) in enumerate(((1, head_dim), (1, 0), (0, 0), (0, head_dim))):
-                ready[j, i, job] = jnp.concatenate(
-                    [side[kind, :, at : at + head_dim] for side in sides], axis=1
-                )
+            for i, (kind, half) in enumerate(((1, 1), (1, 0), (0, 0), (0, 1))):
+                ready[j, i, job] = join(sides[0][kind], sides[1][kind], head_dim, half)
                 send(j, job, i).start()
     for j in range(len(items)):
         for job in range(len(jobs)):
@@ -710,7 +716,8 @@
             parts = (
                 [peers - 1, *near[::2]],
                 list(range(half // 2)),
-                [*range(half // 2, half), *near[1::2]],
+                list(range(half // 2, half - 1)),
+                [half - 1, *near[1::2]],
             )
             for items in parts:
                 outs = unpack_items(me, received, starts, heads_here, items, outs)

time: 304 us -> 304 us (level)
    pallas_call x3 -> x4, Pallas kernels: 7.86 us -> 9.66 us  [unpack_items(): pl.pallas_call(functools.partial(unpack_items_kernel, items=items, peers=...]
  transfers between devices with their start and end apart: 20 -> 20, of which waited for: 13 -> 13; matrix products, arithmetic and copies ran while one was open for 1% -> 1% of each run, Pallas kernels for 29% -> 30%
where the time goes in v17:
time: 304 us; the launch traced here: 298 us
  waiting for transfers between devices  141 us (46%)
  Pallas kernels  95.4 us (31%)
  starting transfers between devices  56.3 us (19%)
    all_to_all x3, waiting for transfers between devices, exchange(): lax.all_to_all(messages[0], 'seq', split_axis=0, concat_axis=0, tiled=True)  81.6 us
    pallas_call x2, Pallas kernels, attend(): pl.pallas_call(functools.partial(attend_kernel, head_dim=lanes // 2, per_...  58.3 us
    ppermute x7, waiting for transfers between devices, exchange(): received[item] = lax.ppermute(messages[item], 'seq', pairs)  53.7 us
    ppermute x10, starting transfers between devices, from_behind(): return lax.ppermute(x, axis, pairs)  27.8 us
    all_to_all x3, starting transfers between devices, exchange(): lax.all_to_all(messages[0], 'seq', split_axis=0, concat_axis=0, tiled=True)  19.3 us
    pallas_call x4, Pallas kernels, unpack_items(): pl.pallas_call(functools.partial(unpack_items_kernel, items=items, peers=...  9.66 us
    ppermute x7, starting transfers between devices, exchange(): received[item] = lax.ppermute(messages[item], 'seq', pairs)  9.18 us
    pallas_call x2, Pallas kernels, prepare(): pl.pallas_call(functools.partial(prepare_kernel, peers=peers), in_specs=[...  8.45 us
  transfers between devices with their start and end apart: 20, of which 13 were waited for; matrix products, arithmetic and copies ran while one was open for 1% of the time, Pallas kernels for 30%

profile of v17, /device:TPU:8, one launch (start us, length us, event | category | flops | bytes accessed | tf_op | source)
XLA Modules:
  0.0 298.5 jit_solution(10716595210367607303)
XLA Ops:
  0.6 3.9 %pack.2 = bf16[8,3,2,256,128]{4,3,2,1,0:T(8,128)(2,1)} custom-call(bf16[256,3072]{1,0:T(8,128)(2,1)} %query.3, bf16[256,3072]{1,0:T(8,128)(2,1)} %key.3, bf16[256,3072]{1,0:T(8,128)(2,1)} %value.3, bf16[256,3072]{1,0:T(8,128)(2,1)} %d_out.3), custom_call_target="tpu_custom_call" | custom-call | tf_op jit(solution)/shard_map/pack/pallas_call | solution.py:116
  4.6 6.3 %all-to-all-start = ((bf16[8,3,2,256,128]{4,3,2,1,0:T(8,128)(2,1)}), bf16[8,3,2,256,128]{4,3,2,1,0:T(8,128)(2,1)S(1)}, u32[]{:S(2)}, u32[]{:S(2)}) async-start(bf16[8,3,2,256,128]{4,3,2,1,0:T(8,128)(2,1)} %pack.2), calls=%async_computation | async-start | bytes 6291456 | tf_op jit(solution)/shard_map/all_to_all | solution.py:50
  11.0 0.2 compare_reduce_fusion.1
  11.2 1.2 top_k.24
  12.5 1.3 collective-permute-start.1
  13.8 1.2 top_k.17
  15.0 1.3 collective-permute-start
  16.6 3.2 %collective-permute-done = s32[4]{0:T(128)S(1)} collective-permute-done((s32[4]{0:T(128)S(1)}, s32[4]{0:T(128)S(1)}, u32[]{:S(2)}, u32[]{:S(2)}) %collective-permute-start) | collective-permute-done | bytes 48 | tf_op jit(solution)/shard_map/ppermute | solution.py:29
  19.9 3.9 %pack.3 = bf16[8,3,2,256,128]{4,3,2,1,0:T(8,128)(2,1)} custom-call(bf16[256,3072]{1,0:T(8,128)(2,1)} %query.3, bf16[256,3072]{1,0:T(8,128)(2,1)} %key.3, bf16[256,3072]{1,0:T(8,128)(2,1)} %value.3, bf16[256,3072]{1,0:T(8,128)(2,1)} %d_out.3, s32[8]{0:T(128)S(1)} %pad_add_fusion.asked.refs_0_, s32[6,16,8]{2,1,0:T(8,128)S(1)} %select_select_fusion.refs_1_), custom_call_target="tpu_custom_call" | custom-call | tf_op jit(solution)/shard_map/pack/pallas_call | solution.py:116
  23.8 55.3 %all-to-all-done.refs_0_ = bf16[8,3,2,256,128]{4,3,2,1,0:T(8,128)(2,1)S(1)} async-done(((bf16[8,3,2,256,128]{4,3,2,1,0:T(8,128)(2,1)}), bf16[8,3,2,256,128]{4,3,2,1,0:T(8,128)(2,1)S(1)}, u32[]{:S(2)}, u32[]{:S(2)}) %all-to-all-start) | async-done | bytes 3145760 | tf_op jit(solution)/shard_map/all_to_all | solution.py:50
  79.1 6.8 %all-to-all-start.2 = ((bf16[8,3,2,256,128]{4,3,2,1,0:T(8,128)(2,1)}), bf16[8,3,2,256,128]{4,3,2,1,0:T(8,128)(2,1)}, u32[]{:S(2)}, u32[]{:S(2)}) async-start(bf16[8,3,2,256,128]{4,3,2,1,0:T(8,128)(2,1)} %pack.3), calls=%async_computation.2 | async-start | bytes 6291456 | tf_op jit(solution)/shard_map/all_to_all | solution.py:50
  85.9 1.4 pick.2
  87.3 1.3 collective-permute-start.2
  88.7 1.3 collective-permute-start.3
  90.0 4.6 %prepare.2 = (bf16[3,24,128,128]{3,2,1,0:T(8,128)(2,1)S(1)}, bf16[8,3,256,128]{3,2,1,0:T(8,128)(2,1)S(1)}, f32[3,24,128,128]{3,2,1,0:T(8,128)S(1)}) custom-call(s32[1]{0:T(128)} %bitcast.me, bf16[3,24,128,128]{3,2,1,0:T(8,128)(2,1)S(1)} %get-tuple-element.58.table.table_in, bf16[8,3,2,256,128]{4,3,2,1,0:T(8,128)(2,1)S(1)} %all-to-all-done.refs_0_), custom_call_target="tpu_custom_call" | custom-call | tf_op jit(solution)/shard_map/prepare/pallas_call | solution.py:418
  94.6 29.4 %attend.2 = (bf16[8,3,256,128]{3,2,1,0:T(8,128)(2,1)S(1)}, bf16[4,3,128,128]{3,2,1,0:T(8,128)(2,1)S(1)}, bf16[4,3,128,128]{3,2,1,0:T(8,128)(2,1)S(1)}, bf16[3,24...) custom-call(s32[3,16,8]{2,1,0:T(8,128)S(1)} %get-tuple-element.105.l, ...), custom_call_target="tpu_custom_call", output_to_operand_aliasing={{3}: (4, {}), {4}: (5, {}), {5}: (6, {})} | custom-call | tf_op jit(solution)/shard_map/attend/pallas_call | solution.py:574
  124.0 1.3 collective-permute-start.4
  125.3 8.4 %collective-permute-start.5 = (bf16[4,3,128,128]{3,2,1,0:T(8,128)(2,1)S(1)}, bf16[4,3,128,128]{3,2,1,0:T(8,128)(2,1)S(1)}, u32[]{:S(2)}, u32[]{:S(2)}) collective-permute-start(bf16[4,3,128,128]{3,2,1,0:T(8,128)(2,1)S(1)} %get-tuple-element.65), channel_id=1, source_target_pairs={{0,8},{8,16},{16,24},{1,9},{9,17},{17,25},{2,10},{10,18},{18,26},{... | collective-permute-start | bytes 1179656 | tf_op jit(solution)/shard_map/ppermute | solution.py:29
  133.7 1.3 collective-permute-done.5.earlier
  135.0 2.6 finish.2.refs_1_
  137.6 16.0 %all-to-all-done.2.refs_0_ = bf16[8,3,2,256,128]{4,3,2,1,0:T(8,128)(2,1)} async-done(((bf16[8,3,2,256,128]{4,3,2,1,0:T(8,128)(2,1)}), bf16[8,3,2,256,128]{4,3,2,1,0:T(8,128)(2,1)}, u32[]{:S(2)}, u32[]{:S(2)}) %all-to-all-start.2) | async-done | bytes 3145760 | tf_op jit(solution)/shard_map/all_to_all | solution.py:50
  153.6 6.2 %all-to-all-start.1 = ((bf16[8,3,2,256,128]{4,3,2,1,0:T(8,128)(2,1)}), bf16[8,3,2,256,128]{4,3,2,1,0:T(8,128)(2,1)S(1)}, u32[]{:S(2)}, u32[]{:S(2)}) async-start(bf16[8,3,2,256,128]{4,3,2,1,0:T(8,128)(2,1)} %finish.2.refs_1_), calls=%async_computation.1 | async-start | bytes 6291456 | tf_op jit(solution)/shard_map/all_to_all | solution.py:50
  159.8 2.2 pick.3
  162.0 1.4 collective-permute-start.6
  163.4 1.3 collective-permute-start.7
  164.7 3.9 %prepare.3 = (bf16[3,24,128,128]{3,2,1,0:T(8,128)(2,1)S(1)}, bf16[8,3,256,128]{3,2,1,0:T(8,128)(2,1)S(1)}, f32[3,24,128,128]{3,2,1,0:T(8,128)S(1)}) custom-call(s32[1]{0:T(128)} %bitcast.me, bf16[3,24,128,128]{3,2,1,0:T(8,128)(2,1)S(1)} %get-tuple-element.68.table.table_in, bf16[8,3,2,256,128]{4,3,2,1,0:T(8,128)(2,1)} %all-to-all-done.2.refs_0_), custom_call_target="tpu_custom_call" | custom-call | tf_op jit(solution)/shard_map/prepare/pallas_call | solution.py:418
  168.7 28.9 %attend.3 = (bf16[8,3,256,128]{3,2,1,0:T(8,128)(2,1)S(1)}, bf16[4,3,128,128]{3,2,1,0:T(8,128)(2,1)S(1)}, bf16[4,3,128,128]{3,2,1,0:T(8,128)(2,1)S(1)}, bf16[3,24...) custom-call(s32[3,16,8]{2,1,0:T(8,128)S(1)} %get-tuple-element.104.l, ...), custom_call_target="tpu_custom_call", output_to_operand_aliasing={{3}: (4, {}), {4}: (5, {}), {5}: (6, {})} | custom-call | tf_op jit(solution)/shard_map/attend/pallas_call | solution.py:574
  197.6 1.3 collective-permute-start.8
  198.9 9.0 %collective-permute-start.9 = (bf16[4,3,128,128]{3,2,1,0:T(8,128)(2,1)S(1)}, bf16[4,3,128,128]{3,2,1,0:T(8,128)(2,1)S(1)}, u32[]{:S(2)}, u32[]{:S(2)}) collective-permute-start(bf16[4,3,128,128]{3,2,1,0:T(8,128)(2,1)S(1)} %get-tuple-element.75), channel_id=1, source_target_pairs={{0,8},{8,16},{16,24},{1,9},{9,17},{17,25},{2,10},{10,18},{18,26},{... | collective-permute-start | bytes 1179656 | tf_op jit(solution)/shard_map/ppermute | solution.py:29
  207.9 1.1 collective-permute-done.9.earlier
  209.0 2.6 finish.3
  211.7 1.5 collective-permute-start.15
  213.3 3.8 %collective-permute-start.13 = (bf16[3,2,256,128]{3,2,1,0:T(8,128)(2,1)}, bf16[3,2,256,128]{3,2,1,0:T(8,128)(2,1)}, u32[]{:S(2)}, u32[]{:S(2)}) collective-permute-start(bf16[3,2,256,128]{3,2,1,0:T(8,128)(2,1)} %get-tuple-element.79), channel_id=1, source_target_pairs={{0,7},{1,6},{2,5},{3,4},{4,3},{5,2},{6,1},{7,0},{8,15},{9,14},{10,... | collective-permute-start | bytes 1179656 | tf_op jit(solution)/shard_map/ppermute | solution.py:55
  217.0 3.8 %collective-permute-start.12 = (bf16[3,2,256,128]{3,2,1,0:T(8,128)(2,1)}, bf16[3,2,256,128]{3,2,1,0:T(8,128)(2,1)}, u32[]{:S(2)}, u32[]{:S(2)}) collective-permute-start(bf16[3,2,256,128]{3,2,1,0:T(8,128)(2,1)} %get-tuple-element.78), channel_id=1, source_target_pairs={{0,5},{1,4},{2,7},{3,6},{4,1},{5,0},{6,3},{7,2},{8,13},{9,12},{10,... | collective-permute-start | bytes 1179656 | tf_op jit(solution)/shard_map/ppermute | solution.py:55
  220.9 17.6 %collective-permute-done.15.refs_2_ = bf16[3,2,256,128]{3,2,1,0:T(8,128)(2,1)S(1)} collective-permute-done((bf16[3,2,256,128]{3,2,1,0:T(8,128)(2,1)}, bf16[3,2,256,128]{3,2,1,0:T(8,128)(2,1)S(1)}, u32[]{:S(2)}, u32[]{:S(2)}) %collective-permute-start.15) | collective-permute-done | bytes 393248 | tf_op jit(solution)/shard_map/ppermute | solution.py:55
  238.5 0.7 copy-done.1
  239.2 11.5 %collective-permute-done.16.refs_3_ = bf16[3,2,256,128]{3,2,1,0:T(8,128)(2,1)S(1)} collective-permute-done((bf16[3,2,256,128]{3,2,1,0:T(8,128)(2,1)}, bf16[3,2,256,128]{3,2,1,0:T(8,128)(2,1)S(1)}, u32[]{:S(2)}, u32[]{:S(2)}) %collective-permute-start.16) | collective-permute-done | bytes 393248 | tf_op jit(solution)/shard_map/ppermute | solution.py:55
  250.7 0.7 copy-done.3
  251.4 10.3 %all-to-all-done.1.refs_0_ = bf16[8,3,2,256,128]{4,3,2,1,0:T(8,128)(2,1)S(1)} async-done(((bf16[8,3,2,256,128]{4,3,2,1,0:T(8,128)(2,1)}), bf16[8,3,2,256,128]{4,3,2,1,0:T(8,128)(2,1)S(1)}, u32[]{:S(2)}, u32[]{:S(2)}) %all-to-all-start.1) | async-done | bytes 3145760 | tf_op jit(solution)/shard_map/all_to_all | solution.py:50
  261.7 2.2 unpack.1
  264.0 2.6 unpack_items.4
  266.7 8.7 %collective-permute-done.13.refs_1_ = bf16[3,2,256,128]{3,2,1,0:T(8,128)(2,1)} collective-permute-done((bf16[3,2,256,128]{3,2,1,0:T(8,128)(2,1)}, bf16[3,2,256,128]{3,2,1,0:T(8,128)(2,1)}, u32[]{:S(2)}, u32[]{:S(2)}) %collective-permute-start.13) | collective-permute-done | bytes 393248 | tf_op jit(solution)/shard_map/ppermute | solution.py:55
  275.4 5.8 %collective-permute-done.14.refs_2_ = bf16[3,2,256,128]{3,2,1,0:T(8,128)(2,1)} collective-permute-done((bf16[3,2,256,128]{3,2,1,0:T(8,128)(2,1)}, bf16[3,2,256,128]{3,2,1,0:T(8,128)(2,1)}, u32[]{:S(2)}, u32[]{:S(2)}) %collective-permute-start.14) | collective-permute-done | bytes 393248 | tf_op jit(solution)/shard_map/ppermute | solution.py:55
  281.2 2.4 unpack_items.5
  283.6 3.8 %collective-permute-done.12.refs_1_ = bf16[3,2,256,128]{3,2,1,0:T(8,128)(2,1)} collective-permute-done((bf16[3,2,256,128]{3,2,1,0:T(8,128)(2,1)}, bf16[3,2,256,128]{3,2,1,0:T(8,128)(2,1)}, u32[]{:S(2)}, u32[]{:S(2)}) %collective-permute-start.12) | collective-permute-done | bytes 393248 | tf_op jit(solution)/shard_map/ppermute | solution.py:55
  287.4 2.1 unpack_items.6
  289.5 6.2 %collective-permute-done.10.refs_1_ = bf16[3,2,256,128]{3,2,1,0:T(8,128)(2,1)S(1)} collective-permute-done((bf16[3,2,256,128]{3,2,1,0:T(8,128)(2,1)}, bf16[3,2,256,128]{3,2,1,0:T(8,128)(2,1)S(1)}, u32[]{:S(2)}, u32[]{:S(2)}) %collective-permute-start.10) | collective-permute-done | bytes 393248 | tf_op jit(solution)/shard_map/ppermute | solution.py:55
  295.7 2.6 unpack_items.7
  (37 shorter events, 0.7 us)
Async XLA Ops:
  4.5 6.3 %copy-start.5 = (s32[6,16,8]{1,2,0:T(8,128)S(1)}, s32[6,16,8]{1,2,0:T(8,128)}, u32[]{:S(2)}) copy-start(s32[6,16,8]{1,2,0:T(8,128)} %param.9) | copy-start | bytes 9220
  4.6 74.5 %all-to-all-start = ((bf16[8,3,2,256,128]{4,3,2,1,0:T(8,128)(2,1)}), bf16[8,3,2,256,128]{4,3,2,1,0:T(8,128)(2,1)S(1)}, u32[]{:S(2)}, u32[]{:S(2)}) async-start(bf16[8,3,2,256,128]{4,3,2,1,0:T(8,128)(2,1)} %pack.2), calls=%async_computation | async-start | bytes 6291456 | tf_op jit(solution)/shard_map/all_to_all | solution.py:50
  12.5 4.1 %collective-permute-start.1 = (s32[4]{0:T(128)S(1)}, s32[4]{0:T(128)S(1)}, u32[]{:S(2)}, u32[]{:S(2)}) collective-permute-start(s32[4]{0:T(128)S(1)} %get-tuple-element.109), channel_id=1, source_target_pairs={{0,8},{8,16},{16,24},{1,9},{9,17},{17,25},{2,10},{10,18},{18,26},{... | collective-permute-start | bytes 56 | tf_op jit(solution)/shard_map/ppermute | solution.py:29
  15.0 4.8 %collective-permute-start = (s32[4]{0:T(128)S(1)}, s32[4]{0:T(128)S(1)}, u32[]{:S(2)}, u32[]{:S(2)}) collective-permute-start(s32[4]{0:T(128)S(1)} %get-tuple-element.107), channel_id=1, source_target_pairs={{8,0},{16,8},{24,16},{9,1},{17,9},{25,17},{10,2},{18,10},{26,18},{... | collective-permute-start | bytes 56 | tf_op jit(solution)/shard_map/ppermute | solution.py:29
  79.1 74.5 %all-to-all-start.2 = ((bf16[8,3,2,256,128]{4,3,2,1,0:T(8,128)(2,1)}), bf16[8,3,2,256,128]{4,3,2,1,0:T(8,128)(2,1)}, u32[]{:S(2)}, u32[]{:S(2)}) async-start(bf16[8,3,2,256,128]{4,3,2,1,0:T(8,128)(2,1)} %pack.3), calls=%async_computation.2 | async-start | bytes 6291456 | tf_op jit(solution)/shard_map/all_to_all | solution.py:50
  87.3 7.2 %collective-permute-start.2 = (bf16[4,3,128,128]{3,2,1,0:T(8,128)(2,1)S(1)}, bf16[4,3,128,128]{3,2,1,0:T(8,128)(2,1)S(1)}, u32[]{:S(2)}, u32[]{:S(2)}) collective-permute-start(bf16[4,3,128,128]{3,2,1,0:T(8,128)(2,1)S(1)} %get-tuple-element.56), channel_id=1, source_target_pairs={{0,8},{8,16},{16,24},{1,9},{9,17},{17,25},{2,10},{10,18},{18,26},{... | collective-permute-start | bytes 1179656 | tf_op jit(solution)/shard_map/ppermute | solution.py:29
  88.7 5.9 %collective-permute-start.3 = (bf16[4,3,128,128]{3,2,1,0:T(8,128)(2,1)S(1)}, bf16[4,3,128,128]{3,2,1,0:T(8,128)(2,1)S(1)}, u32[]{:S(2)}, u32[]{:S(2)}) collective-permute-start(bf16[4,3,128,128]{3,2,1,0:T(8,128)(2,1)S(1)} %get-tuple-element.57), channel_id=1, source_target_pairs={{8,0},{16,8},{24,16},{9,1},{17,9},{25,17},{10,2},{18,10},{26,18},{... | collective-permute-start | bytes 1179656 | tf_op jit(solution)/shard_map/ppermute | solution.py:29
  124.0 9.7 %collective-permute-start.4 = (bf16[4,3,128,128]{3,2,1,0:T(8,128)(2,1)S(1)}, bf16[4,3,128,128]{3,2,1,0:T(8,128)(2,1)S(1)}, u32[]{:S(2)}, u32[]{:S(2)}) collective-permute-start(bf16[4,3,128,128]{3,2,1,0:T(8,128)(2,1)S(1)} %get-tuple-element.64), channel_id=1, source_target_pairs={{8,0},{16,8},{24,16},{9,1},{17,9},{25,17},{10,2},{18,10},{26,18},{... | collective-permute-start | bytes 1179656 | tf_op jit(solution)/shard_map/ppermute | solution.py:29
  125.3 9.7 %collective-permute-start.5 = (bf16[4,3,128,128]{3,2,1,0:T(8,128)(2,1)S(1)}, bf16[4,3,128,128]{3,2,1,0:T(8,128)(2,1)S(1)}, u32[]{:S(2)}, u32[]{:S(2)}) collective-permute-start(bf16[4,3,128,128]{3,2,1,0:T(8,128)(2,1)S(1)} %get-tuple-element.65), channel_id=1, source_target_pairs={{0,8},{8,16},{16,24},{1,9},{9,17},{17,25},{2,10},{10,18},{18,26},{... | collective-permute-start | bytes 1179656 | tf_op jit(solution)/shard_map/ppermute | solution.py:29
  153.6 108.1 %all-to-all-start.1 = ((bf16[8,3,2,256,128]{4,3,2,1,0:T(8,128)(2,1)}), bf16[8,3,2,256,128]{4,3,2,1,0:T(8,128)(2,1)S(1)}, u32[]{:S(2)}, u32[]{:S(2)}) async-start(bf16[8,3,2,256,128]{4,3,2,1,0:T(8,128)(2,1)} %finish.2.refs_1_), calls=%async_computation.1 | async-start | bytes 6291456 | tf_op jit(solution)/shard_map/all_to_all | solution.py:50
  162.0 6.6 %collective-permute-start.6 = (bf16[4,3,128,128]{3,2,1,0:T(8,128)(2,1)S(1)}, bf16[4,3,128,128]{3,2,1,0:T(8,128)(2,1)S(1)}, u32[]{:S(2)}, u32[]{:S(2)}) collective-permute-start(bf16[4,3,128,128]{3,2,1,0:T(8,128)(2,1)S(1)} %get-tuple-element.66), channel_id=1, source_target_pairs={{0,8},{8,16},{16,24},{1,9},{9,17},{17,25},{2,10},{10,18},{18,26},{... | collective-permute-start | bytes 1179656 | tf_op jit(solution)/shard_map/ppermute | solution.py:29
  163.4 5.3 %collective-permute-start.7 = (bf16[4,3,128,128]{3,2,1,0:T(8,128)(2,1)S(1)}, bf16[4,3,128,128]{3,2,1,0:T(8,128)(2,1)S(1)}, u32[]{:S(2)}, u32[]{:S(2)}) collective-permute-start(bf16[4,3,128,128]{3,2,1,0:T(8,128)(2,1)S(1)} %get-tuple-element.67), channel_id=1, source_target_pairs={{8,0},{16,8},{24,16},{9,1},{17,9},{25,17},{10,2},{18,10},{26,18},{... | collective-permute-start | bytes 1179656 | tf_op jit(solution)/shard_map/ppermute | solution.py:29
  197.6 10.3 %collective-permute-start.8 = (bf16[4,3,128,128]{3,2,1,0:T(8,128)(2,1)S(1)}, bf16[4,3,128,128]{3,2,1,0:T(8,128)(2,1)S(1)}, u32[]{:S(2)}, u32[]{:S(2)}) collective-permute-start(bf16[4,3,128,128]{3,2,1,0:T(8,128)(2,1)S(1)} %get-tuple-element.74), channel_id=1, source_target_pairs={{8,0},{16,8},{24,16},{9,1},{17,9},{25,17},{10,2},{18,10},{26,18},{... | collective-permute-start | bytes 1179656 | tf_op jit(solution)/shard_map/ppermute | solution.py:29
  198.9 10.2 %collective-permute-start.9 = (bf16[4,3,128,128]{3,2,1,0:T(8,128)(2,1)S(1)}, bf16[4,3,128,128]{3,2,1,0:T(8,128)(2,1)S(1)}, u32[]{:S(2)}, u32[]{:S(2)}) collective-permute-start(bf16[4,3,128,128]{3,2,1,0:T(8,128)(2,1)S(1)} %get-tuple-element.75), channel_id=1, source_target_pairs={{0,8},{8,16},{16,24},{1,9},{9,17},{17,25},{2,10},{10,18},{18,26},{... | collective-permute-start | bytes 1179656 | tf_op jit(solution)/shard_map/ppermute | solution.py:29
  211.7 26.8 %collective-permute-start.15 = (bf16[3,2,256,128]{3,2,1,0:T(8,128)(2,1)}, bf16[3,2,256,128]{3,2,1,0:T(8,128)(2,1)S(1)}, u32[]{:S(2)}, u32[]{:S(2)}) collective-permute-start(bf16[3,2,256,128]{3,2,1,0:T(8,128)(2,1)} %get-tuple-element.82), channel_id=1, source_target_pairs={{0,1},{1,0},{2,3},{3,2},{4,5},{5,4},{6,7},{7,6},{8,9},{9,8},{10,11... | collective-permute-start | bytes 1179656 | tf_op jit(solution)/shard_map/ppermute | solution.py:55
  213.2 37.5 %collective-permute-start.16 = (bf16[3,2,256,128]{3,2,1,0:T(8,128)(2,1)}, bf16[3,2,256,128]{3,2,1,0:T(8,128)(2,1)S(1)}, u32[]{:S(2)}, u32[]{:S(2)}) collective-permute-start(bf16[3,2,256,128]{3,2,1,0:T(8,128)(2,1)} %get-tuple-element.83), channel_id=1, source_target_pairs={{0,3},{1,2},{2,1},{3,0},{4,7},{5,6},{6,5},{7,4},{8,11},{9,10},{10,... | collective-permute-start | bytes 1179656 | tf_op jit(solution)/shard_map/ppermute | solution.py:55
  213.3 62.1 %collective-permute-start.13 = (bf16[3,2,256,128]{3,2,1,0:T(8,128)(2,1)}, bf16[3,2,256,128]{3,2,1,0:T(8,128)(2,1)}, u32[]{:S(2)}, u32[]{:S(2)}) collective-permute-start(bf16[3,2,256,128]{3,2,1,0:T(8,128)(2,1)} %get-tuple-element.79), channel_id=1, source_target_pairs={{0,7},{1,6},{2,5},{3,4},{4,3},{5,2},{6,1},{7,0},{8,15},{9,14},{10,... | collective-permute-start | bytes 1179656 | tf_op jit(solution)/shard_map/ppermute | solution.py:55
  217.0 64.2 %collective-permute-start.14 = (bf16[3,2,256,128]{3,2,1,0:T(8,128)(2,1)}, bf16[3,2,256,128]{3,2,1,0:T(8,128)(2,1)}, u32[]{:S(2)}, u32[]{:S(2)}) collective-permute-start(bf16[3,2,256,128]{3,2,1,0:T(8,128)(2,1)} %get-tuple-element.80), channel_id=1, source_target_pairs={{0,6},{1,7},{2,4},{3,5},{4,2},{5,3},{6,0},{7,1},{8,14},{9,15},{10,... | collective-permute-start | bytes 1179656 | tf_op jit(solution)/shard_map/ppermute | solution.py:55
  217.0 70.4 %collective-permute-start.12 = (bf16[3,2,256,128]{3,2,1,0:T(8,128)(2,1)}, bf16[3,2,256,128]{3,2,1,0:T(8,128)(2,1)}, u32[]{:S(2)}, u32[]{:S(2)}) collective-permute-start(bf16[3,2,256,128]{3,2,1,0:T(8,128)(2,1)} %get-tuple-element.78), channel_id=1, source_target_pairs={{0,5},{1,4},{2,7},{3,6},{4,1},{5,0},{6,3},{7,2},{8,13},{9,12},{10,... | collective-permute-start | bytes 1179656 | tf_op jit(solution)/shard_map/ppermute | solution.py:55
  238.5 0.7 copy-start.1
  239.2 56.5 %collective-permute-start.10 = (bf16[3,2,256,128]{3,2,1,0:T(8,128)(2,1)}, bf16[3,2,256,128]{3,2,1,0:T(8,128)(2,1)S(1)}, u32[]{:S(2)}, u32[]{:S(2)}) collective-permute-start(bf16[3,2,256,128]{3,2,1,0:T(8,128)(2,1)} %get-tuple-element.76), channel_id=1, source_target_pairs={{0,4},{1,5},{2,6},{3,7},{4,0},{5,1},{6,2},{7,3},{8,12},{9,13},{10,... | collective-permute-start | bytes 1179656 | tf_op jit(solution)/shard_map/ppermute | solution.py:55
  250.7 0.7 copy-start.3
  251.4 44.3 %collective-permute-start.11 = (bf16[3,2,256,128]{3,2,1,0:T(8,128)(2,1)}, bf16[3,2,256,128]{3,2,1,0:T(8,128)(2,1)}, u32[]{:S(2)}, u32[]{:S(2)}) collective-permute-start(bf16[3,2,256,128]{3,2,1,0:T(8,128)(2,1)} %get-tuple-element.77), channel_id=1, source_target_pairs={{0,2},{1,3},{2,0},{3,1},{4,6},{5,7},{6,4},{7,5},{8,10},{9,11},{10,... | collective-permute-start | bytes 1179656 | tf_op jit(solution)/shard_map/ppermute | solution.py:55
  261.7 2.3 copy-start
  261.7 2.3 copy-start.2
  261.7 2.3 copy-start.4

commit v18 on v17

--- a/solution.py
+++ b/solution.py
@@ -243,24 +243,16 @@
     ends = [sum(counts[: c + 1]) for c in range(len(counts))]
     groups = [refs[end - count : end] for end, count in zip(ends, counts)]
     outs = refs[ends[-1] + earlier :][:4]
-    stages = refs[-3 - len(counts) : -3]
-    ready, in_sems, out_sems = refs[-3:]
+    ready, out_sems = refs[-2:]
     head_dim = ready.shape[-1] // 2
-    used = [
-        sorted({head for job in jobs for which, head in job[1:] if which == c})
-        for c in range(len(counts))
-    ]
 
     def peer_of(j):
         return me[0] ^ (peers - 1 - items[j])
 
-    def fetch(which, j):
-        group = groups[which]
-        source = group[0].at[peer_of(j)] if joint[which] else group[j]
-        some = pl.ds(used[which][0], used[which][-1] - used[which][0] + 1)
-        return pltpu.make_async_copy(
-            source.at[some], stages[which].at[j, some], in_sems.at[which, j]
-        )
+    def side_of(which, j, head, kind):
+        if joint[which]:
+            return groups[which][0][peer_of(j), head, kind]
+        return groups[which][j][head, kind]
 
     def send(j, job, i):
         first = pl.multiple_of(peer_of(j) * per_peer, LANES) + jobs[job][0] * LANES
@@ -268,18 +260,15 @@
             ready.at[j, i, job], outs[i].at[:, pl.ds(first, LANES)], out_sems.at[j, i, job]
         )
 
-    steps = [(j, which) for j in range(len(items)) for which in range(len(counts))]
-    steps = [(j, which) for j, which in steps if used[which]]
-    for j, which in steps:
-        fetch(which, j).start()
     for j in range(len(items)):
-        for at, which in steps:
-            if at == j:
-                fetch(which, j).wait()
         for job, (_, left, right) in enumerate(jobs):
-            sides = [stages[which][j, head] for which, head in (left, right)]
             for i, (kind, half) in enumerate(((1, 1), (1, 0), (0, 0), (0, 1))):
-                ready[j, i, job] = join(sides[0][kind], sides[1][kind], head_dim, half)
+                ready[j, i, job] = join(
+                    side_of(left[0], j, left[1], kind),
+                    side_of(right[0], j, right[1], kind),
+                    head_dim,
+                    half,
+                )
                 send(j, job, i).start()
     for j in range(len(items)):
         for job in range(len(jobs)):
@@ -322,22 +311,18 @@
             per_peer=per_peer,
         ),
         in_specs=[pl.BlockSpec(memory_space=pltpu.SMEM)]
-        + [pl.BlockSpec(memory_space=pl.ANY)] * len(flat)
+        + [pl.BlockSpec(memory_space=pltpu.VMEM)] * len(flat)
         + [anywhere] * len(earlier),
         out_specs=[anywhere] * 4,
         out_shape=[pltpu.HBM((rows, peers * per_peer), dtype)] * 4,
         input_output_aliases={1 + len(flat) + i: i for i in range(len(earlier))},
         scratch_shapes=[
-            pltpu.VMEM((len(items),) + message_shape(m), dtype) for m in messages
-        ]
-        + [
             pltpu.VMEM((len(items), 4, len(jobs), rows, LANES), dtype),
-            pltpu.SemaphoreType.DMA((chunk + 1, len(items))),
             pltpu.SemaphoreType.DMA((len(items), 4, len(jobs))),
         ],
         compiler_params=pltpu.CompilerParams(vmem_limit_bytes=SMALL_VMEM),
         name="unpack_items",
-    )(me, *flat, *[in_hbm(x) for x in earlier])
+    )(me, *[in_vmem(x) for x in flat], *[in_hbm(x) for x in earlier])
 
 
 def pick_kernel(me, asked, *refs, count):

time: 304 us -> 303 us (level)
  transfers between devices with their start and end apart: 20 -> 20, of which waited for: 13 -> 13; matrix products, arithmetic and copies ran while one was open for 1% -> 1% of each run, Pallas kernels for 30% -> 29%
where the time goes in v18:
time: 303 us; the launch traced here: 298 us
  waiting for transfers between devices  142 us (47%)
  Pallas kernels  93.5 us (31%)
  starting transfers between devices  56.3 us (19%)
    all_to_all x3, waiting for transfers between devices, exchange(): lax.all_to_all(messages[0], 'seq', split_axis=0, concat_axis=0, tiled=True)  81.6 us
    pallas_call x2, Pallas kernels, attend(): pl.pallas_call(functools.partial(attend_kernel, head_dim=lanes // 2, per_...  58.3 us
    ppermute x7, waiting for transfers between devices, exchange(): received[item] = lax.ppermute(messages[item], 'seq', pairs)  55.1 us
    ppermute x10, starting transfers between devices, from_behind(): return lax.ppermute(x, axis, pairs)  27.8 us
    all_to_all x3, starting transfers between devices, exchange(): lax.all_to_all(messages[0], 'seq', split_axis=0, concat_axis=0, tiled=True)  19.3 us
    ppermute x7, starting transfers between devices, exchange(): received[item] = lax.ppermute(messages[item], 'seq', pairs)  9.18 us
    pallas_call x2, Pallas kernels, prepare(): pl.pallas_call(functools.partial(prepare_kernel, peers=peers), in_specs=[...  8.45 us
    pallas_call x2, Pallas kernels, pack(): pl.pallas_call(functools.partial(pack_kernel, first=start * head_dim, hea...  7.81 us
  transfers between devices with their start and end apart: 20, of which 13 were waited for; matrix products, arithmetic and copies ran while one was open for 1% of the time, Pallas kernels for 29%

profile of v18, /device:TPU:8, one launch (start us, length us, event | category | flops | bytes accessed | tf_op | source)
XLA Modules:
  0.0 298.1 jit_solution(13148160592209685808)
XLA Ops:
  0.6 3.9 %pack.2 = bf16[8,3,2,256,128]{4,3,2,1,0:T(8,128)(2,1)} custom-call(bf16[256,3072]{1,0:T(8,128)(2,1)} %query.3, bf16[256,3072]{1,0:T(8,128)(2,1)} %key.3, bf16[256,3072]{1,0:T(8,128)(2,1)} %value.3, bf16[256,3072]{1,0:T(8,128)(2,1)} %d_out.3), custom_call_target="tpu_custom_call" | custom-call | tf_op jit(solution)/shard_map/pack/pallas_call | solution.py:116
  4.6 6.3 %all-to-all-start = ((bf16[8,3,2,256,128]{4,3,2,1,0:T(8,128)(2,1)}), bf16[8,3,2,256,128]{4,3,2,1,0:T(8,128)(2,1)S(1)}, u32[]{:S(2)}, u32[]{:S(2)}) async-start(bf16[8,3,2,256,128]{4,3,2,1,0:T(8,128)(2,1)} %pack.2), calls=%async_computation | async-start | bytes 6291456 | tf_op jit(solution)/shard_map/all_to_all | solution.py:50
  11.0 0.2 compare_reduce_fusion.1
  11.2 1.2 top_k.24
  12.5 1.3 collective-permute-start.1
  13.8 1.2 top_k.17
  15.0 1.3 collective-permute-start
  16.6 3.2 %collective-permute-done = s32[4]{0:T(128)S(1)} collective-permute-done((s32[4]{0:T(128)S(1)}, s32[4]{0:T(128)S(1)}, u32[]{:S(2)}, u32[]{:S(2)}) %collective-permute-start) | collective-permute-done | bytes 48 | tf_op jit(solution)/shard_map/ppermute | solution.py:29
  19.9 3.9 %pack.3 = bf16[8,3,2,256,128]{4,3,2,1,0:T(8,128)(2,1)} custom-call(bf16[256,3072]{1,0:T(8,128)(2,1)} %query.3, bf16[256,3072]{1,0:T(8,128)(2,1)} %key.3, bf16[256,3072]{1,0:T(8,128)(2,1)} %value.3, bf16[256,3072]{1,0:T(8,128)(2,1)} %d_out.3, s32[8]{0:T(128)S(1)} %pad_add_fusion.asked.refs_0_, s32[6,16,8]{2,1,0:T(8,128)S(1)} %select_select_fusion.refs_1_), custom_call_target="tpu_custom_call" | custom-call | tf_op jit(solution)/shard_map/pack/pallas_call | solution.py:116
  23.8 55.3 %all-to-all-done.refs_0_ = bf16[8,3,2,256,128]{4,3,2,1,0:T(8,128)(2,1)S(1)} async-done(((bf16[8,3,2,256,128]{4,3,2,1,0:T(8,128)(2,1)}), bf16[8,3,2,256,128]{4,3,2,1,0:T(8,128)(2,1)S(1)}, u32[]{:S(2)}, u32[]{:S(2)}) %all-to-all-start) | async-done | bytes 3145760 | tf_op jit(solution)/shard_map/all_to_all | solution.py:50
  79.1 6.8 %all-to-all-start.2 = ((bf16[8,3,2,256,128]{4,3,2,1,0:T(8,128)(2,1)}), bf16[8,3,2,256,128]{4,3,2,1,0:T(8,128)(2,1)}, u32[]{:S(2)}, u32[]{:S(2)}) async-start(bf16[8,3,2,256,128]{4,3,2,1,0:T(8,128)(2,1)} %pack.3), calls=%async_computation.2 | async-start | bytes 6291456 | tf_op jit(solution)/shard_map/all_to_all | solution.py:50
  85.9 1.4 pick.2
  87.3 1.3 collective-permute-start.2
  88.7 1.3 collective-permute-start.3
  90.0 4.6 %prepare.2 = (bf16[3,24,128,128]{3,2,1,0:T(8,128)(2,1)S(1)}, bf16[8,3,256,128]{3,2,1,0:T(8,128)(2,1)S(1)}, f32[3,24,128,128]{3,2,1,0:T(8,128)S(1)}) custom-call(s32[1]{0:T(128)} %bitcast.me, bf16[3,24,128,128]{3,2,1,0:T(8,128)(2,1)S(1)} %get-tuple-element.58.table.table_in, bf16[8,3,2,256,128]{4,3,2,1,0:T(8,128)(2,1)S(1)} %all-to-all-done.refs_0_), custom_call_target="tpu_custom_call" | custom-call | tf_op jit(solution)/shard_map/prepare/pallas_call | solution.py:403
  94.6 29.4 %attend.2 = (bf16[8,3,256,128]{3,2,1,0:T(8,128)(2,1)S(1)}, bf16[4,3,128,128]{3,2,1,0:T(8,128)(2,1)S(1)}, bf16[4,3,128,128]{3,2,1,0:T(8,128)(2,1)S(1)}, bf16[3,24...) custom-call(s32[3,16,8]{2,1,0:T(8,128)S(1)} %get-tuple-element.105.l, ...), custom_call_target="tpu_custom_call", output_to_operand_aliasing={{3}: (4, {}), {4}: (5, {}), {5}: (6, {})} | custom-call | tf_op jit(solution)/shard_map/attend/pallas_call | solution.py:559
  124.0 1.3 collective-permute-start.4
  125.3 8.4 %collective-permute-start.5 = (bf16[4,3,128,128]{3,2,1,0:T(8,128)(2,1)S(1)}, bf16[4,3,128,128]{3,2,1,0:T(8,128)(2,1)S(1)}, u32[]{:S(2)}, u32[]{:S(2)}) collective-permute-start(bf16[4,3,128,128]{3,2,1,0:T(8,128)(2,1)S(1)} %get-tuple-element.65), channel_id=1, source_target_pairs={{0,8},{8,16},{16,24},{1,9},{9,17},{17,25},{2,10},{10,18},{18,26},{... | collective-permute-start | bytes 1179656 | tf_op jit(solution)/shard_map/ppermute | solution.py:29
  133.7 1.3 collective-permute-done.5.earlier
  135.0 2.6 finish.2.refs_1_
  137.6 16.0 %all-to-all-done.2.refs_0_ = bf16[8,3,2,256,128]{4,3,2,1,0:T(8,128)(2,1)} async-done(((bf16[8,3,2,256,128]{4,3,2,1,0:T(8,128)(2,1)}), bf16[8,3,2,256,128]{4,3,2,1,0:T(8,128)(2,1)}, u32[]{:S(2)}, u32[]{:S(2)}) %all-to-all-start.2) | async-done | bytes 3145760 | tf_op jit(solution)/shard_map/all_to_all | solution.py:50
  153.6 6.2 %all-to-all-start.1 = ((bf16[8,3,2,256,128]{4,3,2,1,0:T(8,128)(2,1)}), bf16[8,3,2,256,128]{4,3,2,1,0:T(8,128)(2,1)S(1)}, u32[]{:S(2)}, u32[]{:S(2)}) async-start(bf16[8,3,2,256,128]{4,3,2,1,0:T(8,128)(2,1)} %finish.2.refs_1_), calls=%async_computation.1 | async-start | bytes 6291456 | tf_op jit(solution)/shard_map/all_to_all | solution.py:50
  159.8 2.2 pick.3
  162.0 1.4 collective-permute-start.6
  163.4 1.3 collective-permute-start.7
  164.7 3.9 %prepare.3 = (bf16[3,24,128,128]{3,2,1,0:T(8,128)(2,1)S(1)}, bf16[8,3,256,128]{3,2,1,0:T(8,128)(2,1)S(1)}, f32[3,24,128,128]{3,2,1,0:T(8,128)S(1)}) custom-call(s32[1]{0:T(128)} %bitcast.me, bf16[3,24,128,128]{3,2,1,0:T(8,128)(2,1)S(1)} %get-tuple-element.68.table.table_in, bf16[8,3,2,256,128]{4,3,2,1,0:T(8,128)(2,1)} %all-to-all-done.2.refs_0_), custom_call_target="tpu_custom_call" | custom-call | tf_op jit(solution)/shard_map/prepare/pallas_call | solution.py:403
  168.7 28.9 %attend.3 = (bf16[8,3,256,128]{3,2,1,0:T(8,128)(2,1)S(1)}, bf16[4,3,128,128]{3,2,1,0:T(8,128)(2,1)S(1)}, bf16[4,3,128,128]{3,2,1,0:T(8,128)(2,1)S(1)}, bf16[3,24...) custom-call(s32[3,16,8]{2,1,0:T(8,128)S(1)} %get-tuple-element.104.l, ...), custom_call_target="tpu_custom_call", output_to_operand_aliasing={{3}: (4, {}), {4}: (5, {}), {5}: (6, {})} | custom-call | tf_op jit(solution)/shard_map/attend/pallas_call | solution.py:559
  197.6 1.3 collective-permute-start.8
  198.9 9.0 %collective-permute-start.9 = (bf16[4,3,128,128]{3,2,1,0:T(8,128)(2,1)S(1)}, bf16[4,3,128,128]{3,2,1,0:T(8,128)(2,1)S(1)}, u32[]{:S(2)}, u32[]{:S(2)}) collective-permute-start(bf16[4,3,128,128]{3,2,1,0:T(8,128)(2,1)S(1)} %get-tuple-element.75), channel_id=1, source_target_pairs={{0,8},{8,16},{16,24},{1,9},{9,17},{17,25},{2,10},{10,18},{18,26},{... | collective-permute-start | bytes 1179656 | tf_op jit(solution)/shard_map/ppermute | solution.py:29
  207.9 1.1 collective-permute-done.9.earlier
  209.0 2.6 finish.3
  211.7 1.5 collective-permute-start.15
  213.3 3.8 %collective-permute-start.13 = (bf16[3,2,256,128]{3,2,1,0:T(8,128)(2,1)}, bf16[3,2,256,128]{3,2,1,0:T(8,128)(2,1)}, u32[]{:S(2)}, u32[]{:S(2)}) collective-permute-start(bf16[3,2,256,128]{3,2,1,0:T(8,128)(2,1)} %get-tuple-element.79), channel_id=1, source_target_pairs={{0,7},{1,6},{2,5},{3,4},{4,3},{5,2},{6,1},{7,0},{8,15},{9,14},{10,... | collective-permute-start | bytes 1179656 | tf_op jit(solution)/shard_map/ppermute | solution.py:55
  217.0 3.8 %collective-permute-start.12 = (bf16[3,2,256,128]{3,2,1,0:T(8,128)(2,1)}, bf16[3,2,256,128]{3,2,1,0:T(8,128)(2,1)}, u32[]{:S(2)}, u32[]{:S(2)}) collective-permute-start(bf16[3,2,256,128]{3,2,1,0:T(8,128)(2,1)} %get-tuple-element.78), channel_id=1, source_target_pairs={{0,5},{1,4},{2,7},{3,6},{4,1},{5,0},{6,3},{7,2},{8,13},{9,12},{10,... | collective-permute-start | bytes 1179656 | tf_op jit(solution)/shard_map/ppermute | solution.py:55
  220.9 17.6 %collective-permute-done.15.refs_2_ = bf16[3,2,256,128]{3,2,1,0:T(8,128)(2,1)S(1)} collective-permute-done((bf16[3,2,256,128]{3,2,1,0:T(8,128)(2,1)}, bf16[3,2,256,128]{3,2,1,0:T(8,128)(2,1)S(1)}, u32[]{:S(2)}, u32[]{:S(2)}) %collective-permute-start.15) | collective-permute-done | bytes 393248 | tf_op jit(solution)/shard_map/ppermute | solution.py:55
  238.5 0.7 copy-done.1
  239.2 11.5 %collective-permute-done.16.refs_3_ = bf16[3,2,256,128]{3,2,1,0:T(8,128)(2,1)S(1)} collective-permute-done((bf16[3,2,256,128]{3,2,1,0:T(8,128)(2,1)}, bf16[3,2,256,128]{3,2,1,0:T(8,128)(2,1)S(1)}, u32[]{:S(2)}, u32[]{:S(2)}) %collective-permute-start.16) | collective-permute-done | bytes 393248 | tf_op jit(solution)/shard_map/ppermute | solution.py:55
  250.7 0.7 copy-done.3
  251.4 10.3 %all-to-all-done.1.refs_0_ = bf16[8,3,2,256,128]{4,3,2,1,0:T(8,128)(2,1)S(1)} async-done(((bf16[8,3,2,256,128]{4,3,2,1,0:T(8,128)(2,1)}), bf16[8,3,2,256,128]{4,3,2,1,0:T(8,128)(2,1)S(1)}, u32[]{:S(2)}, u32[]{:S(2)}) %all-to-all-start.1) | async-done | bytes 3145760 | tf_op jit(solution)/shard_map/all_to_all | solution.py:50
  261.7 2.2 unpack.1
  264.0 1.4 unpack_items.4
  265.5 9.9 %collective-permute-done.13.refs_1_ = bf16[3,2,256,128]{3,2,1,0:T(8,128)(2,1)} collective-permute-done((bf16[3,2,256,128]{3,2,1,0:T(8,128)(2,1)}, bf16[3,2,256,128]{3,2,1,0:T(8,128)(2,1)}, u32[]{:S(2)}, u32[]{:S(2)}) %collective-permute-start.13) | collective-permute-done | bytes 393248 | tf_op jit(solution)/shard_map/ppermute | solution.py:55
  275.4 5.8 %collective-permute-done.14.refs_2_ = bf16[3,2,256,128]{3,2,1,0:T(8,128)(2,1)} collective-permute-done((bf16[3,2,256,128]{3,2,1,0:T(8,128)(2,1)}, bf16[3,2,256,128]{3,2,1,0:T(8,128)(2,1)}, u32[]{:S(2)}, u32[]{:S(2)}) %collective-permute-start.14) | collective-permute-done | bytes 393248 | tf_op jit(solution)/shard_map/ppermute | solution.py:55
  281.2 2.3 unpack_items.5
  283.5 3.9 %collective-permute-done.12.refs_1_ = bf16[3,2,256,128]{3,2,1,0:T(8,128)(2,1)} collective-permute-done((bf16[3,2,256,128]{3,2,1,0:T(8,128)(2,1)}, bf16[3,2,256,128]{3,2,1,0:T(8,128)(2,1)}, u32[]{:S(2)}, u32[]{:S(2)}) %collective-permute-start.12) | collective-permute-done | bytes 393248 | tf_op jit(solution)/shard_map/ppermute | solution.py:55
  287.4 1.9 unpack_items.6
  289.3 6.4 %collective-permute-done.10.refs_1_ = bf16[3,2,256,128]{3,2,1,0:T(8,128)(2,1)S(1)} collective-permute-done((bf16[3,2,256,128]{3,2,1,0:T(8,128)(2,1)}, bf16[3,2,256,128]{3,2,1,0:T(8,128)(2,1)S(1)}, u32[]{:S(2)}, u32[]{:S(2)}) %collective-permute-start.10) | collective-permute-done | bytes 393248 | tf_op jit(solution)/shard_map/ppermute | solution.py:55
  295.7 2.2 unpack_items.7
  (37 shorter events, 0.7 us)
Async XLA Ops:
  4.5 6.3 %copy-start.5 = (s32[6,16,8]{1,2,0:T(8,128)S(1)}, s32[6,16,8]{1,2,0:T(8,128)}, u32[]{:S(2)}) copy-start(s32[6,16,8]{1,2,0:T(8,128)} %param.9) | copy-start | bytes 9220
  4.6 74.5 %all-to-all-start = ((bf16[8,3,2,256,128]{4,3,2,1,0:T(8,128)(2,1)}), bf16[8,3,2,256,128]{4,3,2,1,0:T(8,128)(2,1)S(1)}, u32[]{:S(2)}, u32[]{:S(2)}) async-start(bf16[8,3,2,256,128]{4,3,2,1,0:T(8,128)(2,1)} %pack.2), calls=%async_computation | async-start | bytes 6291456 | tf_op jit(solution)/shard_map/all_to_all | solution.py:50
  12.5 4.1 %collective-permute-start.1 = (s32[4]{0:T(128)S(1)}, s32[4]{0:T(128)S(1)}, u32[]{:S(2)}, u32[]{:S(2)}) collective-permute-start(s32[4]{0:T(128)S(1)} %get-tuple-element.109), channel_id=1, source_target_pairs={{0,8},{8,16},{16,24},{1,9},{9,17},{17,25},{2,10},{10,18},{18,26},{... | collective-permute-start | bytes 56 | tf_op jit(solution)/shard_map/ppermute | solution.py:29
  15.0 4.8 %collective-permute-start = (s32[4]{0:T(128)S(1)}, s32[4]{0:T(128)S(1)}, u32[]{:S(2)}, u32[]{:S(2)}) collective-permute-start(s32[4]{0:T(128)S(1)} %get-tuple-element.107), channel_id=1, source_target_pairs={{8,0},{16,8},{24,16},{9,1},{17,9},{25,17},{10,2},{18,10},{26,18},{... | collective-permute-start | bytes 56 | tf_op jit(solution)/shard_map/ppermute | solution.py:29
  79.1 74.5 %all-to-all-start.2 = ((bf16[8,3,2,256,128]{4,3,2,1,0:T(8,128)(2,1)}), bf16[8,3,2,256,128]{4,3,2,1,0:T(8,128)(2,1)}, u32[]{:S(2)}, u32[]{:S(2)}) async-start(bf16[8,3,2,256,128]{4,3,2,1,0:T(8,128)(2,1)} %pack.3), calls=%async_computation.2 | async-start | bytes 6291456 | tf_op jit(solution)/shard_map/all_to_all | solution.py:50
  87.3 7.2 %collective-permute-start.2 = (bf16[4,3,128,128]{3,2,1,0:T(8,128)(2,1)S(1)}, bf16[4,3,128,128]{3,2,1,0:T(8,128)(2,1)S(1)}, u32[]{:S(2)}, u32[]{:S(2)}) collective-permute-start(bf16[4,3,128,128]{3,2,1,0:T(8,128)(2,1)S(1)} %get-tuple-element.56), channel_id=1, source_target_pairs={{0,8},{8,16},{16,24},{1,9},{9,17},{17,25},{2,10},{10,18},{18,26},{... | collective-permute-start | bytes 1179656 | tf_op jit(solution)/shard_map/ppermute | solution.py:29
  88.7 5.9 %collective-permute-start.3 = (bf16[4,3,128,128]{3,2,1,0:T(8,128)(2,1)S(1)}, bf16[4,3,128,128]{3,2,1,0:T(8,128)(2,1)S(1)}, u32[]{:S(2)}, u32[]{:S(2)}) collective-permute-start(bf16[4,3,128,128]{3,2,1,0:T(8,128)(2,1)S(1)} %get-tuple-element.57), channel_id=1, source_target_pairs={{8,0},{16,8},{24,16},{9,1},{17,9},{25,17},{10,2},{18,10},{26,18},{... | collective-permute-start | bytes 1179656 | tf_op jit(solution)/shard_map/ppermute | solution.py:29
  124.0 9.7 %collective-permute-start.4 = (bf16[4,3,128,128]{3,2,1,0:T(8,128)(2,1)S(1)}, bf16[4,3,128,128]{3,2,1,0:T(8,128)(2,1)S(1)}, u32[]{:S(2)}, u32[]{:S(2)}) collective-permute-start(bf16[4,3,128,128]{3,2,1,0:T(8,128)(2,1)S(1)} %get-tuple-element.64), channel_id=1, source_target_pairs={{8,0},{16,8},{24,16},{9,1},{17,9},{25,17},{10,2},{18,10},{26,18},{... | collective-permute-start | bytes 1179656 | tf_op jit(solution)/shard_map/ppermute | solution.py:29
  125.3 9.7 %collective-permute-start.5 = (bf16[4,3,128,128]{3,2,1,0:T(8,128)(2,1)S(1)}, bf16[4,3,128,128]{3,2,1,0:T(8,128)(2,1)S(1)}, u32[]{:S(2)}, u32[]{:S(2)}) collective-permute-start(bf16[4,3,128,128]{3,2,1,0:T(8,128)(2,1)S(1)} %get-tuple-element.65), channel_id=1, source_target_pairs={{0,8},{8,16},{16,24},{1,9},{9,17},{17,25},{2,10},{10,18},{18,26},{... | collective-permute-start | bytes 1179656 | tf_op jit(solution)/shard_map/ppermute | solution.py:29
  153.6 108.1 %all-to-all-start.1 = ((bf16[8,3,2,256,128]{4,3,2,1,0:T(8,128)(2,1)}), bf16[8,3,2,256,128]{4,3,2,1,0:T(8,128)(2,1)S(1)}, u32[]{:S(2)}, u32[]{:S(2)}) async-start(bf16[8,3,2,256,128]{4,3,2,1,0:T(8,128)(2,1)} %finish.2.refs_1_), calls=%async_computation.1 | async-start | bytes 6291456 | tf_op jit(solution)/shard_map/all_to_all | solution.py:50
  162.0 6.6 %collective-permute-start.6 = (bf16[4,3,128,128]{3,2,1,0:T(8,128)(2,1)S(1)}, bf16[4,3,128,128]{3,2,1,0:T(8,128)(2,1)S(1)}, u32[]{:S(2)}, u32[]{:S(2)}) collective-permute-start(bf16[4,3,128,128]{3,2,1,0:T(8,128)(2,1)S(1)} %get-tuple-element.66), channel_id=1, source_target_pairs={{0,8},{8,16},{16,24},{1,9},{9,17},{17,25},{2,10},{10,18},{18,26},{... | collective-permute-start | bytes 1179656 | tf_op jit(solution)/shard_map/ppermute | solution.py:29
  163.4 5.3 %collective-permute-start.7 = (bf16[4,3,128,128]{3,2,1,0:T(8,128)(2,1)S(1)}, bf16[4,3,128,128]{3,2,1,0:T(8,128)(2,1)S(1)}, u32[]{:S(2)}, u32[]{:S(2)}) collective-permute-start(bf16[4,3,128,128]{3,2,1,0:T(8,128)(2,1)S(1)} %get-tuple-element.67), channel_id=1, source_target_pairs={{8,0},{16,8},{24,16},{9,1},{17,9},{25,17},{10,2},{18,10},{26,18},{... | collective-permute-start | bytes 1179656 | tf_op jit(solution)/shard_map/ppermute | solution.py:29
  197.6 10.3 %collective-permute-start.8 = (bf16[4,3,128,128]{3,2,1,0:T(8,128)(2,1)S(1)}, bf16[4,3,128,128]{3,2,1,0:T(8,128)(2,1)S(1)}, u32[]{:S(2)}, u32[]{:S(2)}) collective-permute-start(bf16[4,3,128,128]{3,2,1,0:T(8,128)(2,1)S(1)} %get-tuple-element.74), channel_id=1, source_target_pairs={{8,0},{16,8},{24,16},{9,1},{17,9},{25,17},{10,2},{18,10},{26,18},{... | collective-permute-start | bytes 1179656 | tf_op jit(solution)/shard_map/ppermute | solution.py:29
  198.9 10.2 %collective-permute-start.9 = (bf16[4,3,128,128]{3,2,1,0:T(8,128)(2,1)S(1)}, bf16[4,3,128,128]{3,2,1,0:T(8,128)(2,1)S(1)}, u32[]{:S(2)}, u32[]{:S(2)}) collective-permute-start(bf16[4,3,128,128]{3,2,1,0:T(8,128)(2,1)S(1)} %get-tuple-element.75), channel_id=1, source_target_pairs={{0,8},{8,16},{16,24},{1,9},{9,17},{17,25},{2,10},{10,18},{18,26},{... | collective-permute-start | bytes 1179656 | tf_op jit(solution)/shard_map/ppermute | solution.py:29
  211.7 26.8 %collective-permute-start.15 = (bf16[3,2,256,128]{3,2,1,0:T(8,128)(2,1)}, bf16[3,2,256,128]{3,2,1,0:T(8,128)(2,1)S(1)}, u32[]{:S(2)}, u32[]{:S(2)}) collective-permute-start(bf16[3,2,256,128]{3,2,1,0:T(8,128)(2,1)} %get-tuple-element.82), channel_id=1, source_target_pairs={{0,1},{1,0},{2,3},{3,2},{4,5},{5,4},{6,7},{7,6},{8,9},{9,8},{10,11... | collective-permute-start | bytes 1179656 | tf_op jit(solution)/shard_map/ppermute | solution.py:55
  213.2 37.5 %collective-permute-start.16 = (bf16[3,2,256,128]{3,2,1,0:T(8,128)(2,1)}, bf16[3,2,256,128]{3,2,1,0:T(8,128)(2,1)S(1)}, u32[]{:S(2)}, u32[]{:S(2)}) collective-permute-start(bf16[3,2,256,128]{3,2,1,0:T(8,128)(2,1)} %get-tuple-element.83), channel_id=1, source_target_pairs={{0,3},{1,2},{2,1},{3,0},{4,7},{5,6},{6,5},{7,4},{8,11},{9,10},{10,... | collective-permute-start | bytes 1179656 | tf_op jit(solution)/shard_map/ppermute | solution.py:55
  213.3 62.1 %collective-permute-start.13 = (bf16[3,2,256,128]{3,2,1,0:T(8,128)(2,1)}, bf16[3,2,256,128]{3,2,1,0:T(8,128)(2,1)}, u32[]{:S(2)}, u32[]{:S(2)}) collective-permute-start(bf16[3,2,256,128]{3,2,1,0:T(8,128)(2,1)} %get-tuple-element.79), channel_id=1, source_target_pairs={{0,7},{1,6},{2,5},{3,4},{4,3},{5,2},{6,1},{7,0},{8,15},{9,14},{10,... | collective-permute-start | bytes 1179656 | tf_op jit(solution)/shard_map/ppermute | solution.py:55
  217.0 64.2 %collective-permute-start.14 = (bf16[3,2,256,128]{3,2,1,0:T(8,128)(2,1)}, bf16[3,2,256,128]{3,2,1,0:T(8,128)(2,1)}, u32[]{:S(2)}, u32[]{:S(2)}) collective-permute-start(bf16[3,2,256,128]{3,2,1,0:T(8,128)(2,1)} %get-tuple-element.80), channel_id=1, source_target_pairs={{0,6},{1,7},{2,4},{3,5},{4,2},{5,3},{6,0},{7,1},{8,14},{9,15},{10,... | collective-permute-start | bytes 1179656 | tf_op jit(solution)/shard_map/ppermute | solution.py:55
  217.0 70.4 %collective-permute-start.12 = (bf16[3,2,256,128]{3,2,1,0:T(8,128)(2,1)}, bf16[3,2,256,128]{3,2,1,0:T(8,128)(2,1)}, u32[]{:S(2)}, u32[]{:S(2)}) collective-permute-start(bf16[3,2,256,128]{3,2,1,0:T(8,128)(2,1)} %get-tuple-element.78), channel_id=1, source_target_pairs={{0,5},{1,4},{2,7},{3,6},{4,1},{5,0},{6,3},{7,2},{8,13},{9,12},{10,... | collective-permute-start | bytes 1179656 | tf_op jit(solution)/shard_map/ppermute | solution.py:55
  238.5 0.7 copy-start.1
  239.2 56.5 %collective-permute-start.10 = (bf16[3,2,256,128]{3,2,1,0:T(8,128)(2,1)}, bf16[3,2,256,128]{3,2,1,0:T(8,128)(2,1)S(1)}, u32[]{:S(2)}, u32[]{:S(2)}) collective-permute-start(bf16[3,2,256,128]{3,2,1,0:T(8,128)(2,1)} %get-tuple-element.76), channel_id=1, source_target_pairs={{0,4},{1,5},{2,6},{3,7},{4,0},{5,1},{6,2},{7,3},{8,12},{9,13},{10,... | collective-permute-start | bytes 1179656 | tf_op jit(solution)/shard_map/ppermute | solution.py:55
  250.7 0.7 copy-start.3
  251.4 44.3 %collective-permute-start.11 = (bf16[3,2,256,128]{3,2,1,0:T(8,128)(2,1)}, bf16[3,2,256,128]{3,2,1,0:T(8,128)(2,1)}, u32[]{:S(2)}, u32[]{:S(2)}) collective-permute-start(bf16[3,2,256,128]{3,2,1,0:T(8,128)(2,1)} %get-tuple-element.77), channel_id=1, source_target_pairs={{0,2},{1,3},{2,0},{3,1},{4,6},{5,7},{6,4},{7,5},{8,10},{9,11},{10,... | collective-permute-start | bytes 1179656 | tf_op jit(solution)/shard_map/ppermute | solution.py:55
  261.7 2.3 copy-start
  261.7 2.3 copy-start.2
  261.7 2.3 copy-start.4

commit v19 on v18

--- a/solution.py
+++ b/solution.py
@@ -699,10 +699,10 @@
             half = peers // 2
             near = list(range(peers - 2, half - 1, -1))
             parts = (
-                [peers - 1, *near[::2]],
+                [peers - 1, near[0]],
                 list(range(half // 2)),
                 list(range(half // 2, half - 1)),
-                [half - 1, *near[1::2]],
+                [half - 1, *near[1:]],
             )
             for items in parts:
                 outs = unpack_items(me, received, starts, heads_here, items, outs)

time: 303 us -> 305 us (level)
  starting transfers between devices: 56.3 us -> 64.1 us
  waiting for transfers between devices: 142 us -> 138 us
    all_to_all x3, waiting for transfers between devices: 81.6 us -> 71.3 us  [exchange(): lax.all_to_all(messages[0], 'seq', split_axis=0, concat_axis=0, tiled=True)]
    ppermute x7, starting transfers between devices: 9.18 us -> 17 us  [exchange(): received[item] = lax.ppermute(messages[item], 'seq', pairs)]
    ppermute x7, waiting for transfers between devices: 55.1 us -> 61.3 us  [exchange(): received[item] = lax.ppermute(messages[item], 'seq', pairs)]
  transfers between devices with their start and end apart: 20 -> 20, of which waited for: 13 -> 12; matrix products, arithmetic and copies ran while one was open for 1% -> 1% of each run, Pallas kernels for 29% -> 29%
where the time goes in v19:
time: 305 us; the launch traced here: 301 us
  waiting for transfers between devices  138 us (45%)
  Pallas kernels  92.7 us (30%)
  starting transfers between devices  64.1 us (21%)
    all_to_all x3, waiting for transfers between devices, exchange(): lax.all_to_all(messages[0], 'seq', split_axis=0, concat_axis=0, tiled=True)  71.3 us
    ppermute x7, waiting for transfers between devices, exchange(): received[item] = lax.ppermute(messages[item], 'seq', pairs)  61.3 us
    pallas_call x2, Pallas kernels, attend(): pl.pallas_call(functools.partial(attend_kernel, head_dim=lanes // 2, per_...  58.3 us
    ppermute x10, starting transfers between devices, from_behind(): return lax.ppermute(x, axis, pairs)  27.8 us
    all_to_all x3, starting transfers between devices, exchange(): lax.all_to_all(messages[0], 'seq', split_axis=0, concat_axis=0, tiled=True)  19.3 us
    ppermute x7, starting transfers between devices, exchange(): received[item] = lax.ppermute(messages[item], 'seq', pairs)  17 us
    pallas_call x2, Pallas kernels, prepare(): pl.pallas_call(functools.partial(prepare_kernel, peers=peers), in_specs=[...  8.45 us
    pallas_call x2, Pallas kernels, pack(): pl.pallas_call(functools.partial(pack_kernel, first=start * head_dim, hea...  7.81 us
  transfers between devices with their start and end apart: 20, of which 12 were waited for; matrix products, arithmetic and copies ran while one was open for 1% of the time, Pallas kernels for 29%

profile of v19, /device:TPU:8, one launch (start us, length us, event | category | flops | bytes accessed | tf_op | source)
XLA Modules:
  0.0 300.9 jit_solution(12404559961193758253)
XLA Ops:
  0.6 3.9 %pack.2 = bf16[8,3,2,256,128]{4,3,2,1,0:T(8,128)(2,1)} custom-call(bf16[256,3072]{1,0:T(8,128)(2,1)} %query.3, bf16[256,3072]{1,0:T(8,128)(2,1)} %key.3, bf16[256,3072]{1,0:T(8,128)(2,1)} %value.3, bf16[256,3072]{1,0:T(8,128)(2,1)} %d_out.3), custom_call_target="tpu_custom_call" | custom-call | tf_op jit(solution)/shard_map/pack/pallas_call | solution.py:116
  4.6 6.3 %all-to-all-start = ((bf16[8,3,2,256,128]{4,3,2,1,0:T(8,128)(2,1)}), bf16[8,3,2,256,128]{4,3,2,1,0:T(8,128)(2,1)S(1)}, u32[]{:S(2)}, u32[]{:S(2)}) async-start(bf16[8,3,2,256,128]{4,3,2,1,0:T(8,128)(2,1)} %pack.2), calls=%async_computation | async-start | bytes 6291456 | tf_op jit(solution)/shard_map/all_to_all | solution.py:50
  11.2 1.2 top_k.24
  12.5 1.3 collective-permute-start.1
  13.8 1.2 top_k.17
  15.0 1.3 collective-permute-start
  16.6 3.2 %collective-permute-done = s32[4]{0:T(128)S(1)} collective-permute-done((s32[4]{0:T(128)S(1)}, s32[4]{0:T(128)S(1)}, u32[]{:S(2)}, u32[]{:S(2)}) %collective-permute-start) | collective-permute-done | bytes 48 | tf_op jit(solution)/shard_map/ppermute | solution.py:29
  19.9 3.9 %pack.3 = bf16[8,3,2,256,128]{4,3,2,1,0:T(8,128)(2,1)} custom-call(bf16[256,3072]{1,0:T(8,128)(2,1)} %query.3, bf16[256,3072]{1,0:T(8,128)(2,1)} %key.3, bf16[256,3072]{1,0:T(8,128)(2,1)} %value.3, bf16[256,3072]{1,0:T(8,128)(2,1)} %d_out.3, s32[8]{0:T(128)S(1)} %pad_add_fusion.asked.refs_0_, s32[6,16,8]{2,1,0:T(8,128)S(1)} %select_select_fusion.refs_1_), custom_call_target="tpu_custom_call" | custom-call | tf_op jit(solution)/shard_map/pack/pallas_call | solution.py:116
  23.8 55.3 %all-to-all-done.refs_0_ = bf16[8,3,2,256,128]{4,3,2,1,0:T(8,128)(2,1)S(1)} async-done(((bf16[8,3,2,256,128]{4,3,2,1,0:T(8,128)(2,1)}), bf16[8,3,2,256,128]{4,3,2,1,0:T(8,128)(2,1)S(1)}, u32[]{:S(2)}, u32[]{:S(2)}) %all-to-all-start) | async-done | bytes 3145760 | tf_op jit(solution)/shard_map/all_to_all | solution.py:50
  79.1 6.8 %all-to-all-start.2 = ((bf16[8,3,2,256,128]{4,3,2,1,0:T(8,128)(2,1)}), bf16[8,3,2,256,128]{4,3,2,1,0:T(8,128)(2,1)}, u32[]{:S(2)}, u32[]{:S(2)}) async-start(bf16[8,3,2,256,128]{4,3,2,1,0:T(8,128)(2,1)} %pack.3), calls=%async_computation.2 | async-start | bytes 6291456 | tf_op jit(solution)/shard_map/all_to_all | solution.py:50
  85.9 1.4 pick.2
  87.3 1.3 collective-permute-start.2
  88.7 1.3 collective-permute-start.3
  90.0 4.6 %prepare.2 = (bf16[3,24,128,128]{3,2,1,0:T(8,128)(2,1)S(1)}, bf16[8,3,256,128]{3,2,1,0:T(8,128)(2,1)S(1)}, f32[3,24,128,128]{3,2,1,0:T(8,128)S(1)}) custom-call(s32[1]{0:T(128)} %bitcast.me, bf16[3,24,128,128]{3,2,1,0:T(8,128)(2,1)S(1)} %get-tuple-element.58.table.table_in, bf16[8,3,2,256,128]{4,3,2,1,0:T(8,128)(2,1)S(1)} %all-to-all-done.refs_0_), custom_call_target="tpu_custom_call" | custom-call | tf_op jit(solution)/shard_map/prepare/pallas_call | solution.py:403
  94.6 29.4 %attend.2 = (bf16[8,3,256,128]{3,2,1,0:T(8,128)(2,1)S(1)}, bf16[4,3,128,128]{3,2,1,0:T(8,128)(2,1)S(1)}, bf16[4,3,128,128]{3,2,1,0:T(8,128)(2,1)S(1)}, bf16[3,24...) custom-call(s32[3,16,8]{2,1,0:T(8,128)S(1)} %get-tuple-element.105.l, ...), custom_call_target="tpu_custom_call", output_to_operand_aliasing={{3}: (4, {}), {4}: (5, {}), {5}: (6, {})} | custom-call | tf_op jit(solution)/shard_map/attend/pallas_call | solution.py:559
  124.0 1.3 collective-permute-start.4
  125.3 8.4 %collective-permute-start.5 = (bf16[4,3,128,128]{3,2,1,0:T(8,128)(2,1)S(1)}, bf16[4,3,128,128]{3,2,1,0:T(8,128)(2,1)S(1)}, u32[]{:S(2)}, u32[]{:S(2)}) collective-permute-start(bf16[4,3,128,128]{3,2,1,0:T(8,128)(2,1)S(1)} %get-tuple-element.65), channel_id=1, source_target_pairs={{0,8},{8,16},{16,24},{1,9},{9,17},{17,25},{2,10},{10,18},{18,26},{... | collective-permute-start | bytes 1179656 | tf_op jit(solution)/shard_map/ppermute | solution.py:29
  133.7 1.3 collective-permute-done.5.earlier
  135.0 2.6 finish.2.refs_1_
  137.6 16.0 %all-to-all-done.2.refs_0_ = bf16[8,3,2,256,128]{4,3,2,1,0:T(8,128)(2,1)} async-done(((bf16[8,3,2,256,128]{4,3,2,1,0:T(8,128)(2,1)}), bf16[8,3,2,256,128]{4,3,2,1,0:T(8,128)(2,1)}, u32[]{:S(2)}, u32[]{:S(2)}) %all-to-all-start.2) | async-done | bytes 3145760 | tf_op jit(solution)/shard_map/all_to_all | solution.py:50
  153.6 6.2 %all-to-all-start.1 = ((bf16[8,3,2,256,128]{4,3,2,1,0:T(8,128)(2,1)}), bf16[8,3,2,256,128]{4,3,2,1,0:T(8,128)(2,1)S(1)}, u32[]{:S(2)}, u32[]{:S(2)}) async-start(bf16[8,3,2,256,128]{4,3,2,1,0:T(8,128)(2,1)} %finish.2.refs_1_), calls=%async_computation.1 | async-start | bytes 6291456 | tf_op jit(solution)/shard_map/all_to_all | solution.py:50
  159.8 2.2 pick.3
  162.0 1.4 collective-permute-start.6
  163.4 1.3 collective-permute-start.7
  164.7 3.9 %prepare.3 = (bf16[3,24,128,128]{3,2,1,0:T(8,128)(2,1)S(1)}, bf16[8,3,256,128]{3,2,1,0:T(8,128)(2,1)S(1)}, f32[3,24,128,128]{3,2,1,0:T(8,128)S(1)}) custom-call(s32[1]{0:T(128)} %bitcast.me, bf16[3,24,128,128]{3,2,1,0:T(8,128)(2,1)S(1)} %get-tuple-element.68.table.table_in, bf16[8,3,2,256,128]{4,3,2,1,0:T(8,128)(2,1)} %all-to-all-done.2.refs_0_), custom_call_target="tpu_custom_call" | custom-call | tf_op jit(solution)/shard_map/prepare/pallas_call | solution.py:403
  168.7 28.9 %attend.3 = (bf16[8,3,256,128]{3,2,1,0:T(8,128)(2,1)S(1)}, bf16[4,3,128,128]{3,2,1,0:T(8,128)(2,1)S(1)}, bf16[4,3,128,128]{3,2,1,0:T(8,128)(2,1)S(1)}, bf16[3,24...) custom-call(s32[3,16,8]{2,1,0:T(8,128)S(1)} %get-tuple-element.104.l, ...), custom_call_target="tpu_custom_call", output_to_operand_aliasing={{3}: (4, {}), {4}: (5, {}), {5}: (6, {})} | custom-call | tf_op jit(solution)/shard_map/attend/pallas_call | solution.py:559
  197.6 1.3 collective-permute-start.8
  198.9 9.0 %collective-permute-start.9 = (bf16[4,3,128,128]{3,2,1,0:T(8,128)(2,1)S(1)}, bf16[4,3,128,128]{3,2,1,0:T(8,128)(2,1)S(1)}, u32[]{:S(2)}, u32[]{:S(2)}) collective-permute-start(bf16[4,3,128,128]{3,2,1,0:T(8,128)(2,1)S(1)} %get-tuple-element.75), channel_id=1, source_target_pairs={{0,8},{8,16},{16,24},{1,9},{9,17},{17,25},{2,10},{10,18},{18,26},{... | collective-permute-start | bytes 1179656 | tf_op jit(solution)/shard_map/ppermute | solution.py:29
  207.9 1.1 collective-permute-done.9.earlier
  209.0 2.6 finish.3
  211.7 1.5 collective-permute-start.16
  213.2 1.5 collective-permute-start.14
  214.6 0.6 collective-permute-start.15
  215.2 5.1 %collective-permute-start.13 = (bf16[3,2,256,128]{3,2,1,0:T(8,128)(2,1)}, bf16[3,2,256,128]{3,2,1,0:T(8,128)(2,1)S(1)}, u32[]{:S(2)}, u32[]{:S(2)}) collective-permute-start(bf16[3,2,256,128]{3,2,1,0:T(8,128)(2,1)} %get-tuple-element.79), channel_id=1, source_target_pairs={{0,5},{1,4},{2,7},{3,6},{4,1},{5,0},{6,3},{7,2},{8,13},{9,12},{10,... | collective-permute-start | bytes 1179656 | tf_op jit(solution)/shard_map/ppermute | solution.py:55
  220.3 6.1 %collective-permute-done.16.refs_2_ = bf16[3,2,256,128]{3,2,1,0:T(8,128)(2,1)S(1)} collective-permute-done((bf16[3,2,256,128]{3,2,1,0:T(8,128)(2,1)}, bf16[3,2,256,128]{3,2,1,0:T(8,128)(2,1)S(1)}, u32[]{:S(2)}, u32[]{:S(2)}) %collective-permute-start.16) | collective-permute-done | bytes 393248 | tf_op jit(solution)/shard_map/ppermute | solution.py:55
  226.4 0.7 copy-done.3
  227.1 8.4 %collective-permute-start.11 = (bf16[3,2,256,128]{3,2,1,0:T(8,128)(2,1)}, bf16[3,2,256,128]{3,2,1,0:T(8,128)(2,1)}, u32[]{:S(2)}, u32[]{:S(2)}) collective-permute-start(bf16[3,2,256,128]{3,2,1,0:T(8,128)(2,1)} %get-tuple-element.77), channel_id=1, source_target_pairs={{0,2},{1,3},{2,0},{3,1},{4,6},{5,7},{6,4},{7,5},{8,10},{9,11},{10,... | collective-permute-start | bytes 1179656 | tf_op jit(solution)/shard_map/ppermute | solution.py:55
  235.5 37.8 %collective-permute-done.14.refs_1_ = bf16[3,2,256,128]{3,2,1,0:T(8,128)(2,1)S(1)} collective-permute-done((bf16[3,2,256,128]{3,2,1,0:T(8,128)(2,1)}, bf16[3,2,256,128]{3,2,1,0:T(8,128)(2,1)S(1)}, u32[]{:S(2)}, u32[]{:S(2)}) %collective-permute-start.14) | collective-permute-done | bytes 393248 | tf_op jit(solution)/shard_map/ppermute | solution.py:55
  273.3 0.7 copy-done.1
  274.1 2.3 unpack.1
  276.4 1.2 unpack_items.4
  277.6 3.5 %collective-permute-done.15.refs_2_ = bf16[3,2,256,128]{3,2,1,0:T(8,128)(2,1)} collective-permute-done((bf16[3,2,256,128]{3,2,1,0:T(8,128)(2,1)}, bf16[3,2,256,128]{3,2,1,0:T(8,128)(2,1)}, u32[]{:S(2)}, u32[]{:S(2)}) %collective-permute-start.15) | collective-permute-done | bytes 393248 | tf_op jit(solution)/shard_map/ppermute | solution.py:55
  281.1 2.2 unpack_items.5
  283.3 4.1 %collective-permute-done.13.refs_1_ = bf16[3,2,256,128]{3,2,1,0:T(8,128)(2,1)S(1)} collective-permute-done((bf16[3,2,256,128]{3,2,1,0:T(8,128)(2,1)}, bf16[3,2,256,128]{3,2,1,0:T(8,128)(2,1)S(1)}, u32[]{:S(2)}, u32[]{:S(2)}) %collective-permute-start.13) | collective-permute-done | bytes 393248 | tf_op jit(solution)/shard_map/ppermute | solution.py:55
  287.4 0.9 unpack_items.6
  288.3 7.4 %collective-permute-done.10.refs_1_ = bf16[3,2,256,128]{3,2,1,0:T(8,128)(2,1)} collective-permute-done((bf16[3,2,256,128]{3,2,1,0:T(8,128)(2,1)}, bf16[3,2,256,128]{3,2,1,0:T(8,128)(2,1)}, u32[]{:S(2)}, u32[]{:S(2)}) %collective-permute-start.10) | collective-permute-done | bytes 393248 | tf_op jit(solution)/shard_map/ppermute | solution.py:55
  295.7 2.4 collective-permute-done.12.refs_3_
  298.1 2.6 unpack_items.7
  (37 shorter events, 0.8 us)
Async XLA Ops:
  4.5 6.3 %copy-start.5 = (s32[6,16,8]{1,2,0:T(8,128)S(1)}, s32[6,16,8]{1,2,0:T(8,128)}, u32[]{:S(2)}) copy-start(s32[6,16,8]{1,2,0:T(8,128)} %param.9) | copy-start | bytes 9220
  4.6 74.5 %all-to-all-start = ((bf16[8,3,2,256,128]{4,3,2,1,0:T(8,128)(2,1)}), bf16[8,3,2,256,128]{4,3,2,1,0:T(8,128)(2,1)S(1)}, u32[]{:S(2)}, u32[]{:S(2)}) async-start(bf16[8,3,2,256,128]{4,3,2,1,0:T(8,128)(2,1)} %pack.2), calls=%async_computation | async-start | bytes 6291456 | tf_op jit(solution)/shard_map/all_to_all | solution.py:50
  12.5 4.1 %collective-permute-start.1 = (s32[4]{0:T(128)S(1)}, s32[4]{0:T(128)S(1)}, u32[]{:S(2)}, u32[]{:S(2)}) collective-permute-start(s32[4]{0:T(128)S(1)} %get-tuple-element.109), channel_id=1, source_target_pairs={{0,8},{8,16},{16,24},{1,9},{9,17},{17,25},{2,10},{10,18},{18,26},{... | collective-permute-start | bytes 56 | tf_op jit(solution)/shard_map/ppermute | solution.py:29
  15.0 4.8 %collective-permute-start = (s32[4]{0:T(128)S(1)}, s32[4]{0:T(128)S(1)}, u32[]{:S(2)}, u32[]{:S(2)}) collective-permute-start(s32[4]{0:T(128)S(1)} %get-tuple-element.107), channel_id=1, source_target_pairs={{8,0},{16,8},{24,16},{9,1},{17,9},{25,17},{10,2},{18,10},{26,18},{... | collective-permute-start | bytes 56 | tf_op jit(solution)/shard_map/ppermute | solution.py:29
  79.1 74.5 %all-to-all-start.2 = ((bf16[8,3,2,256,128]{4,3,2,1,0:T(8,128)(2,1)}), bf16[8,3,2,256,128]{4,3,2,1,0:T(8,128)(2,1)}, u32[]{:S(2)}, u32[]{:S(2)}) async-start(bf16[8,3,2,256,128]{4,3,2,1,0:T(8,128)(2,1)} %pack.3), calls=%async_computation.2 | async-start | bytes 6291456 | tf_op jit(solution)/shard_map/all_to_all | solution.py:50
  87.3 7.2 %collective-permute-start.2 = (bf16[4,3,128,128]{3,2,1,0:T(8,128)(2,1)S(1)}, bf16[4,3,128,128]{3,2,1,0:T(8,128)(2,1)S(1)}, u32[]{:S(2)}, u32[]{:S(2)}) collective-permute-start(bf16[4,3,128,128]{3,2,1,0:T(8,128)(2,1)S(1)} %get-tuple-element.56), channel_id=1, source_target_pairs={{0,8},{8,16},{16,24},{1,9},{9,17},{17,25},{2,10},{10,18},{18,26},{... | collective-permute-start | bytes 1179656 | tf_op jit(solution)/shard_map/ppermute | solution.py:29
  88.7 5.9 %collective-permute-start.3 = (bf16[4,3,128,128]{3,2,1,0:T(8,128)(2,1)S(1)}, bf16[4,3,128,128]{3,2,1,0:T(8,128)(2,1)S(1)}, u32[]{:S(2)}, u32[]{:S(2)}) collective-permute-start(bf16[4,3,128,128]{3,2,1,0:T(8,128)(2,1)S(1)} %get-tuple-element.57), channel_id=1, source_target_pairs={{8,0},{16,8},{24,16},{9,1},{17,9},{25,17},{10,2},{18,10},{26,18},{... | collective-permute-start | bytes 1179656 | tf_op jit(solution)/shard_map/ppermute | solution.py:29
  124.0 9.7 %collective-permute-start.4 = (bf16[4,3,128,128]{3,2,1,0:T(8,128)(2,1)S(1)}, bf16[4,3,128,128]{3,2,1,0:T(8,128)(2,1)S(1)}, u32[]{:S(2)}, u32[]{:S(2)}) collective-permute-start(bf16[4,3,128,128]{3,2,1,0:T(8,128)(2,1)S(1)} %get-tuple-element.64), channel_id=1, source_target_pairs={{8,0},{16,8},{24,16},{9,1},{17,9},{25,17},{10,2},{18,10},{26,18},{... | collective-permute-start | bytes 1179656 | tf_op jit(solution)/shard_map/ppermute | solution.py:29
  125.3 9.7 %collective-permute-start.5 = (bf16[4,3,128,128]{3,2,1,0:T(8,128)(2,1)S(1)}, bf16[4,3,128,128]{3,2,1,0:T(8,128)(2,1)S(1)}, u32[]{:S(2)}, u32[]{:S(2)}) collective-permute-start(bf16[4,3,128,128]{3,2,1,0:T(8,128)(2,1)S(1)} %get-tuple-element.65), channel_id=1, source_target_pairs={{0,8},{8,16},{16,24},{1,9},{9,17},{17,25},{2,10},{10,18},{18,26},{... | collective-permute-start | bytes 1179656 | tf_op jit(solution)/shard_map/ppermute | solution.py:29
  153.6 120.5 %all-to-all-start.1 = ((bf16[8,3,2,256,128]{4,3,2,1,0:T(8,128)(2,1)}), bf16[8,3,2,256,128]{4,3,2,1,0:T(8,128)(2,1)S(1)}, u32[]{:S(2)}, u32[]{:S(2)}) async-start(bf16[8,3,2,256,128]{4,3,2,1,0:T(8,128)(2,1)} %finish.2.refs_1_), calls=%async_computation.1 | async-start | bytes 6291456 | tf_op jit(solution)/shard_map/all_to_all | solution.py:50
  162.0 6.6 %collective-permute-start.6 = (bf16[4,3,128,128]{3,2,1,0:T(8,128)(2,1)S(1)}, bf16[4,3,128,128]{3,2,1,0:T(8,128)(2,1)S(1)}, u32[]{:S(2)}, u32[]{:S(2)}) collective-permute-start(bf16[4,3,128,128]{3,2,1,0:T(8,128)(2,1)S(1)} %get-tuple-element.66), channel_id=1, source_target_pairs={{0,8},{8,16},{16,24},{1,9},{9,17},{17,25},{2,10},{10,18},{18,26},{... | collective-permute-start | bytes 1179656 | tf_op jit(solution)/shard_map/ppermute | solution.py:29
  163.4 5.3 %collective-permute-start.7 = (bf16[4,3,128,128]{3,2,1,0:T(8,128)(2,1)S(1)}, bf16[4,3,128,128]{3,2,1,0:T(8,128)(2,1)S(1)}, u32[]{:S(2)}, u32[]{:S(2)}) collective-permute-start(bf16[4,3,128,128]{3,2,1,0:T(8,128)(2,1)S(1)} %get-tuple-element.67), channel_id=1, source_target_pairs={{8,0},{16,8},{24,16},{9,1},{17,9},{25,17},{10,2},{18,10},{26,18},{... | collective-permute-start | bytes 1179656 | tf_op jit(solution)/shard_map/ppermute | solution.py:29
  197.6 10.3 %collective-permute-start.8 = (bf16[4,3,128,128]{3,2,1,0:T(8,128)(2,1)S(1)}, bf16[4,3,128,128]{3,2,1,0:T(8,128)(2,1)S(1)}, u32[]{:S(2)}, u32[]{:S(2)}) collective-permute-start(bf16[4,3,128,128]{3,2,1,0:T(8,128)(2,1)S(1)} %get-tuple-element.74), channel_id=1, source_target_pairs={{8,0},{16,8},{24,16},{9,1},{17,9},{25,17},{10,2},{18,10},{26,18},{... | collective-permute-start | bytes 1179656 | tf_op jit(solution)/shard_map/ppermute | solution.py:29
  198.9 10.2 %collective-permute-start.9 = (bf16[4,3,128,128]{3,2,1,0:T(8,128)(2,1)S(1)}, bf16[4,3,128,128]{3,2,1,0:T(8,128)(2,1)S(1)}, u32[]{:S(2)}, u32[]{:S(2)}) collective-permute-start(bf16[4,3,128,128]{3,2,1,0:T(8,128)(2,1)S(1)} %get-tuple-element.75), channel_id=1, source_target_pairs={{0,8},{8,16},{16,24},{1,9},{9,17},{17,25},{2,10},{10,18},{18,26},{... | collective-permute-start | bytes 1179656 | tf_op jit(solution)/shard_map/ppermute | solution.py:29
  211.7 14.7 %collective-permute-start.16 = (bf16[3,2,256,128]{3,2,1,0:T(8,128)(2,1)}, bf16[3,2,256,128]{3,2,1,0:T(8,128)(2,1)S(1)}, u32[]{:S(2)}, u32[]{:S(2)}) collective-permute-start(bf16[3,2,256,128]{3,2,1,0:T(8,128)(2,1)} %get-tuple-element.83), channel_id=1, source_target_pairs={{0,1},{1,0},{2,3},{3,2},{4,5},{5,4},{6,7},{7,6},{8,9},{9,8},{10,11... | collective-permute-start | bytes 1179656 | tf_op jit(solution)/shard_map/ppermute | solution.py:55
  213.2 60.1 %collective-permute-start.14 = (bf16[3,2,256,128]{3,2,1,0:T(8,128)(2,1)}, bf16[3,2,256,128]{3,2,1,0:T(8,128)(2,1)S(1)}, u32[]{:S(2)}, u32[]{:S(2)}) collective-permute-start(bf16[3,2,256,128]{3,2,1,0:T(8,128)(2,1)} %get-tuple-element.80), channel_id=1, source_target_pairs={{0,7},{1,6},{2,5},{3,4},{4,3},{5,2},{6,1},{7,0},{8,15},{9,14},{10,... | collective-permute-start | bytes 1179656 | tf_op jit(solution)/shard_map/ppermute | solution.py:55
  214.6 66.5 %collective-permute-start.15 = (bf16[3,2,256,128]{3,2,1,0:T(8,128)(2,1)}, bf16[3,2,256,128]{3,2,1,0:T(8,128)(2,1)}, u32[]{:S(2)}, u32[]{:S(2)}) collective-permute-start(bf16[3,2,256,128]{3,2,1,0:T(8,128)(2,1)} %get-tuple-element.81), channel_id=1, source_target_pairs={{0,6},{1,7},{2,4},{3,5},{4,2},{5,3},{6,0},{7,1},{8,14},{9,15},{10,... | collective-permute-start | bytes 1179656 | tf_op jit(solution)/shard_map/ppermute | solution.py:55
  215.2 72.1 %collective-permute-start.13 = (bf16[3,2,256,128]{3,2,1,0:T(8,128)(2,1)}, bf16[3,2,256,128]{3,2,1,0:T(8,128)(2,1)S(1)}, u32[]{:S(2)}, u32[]{:S(2)}) collective-permute-start(bf16[3,2,256,128]{3,2,1,0:T(8,128)(2,1)} %get-tuple-element.79), channel_id=1, source_target_pairs={{0,5},{1,4},{2,7},{3,6},{4,1},{5,0},{6,3},{7,2},{8,13},{9,12},{10,... | collective-permute-start | bytes 1179656 | tf_op jit(solution)/shard_map/ppermute | solution.py:55
  220.3 75.4 %collective-permute-start.10 = (bf16[3,2,256,128]{3,2,1,0:T(8,128)(2,1)}, bf16[3,2,256,128]{3,2,1,0:T(8,128)(2,1)}, u32[]{:S(2)}, u32[]{:S(2)}) collective-permute-start(bf16[3,2,256,128]{3,2,1,0:T(8,128)(2,1)} %get-tuple-element.76), channel_id=1, source_target_pairs={{0,4},{1,5},{2,6},{3,7},{4,0},{5,1},{6,2},{7,3},{8,12},{9,13},{10,... | collective-permute-start | bytes 1179656 | tf_op jit(solution)/shard_map/ppermute | solution.py:55
  226.4 0.7 copy-start.3
  227.1 68.6 %collective-permute-start.11 = (bf16[3,2,256,128]{3,2,1,0:T(8,128)(2,1)}, bf16[3,2,256,128]{3,2,1,0:T(8,128)(2,1)}, u32[]{:S(2)}, u32[]{:S(2)}) collective-permute-start(bf16[3,2,256,128]{3,2,1,0:T(8,128)(2,1)} %get-tuple-element.77), channel_id=1, source_target_pairs={{0,2},{1,3},{2,0},{3,1},{4,6},{5,7},{6,4},{7,5},{8,10},{9,11},{10,... | collective-permute-start | bytes 1179656 | tf_op jit(solution)/shard_map/ppermute | solution.py:55
  273.3 0.7 copy-start.1
  274.1 24.0 %collective-permute-start.12 = (bf16[3,2,256,128]{3,2,1,0:T(8,128)(2,1)}, bf16[3,2,256,128]{3,2,1,0:T(8,128)(2,1)}, u32[]{:S(2)}, u32[]{:S(2)}) collective-permute-start(bf16[3,2,256,128]{3,2,1,0:T(8,128)(2,1)} %get-tuple-element.78), channel_id=1, source_target_pairs={{0,3},{1,2},{2,1},{3,0},{4,7},{5,6},{6,5},{7,4},{8,11},{9,10},{10,... | collective-permute-start | bytes 1179656 | tf_op jit(solution)/shard_map/ppermute | solution.py:55
  274.1 2.3 copy-start
  274.1 2.3 copy-start.4
  276.4 4.7 %copy-start.2 = (bf16[3,2,256,128]{3,2,1,0:T(8,128)(2,1)S(1)}, bf16[3,2,256,128]{3,2,1,0:T(8,128)(2,1)}, u32[]{:S(2)}) copy-start(bf16[3,2,256,128]{3,2,1,0:T(8,128)(2,1)} %copy-done.1) | copy-start | bytes 1179652
